TPU v7x, 32 devices: a whole 2x2x4 slice. The times are simulated.
32 devices in a mesh: rep: 4 (over y, x), blk: 8 (over z, core).
Axes of the slice: x: 2, y: 2, z: 4, core: 2. Of those that a mesh axis runs over, the one named last changes fastest.
Arguments:
- features: bfloat16 [8, 1024, 128], P('blk', 'rep'), may hold values from -6 to 6
- node_ids: int32 [8, 1024], P('blk', 'rep'), may hold values from 0 to 8388607
- labels: int32 [8, 1024], P('blk', 'rep'), may hold values from 0 to 171
- train_mask: int32 [8, 1024], P('blk', 'rep'), may hold values 0 or 1
- tile_values: bfloat16 [8, 4, 2, 16, 128, 128], P('blk', 'rep'), may hold values from -0.1875 to 0.1875
- tile_place: int32 [8, 4, 2, 16], P('blk', 'rep'), may hold values from 0 to 63, as said below
- tile_count: int32 [8, 4, 2], P('blk', 'rep'), may hold values from 1 to 16, as said below
- weight_in: bfloat16 [128, 256], replicated, may hold values from -0.5 to 0.5
- weight_out: bfloat16 [256, 172], replicated, may hold values from -8 to 8
- class_bias: float32 [172], replicated, may hold values from -5 to 5
Outputs:
- logits: float32 [8, 1024, 172], P('blk', 'rep')
- grad_in: float32 [128, 256], replicated
- grad_out: float32 [256, 172], replicated
Inputs may be any that keep to these rules, and one draw needn't show every extreme that they name: `tile_place`: within one block pair the slots name distinct positions. `tile_count`: the live slots of a pair are its first ones; some device has 16 live slots in each of its pairs.
All inputs are finite; a program needn't handle non-finite values. No bound on the sum of `train_mask` on one device may be relied on, other than what follows from the above.
Results may differ from a plain program's by a relative error of at most 0.015.
The roundings to bfloat16 on the way count: a program that leaves them out, or rounds other values in their place, can miss the bound.
Values may be sent and summed in bfloat16 or wider, within the bound.
No kernel may reach another device: no remote copies, remote signals or barrier semaphores. Data moves between devices by JAX's collectives and lax.ppermute only.
A program may use at most 128 MiB of HBM per device.

v0:
```python
import math

import jax
import jax.numpy as jnp
from jax import lax
from jax.sharding import PartitionSpec as P


def from_behind(value, axis, steps):
    count = lax.axis_size(axis)
    pairs = [(source, (source + steps) % count) for source in range(count)]
    return lax.ppermute(value, axis, pairs)


def keep_factor(id_values, unit_count):
    columns = jnp.arange(unit_count, dtype=jnp.int32)
    mixed = id_values[:, None] * 73244475 + columns[None, :] * 19349663 + 12345
    mixed = mixed ^ jnp.right_shift(mixed, 15)
    mixed = mixed * 40503
    mixed = mixed ^ jnp.right_shift(mixed, 13)
    kept_mask = jnp.bitwise_and(mixed, 3) != 0
    return jnp.where(kept_mask, jnp.float32(4.0 / 3.0), jnp.float32(0.0))


def place_rows(tile_group, place_group, live_slots, source, tile_side, backward):
    tile_edge = tile_group.shape[-1]
    feat_width = source.shape[-1]
    pieces = source.reshape(tile_side, tile_edge, feat_width)
    if backward:
        gathered = jnp.take(pieces, place_group // tile_side, axis=0)
        products = jnp.einsum(
            "tji,tjf->tif", tile_group, gathered, preferred_element_type=jnp.float32
        )
        target = place_group % tile_side
    else:
        gathered = jnp.take(pieces, place_group % tile_side, axis=0)
        products = jnp.einsum(
            "tij,tjf->tif", tile_group, gathered, preferred_element_type=jnp.float32
        )
        target = place_group // tile_side
    masked = products * live_slots.astype(jnp.float32)[:, None, None]
    summed = jnp.zeros((tile_side, tile_edge, feat_width), jnp.float32).at[target].add(masked)
    return summed.reshape(tile_side * tile_edge, feat_width)


def section_terms(section_tiles, section_place, section_count, source, tile_side, backward):
    slot_count = section_tiles.shape[0]
    live_slots = jnp.arange(slot_count, dtype=jnp.int32) < section_count
    return place_rows(section_tiles, section_place, live_slots, source, tile_side, backward)


def slope_of(logits, label_ids, node_mask, scale):
    likelihood = jax.nn.softmax(logits, axis=-1)
    onehot = (label_ids[:, None] == jnp.arange(logits.shape[-1], dtype=jnp.int32)[None, :]).astype(
        jnp.float32
    )
    return ((likelihood - onehot) * node_mask[:, None].astype(jnp.float32) * scale).astype(
        jnp.bfloat16
    )


def on_device(
    features,
    node_ids,
    labels,
    train_mask,
    tile_values,
    tile_place,
    tile_count,
    weight_in,
    weight_out,
    class_bias,
):
    own_rows = features.shape[1]
    rep_size = lax.axis_size("rep")
    blk_size = lax.axis_size("blk")
    rep_index = lax.axis_index("rep")
    rep_bits = (rep_size - 1).bit_length()
    section_total = tile_values.shape[2]
    tile_edge = tile_values.shape[-1]
    group_rows = own_rows * rep_size
    tile_side = group_rows // tile_edge
    hidden_width = weight_in.shape[1]
    tiles_here = tile_values[0, 0]
    place_here = tile_place[0, 0]
    count_here = tile_count[0, 0]
    scale = 1.0 / math.sqrt(group_rows * blk_size)

    def spread(source):
        for bit_index in range(rep_bits):
            shifted = from_behind(source, "blk", section_total * (1 << bit_index))
            source = jnp.where(jnp.right_shift(rep_index, bit_index) % 2 == 1, shifted, source)
        running_sum = jnp.zeros((group_rows, source.shape[1]), jnp.float32)
        for section_index in range(section_total):
            running_sum = running_sum + section_terms(
                tiles_here[section_index],
                place_here[section_index],
                count_here[section_index],
                source,
                tile_side,
                False,
            )
            if section_index + 1 < section_total:
                source = from_behind(source, "blk", 1)
        return running_sum

    feature_block = lax.all_gather(features[0], "rep", axis=0, tiled=True)
    z_input = lax.psum_scatter(
        spread(feature_block), "rep", scatter_dimension=0, tiled=True
    ).astype(jnp.bfloat16)
    kept = keep_factor(node_ids[0], hidden_width)
    pre_act = jnp.dot(z_input, weight_in, preferred_element_type=jnp.float32)
    dropped = (jnp.maximum(pre_act, 0.0) * kept).astype(jnp.bfloat16)
    hidden_block = lax.all_gather(dropped, "rep", axis=0, tiled=True)
    z_output = lax.psum_scatter(
        spread(hidden_block), "rep", scatter_dimension=0, tiled=True
    ).astype(jnp.bfloat16)
    logits = jnp.dot(z_output, weight_out, preferred_element_type=jnp.float32) + class_bias
    slope = slope_of(logits, labels[0], train_mask[0], scale)
    grad_rows = jnp.einsum(
        "nc,hc->nh", slope, weight_out, preferred_element_type=jnp.float32
    ).astype(jnp.bfloat16)
    gradient_block = lax.all_gather(grad_rows, "rep", axis=0, tiled=True)
    out_terms = jnp.einsum("nh,nc->hc", z_output, slope, preferred_element_type=jnp.float32)
    grad_out = lax.psum(out_terms, ("rep", "blk"))
    running_sum = jnp.zeros((group_rows, gradient_block.shape[1]), jnp.float32)
    for section_index in reversed(range(section_total)):
        running_sum = running_sum + section_terms(
            tiles_here[section_index],
            place_here[section_index],
            count_here[section_index],
            gradient_block,
            tile_side,
            True,
        )
        if section_index > 0:
            running_sum = from_behind(running_sum.astype(jnp.bfloat16), "blk", -1).astype(
                running_sum.dtype
            )
    for bit_index in range(rep_bits):
        shifted = from_behind(
            running_sum.astype(jnp.bfloat16), "blk", -section_total * (1 << bit_index)
        ).astype(running_sum.dtype)
        running_sum = jnp.where(
            jnp.right_shift(rep_index, bit_index) % 2 == 1, shifted, running_sum
        )
    back_rows = lax.psum_scatter(
        running_sum.astype(jnp.bfloat16), "rep", scatter_dimension=0, tiled=True
    ).astype(jnp.float32)
    pre_slope = (back_rows * kept * (pre_act > 0)).astype(jnp.bfloat16)
    in_terms = jnp.einsum("nf,nh->fh", z_input, pre_slope, preferred_element_type=jnp.float32)
    grad_in = lax.psum(in_terms, ("rep", "blk"))
    return (logits[None], grad_in, grad_out)


def solution(mesh):
    placed = (
        P("blk", "rep", None),
        P("blk", "rep"),
        P("blk", "rep"),
        P("blk", "rep"),
        P("blk", "rep", None, None, None, None),
        P("blk", "rep", None, None),
        P("blk", "rep", None),
        P(),
        P(),
        P(),
    )
    return jax.shard_map(
        on_device,
        mesh=mesh,
        in_specs=placed,
        out_specs=(P("blk", "rep", None), P(), P()),
        check_vma=False,
    )
```

profile of v0, /device:TPU:0, one launch (start us, length us, event | category | flops | bytes accessed | tf_op | source)
XLA Modules:
  0.0 413.9 jit_solution(2296358625455609988)
XLA Ops:
  7.2 10.9 %all-gather = bf16[1,1024,128]{2,1,0:T(8,128)(2,1)S(1)} all-gather(bf16[1,256,128]{2,1,0:T(8,128)(2,1)} %param.14), channel_id=2, replica_groups=mesh['rep'=4,'blk'=8] {'rep'}, dimensions={1}, use_global_device_ids=true | all-gather | bytes 327680 | tf_op jit(solution)/shard_map/all_gather | solution.py:107
  23.2 3.2 collective-permute-done
  28.6 8.9 %collective-permute-done.1 = bf16[1024,128]{1,0:T(8,128)(2,1)S(1)} collective-permute-done((bf16[1024,128]{1,0:T(8,128)(2,1)S(1)}, bf16[1024,128]{1,0:T(8,128)(2,1)S(1)}, u32[]{:S(2)}, u32[]{:S(2)}) %collective-permute-start.1) | collective-permute-done | bytes 262176 | tf_op jit(solution)/shard_map/ppermute | solution.py:12
  43.0 2.2 collective-permute-done.2
  51.6 23.0 %reduce-scatter.4.cloned.1.call-done = f32[256,128]{1,0:T(8,128)} async-done(((f32[1024,128]{1,0:T(8,128)}), f32[256,128]{1,0:T(8,128)}) %reduce-scatter.4.cloned.1.call-update) | async-done | bytes 131088 | tf_op jit(solution)/shard_map/reduce_scatter | solution.py:108
  74.5 1.8 fusion.32
  76.3 10.0 %all_gather.10 = bf16[1024,256]{1,0:T(8,128)(2,1)S(1)} all-gather(bf16[256,256]{1,0:T(8,128)(2,1)S(1)} %get-tuple-element.36), channel_id=1, replica_groups=mesh['rep'=4,'blk'=8] {'rep'}, dimensions={0}, use_global_device_ids=true | all-gather | bytes 655360 | tf_op jit(solution)/shard_map/all_gather | solution.py:114
  87.8 12.2 %collective-permute-done.3 = bf16[1024,256]{1,0:T(8,128)(2,1)S(1)} collective-permute-done((bf16[1024,256]{1,0:T(8,128)(2,1)S(1)}, bf16[1024,256]{1,0:T(8,128)(2,1)S(1)}, u32[]{:S(2)}, u32[]{:S(2)}) %collective-permute-start.3) | collective-permute-done | bytes 524320 | tf_op jit(solution)/shard_map/ppermute | solution.py:12
  100.3 21.7 %collective-permute-done.4 = bf16[1024,256]{1,0:T(8,128)(2,1)S(1)} collective-permute-done((bf16[1024,256]{1,0:T(8,128)(2,1)S(1)}, bf16[1024,256]{1,0:T(8,128)(2,1)S(1)}, u32[]{:S(2)}, u32[]{:S(2)}) %collective-permute-start.4) | collective-permute-done | bytes 524320 | tf_op jit(solution)/shard_map/ppermute | solution.py:12
  122.9 2.6 gather_fusion.2
  125.5 1.8 multiply_bitcast_fusion.3
  127.4 1.9 copy.25
  129.3 3.5 scatter_fusion.2
  133.6 1.7 gather_fusion.3
  135.3 1.9 multiply_bitcast_fusion.2
  137.2 2.9 copy.27
  140.2 3.5 scatter_fusion.3
  145.0 27.2 %reduce-scatter.6.cloned.1.call-done = f32[256,256]{1,0:T(8,128)} async-done(((f32[1024,256]{1,0:T(8,128)}), f32[256,256]{1,0:T(8,128)}) %reduce-scatter.6.cloned.1.call-update) | async-done | bytes 262160 | tf_op jit(solution)/shard_map/reduce_scatter | solution.py:115
  173.8 10.1 %all_gather.11 = bf16[1024,256]{1,0:T(8,128)(2,1)S(1)} all-gather(bf16[256,256]{1,0:T(8,128)(2,1)S(1)} %convolution_convert_fusion), channel_id=1, replica_groups=mesh['rep'=4,'blk'=8] {'rep'}, dimensions={0}, use_global_device_ids=true | all-gather | bytes 655360 | tf_op jit(solution)/shard_map/all_gather | solution.py:123
  184.5 1.9 multiply_bitcast_fusion.1
  186.5 2.9 copy.29
  189.5 3.5 scatter_fusion.4
  195.2 1.9 multiply_bitcast_fusion
  197.2 1.9 copy.31
  199.2 2.2 scatter_fusion.5
  202.9 2.6 collective-permute-start.7
  205.5 12.2 %collective-permute-done.7 = bf16[1024,256]{1,0:T(8,128)(2,1)S(1)} collective-permute-done((bf16[1024,256]{1,0:T(8,128)(2,1)S(1)}, bf16[1024,256]{1,0:T(8,128)(2,1)S(1)}, u32[]{:S(2)}, u32[]{:S(2)}) %collective-permute-start.7) | collective-permute-done | bytes 524320 | tf_op jit(solution)/shard_map/ppermute | solution.py:12
  220.0 25.3 %collective-permute-done.8 = bf16[1024,256]{1,0:T(8,128)(2,1)S(1)} collective-permute-done((bf16[1024,256]{1,0:T(8,128)(2,1)S(1)}, bf16[1024,256]{1,0:T(8,128)(2,1)S(1)}, u32[]{:S(2)}, u32[]{:S(2)}) %collective-permute-start.8) | collective-permute-done | bytes 524320 | tf_op jit(solution)/shard_map/ppermute | solution.py:12
  245.3 2.2 select_convert_fusion
  248.5 22.8 %reduce-scatter.8.cloned.1.call-done = bf16[256,256]{1,0:T(8,128)(2,1)} async-done(((bf16[1024,256]{1,0:T(8,128)(2,1)}), bf16[256,256]{1,0:T(8,128)(2,1)}) %reduce-scatter.8.cloned.1.call-update) | async-done | bytes 131088 | tf_op jit(solution)/shard_map/reduce_scatter | solution.py:147
  271.4 1.9 fusion.41
  274.1 130.1 %all-reduce.3.cloned.1.call-done = (f32[128,256]{1,0:T(8,128)}, f32[256,172]{0,1:T(8,128)}) async-done(((f32[128,256]{1,0:T(8,128)}, f32[256,172]{0,1:T(8,128)}), (f32[128,256]{1,0:T(8,128)}, f32[256,172]{0,1:T(8,128)})) %all-reduce.3.cloned.1.call-update) | async-done | bytes 307216 | tf_op jit(solution)/shard_map/psum | solution.py:152
  (83 shorter events, 37.3 us)
Async XLA Ops:
  7.2 165.1 %copy-start = (bf16[256,172]{0,1:T(8,128)(2,1)S(1)}, bf16[256,172]{0,1:T(8,128)(2,1)}, u32[]{:S(2)}) copy-start(bf16[256,172]{0,1:T(8,128)(2,1)} %param.22) | copy-start | bytes 264196
  7.2 31.1 %copy-start.1 = (bf16[1,1,2,16,128,128]{5,4,3,2,1,0:T(8,128)(2,1)S(1)}, bf16[1,1,2,16,128,128]{5,4,3,2,1,0:T(8,128)(2,1)}, u32[]{:S(2)}) copy-start(bf16[1,1,2,16,128,128]{5,4,3,2,1,0:T(8,128)(2,1)} %param.18) | copy-start | bytes 3145732
  7.2 67.3 %reduce-scatter.4.cloned.1.call-start = ((), (), s32[]{:S(2)}) async-start(), calls=%async_computation.3 | async-start | bytes 655360 | tf_op jit(solution)/shard_map/reduce_scatter | solution.py:108
  18.1 8.4 %collective-permute-start = (bf16[1024,128]{1,0:T(8,128)(2,1)S(1)}, bf16[1024,128]{1,0:T(8,128)(2,1)S(1)}, u32[]{:S(2)}, u32[]{:S(2)}) collective-permute-start(bf16[1024,128]{1,0:T(8,128)(2,1)S(1)} %bitcast.125), channel_id=1, source_target_pairs={{0,2},{1,3},{2,4},{3,5},{4,6},{5,7},{6,0},{7,1},{8,10},{9,11},{10,... | collective-permute-start | bytes 786440 | tf_op jit(solution)/shard_map/ppermute | solution.py:12
  26.5 11.0 %collective-permute-start.1 = (bf16[1024,128]{1,0:T(8,128)(2,1)S(1)}, bf16[1024,128]{1,0:T(8,128)(2,1)S(1)}, u32[]{:S(2)}, u32[]{:S(2)}) collective-permute-start(bf16[1024,128]{1,0:T(8,128)(2,1)S(1)} %broadcast_select_fusion.2), channel_id=1, source_target_pairs={{0,4},{1,5},{2,6},{3,7},{4,0},{5,1},{6,2},{7,3},{8,12},{9,13},{10,... | collective-permute-start | bytes 786440 | tf_op jit(solution)/shard_map/ppermute | solution.py:12
  37.5 7.6 %collective-permute-start.2 = (bf16[1024,128]{1,0:T(8,128)(2,1)S(1)}, bf16[1024,128]{1,0:T(8,128)(2,1)S(1)}, u32[]{:S(2)}, u32[]{:S(2)}) collective-permute-start(bf16[1024,128]{1,0:T(8,128)(2,1)S(1)} %broadcast_select_fusion.3), channel_id=1, source_target_pairs={{0,1},{1,2},{2,3},{3,4},{4,5},{5,6},{6,7},{7,0},{8,9},{9,10},{10,1... | collective-permute-start | bytes 786440 | tf_op jit(solution)/shard_map/ppermute | solution.py:12
  49.0 2.6 copy-start.4
  49.0 25.5 %copy-start.7 = (bf16[128,256]{1,0:T(8,128)(2,1)S(1)}, bf16[128,256]{1,0:T(8,128)(2,1)}, u32[]{:S(2)}) copy-start(bf16[128,256]{1,0:T(8,128)(2,1)} %param.21) | copy-start | bytes 196612
  51.5 120.7 %reduce-scatter.6.cloned.1.call-start = ((), (), s32[]{:S(2)}) async-start(), calls=%async_computation.4 | async-start | bytes 1310720 | tf_op jit(solution)/shard_map/reduce_scatter | solution.py:115
  86.3 13.7 %collective-permute-start.3 = (bf16[1024,256]{1,0:T(8,128)(2,1)S(1)}, bf16[1024,256]{1,0:T(8,128)(2,1)S(1)}, u32[]{:S(2)}, u32[]{:S(2)}) collective-permute-start(bf16[1024,256]{1,0:T(8,128)(2,1)S(1)} %all_gather.10), channel_id=1, source_target_pairs={{0,2},{1,3},{2,4},{3,5},{4,6},{5,7},{6,0},{7,1},{8,10},{9,11},{10,... | collective-permute-start | bytes 1572872 | tf_op jit(solution)/shard_map/ppermute | solution.py:12
  100.0 22.0 %collective-permute-start.4 = (bf16[1024,256]{1,0:T(8,128)(2,1)S(1)}, bf16[1024,256]{1,0:T(8,128)(2,1)S(1)}, u32[]{:S(2)}, u32[]{:S(2)}) collective-permute-start(bf16[1024,256]{1,0:T(8,128)(2,1)S(1)} %broadcast_select_fusion), channel_id=1, source_target_pairs={{0,4},{1,5},{2,6},{3,7},{4,0},{5,1},{6,2},{7,3},{8,12},{9,13},{10,... | collective-permute-start | bytes 1572872 | tf_op jit(solution)/shard_map/ppermute | solution.py:12
  122.9 10.7 %collective-permute-start.5 = (bf16[1024,256]{1,0:T(8,128)(2,1)}, bf16[1024,256]{1,0:T(8,128)(2,1)}, u32[]{:S(2)}, u32[]{:S(2)}) collective-permute-start(bf16[1024,256]{1,0:T(8,128)(2,1)} %broadcast_select_fusion.1), channel_id=1, source_target_pairs={{0,1},{1,2},{2,3},{3,4},{4,5},{5,6},{6,7},{7,0},{8,9},{9,10},{10,1... | collective-permute-start | bytes 1572872 | tf_op jit(solution)/shard_map/ppermute | solution.py:12
  143.7 1.3 copy-start.5
  143.7 28.5 %copy-start.3 = (f32[172]{0:T(256)S(1)}, f32[172]{0:T(256)}, u32[]{:S(2)}) copy-start(f32[172]{0:T(256)} %param.23) | copy-start | bytes 2068
  143.7 29.8 %copy-start.8 = (s32[1,256]{1,0:T(1,128)S(1)}, s32[1,256]{1,0:T(1,128)}, u32[]{:S(2)}) copy-start(s32[1,256]{1,0:T(1,128)} %param.16) | copy-start | bytes 3076
  144.9 126.4 %reduce-scatter.8.cloned.1.call-start = ((), (), s32[]{:S(2)}) async-start(), calls=%async_computation.5 | async-start | bytes 655360 | tf_op jit(solution)/shard_map/reduce_scatter | solution.py:147
  193.8 7.8 %collective-permute-start.6 = (bf16[1024,256]{1,0:T(8,128)(2,1)}, bf16[1024,256]{1,0:T(8,128)(2,1)}, u32[]{:S(2)}, u32[]{:S(2)}) collective-permute-start(bf16[1024,256]{1,0:T(8,128)(2,1)} %bitcast.28), channel_id=1, source_target_pairs={{0,7},{1,0},{2,1},{3,2},{4,3},{5,4},{6,5},{7,6},{8,15},{9,8},{10,9... | collective-permute-start | bytes 1572872 | tf_op jit(solution)/shard_map/ppermute | solution.py:12
  202.9 14.8 %collective-permute-start.7 = (bf16[1024,256]{1,0:T(8,128)(2,1)S(1)}, bf16[1024,256]{1,0:T(8,128)(2,1)S(1)}, u32[]{:S(2)}, u32[]{:S(2)}) collective-permute-start(bf16[1024,256]{1,0:T(8,128)(2,1)S(1)} %fusion.25), channel_id=1, source_target_pairs={{0,6},{1,7},{2,0},{3,1},{4,2},{5,3},{6,4},{7,5},{8,14},{9,15},{10,... | collective-permute-start | bytes 1572872 | tf_op jit(solution)/shard_map/ppermute | solution.py:12
  219.0 28.6 %copy-start.2 = (f32[256,256]{1,0:T(8,128)S(1)}, f32[256,256]{1,0:T(8,128)}, u32[]{:S(2)}) copy-start(f32[256,256]{1,0:T(8,128)} %reduce-scatter.6.cloned.1.call-done) | copy-start | bytes 786436
  219.0 52.3 %copy-start.6 = (f32[256,128]{1,0:T(8,128)S(1)}, f32[256,128]{1,0:T(8,128)}, u32[]{:S(2)}) copy-start(f32[256,128]{1,0:T(8,128)} %reduce-scatter.4.cloned.1.call-done) | copy-start | bytes 393220
  219.0 52.3 %copy-start.9 = (f32[256,256]{1,0:T(8,128)S(1)}, f32[256,256]{1,0:T(8,128)}, u32[]{:S(2)}) copy-start(f32[256,256]{1,0:T(8,128)} %get-tuple-element.37) | copy-start | bytes 786436
  219.1 26.3 %collective-permute-start.8 = (bf16[1024,256]{1,0:T(8,128)(2,1)S(1)}, bf16[1024,256]{1,0:T(8,128)(2,1)S(1)}, u32[]{:S(2)}, u32[]{:S(2)}) collective-permute-start(bf16[1024,256]{1,0:T(8,128)(2,1)S(1)} %fusion.10), channel_id=1, source_target_pairs={{0,4},{1,5},{2,6},{3,7},{4,0},{5,1},{6,2},{7,3},{8,12},{9,13},{10,... | collective-permute-start | bytes 1572872 | tf_op jit(solution)/shard_map/ppermute | solution.py:12
  247.6 156.6 %all-reduce.3.cloned.1.call-start = ((), (), s32[]{:S(2)}) async-start(), calls=%async_computation.6 | async-start | bytes 622592 | tf_op jit(solution)/shard_map/psum | solution.py:152
Sparse Core Ops, SparseCore 0:
  51.6 22.8 reduce-scatter.3
  145.0 27.1 reduce-scatter.5
  247.7 23.5 reduce-scatter.7
  278.1 126.0 all-reduce.2
where the time goes:
time: 415 us; the launch traced here: 414 us
  waiting for transfers between devices  290 us (70%)
  blocking collectives  31 us (7%)
  other arithmetic  28.2 us (7%)
  local copies, waits for them, and re-layouts  25.3 us (6%)
  matrix products  16.7 us (4%)
  between operations  14.2 us (3%)
  starting transfers between devices  8.65 us (2%)
    psum x1, waiting for transfers between devices, on_device(): grad_in = lax.psum(in_terms, ('rep', 'blk'))  130 us
    ppermute x9, waiting for transfers between devices, from_behind(): return lax.ppermute(value, axis, pairs)  86.7 us
    reduce_scatter x1, waiting for transfers between devices, on_device(): lax.psum_scatter(spread(hidden_block), 'rep', scatter_dimension=0, tiled=...  27.2 us
    reduce_scatter x1, waiting for transfers between devices, on_device(): lax.psum_scatter(spread(feature_block), 'rep', scatter_dimension=0, tiled...  23 us
    reduce_scatter x1, waiting for transfers between devices, on_device(): lax.psum_scatter(running_sum.astype(jnp.bfloat16), 'rep', scatter_dimensi...  22.8 us
    scatter-add x6, other arithmetic, place_rows(): jnp.zeros((tile_side, tile_edge, feat_width), jnp.float32).at[target]  15.9 us
    mul x6, local copies, waits for them, and re-layouts, place_rows(): masked = products * live_slots.astype(jnp.float32)[:, None, None]  12.7 us
    all_gather x1, blocking collectives, on_device(): feature_block = lax.all_gather(features[0], 'rep', axis=0, tiled=True)  10.9 us
  transfers between devices with their start and end apart: 13, of which 13 were waited for; matrix products, arithmetic and copies ran while one was open for 7% of the time, Pallas kernels for 0%

commit v1 on v0

v1 whole, which is shorter than its diff:
```python
import functools
import math

import jax
import jax.numpy as jnp
from jax import lax
from jax.experimental import pallas as pl
from jax.experimental.pallas import tpu as pltpu
from jax.sharding import PartitionSpec as P


def keep_mask(id_values, unit_count):
    columns = jnp.arange(unit_count, dtype=jnp.int32)
    mixed = id_values[:, None] * 73244475 + columns[None, :] * 19349663 + 12345
    mixed = mixed ^ jnp.right_shift(mixed, 15)
    mixed = mixed * 40503
    mixed = mixed ^ jnp.right_shift(mixed, 13)
    return jnp.bitwise_and(mixed, 3) != 0


def dense_kernel(per_rep, tile_side, rep_ref, count_ref, place_ref, tiles_ref, dense_ref):
    section = pl.program_id(0)
    edge = tiles_ref.shape[-1]
    dense_ref[...] = jnp.zeros_like(dense_ref)
    rep_index = rep_ref[0]

    def put(slot, carried):
        place = place_ref[section, slot]
        row = place // tile_side
        column = place % tile_side
        row = ((row // per_rep) ^ rep_index) * per_rep + row % per_rep
        column = ((column // per_rep) ^ rep_index) * per_rep + column % per_rep
        dense_ref[
            pl.ds(pl.multiple_of(row * edge, edge), edge),
            pl.ds(pl.multiple_of(column * edge, edge), edge),
        ] = tiles_ref[0, slot]
        return carried

    lax.fori_loop(0, count_ref[section], put, 0)


def build_dense(tiles, place, count, rep_index, own_rows, group_rows):
    sections, slots, edge, _ = tiles.shape
    body = functools.partial(dense_kernel, own_rows // edge, group_rows // edge)
    smem = pl.BlockSpec(memory_space=pltpu.SMEM)
    return pl.pallas_call(
        body,
        grid=(sections,),
        in_specs=[
            smem,
            smem,
            smem,
            pl.BlockSpec((1, slots, edge, edge), lambda s: (s, 0, 0, 0)),
        ],
        out_specs=pl.BlockSpec((group_rows, group_rows), lambda s: (0, s)),
        out_shape=jax.ShapeDtypeStruct((group_rows, sections * group_rows), tiles.dtype),
        compiler_params=pltpu.CompilerParams(vmem_limit_bytes=40 * 1024 * 1024),
        cost_estimate=pl.CostEstimate(
            flops=0, bytes_accessed=2 * sections * group_rows * group_rows, transcendentals=0
        ),
        name="dense_tiles",
    )(rep_index.reshape(1), count, place, tiles)


def on_device(
    features,
    node_ids,
    labels,
    train_mask,
    tile_values,
    tile_place,
    tile_count,
    weight_in,
    weight_out,
    class_bias,
):
    own_rows = features.shape[1]
    reps = lax.axis_size("rep")
    blks = lax.axis_size("blk")
    rep_index = lax.axis_index("rep")
    sections = tile_values.shape[2]
    group_rows = own_rows * reps
    hidden_width = weight_in.shape[1]
    scale = 1.0 / math.sqrt(group_rows * blks)
    f32 = jnp.float32
    bf16 = jnp.bfloat16

    def swap(value, delta):
        if delta == 0:
            return value
        return lax.ppermute(value, "rep", [(r, r ^ delta) for r in range(reps)])

    def to_columns(value):
        pieces = []
        for section in range(sections):
            for delta in range(reps):
                pairs = []
                for r in range(reps):
                    for c in range(blks):
                        target = r ^ delta
                        row_block = (c + sections * target + section) % blks
                        pairs.append((r * blks + c, target * blks + row_block))
                pieces.append(lax.ppermute(value, ("rep", "blk"), pairs))
        return jnp.concatenate(pieces, axis=0)

    def shift(value, steps):
        return lax.ppermute(value, "blk", [(c, (c + steps) % blks) for c in range(blks)])

    def scatter_rows(partial):
        chunks = partial.reshape(reps, own_rows, partial.shape[1])
        total = chunks[0]
        for delta in range(1, reps):
            total = total + swap(chunks[delta], delta)
        return total

    def sum_everywhere(value):
        rows, width = value.shape
        chunk = rows // reps
        mine = lax.dynamic_slice_in_dim(value, rep_index * chunk, chunk, 0)
        total = mine
        for delta in range(1, reps):
            other = lax.dynamic_slice_in_dim(value, (rep_index ^ delta) * chunk, chunk, 0)
            total = total + swap(other, delta)
        part = total
        for steps in range(1, blks):
            total = total + shift(part, steps)
        whole = jnp.zeros((rows, width), value.dtype)
        for delta in range(reps):
            whole = lax.dynamic_update_slice_in_dim(
                whole, swap(total, delta), (rep_index ^ delta) * chunk, 0
            )
        return whole

    dense = build_dense(
        tile_values[0, 0], tile_place[0, 0], tile_count[0, 0], rep_index, own_rows, group_rows
    )
    feature_columns = to_columns(features[0])
    id_columns = to_columns(node_ids[0])
    first = jnp.dot(dense, feature_columns, preferred_element_type=f32)
    z_input = scatter_rows(first).astype(bf16)
    kept = jnp.where(keep_mask(id_columns, hidden_width), f32(4.0 / 3.0), f32(0.0))
    z_columns = to_columns(z_input)
    pre_act = jnp.dot(z_columns, weight_in, preferred_element_type=f32)
    dropped = (jnp.maximum(pre_act, 0.0) * kept).astype(bf16)
    factor = kept * (pre_act > 0)
    second = jnp.dot(dense, dropped, preferred_element_type=f32)
    z_output = scatter_rows(second).astype(bf16)
    logits = jnp.dot(z_output, weight_out, preferred_element_type=f32) + class_bias
    likelihood = jax.nn.softmax(logits, axis=-1)
    onehot = labels[0][:, None] == jnp.arange(logits.shape[-1], dtype=jnp.int32)[None, :]
    slope = (
        (likelihood - onehot.astype(f32)) * train_mask[0][:, None].astype(f32) * scale
    ).astype(bf16)
    grad_rows = jnp.einsum(
        "nc,hc->nh", slope, weight_out, preferred_element_type=f32
    ).astype(bf16)
    grad_block = jnp.concatenate([swap(grad_rows, delta) for delta in range(reps)], axis=0)
    out_terms = jnp.einsum("nh,nc->hc", z_output, slope, preferred_element_type=f32)
    grad_out = sum_everywhere(out_terms)
    back = jnp.einsum("nc,nh->ch", dense, grad_block, preferred_element_type=f32)
    pre_slope = (back * factor).astype(bf16)
    in_terms = jnp.einsum("nf,nh->fh", z_columns, pre_slope, preferred_element_type=f32)
    grad_in = sum_everywhere(in_terms)
    return (logits[None], grad_in, grad_out)


def solution(mesh):
    placed = (
        P("blk", "rep", None),
        P("blk", "rep"),
        P("blk", "rep"),
        P("blk", "rep"),
        P("blk", "rep", None, None, None, None),
        P("blk", "rep", None, None),
        P("blk", "rep", None),
        P(),
        P(),
        P(),
    )
    return jax.shard_map(
        on_device,
        mesh=mesh,
        in_specs=placed,
        out_specs=(P("blk", "rep", None), P(), P()),
        check_vma=False,
    )
```

time: 415 us -> 166 us (0.40)
  waiting for transfers between devices: 290 us -> 49 us
  starting transfers between devices: 8.65 us -> 94.2 us
  blocking collectives: 31 us -> 0 us
  other arithmetic: 28.2 us -> 1.4 us
  local copies, waits for them, and re-layouts: 25.3 us -> 8.65 us
  between operations: 14.2 us -> 1.15 us
  matrix products: 16.7 us -> 8.54 us
    psum x1 -> x0, waiting for transfers between devices: 130 us -> none  [on_device(): grad_in = lax.psum(in_terms, ('rep', 'blk'))]
    ppermute x9 -> x59, starting transfers between devices: 8.48 us -> 94.2 us  [the longest x24 51.3 us: to_columns(): pieces.append(lax.ppermute(value, ('rep', 'blk'), pairs))]
    reduce_scatter x3 -> x0, waiting for transfers between devices: 73 us -> none  [the longest x1 27.2 us: on_device(): lax.psum_scatter(spread(hidden_block), 'rep', scatter_dimension=0, tiled=...]
    ppermute x9 -> x59, waiting for transfers between devices: 86.7 us -> 49 us  [the longest x21 25.3 us: swap(): return lax.ppermute(value, 'rep', [(r, r ^ delta) for r in range(reps)])]
    all_gather x3 -> x0, blocking collectives: 31 us -> none  [the longest x1 10.9 us: on_device(): feature_block = lax.all_gather(features[0], 'rep', axis=0, tiled=True)]
    scatter-add x6 -> x0, other arithmetic: 15.9 us -> none  [place_rows(): jnp.zeros((tile_side, tile_edge, feat_width), jnp.float32).at[target]]
    mul x6 -> x0, local copies, waits for them, and re-layouts: 12.7 us -> none  [place_rows(): masked = products * live_slots.astype(jnp.float32)[:, None, None]]
    dot_general x11 -> x7, matrix products: 16.7 us -> 8.54 us  [the longest x1 4.63 us: on_device(): jnp.einsum('nf,nh->fh', z_columns, pre_slope, preferred_element_type=f32)]
  transfers between devices with their start and end apart: 13 -> 59, of which waited for: 13 -> 21; matrix products, arithmetic and copies ran while one was open for 7% -> 6% of each run, Pallas kernels for 0% -> 1%
where the time goes in v1:
time: 166 us; the launch traced here: 165 us
  starting transfers between devices  94.2 us (57%)
  waiting for transfers between devices  49 us (30%)
  local copies, waits for them, and re-layouts  8.65 us (5%)
  matrix products  8.54 us (5%)
  Pallas kernels  2.12 us (1%)
    ppermute x24, starting transfers between devices, to_columns(): pieces.append(lax.ppermute(value, ('rep', 'blk'), pairs))  51.3 us
    ppermute x21, waiting for transfers between devices, swap(): return lax.ppermute(value, 'rep', [(r, r ^ delta) for r in range(reps)])  25.3 us
    ppermute x21, starting transfers between devices, swap(): return lax.ppermute(value, 'rep', [(r, r ^ delta) for r in range(reps)])  24.9 us
    ppermute x24, waiting for transfers between devices, to_columns(): pieces.append(lax.ppermute(value, ('rep', 'blk'), pairs))  19.9 us
    ppermute x14, starting transfers between devices, shift(): lax.ppermute(value, 'blk', [(c, (c + steps) % blks) for c in range(blks)])  18.1 us
    dot_general x1, matrix products, on_device(): jnp.einsum('nf,nh->fh', z_columns, pre_slope, preferred_element_type=f32)  4.63 us
    unnamed x52, local copies, waits for them, and re-layouts  4.32 us
    ppermute x14, waiting for transfers between devices, shift(): lax.ppermute(value, 'blk', [(c, (c + steps) % blks) for c in range(blks)])  3.82 us
  transfers between devices with their start and end apart: 59, of which 21 were waited for; matrix products, arithmetic and copies ran while one was open for 6% of the time, Pallas kernels for 1%

profile of v1, /device:TPU:0, one launch (start us, length us, event | category | flops | bytes accessed | tf_op | source)
XLA Modules:
  0.0 165.1 jit_solution(3915872217055943262)
XLA Ops:
  2.3 6.0 %collective-permute-start.1 = (bf16[256,128]{1,0:T(8,128)(2,1)}, bf16[256,128]{1,0:T(8,128)(2,1)S(1)}, u32[]{:S(2)}, u32[]{:S(2)}) collective-permute-start(bf16[256,128]{1,0:T(8,128)(2,1)} %bitcast.27), channel_id=1, source_target_pairs={{0,10},{1,11},{2,12},{3,13},{4,14},{5,15},{6,8},{7,9},{8,0},{9,1},... | collective-permute-start | bytes 196616 | tf_op jit(solution)/shard_map/ppermute | solution.py:103
  9.6 3.0 %collective-permute-start.3 = (bf16[256,128]{1,0:T(8,128)(2,1)}, bf16[256,128]{1,0:T(8,128)(2,1)S(1)}, u32[]{:S(2)}, u32[]{:S(2)}) collective-permute-start(bf16[256,128]{1,0:T(8,128)(2,1)} %bitcast.29), channel_id=1, source_target_pairs={{0,30},{1,31},{2,24},{3,25},{4,26},{5,27},{6,28},{7,29},{8,20},{9,... | collective-permute-start | bytes 196616 | tf_op jit(solution)/shard_map/ppermute | solution.py:103
  16.5 2.1 %dense_tiles.1 = bf16[1024,2048]{1,0:T(8,128)(2,1)S(1)} custom-call(s32[1]{0:T(128)} %bitcast.rep_ref, s32[2]{0:T(128)S(1)} %bitcast.22, s32[2,16]{1,0:T(2,128)S(1)} %bitcast.21, bf16[2,16,128,128]{3,2,1,0:T(8,128)(2,1)S(1)} %bitcast.20), custom_call_target="tpu_custom_call" | custom-call | bytes 4194304 | tf_op jit(solution)/shard_map/dense_tiles/pallas_call | solution.py:46
  18.6 1.9 %collective-permute-start.20 = (s32[256]{0:T(256)S(1)}, s32[256]{0:T(256)S(1)}, u32[]{:S(2)}, u32[]{:S(2)}) collective-permute-start(s32[256]{0:T(256)S(1)} %bitcast.35), channel_id=1, source_target_pairs={{0,10},{1,11},{2,12},{3,13},{4,14},{5,15},{6,8},{7,9},{8,0},{9,1},... | collective-permute-start | bytes 3080 | tf_op jit(solution)/shard_map/ppermute | solution.py:103
  20.5 1.8 %collective-permute-done.20 = s32[256]{0:T(256)S(1)} collective-permute-done((s32[256]{0:T(256)S(1)}, s32[256]{0:T(256)S(1)}, u32[]{:S(2)}, u32[]{:S(2)}) %collective-permute-start.20) | collective-permute-done | bytes 1056 | tf_op jit(solution)/shard_map/ppermute | solution.py:103
  22.3 4.8 %collective-permute-start.21 = (s32[256]{0:T(256)S(1)}, s32[256]{0:T(256)S(1)}, u32[]{:S(2)}, u32[]{:S(2)}) collective-permute-start(s32[256]{0:T(256)S(1)} %bitcast.36), channel_id=1, source_target_pairs={{0,20},{1,21},{2,22},{3,23},{4,16},{5,17},{6,18},{7,19},{8,30},{9,... | collective-permute-start | bytes 3080 | tf_op jit(solution)/shard_map/ppermute | solution.py:103
  28.7 7.7 %collective-permute-start.22 = (s32[256]{0:T(256)S(1)}, s32[256]{0:T(256)S(1)}, u32[]{:S(2)}, u32[]{:S(2)}) collective-permute-start(s32[256]{0:T(256)S(1)} %bitcast.37), channel_id=1, source_target_pairs={{0,30},{1,31},{2,24},{3,25},{4,26},{5,27},{6,28},{7,29},{8,20},{9,... | collective-permute-start | bytes 3080 | tf_op jit(solution)/shard_map/ppermute | solution.py:103
  37.7 4.8 %collective-permute-done.23 = s32[256]{0:T(256)S(1)} collective-permute-done((s32[256]{0:T(256)S(1)}, s32[256]{0:T(256)S(1)}, u32[]{:S(2)}, u32[]{:S(2)}) %collective-permute-start.23) | collective-permute-done | bytes 1056 | tf_op jit(solution)/shard_map/ppermute | solution.py:103
  42.7 5.5 %collective-permute-done.24 = s32[256]{0:T(256)S(1)} collective-permute-done((s32[256]{0:T(256)S(1)}, s32[256]{0:T(256)S(1)}, u32[]{:S(2)}, u32[]{:S(2)}) %collective-permute-start.24) | collective-permute-done | bytes 1056 | tf_op jit(solution)/shard_map/ppermute | solution.py:103
  49.2 2.2 %collective-permute-start.7 = (bf16[256,128]{1,0:T(8,128)(2,1)S(1)}, bf16[256,128]{1,0:T(8,128)(2,1)S(1)}, u32[]{:S(2)}, u32[]{:S(2)}) collective-permute-start(bf16[256,128]{1,0:T(8,128)(2,1)S(1)} %bitcast.33), channel_id=1, source_target_pairs={{0,31},{1,24},{2,25},{3,26},{4,27},{5,28},{6,29},{7,30},{8,21},{9,... | collective-permute-start | bytes 196616 | tf_op jit(solution)/shard_map/ppermute | solution.py:103
  51.4 3.6 %collective-permute-start.25 = (s32[256]{0:T(256)S(1)}, s32[256]{0:T(256)S(1)}, u32[]{:S(2)}, u32[]{:S(2)}) collective-permute-start(s32[256]{0:T(256)S(1)} %bitcast.40), channel_id=1, source_target_pairs={{0,21},{1,22},{2,23},{3,16},{4,17},{5,18},{6,19},{7,20},{8,31},{9,... | collective-permute-start | bytes 3080 | tf_op jit(solution)/shard_map/ppermute | solution.py:103
  55.0 2.5 %collective-permute-start.26 = (s32[256]{0:T(256)S(1)}, s32[256]{0:T(256)S(1)}, u32[]{:S(2)}, u32[]{:S(2)}) collective-permute-start(s32[256]{0:T(256)S(1)} %bitcast.41), channel_id=1, source_target_pairs={{0,31},{1,24},{2,25},{3,26},{4,27},{5,28},{6,29},{7,30},{8,21},{9,... | collective-permute-start | bytes 3080 | tf_op jit(solution)/shard_map/ppermute | solution.py:103
  60.2 2.3 %collective-permute-start.9 = (f32[256,128]{1,0:T(8,128)S(1)}, f32[256,128]{1,0:T(8,128)S(1)}, u32[]{:S(2)}, u32[]{:S(2)}) collective-permute-start(f32[256,128]{1,0:T(8,128)S(1)} %get-tuple-element.13), channel_id=1, source_target_pairs={{0,16},{8,24},{16,0},{24,8},{1,17},{9,25},{17,1},{25,9},{2,18},{10... | collective-permute-start | bytes 393224 | tf_op jit(solution)/shard_map/ppermute | solution.py:91
  62.5 3.7 %collective-permute-done.10 = f32[256,128]{1,0:T(8,128)S(1)} collective-permute-done((f32[256,128]{1,0:T(8,128)S(1)}, f32[256,128]{1,0:T(8,128)S(1)}, u32[]{:S(2)}, u32[]{:S(2)}) %collective-permute-start.10) | collective-permute-done | bytes 131104 | tf_op jit(solution)/shard_map/ppermute | solution.py:91
  66.2 2.1 %collective-permute-done.9 = f32[256,128]{1,0:T(8,128)S(1)} collective-permute-done((f32[256,128]{1,0:T(8,128)S(1)}, f32[256,128]{1,0:T(8,128)S(1)}, u32[]{:S(2)}, u32[]{:S(2)}) %collective-permute-start.9) | collective-permute-done | bytes 131104 | tf_op jit(solution)/shard_map/ppermute | solution.py:91
  69.0 4.5 %collective-permute-start.12 = (bf16[256,128]{1,0:T(8,128)(2,1)S(1)}, bf16[256,128]{1,0:T(8,128)(2,1)S(1)}, u32[]{:S(2)}, u32[]{:S(2)}) collective-permute-start(bf16[256,128]{1,0:T(8,128)(2,1)S(1)} %fusion.34), channel_id=1, source_target_pairs={{0,10},{1,11},{2,12},{3,13},{4,14},{5,15},{6,8},{7,9},{8,0},{9,1},... | collective-permute-start | bytes 196616 | tf_op jit(solution)/shard_map/ppermute | solution.py:103
  74.8 2.9 %collective-permute-start.14 = (bf16[256,128]{1,0:T(8,128)(2,1)S(1)}, bf16[256,128]{1,0:T(8,128)(2,1)S(1)}, u32[]{:S(2)}, u32[]{:S(2)}) collective-permute-start(bf16[256,128]{1,0:T(8,128)(2,1)S(1)} %fusion.34), channel_id=1, source_target_pairs={{0,30},{1,31},{2,24},{3,25},{4,26},{5,27},{6,28},{7,29},{8,20},{9,... | collective-permute-start | bytes 196616 | tf_op jit(solution)/shard_map/ppermute | solution.py:103
  80.2 2.5 %collective-permute-start.18 = (bf16[256,128]{1,0:T(8,128)(2,1)S(1)}, bf16[256,128]{1,0:T(8,128)(2,1)S(1)}, u32[]{:S(2)}, u32[]{:S(2)}) collective-permute-start(bf16[256,128]{1,0:T(8,128)(2,1)S(1)} %fusion.34), channel_id=1, source_target_pairs={{0,31},{1,24},{2,25},{3,26},{4,27},{5,28},{6,29},{7,30},{8,21},{9,... | collective-permute-start | bytes 196616 | tf_op jit(solution)/shard_map/ppermute | solution.py:103
  84.1 1.9 %collective-permute-done.17 = bf16[256,128]{1,0:T(8,128)(2,1)S(1)} collective-permute-done((bf16[256,128]{1,0:T(8,128)(2,1)S(1)}, bf16[256,128]{1,0:T(8,128)(2,1)S(1)}, u32[]{:S(2)}, u32[]{:S(2)}) %collective-permute-start.17) | collective-permute-done | bytes 65568 | tf_op jit(solution)/shard_map/ppermute | solution.py:103
  92.0 2.1 %collective-permute-start.29 = (f32[256,256]{1,0:T(8,128)}, f32[256,256]{1,0:T(8,128)}, u32[]{:S(2)}, u32[]{:S(2)}) collective-permute-start(f32[256,256]{1,0:T(8,128)} %get-tuple-element.9), channel_id=1, source_target_pairs={{0,24},{8,16},{16,8},{24,0},{1,25},{9,17},{17,9},{25,1},{2,26},{10... | collective-permute-start | bytes 786440 | tf_op jit(solution)/shard_map/ppermute | solution.py:91
  94.1 5.8 %collective-permute-done.27 = f32[256,256]{1,0:T(8,128)S(1)} collective-permute-done((f32[256,256]{1,0:T(8,128)}, f32[256,256]{1,0:T(8,128)S(1)}, u32[]{:S(2)}, u32[]{:S(2)}) %collective-permute-start.27) | collective-permute-done | bytes 262176 | tf_op jit(solution)/shard_map/ppermute | solution.py:91
  99.8 6.6 %collective-permute-done.28 = f32[256,256]{1,0:T(8,128)} collective-permute-done((f32[256,256]{1,0:T(8,128)}, f32[256,256]{1,0:T(8,128)}, u32[]{:S(2)}, u32[]{:S(2)}) %collective-permute-start.28) | collective-permute-done | bytes 262176 | tf_op jit(solution)/shard_map/ppermute | solution.py:91
  109.6 2.2 %collective-permute-start.48 = (f32[64,172]{0,1:T(8,128)S(1)}, f32[64,172]{0,1:T(8,128)S(1)}, u32[]{:S(2)}, u32[]{:S(2)}) collective-permute-start(f32[64,172]{0,1:T(8,128)S(1)} %get-tuple-element.15), channel_id=1, source_target_pairs={{0,24},{8,16},{16,8},{24,0},{1,25},{9,17},{17,9},{25,1},{2,26},{10... | collective-permute-start | bytes 132104 | tf_op jit(solution)/shard_map/ppermute | solution.py:91
  113.4 2.2 %collective-permute-start.32 = (bf16[256,256]{1,0:T(8,128)(2,1)S(1)}, bf16[256,256]{1,0:T(8,128)(2,1)}, u32[]{:S(2)}, u32[]{:S(2)}) collective-permute-start(bf16[256,256]{1,0:T(8,128)(2,1)S(1)} %convolution_convert_fusion), channel_id=1, source_target_pairs={{0,24},{8,16},{16,8},{24,0},{1,25},{9,17},{17,9},{25,1},{2,26},{10... | collective-permute-start | bytes 393224 | tf_op jit(solution)/shard_map/ppermute | solution.py:91
  116.1 1.7 %collective-permute-start.50 = (f32[64,172]{0,1:T(8,128)S(1)}, f32[64,172]{0,1:T(8,128)S(1)}, u32[]{:S(2)}, u32[]{:S(2)}) collective-permute-start(f32[64,172]{0,1:T(8,128)S(1)} %add_add_fusion.1), channel_id=1, source_target_pairs={{0,2},{1,3},{2,4},{3,5},{4,6},{5,7},{6,0},{7,1},{8,10},{9,11},{10,... | collective-permute-start | bytes 132104 | tf_op jit(solution)/shard_map/ppermute | solution.py:107
  119.1 2.2 %collective-permute-done.31 = bf16[256,256]{1,0:T(8,128)(2,1)} collective-permute-done((bf16[256,256]{1,0:T(8,128)(2,1)S(1)}, bf16[256,256]{1,0:T(8,128)(2,1)}, u32[]{:S(2)}, u32[]{:S(2)}) %collective-permute-start.31) | collective-permute-done | bytes 131104 | tf_op jit(solution)/shard_map/ppermute | solution.py:91
  121.4 4.6 %fusion.5 = f32[128,256]{1,0:T(8,128)S(1)} fusion(bf16[2048,128]{1,0:T(8,128)(2,1)S(1)} %copy-done.6, bf16[1024,2048]{1,0:T(8,128)(2,1)} %copy-done.1, f32[2048,256]{1,0:T(8,128)S(1)} %fusion.58, s32[256]{0:T(256)S(1)} %iota_multiply_fusion, s32[2048]{0:T(1024)S(1)} %broadcast_multiply_fusion, bf16[256,256]{1,0:T(8,128)(2,1)} %collective-permute-done.32, ...), kind=kOutput, calls=%fused_computation.12 | convolution fusion | flops 1217396736 | bytes 7480320 | tf_op jit(solution)/shard_map/nf,nh->fh/dot_general | solution.py:162
  129.6 2.5 %collective-permute-start.52 = (f32[64,172]{0,1:T(8,128)S(1)}, f32[64,172]{0,1:T(8,128)S(1)}, u32[]{:S(2)}, u32[]{:S(2)}) collective-permute-start(f32[64,172]{0,1:T(8,128)S(1)} %add_add_fusion.1), channel_id=1, source_target_pairs={{0,4},{1,5},{2,6},{3,7},{4,0},{5,1},{6,2},{7,3},{8,12},{9,13},{10,... | collective-permute-start | bytes 132104 | tf_op jit(solution)/shard_map/ppermute | solution.py:107
  132.1 2.3 %collective-permute-start.53 = (f32[64,172]{0,1:T(8,128)S(1)}, f32[64,172]{0,1:T(8,128)S(1)}, u32[]{:S(2)}, u32[]{:S(2)}) collective-permute-start(f32[64,172]{0,1:T(8,128)S(1)} %add_add_fusion.1), channel_id=1, source_target_pairs={{0,5},{1,6},{2,7},{3,0},{4,1},{5,2},{6,3},{7,4},{8,13},{9,14},{10,... | collective-permute-start | bytes 132104 | tf_op jit(solution)/shard_map/ppermute | solution.py:107
  135.6 3.7 %collective-permute-done.51 = f32[64,172]{0,1:T(8,128)S(1)} collective-permute-done((f32[64,172]{0,1:T(8,128)S(1)}, f32[64,172]{0,1:T(8,128)S(1)}, u32[]{:S(2)}, u32[]{:S(2)}) %collective-permute-start.51) | collective-permute-done | bytes 44064 | tf_op jit(solution)/shard_map/ppermute | solution.py:107
  139.4 3.1 %collective-permute-start.37 = (f32[32,256]{1,0:T(8,128)S(1)}, f32[32,256]{1,0:T(8,128)S(1)}, u32[]{:S(2)}, u32[]{:S(2)}) collective-permute-start(f32[32,256]{1,0:T(8,128)S(1)} %add_add_fusion.3), channel_id=1, source_target_pairs={{0,2},{1,3},{2,4},{3,5},{4,6},{5,7},{6,0},{7,1},{8,10},{9,11},{10,... | collective-permute-start | bytes 98312 | tf_op jit(solution)/shard_map/ppermute | solution.py:107
  142.7 4.6 %collective-permute-start.39 = (f32[32,256]{1,0:T(8,128)S(1)}, f32[32,256]{1,0:T(8,128)S(1)}, u32[]{:S(2)}, u32[]{:S(2)}) collective-permute-start(f32[32,256]{1,0:T(8,128)S(1)} %add_add_fusion.3), channel_id=1, source_target_pairs={{0,4},{1,5},{2,6},{3,7},{4,0},{5,1},{6,2},{7,3},{8,12},{9,13},{10,... | collective-permute-start | bytes 98312 | tf_op jit(solution)/shard_map/ppermute | solution.py:107
  (173 shorter events, 54.9 us)
Async XLA Ops:
  0.6 47.6 %collective-permute-start = (bf16[256,128]{1,0:T(8,128)(2,1)}, bf16[256,128]{1,0:T(8,128)(2,1)S(1)}, u32[]{:S(2)}, u32[]{:S(2)}) collective-permute-start(bf16[256,128]{1,0:T(8,128)(2,1)} %bitcast.26), channel_id=1, source_target_pairs={{0,0},{1,1},{2,2},{3,3},{4,4},{5,5},{6,6},{7,7},{8,10},{9,11},{10,... | collective-permute-start | bytes 196616 | tf_op jit(solution)/shard_map/ppermute | solution.py:103
  2.3 46.0 %collective-permute-start.1 = (bf16[256,128]{1,0:T(8,128)(2,1)}, bf16[256,128]{1,0:T(8,128)(2,1)S(1)}, u32[]{:S(2)}, u32[]{:S(2)}) collective-permute-start(bf16[256,128]{1,0:T(8,128)(2,1)} %bitcast.27), channel_id=1, source_target_pairs={{0,10},{1,11},{2,12},{3,13},{4,14},{5,15},{6,8},{7,9},{8,0},{9,1},... | collective-permute-start | bytes 196616 | tf_op jit(solution)/shard_map/ppermute | solution.py:103
  8.3 40.9 %collective-permute-start.2 = (bf16[256,128]{1,0:T(8,128)(2,1)}, bf16[256,128]{1,0:T(8,128)(2,1)S(1)}, u32[]{:S(2)}, u32[]{:S(2)}) collective-permute-start(bf16[256,128]{1,0:T(8,128)(2,1)} %bitcast.28), channel_id=1, source_target_pairs={{0,20},{1,21},{2,22},{3,23},{4,16},{5,17},{6,18},{7,19},{8,30},{9,... | collective-permute-start | bytes 196616 | tf_op jit(solution)/shard_map/ppermute | solution.py:103
  9.6 41.8 %collective-permute-start.3 = (bf16[256,128]{1,0:T(8,128)(2,1)}, bf16[256,128]{1,0:T(8,128)(2,1)S(1)}, u32[]{:S(2)}, u32[]{:S(2)}) collective-permute-start(bf16[256,128]{1,0:T(8,128)(2,1)} %bitcast.29), channel_id=1, source_target_pairs={{0,30},{1,31},{2,24},{3,25},{4,26},{5,27},{6,28},{7,29},{8,20},{9,... | collective-permute-start | bytes 196616 | tf_op jit(solution)/shard_map/ppermute | solution.py:103
  28.7 9.0 %collective-permute-start.22 = (s32[256]{0:T(256)S(1)}, s32[256]{0:T(256)S(1)}, u32[]{:S(2)}, u32[]{:S(2)}) collective-permute-start(s32[256]{0:T(256)S(1)} %bitcast.37), channel_id=1, source_target_pairs={{0,30},{1,31},{2,24},{3,25},{4,26},{5,27},{6,28},{7,29},{8,20},{9,... | collective-permute-start | bytes 3080 | tf_op jit(solution)/shard_map/ppermute | solution.py:103
  48.2 9.3 %collective-permute-start.5 = (bf16[256,128]{1,0:T(8,128)(2,1)S(1)}, bf16[256,128]{1,0:T(8,128)(2,1)S(1)}, u32[]{:S(2)}, u32[]{:S(2)}) collective-permute-start(bf16[256,128]{1,0:T(8,128)(2,1)S(1)} %bitcast.31), channel_id=1, source_target_pairs={{0,11},{1,12},{2,13},{3,14},{4,15},{5,8},{6,9},{7,10},{8,1},{9,2},... | collective-permute-start | bytes 196616 | tf_op jit(solution)/shard_map/ppermute | solution.py:103
  48.3 9.2 %collective-permute-start.6 = (bf16[256,128]{1,0:T(8,128)(2,1)S(1)}, bf16[256,128]{1,0:T(8,128)(2,1)S(1)}, u32[]{:S(2)}, u32[]{:S(2)}) collective-permute-start(bf16[256,128]{1,0:T(8,128)(2,1)S(1)} %bitcast.32), channel_id=1, source_target_pairs={{0,21},{1,22},{2,23},{3,16},{4,17},{5,18},{6,19},{7,20},{8,31},{9,... | collective-permute-start | bytes 196616 | tf_op jit(solution)/shard_map/ppermute | solution.py:103
  49.2 8.4 %collective-permute-start.7 = (bf16[256,128]{1,0:T(8,128)(2,1)S(1)}, bf16[256,128]{1,0:T(8,128)(2,1)S(1)}, u32[]{:S(2)}, u32[]{:S(2)}) collective-permute-start(bf16[256,128]{1,0:T(8,128)(2,1)S(1)} %bitcast.33), channel_id=1, source_target_pairs={{0,31},{1,24},{2,25},{3,26},{4,27},{5,28},{6,29},{7,30},{8,21},{9,... | collective-permute-start | bytes 196616 | tf_op jit(solution)/shard_map/ppermute | solution.py:103
  51.4 11.1 %collective-permute-start.25 = (s32[256]{0:T(256)S(1)}, s32[256]{0:T(256)S(1)}, u32[]{:S(2)}, u32[]{:S(2)}) collective-permute-start(s32[256]{0:T(256)S(1)} %bitcast.40), channel_id=1, source_target_pairs={{0,21},{1,22},{2,23},{3,16},{4,17},{5,18},{6,19},{7,20},{8,31},{9,... | collective-permute-start | bytes 3080 | tf_op jit(solution)/shard_map/ppermute | solution.py:103
  55.0 7.5 %collective-permute-start.26 = (s32[256]{0:T(256)S(1)}, s32[256]{0:T(256)S(1)}, u32[]{:S(2)}, u32[]{:S(2)}) collective-permute-start(s32[256]{0:T(256)S(1)} %bitcast.41), channel_id=1, source_target_pairs={{0,31},{1,24},{2,25},{3,26},{4,27},{5,28},{6,29},{7,30},{8,21},{9,... | collective-permute-start | bytes 3080 | tf_op jit(solution)/shard_map/ppermute | solution.py:103
  58.9 7.3 %collective-permute-start.10 = (f32[256,128]{1,0:T(8,128)S(1)}, f32[256,128]{1,0:T(8,128)S(1)}, u32[]{:S(2)}, u32[]{:S(2)}) collective-permute-start(f32[256,128]{1,0:T(8,128)S(1)} %get-tuple-element.12), channel_id=1, source_target_pairs={{0,24},{8,16},{16,8},{24,0},{1,25},{9,17},{17,9},{25,1},{2,26},{10... | collective-permute-start | bytes 393224 | tf_op jit(solution)/shard_map/ppermute | solution.py:91
  60.2 8.1 %collective-permute-start.9 = (f32[256,128]{1,0:T(8,128)S(1)}, f32[256,128]{1,0:T(8,128)S(1)}, u32[]{:S(2)}, u32[]{:S(2)}) collective-permute-start(f32[256,128]{1,0:T(8,128)S(1)} %get-tuple-element.13), channel_id=1, source_target_pairs={{0,16},{8,24},{16,0},{24,8},{1,17},{9,25},{17,1},{25,9},{2,18},{10... | collective-permute-start | bytes 393224 | tf_op jit(solution)/shard_map/ppermute | solution.py:91
  68.3 9.4 %collective-permute-start.11 = (bf16[256,128]{1,0:T(8,128)(2,1)S(1)}, bf16[256,128]{1,0:T(8,128)(2,1)S(1)}, u32[]{:S(2)}, u32[]{:S(2)}) collective-permute-start(bf16[256,128]{1,0:T(8,128)(2,1)S(1)} %fusion.34), channel_id=1, source_target_pairs={{0,0},{1,1},{2,2},{3,3},{4,4},{5,5},{6,6},{7,7},{8,10},{9,11},{10,... | collective-permute-start | bytes 196616 | tf_op jit(solution)/shard_map/ppermute | solution.py:103
  69.0 9.9 %collective-permute-start.12 = (bf16[256,128]{1,0:T(8,128)(2,1)S(1)}, bf16[256,128]{1,0:T(8,128)(2,1)S(1)}, u32[]{:S(2)}, u32[]{:S(2)}) collective-permute-start(bf16[256,128]{1,0:T(8,128)(2,1)S(1)} %fusion.34), channel_id=1, source_target_pairs={{0,10},{1,11},{2,12},{3,13},{4,14},{5,15},{6,8},{7,9},{8,0},{9,1},... | collective-permute-start | bytes 196616 | tf_op jit(solution)/shard_map/ppermute | solution.py:103
  74.8 7.9 %collective-permute-start.14 = (bf16[256,128]{1,0:T(8,128)(2,1)S(1)}, bf16[256,128]{1,0:T(8,128)(2,1)S(1)}, u32[]{:S(2)}, u32[]{:S(2)}) collective-permute-start(bf16[256,128]{1,0:T(8,128)(2,1)S(1)} %fusion.34), channel_id=1, source_target_pairs={{0,30},{1,31},{2,24},{3,25},{4,26},{5,27},{6,28},{7,29},{8,20},{9,... | collective-permute-start | bytes 196616 | tf_op jit(solution)/shard_map/ppermute | solution.py:103
  80.2 7.5 %collective-permute-start.18 = (bf16[256,128]{1,0:T(8,128)(2,1)S(1)}, bf16[256,128]{1,0:T(8,128)(2,1)S(1)}, u32[]{:S(2)}, u32[]{:S(2)}) collective-permute-start(bf16[256,128]{1,0:T(8,128)(2,1)S(1)} %fusion.34), channel_id=1, source_target_pairs={{0,31},{1,24},{2,25},{3,26},{4,27},{5,28},{6,29},{7,30},{8,21},{9,... | collective-permute-start | bytes 196616 | tf_op jit(solution)/shard_map/ppermute | solution.py:103
  90.6 9.3 %collective-permute-start.27 = (f32[256,256]{1,0:T(8,128)}, f32[256,256]{1,0:T(8,128)S(1)}, u32[]{:S(2)}, u32[]{:S(2)}) collective-permute-start(f32[256,256]{1,0:T(8,128)} %get-tuple-element.8), channel_id=1, source_target_pairs={{0,8},{8,0},{16,24},{24,16},{1,9},{9,1},{17,25},{25,17},{2,10},{10... | collective-permute-start | bytes 786440 | tf_op jit(solution)/shard_map/ppermute | solution.py:91
  91.3 15.1 %collective-permute-start.28 = (f32[256,256]{1,0:T(8,128)}, f32[256,256]{1,0:T(8,128)}, u32[]{:S(2)}, u32[]{:S(2)}) collective-permute-start(f32[256,256]{1,0:T(8,128)} %get-tuple-element.10), channel_id=1, source_target_pairs={{0,16},{8,24},{16,0},{24,8},{1,17},{9,25},{17,1},{25,9},{2,18},{10... | collective-permute-start | bytes 786440 | tf_op jit(solution)/shard_map/ppermute | solution.py:91
  92.0 14.4 %collective-permute-start.29 = (f32[256,256]{1,0:T(8,128)}, f32[256,256]{1,0:T(8,128)}, u32[]{:S(2)}, u32[]{:S(2)}) collective-permute-start(f32[256,256]{1,0:T(8,128)} %get-tuple-element.9), channel_id=1, source_target_pairs={{0,24},{8,16},{16,8},{24,0},{1,25},{9,17},{17,9},{25,1},{2,26},{10... | collective-permute-start | bytes 786440 | tf_op jit(solution)/shard_map/ppermute | solution.py:91
  113.1 8.3 %collective-permute-start.31 = (bf16[256,256]{1,0:T(8,128)(2,1)S(1)}, bf16[256,256]{1,0:T(8,128)(2,1)}, u32[]{:S(2)}, u32[]{:S(2)}) collective-permute-start(bf16[256,256]{1,0:T(8,128)(2,1)S(1)} %convolution_convert_fusion), channel_id=1, source_target_pairs={{0,16},{8,24},{16,0},{24,8},{1,17},{9,25},{17,1},{25,9},{2,18},{10... | collective-permute-start | bytes 393224 | tf_op jit(solution)/shard_map/ppermute | solution.py:91
  113.4 8.0 %collective-permute-start.32 = (bf16[256,256]{1,0:T(8,128)(2,1)S(1)}, bf16[256,256]{1,0:T(8,128)(2,1)}, u32[]{:S(2)}, u32[]{:S(2)}) collective-permute-start(bf16[256,256]{1,0:T(8,128)(2,1)S(1)} %convolution_convert_fusion), channel_id=1, source_target_pairs={{0,24},{8,16},{16,8},{24,0},{1,25},{9,17},{17,9},{25,1},{2,26},{10... | collective-permute-start | bytes 393224 | tf_op jit(solution)/shard_map/ppermute | solution.py:91
  116.1 13.5 %collective-permute-start.49 = (f32[64,172]{0,1:T(8,128)S(1)}, f32[64,172]{0,1:T(8,128)S(1)}, u32[]{:S(2)}, u32[]{:S(2)}) collective-permute-start(f32[64,172]{0,1:T(8,128)S(1)} %add_add_fusion.1), channel_id=1, source_target_pairs={{0,1},{1,2},{2,3},{3,4},{4,5},{5,6},{6,7},{7,0},{8,9},{9,10},{10,1... | collective-permute-start | bytes 132104 | tf_op jit(solution)/shard_map/ppermute | solution.py:107
  116.1 13.4 %collective-permute-start.50 = (f32[64,172]{0,1:T(8,128)S(1)}, f32[64,172]{0,1:T(8,128)S(1)}, u32[]{:S(2)}, u32[]{:S(2)}) collective-permute-start(f32[64,172]{0,1:T(8,128)S(1)} %add_add_fusion.1), channel_id=1, source_target_pairs={{0,2},{1,3},{2,4},{3,5},{4,6},{5,7},{6,0},{7,1},{8,10},{9,11},{10,... | collective-permute-start | bytes 132104 | tf_op jit(solution)/shard_map/ppermute | solution.py:107
  129.6 9.7 %collective-permute-start.51 = (f32[64,172]{0,1:T(8,128)S(1)}, f32[64,172]{0,1:T(8,128)S(1)}, u32[]{:S(2)}, u32[]{:S(2)}) collective-permute-start(f32[64,172]{0,1:T(8,128)S(1)} %add_add_fusion.1), channel_id=1, source_target_pairs={{0,3},{1,4},{2,5},{3,6},{4,7},{5,0},{6,1},{7,2},{8,11},{9,12},{10,... | collective-permute-start | bytes 132104 | tf_op jit(solution)/shard_map/ppermute | solution.py:107
  129.6 9.8 %collective-permute-start.52 = (f32[64,172]{0,1:T(8,128)S(1)}, f32[64,172]{0,1:T(8,128)S(1)}, u32[]{:S(2)}, u32[]{:S(2)}) collective-permute-start(f32[64,172]{0,1:T(8,128)S(1)} %add_add_fusion.1), channel_id=1, source_target_pairs={{0,4},{1,5},{2,6},{3,7},{4,0},{5,1},{6,2},{7,3},{8,12},{9,13},{10,... | collective-permute-start | bytes 132104 | tf_op jit(solution)/shard_map/ppermute | solution.py:107
  132.1 10.4 %collective-permute-start.53 = (f32[64,172]{0,1:T(8,128)S(1)}, f32[64,172]{0,1:T(8,128)S(1)}, u32[]{:S(2)}, u32[]{:S(2)}) collective-permute-start(f32[64,172]{0,1:T(8,128)S(1)} %add_add_fusion.1), channel_id=1, source_target_pairs={{0,5},{1,6},{2,7},{3,0},{4,1},{5,2},{6,3},{7,4},{8,13},{9,14},{10,... | collective-permute-start | bytes 132104 | tf_op jit(solution)/shard_map/ppermute | solution.py:107
  134.4 8.4 %collective-permute-start.54 = (f32[64,172]{0,1:T(8,128)S(1)}, f32[64,172]{0,1:T(8,128)S(1)}, u32[]{:S(2)}, u32[]{:S(2)}) collective-permute-start(f32[64,172]{0,1:T(8,128)S(1)} %add_add_fusion.1), channel_id=1, source_target_pairs={{0,6},{1,7},{2,0},{3,1},{4,2},{5,3},{6,4},{7,5},{8,14},{9,15},{10,... | collective-permute-start | bytes 132104 | tf_op jit(solution)/shard_map/ppermute | solution.py:107
  134.4 12.9 %collective-permute-start.55 = (f32[64,172]{0,1:T(8,128)S(1)}, f32[64,172]{0,1:T(8,128)S(1)}, u32[]{:S(2)}, u32[]{:S(2)}) collective-permute-start(f32[64,172]{0,1:T(8,128)S(1)} %add_add_fusion.1), channel_id=1, source_target_pairs={{0,7},{1,0},{2,1},{3,2},{4,3},{5,4},{6,5},{7,6},{8,15},{9,8},{10,9... | collective-permute-start | bytes 132104 | tf_op jit(solution)/shard_map/ppermute | solution.py:107
  139.3 9.2 %collective-permute-start.36 = (f32[32,256]{1,0:T(8,128)S(1)}, f32[32,256]{1,0:T(8,128)S(1)}, u32[]{:S(2)}, u32[]{:S(2)}) collective-permute-start(f32[32,256]{1,0:T(8,128)S(1)} %add_add_fusion.3), channel_id=1, source_target_pairs={{0,1},{1,2},{2,3},{3,4},{4,5},{5,6},{6,7},{7,0},{8,9},{9,10},{10,1... | collective-permute-start | bytes 98312 | tf_op jit(solution)/shard_map/ppermute | solution.py:107
  139.4 10.0 %collective-permute-start.37 = (f32[32,256]{1,0:T(8,128)S(1)}, f32[32,256]{1,0:T(8,128)S(1)}, u32[]{:S(2)}, u32[]{:S(2)}) collective-permute-start(f32[32,256]{1,0:T(8,128)S(1)} %add_add_fusion.3), channel_id=1, source_target_pairs={{0,2},{1,3},{2,4},{3,5},{4,6},{5,7},{6,0},{7,1},{8,10},{9,11},{10,... | collective-permute-start | bytes 98312 | tf_op jit(solution)/shard_map/ppermute | solution.py:107
  142.7 8.4 %collective-permute-start.39 = (f32[32,256]{1,0:T(8,128)S(1)}, f32[32,256]{1,0:T(8,128)S(1)}, u32[]{:S(2)}, u32[]{:S(2)}) collective-permute-start(f32[32,256]{1,0:T(8,128)S(1)} %add_add_fusion.3), channel_id=1, source_target_pairs={{0,4},{1,5},{2,6},{3,7},{4,0},{5,1},{6,2},{7,3},{8,12},{9,13},{10,... | collective-permute-start | bytes 98312 | tf_op jit(solution)/shard_map/ppermute | solution.py:107
  153.4 7.8 %collective-permute-start.43 = (f32[32,256]{1,0:T(8,128)S(1)}, f32[32,256]{1,0:T(8,128)S(1)}, u32[]{:S(2)}, u32[]{:S(2)}) collective-permute-start(f32[32,256]{1,0:T(8,128)S(1)} %get-tuple-element.7), channel_id=1, source_target_pairs={{0,8},{8,0},{16,24},{24,16},{1,9},{9,1},{17,25},{25,17},{2,10},{10... | collective-permute-start | bytes 98312 | tf_op jit(solution)/shard_map/ppermute | solution.py:91
  (42 other events, 465.0 us)

commit v2 on v1

v2 whole, which is shorter than its diff:
```python
import functools
import math

import jax
import jax.numpy as jnp
from jax import lax
from jax.experimental import pallas as pl
from jax.experimental.pallas import tpu as pltpu
from jax.sharding import PartitionSpec as P


def keep_mask(id_values, unit_count):
    columns = jnp.arange(unit_count, dtype=jnp.int32)
    mixed = id_values[:, None] * 73244475 + columns[None, :] * 19349663 + 12345
    mixed = mixed ^ jnp.right_shift(mixed, 15)
    mixed = mixed * 40503
    mixed = mixed ^ jnp.right_shift(mixed, 13)
    return jnp.bitwise_and(mixed, 3) != 0


def dense_kernel(tile_side, count_ref, place_ref, tiles_ref, dense_ref):
    section = pl.program_id(0)
    edge = tiles_ref.shape[-1]
    dense_ref[...] = jnp.zeros_like(dense_ref)

    def put(slot, carried):
        place = place_ref[section, slot]
        row = place // tile_side
        column = place % tile_side
        dense_ref[
            pl.ds(pl.multiple_of(row * edge, edge), edge),
            pl.ds(pl.multiple_of(column * edge, edge), edge),
        ] = tiles_ref[0, slot]
        return carried

    lax.fori_loop(0, count_ref[section], put, 0)


def build_dense(tiles, place, count, group_rows):
    sections, slots, edge, _ = tiles.shape
    body = functools.partial(dense_kernel, group_rows // edge)
    smem = pl.BlockSpec(memory_space=pltpu.SMEM)
    return pl.pallas_call(
        body,
        grid=(sections,),
        in_specs=[
            smem,
            smem,
            pl.BlockSpec((1, slots, edge, edge), lambda s: (s, 0, 0, 0)),
        ],
        out_specs=pl.BlockSpec((group_rows, group_rows), lambda s: (0, s)),
        out_shape=jax.ShapeDtypeStruct((group_rows, sections * group_rows), tiles.dtype),
        compiler_params=pltpu.CompilerParams(vmem_limit_bytes=40 * 1024 * 1024),
        cost_estimate=pl.CostEstimate(
            flops=0, bytes_accessed=2 * sections * group_rows * group_rows, transcendentals=0
        ),
        name="dense_tiles",
    )(count, place, tiles)


def on_device(
    features,
    node_ids,
    labels,
    train_mask,
    tile_values,
    tile_place,
    tile_count,
    weight_in,
    weight_out,
    class_bias,
):
    own_rows = features.shape[1]
    reps = lax.axis_size("rep")
    blks = lax.axis_size("blk")
    rep_index = lax.axis_index("rep")
    blk_index = lax.axis_index("blk")
    sections = tile_values.shape[2]
    group_rows = own_rows * reps
    hidden_width = weight_in.shape[1]
    scale = 1.0 / math.sqrt(group_rows * blks)
    f32 = jnp.float32
    bf16 = jnp.bfloat16

    everywhere = ("blk", "rep")

    def pick(blocks):
        return jnp.concatenate(
            [blocks[(blk_index - sections * rep_index - j) % blks] for j in range(sections)], axis=0
        )

    def swap_chunks(chunks):
        return lax.all_to_all(chunks, "rep", split_axis=0, concat_axis=0, tiled=True)

    def scatter_rows(partial):
        return jnp.sum(swap_chunks(partial.reshape(reps, own_rows, partial.shape[1])), axis=0)

    def to_columns(value):
        held = lax.all_gather(value, "blk", axis=0)
        wanted = [
            held[(blk_index - sections * r - j) % blks] for r in range(reps) for j in range(sections)
        ]
        wanted = jnp.stack(wanted).reshape(reps, sections, own_rows, value.shape[1])
        got = swap_chunks(wanted)
        return jnp.swapaxes(got, 0, 1).reshape(sections * group_rows, value.shape[1])

    def sum_everywhere(value):
        devices = reps * blks
        tall = value if value.shape[0] % devices == 0 else value.reshape(devices, -1)
        chunks = tall.reshape(devices, tall.shape[0] // devices, tall.shape[1])
        chunks = lax.all_to_all(chunks, everywhere, split_axis=0, concat_axis=0, tiled=True)
        whole = lax.all_gather(jnp.sum(chunks, axis=0), everywhere, axis=0, tiled=True)
        return whole.reshape(value.shape)

    dense = build_dense(tile_values[0, 0], tile_place[0, 0], tile_count[0, 0], group_rows)
    feature_columns = pick(
        lax.all_gather(features[0], everywhere, axis=0).reshape(blks, group_rows, features.shape[2])
    )
    id_columns = pick(lax.all_gather(node_ids[0], everywhere, axis=0).reshape(blks, group_rows))
    first = jnp.dot(dense, feature_columns, preferred_element_type=f32)
    z_input = scatter_rows(first).astype(bf16)
    kept = jnp.where(keep_mask(id_columns, hidden_width), f32(4.0 / 3.0), f32(0.0))
    z_columns = to_columns(z_input)
    pre_act = jnp.dot(z_columns, weight_in, preferred_element_type=f32)
    dropped = (jnp.maximum(pre_act, 0.0) * kept).astype(bf16)
    factor = kept * (pre_act > 0)
    second = jnp.dot(dense, dropped, preferred_element_type=f32)
    z_output = scatter_rows(second).astype(bf16)
    logits = jnp.dot(z_output, weight_out, preferred_element_type=f32) + class_bias
    likelihood = jax.nn.softmax(logits, axis=-1)
    onehot = labels[0][:, None] == jnp.arange(logits.shape[-1], dtype=jnp.int32)[None, :]
    slope = (
        (likelihood - onehot.astype(f32)) * train_mask[0][:, None].astype(f32) * scale
    ).astype(bf16)
    grad_rows = jnp.einsum(
        "nc,hc->nh", slope, weight_out, preferred_element_type=f32
    ).astype(bf16)
    grad_block = swap_chunks(jnp.broadcast_to(grad_rows[None], (reps,) + grad_rows.shape))
    grad_block = grad_block.reshape(group_rows, hidden_width)
    out_terms = jnp.einsum("nh,nc->hc", z_output, slope, preferred_element_type=f32)
    grad_out = sum_everywhere(out_terms)
    back = jnp.einsum("nc,nh->ch", dense, grad_block, preferred_element_type=f32)
    pre_slope = (back * factor).astype(bf16)
    in_terms = jnp.einsum("nf,nh->fh", z_columns, pre_slope, preferred_element_type=f32)
    grad_in = sum_everywhere(in_terms)
    return (logits[None], grad_in, grad_out)


def solution(mesh):
    placed = (
        P("blk", "rep", None),
        P("blk", "rep"),
        P("blk", "rep"),
        P("blk", "rep"),
        P("blk", "rep", None, None, None, None),
        P("blk", "rep", None, None),
        P("blk", "rep", None),
        P(),
        P(),
        P(),
    )
    return jax.shard_map(
        on_device,
        mesh=mesh,
        in_specs=placed,
        out_specs=(P("blk", "rep", None), P(), P()),
        check_vma=False,
    )
```

time: 166 us -> 371 us (2.23)
  blocking collectives: 0 us -> 217 us
  starting transfers between devices: 94.2 us -> 20.2 us
  waiting for transfers between devices: 49 us -> 83.6 us
  between operations: 1.15 us -> 14.6 us
  matrix products: 8.54 us -> 17.3 us
  local copies, waits for them, and re-layouts: 8.65 us -> 16.4 us
    all_gather x0 -> x4, blocking collectives: none -> 217 us  [the longest x2 134 us: sum_everywhere(): lax.all_gather(jnp.sum(chunks, axis=0), everywhere, axis=0, tiled=True)]
    ppermute x59 -> x0, starting transfers between devices: 94.2 us -> none  [the longest x24 51.3 us: to_columns(): pieces.append(lax.ppermute(value, ('rep', 'blk'), pairs))]
    all_gather x0 -> x1, waiting for transfers between devices: none -> 55.8 us  [on_device(): lax.all_gather(features[0], everywhere, axis=0)]
    ppermute x59 -> x0, waiting for transfers between devices: 49 us -> none  [the longest x21 25.3 us: swap(): return lax.ppermute(value, 'rep', [(r, r ^ delta) for r in range(reps)])]
    all_to_all x0 -> x6, waiting for transfers between devices: none -> 27.1 us  [the longest x4 21.9 us: swap_chunks(): lax.all_to_all(chunks, 'rep', split_axis=0, concat_axis=0, tiled=True)]
    all_to_all x0 -> x6, starting transfers between devices: none -> 20.1 us  [the longest x4 15 us: swap_chunks(): lax.all_to_all(chunks, 'rep', split_axis=0, concat_axis=0, tiled=True)]
    unnamed x52 -> x44, local copies, waits for them, and re-layouts: 4.32 us -> 11.9 us
    dot_general x1, matrix products: 1.55 us -> 5.48 us  [on_device(): second = jnp.dot(dense, dropped, preferred_element_type=f32)]
  transfers between devices with their start and end apart: 59 -> 7, of which waited for: 21 -> 5; matrix products, arithmetic and copies ran while one was open for 6% -> 3% of each run, Pallas kernels for 1% -> 0%
where the time goes in v2:
time: 371 us
  blocking collectives  217 us (58%)
  waiting for transfers between devices  83.6 us (23%)
  starting transfers between devices  20.2 us (5%)
  matrix products  17.3 us (5%)
  local copies, waits for them, and re-layouts  16.4 us (4%)
  between operations  14.6 us (4%)
    all_gather x2, blocking collectives, sum_everywhere(): lax.all_gather(jnp.sum(chunks, axis=0), everywhere, axis=0, tiled=True)  134 us
    all_gather x1, blocking collectives, on_device(): lax.all_gather(node_ids[0], everywhere, axis=0).reshape(blks, group_rows)  67.6 us
    all_gather x1, waiting for transfers between devices, on_device(): lax.all_gather(features[0], everywhere, axis=0)  55.8 us
    all_to_all x4, waiting for transfers between devices, swap_chunks(): lax.all_to_all(chunks, 'rep', split_axis=0, concat_axis=0, tiled=True)  21.9 us
    all_to_all x4, starting transfers between devices, swap_chunks(): lax.all_to_all(chunks, 'rep', split_axis=0, concat_axis=0, tiled=True)  15 us
    all_gather x1, blocking collectives, to_columns(): held = lax.all_gather(value, 'blk', axis=0)  14.9 us
    unnamed x44, local copies, waits for them, and re-layouts  11.9 us
  transfers between devices with their start and end apart: 7, of which 5 were waited for; matrix products, arithmetic and copies ran while one was open for 3% of the time, Pallas kernels for 0%

profile of v2, /device:TPU:0, one launch (start us, length us, event | category | flops | bytes accessed | tf_op | source)
XLA Modules:
  0.0 370.6 jit_solution(9993620926873150915)
XLA Ops:
  7.2 0.7 all-gather.5.cloned.1.call-update
  8.0 1.2 copy-done.2
  9.2 0.7 copy-done.3
  9.9 0.7 copy-done.4
  10.5 1.7 dense_tiles.1
  12.3 1.9 copy-done.1
  14.2 55.8 %all-gather.5.cloned.1.call-done = bf16[32,256,128]{2,1,0:T(8,128)(2,1)} async-done(((bf16[1,256,128]{2,1,0:T(8,128)(2,1)}), bf16[32,256,128]{2,1,0:T(8,128)(2,1)}) %all-gather.5.cloned.1.call-update) | async-done | bytes 2097168 | tf_op jit(solution)/shard_map/all_gather | solution.py:117
  70.0 1.1 dynamic-slice_bitcast_fusion.1
  71.1 4.2 %fusion.15 = f32[1024,128]{1,0:T(8,128)} fusion(bf16[1024,2048]{1,0:T(8,128)(2,1)} %copy-done.1, bf16[1024,128]{1,0:T(8,128)(2,1)S(1)} %get-tuple-element.16, bf16[1024,128]{1,0:T(8,128)(2,1)S(1)} %get-tuple-element.15), kind=kOutput, calls=%fused_computation.20 | convolution fusion | flops 537919488 | bytes 5242880 | tf_op jit(solution)/shard_map/dot_general | solution.py:120
  75.3 3.6 all-to-all-start
  79.1 8.5 %all-to-all-done = f32[4,256,128]{2,1,0:T(8,128)S(1)} async-done(((f32[4,256,128]{2,1,0:T(8,128)}), f32[4,256,128]{2,1,0:T(8,128)S(1)}, u32[]{:S(2)}, u32[]{:S(2)}) %all-to-all-start) | async-done | bytes 524320 | tf_op jit(solution)/shard_map/all_to_all | solution.py:93
  87.7 14.9 %all-gather = bf16[2048,128]{1,0:T(8,128)(2,1)S(1)} all-gather(bf16[256,128]{1,0:T(8,128)(2,1)S(1)} %reduce_sum.45), channel_id=2, replica_groups=mesh['rep'=4,'blk'=8] {'blk'}, dimensions={0}, use_global_device_ids=true | all-gather | bytes 589824 | tf_op jit(solution)/shard_map/all_gather | solution.py:99
  107.6 3.5 all-to-all-start.1
  111.1 67.6 %all-gather.1 = s32[32,1,256]{2,1,0:T(1,128)S(1)} all-gather(s32[1,1,256]{2,1,0:T(1,128)S(1)} %bitcast.59), channel_id=1, replica_groups=mesh['rep'=4,'blk'=8] {'blk','rep'}, dimensions={0}, use_global_device_ids=true | all-gather | bytes 33792 | tf_op jit(solution)/shard_map/all_gather | solution.py:119
  179.3 5.5 %fusion.7 = f32[1024,256]{1,0:T(8,128)} fusion(bf16[1024,2048]{1,0:T(8,128)(2,1)} %copy-done.1, f32[2048,256]{1,0:T(8,128)S(1)} %fusion.41, s32[256]{0:T(256)S(1)} %iota_multiply_fusion, s32[2048]{0:T(1024)S(1)} %add_multiply_fusion), kind=kOutput, calls=%fused_computation.15 | convolution fusion | flops 1080557568 | bytes 7349248 | tf_op jit(solution)/shard_map/dot_general | solution.py:127
  184.9 3.7 all-to-all-start.2
  188.6 9.6 %all-to-all-done.2 = f32[4,256,256]{2,1,0:T(8,128)S(1)} async-done(((f32[4,256,256]{2,1,0:T(8,128)}), f32[4,256,256]{2,1,0:T(8,128)S(1)}, u32[]{:S(2)}, u32[]{:S(2)}) %all-to-all-start.2) | async-done | bytes 1048608 | tf_op jit(solution)/shard_map/all_to_all | solution.py:93
  199.4 0.8 broadcast_in_dim.12
  200.2 4.3 %all-to-all-start.3 = ((bf16[4,256,256]{2,1,0:T(8,128)(2,1)}), bf16[4,256,256]{2,1,0:T(8,128)(2,1)}, u32[]{:S(2)}, u32[]{:S(2)}) async-start(bf16[4,256,256]{2,1,0:T(8,128)(2,1)} %broadcast_in_dim.12), calls=%async_computation.3 | async-start | bytes 1048576 | tf_op jit(solution)/shard_map/all_to_all | solution.py:93
  204.7 1.0 dot_general.33
  205.7 1.7 convolution_bitcast_fusion
  207.4 3.7 %all-to-all-done.3 = bf16[4,256,256]{2,1,0:T(8,128)(2,1)} async-done(((bf16[4,256,256]{2,1,0:T(8,128)(2,1)}), bf16[4,256,256]{2,1,0:T(8,128)(2,1)}, u32[]{:S(2)}, u32[]{:S(2)}) %all-to-all-start.3) | async-done | bytes 524320 | tf_op jit(solution)/shard_map/all_to_all | solution.py:93
  211.2 2.6 all-to-all-start.5
  213.8 4.9 %fusion.6 = f32[32,4,256]{2,0,1:T(8,128)S(1)} fusion(bf16[1024,2048]{1,0:T(8,128)(2,1)} %copy-done.1, bf16[1024,256]{1,0:T(8,128)(2,1)} %bitcast.19, f32[2048,256]{1,0:T(8,128)S(1)} %copy-done.6, s32[256]{0:T(256)S(1)} %copy-done.16, s32[2048]{0:T(1024)S(1)} %add_multiply_fusion, bf16[32,4,2048]{2,1,0:T(4,128)(2,1)} %dot_general.33), kind=kOutput, calls=%fused_computation.14 | convolution fusion | flops 1215299584 | bytes 7480320 | tf_op jit(solution)/shard_map/nf,nh->fh/dot_general | solution.py:144
  218.7 0.7 copy.26
  219.5 5.2 %all-to-all-done.5 = f32[32,8,172]{2,1,0:T(8,128)S(1)} async-done(((f32[32,8,172]{2,1,0:T(8,128)}), f32[32,8,172]{2,1,0:T(8,128)S(1)}, u32[]{:S(2)}, u32[]{:S(2)}) %all-to-all-start.5) | async-done | bytes 176160 | tf_op jit(solution)/shard_map/all_to_all | solution.py:111
  224.7 2.6 all-to-all-start.4
  227.3 0.9 copy.28
  228.2 69.9 %all_gather.20 = f32[256,172]{1,0:T(8,128)S(1)} all-gather(f32[8,172]{1,0:T(8,128)S(1)} %reduce_sum.49), channel_id=1, replica_groups=mesh['rep'=4,'blk'=8] {'blk','rep'}, dimensions={0}, use_global_device_ids=true | all-gather | bytes 181632 | tf_op jit(solution)/shard_map/all_gather | solution.py:112
  298.1 0.8 copy.29
  298.9 64.1 %all-gather.2 = f32[32,4,256]{2,1,0:T(4,128)S(1)} all-gather(f32[1,4,256]{2,1,0:T(4,128)S(1)} %bitcast.56), channel_id=1, replica_groups=mesh['rep'=4,'blk'=8] {'blk','rep'}, dimensions={0}, use_global_device_ids=true | all-gather | bytes 135168 | tf_op jit(solution)/shard_map/all_gather | solution.py:112
  363.0 0.7 reshape.88
  (57 shorter events, 7.2 us)
Async XLA Ops:
  7.2 191.1 %copy-start = (bf16[256,172]{0,1:T(8,128)(2,1)S(1)}, bf16[256,172]{0,1:T(8,128)(2,1)}, u32[]{:S(2)}) copy-start(bf16[256,172]{0,1:T(8,128)(2,1)} %param.18) | copy-start | bytes 264196
  7.2 62.8 %all-gather.5.cloned.1.call-start = ((), (), s32[]{:S(2)}) async-start(), calls=%async_computation.6 | async-start | bytes 2162688 | tf_op jit(solution)/shard_map/all_gather | solution.py:117
  8.0 1.2 copy-start.2
  9.2 0.7 copy-start.3
  9.9 0.7 copy-start.4
  12.2 1.9 copy-start.1
  75.3 35.7 %copy-start.11 = (s32[1,256]{1,0:T(1,128)S(1)}, s32[1,256]{1,0:T(1,128)}, u32[]{:S(2)}) copy-start(s32[1,256]{1,0:T(1,128)} %param.11) | copy-start | bytes 3076
  75.3 12.3 %all-to-all-start = ((f32[4,256,128]{2,1,0:T(8,128)}), f32[4,256,128]{2,1,0:T(8,128)S(1)}, u32[]{:S(2)}, u32[]{:S(2)}) async-start(f32[4,256,128]{2,1,0:T(8,128)} %bitcast.6), calls=%async_computation | async-start | bytes 1048576 | tf_op jit(solution)/shard_map/all_to_all | solution.py:93
  87.7 91.3 %copy-start.7 = (bf16[128,256]{1,0:T(8,128)(2,1)S(1)}, bf16[128,256]{1,0:T(8,128)(2,1)}, u32[]{:S(2)}) copy-start(bf16[128,256]{1,0:T(8,128)(2,1)} %param.17) | copy-start | bytes 196612
  107.6 71.3 %all-to-all-start.1 = ((bf16[4,2,256,128]{3,2,1,0:T(8,128)(2,1)}), bf16[4,2,256,128]{3,2,1,0:T(8,128)(2,1)S(1)}, u32[]{:S(2)}, u32[]{:S(2)}) async-start(bf16[4,2,256,128]{3,2,1,0:T(8,128)(2,1)} %bitcast.8), calls=%async_computation.1 | async-start | bytes 1048576 | tf_op jit(solution)/shard_map/all_to_all | solution.py:93
  178.8 6.0 %copy-start.15 = (s32[256]{0:T(256)}, s32[256]{0:T(256)S(1)}, u32[]{:S(2)}) copy-start(s32[256]{0:T(256)S(1)} %iota_multiply_fusion) | copy-start | bytes 3076
  179.3 5.5 %copy-start.5 = (f32[2048,256]{1,0:T(8,128)}, f32[2048,256]{1,0:T(8,128)S(1)}, u32[]{:S(2)}) copy-start(f32[2048,256]{1,0:T(8,128)S(1)} %fusion.41) | copy-start | bytes 6291460
  184.8 3.7 copy-start.12
  184.8 13.4 %copy-start.9 = (f32[172]{0:T(256)S(1)}, f32[172]{0:T(256)}, u32[]{:S(2)}) copy-start(f32[172]{0:T(256)} %param.19) | copy-start | bytes 2068
  184.8 14.3 %copy-start.14 = (s32[1,256]{1,0:T(1,128)S(1)}, s32[1,256]{1,0:T(1,128)}, u32[]{:S(2)}) copy-start(s32[1,256]{1,0:T(1,128)} %param.12) | copy-start | bytes 3076
  184.9 13.3 %all-to-all-start.2 = ((f32[4,256,256]{2,1,0:T(8,128)}), f32[4,256,256]{2,1,0:T(8,128)S(1)}, u32[]{:S(2)}, u32[]{:S(2)}) async-start(f32[4,256,256]{2,1,0:T(8,128)} %bitcast.14), calls=%async_computation.2 | async-start | bytes 2097152 | tf_op jit(solution)/shard_map/all_to_all | solution.py:93
  188.5 10.9 %copy-start.13 = (f32[1,256]{1,0:T(1,128)}, f32[1,256]{1,0:T(1,128)S(1)}, u32[]{:S(2)}) copy-start(f32[1,256]{1,0:T(1,128)S(1)} %convert_element_type.48) | copy-start | bytes 3076
  198.5 0.6 copy-start.8
  198.6 0.6 copy-start.10
  200.2 13.5 %copy-start.6 = (f32[2048,256]{1,0:T(8,128)S(1)}, f32[2048,256]{1,0:T(8,128)}, u32[]{:S(2)}) copy-start(f32[2048,256]{1,0:T(8,128)} %copy-done.5) | copy-start | bytes 6291460
  200.2 10.9 %all-to-all-start.3 = ((bf16[4,256,256]{2,1,0:T(8,128)(2,1)}), bf16[4,256,256]{2,1,0:T(8,128)(2,1)}, u32[]{:S(2)}, u32[]{:S(2)}) async-start(bf16[4,256,256]{2,1,0:T(8,128)(2,1)} %broadcast_in_dim.12), calls=%async_computation.3 | async-start | bytes 1048576 | tf_op jit(solution)/shard_map/all_to_all | solution.py:93
  204.7 9.0 %copy-start.16 = (s32[256]{0:T(256)S(1)}, s32[256]{0:T(256)}, u32[]{:S(2)}) copy-start(s32[256]{0:T(256)} %copy-done.15) | copy-start | bytes 3076
  211.2 13.5 %all-to-all-start.5 = ((f32[32,8,172]{2,1,0:T(8,128)}), f32[32,8,172]{2,1,0:T(8,128)S(1)}, u32[]{:S(2)}, u32[]{:S(2)}) async-start(f32[32,8,172]{2,1,0:T(8,128)} %convolution_bitcast_fusion), calls=%async_computation.5 | async-start | bytes 524288 | tf_op jit(solution)/shard_map/all_to_all | solution.py:111
  224.7 74.2 %all-to-all-start.4 = ((f32[32,4,256]{2,1,0:T(4,128)}), f32[32,4,256]{2,1,0:T(4,128)S(1)}, u32[]{:S(2)}, u32[]{:S(2)}) async-start(f32[32,4,256]{2,1,0:T(4,128)} %copy.26), calls=%async_computation.4 | async-start | bytes 262144 | tf_op jit(solution)/shard_map/all_to_all | solution.py:111
Sparse Core Ops, SparseCore 0:
  10.9 59.0 all-gather.4

commit v3 on v1

v3 whole, which is shorter than its diff:
```python
import functools
import math

import jax
import jax.numpy as jnp
from jax import lax
from jax.experimental import pallas as pl
from jax.experimental.pallas import tpu as pltpu
from jax.sharding import PartitionSpec as P


def keep_mask(id_values, unit_count):
    columns = jnp.arange(unit_count, dtype=jnp.int32)
    mixed = id_values[:, None] * 73244475 + columns[None, :] * 19349663 + 12345
    mixed = mixed ^ jnp.right_shift(mixed, 15)
    mixed = mixed * 40503
    mixed = mixed ^ jnp.right_shift(mixed, 13)
    return jnp.bitwise_and(mixed, 3) != 0


def dense_kernel(
    per_rep, tile_side, spot_ref, order_ref, moved_ref, place_ref, own_ref, other_ref, dense_ref
):
    position = pl.program_id(0)
    rep_index = spot_ref[0]
    edge = own_ref.shape[-1]
    slots = own_ref.shape[1]
    dense_ref[...] = jnp.zeros_like(dense_ref)

    def put_all(tiles_ref):
        def put(slot, carried):
            place = place_ref[position, slot]
            row = place // tile_side
            column = place % tile_side
            row = ((row // per_rep) ^ rep_index) * per_rep + row % per_rep
            column = ((column // per_rep) ^ rep_index) * per_rep + column % per_rep

            @pl.when(place >= 0)
            def _():
                dense_ref[
                    pl.ds(pl.multiple_of(row * edge, edge), edge),
                    pl.ds(pl.multiple_of(column * edge, edge), edge),
                ] = tiles_ref[0, slot]

            return carried

        lax.fori_loop(0, slots, put, 0)

    @pl.when(moved_ref[position] == 0)
    def _():
        put_all(own_ref)

    @pl.when(moved_ref[position] != 0)
    def _():
        put_all(other_ref)


def build_dense(tiles, others, place, spot, order, moved, own_rows, group_rows):
    sections, slots, edge, _ = tiles.shape
    body = functools.partial(dense_kernel, own_rows // edge, group_rows // edge)
    tile_block = (1, slots, edge, edge)
    return pl.pallas_call(
        body,
        grid_spec=pltpu.PrefetchScalarGridSpec(
            num_scalar_prefetch=4,
            grid=(sections,),
            in_specs=[
                pl.BlockSpec(tile_block, lambda p, spot, order, *_: (order[p], 0, 0, 0)),
                pl.BlockSpec(
                    tile_block, lambda p, spot, order, *_: (jnp.maximum(order[p] - 1, 0), 0, 0, 0)
                ),
            ],
            out_specs=pl.BlockSpec((group_rows, group_rows), lambda p, *_: (0, p)),
        ),
        out_shape=jax.ShapeDtypeStruct((group_rows, sections * group_rows), tiles.dtype),
        compiler_params=pltpu.CompilerParams(vmem_limit_bytes=40 * 1024 * 1024),
        cost_estimate=pl.CostEstimate(
            flops=0, bytes_accessed=2 * sections * group_rows * group_rows, transcendentals=0
        ),
        name="dense_tiles",
    )(spot, order, moved, place, tiles, others)


def on_device(
    features,
    node_ids,
    labels,
    train_mask,
    tile_values,
    tile_place,
    tile_count,
    weight_in,
    weight_out,
    class_bias,
):
    own_rows = features.shape[1]
    reps = lax.axis_size("rep")
    blks = lax.axis_size("blk")
    rep_index = lax.axis_index("rep")
    blk_index = lax.axis_index("blk")
    sections = tile_values.shape[2]
    group_rows = own_rows * reps
    hidden_width = weight_in.shape[1]
    scale = 1.0 / math.sqrt(group_rows * blks)
    f32 = jnp.float32
    bf16 = jnp.bfloat16

    def swap(value, delta):
        if delta == 0:
            return value
        return lax.ppermute(value, "rep", [(r, r ^ delta) for r in range(reps)])

    def exchange(value, delta):
        return lax.ppermute(value, "blk", [(c, c ^ delta) for c in range(blks)])

    def to_columns(value):
        pieces = []
        for delta in range(reps):
            pairs = []
            for r in range(reps):
                for c in range(blks):
                    target = r ^ delta
                    pairs.append((r * blks + c, target * blks + (c + sections * target) % blks))
            pieces.append(lax.ppermute(value, ("rep", "blk"), pairs))
        block = jnp.concatenate(pieces, axis=0)
        return [block] + [exchange(block, delta) for delta in range(1, sections)]

    def scatter_rows(partial):
        chunks = partial.reshape(reps, own_rows, partial.shape[1])
        total = chunks[0]
        for delta in range(1, reps):
            total = total + swap(chunks[delta], delta)
        return total

    def sum_everywhere(value):
        half = value.shape[0] // 2
        side = lax.rem(blk_index, 2)
        theirs = exchange(lax.dynamic_slice_in_dim(value, (1 - side) * half, half, 0), 1)
        total = lax.dynamic_slice_in_dim(value, side * half, half, 0) + theirs
        steps = [(exchange, 1 << bit) for bit in range(1, (blks - 1).bit_length())]
        steps += [(swap, 1 << bit) for bit in range((reps - 1).bit_length())]
        for move, delta in steps:
            rounded = total.astype(bf16)
            total = rounded.astype(f32) + move(rounded, delta).astype(f32)
        other = exchange(total, 1)
        lower = jnp.where(side == 0, total, other)
        upper = jnp.where(side == 0, other, total)
        return jnp.concatenate([lower, upper], axis=0)

    def digits(ids):
        lanes = features.shape[2]
        parts = [ids & 255, (ids >> 8) & 255, ids >> 16]
        rows = jnp.concatenate([part.reshape(-1, lanes) for part in parts], axis=0)
        return jnp.pad(rows, ((0, -rows.shape[0] % 16), (0, 0))).astype(bf16)

    def undo_digits(rows):
        count = own_rows // rows.shape[1]
        parts = [rows[i * count : (i + 1) * count].astype(jnp.int32) for i in range(3)]
        return (parts[0] + (parts[1] << 8) + (parts[2] << 16)).reshape(own_rows)

    member = lax.rem(blk_index, sections)
    live = jnp.arange(tile_values.shape[3], dtype=jnp.int32)[None, :] < tile_count[0, 0][:, None]
    place = jnp.where(live, tile_place[0, 0], -1)
    other_tiles = []
    other_place = [place[0]]
    for j in range(1, sections):
        pairs = []
        for r in range(reps):
            for c in range(blks):
                if c % sections < j:
                    pairs.append((r * blks + c, (r + 1) % reps * blks + c))
        other_tiles.append(lax.ppermute(tile_values[0, 0, j], ("rep", "blk"), pairs))
        other_place.append(lax.ppermute(place[j], ("rep", "blk"), pairs))
    position = jnp.arange(sections, dtype=jnp.int32)
    column = position ^ member
    order = jnp.mod(member - column, sections)
    moved = (column > member).astype(jnp.int32)
    placed = jnp.where(moved[:, None] != 0, jnp.stack(other_place)[order], place[order])
    dense = build_dense(
        tile_values[0, 0],
        jnp.stack(other_tiles),
        placed,
        rep_index.reshape(1),
        order,
        moved,
        own_rows,
        group_rows,
    )
    bundle = jnp.concatenate([features[0], digits(node_ids[0])], axis=0)
    bundles = jnp.concatenate(to_columns(bundle), axis=0).reshape(sections * reps, -1, features.shape[2])
    feature_columns = bundles[:, :own_rows].reshape(sections * group_rows, features.shape[2])
    id_columns = jnp.concatenate(
        [undo_digits(bundles[i, own_rows:]) for i in range(sections * reps)]
    )
    first = jnp.dot(dense, feature_columns, preferred_element_type=f32)
    z_input = scatter_rows(first).astype(bf16)
    kept = jnp.where(keep_mask(id_columns, hidden_width), f32(4.0 / 3.0), f32(0.0))
    z_columns = jnp.concatenate(to_columns(z_input), axis=0)
    pre_act = jnp.dot(z_columns, weight_in, preferred_element_type=f32)
    dropped = (jnp.maximum(pre_act, 0.0) * kept).astype(bf16)
    factor = kept * (pre_act > 0)
    second = jnp.dot(dense, dropped, preferred_element_type=f32)
    z_output = scatter_rows(second).astype(bf16)
    logits = jnp.dot(z_output, weight_out, preferred_element_type=f32) + class_bias
    likelihood = jax.nn.softmax(logits, axis=-1)
    onehot = labels[0][:, None] == jnp.arange(logits.shape[-1], dtype=jnp.int32)[None, :]
    slope = (
        (likelihood - onehot.astype(f32)) * train_mask[0][:, None].astype(f32) * scale
    ).astype(bf16)
    grad_rows = jnp.einsum(
        "nc,hc->nh", slope, weight_out, preferred_element_type=f32
    ).astype(bf16)
    grad_block = jnp.concatenate([swap(grad_rows, delta) for delta in range(reps)], axis=0)
    out_terms = jnp.einsum("nh,nc->hc", z_output, slope, preferred_element_type=f32)
    grad_out = sum_everywhere(out_terms)
    back = jnp.einsum("nc,nh->ch", dense, grad_block, preferred_element_type=f32)
    pre_slope = (back * factor).astype(bf16)
    in_terms = jnp.einsum("nf,nh->fh", z_columns, pre_slope, preferred_element_type=f32)
    grad_in = sum_everywhere(in_terms)
    return (logits[None], grad_in, grad_out)


def solution(mesh):
    placed = (
        P("blk", "rep", None),
        P("blk", "rep"),
        P("blk", "rep"),
        P("blk", "rep"),
        P("blk", "rep", None, None, None, None),
        P("blk", "rep", None, None),
        P("blk", "rep", None),
        P(),
        P(),
        P(),
    )
    return jax.shard_map(
        on_device,
        mesh=mesh,
        in_specs=placed,
        out_specs=(P("blk", "rep", None), P(), P()),
        check_vma=False,
    )
```

time: 166 us -> 118 us (0.71)
  starting transfers between devices: 94.2 us -> 49.8 us
  local copies, waits for them, and re-layouts: 8.65 us -> 4.28 us
  other arithmetic: 1.4 us -> 5.42 us
  waiting for transfers between devices: 49 us -> 45.9 us
    ppermute x24 -> x8, starting transfers between devices: 51.3 us -> 22.9 us  [to_columns(): pieces.append(lax.ppermute(value, ('rep', 'blk'), pairs))]
    ppermute x24 -> x8, waiting for transfers between devices: 19.9 us -> 2.26 us  [to_columns(): pieces.append(lax.ppermute(value, ('rep', 'blk'), pairs))]
    ppermute x14 -> x12, waiting for transfers between devices: 3.82 us -> 19.4 us  [the longest x10 9.79 us: exchange(): return lax.ppermute(value, 'blk', [(c, c ^ delta) for c in range(blks)])]
    ppermute x14 -> x12, starting transfers between devices: 18.1 us -> 8.05 us  [the longest x10 3.68 us: exchange(): return lax.ppermute(value, 'blk', [(c, c ^ delta) for c in range(blks)])]
    ppermute x21 -> x13, starting transfers between devices: 24.9 us -> 18.9 us  [swap(): return lax.ppermute(value, 'rep', [(r, r ^ delta) for r in range(reps)])]
    unnamed x52 -> x27, local copies, waits for them, and re-layouts: 4.32 us -> 1.01 us
    dynamic_update_slice x7 -> x0, local copies, waits for them, and re-layouts: 3.18 us -> none  [sum_everywhere(): lax.dynamic_update_slice_in_dim(whole, swap(total, delta), (rep_index ^ d...]
    concatenate x0 -> x7, other arithmetic: none -> 2.26 us  [the longest x2 1.35 us: sum_everywhere(): return jnp.concatenate([lower, upper], axis=0)]
  transfers between devices with their start and end apart: 59 -> 33, of which waited for: 21 -> 21; matrix products, arithmetic and copies ran while one was open for 6% -> 8% of each run, Pallas kernels for 1% -> 0%
where the time goes in v3:
time: 118 us; the launch traced here: 117 us
  starting transfers between devices  49.8 us (42%)
  waiting for transfers between devices  45.9 us (39%)
  matrix products  8.53 us (7%)
  other arithmetic  5.42 us (5%)
  local copies, waits for them, and re-layouts  4.28 us (4%)
  Pallas kernels  2.32 us (2%)
  between operations  1.18 us (1%)
    ppermute x13, waiting for transfers between devices, swap(): return lax.ppermute(value, 'rep', [(r, r ^ delta) for r in range(reps)])  24.2 us
    ppermute x8, starting transfers between devices, to_columns(): pieces.append(lax.ppermute(value, ('rep', 'blk'), pairs))  22.9 us
    ppermute x13, starting transfers between devices, swap(): return lax.ppermute(value, 'rep', [(r, r ^ delta) for r in range(reps)])  18.9 us
    ppermute x10, waiting for transfers between devices, exchange(): return lax.ppermute(value, 'blk', [(c, c ^ delta) for c in range(blks)])  9.79 us
    ppermute x1, waiting for transfers between devices, on_device(): lax.ppermute(tile_values[0, 0, j], ('rep', 'blk'), pairs)  7.51 us
    dot_general x1, matrix products, on_device(): jnp.einsum('nf,nh->fh', z_columns, pre_slope, preferred_element_type=f32)  4.61 us
    ppermute x10, starting transfers between devices, exchange(): return lax.ppermute(value, 'blk', [(c, c ^ delta) for c in range(blks)])  3.68 us
    ppermute x1, starting transfers between devices, on_device(): other_place.append(lax.ppermute(place[j], ('rep', 'blk'), pairs))  2.46 us
  transfers between devices with their start and end apart: 33, of which 21 were waited for; matrix products, arithmetic and copies ran while one was open for 8% of the time, Pallas kernels for 0%

profile of v3, /device:TPU:0, one launch (start us, length us, event | category | flops | bytes accessed | tf_op | source)
XLA Modules:
  0.0 117.5 jit_solution(13771232646818582370)
XLA Ops:
  3.0 6.8 %collective-permute-start.3 = (bf16[272,128]{1,0:T(8,128)(2,1)S(1)}, bf16[272,128]{1,0:T(8,128)(2,1)S(1)}, u32[]{:S(2)}, u32[]{:S(2)}) collective-permute-start(bf16[272,128]{1,0:T(8,128)(2,1)S(1)} %pad_maximum_fusion.4), channel_id=1, source_target_pairs={{0,10},{1,11},{2,12},{3,13},{4,14},{5,15},{6,8},{7,9},{8,0},{9,1},... | collective-permute-start | bytes 208904 | tf_op jit(solution)/shard_map/ppermute | solution.py:124
  9.8 1.3 %collective-permute-start.4 = (bf16[272,128]{1,0:T(8,128)(2,1)S(1)}, bf16[272,128]{1,0:T(8,128)(2,1)S(1)}, u32[]{:S(2)}, u32[]{:S(2)}) collective-permute-start(bf16[272,128]{1,0:T(8,128)(2,1)S(1)} %pad_maximum_fusion.4), channel_id=1, source_target_pairs={{0,20},{1,21},{2,22},{3,23},{4,16},{5,17},{6,18},{7,19},{8,30},{9,... | collective-permute-start | bytes 208904 | tf_op jit(solution)/shard_map/ppermute | solution.py:124
  11.1 3.0 %collective-permute-start.5 = (bf16[272,128]{1,0:T(8,128)(2,1)S(1)}, bf16[272,128]{1,0:T(8,128)(2,1)S(1)}, u32[]{:S(2)}, u32[]{:S(2)}) collective-permute-start(bf16[272,128]{1,0:T(8,128)(2,1)S(1)} %pad_maximum_fusion.4), channel_id=1, source_target_pairs={{0,30},{1,31},{2,24},{3,25},{4,26},{5,27},{6,28},{7,29},{8,20},{9,... | collective-permute-start | bytes 208904 | tf_op jit(solution)/shard_map/ppermute | solution.py:124
  14.9 2.5 %collective-permute-start = (s32[16]{0:T(128)S(1)}, s32[16]{0:T(128)S(1)}, u32[]{:S(2)}, u32[]{:S(2)}) collective-permute-start(s32[16]{0:T(128)S(1)} %get-tuple-element.20), channel_id=1, source_target_pairs={{0,8},{2,10},{4,12},{6,14},{8,16},{10,18},{12,20},{14,22},{16,24},... | collective-permute-start | bytes 200 | tf_op jit(solution)/shard_map/ppermute | solution.py:173
  19.1 2.1 %collective-permute-done = s32[16]{0:T(128)S(1)} collective-permute-done((s32[16]{0:T(128)S(1)}, s32[16]{0:T(128)S(1)}, u32[]{:S(2)}, u32[]{:S(2)}) %collective-permute-start) | collective-permute-done | bytes 96 | tf_op jit(solution)/shard_map/ppermute | solution.py:173
  21.2 1.9 %collective-permute-start.1 = (bf16[16,128,128]{2,1,0:T(8,128)(2,1)S(1)}, bf16[16,128,128]{2,1,0:T(8,128)(2,1)S(1)}, u32[]{:S(2)}, u32[]{:S(2)}) collective-permute-start(bf16[16,128,128]{2,1,0:T(8,128)(2,1)S(1)} %slice_bitcast_fusion), channel_id=1, source_target_pairs={{0,8},{2,10},{4,12},{6,14},{8,16},{10,18},{12,20},{14,22},{16,24},... | collective-permute-start | bytes 1572872 | tf_op jit(solution)/shard_map/ppermute | solution.py:172
  24.0 1.5 %collective-permute-done.6 = bf16[1088,128]{1,0:T(8,128)(2,1)S(1)} collective-permute-done((bf16[1088,128]{1,0:T(8,128)(2,1)S(1)}, bf16[1088,128]{1,0:T(8,128)(2,1)S(1)}, u32[]{:S(2)}, u32[]{:S(2)}) %collective-permute-start.6) | collective-permute-done | bytes 278560 | tf_op jit(solution)/shard_map/ppermute | solution.py:114
  25.6 7.5 %collective-permute-done.1 = bf16[16,128,128]{2,1,0:T(8,128)(2,1)S(1)} collective-permute-done((bf16[16,128,128]{2,1,0:T(8,128)(2,1)S(1)}, bf16[16,128,128]{2,1,0:T(8,128)(2,1)S(1)}, u32[]{:S(2)}, u32[]{:S(2)}) %collective-permute-start.1) | collective-permute-done | bytes 524320 | tf_op jit(solution)/shard_map/ppermute | solution.py:172
  33.1 2.3 %dense_tiles.1 = bf16[1024,2048]{1,0:T(8,128)(2,1)S(1)} custom-call(s32[1]{0:T(128)} %bitcast.spot_ref, s32[2]{0:T(128)S(1)} %and_select_fusion.1.order_ref, s32[2]{0:T(128)S(1)} %get-tuple-element.23.moved_ref, s32[2,16]{1,0:T(2,128)S(1)} %broadcast_select_fusion.4.place_ref, bf16[2,16,128,128]{3,2,1,0:T(8,128)(2,1)S(1)} %bitcast.49, ...), custom_call_target="tpu_custom_call" | custom-call | bytes 4194304 | tf_op jit(solution)/shard_map/dense_tiles/pallas_call | solution.py:62
  37.4 3.0 %collective-permute-start.9 = (f32[256,128]{1,0:T(8,128)S(1)}, f32[256,128]{1,0:T(8,128)S(1)}, u32[]{:S(2)}, u32[]{:S(2)}) collective-permute-start(f32[256,128]{1,0:T(8,128)S(1)} %get-tuple-element.13), channel_id=1, source_target_pairs={{0,24},{8,16},{16,8},{24,0},{1,25},{9,17},{17,9},{25,1},{2,26},{10... | collective-permute-start | bytes 393224 | tf_op jit(solution)/shard_map/ppermute | solution.py:111
  40.4 2.2 %collective-permute-done.7 = f32[256,128]{1,0:T(8,128)S(1)} collective-permute-done((f32[256,128]{1,0:T(8,128)S(1)}, f32[256,128]{1,0:T(8,128)S(1)}, u32[]{:S(2)}, u32[]{:S(2)}) %collective-permute-start.7) | collective-permute-done | bytes 131104 | tf_op jit(solution)/shard_map/ppermute | solution.py:111
  44.3 4.8 %collective-permute-start.11 = (bf16[256,128]{1,0:T(8,128)(2,1)S(1)}, bf16[256,128]{1,0:T(8,128)(2,1)S(1)}, u32[]{:S(2)}, u32[]{:S(2)}) collective-permute-start(bf16[256,128]{1,0:T(8,128)(2,1)S(1)} %fusion.34), channel_id=1, source_target_pairs={{0,10},{1,11},{2,12},{3,13},{4,14},{5,15},{6,8},{7,9},{8,0},{9,1},... | collective-permute-start | bytes 196616 | tf_op jit(solution)/shard_map/ppermute | solution.py:124
  49.1 2.8 %collective-permute-start.12 = (bf16[256,128]{1,0:T(8,128)(2,1)S(1)}, bf16[256,128]{1,0:T(8,128)(2,1)S(1)}, u32[]{:S(2)}, u32[]{:S(2)}) collective-permute-start(bf16[256,128]{1,0:T(8,128)(2,1)S(1)} %fusion.34), channel_id=1, source_target_pairs={{0,20},{1,21},{2,22},{3,23},{4,16},{5,17},{6,18},{7,19},{8,30},{9,... | collective-permute-start | bytes 196616 | tf_op jit(solution)/shard_map/ppermute | solution.py:124
  51.9 2.9 %collective-permute-start.13 = (bf16[256,128]{1,0:T(8,128)(2,1)S(1)}, bf16[256,128]{1,0:T(8,128)(2,1)S(1)}, u32[]{:S(2)}, u32[]{:S(2)}) collective-permute-start(bf16[256,128]{1,0:T(8,128)(2,1)S(1)} %fusion.34), channel_id=1, source_target_pairs={{0,30},{1,31},{2,24},{3,25},{4,26},{5,27},{6,28},{7,29},{8,20},{9,... | collective-permute-start | bytes 196616 | tf_op jit(solution)/shard_map/ppermute | solution.py:124
  54.8 2.2 %collective-permute-done.13 = bf16[256,128]{1,0:T(8,128)(2,1)S(1)} collective-permute-done((bf16[256,128]{1,0:T(8,128)(2,1)S(1)}, bf16[256,128]{1,0:T(8,128)(2,1)S(1)}, u32[]{:S(2)}, u32[]{:S(2)}) %collective-permute-start.13) | collective-permute-done | bytes 65568 | tf_op jit(solution)/shard_map/ppermute | solution.py:124
  57.2 1.5 %collective-permute-done.14 = bf16[1024,128]{1,0:T(8,128)(2,1)S(1)} collective-permute-done((bf16[1024,128]{1,0:T(8,128)(2,1)S(1)}, bf16[1024,128]{1,0:T(8,128)(2,1)S(1)}, u32[]{:S(2)}, u32[]{:S(2)}) %collective-permute-start.14) | collective-permute-done | bytes 262176 | tf_op jit(solution)/shard_map/ppermute | solution.py:114
  59.2 1.6 %fusion.6 = f32[1024,256]{1,0:T(8,128)S(1)} fusion(bf16[1024,2048]{1,0:T(8,128)(2,1)S(1)} %dense_tiles.1, f32[2048,256]{1,0:T(8,128)S(1)} %fusion.67, s32[256]{0:T(256)S(1)} %iota_multiply_fusion, s32[2048]{0:T(1024)S(1)} %broadcast_multiply_fusion), kind=kOutput, calls=%fused_computation.15 | convolution fusion | flops 1080557568 | bytes 7349248 | tf_op jit(solution)/shard_map/dot_general | solution.py:202
  61.7 6.1 %collective-permute-start.15 = (f32[256,256]{1,0:T(8,128)}, f32[256,256]{1,0:T(8,128)S(1)}, u32[]{:S(2)}, u32[]{:S(2)}) collective-permute-start(f32[256,256]{1,0:T(8,128)} %get-tuple-element.9), channel_id=1, source_target_pairs={{0,8},{8,0},{16,24},{24,16},{1,9},{9,1},{17,25},{25,17},{2,10},{10... | collective-permute-start | bytes 786440 | tf_op jit(solution)/shard_map/ppermute | solution.py:111
  67.8 1.5 %collective-permute-start.17 = (f32[256,256]{1,0:T(8,128)}, f32[256,256]{1,0:T(8,128)}, u32[]{:S(2)}, u32[]{:S(2)}) collective-permute-start(f32[256,256]{1,0:T(8,128)} %get-tuple-element.10), channel_id=1, source_target_pairs={{0,24},{8,16},{16,8},{24,0},{1,25},{9,17},{17,9},{25,1},{2,26},{10... | collective-permute-start | bytes 786440 | tf_op jit(solution)/shard_map/ppermute | solution.py:111
  69.3 5.8 %collective-permute-done.15 = f32[256,256]{1,0:T(8,128)S(1)} collective-permute-done((f32[256,256]{1,0:T(8,128)}, f32[256,256]{1,0:T(8,128)S(1)}, u32[]{:S(2)}, u32[]{:S(2)}) %collective-permute-start.15) | collective-permute-done | bytes 262176 | tf_op jit(solution)/shard_map/ppermute | solution.py:111
  75.1 6.7 %collective-permute-done.16 = f32[256,256]{1,0:T(8,128)} collective-permute-done((f32[256,256]{1,0:T(8,128)}, f32[256,256]{1,0:T(8,128)}, u32[]{:S(2)}, u32[]{:S(2)}) %collective-permute-start.16) | collective-permute-done | bytes 262176 | tf_op jit(solution)/shard_map/ppermute | solution.py:111
  83.9 1.5 %collective-permute-start.19 = (bf16[256,256]{1,0:T(8,128)(2,1)S(1)}, bf16[256,256]{1,0:T(8,128)(2,1)}, u32[]{:S(2)}, u32[]{:S(2)}) collective-permute-start(bf16[256,256]{1,0:T(8,128)(2,1)S(1)} %convolution_convert_fusion), channel_id=1, source_target_pairs={{0,16},{8,24},{16,0},{24,8},{1,17},{9,25},{17,1},{25,9},{2,18},{10... | collective-permute-start | bytes 393224 | tf_op jit(solution)/shard_map/ppermute | solution.py:111
  85.3 1.8 %collective-permute-start.20 = (bf16[256,256]{1,0:T(8,128)(2,1)S(1)}, bf16[256,256]{1,0:T(8,128)(2,1)}, u32[]{:S(2)}, u32[]{:S(2)}) collective-permute-start(bf16[256,256]{1,0:T(8,128)(2,1)S(1)} %convolution_convert_fusion), channel_id=1, source_target_pairs={{0,24},{8,16},{16,8},{24,0},{1,25},{9,17},{17,9},{25,1},{2,26},{10... | collective-permute-start | bytes 393224 | tf_op jit(solution)/shard_map/ppermute | solution.py:111
  88.2 1.3 %collective-permute-done.18 = bf16[256,256]{1,0:T(8,128)(2,1)S(1)} collective-permute-done((bf16[256,256]{1,0:T(8,128)(2,1)S(1)}, bf16[256,256]{1,0:T(8,128)(2,1)S(1)}, u32[]{:S(2)}, u32[]{:S(2)}) %collective-permute-start.18) | collective-permute-done | bytes 131104 | tf_op jit(solution)/shard_map/ppermute | solution.py:111
  89.5 2.3 %collective-permute-done.19 = bf16[256,256]{1,0:T(8,128)(2,1)} collective-permute-done((bf16[256,256]{1,0:T(8,128)(2,1)S(1)}, bf16[256,256]{1,0:T(8,128)(2,1)}, u32[]{:S(2)}, u32[]{:S(2)}) %collective-permute-start.19) | collective-permute-done | bytes 131104 | tf_op jit(solution)/shard_map/ppermute | solution.py:111
  91.8 4.6 %fusion.5 = f32[128,256]{1,0:T(8,128)S(1)} fusion(bf16[2048,128]{1,0:T(8,128)(2,1)S(1)} %copy-done.4, bf16[1024,2048]{1,0:T(8,128)(2,1)} %copy-done.1, f32[2048,256]{1,0:T(8,128)S(1)} %fusion.67, s32[256]{0:T(256)S(1)} %iota_multiply_fusion, s32[2048]{0:T(1024)S(1)} %broadcast_multiply_fusion, bf16[256,256]{1,0:T(8,128)(2,1)} %collective-permute-done.20, ...), kind=kOutput, calls=%fused_computation.14 | convolution fusion | flops 1217396736 | bytes 7480320 | tf_op jit(solution)/shard_map/nf,nh->fh/dot_general | solution.py:218
  98.7 2.1 %collective-permute-done.28 = bf16[128,172]{0,1:T(8,128)(2,1)S(1)} collective-permute-done((bf16[128,172]{0,1:T(8,128)(2,1)S(1)}, bf16[128,172]{0,1:T(8,128)(2,1)S(1)}, u32[]{:S(2)}, u32[]{:S(2)}) %collective-permute-start.28) | collective-permute-done | bytes 44064 | tf_op jit(solution)/shard_map/ppermute | solution.py:114
  101.7 2.2 %collective-permute-start.23 = (bf16[64,256]{1,0:T(8,128)(2,1)S(1)}, bf16[64,256]{1,0:T(8,128)(2,1)S(1)}, u32[]{:S(2)}, u32[]{:S(2)}) collective-permute-start(bf16[64,256]{1,0:T(8,128)(2,1)S(1)} %add_convert_fusion.6), channel_id=1, source_target_pairs={{0,4},{1,5},{2,6},{3,7},{4,0},{5,1},{6,2},{7,3},{8,12},{9,13},{10,... | collective-permute-start | bytes 98312 | tf_op jit(solution)/shard_map/ppermute | solution.py:114
  103.9 2.3 %collective-permute-done.29 = bf16[128,172]{0,1:T(8,128)(2,1)S(1)} collective-permute-done((bf16[128,172]{0,1:T(8,128)(2,1)S(1)}, bf16[128,172]{0,1:T(8,128)(2,1)S(1)}, u32[]{:S(2)}, u32[]{:S(2)}) %collective-permute-start.29) | collective-permute-done | bytes 44064 | tf_op jit(solution)/shard_map/ppermute | solution.py:114
  106.2 1.3 %collective-permute-start.30 = (bf16[128,172]{0,1:T(8,128)(2,1)S(1)}, bf16[128,172]{0,1:T(8,128)(2,1)S(1)}, u32[]{:S(2)}, u32[]{:S(2)}) collective-permute-start(bf16[128,172]{0,1:T(8,128)(2,1)S(1)} %add_convert_fusion.1), channel_id=1, source_target_pairs={{0,8},{8,0},{16,24},{24,16},{1,9},{9,1},{17,25},{25,17},{2,10},{10... | collective-permute-start | bytes 132104 | tf_op jit(solution)/shard_map/ppermute | solution.py:111
  108.4 1.9 %collective-permute-done.30 = bf16[128,172]{0,1:T(8,128)(2,1)S(1)} collective-permute-done((bf16[128,172]{0,1:T(8,128)(2,1)S(1)}, bf16[128,172]{0,1:T(8,128)(2,1)S(1)}, u32[]{:S(2)}, u32[]{:S(2)}) %collective-permute-start.30) | collective-permute-done | bytes 44064 | tf_op jit(solution)/shard_map/ppermute | solution.py:111
  112.5 1.9 %collective-permute-done.31 = bf16[128,172]{0,1:T(8,128)(2,1)S(1)} collective-permute-done((bf16[128,172]{0,1:T(8,128)(2,1)S(1)}, bf16[128,172]{0,1:T(8,128)(2,1)S(1)}, u32[]{:S(2)}, u32[]{:S(2)}) %collective-permute-start.31) | collective-permute-done | bytes 44064 | tf_op jit(solution)/shard_map/ppermute | solution.py:111
  (121 shorter events, 23.4 us)
Async XLA Ops:
  2.3 21.4 %collective-permute-start.2 = (bf16[272,128]{1,0:T(8,128)(2,1)S(1)}, bf16[272,128]{1,0:T(8,128)(2,1)S(1)}, u32[]{:S(2)}, u32[]{:S(2)}) collective-permute-start(bf16[272,128]{1,0:T(8,128)(2,1)S(1)} %pad_maximum_fusion.4), channel_id=1, source_target_pairs={{0,0},{1,1},{2,2},{3,3},{4,4},{5,5},{6,6},{7,7},{8,10},{9,11},{10,... | collective-permute-start | bytes 208904 | tf_op jit(solution)/shard_map/ppermute | solution.py:124
  3.0 20.8 %collective-permute-start.3 = (bf16[272,128]{1,0:T(8,128)(2,1)S(1)}, bf16[272,128]{1,0:T(8,128)(2,1)S(1)}, u32[]{:S(2)}, u32[]{:S(2)}) collective-permute-start(bf16[272,128]{1,0:T(8,128)(2,1)S(1)} %pad_maximum_fusion.4), channel_id=1, source_target_pairs={{0,10},{1,11},{2,12},{3,13},{4,14},{5,15},{6,8},{7,9},{8,0},{9,1},... | collective-permute-start | bytes 208904 | tf_op jit(solution)/shard_map/ppermute | solution.py:124
  9.8 14.0 %collective-permute-start.4 = (bf16[272,128]{1,0:T(8,128)(2,1)S(1)}, bf16[272,128]{1,0:T(8,128)(2,1)S(1)}, u32[]{:S(2)}, u32[]{:S(2)}) collective-permute-start(bf16[272,128]{1,0:T(8,128)(2,1)S(1)} %pad_maximum_fusion.4), channel_id=1, source_target_pairs={{0,20},{1,21},{2,22},{3,23},{4,16},{5,17},{6,18},{7,19},{8,30},{9,... | collective-permute-start | bytes 208904 | tf_op jit(solution)/shard_map/ppermute | solution.py:124
  11.1 12.7 %collective-permute-start.5 = (bf16[272,128]{1,0:T(8,128)(2,1)S(1)}, bf16[272,128]{1,0:T(8,128)(2,1)S(1)}, u32[]{:S(2)}, u32[]{:S(2)}) collective-permute-start(bf16[272,128]{1,0:T(8,128)(2,1)S(1)} %pad_maximum_fusion.4), channel_id=1, source_target_pairs={{0,30},{1,31},{2,24},{3,25},{4,26},{5,27},{6,28},{7,29},{8,20},{9,... | collective-permute-start | bytes 208904 | tf_op jit(solution)/shard_map/ppermute | solution.py:124
  14.9 6.3 %collective-permute-start = (s32[16]{0:T(128)S(1)}, s32[16]{0:T(128)S(1)}, u32[]{:S(2)}, u32[]{:S(2)}) collective-permute-start(s32[16]{0:T(128)S(1)} %get-tuple-element.20), channel_id=1, source_target_pairs={{0,8},{2,10},{4,12},{6,14},{8,16},{10,18},{12,20},{14,22},{16,24},... | collective-permute-start | bytes 200 | tf_op jit(solution)/shard_map/ppermute | solution.py:173
  21.2 12.0 %collective-permute-start.1 = (bf16[16,128,128]{2,1,0:T(8,128)(2,1)S(1)}, bf16[16,128,128]{2,1,0:T(8,128)(2,1)S(1)}, u32[]{:S(2)}, u32[]{:S(2)}) collective-permute-start(bf16[16,128,128]{2,1,0:T(8,128)(2,1)S(1)} %slice_bitcast_fusion), channel_id=1, source_target_pairs={{0,8},{2,10},{4,12},{6,14},{8,16},{10,18},{12,20},{14,22},{16,24},... | collective-permute-start | bytes 1572872 | tf_op jit(solution)/shard_map/ppermute | solution.py:172
  23.8 1.6 %collective-permute-start.6 = (bf16[1088,128]{1,0:T(8,128)(2,1)S(1)}, bf16[1088,128]{1,0:T(8,128)(2,1)S(1)}, u32[]{:S(2)}, u32[]{:S(2)}) collective-permute-start(bf16[1088,128]{1,0:T(8,128)(2,1)S(1)} %pad_maximum_fusion), channel_id=1, source_target_pairs={{0,1},{1,0},{2,3},{3,2},{4,5},{5,4},{6,7},{7,6},{8,9},{9,8},{10,11... | collective-permute-start | bytes 835592 | tf_op jit(solution)/shard_map/ppermute | solution.py:114
  36.8 5.7 %collective-permute-start.7 = (f32[256,128]{1,0:T(8,128)S(1)}, f32[256,128]{1,0:T(8,128)S(1)}, u32[]{:S(2)}, u32[]{:S(2)}) collective-permute-start(f32[256,128]{1,0:T(8,128)S(1)} %get-tuple-element.12), channel_id=1, source_target_pairs={{0,8},{8,0},{16,24},{24,16},{1,9},{9,1},{17,25},{25,17},{2,10},{10... | collective-permute-start | bytes 393224 | tf_op jit(solution)/shard_map/ppermute | solution.py:111
  36.9 5.6 %collective-permute-start.8 = (f32[256,128]{1,0:T(8,128)S(1)}, f32[256,128]{1,0:T(8,128)S(1)}, u32[]{:S(2)}, u32[]{:S(2)}) collective-permute-start(f32[256,128]{1,0:T(8,128)S(1)} %get-tuple-element.14), channel_id=1, source_target_pairs={{0,16},{8,24},{16,0},{24,8},{1,17},{9,25},{17,1},{25,9},{2,18},{10... | collective-permute-start | bytes 393224 | tf_op jit(solution)/shard_map/ppermute | solution.py:111
  37.4 6.2 %collective-permute-start.9 = (f32[256,128]{1,0:T(8,128)S(1)}, f32[256,128]{1,0:T(8,128)S(1)}, u32[]{:S(2)}, u32[]{:S(2)}) collective-permute-start(f32[256,128]{1,0:T(8,128)S(1)} %get-tuple-element.13), channel_id=1, source_target_pairs={{0,24},{8,16},{16,8},{24,0},{1,25},{9,17},{17,9},{25,1},{2,26},{10... | collective-permute-start | bytes 393224 | tf_op jit(solution)/shard_map/ppermute | solution.py:111
  43.6 11.1 %collective-permute-start.10 = (bf16[256,128]{1,0:T(8,128)(2,1)S(1)}, bf16[256,128]{1,0:T(8,128)(2,1)S(1)}, u32[]{:S(2)}, u32[]{:S(2)}) collective-permute-start(bf16[256,128]{1,0:T(8,128)(2,1)S(1)} %fusion.34), channel_id=1, source_target_pairs={{0,0},{1,1},{2,2},{3,3},{4,4},{5,5},{6,6},{7,7},{8,10},{9,11},{10,... | collective-permute-start | bytes 196616 | tf_op jit(solution)/shard_map/ppermute | solution.py:124
  44.3 10.5 %collective-permute-start.11 = (bf16[256,128]{1,0:T(8,128)(2,1)S(1)}, bf16[256,128]{1,0:T(8,128)(2,1)S(1)}, u32[]{:S(2)}, u32[]{:S(2)}) collective-permute-start(bf16[256,128]{1,0:T(8,128)(2,1)S(1)} %fusion.34), channel_id=1, source_target_pairs={{0,10},{1,11},{2,12},{3,13},{4,14},{5,15},{6,8},{7,9},{8,0},{9,1},... | collective-permute-start | bytes 196616 | tf_op jit(solution)/shard_map/ppermute | solution.py:124
  49.1 5.7 %collective-permute-start.12 = (bf16[256,128]{1,0:T(8,128)(2,1)S(1)}, bf16[256,128]{1,0:T(8,128)(2,1)S(1)}, u32[]{:S(2)}, u32[]{:S(2)}) collective-permute-start(bf16[256,128]{1,0:T(8,128)(2,1)S(1)} %fusion.34), channel_id=1, source_target_pairs={{0,20},{1,21},{2,22},{3,23},{4,16},{5,17},{6,18},{7,19},{8,30},{9,... | collective-permute-start | bytes 196616 | tf_op jit(solution)/shard_map/ppermute | solution.py:124
  51.9 5.2 %collective-permute-start.13 = (bf16[256,128]{1,0:T(8,128)(2,1)S(1)}, bf16[256,128]{1,0:T(8,128)(2,1)S(1)}, u32[]{:S(2)}, u32[]{:S(2)}) collective-permute-start(bf16[256,128]{1,0:T(8,128)(2,1)S(1)} %fusion.34), channel_id=1, source_target_pairs={{0,30},{1,31},{2,24},{3,25},{4,26},{5,27},{6,28},{7,29},{8,20},{9,... | collective-permute-start | bytes 196616 | tf_op jit(solution)/shard_map/ppermute | solution.py:124
  57.1 1.6 %collective-permute-start.14 = (bf16[1024,128]{1,0:T(8,128)(2,1)S(1)}, bf16[1024,128]{1,0:T(8,128)(2,1)S(1)}, u32[]{:S(2)}, u32[]{:S(2)}) collective-permute-start(bf16[1024,128]{1,0:T(8,128)(2,1)S(1)} %pad_maximum_fusion.1), channel_id=1, source_target_pairs={{0,1},{1,0},{2,3},{3,2},{4,5},{5,4},{6,7},{7,6},{8,9},{9,8},{10,11... | collective-permute-start | bytes 786440 | tf_op jit(solution)/shard_map/ppermute | solution.py:114
  61.7 13.4 %collective-permute-start.15 = (f32[256,256]{1,0:T(8,128)}, f32[256,256]{1,0:T(8,128)S(1)}, u32[]{:S(2)}, u32[]{:S(2)}) collective-permute-start(f32[256,256]{1,0:T(8,128)} %get-tuple-element.9), channel_id=1, source_target_pairs={{0,8},{8,0},{16,24},{24,16},{1,9},{9,1},{17,25},{25,17},{2,10},{10... | collective-permute-start | bytes 786440 | tf_op jit(solution)/shard_map/ppermute | solution.py:111
  67.8 14.0 %collective-permute-start.16 = (f32[256,256]{1,0:T(8,128)}, f32[256,256]{1,0:T(8,128)}, u32[]{:S(2)}, u32[]{:S(2)}) collective-permute-start(f32[256,256]{1,0:T(8,128)} %get-tuple-element.11), channel_id=1, source_target_pairs={{0,16},{8,24},{16,0},{24,8},{1,17},{9,25},{17,1},{25,9},{2,18},{10... | collective-permute-start | bytes 786440 | tf_op jit(solution)/shard_map/ppermute | solution.py:111
  67.8 14.0 %collective-permute-start.17 = (f32[256,256]{1,0:T(8,128)}, f32[256,256]{1,0:T(8,128)}, u32[]{:S(2)}, u32[]{:S(2)}) collective-permute-start(f32[256,256]{1,0:T(8,128)} %get-tuple-element.10), channel_id=1, source_target_pairs={{0,24},{8,16},{16,8},{24,0},{1,25},{9,17},{17,9},{25,1},{2,26},{10... | collective-permute-start | bytes 786440 | tf_op jit(solution)/shard_map/ppermute | solution.py:111
  83.5 6.0 %collective-permute-start.18 = (bf16[256,256]{1,0:T(8,128)(2,1)S(1)}, bf16[256,256]{1,0:T(8,128)(2,1)S(1)}, u32[]{:S(2)}, u32[]{:S(2)}) collective-permute-start(bf16[256,256]{1,0:T(8,128)(2,1)S(1)} %convolution_convert_fusion), channel_id=1, source_target_pairs={{0,8},{8,0},{16,24},{24,16},{1,9},{9,1},{17,25},{25,17},{2,10},{10... | collective-permute-start | bytes 393224 | tf_op jit(solution)/shard_map/ppermute | solution.py:111
  83.9 7.9 %collective-permute-start.19 = (bf16[256,256]{1,0:T(8,128)(2,1)S(1)}, bf16[256,256]{1,0:T(8,128)(2,1)}, u32[]{:S(2)}, u32[]{:S(2)}) collective-permute-start(bf16[256,256]{1,0:T(8,128)(2,1)S(1)} %convolution_convert_fusion), channel_id=1, source_target_pairs={{0,16},{8,24},{16,0},{24,8},{1,17},{9,25},{17,1},{25,9},{2,18},{10... | collective-permute-start | bytes 393224 | tf_op jit(solution)/shard_map/ppermute | solution.py:111
  85.3 6.4 %collective-permute-start.20 = (bf16[256,256]{1,0:T(8,128)(2,1)S(1)}, bf16[256,256]{1,0:T(8,128)(2,1)}, u32[]{:S(2)}, u32[]{:S(2)}) collective-permute-start(bf16[256,256]{1,0:T(8,128)(2,1)S(1)} %convolution_convert_fusion), channel_id=1, source_target_pairs={{0,24},{8,16},{16,8},{24,0},{1,25},{9,17},{17,9},{25,1},{2,26},{10... | collective-permute-start | bytes 393224 | tf_op jit(solution)/shard_map/ppermute | solution.py:111
  87.3 9.2 %collective-permute-start.27 = (f32[128,172]{0,1:T(8,128)S(1)}, f32[128,172]{0,1:T(8,128)S(1)}, u32[]{:S(2)}, u32[]{:S(2)}) collective-permute-start(f32[128,172]{0,1:T(8,128)S(1)} %constant_dynamic-slice_fusion), channel_id=1, source_target_pairs={{0,1},{1,0},{2,3},{3,2},{4,5},{5,4},{6,7},{7,6},{8,9},{9,8},{10,11... | collective-permute-start | bytes 264200 | tf_op jit(solution)/shard_map/ppermute | solution.py:114
  96.4 1.3 %collective-permute-start.21 = (f32[64,256]{1,0:T(8,128)S(1)}, f32[64,256]{1,0:T(8,128)S(1)}, u32[]{:S(2)}, u32[]{:S(2)}) collective-permute-start(f32[64,256]{1,0:T(8,128)S(1)} %constant_dynamic-slice_fusion.1), channel_id=1, source_target_pairs={{0,1},{1,0},{2,3},{3,2},{4,5},{5,4},{6,7},{7,6},{8,9},{9,8},{10,11... | collective-permute-start | bytes 196616 | tf_op jit(solution)/shard_map/ppermute | solution.py:114
  96.5 4.3 %collective-permute-start.28 = (bf16[128,172]{0,1:T(8,128)(2,1)S(1)}, bf16[128,172]{0,1:T(8,128)(2,1)S(1)}, u32[]{:S(2)}, u32[]{:S(2)}) collective-permute-start(bf16[128,172]{0,1:T(8,128)(2,1)S(1)} %add_convert_fusion.3), channel_id=1, source_target_pairs={{0,2},{1,3},{2,0},{3,1},{4,6},{5,7},{6,4},{7,5},{8,10},{9,11},{10,... | collective-permute-start | bytes 132104 | tf_op jit(solution)/shard_map/ppermute | solution.py:114
  97.7 4.0 %collective-permute-start.22 = (bf16[64,256]{1,0:T(8,128)(2,1)S(1)}, bf16[64,256]{1,0:T(8,128)(2,1)S(1)}, u32[]{:S(2)}, u32[]{:S(2)}) collective-permute-start(bf16[64,256]{1,0:T(8,128)(2,1)S(1)} %add_convert_fusion.7), channel_id=1, source_target_pairs={{0,2},{1,3},{2,0},{3,1},{4,6},{5,7},{6,4},{7,5},{8,10},{9,11},{10,... | collective-permute-start | bytes 98312 | tf_op jit(solution)/shard_map/ppermute | solution.py:114
  100.8 5.4 %collective-permute-start.29 = (bf16[128,172]{0,1:T(8,128)(2,1)S(1)}, bf16[128,172]{0,1:T(8,128)(2,1)S(1)}, u32[]{:S(2)}, u32[]{:S(2)}) collective-permute-start(bf16[128,172]{0,1:T(8,128)(2,1)S(1)} %add_convert_fusion.2), channel_id=1, source_target_pairs={{0,4},{1,5},{2,6},{3,7},{4,0},{5,1},{6,2},{7,3},{8,12},{9,13},{10,... | collective-permute-start | bytes 132104 | tf_op jit(solution)/shard_map/ppermute | solution.py:114
  101.7 5.7 %collective-permute-start.23 = (bf16[64,256]{1,0:T(8,128)(2,1)S(1)}, bf16[64,256]{1,0:T(8,128)(2,1)S(1)}, u32[]{:S(2)}, u32[]{:S(2)}) collective-permute-start(bf16[64,256]{1,0:T(8,128)(2,1)S(1)} %add_convert_fusion.6), channel_id=1, source_target_pairs={{0,4},{1,5},{2,6},{3,7},{4,0},{5,1},{6,2},{7,3},{8,12},{9,13},{10,... | collective-permute-start | bytes 98312 | tf_op jit(solution)/shard_map/ppermute | solution.py:114
  106.2 4.1 %collective-permute-start.30 = (bf16[128,172]{0,1:T(8,128)(2,1)S(1)}, bf16[128,172]{0,1:T(8,128)(2,1)S(1)}, u32[]{:S(2)}, u32[]{:S(2)}) collective-permute-start(bf16[128,172]{0,1:T(8,128)(2,1)S(1)} %add_convert_fusion.1), channel_id=1, source_target_pairs={{0,8},{8,0},{16,24},{24,16},{1,9},{9,1},{17,25},{25,17},{2,10},{10... | collective-permute-start | bytes 132104 | tf_op jit(solution)/shard_map/ppermute | solution.py:111
  107.5 4.0 %collective-permute-start.24 = (bf16[64,256]{1,0:T(8,128)(2,1)S(1)}, bf16[64,256]{1,0:T(8,128)(2,1)S(1)}, u32[]{:S(2)}, u32[]{:S(2)}) collective-permute-start(bf16[64,256]{1,0:T(8,128)(2,1)S(1)} %add_convert_fusion.5), channel_id=1, source_target_pairs={{0,8},{8,0},{16,24},{24,16},{1,9},{9,1},{17,25},{25,17},{2,10},{10... | collective-permute-start | bytes 98312 | tf_op jit(solution)/shard_map/ppermute | solution.py:111
  110.3 4.1 %collective-permute-start.31 = (bf16[128,172]{0,1:T(8,128)(2,1)S(1)}, bf16[128,172]{0,1:T(8,128)(2,1)S(1)}, u32[]{:S(2)}, u32[]{:S(2)}) collective-permute-start(bf16[128,172]{0,1:T(8,128)(2,1)S(1)} %add_convert_fusion), channel_id=1, source_target_pairs={{0,16},{8,24},{16,0},{24,8},{1,17},{9,25},{17,1},{25,9},{2,18},{10... | collective-permute-start | bytes 132104 | tf_op jit(solution)/shard_map/ppermute | solution.py:111
  111.5 4.0 %collective-permute-start.25 = (bf16[64,256]{1,0:T(8,128)(2,1)S(1)}, bf16[64,256]{1,0:T(8,128)(2,1)S(1)}, u32[]{:S(2)}, u32[]{:S(2)}) collective-permute-start(bf16[64,256]{1,0:T(8,128)(2,1)S(1)} %add_convert_fusion.4), channel_id=1, source_target_pairs={{0,16},{8,24},{16,0},{24,8},{1,17},{9,25},{17,1},{25,9},{2,18},{10... | collective-permute-start | bytes 98312 | tf_op jit(solution)/shard_map/ppermute | solution.py:111
  114.5 1.4 %collective-permute-start.32 = (f32[128,172]{0,1:T(8,128)S(1)}, f32[128,172]{0,1:T(8,128)S(1)}, u32[]{:S(2)}, u32[]{:S(2)}) collective-permute-start(f32[128,172]{0,1:T(8,128)S(1)} %convert_add_fusion), channel_id=1, source_target_pairs={{0,1},{1,0},{2,3},{3,2},{4,5},{5,4},{6,7},{7,6},{8,9},{9,8},{10,11... | collective-permute-start | bytes 264200 | tf_op jit(solution)/shard_map/ppermute | solution.py:114
  (10 other events, 227.4 us)

commit v4 on v3

--- a/solution.py
+++ b/solution.py
@@ -9,13 +9,212 @@
 from jax.sharding import PartitionSpec as P
 
 
-def keep_mask(id_values, unit_count):
-    columns = jnp.arange(unit_count, dtype=jnp.int32)
-    mixed = id_values[:, None] * 73244475 + columns[None, :] * 19349663 + 12345
+CODE_BITS = 14
+HEAD_ROWS = 16
+
+
+def keep_mask(id_values, unit_values):
+    mixed = id_values * 73244475 + unit_values * 19349663 + 12345
     mixed = mixed ^ jnp.right_shift(mixed, 15)
     mixed = mixed * 40503
     mixed = mixed ^ jnp.right_shift(mixed, 13)
-    return jnp.bitwise_and(mixed, 3) != 0
+    return (jnp.bitwise_and(mixed, 3) != 0).astype(jnp.bfloat16)
+
+
+def eye_of(count):
+    rows = lax.broadcasted_iota(jnp.int32, (count, count), 0)
+    columns = lax.broadcasted_iota(jnp.int32, (count, count), 1)
+    return rows == columns
+
+
+def dot(left, right):
+    return jnp.dot(left, right, preferred_element_type=jnp.float32)
+
+
+def dot_wide(left, right):
+    return lax.dot_general(
+        left, right, (((1,), (1,)), ((), ())), preferred_element_type=jnp.float32
+    )
+
+
+def encode(values):
+    rows, width = values.shape
+    largest = jnp.max(jnp.abs(values), axis=1, keepdims=True)
+    power = jnp.ceil(jnp.log2(jnp.maximum(largest, 1e-30)))
+    coded = jnp.round(values * jnp.exp2(CODE_BITS - power))
+    square = eye_of(width)
+    index = lax.broadcasted_iota(jnp.int32, (HEAD_ROWS, width), 0)
+    head = jnp.zeros((HEAD_ROWS, width), jnp.float32)
+    for part in range(rows // width):
+        column = power[part * width : (part + 1) * width]
+        line = jnp.sum(jnp.where(square, column, 0.0), axis=0, keepdims=True)
+        head = jnp.where(index == part, line, head)
+    whole = jnp.concatenate([coded, head], axis=0)
+    return whole.astype(jnp.int32).astype(jnp.int16)
+
+
+def decode(coded):
+    whole = coded.astype(jnp.int32).astype(jnp.float32)
+    rows, width = whole.shape[0] - HEAD_ROWS, whole.shape[1]
+    square = eye_of(width)
+    columns = []
+    for part in range(rows // width):
+        line = whole[rows + part : rows + part + 1]
+        columns.append(jnp.sum(jnp.where(square, line, 0.0), axis=1, keepdims=True))
+    power = jnp.concatenate(columns, axis=0)
+    return whole[:rows] * jnp.exp2(power - CODE_BITS)
+
+
+def share_out(values, own_ref, coded_refs):
+    step = pl.program_id(0)
+
+    @pl.when(step == 0)
+    def _():
+        own_ref[...] = values
+
+    @pl.when(step != 0)
+    def _():
+        coded = encode(values)
+        for delta, coded_ref in enumerate(coded_refs, 1):
+
+            @pl.when(step == delta)
+            def _():
+                coded_ref[...] = coded
+
+
+def first_kernel(sections, reps, dense_ref, *refs):
+    block_refs, own_ref, coded_refs = refs[:sections], refs[sections], refs[sections + 1 :]
+    own_rows = own_ref.shape[0]
+    total = jnp.zeros(own_ref.shape, jnp.float32)
+    stride = block_refs[0].shape[0] // reps
+    for p in range(sections):
+        for d in range(reps):
+            start = (p * reps + d) * own_rows
+            total += dot(
+                dense_ref[:, start : start + own_rows],
+                block_refs[p][d * stride : d * stride + own_rows, :],
+            )
+    share_out(total, own_ref, coded_refs)
+
+
+def second_kernel(sections, dense_ref, weight_ref, kept_ref, *refs):
+    block_refs, own_ref = refs[:sections], refs[sections]
+    coded_refs, dropped_ref = refs[sections + 1 : -1], refs[-1]
+    size = block_refs[0].shape[0]
+
+    @pl.when(pl.program_id(0) == 0)
+    def _():
+        for p in range(sections):
+            rows = pl.ds(p * size, size)
+            pre_act = dot(block_refs[p][...], weight_ref[...])
+            kept = kept_ref[rows, :].astype(jnp.float32) * jnp.float32(4.0 / 3.0)
+            dropped_ref[rows, :] = (jnp.maximum(pre_act, 0.0) * kept).astype(jnp.bfloat16)
+
+    share_out(dot(dense_ref[...], dropped_ref[...]), own_ref, coded_refs)
+
+
+def partial_product(body, dense, fixed, blocks, reps, width, scratch, name):
+    own_rows, columns = dense.shape[0] // reps, dense.shape[1]
+    whole = [pl.BlockSpec(value.shape, lambda i: (0, 0)) for value in fixed + blocks]
+    kept_here = jax.ShapeDtypeStruct((own_rows, width), jnp.float32)
+    sent = jax.ShapeDtypeStruct((own_rows + HEAD_ROWS, width), jnp.int16)
+    shapes = [kept_here] + [sent] * (reps - 1)
+    return pl.pallas_call(
+        body,
+        grid=(reps,),
+        in_specs=[pl.BlockSpec((own_rows, columns), lambda i: (i, 0))] + whole,
+        out_specs=[pl.BlockSpec(shape.shape, lambda i: (0, 0)) for shape in shapes],
+        out_shape=shapes,
+        scratch_shapes=scratch,
+        compiler_params=pltpu.CompilerParams(vmem_limit_bytes=48 * 1024 * 1024),
+        name=name,
+    )(dense, *fixed, *blocks)
+
+
+def sum_kernel(own_ref, *refs):
+    coded_refs, out_ref = refs[:-1], refs[-1]
+    total = own_ref[...]
+    for coded_ref in coded_refs:
+        total += decode(coded_ref[...])
+    out_ref[...] = total.astype(out_ref.dtype)
+
+
+def head_kernel(scale, weight_ref, bias_ref, label_ref, mask_ref, own_ref, *refs):
+    coded_refs, (logits_ref, grad_rows_ref, out_terms_ref) = refs[:-3], refs[-3:]
+    total = own_ref[...]
+    for coded_ref in coded_refs:
+        total += decode(coded_ref[...])
+    z_output = total.astype(jnp.bfloat16)
+    logits = dot(z_output, weight_ref[...]) + bias_ref[...]
+    logits_ref[...] = logits
+    shifted = jnp.exp(logits - jnp.max(logits, axis=1, keepdims=True))
+    likelihood = shifted / jnp.sum(shifted, axis=1, keepdims=True)
+    onehot = label_ref[...] == lax.broadcasted_iota(jnp.int32, logits.shape, 1)
+    slope = (likelihood - onehot.astype(jnp.float32)) * mask_ref[...].astype(jnp.float32) * scale
+    slope = slope.astype(jnp.bfloat16)
+    grad_rows_ref[...] = dot_wide(weight_ref[...], slope).astype(jnp.bfloat16)
+    classes = logits.shape[1]
+    terms = lax.dot_general(
+        slope, z_output, (((0,), (0,)), ((), ())), preferred_element_type=jnp.float32
+    )
+    out_terms_ref[:classes, :] = terms
+    pad = out_terms_ref.shape[0] - classes
+    if pad:
+        out_terms_ref[classes:, :] = jnp.zeros((pad, terms.shape[1]), jnp.float32)
+
+
+def back_kernel(reps, dense_ref, block_ref, kept_ref, weight_ref, *refs):
+    grad_refs, out_ref, total_ref = refs[:reps], refs[reps], refs[reps + 1]
+    own_rows = grad_refs[0].shape[1]
+    back = jnp.zeros(kept_ref.shape, jnp.float32)
+    for d in range(reps):
+        back += dot(grad_refs[d][...], dense_ref[d * own_rows : (d + 1) * own_rows, :])
+    pre_act = dot_wide(weight_ref[...], block_ref[...])
+    factor = jnp.where(pre_act > 0, kept_ref[...].astype(jnp.float32), 0.0)
+    pre_slope = (back * (factor * jnp.float32(4.0 / 3.0))).astype(jnp.bfloat16)
+    terms = dot(pre_slope, block_ref[...])
+
+    @pl.when(pl.program_id(0) == 0)
+    def _():
+        total_ref[...] = terms
+
+    @pl.when(pl.program_id(0) != 0)
+    def _():
+        total_ref[...] += terms
+
+    @pl.when(pl.program_id(0) == pl.num_programs(0) - 1)
+    def _():
+        out_ref[...] = total_ref[...].T
+
+
+def backward(dense, z_columns, kept_wide, weight_wide, grad_parts, reps):
+    step = dense.shape[0] // 2
+    hidden, inputs = weight_wide.shape
+    whole = [pl.BlockSpec(value.shape, lambda i: (0, 0)) for value in [weight_wide] + grad_parts]
+    return pl.pallas_call(
+        functools.partial(back_kernel, reps),
+        grid=(dense.shape[1] // step,),
+        in_specs=[
+            pl.BlockSpec((dense.shape[0], step), lambda i: (0, i)),
+            pl.BlockSpec((step, inputs), lambda i: (i, 0)),
+            pl.BlockSpec((hidden, step), lambda i: (0, i)),
+        ]
+        + whole,
+        out_specs=pl.BlockSpec((inputs, hidden), lambda i: (0, 0)),
+        out_shape=jax.ShapeDtypeStruct((inputs, hidden), jnp.float32),
+        scratch_shapes=[pltpu.VMEM((hidden, inputs), jnp.float32)],
+        compiler_params=pltpu.CompilerParams(vmem_limit_bytes=48 * 1024 * 1024),
+        name="backward",
+    )(dense, z_columns, kept_wide, weight_wide, *grad_parts)
+
+
+def simple_call(body, shapes, name, *values):
+    return pl.pallas_call(
+        body,
+        out_shape=shapes,
+        compiler_params=pltpu.CompilerParams(vmem_limit_bytes=32 * 1024 * 1024),
+        name=name,
+    )(*values)
 
 
 def dense_kernel(
@@ -24,7 +223,7 @@
     position = pl.program_id(0)
     rep_index = spot_ref[0]
     edge = own_ref.shape[-1]
-    slots = own_ref.shape[1]
+    slots = place_ref.shape[1]
     dense_ref[...] = jnp.zeros_like(dense_ref)
 
     def put_all(tiles_ref):
@@ -59,6 +258,7 @@
     sections, slots, edge, _ = tiles.shape
     body = functools.partial(dense_kernel, own_rows // edge, group_rows // edge)
     tile_block = (1, slots, edge, edge)
+    other_block = (1, slots + 1, edge, edge)
     return pl.pallas_call(
         body,
         grid_spec=pltpu.PrefetchScalarGridSpec(
@@ -67,7 +267,7 @@
             in_specs=[
                 pl.BlockSpec(tile_block, lambda p, spot, order, *_: (order[p], 0, 0, 0)),
                 pl.BlockSpec(
-                    tile_block, lambda p, spot, order, *_: (jnp.maximum(order[p] - 1, 0), 0, 0, 0)
+                    other_block, lambda p, spot, order, *_: (jnp.maximum(order[p] - 1, 0), 0, 0, 0)
                 ),
             ],
             out_specs=pl.BlockSpec((group_rows, group_rows), lambda p, *_: (0, p)),
@@ -125,27 +325,25 @@
         block = jnp.concatenate(pieces, axis=0)
         return [block] + [exchange(block, delta) for delta in range(1, sections)]
 
-    def scatter_rows(partial):
-        chunks = partial.reshape(reps, own_rows, partial.shape[1])
-        total = chunks[0]
-        for delta in range(1, reps):
-            total = total + swap(chunks[delta], delta)
-        return total
-
-    def sum_everywhere(value):
+    def halve(value):
         half = value.shape[0] // 2
         side = lax.rem(blk_index, 2)
         theirs = exchange(lax.dynamic_slice_in_dim(value, (1 - side) * half, half, 0), 1)
         total = lax.dynamic_slice_in_dim(value, side * half, half, 0) + theirs
-        steps = [(exchange, 1 << bit) for bit in range(1, (blks - 1).bit_length())]
-        steps += [(swap, 1 << bit) for bit in range((reps - 1).bit_length())]
-        for move, delta in steps:
-            rounded = total.astype(bf16)
-            total = rounded.astype(f32) + move(rounded, delta).astype(f32)
+        for bit in range(1, (blks - 1).bit_length()):
+            total = add_other(total, exchange, 1 << bit)
+        return total
+
+    def add_other(total, move, delta):
+        rounded = total.astype(bf16)
+        return rounded.astype(f32) + move(rounded, delta).astype(f32)
+
+    def finish(total):
+        for bit in range((reps - 1).bit_length()):
+            total = add_other(total, swap, 1 << bit)
         other = exchange(total, 1)
-        lower = jnp.where(side == 0, total, other)
-        upper = jnp.where(side == 0, other, total)
-        return jnp.concatenate([lower, upper], axis=0)
+        side = lax.rem(blk_index, 2)
+        return jnp.where(side == 0, total, other), jnp.where(side == 0, other, total)
 
     def digits(ids):
         lanes = features.shape[2]
@@ -161,6 +359,8 @@
     member = lax.rem(blk_index, sections)
     live = jnp.arange(tile_values.shape[3], dtype=jnp.int32)[None, :] < tile_count[0, 0][:, None]
     place = jnp.where(live, tile_place[0, 0], -1)
+    edge = tile_values.shape[-1]
+    slots = tile_values.shape[3]
     other_tiles = []
     other_place = [place[0]]
     for j in range(1, sections):
@@ -169,8 +369,11 @@
             for c in range(blks):
                 if c % sections < j:
                     pairs.append((r * blks + c, (r + 1) % reps * blks + c))
-        other_tiles.append(lax.ppermute(tile_values[0, 0, j], ("rep", "blk"), pairs))
-        other_place.append(lax.ppermute(place[j], ("rep", "blk"), pairs))
+        extra = jnp.pad(place[j][None] + 1, ((0, edge - 1), (0, edge - slots)))
+        parcel = jnp.concatenate([tile_values[0, 0, j], extra[None].astype(bf16)], axis=0)
+        parcel = lax.ppermute(parcel, ("rep", "blk"), pairs)
+        other_tiles.append(parcel)
+        other_place.append(parcel[slots, 0, :slots].astype(jnp.int32) - 1)
     position = jnp.arange(sections, dtype=jnp.int32)
     column = position ^ member
     order = jnp.mod(member - column, sections)
@@ -186,37 +389,58 @@
         own_rows,
         group_rows,
     )
+    width = features.shape[2]
     bundle = jnp.concatenate([features[0], digits(node_ids[0])], axis=0)
-    bundles = jnp.concatenate(to_columns(bundle), axis=0).reshape(sections * reps, -1, features.shape[2])
-    feature_columns = bundles[:, :own_rows].reshape(sections * group_rows, features.shape[2])
+    bundles = to_columns(bundle)
+    stride = bundle.shape[0]
     id_columns = jnp.concatenate(
-        [undo_digits(bundles[i, own_rows:]) for i in range(sections * reps)]
-    )
-    first = jnp.dot(dense, feature_columns, preferred_element_type=f32)
-    z_input = scatter_rows(first).astype(bf16)
-    kept = jnp.where(keep_mask(id_columns, hidden_width), f32(4.0 / 3.0), f32(0.0))
-    z_columns = jnp.concatenate(to_columns(z_input), axis=0)
-    pre_act = jnp.dot(z_columns, weight_in, preferred_element_type=f32)
-    dropped = (jnp.maximum(pre_act, 0.0) * kept).astype(bf16)
-    factor = kept * (pre_act > 0)
-    second = jnp.dot(dense, dropped, preferred_element_type=f32)
-    z_output = scatter_rows(second).astype(bf16)
-    logits = jnp.dot(z_output, weight_out, preferred_element_type=f32) + class_bias
-    likelihood = jax.nn.softmax(logits, axis=-1)
-    onehot = labels[0][:, None] == jnp.arange(logits.shape[-1], dtype=jnp.int32)[None, :]
-    slope = (
-        (likelihood - onehot.astype(f32)) * train_mask[0][:, None].astype(f32) * scale
-    ).astype(bf16)
-    grad_rows = jnp.einsum(
-        "nc,hc->nh", slope, weight_out, preferred_element_type=f32
-    ).astype(bf16)
-    grad_block = jnp.concatenate([swap(grad_rows, delta) for delta in range(reps)], axis=0)
-    out_terms = jnp.einsum("nh,nc->hc", z_output, slope, preferred_element_type=f32)
-    grad_out = sum_everywhere(out_terms)
-    back = jnp.einsum("nc,nh->ch", dense, grad_block, preferred_element_type=f32)
-    pre_slope = (back * factor).astype(bf16)
-    in_terms = jnp.einsum("nf,nh->fh", z_columns, pre_slope, preferred_element_type=f32)
-    grad_in = sum_everywhere(in_terms)
+        [
+            undo_digits(block[d * stride + own_rows : (d + 1) * stride])
+            for block in bundles
+            for d in range(reps)
+        ]
+    )
+    units = jnp.arange(hidden_width, dtype=jnp.int32)
+    kept = keep_mask(id_columns[:, None], units[None, :])
+    kept_wide = keep_mask(id_columns[None, :], units[:, None])
+    first = partial_product(
+        functools.partial(first_kernel, sections, reps),
+        dense, [], bundles, reps, width, [], "first_product",
+    )
+    arrived = [swap(first[d], d) for d in range(1, reps)]
+    z_input = simple_call(
+        sum_kernel, jax.ShapeDtypeStruct((own_rows, width), bf16), "first_sum", first[0], *arrived
+    )
+    z_blocks = to_columns(z_input)
+    kept, z_blocks = lax.optimization_barrier((kept, z_blocks))
+    second = partial_product(
+        functools.partial(second_kernel, sections),
+        dense, [weight_in, kept], z_blocks, reps, hidden_width,
+        [pltpu.VMEM((sections * group_rows, hidden_width), bf16)], "second_product",
+    )
+    arrived = [swap(second[d], d) for d in range(1, reps)]
+    classes = weight_out.shape[1]
+    logits, grad_rows, out_terms = simple_call(
+        functools.partial(head_kernel, scale),
+        (
+            jax.ShapeDtypeStruct((own_rows, classes), f32),
+            jax.ShapeDtypeStruct((hidden_width, own_rows), bf16),
+            jax.ShapeDtypeStruct((classes + -classes % 16, hidden_width), f32),
+        ),
+        "head",
+        weight_out, class_bias[None], labels[0][:, None], train_mask[0][:, None],
+        second[0], *arrived,
+    )
+    grad_parts = [swap(grad_rows, d) for d in range(reps)]
+    out_total = halve(out_terms)
+    z_columns = jnp.concatenate(z_blocks, axis=0)
+    grad_parts, out_total = lax.optimization_barrier((grad_parts, out_total))
+    in_terms = backward(dense, z_columns, kept_wide, weight_in.T, grad_parts, reps)
+    both = jnp.concatenate([halve(in_terms), out_total], axis=0)
+    lower, upper = finish(both)
+    cut = in_terms.shape[0] // 2
+    grad_in = jnp.concatenate([lower[:cut], upper[:cut]], axis=0)
+    grad_out = jnp.concatenate([lower[cut:], upper[cut:]], axis=0)[:classes].T
     return (logits[None], grad_in, grad_out)
 
 

time: 118 us -> 116 us (0.983)
  Pallas kernels: 2.32 us -> 15 us
  matrix products: 8.53 us -> 0 us
  starting transfers between devices: 49.8 us -> 45.5 us
  waiting for transfers between devices: 45.9 us -> 43.9 us
    pallas_call x0 -> x5, Pallas kernels: none -> 12.7 us  [the longest x2 6.84 us: partial_product(): pl.pallas_call(body, grid=(reps,), in_specs=[pl.BlockSpec((own_rows, colu...]
    dot_general x7 -> x0, matrix products: 8.53 us -> none  [the longest x1 4.61 us: on_device(): jnp.einsum('nf,nh->fh', z_columns, pre_slope, preferred_element_type=f32)]
    ppermute x10 -> x9, waiting for transfers between devices: 9.79 us -> 15.1 us  [exchange(): return lax.ppermute(value, 'blk', [(c, c ^ delta) for c in range(blks)])]
    ppermute x13 -> x11, waiting for transfers between devices: 24.2 us -> 19.1 us  [swap(): return lax.ppermute(value, 'rep', [(r, r ^ delta) for r in range(reps)])]
    ppermute x13 -> x11, starting transfers between devices: 18.9 us -> 16.5 us  [swap(): return lax.ppermute(value, 'rep', [(r, r ^ delta) for r in range(reps)])]
    ppermute x2 -> x1, waiting for transfers between devices: 9.63 us -> 7.4 us  [on_device(): parcel = lax.ppermute(parcel, ('rep', 'blk'), pairs)]
    ppermute x2 -> x1, starting transfers between devices: 4.37 us -> 2.47 us  [on_device(): parcel = lax.ppermute(parcel, ('rep', 'blk'), pairs)]
    ppermute x10 -> x9, starting transfers between devices: 3.68 us -> 4.23 us  [exchange(): return lax.ppermute(value, 'blk', [(c, c ^ delta) for c in range(blks)])]
  transfers between devices with their start and end apart: 33 -> 29, of which waited for: 21 -> 19; matrix products, arithmetic and copies ran while one was open for 8% -> 5% of each run, Pallas kernels for 0% -> 0%
where the time goes in v4:
time: 116 us; the launch traced here: 115 us
  starting transfers between devices  45.5 us (39%)
  waiting for transfers between devices  43.9 us (38%)
  Pallas kernels  15 us (13%)
  other arithmetic  5.91 us (5%)
  local copies, waits for them, and re-layouts  3.68 us (3%)
  between operations  1.22 us (1%)
    ppermute x8, starting transfers between devices, to_columns(): pieces.append(lax.ppermute(value, ('rep', 'blk'), pairs))  22.3 us
    ppermute x11, waiting for transfers between devices, swap(): return lax.ppermute(value, 'rep', [(r, r ^ delta) for r in range(reps)])  19.1 us
    ppermute x11, starting transfers between devices, swap(): return lax.ppermute(value, 'rep', [(r, r ^ delta) for r in range(reps)])  16.5 us
    ppermute x9, waiting for transfers between devices, exchange(): return lax.ppermute(value, 'blk', [(c, c ^ delta) for c in range(blks)])  15.1 us
    ppermute x1, waiting for transfers between devices, on_device(): parcel = lax.ppermute(parcel, ('rep', 'blk'), pairs)  7.4 us
    pallas_call x2, Pallas kernels, partial_product(): pl.pallas_call(body, grid=(reps,), in_specs=[pl.BlockSpec((own_rows, colu...  6.84 us
    pallas_call x1, Pallas kernels, backward(): pl.pallas_call(functools.partial(back_kernel, reps), grid=(dense.shape[1]...  4.78 us
    ppermute x9, starting transfers between devices, exchange(): return lax.ppermute(value, 'blk', [(c, c ^ delta) for c in range(blks)])  4.23 us
  transfers between devices with their start and end apart: 29, of which 19 were waited for; matrix products, arithmetic and copies ran while one was open for 5% of the time, Pallas kernels for 0%

profile of v4, /device:TPU:0, one launch (start us, length us, event | category | flops | bytes accessed | tf_op | source)
XLA Modules:
  0.0 115.3 jit_solution(6819955414225930546)
XLA Ops:
  3.0 6.8 %collective-permute-start.2 = (bf16[272,128]{1,0:T(8,128)(2,1)S(1)}, bf16[272,128]{1,0:T(8,128)(2,1)S(1)}, u32[]{:S(2)}, u32[]{:S(2)}) collective-permute-start(bf16[272,128]{1,0:T(8,128)(2,1)S(1)} %pad_maximum_fusion.5), channel_id=1, source_target_pairs={{0,10},{1,11},{2,12},{3,13},{4,14},{5,15},{6,8},{7,9},{8,0},{9,1},... | collective-permute-start | bytes 208904 | tf_op jit(solution)/shard_map/ppermute | solution.py:324
  9.8 1.3 %collective-permute-start.3 = (bf16[272,128]{1,0:T(8,128)(2,1)S(1)}, bf16[272,128]{1,0:T(8,128)(2,1)S(1)}, u32[]{:S(2)}, u32[]{:S(2)}) collective-permute-start(bf16[272,128]{1,0:T(8,128)(2,1)S(1)} %pad_maximum_fusion.5), channel_id=1, source_target_pairs={{0,20},{1,21},{2,22},{3,23},{4,16},{5,17},{6,18},{7,19},{8,30},{9,... | collective-permute-start | bytes 208904 | tf_op jit(solution)/shard_map/ppermute | solution.py:324
  11.1 3.0 %collective-permute-start.4 = (bf16[272,128]{1,0:T(8,128)(2,1)S(1)}, bf16[272,128]{1,0:T(8,128)(2,1)S(1)}, u32[]{:S(2)}, u32[]{:S(2)}) collective-permute-start(bf16[272,128]{1,0:T(8,128)(2,1)S(1)} %pad_maximum_fusion.5), channel_id=1, source_target_pairs={{0,30},{1,31},{2,24},{3,25},{4,26},{5,27},{6,28},{7,29},{8,20},{9,... | collective-permute-start | bytes 208904 | tf_op jit(solution)/shard_map/ppermute | solution.py:324
  16.0 2.5 %collective-permute-start = (bf16[17,128,128]{2,1,0:T(8,128)(2,1)S(1)}, bf16[17,128,128]{2,1,0:T(8,128)(2,1)S(1)}, u32[]{:S(2)}, u32[]{:S(2)}) collective-permute-start(bf16[17,128,128]{2,1,0:T(8,128)(2,1)S(1)} %pad_maximum_fusion), channel_id=1, source_target_pairs={{0,8},{2,10},{4,12},{6,14},{8,16},{10,18},{12,20},{14,22},{16,24},... | collective-permute-start | bytes 1671176 | tf_op jit(solution)/shard_map/ppermute | solution.py:374
  19.4 1.5 %collective-permute-done.5.refs_1_ = bf16[1088,128]{1,0:T(8,128)(2,1)S(1)} collective-permute-done((bf16[1088,128]{1,0:T(8,128)(2,1)S(1)}, bf16[1088,128]{1,0:T(8,128)(2,1)S(1)}, u32[]{:S(2)}, u32[]{:S(2)}) %collective-permute-start.5) | collective-permute-done | bytes 278560 | tf_op jit(solution)/shard_map/ppermute | solution.py:314
  20.9 7.4 %collective-permute-done = bf16[17,128,128]{2,1,0:T(8,128)(2,1)S(1)} collective-permute-done((bf16[17,128,128]{2,1,0:T(8,128)(2,1)S(1)}, bf16[17,128,128]{2,1,0:T(8,128)(2,1)S(1)}, u32[]{:S(2)}, u32[]{:S(2)}) %collective-permute-start) | collective-permute-done | bytes 557088 | tf_op jit(solution)/shard_map/ppermute | solution.py:374
  29.0 2.3 %dense_tiles.1.dense_ref = bf16[1024,2048]{1,0:T(8,128)(2,1)S(1)} custom-call(s32[1]{0:T(128)} %bitcast.3.spot_ref, s32[2]{0:T(128)S(1)} %and_select_fusion.1.order_ref, s32[2]{0:T(128)S(1)} %compare_convert_fusion.moved_ref, s32[2,16]{1,0:T(2,128)S(1)} %broadcast_select_fusion.2.place_ref, bf16[2,16,128,128]{3,2,1,0:T(8,128)(2,1)S(1)} %bitcast.41, ...), custom_call_target="tpu_custom_call" | custom-call | bytes 4194304 | tf_op jit(solution)/shard_map/dense_tiles/pallas_call | solution.py:262
  31.3 2.2 %first_product.1 = (f32[256,128]{1,0:T(8,128)S(1)}, s16[272,128]{1,0:T(8,128)(2,1)S(1)}, s16[272,128]{1,0:T(8,128)(2,1)S(1)}, s16[272,128]{1,0:T(8,128)(2,1)S(1)}) custom-call(bf16[1024,2048]{1,0:T(8,128)(2,1)S(1)} %dense_tiles.1.dense_ref, bf16[1088,128]{1,0:T(8,128)(2,1)S(1)} %constant_dynamic-update-slice_fusion.refs_0_, ...), custom_call_target="tpu_custom_call" | custom-call | tf_op jit(solution)/shard_map/first_product/pallas_call | solution.py:122
  34.3 2.8 %collective-permute-start.8 = (s16[272,128]{1,0:T(8,128)(2,1)S(1)}, s16[272,128]{1,0:T(8,128)(2,1)S(1)}, u32[]{:S(2)}, u32[]{:S(2)}) collective-permute-start(s16[272,128]{1,0:T(8,128)(2,1)S(1)} %get-tuple-element.25), channel_id=1, source_target_pairs={{0,24},{8,16},{16,8},{24,0},{1,25},{9,17},{17,9},{25,1},{2,26},{10... | collective-permute-start | bytes 208904 | tf_op jit(solution)/shard_map/ppermute | solution.py:311
  37.1 1.4 %collective-permute-done.6.refs_0_ = s16[272,128]{1,0:T(8,128)(2,1)S(1)} collective-permute-done((s16[272,128]{1,0:T(8,128)(2,1)S(1)}, s16[272,128]{1,0:T(8,128)(2,1)S(1)}, u32[]{:S(2)}, u32[]{:S(2)}) %collective-permute-start.6) | collective-permute-done | bytes 69664 | tf_op jit(solution)/shard_map/ppermute | solution.py:311
  40.5 5.0 %collective-permute-start.10 = (bf16[256,128]{1,0:T(8,128)(2,1)S(1)}, bf16[256,128]{1,0:T(8,128)(2,1)S(1)}, u32[]{:S(2)}, u32[]{:S(2)}) collective-permute-start(bf16[256,128]{1,0:T(8,128)(2,1)S(1)} %first_sum.1), channel_id=1, source_target_pairs={{0,10},{1,11},{2,12},{3,13},{4,14},{5,15},{6,8},{7,9},{8,0},{9,1},... | collective-permute-start | bytes 196616 | tf_op jit(solution)/shard_map/ppermute | solution.py:324
  45.4 2.1 %collective-permute-start.11 = (bf16[256,128]{1,0:T(8,128)(2,1)S(1)}, bf16[256,128]{1,0:T(8,128)(2,1)S(1)}, u32[]{:S(2)}, u32[]{:S(2)}) collective-permute-start(bf16[256,128]{1,0:T(8,128)(2,1)S(1)} %first_sum.1), channel_id=1, source_target_pairs={{0,20},{1,21},{2,22},{3,23},{4,16},{5,17},{6,18},{7,19},{8,30},{9,... | collective-permute-start | bytes 196616 | tf_op jit(solution)/shard_map/ppermute | solution.py:324
  47.5 2.8 %collective-permute-start.12 = (bf16[256,128]{1,0:T(8,128)(2,1)S(1)}, bf16[256,128]{1,0:T(8,128)(2,1)S(1)}, u32[]{:S(2)}, u32[]{:S(2)}) collective-permute-start(bf16[256,128]{1,0:T(8,128)(2,1)S(1)} %first_sum.1), channel_id=1, source_target_pairs={{0,30},{1,31},{2,24},{3,25},{4,26},{5,27},{6,28},{7,29},{8,20},{9,... | collective-permute-start | bytes 196616 | tf_op jit(solution)/shard_map/ppermute | solution.py:324
  50.4 2.3 %collective-permute-done.12 = bf16[256,128]{1,0:T(8,128)(2,1)S(1)} collective-permute-done((bf16[256,128]{1,0:T(8,128)(2,1)S(1)}, bf16[256,128]{1,0:T(8,128)(2,1)S(1)}, u32[]{:S(2)}, u32[]{:S(2)}) %collective-permute-start.12) | collective-permute-done | bytes 65568 | tf_op jit(solution)/shard_map/ppermute | solution.py:324
  54.3 4.7 %second_product.1 = (f32[256,256]{1,0:T(8,128)S(1)}, s16[272,256]{1,0:T(8,128)(2,1)S(1)}, s16[272,256]{1,0:T(8,128)(2,1)S(1)}, s16[272,256]{1,0:T(8,128)(2,1)S(1)}) custom-call(bf16[1024,2048]{1,0:T(8,128)(2,1)} %copy-done, bf16[128,256]{1,0:T(8,128)(2,1)S(1)} %copy-done.2, bf16[2048,256]{1,0:T(8,128)(2,1)S(1)} %fusion.7.kept_ref, ...), custom_call_target="tpu_custom_call" | custom-call | tf_op jit(solution)/shard_map/second_product/pallas_call | solution.py:122
  59.0 6.2 %collective-permute-start.14 = (s16[272,256]{1,0:T(8,128)(2,1)S(1)}, s16[272,256]{1,0:T(8,128)(2,1)S(1)}, u32[]{:S(2)}, u32[]{:S(2)}) collective-permute-start(s16[272,256]{1,0:T(8,128)(2,1)S(1)} %get-tuple-element.30), channel_id=1, source_target_pairs={{0,8},{8,0},{16,24},{24,16},{1,9},{9,1},{17,25},{25,17},{2,10},{10... | collective-permute-start | bytes 417800 | tf_op jit(solution)/shard_map/ppermute | solution.py:311
  65.1 1.5 %collective-permute-start.16 = (s16[272,256]{1,0:T(8,128)(2,1)S(1)}, s16[272,256]{1,0:T(8,128)(2,1)S(1)}, u32[]{:S(2)}, u32[]{:S(2)}) collective-permute-start(s16[272,256]{1,0:T(8,128)(2,1)S(1)} %get-tuple-element.32), channel_id=1, source_target_pairs={{0,24},{8,16},{16,8},{24,0},{1,25},{9,17},{17,9},{25,1},{2,26},{10... | collective-permute-start | bytes 417800 | tf_op jit(solution)/shard_map/ppermute | solution.py:311
  67.1 2.3 %collective-permute-done.14.refs_0_ = s16[272,256]{1,0:T(8,128)(2,1)S(1)} collective-permute-done((s16[272,256]{1,0:T(8,128)(2,1)S(1)}, s16[272,256]{1,0:T(8,128)(2,1)S(1)}, u32[]{:S(2)}, u32[]{:S(2)}) %collective-permute-start.14) | collective-permute-done | bytes 139296 | tf_op jit(solution)/shard_map/ppermute | solution.py:311
  69.4 4.2 %collective-permute-done.15.refs_1_ = s16[272,256]{1,0:T(8,128)(2,1)S(1)} collective-permute-done((s16[272,256]{1,0:T(8,128)(2,1)S(1)}, s16[272,256]{1,0:T(8,128)(2,1)S(1)}, u32[]{:S(2)}, u32[]{:S(2)}) %collective-permute-start.15) | collective-permute-done | bytes 139296 | tf_op jit(solution)/shard_map/ppermute | solution.py:311
  74.6 1.1 collective-permute-done.20
  76.7 3.1 %collective-permute-done.21 = bf16[88,256]{1,0:T(8,128)(2,1)S(1)} collective-permute-done((bf16[88,256]{1,0:T(8,128)(2,1)S(1)}, bf16[88,256]{1,0:T(8,128)(2,1)S(1)}, u32[]{:S(2)}, u32[]{:S(2)}) %collective-permute-start.21) | collective-permute-done | bytes 45088 | tf_op jit(solution)/shard_map/ppermute | solution.py:314
  80.4 1.5 %collective-permute-start.18 = (bf16[256,256]{1,0:T(8,128)(2,1)S(1)}, bf16[256,256]{1,0:T(8,128)(2,1)S(1)}, u32[]{:S(2)}, u32[]{:S(2)}) collective-permute-start(bf16[256,256]{1,0:T(8,128)(2,1)S(1)} %get-tuple-element.36.refs_0_), channel_id=1, source_target_pairs={{0,16},{8,24},{16,0},{24,8},{1,17},{9,25},{17,1},{25,9},{2,18},{10... | collective-permute-start | bytes 393224 | tf_op jit(solution)/shard_map/ppermute | solution.py:311
  81.9 1.6 %collective-permute-start.19 = (bf16[256,256]{1,0:T(8,128)(2,1)S(1)}, bf16[256,256]{1,0:T(8,128)(2,1)S(1)}, u32[]{:S(2)}, u32[]{:S(2)}) collective-permute-start(bf16[256,256]{1,0:T(8,128)(2,1)S(1)} %get-tuple-element.36.refs_0_), channel_id=1, source_target_pairs={{0,24},{8,16},{16,8},{24,0},{1,25},{9,17},{17,9},{25,1},{2,26},{10... | collective-permute-start | bytes 393224 | tf_op jit(solution)/shard_map/ppermute | solution.py:311
  83.5 1.4 %collective-permute-done.22 = bf16[88,256]{1,0:T(8,128)(2,1)S(1)} collective-permute-done((bf16[88,256]{1,0:T(8,128)(2,1)S(1)}, bf16[88,256]{1,0:T(8,128)(2,1)S(1)}, u32[]{:S(2)}, u32[]{:S(2)}) %collective-permute-start.22) | collective-permute-done | bytes 45088 | tf_op jit(solution)/shard_map/ppermute | solution.py:314
  85.8 2.2 %collective-permute-done.18.refs_2_ = bf16[256,256]{1,0:T(8,128)(2,1)S(1)} collective-permute-done((bf16[256,256]{1,0:T(8,128)(2,1)S(1)}, bf16[256,256]{1,0:T(8,128)(2,1)S(1)}, u32[]{:S(2)}, u32[]{:S(2)}) %collective-permute-start.18) | collective-permute-done | bytes 131104 | tf_op jit(solution)/shard_map/ppermute | solution.py:311
  88.0 4.8 %backward.1 = f32[128,256]{1,0:T(8,128)S(1)} custom-call(bf16[1024,2048]{1,0:T(8,128)(2,1)} %copy-done, bf16[2048,128]{1,0:T(8,128)(2,1)S(1)} %pad_maximum_fusion.1.block_ref, bf16[256,2048]{1,0:T(8,128)(2,1)S(1)} %fusion.6.kept_ref, bf16[256,128]{1,0:T(8,128)(2,1)S(1)} %bitcast.43, bf16[256,256]{1,0:T(8,128)(2,1)S(1)} %get-tuple-element.36.refs_0_, ...), custom_call_target="tpu_custom_call" | custom-call | tf_op jit(solution)/shard_map/backward/pallas_call | solution.py:194
  92.9 1.2 %collective-permute-done.23 = f32[64,256]{1,0:T(8,128)S(1)} collective-permute-done((f32[64,256]{1,0:T(8,128)S(1)}, f32[64,256]{1,0:T(8,128)S(1)}, u32[]{:S(2)}, u32[]{:S(2)}) %collective-permute-start.23) | collective-permute-done | bytes 65568 | tf_op jit(solution)/shard_map/ppermute | solution.py:314
  94.8 3.3 %collective-permute-done.24 = bf16[64,256]{1,0:T(8,128)(2,1)S(1)} collective-permute-done((bf16[64,256]{1,0:T(8,128)(2,1)S(1)}, bf16[64,256]{1,0:T(8,128)(2,1)S(1)}, u32[]{:S(2)}, u32[]{:S(2)}) %collective-permute-start.24) | collective-permute-done | bytes 32800 | tf_op jit(solution)/shard_map/ppermute | solution.py:314
  98.1 2.9 %collective-permute-start.25 = (bf16[64,256]{1,0:T(8,128)(2,1)S(1)}, bf16[64,256]{1,0:T(8,128)(2,1)S(1)}, u32[]{:S(2)}, u32[]{:S(2)}) collective-permute-start(bf16[64,256]{1,0:T(8,128)(2,1)S(1)} %add_convert_fusion.4), channel_id=1, source_target_pairs={{0,4},{1,5},{2,6},{3,7},{4,0},{5,1},{6,2},{7,3},{8,12},{9,13},{10,... | collective-permute-start | bytes 98312 | tf_op jit(solution)/shard_map/ppermute | solution.py:314
  101.0 2.4 %collective-permute-done.25 = bf16[64,256]{1,0:T(8,128)(2,1)S(1)} collective-permute-done((bf16[64,256]{1,0:T(8,128)(2,1)S(1)}, bf16[64,256]{1,0:T(8,128)(2,1)S(1)}, u32[]{:S(2)}, u32[]{:S(2)}) %collective-permute-start.25) | collective-permute-done | bytes 32800 | tf_op jit(solution)/shard_map/ppermute | solution.py:314
  104.2 3.7 %collective-permute-done.26 = bf16[152,256]{1,0:T(8,128)(2,1)S(1)} collective-permute-done((bf16[152,256]{1,0:T(8,128)(2,1)S(1)}, bf16[152,256]{1,0:T(8,128)(2,1)S(1)}, u32[]{:S(2)}, u32[]{:S(2)}) %collective-permute-start.26) | collective-permute-done | bytes 77856 | tf_op jit(solution)/shard_map/ppermute | solution.py:311
  108.8 3.5 %collective-permute-done.27 = bf16[152,256]{1,0:T(8,128)(2,1)S(1)} collective-permute-done((bf16[152,256]{1,0:T(8,128)(2,1)S(1)}, bf16[152,256]{1,0:T(8,128)(2,1)S(1)}, u32[]{:S(2)}, u32[]{:S(2)}) %collective-permute-start.27) | collective-permute-done | bytes 77856 | tf_op jit(solution)/shard_map/ppermute | solution.py:311
  (109 shorter events, 19.2 us)
Async XLA Ops:
  0.6 28.4 %copy-start.1 = (bf16[1,1,2,16,128,128]{5,4,3,2,1,0:T(8,128)(2,1)S(1)}, bf16[1,1,2,16,128,128]{5,4,3,2,1,0:T(8,128)(2,1)}, u32[]{:S(2)}) copy-start(bf16[1,1,2,16,128,128]{5,4,3,2,1,0:T(8,128)(2,1)} %param.14) | copy-start | bytes 3145732
  2.3 16.9 %collective-permute-start.1 = (bf16[272,128]{1,0:T(8,128)(2,1)S(1)}, bf16[272,128]{1,0:T(8,128)(2,1)S(1)}, u32[]{:S(2)}, u32[]{:S(2)}) collective-permute-start(bf16[272,128]{1,0:T(8,128)(2,1)S(1)} %pad_maximum_fusion.5), channel_id=1, source_target_pairs={{0,0},{1,1},{2,2},{3,3},{4,4},{5,5},{6,6},{7,7},{8,10},{9,11},{10,... | collective-permute-start | bytes 208904 | tf_op jit(solution)/shard_map/ppermute | solution.py:324
  3.0 16.2 %collective-permute-start.2 = (bf16[272,128]{1,0:T(8,128)(2,1)S(1)}, bf16[272,128]{1,0:T(8,128)(2,1)S(1)}, u32[]{:S(2)}, u32[]{:S(2)}) collective-permute-start(bf16[272,128]{1,0:T(8,128)(2,1)S(1)} %pad_maximum_fusion.5), channel_id=1, source_target_pairs={{0,10},{1,11},{2,12},{3,13},{4,14},{5,15},{6,8},{7,9},{8,0},{9,1},... | collective-permute-start | bytes 208904 | tf_op jit(solution)/shard_map/ppermute | solution.py:324
  9.8 9.4 %collective-permute-start.3 = (bf16[272,128]{1,0:T(8,128)(2,1)S(1)}, bf16[272,128]{1,0:T(8,128)(2,1)S(1)}, u32[]{:S(2)}, u32[]{:S(2)}) collective-permute-start(bf16[272,128]{1,0:T(8,128)(2,1)S(1)} %pad_maximum_fusion.5), channel_id=1, source_target_pairs={{0,20},{1,21},{2,22},{3,23},{4,16},{5,17},{6,18},{7,19},{8,30},{9,... | collective-permute-start | bytes 208904 | tf_op jit(solution)/shard_map/ppermute | solution.py:324
  11.1 8.2 %collective-permute-start.4 = (bf16[272,128]{1,0:T(8,128)(2,1)S(1)}, bf16[272,128]{1,0:T(8,128)(2,1)S(1)}, u32[]{:S(2)}, u32[]{:S(2)}) collective-permute-start(bf16[272,128]{1,0:T(8,128)(2,1)S(1)} %pad_maximum_fusion.5), channel_id=1, source_target_pairs={{0,30},{1,31},{2,24},{3,25},{4,26},{5,27},{6,28},{7,29},{8,20},{9,... | collective-permute-start | bytes 208904 | tf_op jit(solution)/shard_map/ppermute | solution.py:324
  16.0 12.3 %collective-permute-start = (bf16[17,128,128]{2,1,0:T(8,128)(2,1)S(1)}, bf16[17,128,128]{2,1,0:T(8,128)(2,1)S(1)}, u32[]{:S(2)}, u32[]{:S(2)}) collective-permute-start(bf16[17,128,128]{2,1,0:T(8,128)(2,1)S(1)} %pad_maximum_fusion), channel_id=1, source_target_pairs={{0,8},{2,10},{4,12},{6,14},{8,16},{10,18},{12,20},{14,22},{16,24},... | collective-permute-start | bytes 1671176 | tf_op jit(solution)/shard_map/ppermute | solution.py:374
  19.3 1.6 %collective-permute-start.5 = (bf16[1088,128]{1,0:T(8,128)(2,1)S(1)}, bf16[1088,128]{1,0:T(8,128)(2,1)S(1)}, u32[]{:S(2)}, u32[]{:S(2)}) collective-permute-start(bf16[1088,128]{1,0:T(8,128)(2,1)S(1)} %constant_dynamic-update-slice_fusion.refs_0_), channel_id=1, source_target_pairs={{0,1},{1,0},{2,3},{3,2},{4,5},{5,4},{6,7},{7,6},{8,9},{9,8},{10,11... | collective-permute-start | bytes 835592 | tf_op jit(solution)/shard_map/ppermute | solution.py:314
  31.3 23.0 %copy-start.2 = (bf16[128,256]{1,0:T(8,128)(2,1)S(1)}, bf16[128,256]{1,0:T(8,128)(2,1)}, u32[]{:S(2)}) copy-start(bf16[128,256]{1,0:T(8,128)(2,1)} %weight_ref.2) | copy-start | bytes 196612
  33.5 5.0 %collective-permute-start.6 = (s16[272,128]{1,0:T(8,128)(2,1)S(1)}, s16[272,128]{1,0:T(8,128)(2,1)S(1)}, u32[]{:S(2)}, u32[]{:S(2)}) collective-permute-start(s16[272,128]{1,0:T(8,128)(2,1)S(1)} %get-tuple-element.23), channel_id=1, source_target_pairs={{0,8},{8,0},{16,24},{24,16},{1,9},{9,1},{17,25},{25,17},{2,10},{10... | collective-permute-start | bytes 208904 | tf_op jit(solution)/shard_map/ppermute | solution.py:311
  33.6 4.9 %collective-permute-start.7 = (s16[272,128]{1,0:T(8,128)(2,1)S(1)}, s16[272,128]{1,0:T(8,128)(2,1)S(1)}, u32[]{:S(2)}, u32[]{:S(2)}) collective-permute-start(s16[272,128]{1,0:T(8,128)(2,1)S(1)} %get-tuple-element.24), channel_id=1, source_target_pairs={{0,16},{8,24},{16,0},{24,8},{1,17},{9,25},{17,1},{25,9},{2,18},{10... | collective-permute-start | bytes 208904 | tf_op jit(solution)/shard_map/ppermute | solution.py:311
  34.3 5.2 %collective-permute-start.8 = (s16[272,128]{1,0:T(8,128)(2,1)S(1)}, s16[272,128]{1,0:T(8,128)(2,1)S(1)}, u32[]{:S(2)}, u32[]{:S(2)}) collective-permute-start(s16[272,128]{1,0:T(8,128)(2,1)S(1)} %get-tuple-element.25), channel_id=1, source_target_pairs={{0,24},{8,16},{16,8},{24,0},{1,25},{9,17},{17,9},{25,1},{2,26},{10... | collective-permute-start | bytes 208904 | tf_op jit(solution)/shard_map/ppermute | solution.py:311
  39.8 10.6 %collective-permute-start.9 = (bf16[256,128]{1,0:T(8,128)(2,1)S(1)}, bf16[256,128]{1,0:T(8,128)(2,1)S(1)}, u32[]{:S(2)}, u32[]{:S(2)}) collective-permute-start(bf16[256,128]{1,0:T(8,128)(2,1)S(1)} %first_sum.1), channel_id=1, source_target_pairs={{0,0},{1,1},{2,2},{3,3},{4,4},{5,5},{6,6},{7,7},{8,10},{9,11},{10,... | collective-permute-start | bytes 196616 | tf_op jit(solution)/shard_map/ppermute | solution.py:324
  40.5 9.9 %collective-permute-start.10 = (bf16[256,128]{1,0:T(8,128)(2,1)S(1)}, bf16[256,128]{1,0:T(8,128)(2,1)S(1)}, u32[]{:S(2)}, u32[]{:S(2)}) collective-permute-start(bf16[256,128]{1,0:T(8,128)(2,1)S(1)} %first_sum.1), channel_id=1, source_target_pairs={{0,10},{1,11},{2,12},{3,13},{4,14},{5,15},{6,8},{7,9},{8,0},{9,1},... | collective-permute-start | bytes 196616 | tf_op jit(solution)/shard_map/ppermute | solution.py:324
  45.4 5.0 %collective-permute-start.11 = (bf16[256,128]{1,0:T(8,128)(2,1)S(1)}, bf16[256,128]{1,0:T(8,128)(2,1)S(1)}, u32[]{:S(2)}, u32[]{:S(2)}) collective-permute-start(bf16[256,128]{1,0:T(8,128)(2,1)S(1)} %first_sum.1), channel_id=1, source_target_pairs={{0,20},{1,21},{2,22},{3,23},{4,16},{5,17},{6,18},{7,19},{8,30},{9,... | collective-permute-start | bytes 196616 | tf_op jit(solution)/shard_map/ppermute | solution.py:324
  47.5 5.2 %collective-permute-start.12 = (bf16[256,128]{1,0:T(8,128)(2,1)S(1)}, bf16[256,128]{1,0:T(8,128)(2,1)S(1)}, u32[]{:S(2)}, u32[]{:S(2)}) collective-permute-start(bf16[256,128]{1,0:T(8,128)(2,1)S(1)} %first_sum.1), channel_id=1, source_target_pairs={{0,30},{1,31},{2,24},{3,25},{4,26},{5,27},{6,28},{7,29},{8,20},{9,... | collective-permute-start | bytes 196616 | tf_op jit(solution)/shard_map/ppermute | solution.py:324
  52.7 1.6 %collective-permute-start.13 = (bf16[1024,128]{1,0:T(8,128)(2,1)S(1)}, bf16[1024,128]{1,0:T(8,128)(2,1)S(1)}, u32[]{:S(2)}, u32[]{:S(2)}) collective-permute-start(bf16[1024,128]{1,0:T(8,128)(2,1)S(1)} %constant_dynamic-update-slice_fusion.5.refs_0_), channel_id=1, source_target_pairs={{0,1},{1,0},{2,3},{3,2},{4,5},{5,4},{6,7},{7,6},{8,9},{9,8},{10,11... | collective-permute-start | bytes 786440 | tf_op jit(solution)/shard_map/ppermute | solution.py:314
  53.7 19.8 %copy-start.3 = (f32[172]{0:T(256)S(1)}, f32[172]{0:T(256)}, u32[]{:S(2)}) copy-start(f32[172]{0:T(256)} %param.19) | copy-start | bytes 2068
  59.0 10.4 %collective-permute-start.14 = (s16[272,256]{1,0:T(8,128)(2,1)S(1)}, s16[272,256]{1,0:T(8,128)(2,1)S(1)}, u32[]{:S(2)}, u32[]{:S(2)}) collective-permute-start(s16[272,256]{1,0:T(8,128)(2,1)S(1)} %get-tuple-element.30), channel_id=1, source_target_pairs={{0,8},{8,0},{16,24},{24,16},{1,9},{9,1},{17,25},{25,17},{2,10},{10... | collective-permute-start | bytes 417800 | tf_op jit(solution)/shard_map/ppermute | solution.py:311
  65.1 8.4 %collective-permute-start.15 = (s16[272,256]{1,0:T(8,128)(2,1)S(1)}, s16[272,256]{1,0:T(8,128)(2,1)S(1)}, u32[]{:S(2)}, u32[]{:S(2)}) collective-permute-start(s16[272,256]{1,0:T(8,128)(2,1)S(1)} %get-tuple-element.31), channel_id=1, source_target_pairs={{0,16},{8,24},{16,0},{24,8},{1,17},{9,25},{17,1},{25,9},{2,18},{10... | collective-permute-start | bytes 417800 | tf_op jit(solution)/shard_map/ppermute | solution.py:311
  65.1 8.4 %collective-permute-start.16 = (s16[272,256]{1,0:T(8,128)(2,1)S(1)}, s16[272,256]{1,0:T(8,128)(2,1)S(1)}, u32[]{:S(2)}, u32[]{:S(2)}) collective-permute-start(s16[272,256]{1,0:T(8,128)(2,1)S(1)} %get-tuple-element.32), channel_id=1, source_target_pairs={{0,24},{8,16},{16,8},{24,0},{1,25},{9,17},{17,9},{25,1},{2,26},{10... | collective-permute-start | bytes 417800 | tf_op jit(solution)/shard_map/ppermute | solution.py:311
  74.3 1.4 %collective-permute-start.20 = (f32[88,256]{1,0:T(8,128)S(1)}, f32[88,256]{1,0:T(8,128)S(1)}, u32[]{:S(2)}, u32[]{:S(2)}) collective-permute-start(f32[88,256]{1,0:T(8,128)S(1)} %constant_dynamic-slice_fusion.1), channel_id=1, source_target_pairs={{0,1},{1,0},{2,3},{3,2},{4,5},{5,4},{6,7},{7,6},{8,9},{9,8},{10,11... | collective-permute-start | bytes 270344 | tf_op jit(solution)/shard_map/ppermute | solution.py:314
  75.7 4.1 %collective-permute-start.21 = (bf16[88,256]{1,0:T(8,128)(2,1)S(1)}, bf16[88,256]{1,0:T(8,128)(2,1)S(1)}, u32[]{:S(2)}, u32[]{:S(2)}) collective-permute-start(bf16[88,256]{1,0:T(8,128)(2,1)S(1)} %add_convert_fusion.2), channel_id=1, source_target_pairs={{0,2},{1,3},{2,0},{3,1},{4,6},{5,7},{6,4},{7,5},{8,10},{9,11},{10,... | collective-permute-start | bytes 135176 | tf_op jit(solution)/shard_map/ppermute | solution.py:314
  79.8 5.1 %collective-permute-start.22 = (bf16[88,256]{1,0:T(8,128)(2,1)S(1)}, bf16[88,256]{1,0:T(8,128)(2,1)S(1)}, u32[]{:S(2)}, u32[]{:S(2)}) collective-permute-start(bf16[88,256]{1,0:T(8,128)(2,1)S(1)} %add_convert_fusion.1), channel_id=1, source_target_pairs={{0,4},{1,5},{2,6},{3,7},{4,0},{5,1},{6,2},{7,3},{8,12},{9,13},{10,... | collective-permute-start | bytes 135176 | tf_op jit(solution)/shard_map/ppermute | solution.py:314
  80.0 5.9 %collective-permute-start.17 = (bf16[256,256]{1,0:T(8,128)(2,1)S(1)}, bf16[256,256]{1,0:T(8,128)(2,1)S(1)}, u32[]{:S(2)}, u32[]{:S(2)}) collective-permute-start(bf16[256,256]{1,0:T(8,128)(2,1)S(1)} %get-tuple-element.36.refs_0_), channel_id=1, source_target_pairs={{0,8},{8,0},{16,24},{24,16},{1,9},{9,1},{17,25},{25,17},{2,10},{10... | collective-permute-start | bytes 393224 | tf_op jit(solution)/shard_map/ppermute | solution.py:311
  80.4 7.6 %collective-permute-start.18 = (bf16[256,256]{1,0:T(8,128)(2,1)S(1)}, bf16[256,256]{1,0:T(8,128)(2,1)S(1)}, u32[]{:S(2)}, u32[]{:S(2)}) collective-permute-start(bf16[256,256]{1,0:T(8,128)(2,1)S(1)} %get-tuple-element.36.refs_0_), channel_id=1, source_target_pairs={{0,16},{8,24},{16,0},{24,8},{1,17},{9,25},{17,1},{25,9},{2,18},{10... | collective-permute-start | bytes 393224 | tf_op jit(solution)/shard_map/ppermute | solution.py:311
  81.9 6.1 %collective-permute-start.19 = (bf16[256,256]{1,0:T(8,128)(2,1)S(1)}, bf16[256,256]{1,0:T(8,128)(2,1)S(1)}, u32[]{:S(2)}, u32[]{:S(2)}) collective-permute-start(bf16[256,256]{1,0:T(8,128)(2,1)S(1)} %get-tuple-element.36.refs_0_), channel_id=1, source_target_pairs={{0,24},{8,16},{16,8},{24,0},{1,25},{9,17},{17,9},{25,1},{2,26},{10... | collective-permute-start | bytes 393224 | tf_op jit(solution)/shard_map/ppermute | solution.py:311
  92.8 1.3 %collective-permute-start.23 = (f32[64,256]{1,0:T(8,128)S(1)}, f32[64,256]{1,0:T(8,128)S(1)}, u32[]{:S(2)}, u32[]{:S(2)}) collective-permute-start(f32[64,256]{1,0:T(8,128)S(1)} %constant_dynamic-slice_fusion), channel_id=1, source_target_pairs={{0,1},{1,0},{2,3},{3,2},{4,5},{5,4},{6,7},{7,6},{8,9},{9,8},{10,11... | collective-permute-start | bytes 196616 | tf_op jit(solution)/shard_map/ppermute | solution.py:314
  94.1 4.0 %collective-permute-start.24 = (bf16[64,256]{1,0:T(8,128)(2,1)S(1)}, bf16[64,256]{1,0:T(8,128)(2,1)S(1)}, u32[]{:S(2)}, u32[]{:S(2)}) collective-permute-start(bf16[64,256]{1,0:T(8,128)(2,1)S(1)} %add_convert_fusion.5), channel_id=1, source_target_pairs={{0,2},{1,3},{2,0},{3,1},{4,6},{5,7},{6,4},{7,5},{8,10},{9,11},{10,... | collective-permute-start | bytes 98312 | tf_op jit(solution)/shard_map/ppermute | solution.py:314
  98.1 5.2 %collective-permute-start.25 = (bf16[64,256]{1,0:T(8,128)(2,1)S(1)}, bf16[64,256]{1,0:T(8,128)(2,1)S(1)}, u32[]{:S(2)}, u32[]{:S(2)}) collective-permute-start(bf16[64,256]{1,0:T(8,128)(2,1)S(1)} %add_convert_fusion.4), channel_id=1, source_target_pairs={{0,4},{1,5},{2,6},{3,7},{4,0},{5,1},{6,2},{7,3},{8,12},{9,13},{10,... | collective-permute-start | bytes 98312 | tf_op jit(solution)/shard_map/ppermute | solution.py:314
  103.4 4.5 %collective-permute-start.26 = (bf16[152,256]{1,0:T(8,128)(2,1)S(1)}, bf16[152,256]{1,0:T(8,128)(2,1)S(1)}, u32[]{:S(2)}, u32[]{:S(2)}) collective-permute-start(bf16[152,256]{1,0:T(8,128)(2,1)S(1)} %pad_maximum_fusion.4), channel_id=1, source_target_pairs={{0,8},{8,0},{16,24},{24,16},{1,9},{9,1},{17,25},{25,17},{2,10},{10... | collective-permute-start | bytes 233480 | tf_op jit(solution)/shard_map/ppermute | solution.py:311
  107.9 4.5 %collective-permute-start.27 = (bf16[152,256]{1,0:T(8,128)(2,1)S(1)}, bf16[152,256]{1,0:T(8,128)(2,1)S(1)}, u32[]{:S(2)}, u32[]{:S(2)}) collective-permute-start(bf16[152,256]{1,0:T(8,128)(2,1)S(1)} %add_convert_fusion), channel_id=1, source_target_pairs={{0,16},{8,24},{16,0},{24,8},{1,17},{9,25},{17,1},{25,9},{2,18},{10... | collective-permute-start | bytes 233480 | tf_op jit(solution)/shard_map/ppermute | solution.py:311
  112.4 1.4 %collective-permute-start.28 = (f32[152,256]{1,0:T(8,128)S(1)}, f32[152,256]{1,0:T(8,128)S(1)}, u32[]{:S(2)}, u32[]{:S(2)}) collective-permute-start(f32[152,256]{1,0:T(8,128)S(1)} %convert_add_fusion), channel_id=1, source_target_pairs={{0,1},{1,0},{2,3},{3,2},{4,5},{5,4},{6,7},{7,6},{8,9},{9,8},{10,11... | collective-permute-start | bytes 466952 | tf_op jit(solution)/shard_map/ppermute | solution.py:314
  (4 other events, 41.5 us)

commit v5 on v3

v5 whole, which is shorter than its diff:
```python
import functools
import math

import jax
import jax.numpy as jnp
from jax import lax
from jax.experimental import pallas as pl
from jax.experimental.pallas import tpu as pltpu
from jax.sharding import PartitionSpec as P


LEVELS = 32767.0
MANTISSA_BITS = 14
HEAD_ROWS = 16


def keep_mask(id_values, unit_values):
    mixed = id_values * 73244475 + unit_values * 19349663 + 12345
    mixed = mixed ^ jnp.right_shift(mixed, 15)
    mixed = mixed * 40503
    mixed = mixed ^ jnp.right_shift(mixed, 13)
    return (jnp.bitwise_and(mixed, 3) != 0).astype(jnp.bfloat16)


def eye_of(count):
    rows = lax.broadcasted_iota(jnp.int32, (count, count), 0)
    columns = lax.broadcasted_iota(jnp.int32, (count, count), 1)
    return rows == columns


def dot(left, right):
    return jnp.dot(left, right, preferred_element_type=jnp.float32)


def dot_wide(left, right):
    return lax.dot_general(
        left, right, (((1,), (1,)), ((), ())), preferred_element_type=jnp.float32
    )


def encode(values):
    rows, width = values.shape
    largest = jnp.maximum(jnp.max(jnp.abs(values), axis=1, keepdims=True), 1e-30)
    power = jnp.ceil(jnp.log2(largest))
    mantissa = jnp.ceil(largest * jnp.exp2(MANTISSA_BITS - power))
    scale = mantissa * jnp.exp2(power - MANTISSA_BITS)
    coded = jnp.clip(jnp.round(values * (LEVELS / scale)), -LEVELS, LEVELS)
    square = eye_of(width)
    index = lax.broadcasted_iota(jnp.int32, (HEAD_ROWS, width), 0)
    head = jnp.zeros((HEAD_ROWS, width), jnp.float32)
    for part in range(rows // width):
        for offset, column in enumerate((power, mantissa)):
            column = column[part * width : (part + 1) * width]
            line = jnp.sum(jnp.where(square, column, 0.0), axis=0, keepdims=True)
            head = jnp.where(index == 2 * part + offset, line, head)
    whole = jnp.concatenate([coded, head], axis=0)
    return whole.astype(jnp.int32).astype(jnp.int16)


def decode(coded):
    whole = coded.astype(jnp.int32).astype(jnp.float32)
    rows, width = whole.shape[0] - HEAD_ROWS, whole.shape[1]
    square = eye_of(width)
    columns = [[], []]
    for part in range(rows // width):
        for offset in range(2):
            start = rows + 2 * part + offset
            line = whole[start : start + 1]
            columns[offset].append(jnp.sum(jnp.where(square, line, 0.0), axis=1, keepdims=True))
    power, mantissa = (jnp.concatenate(parts, axis=0) for parts in columns)
    return whole[:rows] * (mantissa * jnp.exp2(power - MANTISSA_BITS) * (1.0 / LEVELS))


def encode_kernel(partial_ref, *coded_refs):
    own_rows = partial_ref.shape[0] // (len(coded_refs) + 1)
    for delta, coded_ref in enumerate(coded_refs, 1):
        coded_ref[...] = encode(partial_ref[delta * own_rows : (delta + 1) * own_rows, :])


def pack_kernel(count_ref, feature_ref, id_ref, place_ref, tiles_ref, bundle_ref, *parcel_refs):
    own_rows, lanes = feature_ref.shape
    bundle_ref[:own_rows, :] = feature_ref[...]
    ids = id_ref[...]
    rows = ids.shape[0]
    parts = [ids & 255, jnp.right_shift(ids, 8) & 255, jnp.right_shift(ids, 16)]
    pad = bundle_ref.shape[0] - own_rows - 3 * rows
    parts += [jnp.zeros((pad, lanes), jnp.int32)] if pad else []
    bundle_ref[own_rows:, :] = jnp.concatenate(parts, axis=0).astype(jnp.float32).astype(jnp.bfloat16)
    slots, edge = tiles_ref.shape[1], tiles_ref.shape[2]
    slot = lax.broadcasted_iota(jnp.int32, (1, slots), 1)
    for section, parcel_ref in enumerate(parcel_refs, 1):
        parcel_ref[:slots] = tiles_ref[section]
        place = place_ref[section : section + 1, :]
        line = jnp.where(slot < count_ref[section], place + 1, 0)
        line = jnp.concatenate([line, jnp.zeros((1, edge - slots), jnp.int32)], axis=1)
        first = lax.broadcasted_iota(jnp.int32, (edge, edge), 0) == 0
        parcel_ref[slots] = jnp.where(first, line, 0).astype(jnp.float32).astype(jnp.bfloat16)


def last_kernel(classes, side_ref, total_ref, other_ref, grad_in_ref, grad_out_ref):
    half = grad_in_ref.shape[0] // 2
    mine, theirs = total_ref[...], other_ref[...]
    lower = jnp.where(side_ref[0] == 0, mine, theirs)
    upper = jnp.where(side_ref[0] == 0, theirs, mine)
    grad_in_ref[...] = jnp.concatenate([lower[:half], upper[:half]], axis=0)
    grad_out = jnp.concatenate([lower[half:], upper[half:]], axis=0)
    grad_out_ref[...] = grad_out.T[:, :classes]


def head_kernel(scale, weight_ref, bias_ref, label_ref, mask_ref, own_ref, *refs):
    coded_refs, (logits_ref, grad_rows_ref, out_terms_ref) = refs[:-3], refs[-3:]
    total = own_ref[: logits_ref.shape[0], :]
    for coded_ref in coded_refs:
        total += decode(coded_ref[...])
    z_output = total.astype(jnp.bfloat16)
    logits = dot(z_output, weight_ref[...]) + bias_ref[...]
    logits_ref[...] = logits
    shifted = jnp.exp(logits - jnp.max(logits, axis=1, keepdims=True))
    likelihood = shifted / jnp.sum(shifted, axis=1, keepdims=True)
    onehot = label_ref[...] == lax.broadcasted_iota(jnp.int32, logits.shape, 1)
    slope = (likelihood - onehot.astype(jnp.float32)) * mask_ref[...].astype(jnp.float32) * scale
    slope = slope.astype(jnp.bfloat16)
    grad_rows_ref[...] = dot_wide(weight_ref[...], slope).astype(jnp.bfloat16)
    classes = logits.shape[1]
    terms = lax.dot_general(
        slope, z_output, (((0,), (0,)), ((), ())), preferred_element_type=jnp.float32
    )
    out_terms_ref[:classes, :] = terms
    pad = out_terms_ref.shape[0] - classes
    if pad:
        out_terms_ref[classes:, :] = jnp.zeros((pad, terms.shape[1]), jnp.float32)


def simple_call(body, shapes, name, *values):
    return pl.pallas_call(
        body,
        out_shape=shapes,
        compiler_params=pltpu.CompilerParams(vmem_limit_bytes=32 * 1024 * 1024),
        name=name,
    )(*values)


def dense_kernel(
    per_rep, tile_side, spot_ref, order_ref, moved_ref, place_ref, own_ref, other_ref, dense_ref
):
    position = pl.program_id(0)
    rep_index = spot_ref[0]
    edge = own_ref.shape[-1]
    slots = place_ref.shape[1]
    dense_ref[...] = jnp.zeros_like(dense_ref)

    def put_all(tiles_ref):
        def put(slot, carried):
            place = place_ref[position, slot]
            row = place // tile_side
            column = place % tile_side
            row = ((row // per_rep) ^ rep_index) * per_rep + row % per_rep
            column = ((column // per_rep) ^ rep_index) * per_rep + column % per_rep

            @pl.when(place >= 0)
            def _():
                dense_ref[
                    pl.ds(pl.multiple_of(row * edge, edge), edge),
                    pl.ds(pl.multiple_of(column * edge, edge), edge),
                ] = tiles_ref[0, slot]

            return carried

        lax.fori_loop(0, slots, put, 0)

    @pl.when(moved_ref[position] == 0)
    def _():
        put_all(own_ref)

    @pl.when(moved_ref[position] != 0)
    def _():
        put_all(other_ref)


def build_dense(tiles, others, place, spot, order, moved, own_rows, group_rows):
    sections, slots, edge, _ = tiles.shape
    body = functools.partial(dense_kernel, own_rows // edge, group_rows // edge)
    tile_block = (1, slots, edge, edge)
    other_block = (1, slots + 1, edge, edge)
    return pl.pallas_call(
        body,
        grid_spec=pltpu.PrefetchScalarGridSpec(
            num_scalar_prefetch=4,
            grid=(sections,),
            in_specs=[
                pl.BlockSpec(tile_block, lambda p, spot, order, *_: (order[p], 0, 0, 0)),
                pl.BlockSpec(
                    other_block, lambda p, spot, order, *_: (jnp.maximum(order[p] - 1, 0), 0, 0, 0)
                ),
            ],
            out_specs=pl.BlockSpec((group_rows, group_rows), lambda p, *_: (0, p)),
        ),
        out_shape=jax.ShapeDtypeStruct((group_rows, sections * group_rows), tiles.dtype),
        compiler_params=pltpu.CompilerParams(vmem_limit_bytes=40 * 1024 * 1024),
        cost_estimate=pl.CostEstimate(
            flops=0, bytes_accessed=2 * sections * group_rows * group_rows, transcendentals=0
        ),
        name="dense_tiles",
    )(spot, order, moved, place, tiles, others)


def on_device(
    features,
    node_ids,
    labels,
    train_mask,
    tile_values,
    tile_place,
    tile_count,
    weight_in,
    weight_out,
    class_bias,
):
    own_rows = features.shape[1]
    reps = lax.axis_size("rep")
    blks = lax.axis_size("blk")
    rep_index = lax.axis_index("rep")
    blk_index = lax.axis_index("blk")
    sections = tile_values.shape[2]
    group_rows = own_rows * reps
    hidden_width = weight_in.shape[1]
    scale = 1.0 / math.sqrt(group_rows * blks)
    f32 = jnp.float32
    bf16 = jnp.bfloat16

    def swap(value, delta):
        if delta == 0:
            return value
        return lax.ppermute(value, "rep", [(r, r ^ delta) for r in range(reps)])

    def exchange(value, delta):
        return lax.ppermute(value, "blk", [(c, c ^ delta) for c in range(blks)])

    def to_block(value):
        pieces = []
        for delta in range(reps):
            pairs = []
            for r in range(reps):
                for c in range(blks):
                    target = r ^ delta
                    pairs.append((r * blks + c, target * blks + (c + sections * target) % blks))
            pieces.append(lax.ppermute(value, ("rep", "blk"), pairs))
        return jnp.concatenate(pieces, axis=0)

    def to_both(block):
        return [block] + [exchange(block, delta) for delta in range(1, sections)]

    side = lax.rem(blk_index, 2)

    def halve(value):
        half = value.shape[0] // 2
        theirs = exchange(lax.dynamic_slice_in_dim(value, (1 - side) * half, half, 0), 1)
        return lax.dynamic_slice_in_dim(value, side * half, half, 0) + theirs

    def sum_over(value, move, first, size):
        rounded = value.astype(bf16)
        parts = [rounded if d == 0 else move(rounded, d) for d in range(0, size, first)]
        parts = [part.astype(f32) for part in parts]
        while len(parts) > 1:
            parts = [parts[i] + parts[i + 1] for i in range(0, len(parts), 2)]
        return parts[0]

    def undo_digits(rows):
        count = own_rows // rows.shape[1]
        parts = [rows[i * count : (i + 1) * count].astype(jnp.int32) for i in range(3)]
        return (parts[0] + (parts[1] << 8) + (parts[2] << 16)).reshape(own_rows)

    member = lax.rem(blk_index, sections)
    live = jnp.arange(tile_values.shape[3], dtype=jnp.int32)[None, :] < tile_count[0, 0][:, None]
    place = jnp.where(live, tile_place[0, 0], -1)
    slots, edge = tile_values.shape[3], tile_values.shape[4]
    width = features.shape[2]
    digit_rows = 3 * own_rows // width
    stride = own_rows + digit_rows + -digit_rows % 16
    vmem = pl.BlockSpec(memory_space=pltpu.VMEM)
    smem = pl.BlockSpec(memory_space=pltpu.SMEM)
    bundle, *parcels = pl.pallas_call(
        pack_kernel,
        in_specs=[smem, vmem, vmem, vmem, vmem],
        out_shape=[jax.ShapeDtypeStruct((stride, width), bf16)]
        + [jax.ShapeDtypeStruct((slots + 1, edge, edge), bf16)] * (sections - 1),
        compiler_params=pltpu.CompilerParams(vmem_limit_bytes=32 * 1024 * 1024),
        name="pack",
    )(
        tile_count[0, 0], features[0], node_ids.reshape(-1, width), tile_place[0, 0],
        tile_values[0, 0],
    )
    for j in range(1, sections):
        pairs = []
        for r in range(reps):
            for c in range(blks):
                if c % sections < j:
                    pairs.append((r * blks + c, (r + 1) % reps * blks + c))
        parcels[j - 1] = lax.ppermute(parcels[j - 1], ("rep", "blk"), pairs)
    block = to_block(bundle)
    block, parcels = lax.optimization_barrier((block, parcels))
    other_place = [place[0]]
    other_place += [parcel[slots, 0, :slots].astype(jnp.int32) - 1 for parcel in parcels]
    position = jnp.arange(sections, dtype=jnp.int32)
    column = position ^ member
    order = jnp.mod(member - column, sections)
    moved = (column > member).astype(jnp.int32)
    placed = jnp.where(moved[:, None] != 0, jnp.stack(other_place)[order], place[order])
    dense = build_dense(
        tile_values[0, 0],
        jnp.stack(parcels),
        placed,
        rep_index.reshape(1),
        order,
        moved,
        own_rows,
        group_rows,
    )
    pieces = [
        whole[d * stride : (d + 1) * stride] for whole in to_both(block) for d in range(reps)
    ]
    id_columns = jnp.concatenate([undo_digits(piece[own_rows:]) for piece in pieces])
    feature_columns = jnp.concatenate([piece[:own_rows] for piece in pieces], axis=0)
    units = jnp.arange(hidden_width, dtype=jnp.int32)
    kept = keep_mask(id_columns[:, None], units[None, :])
    kept_wide = keep_mask(id_columns[None, :], units[:, None])
    chunks = dot(dense, feature_columns).reshape(reps, own_rows, width)
    total = chunks[0]
    for delta in range(1, reps):
        total = total + swap(chunks[delta], delta)
    z_input = total.astype(bf16)
    z_columns = jnp.concatenate(to_both(to_block(z_input)), axis=0)
    kept, kept_wide, z_columns = lax.optimization_barrier((kept, kept_wide, z_columns))
    third = f32(4.0 / 3.0)
    pre_act = dot(z_columns, weight_in)
    dropped = (jnp.maximum(pre_act, 0.0) * (kept.astype(f32) * third)).astype(bf16)
    second = dot(dense, dropped)
    sent = simple_call(
        encode_kernel,
        [jax.ShapeDtypeStruct((own_rows + HEAD_ROWS, hidden_width), jnp.int16)] * (reps - 1),
        "encode", second,
    )
    arrived = [swap(sent[d - 1], d) for d in range(1, reps)]
    classes = weight_out.shape[1]
    logits, grad_rows, out_terms = simple_call(
        functools.partial(head_kernel, scale),
        (
            jax.ShapeDtypeStruct((own_rows, classes), f32),
            jax.ShapeDtypeStruct((hidden_width, own_rows), bf16),
            jax.ShapeDtypeStruct((classes + -classes % 16, hidden_width), f32),
        ),
        "head",
        weight_out, class_bias[None], labels[0][:, None], train_mask[0][:, None],
        second, *arrived,
    )
    grad_parts = [swap(grad_rows, d) for d in range(reps)]
    grad_parts, out_half = lax.optimization_barrier((grad_parts, halve(out_terms)))
    out_total = sum_over(out_half, exchange, 2, blks)
    pre_wide = lax.dot_general(
        weight_in, z_columns, (((0,), (1,)), ((), ())), preferred_element_type=f32
    )
    factor = jnp.where(pre_wide > 0, kept_wide.astype(f32) * third, 0.0)
    back = dot(jnp.concatenate(grad_parts, axis=1), dense)
    pre_slope = (back * factor).astype(bf16)
    in_terms = lax.dot_general(
        z_columns, pre_slope, (((0,), (1,)), ((), ())), preferred_element_type=f32
    )
    in_total = sum_over(halve(in_terms), exchange, 2, blks)
    both = sum_over(jnp.concatenate([in_total, out_total], axis=0), swap, 1, reps)
    grad_in, grad_out = pl.pallas_call(
        functools.partial(last_kernel, classes),
        in_specs=[smem, vmem, vmem],
        out_shape=[
            jax.ShapeDtypeStruct((width, hidden_width), f32),
            jax.ShapeDtypeStruct((hidden_width, classes), f32),
        ],
        name="last",
    )(side.reshape(1), both, exchange(both, 1))
    return (logits[None], grad_in, grad_out)


def solution(mesh):
    placed = (
        P("blk", "rep", None),
        P("blk", "rep"),
        P("blk", "rep"),
        P("blk", "rep"),
        P("blk", "rep", None, None, None, None),
        P("blk", "rep", None, None),
        P("blk", "rep", None),
        P(),
        P(),
        P(),
    )
    return jax.shard_map(
        on_device,
        mesh=mesh,
        in_specs=placed,
        out_specs=(P("blk", "rep", None), P(), P()),
        check_vma=False,
    )
```

time: 118 us -> 113 us (0.958)
  waiting for transfers between devices: 45.9 us -> 35.7 us
  local copies, waits for them, and re-layouts: 4.28 us -> 9.07 us
  Pallas kernels: 2.32 us -> 5.93 us
  other arithmetic: 5.42 us -> 3.09 us
    unnamed x27 -> x44, local copies, waits for them, and re-layouts: 1.01 us -> 7.58 us
    ppermute x10 -> x9, starting transfers between devices: 27.3 us -> 21.1 us  [the longest x8 18.7 us: to_block(): pieces.append(lax.ppermute(value, ('rep', 'blk'), pairs))]
    ppermute x10 -> x11, starting transfers between devices: 3.68 us -> 9.18 us  [exchange(): return lax.ppermute(value, 'blk', [(c, c ^ delta) for c in range(blks)])]
    ppermute x13 -> x12, waiting for transfers between devices: 24.2 us -> 19.1 us  [swap(): return lax.ppermute(value, 'rep', [(r, r ^ delta) for r in range(reps)])]
    ppermute x10 -> x11, waiting for transfers between devices: 9.79 us -> 5.96 us  [exchange(): return lax.ppermute(value, 'blk', [(c, c ^ delta) for c in range(blks)])]
    pallas_call x0 -> x4, Pallas kernels: none -> 3.71 us  [the longest x1 1.82 us: on_device(): pl.pallas_call(functools.partial(last_kernel, classes), in_specs=[smem, v...]
    concatenate x7 -> x4, other arithmetic: 2.26 us -> 0.06 us  [the longest x2 0.04 us: to_block(): return jnp.concatenate(pieces, axis=0)]
    convert_element_type x11 -> x4, other arithmetic: 1.28 us -> 2.62 us  [the longest x2 2.57 us: keep_mask(): return (jnp.bitwise_and(mixed, 3) != 0).astype(jnp.bfloat16)]
  transfers between devices with their start and end apart: 33 -> 32, of which waited for: 21 -> 16; matrix products, arithmetic and copies ran while one was open for 8% -> 5% of each run, Pallas kernels for 0% -> 2%
where the time goes in v5:
time: 113 us; the launch traced here: 112 us
  starting transfers between devices  49.3 us (44%)
  waiting for transfers between devices  35.7 us (32%)
  local copies, waits for them, and re-layouts  9.07 us (8%)
  matrix products  8.16 us (7%)
  Pallas kernels  5.93 us (5%)
  other arithmetic  3.09 us (3%)
  between operations  1.23 us (1%)
    ppermute x12, waiting for transfers between devices, swap(): return lax.ppermute(value, 'rep', [(r, r ^ delta) for r in range(reps)])  19.1 us
    ppermute x12, starting transfers between devices, swap(): return lax.ppermute(value, 'rep', [(r, r ^ delta) for r in range(reps)])  19 us
    ppermute x8, starting transfers between devices, to_block(): pieces.append(lax.ppermute(value, ('rep', 'blk'), pairs))  18.7 us
    ppermute x11, starting transfers between devices, exchange(): return lax.ppermute(value, 'blk', [(c, c ^ delta) for c in range(blks)])  9.18 us
    ppermute x1, waiting for transfers between devices, on_device(): parcels[j - 1] = lax.ppermute(parcels[j - 1], ('rep', 'blk'), pairs)  9.04 us
    unnamed x44, local copies, waits for them, and re-layouts  7.58 us
    ppermute x11, waiting for transfers between devices, exchange(): return lax.ppermute(value, 'blk', [(c, c ^ delta) for c in range(blks)])  5.96 us
    dot_general x1, matrix products, on_device(): lax.dot_general(z_columns, pre_slope, (((0,), (1,)), ((), ())), preferred...  5.19 us
  transfers between devices with their start and end apart: 32, of which 16 were waited for; matrix products, arithmetic and copies ran while one was open for 5% of the time, Pallas kernels for 2%

profile of v5, /device:TPU:0, one launch (start us, length us, event | category | flops | bytes accessed | tf_op | source)
XLA Modules:
  0.0 112.5 jit_solution(14759285827081089873)
XLA Ops:
  6.0 6.8 %collective-permute-start.1 = (bf16[272,128]{1,0:T(8,128)(2,1)S(1)}, bf16[272,128]{1,0:T(8,128)(2,1)S(1)}, u32[]{:S(2)}, u32[]{:S(2)}) collective-permute-start(bf16[272,128]{1,0:T(8,128)(2,1)S(1)} %get-tuple-element.23), channel_id=1, source_target_pairs={{0,10},{1,11},{2,12},{3,13},{4,14},{5,15},{6,8},{7,9},{8,0},{9,1},... | collective-permute-start | bytes 208904 | tf_op jit(solution)/shard_map/ppermute | solution.py:247
  14.1 3.0 %collective-permute-start.3 = (bf16[272,128]{1,0:T(8,128)(2,1)S(1)}, bf16[272,128]{1,0:T(8,128)(2,1)S(1)}, u32[]{:S(2)}, u32[]{:S(2)}) collective-permute-start(bf16[272,128]{1,0:T(8,128)(2,1)S(1)} %get-tuple-element.23), channel_id=1, source_target_pairs={{0,30},{1,31},{2,24},{3,25},{4,26},{5,27},{6,28},{7,29},{8,20},{9,... | collective-permute-start | bytes 208904 | tf_op jit(solution)/shard_map/ppermute | solution.py:247
  17.2 2.5 %collective-permute-start.4 = (bf16[17,128,128]{2,1,0:T(8,128)(2,1)S(1)}, bf16[17,128,128]{2,1,0:T(8,128)(2,1)S(1)}, u32[]{:S(2)}, u32[]{:S(2)}) collective-permute-start(bf16[17,128,128]{2,1,0:T(8,128)(2,1)S(1)} %get-tuple-element.24), channel_id=1, source_target_pairs={{0,8},{2,10},{4,12},{6,14},{8,16},{10,18},{12,20},{14,22},{16,24},... | collective-permute-start | bytes 1671176 | tf_op jit(solution)/shard_map/ppermute | solution.py:299
  20.4 9.0 %collective-permute-done.4 = bf16[17,128,128]{2,1,0:T(8,128)(2,1)S(1)} collective-permute-done((bf16[17,128,128]{2,1,0:T(8,128)(2,1)S(1)}, bf16[17,128,128]{2,1,0:T(8,128)(2,1)S(1)}, u32[]{:S(2)}, u32[]{:S(2)}) %collective-permute-start.4) | collective-permute-done | bytes 557088 | tf_op jit(solution)/shard_map/ppermute | solution.py:299
  30.3 2.2 %dense_tiles.1 = bf16[1024,2048]{1,0:T(8,128)(2,1)S(1)} custom-call(s32[1]{0:T(128)} %bitcast.3.spot_ref, s32[2]{0:T(128)S(1)} %and_select_fusion.1.order_ref, s32[2]{0:T(128)S(1)} %compare_convert_fusion.moved_ref, s32[2,16]{1,0:T(2,128)S(1)} %broadcast_select_fusion.place_ref, bf16[2,16,128,128]{3,2,1,0:T(8,128)(2,1)S(1)} %bitcast.45, ...), custom_call_target="tpu_custom_call" | custom-call | bytes 4194304 | tf_op jit(solution)/shard_map/dense_tiles/pallas_call | solution.py:185
  35.2 2.2 %collective-permute-start.8 = (f32[256,128]{1,0:T(8,128)S(1)}, f32[256,128]{1,0:T(8,128)S(1)}, u32[]{:S(2)}, u32[]{:S(2)}) collective-permute-start(f32[256,128]{1,0:T(8,128)S(1)} %get-tuple-element.50), channel_id=1, source_target_pairs={{0,24},{8,16},{16,8},{24,0},{1,25},{9,17},{17,9},{25,1},{2,26},{10... | collective-permute-start | bytes 393224 | tf_op jit(solution)/shard_map/ppermute | solution.py:234
  37.5 1.7 %fusion.7 = bf16[256,2048]{0,1:T(8,128)(2,1)} fusion(s32[256]{0:T(256)S(1)} %iota_multiply_fusion, s32[2048]{0:T(1024)S(1)} %broadcast_multiply_fusion), kind=kLoop, calls=%fused_computation.15 | loop fusion | flops 5242880 | bytes 1057792 | tf_op jit(solution)/shard_map/convert_element_type | solution.py:22
  40.3 2.4 %collective-permute-done.8 = f32[256,128]{1,0:T(8,128)S(1)} collective-permute-done((f32[256,128]{1,0:T(8,128)S(1)}, f32[256,128]{1,0:T(8,128)S(1)}, u32[]{:S(2)}, u32[]{:S(2)}) %collective-permute-start.8) | collective-permute-done | bytes 131104 | tf_op jit(solution)/shard_map/ppermute | solution.py:234
  43.6 2.6 %collective-permute-start.11 = (bf16[256,128]{1,0:T(8,128)(2,1)S(1)}, bf16[256,128]{1,0:T(8,128)(2,1)S(1)}, u32[]{:S(2)}, u32[]{:S(2)}) collective-permute-start(bf16[256,128]{1,0:T(8,128)(2,1)S(1)} %fusion.32), channel_id=1, source_target_pairs={{0,20},{1,21},{2,22},{3,23},{4,16},{5,17},{6,18},{7,19},{8,30},{9,... | collective-permute-start | bytes 196616 | tf_op jit(solution)/shard_map/ppermute | solution.py:247
  46.2 2.8 %collective-permute-start.12 = (bf16[256,128]{1,0:T(8,128)(2,1)S(1)}, bf16[256,128]{1,0:T(8,128)(2,1)S(1)}, u32[]{:S(2)}, u32[]{:S(2)}) collective-permute-start(bf16[256,128]{1,0:T(8,128)(2,1)S(1)} %fusion.32), channel_id=1, source_target_pairs={{0,30},{1,31},{2,24},{3,25},{4,26},{5,27},{6,28},{7,29},{8,20},{9,... | collective-permute-start | bytes 196616 | tf_op jit(solution)/shard_map/ppermute | solution.py:247
  50.6 1.5 %collective-permute-done.11 = bf16[256,128]{1,0:T(8,128)(2,1)S(1)} collective-permute-done((bf16[256,128]{1,0:T(8,128)(2,1)S(1)}, bf16[256,128]{1,0:T(8,128)(2,1)S(1)}, u32[]{:S(2)}, u32[]{:S(2)}) %collective-permute-start.11) | collective-permute-done | bytes 65568 | tf_op jit(solution)/shard_map/ppermute | solution.py:247
  52.3 1.5 %collective-permute-done.13 = bf16[1024,128]{1,0:T(8,128)(2,1)S(1)} collective-permute-done((bf16[1024,128]{1,0:T(8,128)(2,1)S(1)}, bf16[1024,128]{1,0:T(8,128)(2,1)S(1)}, u32[]{:S(2)}, u32[]{:S(2)}) %collective-permute-start.13) | collective-permute-done | bytes 262176 | tf_op jit(solution)/shard_map/ppermute | solution.py:237
  54.3 1.3 %fusion.10.partial_ref.own_ref = f32[1024,256]{1,0:T(8,128)S(1)} fusion(bf16[1024,2048]{1,0:T(8,128)(2,1)S(1)} %dense_tiles.1, bf16[2048,256]{1,0:T(8,128)(2,1)S(1)} %fusion.8, f32[2048,256]{1,0:T(8,128)S(1)} %fusion.44), kind=kOutput, calls=%fused_computation.18 | convolution fusion | flops 1076363264 | bytes 8388608 | tf_op jit(solution)/shard_map/dot_general | solution.py:32
  56.0 6.8 %collective-permute-start.14 = (s16[272,256]{1,0:T(8,128)(2,1)S(1)}, s16[272,256]{1,0:T(8,128)(2,1)S(1)}, u32[]{:S(2)}, u32[]{:S(2)}) collective-permute-start(s16[272,256]{1,0:T(8,128)(2,1)S(1)} %get-tuple-element.29), channel_id=1, source_target_pairs={{0,8},{8,0},{16,24},{24,16},{1,9},{9,1},{17,25},{25,17},{2,10},{10... | collective-permute-start | bytes 417800 | tf_op jit(solution)/shard_map/ppermute | solution.py:234
  62.8 1.5 %collective-permute-start.16 = (s16[272,256]{1,0:T(8,128)(2,1)S(1)}, s16[272,256]{1,0:T(8,128)(2,1)S(1)}, u32[]{:S(2)}, u32[]{:S(2)}) collective-permute-start(s16[272,256]{1,0:T(8,128)(2,1)S(1)} %get-tuple-element.31), channel_id=1, source_target_pairs={{0,24},{8,16},{16,8},{24,0},{1,25},{9,17},{17,9},{25,1},{2,26},{10... | collective-permute-start | bytes 417800 | tf_op jit(solution)/shard_map/ppermute | solution.py:234
  64.8 2.3 %collective-permute-done.14.refs_0_ = s16[272,256]{1,0:T(8,128)(2,1)S(1)} collective-permute-done((s16[272,256]{1,0:T(8,128)(2,1)S(1)}, s16[272,256]{1,0:T(8,128)(2,1)S(1)}, u32[]{:S(2)}, u32[]{:S(2)}) %collective-permute-start.14) | collective-permute-done | bytes 139296 | tf_op jit(solution)/shard_map/ppermute | solution.py:234
  67.1 4.2 %collective-permute-done.15.refs_1_ = s16[272,256]{1,0:T(8,128)(2,1)S(1)} collective-permute-done((s16[272,256]{1,0:T(8,128)(2,1)S(1)}, s16[272,256]{1,0:T(8,128)(2,1)S(1)}, u32[]{:S(2)}, u32[]{:S(2)}) %collective-permute-start.15) | collective-permute-done | bytes 139296 | tf_op jit(solution)/shard_map/ppermute | solution.py:234
  72.7 1.4 %collective-permute-start.18 = (bf16[256,256]{1,0:T(8,128)(2,1)S(1)}, bf16[256,256]{1,0:T(8,128)(2,1)S(1)}, u32[]{:S(2)}, u32[]{:S(2)}) collective-permute-start(bf16[256,256]{1,0:T(8,128)(2,1)S(1)} %get-tuple-element.35), channel_id=1, source_target_pairs={{0,16},{8,24},{16,0},{24,8},{1,17},{9,25},{17,1},{25,9},{2,18},{10... | collective-permute-start | bytes 393224 | tf_op jit(solution)/shard_map/ppermute | solution.py:234
  74.1 1.8 %collective-permute-start.19 = (bf16[256,256]{1,0:T(8,128)(2,1)S(1)}, bf16[256,256]{1,0:T(8,128)(2,1)S(1)}, u32[]{:S(2)}, u32[]{:S(2)}) collective-permute-start(bf16[256,256]{1,0:T(8,128)(2,1)S(1)} %get-tuple-element.35), channel_id=1, source_target_pairs={{0,24},{8,16},{16,8},{24,0},{1,25},{9,17},{17,9},{25,1},{2,26},{10... | collective-permute-start | bytes 393224 | tf_op jit(solution)/shard_map/ppermute | solution.py:234
  75.8 2.8 %collective-permute-done.17 = bf16[256,256]{1,0:T(8,128)(2,1)S(1)} collective-permute-done((bf16[256,256]{1,0:T(8,128)(2,1)S(1)}, bf16[256,256]{1,0:T(8,128)(2,1)S(1)}, u32[]{:S(2)}, u32[]{:S(2)}) %collective-permute-start.17) | collective-permute-done | bytes 131104 | tf_op jit(solution)/shard_map/ppermute | solution.py:234
  78.6 2.4 %collective-permute-done.18 = bf16[256,256]{1,0:T(8,128)(2,1)S(1)} collective-permute-done((bf16[256,256]{1,0:T(8,128)(2,1)S(1)}, bf16[256,256]{1,0:T(8,128)(2,1)S(1)}, u32[]{:S(2)}, u32[]{:S(2)}) %collective-permute-start.18) | collective-permute-done | bytes 131104 | tf_op jit(solution)/shard_map/ppermute | solution.py:234
  81.1 5.2 %fusion.9 = f32[128,256]{1,0:T(8,128)S(1)} fusion(bf16[2048,128]{1,0:T(8,128)(2,1)S(1)} %constant_dynamic-update-slice_fusion.1, bf16[1024,2048]{1,0:T(8,128)(2,1)} %copy-done.1, bf16[256,2048]{0,1:T(8,128)(2,1)} %fusion.7, f32[2048,256]{1,0:T(8,128)} %copy-done.9, bf16[256,256]{1,0:T(8,128)(2,1)S(1)} %collective-permute-done.19, ...), kind=kOutput, calls=%fused_computation.17 | convolution fusion | flops 1213202432 | bytes 8519680 | tf_op jit(solution)/shard_map/dot_general | solution.py:365
  87.0 2.1 %collective-permute-start.26 = (bf16[88,256]{1,0:T(8,128)(2,1)S(1)}, bf16[88,256]{1,0:T(8,128)(2,1)S(1)}, u32[]{:S(2)}, u32[]{:S(2)}) collective-permute-start(bf16[88,256]{1,0:T(8,128)(2,1)S(1)} %dynamic-slice_add_fusion), channel_id=1, source_target_pairs={{0,4},{1,5},{2,6},{3,7},{4,0},{5,1},{6,2},{7,3},{8,12},{9,13},{10,... | collective-permute-start | bytes 135176 | tf_op jit(solution)/shard_map/ppermute | solution.py:237
  89.1 1.8 %collective-permute-start.27 = (bf16[88,256]{1,0:T(8,128)(2,1)S(1)}, bf16[88,256]{1,0:T(8,128)(2,1)S(1)}, u32[]{:S(2)}, u32[]{:S(2)}) collective-permute-start(bf16[88,256]{1,0:T(8,128)(2,1)S(1)} %dynamic-slice_add_fusion), channel_id=1, source_target_pairs={{0,6},{1,7},{2,4},{3,5},{4,2},{5,3},{6,0},{7,1},{8,14},{9,15},{10,... | collective-permute-start | bytes 135176 | tf_op jit(solution)/shard_map/ppermute | solution.py:237
  90.9 2.6 %collective-permute-start.23 = (bf16[64,256]{1,0:T(8,128)(2,1)S(1)}, bf16[64,256]{1,0:T(8,128)(2,1)S(1)}, u32[]{:S(2)}, u32[]{:S(2)}) collective-permute-start(bf16[64,256]{1,0:T(8,128)(2,1)S(1)} %add_convert_fusion.2), channel_id=1, source_target_pairs={{0,4},{1,5},{2,6},{3,7},{4,0},{5,1},{6,2},{7,3},{8,12},{9,13},{10,... | collective-permute-start | bytes 98312 | tf_op jit(solution)/shard_map/ppermute | solution.py:237
  93.5 1.8 %collective-permute-start.24 = (bf16[64,256]{1,0:T(8,128)(2,1)S(1)}, bf16[64,256]{1,0:T(8,128)(2,1)S(1)}, u32[]{:S(2)}, u32[]{:S(2)}) collective-permute-start(bf16[64,256]{1,0:T(8,128)(2,1)S(1)} %add_convert_fusion.2), channel_id=1, source_target_pairs={{0,6},{1,7},{2,4},{3,5},{4,2},{5,3},{6,0},{7,1},{8,14},{9,15},{10,... | collective-permute-start | bytes 98312 | tf_op jit(solution)/shard_map/ppermute | solution.py:237
  96.2 3.0 %collective-permute-done.24 = bf16[64,256]{1,0:T(8,128)(2,1)S(1)} collective-permute-done((bf16[64,256]{1,0:T(8,128)(2,1)S(1)}, bf16[64,256]{1,0:T(8,128)(2,1)S(1)}, u32[]{:S(2)}, u32[]{:S(2)}) %collective-permute-start.24) | collective-permute-done | bytes 32800 | tf_op jit(solution)/shard_map/ppermute | solution.py:237
  99.3 1.5 %collective-permute-start.28 = (bf16[152,256]{1,0:T(8,128)(2,1)S(1)}, bf16[152,256]{1,0:T(8,128)(2,1)S(1)}, u32[]{:S(2)}, u32[]{:S(2)}) collective-permute-start(bf16[152,256]{1,0:T(8,128)(2,1)S(1)} %pad_maximum_fusion.2), channel_id=1, source_target_pairs={{0,8},{8,0},{16,24},{24,16},{1,9},{9,1},{17,25},{25,17},{2,10},{10... | collective-permute-start | bytes 233480 | tf_op jit(solution)/shard_map/ppermute | solution.py:234
  101.5 1.4 %collective-permute-start.30 = (bf16[152,256]{1,0:T(8,128)(2,1)S(1)}, bf16[152,256]{1,0:T(8,128)(2,1)S(1)}, u32[]{:S(2)}, u32[]{:S(2)}) collective-permute-start(bf16[152,256]{1,0:T(8,128)(2,1)S(1)} %pad_maximum_fusion.2), channel_id=1, source_target_pairs={{0,24},{8,16},{16,8},{24,0},{1,25},{9,17},{17,9},{25,1},{2,26},{10... | collective-permute-start | bytes 233480 | tf_op jit(solution)/shard_map/ppermute | solution.py:234
  105.2 1.5 %collective-permute-done.30 = bf16[152,256]{1,0:T(8,128)(2,1)S(1)} collective-permute-done((bf16[152,256]{1,0:T(8,128)(2,1)S(1)}, bf16[152,256]{1,0:T(8,128)(2,1)S(1)}, u32[]{:S(2)}, u32[]{:S(2)}) %collective-permute-start.30) | collective-permute-done | bytes 77856 | tf_op jit(solution)/shard_map/ppermute | solution.py:234
  108.9 1.8 %last.1 = (f32[128,256]{1,0:T(8,128)}, f32[256,172]{1,0:T(8,128)}) custom-call(s32[1]{0:T(128)} %bitcast.21.side_ref, f32[152,256]{1,0:T(8,128)} %copy-done.10, f32[152,256]{1,0:T(8,128)} %copy-done.11), custom_call_target="tpu_custom_call" | custom-call | tf_op jit(solution)/shard_map/last/pallas_call | solution.py:370
  110.7 1.7 %copy.20 = f32[256,172]{0,1:T(8,128)} copy(f32[256,172]{1,0:T(8,128)} %get-tuple-element.48) | data formatting | bytes 352256
  (126 shorter events, 24.1 us)
Async XLA Ops:
  5.4 15.0 %collective-permute-start = (bf16[272,128]{1,0:T(8,128)(2,1)S(1)}, bf16[272,128]{1,0:T(8,128)(2,1)S(1)}, u32[]{:S(2)}, u32[]{:S(2)}) collective-permute-start(bf16[272,128]{1,0:T(8,128)(2,1)S(1)} %get-tuple-element.23), channel_id=1, source_target_pairs={{0,0},{1,1},{2,2},{3,3},{4,4},{5,5},{6,6},{7,7},{8,10},{9,11},{10,... | collective-permute-start | bytes 208904 | tf_op jit(solution)/shard_map/ppermute | solution.py:247
  6.0 14.3 %collective-permute-start.1 = (bf16[272,128]{1,0:T(8,128)(2,1)S(1)}, bf16[272,128]{1,0:T(8,128)(2,1)S(1)}, u32[]{:S(2)}, u32[]{:S(2)}) collective-permute-start(bf16[272,128]{1,0:T(8,128)(2,1)S(1)} %get-tuple-element.23), channel_id=1, source_target_pairs={{0,10},{1,11},{2,12},{3,13},{4,14},{5,15},{6,8},{7,9},{8,0},{9,1},... | collective-permute-start | bytes 208904 | tf_op jit(solution)/shard_map/ppermute | solution.py:247
  12.8 7.5 %collective-permute-start.2 = (bf16[272,128]{1,0:T(8,128)(2,1)S(1)}, bf16[272,128]{1,0:T(8,128)(2,1)S(1)}, u32[]{:S(2)}, u32[]{:S(2)}) collective-permute-start(bf16[272,128]{1,0:T(8,128)(2,1)S(1)} %get-tuple-element.23), channel_id=1, source_target_pairs={{0,20},{1,21},{2,22},{3,23},{4,16},{5,17},{6,18},{7,19},{8,30},{9,... | collective-permute-start | bytes 208904 | tf_op jit(solution)/shard_map/ppermute | solution.py:247
  14.1 6.3 %collective-permute-start.3 = (bf16[272,128]{1,0:T(8,128)(2,1)S(1)}, bf16[272,128]{1,0:T(8,128)(2,1)S(1)}, u32[]{:S(2)}, u32[]{:S(2)}) collective-permute-start(bf16[272,128]{1,0:T(8,128)(2,1)S(1)} %get-tuple-element.23), channel_id=1, source_target_pairs={{0,30},{1,31},{2,24},{3,25},{4,26},{5,27},{6,28},{7,29},{8,20},{9,... | collective-permute-start | bytes 208904 | tf_op jit(solution)/shard_map/ppermute | solution.py:247
  17.2 12.3 %collective-permute-start.4 = (bf16[17,128,128]{2,1,0:T(8,128)(2,1)S(1)}, bf16[17,128,128]{2,1,0:T(8,128)(2,1)S(1)}, u32[]{:S(2)}, u32[]{:S(2)}) collective-permute-start(bf16[17,128,128]{2,1,0:T(8,128)(2,1)S(1)} %get-tuple-element.24), channel_id=1, source_target_pairs={{0,8},{2,10},{4,12},{6,14},{8,16},{10,18},{12,20},{14,22},{16,24},... | collective-permute-start | bytes 1671176 | tf_op jit(solution)/shard_map/ppermute | solution.py:299
  29.5 3.0 %collective-permute-start.5 = (bf16[1088,128]{1,0:T(8,128)(2,1)S(1)}, bf16[1088,128]{1,0:T(8,128)(2,1)S(1)}, u32[]{:S(2)}, u32[]{:S(2)}) collective-permute-start(bf16[1088,128]{1,0:T(8,128)(2,1)S(1)} %pad_maximum_fusion), channel_id=1, source_target_pairs={{0,1},{1,0},{2,3},{3,2},{4,5},{5,4},{6,7},{7,6},{8,9},{9,8},{10,11... | collective-permute-start | bytes 835592 | tf_op jit(solution)/shard_map/ppermute | solution.py:237
  33.9 6.4 %collective-permute-start.6 = (f32[256,128]{1,0:T(8,128)S(1)}, f32[256,128]{1,0:T(8,128)S(1)}, u32[]{:S(2)}, u32[]{:S(2)}) collective-permute-start(f32[256,128]{1,0:T(8,128)S(1)} %get-tuple-element.49), channel_id=1, source_target_pairs={{0,8},{8,0},{16,24},{24,16},{1,9},{9,1},{17,25},{25,17},{2,10},{10... | collective-permute-start | bytes 393224 | tf_op jit(solution)/shard_map/ppermute | solution.py:234
  34.0 6.3 %collective-permute-start.7 = (f32[256,128]{1,0:T(8,128)S(1)}, f32[256,128]{1,0:T(8,128)S(1)}, u32[]{:S(2)}, u32[]{:S(2)}) collective-permute-start(f32[256,128]{1,0:T(8,128)S(1)} %get-tuple-element.51), channel_id=1, source_target_pairs={{0,16},{8,24},{16,0},{24,8},{1,17},{9,25},{17,1},{25,9},{2,18},{10... | collective-permute-start | bytes 393224 | tf_op jit(solution)/shard_map/ppermute | solution.py:234
  35.2 7.5 %collective-permute-start.8 = (f32[256,128]{1,0:T(8,128)S(1)}, f32[256,128]{1,0:T(8,128)S(1)}, u32[]{:S(2)}, u32[]{:S(2)}) collective-permute-start(f32[256,128]{1,0:T(8,128)S(1)} %get-tuple-element.50), channel_id=1, source_target_pairs={{0,24},{8,16},{16,8},{24,0},{1,25},{9,17},{17,9},{25,1},{2,26},{10... | collective-permute-start | bytes 393224 | tf_op jit(solution)/shard_map/ppermute | solution.py:234
  42.8 7.8 %collective-permute-start.10 = (bf16[256,128]{1,0:T(8,128)(2,1)S(1)}, bf16[256,128]{1,0:T(8,128)(2,1)S(1)}, u32[]{:S(2)}, u32[]{:S(2)}) collective-permute-start(bf16[256,128]{1,0:T(8,128)(2,1)S(1)} %fusion.32), channel_id=1, source_target_pairs={{0,10},{1,11},{2,12},{3,13},{4,14},{5,15},{6,8},{7,9},{8,0},{9,1},... | collective-permute-start | bytes 196616 | tf_op jit(solution)/shard_map/ppermute | solution.py:247
  43.6 8.5 %collective-permute-start.11 = (bf16[256,128]{1,0:T(8,128)(2,1)S(1)}, bf16[256,128]{1,0:T(8,128)(2,1)S(1)}, u32[]{:S(2)}, u32[]{:S(2)}) collective-permute-start(bf16[256,128]{1,0:T(8,128)(2,1)S(1)} %fusion.32), channel_id=1, source_target_pairs={{0,20},{1,21},{2,22},{3,23},{4,16},{5,17},{6,18},{7,19},{8,30},{9,... | collective-permute-start | bytes 196616 | tf_op jit(solution)/shard_map/ppermute | solution.py:247
  46.2 5.9 %collective-permute-start.12 = (bf16[256,128]{1,0:T(8,128)(2,1)S(1)}, bf16[256,128]{1,0:T(8,128)(2,1)S(1)}, u32[]{:S(2)}, u32[]{:S(2)}) collective-permute-start(bf16[256,128]{1,0:T(8,128)(2,1)S(1)} %fusion.32), channel_id=1, source_target_pairs={{0,30},{1,31},{2,24},{3,25},{4,26},{5,27},{6,28},{7,29},{8,20},{9,... | collective-permute-start | bytes 196616 | tf_op jit(solution)/shard_map/ppermute | solution.py:247
  49.0 3.1 %collective-permute-start.9 = (bf16[256,128]{1,0:T(8,128)(2,1)S(1)}, bf16[256,128]{1,0:T(8,128)(2,1)S(1)}, u32[]{:S(2)}, u32[]{:S(2)}) collective-permute-start(bf16[256,128]{1,0:T(8,128)(2,1)S(1)} %fusion.32), channel_id=1, source_target_pairs={{0,0},{1,1},{2,2},{3,3},{4,4},{5,5},{6,6},{7,7},{8,10},{9,11},{10,... | collective-permute-start | bytes 196616 | tf_op jit(solution)/shard_map/ppermute | solution.py:247
  52.1 1.6 %collective-permute-start.13 = (bf16[1024,128]{1,0:T(8,128)(2,1)S(1)}, bf16[1024,128]{1,0:T(8,128)(2,1)S(1)}, u32[]{:S(2)}, u32[]{:S(2)}) collective-permute-start(bf16[1024,128]{1,0:T(8,128)(2,1)S(1)} %pad_maximum_fusion.1), channel_id=1, source_target_pairs={{0,1},{1,0},{2,3},{3,2},{4,5},{5,4},{6,7},{7,6},{8,9},{9,8},{10,11... | collective-permute-start | bytes 786440 | tf_op jit(solution)/shard_map/ppermute | solution.py:237
  56.0 11.1 %collective-permute-start.14 = (s16[272,256]{1,0:T(8,128)(2,1)S(1)}, s16[272,256]{1,0:T(8,128)(2,1)S(1)}, u32[]{:S(2)}, u32[]{:S(2)}) collective-permute-start(s16[272,256]{1,0:T(8,128)(2,1)S(1)} %get-tuple-element.29), channel_id=1, source_target_pairs={{0,8},{8,0},{16,24},{24,16},{1,9},{9,1},{17,25},{25,17},{2,10},{10... | collective-permute-start | bytes 417800 | tf_op jit(solution)/shard_map/ppermute | solution.py:234
  62.8 8.4 %collective-permute-start.15 = (s16[272,256]{1,0:T(8,128)(2,1)S(1)}, s16[272,256]{1,0:T(8,128)(2,1)S(1)}, u32[]{:S(2)}, u32[]{:S(2)}) collective-permute-start(s16[272,256]{1,0:T(8,128)(2,1)S(1)} %get-tuple-element.30), channel_id=1, source_target_pairs={{0,16},{8,24},{16,0},{24,8},{1,17},{9,25},{17,1},{25,9},{2,18},{10... | collective-permute-start | bytes 417800 | tf_op jit(solution)/shard_map/ppermute | solution.py:234
  62.8 8.4 %collective-permute-start.16 = (s16[272,256]{1,0:T(8,128)(2,1)S(1)}, s16[272,256]{1,0:T(8,128)(2,1)S(1)}, u32[]{:S(2)}, u32[]{:S(2)}) collective-permute-start(s16[272,256]{1,0:T(8,128)(2,1)S(1)} %get-tuple-element.31), channel_id=1, source_target_pairs={{0,24},{8,16},{16,8},{24,0},{1,25},{9,17},{17,9},{25,1},{2,26},{10... | collective-permute-start | bytes 417800 | tf_op jit(solution)/shard_map/ppermute | solution.py:234
  72.2 3.6 %collective-permute-start.20 = (f32[88,256]{1,0:T(8,128)S(1)}, f32[88,256]{1,0:T(8,128)S(1)}, u32[]{:S(2)}, u32[]{:S(2)}) collective-permute-start(f32[88,256]{1,0:T(8,128)S(1)} %constant_dynamic-slice_fusion.1), channel_id=1, source_target_pairs={{0,1},{1,0},{2,3},{3,2},{4,5},{5,4},{6,7},{7,6},{8,9},{9,8},{10,11... | collective-permute-start | bytes 270344 | tf_op jit(solution)/shard_map/ppermute | solution.py:237
  72.3 6.4 %collective-permute-start.17 = (bf16[256,256]{1,0:T(8,128)(2,1)S(1)}, bf16[256,256]{1,0:T(8,128)(2,1)S(1)}, u32[]{:S(2)}, u32[]{:S(2)}) collective-permute-start(bf16[256,256]{1,0:T(8,128)(2,1)S(1)} %get-tuple-element.35), channel_id=1, source_target_pairs={{0,8},{8,0},{16,24},{24,16},{1,9},{9,1},{17,25},{25,17},{2,10},{10... | collective-permute-start | bytes 393224 | tf_op jit(solution)/shard_map/ppermute | solution.py:234
  72.7 8.4 %collective-permute-start.18 = (bf16[256,256]{1,0:T(8,128)(2,1)S(1)}, bf16[256,256]{1,0:T(8,128)(2,1)S(1)}, u32[]{:S(2)}, u32[]{:S(2)}) collective-permute-start(bf16[256,256]{1,0:T(8,128)(2,1)S(1)} %get-tuple-element.35), channel_id=1, source_target_pairs={{0,16},{8,24},{16,0},{24,8},{1,17},{9,25},{17,1},{25,9},{2,18},{10... | collective-permute-start | bytes 393224 | tf_op jit(solution)/shard_map/ppermute | solution.py:234
  74.1 7.0 %collective-permute-start.19 = (bf16[256,256]{1,0:T(8,128)(2,1)S(1)}, bf16[256,256]{1,0:T(8,128)(2,1)S(1)}, u32[]{:S(2)}, u32[]{:S(2)}) collective-permute-start(bf16[256,256]{1,0:T(8,128)(2,1)S(1)} %get-tuple-element.35), channel_id=1, source_target_pairs={{0,24},{8,16},{16,8},{24,0},{1,25},{9,17},{17,9},{25,1},{2,26},{10... | collective-permute-start | bytes 393224 | tf_op jit(solution)/shard_map/ppermute | solution.py:234
  86.3 4.5 %collective-permute-start.21 = (f32[64,256]{1,0:T(8,128)S(1)}, f32[64,256]{1,0:T(8,128)S(1)}, u32[]{:S(2)}, u32[]{:S(2)}) collective-permute-start(f32[64,256]{1,0:T(8,128)S(1)} %constant_dynamic-slice_fusion), channel_id=1, source_target_pairs={{0,1},{1,0},{2,3},{3,2},{4,5},{5,4},{6,7},{7,6},{8,9},{9,8},{10,11... | collective-permute-start | bytes 196616 | tf_op jit(solution)/shard_map/ppermute | solution.py:237
  86.4 7.2 %collective-permute-start.25 = (bf16[88,256]{1,0:T(8,128)(2,1)S(1)}, bf16[88,256]{1,0:T(8,128)(2,1)S(1)}, u32[]{:S(2)}, u32[]{:S(2)}) collective-permute-start(bf16[88,256]{1,0:T(8,128)(2,1)S(1)} %dynamic-slice_add_fusion), channel_id=1, source_target_pairs={{0,2},{1,3},{2,0},{3,1},{4,6},{5,7},{6,4},{7,5},{8,10},{9,11},{10,... | collective-permute-start | bytes 135176 | tf_op jit(solution)/shard_map/ppermute | solution.py:237
  87.0 8.3 %collective-permute-start.26 = (bf16[88,256]{1,0:T(8,128)(2,1)S(1)}, bf16[88,256]{1,0:T(8,128)(2,1)S(1)}, u32[]{:S(2)}, u32[]{:S(2)}) collective-permute-start(bf16[88,256]{1,0:T(8,128)(2,1)S(1)} %dynamic-slice_add_fusion), channel_id=1, source_target_pairs={{0,4},{1,5},{2,6},{3,7},{4,0},{5,1},{6,2},{7,3},{8,12},{9,13},{10,... | collective-permute-start | bytes 135176 | tf_op jit(solution)/shard_map/ppermute | solution.py:237
  89.1 6.2 %collective-permute-start.27 = (bf16[88,256]{1,0:T(8,128)(2,1)S(1)}, bf16[88,256]{1,0:T(8,128)(2,1)S(1)}, u32[]{:S(2)}, u32[]{:S(2)}) collective-permute-start(bf16[88,256]{1,0:T(8,128)(2,1)S(1)} %dynamic-slice_add_fusion), channel_id=1, source_target_pairs={{0,6},{1,7},{2,4},{3,5},{4,2},{5,3},{6,0},{7,1},{8,14},{9,15},{10,... | collective-permute-start | bytes 135176 | tf_op jit(solution)/shard_map/ppermute | solution.py:237
  90.8 4.6 %collective-permute-start.22 = (bf16[64,256]{1,0:T(8,128)(2,1)S(1)}, bf16[64,256]{1,0:T(8,128)(2,1)S(1)}, u32[]{:S(2)}, u32[]{:S(2)}) collective-permute-start(bf16[64,256]{1,0:T(8,128)(2,1)S(1)} %add_convert_fusion.2), channel_id=1, source_target_pairs={{0,2},{1,3},{2,0},{3,1},{4,6},{5,7},{6,4},{7,5},{8,10},{9,11},{10,... | collective-permute-start | bytes 98312 | tf_op jit(solution)/shard_map/ppermute | solution.py:237
  90.9 5.3 %collective-permute-start.23 = (bf16[64,256]{1,0:T(8,128)(2,1)S(1)}, bf16[64,256]{1,0:T(8,128)(2,1)S(1)}, u32[]{:S(2)}, u32[]{:S(2)}) collective-permute-start(bf16[64,256]{1,0:T(8,128)(2,1)S(1)} %add_convert_fusion.2), channel_id=1, source_target_pairs={{0,4},{1,5},{2,6},{3,7},{4,0},{5,1},{6,2},{7,3},{8,12},{9,13},{10,... | collective-permute-start | bytes 98312 | tf_op jit(solution)/shard_map/ppermute | solution.py:237
  93.5 5.7 %collective-permute-start.24 = (bf16[64,256]{1,0:T(8,128)(2,1)S(1)}, bf16[64,256]{1,0:T(8,128)(2,1)S(1)}, u32[]{:S(2)}, u32[]{:S(2)}) collective-permute-start(bf16[64,256]{1,0:T(8,128)(2,1)S(1)} %add_convert_fusion.2), channel_id=1, source_target_pairs={{0,6},{1,7},{2,4},{3,5},{4,2},{5,3},{6,0},{7,1},{8,14},{9,15},{10,... | collective-permute-start | bytes 98312 | tf_op jit(solution)/shard_map/ppermute | solution.py:237
  99.3 4.8 %collective-permute-start.28 = (bf16[152,256]{1,0:T(8,128)(2,1)S(1)}, bf16[152,256]{1,0:T(8,128)(2,1)S(1)}, u32[]{:S(2)}, u32[]{:S(2)}) collective-permute-start(bf16[152,256]{1,0:T(8,128)(2,1)S(1)} %pad_maximum_fusion.2), channel_id=1, source_target_pairs={{0,8},{8,0},{16,24},{24,16},{1,9},{9,1},{17,25},{25,17},{2,10},{10... | collective-permute-start | bytes 233480 | tf_op jit(solution)/shard_map/ppermute | solution.py:234
  100.8 4.4 %collective-permute-start.29 = (bf16[152,256]{1,0:T(8,128)(2,1)S(1)}, bf16[152,256]{1,0:T(8,128)(2,1)S(1)}, u32[]{:S(2)}, u32[]{:S(2)}) collective-permute-start(bf16[152,256]{1,0:T(8,128)(2,1)S(1)} %pad_maximum_fusion.2), channel_id=1, source_target_pairs={{0,16},{8,24},{16,0},{24,8},{1,17},{9,25},{17,1},{25,9},{2,18},{10... | collective-permute-start | bytes 233480 | tf_op jit(solution)/shard_map/ppermute | solution.py:234
  101.5 5.3 %collective-permute-start.30 = (bf16[152,256]{1,0:T(8,128)(2,1)S(1)}, bf16[152,256]{1,0:T(8,128)(2,1)S(1)}, u32[]{:S(2)}, u32[]{:S(2)}) collective-permute-start(bf16[152,256]{1,0:T(8,128)(2,1)S(1)} %pad_maximum_fusion.2), channel_id=1, source_target_pairs={{0,24},{8,16},{16,8},{24,0},{1,25},{9,17},{17,9},{25,1},{2,26},{10... | collective-permute-start | bytes 233480 | tf_op jit(solution)/shard_map/ppermute | solution.py:234
  106.8 1.4 %collective-permute-start.31 = (f32[152,256]{1,0:T(8,128)S(1)}, f32[152,256]{1,0:T(8,128)S(1)}, u32[]{:S(2)}, u32[]{:S(2)}) collective-permute-start(f32[152,256]{1,0:T(8,128)S(1)} %add_add_fusion.total_ref), channel_id=1, source_target_pairs={{0,1},{1,0},{2,3},{3,2},{4,5},{5,4},{6,7},{7,6},{8,9},{9,8},{10,11... | collective-permute-start | bytes 466952 | tf_op jit(solution)/shard_map/ppermute | solution.py:237
  (15 other events, 155.8 us)

commit v6 on v5

--- a/solution.py
+++ b/solution.py
@@ -77,39 +77,73 @@
         coded_ref[...] = encode(partial_ref[delta * own_rows : (delta + 1) * own_rows, :])
 
 
-def pack_kernel(count_ref, feature_ref, id_ref, place_ref, tiles_ref, bundle_ref, *parcel_refs):
-    own_rows, lanes = feature_ref.shape
-    bundle_ref[:own_rows, :] = feature_ref[...]
+def pack_kernel(sections, count_hbm, feature_hbm, id_hbm, place_hbm, tiles_hbm, bundle_ref, *refs):
+    parcel_refs = refs[: sections - 1]
+    count_ref, id_ref, place_ref, sems = refs[sections - 1 :]
+    own_rows, lanes = feature_hbm.shape
+    slots, edge = tiles_hbm.shape[1], tiles_hbm.shape[2]
+    small = [
+        pltpu.make_async_copy(id_hbm, id_ref, sems.at[0]),
+        pltpu.make_async_copy(count_hbm, count_ref, sems.at[1]),
+        pltpu.make_async_copy(place_hbm, place_ref, sems.at[2]),
+    ]
+    large = [pltpu.make_async_copy(feature_hbm, bundle_ref.at[pl.ds(0, own_rows)], sems.at[3])]
+    for section, parcel_ref in enumerate(parcel_refs, 1):
+        large.append(
+            pltpu.make_async_copy(
+                tiles_hbm.at[section], parcel_ref.at[pl.ds(0, slots)], sems.at[3 + section]
+            )
+        )
+    for copy in small + large:
+        copy.start()
+    for copy in small:
+        copy.wait()
     ids = id_ref[...]
     rows = ids.shape[0]
     parts = [ids & 255, jnp.right_shift(ids, 8) & 255, jnp.right_shift(ids, 16)]
     pad = bundle_ref.shape[0] - own_rows - 3 * rows
     parts += [jnp.zeros((pad, lanes), jnp.int32)] if pad else []
-    bundle_ref[own_rows:, :] = jnp.concatenate(parts, axis=0).astype(jnp.float32).astype(jnp.bfloat16)
-    slots, edge = tiles_ref.shape[1], tiles_ref.shape[2]
+    digit_rows = jnp.concatenate(parts, axis=0).astype(jnp.float32).astype(jnp.bfloat16)
+    bundle_ref[own_rows:, :] = digit_rows
     slot = lax.broadcasted_iota(jnp.int32, (1, slots), 1)
+    first = lax.broadcasted_iota(jnp.int32, (edge, edge), 0) == 0
     for section, parcel_ref in enumerate(parcel_refs, 1):
-        parcel_ref[:slots] = tiles_ref[section]
         place = place_ref[section : section + 1, :]
         line = jnp.where(slot < count_ref[section], place + 1, 0)
         line = jnp.concatenate([line, jnp.zeros((1, edge - slots), jnp.int32)], axis=1)
-        first = lax.broadcasted_iota(jnp.int32, (edge, edge), 0) == 0
         parcel_ref[slots] = jnp.where(first, line, 0).astype(jnp.float32).astype(jnp.bfloat16)
-
-
-def last_kernel(classes, side_ref, total_ref, other_ref, grad_in_ref, grad_out_ref):
+    for copy in large:
+        copy.wait()
+
+
+def last_kernel(chunk, spot_ref, total_ref, other_ref, grad_in_ref, grad_out_ref):
+    side, rep_index = spot_ref[0], spot_ref[1]
     half = grad_in_ref.shape[0] // 2
-    mine, theirs = total_ref[...], other_ref[...]
-    lower = jnp.where(side_ref[0] == 0, mine, theirs)
-    upper = jnp.where(side_ref[0] == 0, theirs, mine)
-    grad_in_ref[...] = jnp.concatenate([lower[:half], upper[:half]], axis=0)
-    grad_out = jnp.concatenate([lower[half:], upper[half:]], axis=0)
-    grad_out_ref[...] = grad_out.T[:, :classes]
-
-
-def head_kernel(scale, weight_ref, bias_ref, label_ref, mask_ref, own_ref, *refs):
-    coded_refs, (logits_ref, grad_rows_ref, out_terms_ref) = refs[:-3], refs[-3:]
-    total = own_ref[: logits_ref.shape[0], :]
+    piece = chunk // 2
+    classes = grad_out_ref.shape[0]
+    reps = (total_ref.shape[0] - half) // piece
+    for part in range(2):
+
+        def take(start, size):
+            rows = pl.ds(start, size)
+            return jnp.where(side == part, total_ref[rows, :], other_ref[rows, :])
+
+        grad_in_ref[part * half : (part + 1) * half, :] = take(0, half)
+        for r in range(reps):
+            start = r * chunk + part * piece
+            size = min(piece, classes - start)
+            if size > 0:
+                spot = pl.multiple_of(half + (r ^ rep_index) * piece, 8)
+                grad_out_ref[start : start + size, :] = take(spot, piece)[:size]
+
+
+def head_kernel(
+    scale, reps, spot_ref, weight_ref, bias_ref, label_ref, mask_ref, own_ref, *refs
+):
+    coded_refs, refs = refs[: reps - 1], refs[reps - 1 :]
+    logits_ref, own_terms_ref, sent_refs, terms_ref = refs[0], refs[1], refs[2:-1], refs[-1]
+    own_rows, classes = logits_ref.shape
+    total = own_ref[:own_rows, :]
     for coded_ref in coded_refs:
         total += decode(coded_ref[...])
     z_output = total.astype(jnp.bfloat16)
@@ -120,34 +154,46 @@
     onehot = label_ref[...] == lax.broadcasted_iota(jnp.int32, logits.shape, 1)
     slope = (likelihood - onehot.astype(jnp.float32)) * mask_ref[...].astype(jnp.float32) * scale
     slope = slope.astype(jnp.bfloat16)
-    grad_rows_ref[...] = dot_wide(weight_ref[...], slope).astype(jnp.bfloat16)
-    classes = logits.shape[1]
+    grad_rows = dot_wide(slope, weight_ref[...]).astype(jnp.bfloat16)
     terms = lax.dot_general(
         slope, z_output, (((0,), (0,)), ((), ())), preferred_element_type=jnp.float32
     )
-    out_terms_ref[:classes, :] = terms
-    pad = out_terms_ref.shape[0] - classes
+    terms_ref[:classes, :] = terms
+    pad = terms_ref.shape[0] - classes
     if pad:
-        out_terms_ref[classes:, :] = jnp.zeros((pad, terms.shape[1]), jnp.float32)
-
-
-def simple_call(body, shapes, name, *values):
+        terms_ref[classes:, :] = jnp.zeros((pad, terms.shape[1]), jnp.float32)
+    chunk = own_terms_ref.shape[0]
+    for delta, sent_ref in enumerate(sent_refs):
+        start = pl.multiple_of((spot_ref[1] ^ delta) * chunk, 8)
+        piece = terms_ref[pl.ds(start, chunk), :]
+        sent_ref[:own_rows, :] = grad_rows
+        sent_ref[own_rows:, :] = piece.astype(jnp.bfloat16)
+        if delta == 0:
+            own_terms_ref[...] = piece
+
+
+def simple_call(body, shapes, name, *values, spot=(), scratch=()):
+    smem = pl.BlockSpec(memory_space=pltpu.SMEM)
+    vmem = pl.BlockSpec(memory_space=pltpu.VMEM)
     return pl.pallas_call(
         body,
+        in_specs=[smem] * len(spot) + [vmem] * len(values),
         out_shape=shapes,
+        scratch_shapes=scratch,
         compiler_params=pltpu.CompilerParams(vmem_limit_bytes=32 * 1024 * 1024),
         name=name,
-    )(*values)
-
-
-def dense_kernel(
-    per_rep, tile_side, spot_ref, order_ref, moved_ref, place_ref, own_ref, other_ref, dense_ref
-):
+    )(*spot, *values)
+
+
+def dense_kernel(per_rep, tile_side, spot_ref, order_ref, moved_ref, place_ref, own_ref, *refs):
+    other_ref, dense_ref, turned_ref = refs if len(refs) == 3 else (None, refs[0], None)
     position = pl.program_id(0)
     rep_index = spot_ref[0]
     edge = own_ref.shape[-1]
     slots = place_ref.shape[1]
     dense_ref[...] = jnp.zeros_like(dense_ref)
+    if turned_ref is not None:
+        turned_ref[...] = jnp.zeros_like(turned_ref)
 
     def put_all(tiles_ref):
         def put(slot, carried):
@@ -159,14 +205,20 @@
 
             @pl.when(place >= 0)
             def _():
-                dense_ref[
-                    pl.ds(pl.multiple_of(row * edge, edge), edge),
-                    pl.ds(pl.multiple_of(column * edge, edge), edge),
-                ] = tiles_ref[0, slot]
+                rows = pl.ds(pl.multiple_of(row * edge, edge), edge)
+                columns = pl.ds(pl.multiple_of(column * edge, edge), edge)
+                tile = tiles_ref[0, slot]
+                dense_ref[rows, columns] = tile
+                if turned_ref is not None:
+                    turned_ref[columns, rows] = tile.T
 
             return carried
 
         lax.fori_loop(0, slots, put, 0)
+
+    if other_ref is None:
+        put_all(own_ref)
+        return
 
     @pl.when(moved_ref[position] == 0)
     def _():
@@ -180,28 +232,32 @@
 def build_dense(tiles, others, place, spot, order, moved, own_rows, group_rows):
     sections, slots, edge, _ = tiles.shape
     body = functools.partial(dense_kernel, own_rows // edge, group_rows // edge)
-    tile_block = (1, slots, edge, edge)
-    other_block = (1, slots + 1, edge, edge)
+    own_block = pl.BlockSpec((1, slots, edge, edge), lambda p, spot, order, *_: (order[p], 0, 0, 0))
+    other_block = pl.BlockSpec(
+        (1, slots + 1, edge, edge),
+        lambda p, spot, order, *_: (jnp.maximum(order[p] - 1, 0), 0, 0, 0),
+    )
+    both = others is not None
+    block = (group_rows, group_rows)
+    flat = jax.ShapeDtypeStruct((group_rows, sections * group_rows), tiles.dtype)
+    tall = jax.ShapeDtypeStruct((sections * group_rows, group_rows), tiles.dtype)
+    flat_spec = pl.BlockSpec(block, lambda p, *_: (0, p))
+    tall_spec = pl.BlockSpec(block, lambda p, *_: (p, 0))
     return pl.pallas_call(
         body,
         grid_spec=pltpu.PrefetchScalarGridSpec(
             num_scalar_prefetch=4,
             grid=(sections,),
-            in_specs=[
-                pl.BlockSpec(tile_block, lambda p, spot, order, *_: (order[p], 0, 0, 0)),
-                pl.BlockSpec(
-                    other_block, lambda p, spot, order, *_: (jnp.maximum(order[p] - 1, 0), 0, 0, 0)
-                ),
-            ],
-            out_specs=pl.BlockSpec((group_rows, group_rows), lambda p, *_: (0, p)),
+            in_specs=[own_block, other_block] if both else [own_block],
+            out_specs=[flat_spec, tall_spec] if both else flat_spec,
         ),
-        out_shape=jax.ShapeDtypeStruct((group_rows, sections * group_rows), tiles.dtype),
+        out_shape=[flat, tall] if both else flat,
         compiler_params=pltpu.CompilerParams(vmem_limit_bytes=40 * 1024 * 1024),
         cost_estimate=pl.CostEstimate(
-            flops=0, bytes_accessed=2 * sections * group_rows * group_rows, transcendentals=0
+            flops=0, bytes_accessed=4 * sections * group_rows * group_rows, transcendentals=0
         ),
-        name="dense_tiles",
-    )(spot, order, moved, place, tiles, others)
+        name="dense_both" if both else "dense_first",
+    )(spot, order, moved, place, *([tiles, others] if both else [tiles]))
 
 
 def on_device(
@@ -233,10 +289,13 @@
             return value
         return lax.ppermute(value, "rep", [(r, r ^ delta) for r in range(reps)])
 
+    def shift(value, steps):
+        return lax.ppermute(value, "blk", [(c, (c + steps) % blks) for c in range(blks)])
+
     def exchange(value, delta):
         return lax.ppermute(value, "blk", [(c, c ^ delta) for c in range(blks)])
 
-    def to_block(value):
+    def to_pieces(value):
         pieces = []
         for delta in range(reps):
             pairs = []
@@ -245,7 +304,7 @@
                     target = r ^ delta
                     pairs.append((r * blks + c, target * blks + (c + sections * target) % blks))
             pieces.append(lax.ppermute(value, ("rep", "blk"), pairs))
-        return jnp.concatenate(pieces, axis=0)
+        return pieces
 
     def to_both(block):
         return [block] + [exchange(block, delta) for delta in range(1, sections)]
@@ -277,19 +336,25 @@
     width = features.shape[2]
     digit_rows = 3 * own_rows // width
     stride = own_rows + digit_rows + -digit_rows % 16
-    vmem = pl.BlockSpec(memory_space=pltpu.VMEM)
-    smem = pl.BlockSpec(memory_space=pltpu.SMEM)
+    anywhere = pl.BlockSpec(memory_space=pl.ANY)
     bundle, *parcels = pl.pallas_call(
-        pack_kernel,
-        in_specs=[smem, vmem, vmem, vmem, vmem],
+        functools.partial(pack_kernel, sections),
+        in_specs=[anywhere] * 5,
         out_shape=[jax.ShapeDtypeStruct((stride, width), bf16)]
         + [jax.ShapeDtypeStruct((slots + 1, edge, edge), bf16)] * (sections - 1),
-        compiler_params=pltpu.CompilerParams(vmem_limit_bytes=32 * 1024 * 1024),
+        scratch_shapes=[
+            pltpu.SMEM((sections,), jnp.int32),
+            pltpu.VMEM((own_rows // width, width), jnp.int32),
+            pltpu.VMEM((sections, slots), jnp.int32),
+            pltpu.SemaphoreType.DMA((sections + 3,)),
+        ],
+        compiler_params=pltpu.CompilerParams(vmem_limit_bytes=60 * 1024 * 1024),
         name="pack",
     )(
         tile_count[0, 0], features[0], node_ids.reshape(-1, width), tile_place[0, 0],
         tile_values[0, 0],
     )
+    arrived = to_pieces(bundle)
     for j in range(1, sections):
         pairs = []
         for r in range(reps):
@@ -297,8 +362,6 @@
                 if c % sections < j:
                     pairs.append((r * blks + c, (r + 1) % reps * blks + c))
         parcels[j - 1] = lax.ppermute(parcels[j - 1], ("rep", "blk"), pairs)
-    block = to_block(bundle)
-    block, parcels = lax.optimization_barrier((block, parcels))
     other_place = [place[0]]
     other_place += [parcel[slots, 0, :slots].astype(jnp.int32) - 1 for parcel in parcels]
     position = jnp.arange(sections, dtype=jnp.int32)
@@ -306,34 +369,33 @@
     order = jnp.mod(member - column, sections)
     moved = (column > member).astype(jnp.int32)
     placed = jnp.where(moved[:, None] != 0, jnp.stack(other_place)[order], place[order])
-    dense = build_dense(
-        tile_values[0, 0],
-        jnp.stack(parcels),
-        placed,
-        rep_index.reshape(1),
-        order,
-        moved,
-        own_rows,
-        group_rows,
-    )
-    pieces = [
-        whole[d * stride : (d + 1) * stride] for whole in to_both(block) for d in range(reps)
-    ]
-    id_columns = jnp.concatenate([undo_digits(piece[own_rows:]) for piece in pieces])
+    tiles = tile_values[0, 0]
+    where = rep_index.reshape(1)
+    dense = build_dense(tiles, None, place, where, position, position, own_rows, group_rows)
+    block = jnp.concatenate(arrived, axis=0)
+    blocks = [block] + [shift(block, j) for j in range(1, sections)]
+    pieces = [whole[d * stride : (d + 1) * stride] for whole in blocks for d in range(reps)]
+    digit_sets = to_both(jnp.stack([part[own_rows:] for part in pieces[:reps]]))
+    id_columns = jnp.concatenate([undo_digits(rows[d]) for rows in digit_sets for d in range(reps)])
     feature_columns = jnp.concatenate([piece[:own_rows] for piece in pieces], axis=0)
     units = jnp.arange(hidden_width, dtype=jnp.int32)
     kept = keep_mask(id_columns[:, None], units[None, :])
-    kept_wide = keep_mask(id_columns[None, :], units[:, None])
     chunks = dot(dense, feature_columns).reshape(reps, own_rows, width)
+    dense, turned = build_dense(
+        tiles, jnp.stack(parcels), placed, where, order, moved, own_rows, group_rows
+    )
     total = chunks[0]
     for delta in range(1, reps):
         total = total + swap(chunks[delta], delta)
     z_input = total.astype(bf16)
-    z_columns = jnp.concatenate(to_both(to_block(z_input)), axis=0)
-    kept, kept_wide, z_columns = lax.optimization_barrier((kept, kept_wide, z_columns))
+    arrived = to_pieces(z_input)
+    dense, turned, arrived = lax.optimization_barrier((dense, turned, arrived))
+    z_columns = jnp.concatenate(to_both(jnp.concatenate(arrived, axis=0)), axis=0)
+    kept, z_columns = lax.optimization_barrier((kept, z_columns))
     third = f32(4.0 / 3.0)
     pre_act = dot(z_columns, weight_in)
-    dropped = (jnp.maximum(pre_act, 0.0) * (kept.astype(f32) * third)).astype(bf16)
+    factor = kept.astype(f32) * third
+    dropped = (jnp.maximum(pre_act, 0.0) * factor).astype(bf16)
     second = dot(dense, dropped)
     sent = simple_call(
         encode_kernel,
@@ -342,40 +404,56 @@
     )
     arrived = [swap(sent[d - 1], d) for d in range(1, reps)]
     classes = weight_out.shape[1]
-    logits, grad_rows, out_terms = simple_call(
-        functools.partial(head_kernel, scale),
-        (
+    chunk = -(-classes // (16 * reps)) * 16
+    spot = jnp.stack([side, rep_index])
+    logits, out_total, *sent = simple_call(
+        functools.partial(head_kernel, scale, reps),
+        [
             jax.ShapeDtypeStruct((own_rows, classes), f32),
-            jax.ShapeDtypeStruct((hidden_width, own_rows), bf16),
-            jax.ShapeDtypeStruct((classes + -classes % 16, hidden_width), f32),
-        ),
+            jax.ShapeDtypeStruct((chunk, hidden_width), f32),
+        ]
+        + [jax.ShapeDtypeStruct((own_rows + chunk, hidden_width), bf16)] * reps,
         "head",
         weight_out, class_bias[None], labels[0][:, None], train_mask[0][:, None],
         second, *arrived,
-    )
-    grad_parts = [swap(grad_rows, d) for d in range(reps)]
-    grad_parts, out_half = lax.optimization_barrier((grad_parts, halve(out_terms)))
-    out_total = sum_over(out_half, exchange, 2, blks)
-    pre_wide = lax.dot_general(
-        weight_in, z_columns, (((0,), (1,)), ((), ())), preferred_element_type=f32
-    )
-    factor = jnp.where(pre_wide > 0, kept_wide.astype(f32) * third, 0.0)
-    back = dot(jnp.concatenate(grad_parts, axis=1), dense)
-    pre_slope = (back * factor).astype(bf16)
+        spot=(spot,),
+        scratch=[pltpu.VMEM((chunk * reps, hidden_width), f32)],
+    )
+    arrived = [swap(sent[d], d) for d in range(reps)]
+    grad_block = jnp.concatenate([part[:own_rows] for part in arrived], axis=0)
+    for part in arrived[1:]:
+        out_total = out_total + part[own_rows:].astype(f32)
+    back = dot(turned, grad_block)
+    pre_slope = (back * jnp.where(pre_act > 0, factor, 0.0)).astype(bf16)
+    pre_slope, out_total = lax.optimization_barrier((pre_slope, out_total))
     in_terms = lax.dot_general(
-        z_columns, pre_slope, (((0,), (1,)), ((), ())), preferred_element_type=f32
-    )
-    in_total = sum_over(halve(in_terms), exchange, 2, blks)
-    both = sum_over(jnp.concatenate([in_total, out_total], axis=0), swap, 1, reps)
-    grad_in, grad_out = pl.pallas_call(
-        functools.partial(last_kernel, classes),
-        in_specs=[smem, vmem, vmem],
-        out_shape=[
+        z_columns, pre_slope, (((0,), (0,)), ((), ())), preferred_element_type=f32
+    )
+    half, piece = width // 2, chunk // 2
+
+    def halves(which):
+        rows = [
+            lax.dynamic_slice_in_dim(in_terms, which * half, half, 0),
+            lax.dynamic_slice_in_dim(out_total, which * piece, piece, 0),
+        ]
+        return jnp.concatenate(rows, axis=0)
+
+    total = halves(side) + exchange(halves(1 - side), 1)
+    total = sum_over(total, exchange, 2, blks).astype(bf16)
+    arrived = [swap(total, d) for d in range(reps)]
+    parts = [part[:half].astype(f32) for part in arrived]
+    while len(parts) > 1:
+        parts = [parts[i] + parts[i + 1] for i in range(0, len(parts), 2)]
+    total = jnp.concatenate(parts + [part[half:].astype(f32) for part in arrived], axis=0)
+    grad_in, grad_wide = simple_call(
+        functools.partial(last_kernel, chunk),
+        [
             jax.ShapeDtypeStruct((width, hidden_width), f32),
-            jax.ShapeDtypeStruct((hidden_width, classes), f32),
+            jax.ShapeDtypeStruct((classes, hidden_width), f32),
         ],
-        name="last",
-    )(side.reshape(1), both, exchange(both, 1))
+        "last", total, exchange(total, 1), spot=(spot,),
+    )
+    grad_out = grad_wide.T
     return (logits[None], grad_in, grad_out)
 
 

time: 113 us -> 102 us (0.903)
  starting transfers between devices: 49.3 us -> 42.2 us
  Pallas kernels: 5.93 us -> 11.4 us
  local copies, waits for them, and re-layouts: 9.07 us -> 3.86 us
  waiting for transfers between devices: 35.7 us -> 32.7 us
    ppermute x1, waiting for transfers between devices: 9.04 us -> 0.01 us  [on_device(): parcels[j - 1] = lax.ppermute(parcels[j - 1], ('rep', 'blk'), pairs)]
    unnamed x44 -> x35, local copies, waits for them, and re-layouts: 7.58 us -> 2.31 us
    dot_general x1, matrix products: 5.19 us -> 0.34 us  [on_device(): lax.dot_general(z_columns, pre_slope, (((0,), (0,)), ((), ())), preferred...]
    dot_general x3 -> x4, matrix products: 2.96 us -> 7.55 us  [dot(): return jnp.dot(left, right, preferred_element_type=jnp.float32)]
    ppermute x8 -> x9, waiting for transfers between devices: 1.54 us -> 5.97 us  [the longest x1 5.95 us: shift(): lax.ppermute(value, 'blk', [(c, (c + steps) % blks) for c in range(blks)])]
    pallas_call x1 -> x2, Pallas kernels: 2.22 us -> 6.1 us  [build_dense(): pl.pallas_call(body, grid_spec=pltpu.PrefetchScalarGridSpec(num_scalar_pr...]
    ppermute x11 -> x7, starting transfers between devices: 9.18 us -> 5.51 us  [exchange(): return lax.ppermute(value, 'blk', [(c, c ^ delta) for c in range(blks)])]
    ppermute x12, starting transfers between devices: 19 us -> 15.5 us  [swap(): return lax.ppermute(value, 'rep', [(r, r ^ delta) for r in range(reps)])]
  transfers between devices with their start and end apart: 32 -> 29, of which waited for: 16 -> 17; matrix products, arithmetic and copies ran while one was open for 5% -> 6% of each run, Pallas kernels for 2% -> 6%
where the time goes in v6:
time: 102 us
  starting transfers between devices  42.2 us (41%)
  waiting for transfers between devices  32.7 us (32%)
  Pallas kernels  11.4 us (11%)
  matrix products  7.89 us (8%)
  local copies, waits for them, and re-layouts  3.86 us (4%)
  other arithmetic  2.94 us (3%)
  between operations  1.32 us (1%)
    ppermute x12, waiting for transfers between devices, swap(): return lax.ppermute(value, 'rep', [(r, r ^ delta) for r in range(reps)])  18.9 us
    ppermute x8, starting transfers between devices, to_pieces(): pieces.append(lax.ppermute(value, ('rep', 'blk'), pairs))  18.7 us
    ppermute x12, starting transfers between devices, swap(): return lax.ppermute(value, 'rep', [(r, r ^ delta) for r in range(reps)])  15.5 us
    ppermute x7, waiting for transfers between devices, exchange(): return lax.ppermute(value, 'blk', [(c, c ^ delta) for c in range(blks)])  7.82 us
    dot_general x4, matrix products, dot(): return jnp.dot(left, right, preferred_element_type=jnp.float32)  7.55 us
    pallas_call x2, Pallas kernels, build_dense(): pl.pallas_call(body, grid_spec=pltpu.PrefetchScalarGridSpec(num_scalar_pr...  6.1 us
    ppermute x1, waiting for transfers between devices, shift(): lax.ppermute(value, 'blk', [(c, (c + steps) % blks) for c in range(blks)])  5.95 us
    ppermute x7, starting transfers between devices, exchange(): return lax.ppermute(value, 'blk', [(c, c ^ delta) for c in range(blks)])  5.51 us
  transfers between devices with their start and end apart: 29, of which 17 were waited for; matrix products, arithmetic and copies ran while one was open for 6% of the time, Pallas kernels for 6%

profile of v6, /device:TPU:0, one launch (start us, length us, event | category | flops | bytes accessed | tf_op | source)
XLA Modules:
  0.0 102.3 jit_solution(3952455959664432718)
XLA Ops:
  0.6 2.0 %pack.1 = (bf16[272,128]{1,0:T(8,128)(2,1)}, bf16[17,128,128]{2,1,0:T(8,128)(2,1)}) custom-call(s32[2]{0:T(128)} %bitcast.58, bf16[256,128]{1,0:T(8,128)(2,1)} %bitcast.56, s32[2,128]{1,0:T(2,128)} %bitcast.62, s32[2,16]{1,0:T(2,128)} %bitcast.57, bf16[2,16,128,128]{3,2,1,0:T(8,128)(2,1)} %bitcast.50), custom_call_target="tpu_custom_call" | custom-call | tf_op jit(solution)/shard_map/pack/pallas_call | solution.py:340
  2.7 1.5 %collective-permute-start.1 = (bf16[272,128]{1,0:T(8,128)(2,1)}, bf16[272,128]{1,0:T(8,128)(2,1)S(1)}, u32[]{:S(2)}, u32[]{:S(2)}) collective-permute-start(bf16[272,128]{1,0:T(8,128)(2,1)} %get-tuple-element.31), channel_id=1, source_target_pairs={{0,0},{1,1},{2,2},{3,3},{4,4},{5,5},{6,6},{7,7},{8,10},{9,11},{10,... | collective-permute-start | bytes 208904 | tf_op jit(solution)/shard_map/ppermute | solution.py:306
  4.2 6.0 %collective-permute-start.2 = (bf16[272,128]{1,0:T(8,128)(2,1)}, bf16[272,128]{1,0:T(8,128)(2,1)S(1)}, u32[]{:S(2)}, u32[]{:S(2)}) collective-permute-start(bf16[272,128]{1,0:T(8,128)(2,1)} %get-tuple-element.31), channel_id=1, source_target_pairs={{0,10},{1,11},{2,12},{3,13},{4,14},{5,15},{6,8},{7,9},{8,0},{9,1},... | collective-permute-start | bytes 208904 | tf_op jit(solution)/shard_map/ppermute | solution.py:306
  10.2 1.3 %collective-permute-start.3 = (bf16[272,128]{1,0:T(8,128)(2,1)}, bf16[272,128]{1,0:T(8,128)(2,1)S(1)}, u32[]{:S(2)}, u32[]{:S(2)}) collective-permute-start(bf16[272,128]{1,0:T(8,128)(2,1)} %get-tuple-element.31), channel_id=1, source_target_pairs={{0,20},{1,21},{2,22},{3,23},{4,16},{5,17},{6,18},{7,19},{8,30},{9,... | collective-permute-start | bytes 208904 | tf_op jit(solution)/shard_map/ppermute | solution.py:306
  11.5 3.0 %collective-permute-start.4 = (bf16[272,128]{1,0:T(8,128)(2,1)}, bf16[272,128]{1,0:T(8,128)(2,1)S(1)}, u32[]{:S(2)}, u32[]{:S(2)}) collective-permute-start(bf16[272,128]{1,0:T(8,128)(2,1)} %get-tuple-element.31), channel_id=1, source_target_pairs={{0,30},{1,31},{2,24},{3,25},{4,26},{5,27},{6,28},{7,29},{8,20},{9,... | collective-permute-start | bytes 208904 | tf_op jit(solution)/shard_map/ppermute | solution.py:306
  14.5 2.5 %collective-permute-start = (bf16[17,128,128]{2,1,0:T(8,128)(2,1)}, bf16[17,128,128]{2,1,0:T(8,128)(2,1)S(1)}, u32[]{:S(2)}, u32[]{:S(2)}) collective-permute-start(bf16[17,128,128]{2,1,0:T(8,128)(2,1)} %get-tuple-element.28), channel_id=1, source_target_pairs={{0,8},{2,10},{4,12},{6,14},{8,16},{10,18},{12,20},{14,22},{16,24},... | collective-permute-start | bytes 1671176 | tf_op jit(solution)/shard_map/ppermute | solution.py:364
  19.6 2.3 %dense_first.1 = bf16[1024,2048]{1,0:T(8,128)(2,1)S(1)} custom-call(s32[1]{0:T(128)} %bitcast.1.spot_ref, s32[2]{0:T(128)S(1)} %iota.23.order_ref.moved_ref, s32[2]{0:T(128)S(1)} %iota.23.order_ref.moved_ref, s32[2,16]{1,0:T(2,128)S(1)} %compare_select_fusion.5.place_ref, bf16[2,16,128,128]{3,2,1,0:T(8,128)(2,1)S(1)} %bitcast.51), custom_call_target="tpu_custom_call" | custom-call | bytes 8388608 | tf_op jit(solution)/shard_map/dense_first/pallas_call | solution.py:246
  23.9 5.9 %collective-permute-done.5 = bf16[1088,128]{1,0:T(8,128)(2,1)S(1)} collective-permute-done((bf16[1088,128]{1,0:T(8,128)(2,1)S(1)}, bf16[1088,128]{1,0:T(8,128)(2,1)S(1)}, u32[]{:S(2)}, u32[]{:S(2)}) %collective-permute-start.5) | collective-permute-done | bytes 278560 | tf_op jit(solution)/shard_map/ppermute | solution.py:293
  31.2 1.6 %collective-permute-start.6 = (f32[256,128]{1,0:T(8,128)S(1)}, f32[256,128]{1,0:T(8,128)S(1)}, u32[]{:S(2)}, u32[]{:S(2)}) collective-permute-start(f32[256,128]{1,0:T(8,128)S(1)} %get-tuple-element.59), channel_id=1, source_target_pairs={{0,8},{8,0},{16,24},{24,16},{1,9},{9,1},{17,25},{25,17},{2,10},{10... | collective-permute-start | bytes 393224 | tf_op jit(solution)/shard_map/ppermute | solution.py:290
  34.7 1.7 %fusion.4 = bf16[2048,256]{1,0:T(8,128)(2,1)} fusion(s32[256]{0:T(256)S(1)} %iota_multiply_fusion, s32[2048]{0:T(1024)S(1)} %broadcast_multiply_fusion), kind=kLoop, calls=%fused_computation.11 | loop fusion | flops 5242880 | bytes 1057792 | tf_op jit(solution)/shard_map/convert_element_type | solution.py:22
  36.4 1.4 %collective-permute-done.7 = f32[256,128]{1,0:T(8,128)S(1)} collective-permute-done((f32[256,128]{1,0:T(8,128)S(1)}, f32[256,128]{1,0:T(8,128)S(1)}, u32[]{:S(2)}, u32[]{:S(2)}) %collective-permute-start.7) | collective-permute-done | bytes 131104 | tf_op jit(solution)/shard_map/ppermute | solution.py:290
  37.8 2.2 %collective-permute-done.8 = f32[256,128]{1,0:T(8,128)S(1)} collective-permute-done((f32[256,128]{1,0:T(8,128)S(1)}, f32[256,128]{1,0:T(8,128)S(1)}, u32[]{:S(2)}, u32[]{:S(2)}) %collective-permute-start.8) | collective-permute-done | bytes 131104 | tf_op jit(solution)/shard_map/ppermute | solution.py:290
  40.0 1.4 %collective-permute-start.11 = (bf16[256,128]{1,0:T(8,128)(2,1)S(1)}, bf16[256,128]{1,0:T(8,128)(2,1)S(1)}, u32[]{:S(2)}, u32[]{:S(2)}) collective-permute-start(bf16[256,128]{1,0:T(8,128)(2,1)S(1)} %fusion.17), channel_id=1, source_target_pairs={{0,20},{1,21},{2,22},{3,23},{4,16},{5,17},{6,18},{7,19},{8,30},{9,... | collective-permute-start | bytes 196616 | tf_op jit(solution)/shard_map/ppermute | solution.py:306
  41.5 4.7 %collective-permute-start.12 = (bf16[256,128]{1,0:T(8,128)(2,1)S(1)}, bf16[256,128]{1,0:T(8,128)(2,1)S(1)}, u32[]{:S(2)}, u32[]{:S(2)}) collective-permute-start(bf16[256,128]{1,0:T(8,128)(2,1)S(1)} %fusion.17), channel_id=1, source_target_pairs={{0,30},{1,31},{2,24},{3,25},{4,26},{5,27},{6,28},{7,29},{8,20},{9,... | collective-permute-start | bytes 196616 | tf_op jit(solution)/shard_map/ppermute | solution.py:306
  47.6 3.8 %dense_both.1 = (bf16[1024,2048]{1,0:T(8,128)(2,1)S(1)}, bf16[2048,1024]{1,0:T(8,128)(2,1)S(1)}) custom-call(s32[1]{0:T(128)} %bitcast.1.spot_ref, s32[2]{0:T(128)S(1)} %and_select_fusion.1.order_ref, s32[2]{0:T(128)S(1)} %get-tuple-element.66.moved_ref, s32[2,16]{1,0:T(2,128)S(1)} %broadcast_select_fusion.place_ref, bf16[2,16,128,128]{3,2,1,0:T(8,128)(2,1)S(1)} %bitcast.52, ...), custom_call_target="tpu_custom_call" | custom-call | bytes 8388608 | tf_op jit(solution)/shard_map/dense_both/pallas_call | solution.py:246
  51.6 1.5 %collective-permute-done.14 = bf16[1024,128]{1,0:T(8,128)(2,1)S(1)} collective-permute-done((bf16[1024,128]{1,0:T(8,128)(2,1)S(1)}, bf16[1024,128]{1,0:T(8,128)(2,1)S(1)}, u32[]{:S(2)}, u32[]{:S(2)}) %collective-permute-start.14) | collective-permute-done | bytes 262176 | tf_op jit(solution)/shard_map/ppermute | solution.py:296
  53.6 1.3 %fusion.5.partial_ref.own_ref = f32[1024,256]{1,0:T(8,128)S(1)} fusion(bf16[1024,2048]{1,0:T(8,128)(2,1)S(1)} %get-tuple-element.32, bf16[2048,256]{1,0:T(8,128)(2,1)S(1)} %copy-done.7, f32[2048,256]{1,0:T(8,128)S(1)} %fusion.29), kind=kOutput, calls=%fused_computation.12 | convolution fusion | flops 1076363264 | bytes 8388608 | tf_op jit(solution)/shard_map/dot_general | solution.py:32
  55.4 3.3 %collective-permute-start.15 = (s16[272,256]{1,0:T(8,128)(2,1)S(1)}, s16[272,256]{1,0:T(8,128)(2,1)S(1)}, u32[]{:S(2)}, u32[]{:S(2)}) collective-permute-start(s16[272,256]{1,0:T(8,128)(2,1)S(1)} %get-tuple-element.39), channel_id=1, source_target_pairs={{0,8},{8,0},{16,24},{24,16},{1,9},{9,1},{17,25},{25,17},{2,10},{10... | collective-permute-start | bytes 417800 | tf_op jit(solution)/shard_map/ppermute | solution.py:290
  58.6 1.5 %collective-permute-start.17 = (s16[272,256]{1,0:T(8,128)(2,1)S(1)}, s16[272,256]{1,0:T(8,128)(2,1)S(1)}, u32[]{:S(2)}, u32[]{:S(2)}) collective-permute-start(s16[272,256]{1,0:T(8,128)(2,1)S(1)} %get-tuple-element.41), channel_id=1, source_target_pairs={{0,24},{8,16},{16,8},{24,0},{1,25},{9,17},{17,9},{25,1},{2,26},{10... | collective-permute-start | bytes 417800 | tf_op jit(solution)/shard_map/ppermute | solution.py:290
  60.6 2.2 %collective-permute-done.15.refs_0_ = s16[272,256]{1,0:T(8,128)(2,1)S(1)} collective-permute-done((s16[272,256]{1,0:T(8,128)(2,1)S(1)}, s16[272,256]{1,0:T(8,128)(2,1)S(1)}, u32[]{:S(2)}, u32[]{:S(2)}) %collective-permute-start.15) | collective-permute-done | bytes 139296 | tf_op jit(solution)/shard_map/ppermute | solution.py:290
  62.9 4.2 %collective-permute-done.16.refs_1_ = s16[272,256]{1,0:T(8,128)(2,1)S(1)} collective-permute-done((s16[272,256]{1,0:T(8,128)(2,1)S(1)}, s16[272,256]{1,0:T(8,128)(2,1)S(1)}, u32[]{:S(2)}, u32[]{:S(2)}) %collective-permute-start.16) | collective-permute-done | bytes 139296 | tf_op jit(solution)/shard_map/ppermute | solution.py:290
  67.0 1.6 %head.1 = (f32[256,172]{1,0:T(8,128)S(1)}, f32[48,256]{1,0:T(8,128)S(1)}, bf16[304,256]{1,0:T(8,128)(2,1)S(1)}, bf16[304,256]{1,0:T(8,128)(2,1)S(1)}, bf16[304,2...) custom-call(s32[2]{0:T(128)S(1)} %pad_add_fusion.1.spot_ref, bf16[256,172]{1,0:T(8,128)(2,1)S(1)} %copy.15.weight_ref, ...), custom_call_target="tpu_custom_call" | custom-call | tf_op jit(solution)/shard_map/head/pallas_call | solution.py:178
  69.1 1.4 %collective-permute-start.19 = (bf16[304,256]{1,0:T(8,128)(2,1)S(1)}, bf16[304,256]{1,0:T(8,128)(2,1)S(1)}, u32[]{:S(2)}, u32[]{:S(2)}) collective-permute-start(bf16[304,256]{1,0:T(8,128)(2,1)S(1)} %get-tuple-element.46), channel_id=1, source_target_pairs={{0,16},{8,24},{16,0},{24,8},{1,17},{9,25},{17,1},{25,9},{2,18},{10... | collective-permute-start | bytes 466952 | tf_op jit(solution)/shard_map/ppermute | solution.py:290
  70.5 1.7 %collective-permute-start.20 = (bf16[304,256]{1,0:T(8,128)(2,1)S(1)}, bf16[304,256]{1,0:T(8,128)(2,1)S(1)}, u32[]{:S(2)}, u32[]{:S(2)}) collective-permute-start(bf16[304,256]{1,0:T(8,128)(2,1)S(1)} %get-tuple-element.47), channel_id=1, source_target_pairs={{0,24},{8,16},{16,8},{24,0},{1,25},{9,17},{17,9},{25,1},{2,26},{10... | collective-permute-start | bytes 466952 | tf_op jit(solution)/shard_map/ppermute | solution.py:290
  72.2 3.0 %collective-permute-done.18 = bf16[304,256]{1,0:T(8,128)(2,1)S(1)} collective-permute-done((bf16[304,256]{1,0:T(8,128)(2,1)S(1)}, bf16[304,256]{1,0:T(8,128)(2,1)S(1)}, u32[]{:S(2)}, u32[]{:S(2)}) %collective-permute-start.18) | collective-permute-done | bytes 155680 | tf_op jit(solution)/shard_map/ppermute | solution.py:290
  75.2 2.4 %collective-permute-done.19 = bf16[304,256]{1,0:T(8,128)(2,1)S(1)} collective-permute-done((bf16[304,256]{1,0:T(8,128)(2,1)S(1)}, bf16[304,256]{1,0:T(8,128)(2,1)S(1)}, u32[]{:S(2)}, u32[]{:S(2)}) %collective-permute-start.19) | collective-permute-done | bytes 155680 | tf_op jit(solution)/shard_map/ppermute | solution.py:290
  77.7 4.6 %fusion = bf16[2048,256]{1,0:T(8,128)(2,1)S(1)} fusion(bf16[2048,1024]{1,0:T(8,128)(2,1)} %copy-done.5, bf16[2048,256]{1,0:T(8,128)(2,1)} %fusion.4, f32[2048,256]{1,0:T(8,128)} %copy-done.6, bf16[256,256]{1,0:T(8,128)(2,1)S(1)} %slice.327, bf16[256,256]{1,0:T(8,128)(2,1)S(1)} %slice.326, bf16[256,256]{1,0:T(8,128)(2,1)S(1)} %slice.325, ...), kind=kOutput, calls=%fused_computation.5 | convolution fusion | flops 1078984704 | bytes 8912896 | tf_op jit(solution)/shard_map/dot_general | solution.py:32
  84.7 1.8 %collective-permute-start.23 = (bf16[88,256]{1,0:T(8,128)(2,1)S(1)}, bf16[88,256]{1,0:T(8,128)(2,1)S(1)}, u32[]{:S(2)}, u32[]{:S(2)}) collective-permute-start(bf16[88,256]{1,0:T(8,128)(2,1)S(1)} %fusion.18), channel_id=1, source_target_pairs={{0,4},{1,5},{2,6},{3,7},{4,0},{5,1},{6,2},{7,3},{8,12},{9,13},{10,... | collective-permute-start | bytes 135176 | tf_op jit(solution)/shard_map/ppermute | solution.py:296
  86.5 2.1 %collective-permute-start.24 = (bf16[88,256]{1,0:T(8,128)(2,1)S(1)}, bf16[88,256]{1,0:T(8,128)(2,1)S(1)}, u32[]{:S(2)}, u32[]{:S(2)}) collective-permute-start(bf16[88,256]{1,0:T(8,128)(2,1)S(1)} %fusion.18), channel_id=1, source_target_pairs={{0,6},{1,7},{2,4},{3,5},{4,2},{5,3},{6,0},{7,1},{8,14},{9,15},{10,... | collective-permute-start | bytes 135176 | tf_op jit(solution)/shard_map/ppermute | solution.py:296
  90.0 2.4 %collective-permute-done.24 = bf16[88,256]{1,0:T(8,128)(2,1)S(1)} collective-permute-done((bf16[88,256]{1,0:T(8,128)(2,1)S(1)}, bf16[88,256]{1,0:T(8,128)(2,1)S(1)}, u32[]{:S(2)}, u32[]{:S(2)}) %collective-permute-start.24) | collective-permute-done | bytes 45088 | tf_op jit(solution)/shard_map/ppermute | solution.py:296
  94.5 1.4 %collective-permute-start.27 = (bf16[88,256]{1,0:T(8,128)(2,1)S(1)}, bf16[88,256]{1,0:T(8,128)(2,1)S(1)}, u32[]{:S(2)}, u32[]{:S(2)}) collective-permute-start(bf16[88,256]{1,0:T(8,128)(2,1)S(1)} %add_convert_fusion), channel_id=1, source_target_pairs={{0,24},{8,16},{16,8},{24,0},{1,25},{9,17},{17,9},{25,1},{2,26},{10... | collective-permute-start | bytes 135176 | tf_op jit(solution)/shard_map/ppermute | solution.py:290
  97.6 1.8 %collective-permute-done.27 = bf16[88,256]{1,0:T(8,128)(2,1)S(1)} collective-permute-done((bf16[88,256]{1,0:T(8,128)(2,1)S(1)}, bf16[88,256]{1,0:T(8,128)(2,1)S(1)}, u32[]{:S(2)}, u32[]{:S(2)}) %collective-permute-start.27) | collective-permute-done | bytes 45088 | tf_op jit(solution)/shard_map/ppermute | solution.py:290
  (126 shorter events, 21.5 us)
Async XLA Ops:
  0.6 52.5 %copy-start = (bf16[128,256]{1,0:T(8,128)(2,1)S(1)}, bf16[128,256]{1,0:T(8,128)(2,1)}, u32[]{:S(2)}) copy-start(bf16[128,256]{1,0:T(8,128)(2,1)} %param.17) | copy-start | bytes 196612
  2.7 19.2 %collective-permute-start.1 = (bf16[272,128]{1,0:T(8,128)(2,1)}, bf16[272,128]{1,0:T(8,128)(2,1)S(1)}, u32[]{:S(2)}, u32[]{:S(2)}) collective-permute-start(bf16[272,128]{1,0:T(8,128)(2,1)} %get-tuple-element.31), channel_id=1, source_target_pairs={{0,0},{1,1},{2,2},{3,3},{4,4},{5,5},{6,6},{7,7},{8,10},{9,11},{10,... | collective-permute-start | bytes 208904 | tf_op jit(solution)/shard_map/ppermute | solution.py:306
  4.2 17.7 %collective-permute-start.2 = (bf16[272,128]{1,0:T(8,128)(2,1)}, bf16[272,128]{1,0:T(8,128)(2,1)S(1)}, u32[]{:S(2)}, u32[]{:S(2)}) collective-permute-start(bf16[272,128]{1,0:T(8,128)(2,1)} %get-tuple-element.31), channel_id=1, source_target_pairs={{0,10},{1,11},{2,12},{3,13},{4,14},{5,15},{6,8},{7,9},{8,0},{9,1},... | collective-permute-start | bytes 208904 | tf_op jit(solution)/shard_map/ppermute | solution.py:306
  10.2 11.8 %collective-permute-start.3 = (bf16[272,128]{1,0:T(8,128)(2,1)}, bf16[272,128]{1,0:T(8,128)(2,1)S(1)}, u32[]{:S(2)}, u32[]{:S(2)}) collective-permute-start(bf16[272,128]{1,0:T(8,128)(2,1)} %get-tuple-element.31), channel_id=1, source_target_pairs={{0,20},{1,21},{2,22},{3,23},{4,16},{5,17},{6,18},{7,19},{8,30},{9,... | collective-permute-start | bytes 208904 | tf_op jit(solution)/shard_map/ppermute | solution.py:306
  11.5 10.5 %collective-permute-start.4 = (bf16[272,128]{1,0:T(8,128)(2,1)}, bf16[272,128]{1,0:T(8,128)(2,1)S(1)}, u32[]{:S(2)}, u32[]{:S(2)}) collective-permute-start(bf16[272,128]{1,0:T(8,128)(2,1)} %get-tuple-element.31), channel_id=1, source_target_pairs={{0,30},{1,31},{2,24},{3,25},{4,26},{5,27},{6,28},{7,29},{8,20},{9,... | collective-permute-start | bytes 208904 | tf_op jit(solution)/shard_map/ppermute | solution.py:306
  14.5 32.4 %collective-permute-start = (bf16[17,128,128]{2,1,0:T(8,128)(2,1)}, bf16[17,128,128]{2,1,0:T(8,128)(2,1)S(1)}, u32[]{:S(2)}, u32[]{:S(2)}) collective-permute-start(bf16[17,128,128]{2,1,0:T(8,128)(2,1)} %get-tuple-element.28), channel_id=1, source_target_pairs={{0,8},{2,10},{4,12},{6,14},{8,16},{10,18},{12,20},{14,22},{16,24},... | collective-permute-start | bytes 1671176 | tf_op jit(solution)/shard_map/ppermute | solution.py:364
  22.0 7.8 %collective-permute-start.5 = (bf16[1088,128]{1,0:T(8,128)(2,1)S(1)}, bf16[1088,128]{1,0:T(8,128)(2,1)S(1)}, u32[]{:S(2)}, u32[]{:S(2)}) collective-permute-start(bf16[1088,128]{1,0:T(8,128)(2,1)S(1)} %pad_maximum_fusion), channel_id=1, source_target_pairs={{0,1},{1,2},{2,3},{3,4},{4,5},{5,6},{6,7},{7,0},{8,9},{9,10},{10,1... | collective-permute-start | bytes 835592 | tf_op jit(solution)/shard_map/ppermute | solution.py:293
  22.1 1.7 %collective-permute-start.13 = (bf16[4,16,128]{2,1,0:T(8,128)(2,1)S(1)}, bf16[4,16,128]{2,1,0:T(8,128)(2,1)S(1)}, u32[]{:S(2)}, u32[]{:S(2)}) collective-permute-start(bf16[4,16,128]{2,1,0:T(8,128)(2,1)S(1)} %pad_maximum_fusion.3), channel_id=1, source_target_pairs={{0,1},{1,0},{2,3},{3,2},{4,5},{5,4},{6,7},{7,6},{8,9},{9,8},{10,11... | collective-permute-start | bytes 49160 | tf_op jit(solution)/shard_map/ppermute | solution.py:296
  31.1 15.8 %slice-start = ((s32[2,16]{1,0:T(2,128)}), s32[1,16]{1,0:T(1,128)S(1)}, s32[]{:S(2)}) async-start(s32[2,16]{1,0:T(2,128)} %copy-done.3), calls=%async_computation | async-start | bytes 1024 | tf_op jit(solution)/shard_map/slice | solution.py:365
  31.1 16.4 %copy-start.2 = (bf16[1,1,2,16,128,128]{5,4,3,2,1,0:T(8,128)(2,1)S(1)}, bf16[1,1,2,16,128,128]{5,4,3,2,1,0:T(8,128)(2,1)}, u32[]{:S(2)}) copy-start(bf16[1,1,2,16,128,128]{5,4,3,2,1,0:T(8,128)(2,1)} %param.14) | copy-start | bytes 3145732
  31.2 5.2 %collective-permute-start.6 = (f32[256,128]{1,0:T(8,128)S(1)}, f32[256,128]{1,0:T(8,128)S(1)}, u32[]{:S(2)}, u32[]{:S(2)}) collective-permute-start(f32[256,128]{1,0:T(8,128)S(1)} %get-tuple-element.59), channel_id=1, source_target_pairs={{0,8},{8,0},{16,24},{24,16},{1,9},{9,1},{17,25},{25,17},{2,10},{10... | collective-permute-start | bytes 393224 | tf_op jit(solution)/shard_map/ppermute | solution.py:290
  32.8 5.0 %collective-permute-start.7 = (f32[256,128]{1,0:T(8,128)S(1)}, f32[256,128]{1,0:T(8,128)S(1)}, u32[]{:S(2)}, u32[]{:S(2)}) collective-permute-start(f32[256,128]{1,0:T(8,128)S(1)} %get-tuple-element.61), channel_id=1, source_target_pairs={{0,16},{8,24},{16,0},{24,8},{1,17},{9,25},{17,1},{25,9},{2,18},{10... | collective-permute-start | bytes 393224 | tf_op jit(solution)/shard_map/ppermute | solution.py:290
  34.0 5.9 %collective-permute-start.8 = (f32[256,128]{1,0:T(8,128)S(1)}, f32[256,128]{1,0:T(8,128)S(1)}, u32[]{:S(2)}, u32[]{:S(2)}) collective-permute-start(f32[256,128]{1,0:T(8,128)S(1)} %get-tuple-element.60), channel_id=1, source_target_pairs={{0,24},{8,16},{16,8},{24,0},{1,25},{9,17},{17,9},{25,1},{2,26},{10... | collective-permute-start | bytes 393224 | tf_op jit(solution)/shard_map/ppermute | solution.py:290
  40.0 11.4 %collective-permute-start.10 = (bf16[256,128]{1,0:T(8,128)(2,1)S(1)}, bf16[256,128]{1,0:T(8,128)(2,1)S(1)}, u32[]{:S(2)}, u32[]{:S(2)}) collective-permute-start(bf16[256,128]{1,0:T(8,128)(2,1)S(1)} %fusion.17), channel_id=1, source_target_pairs={{0,10},{1,11},{2,12},{3,13},{4,14},{5,15},{6,8},{7,9},{8,0},{9,1},... | collective-permute-start | bytes 196616 | tf_op jit(solution)/shard_map/ppermute | solution.py:306
  40.0 11.3 %collective-permute-start.11 = (bf16[256,128]{1,0:T(8,128)(2,1)S(1)}, bf16[256,128]{1,0:T(8,128)(2,1)S(1)}, u32[]{:S(2)}, u32[]{:S(2)}) collective-permute-start(bf16[256,128]{1,0:T(8,128)(2,1)S(1)} %fusion.17), channel_id=1, source_target_pairs={{0,20},{1,21},{2,22},{3,23},{4,16},{5,17},{6,18},{7,19},{8,30},{9,... | collective-permute-start | bytes 196616 | tf_op jit(solution)/shard_map/ppermute | solution.py:306
  41.5 9.9 %collective-permute-start.12 = (bf16[256,128]{1,0:T(8,128)(2,1)S(1)}, bf16[256,128]{1,0:T(8,128)(2,1)S(1)}, u32[]{:S(2)}, u32[]{:S(2)}) collective-permute-start(bf16[256,128]{1,0:T(8,128)(2,1)S(1)} %fusion.17), channel_id=1, source_target_pairs={{0,30},{1,31},{2,24},{3,25},{4,26},{5,27},{6,28},{7,29},{8,20},{9,... | collective-permute-start | bytes 196616 | tf_op jit(solution)/shard_map/ppermute | solution.py:306
  46.2 5.2 %collective-permute-start.9 = (bf16[256,128]{1,0:T(8,128)(2,1)S(1)}, bf16[256,128]{1,0:T(8,128)(2,1)S(1)}, u32[]{:S(2)}, u32[]{:S(2)}) collective-permute-start(bf16[256,128]{1,0:T(8,128)(2,1)S(1)} %fusion.17), channel_id=1, source_target_pairs={{0,0},{1,1},{2,2},{3,3},{4,4},{5,5},{6,6},{7,7},{8,10},{9,11},{10,... | collective-permute-start | bytes 196616 | tf_op jit(solution)/shard_map/ppermute | solution.py:306
  51.5 1.6 %collective-permute-start.14 = (bf16[1024,128]{1,0:T(8,128)(2,1)S(1)}, bf16[1024,128]{1,0:T(8,128)(2,1)S(1)}, u32[]{:S(2)}, u32[]{:S(2)}) collective-permute-start(bf16[1024,128]{1,0:T(8,128)(2,1)S(1)} %pad_maximum_fusion.1), channel_id=1, source_target_pairs={{0,1},{1,0},{2,3},{3,2},{4,5},{5,4},{6,7},{7,6},{8,9},{9,8},{10,11... | collective-permute-start | bytes 786440 | tf_op jit(solution)/shard_map/ppermute | solution.py:296
  55.4 7.5 %collective-permute-start.15 = (s16[272,256]{1,0:T(8,128)(2,1)S(1)}, s16[272,256]{1,0:T(8,128)(2,1)S(1)}, u32[]{:S(2)}, u32[]{:S(2)}) collective-permute-start(s16[272,256]{1,0:T(8,128)(2,1)S(1)} %get-tuple-element.39), channel_id=1, source_target_pairs={{0,8},{8,0},{16,24},{24,16},{1,9},{9,1},{17,25},{25,17},{2,10},{10... | collective-permute-start | bytes 417800 | tf_op jit(solution)/shard_map/ppermute | solution.py:290
  58.6 8.4 %collective-permute-start.16 = (s16[272,256]{1,0:T(8,128)(2,1)S(1)}, s16[272,256]{1,0:T(8,128)(2,1)S(1)}, u32[]{:S(2)}, u32[]{:S(2)}) collective-permute-start(s16[272,256]{1,0:T(8,128)(2,1)S(1)} %get-tuple-element.40), channel_id=1, source_target_pairs={{0,16},{8,24},{16,0},{24,8},{1,17},{9,25},{17,1},{25,9},{2,18},{10... | collective-permute-start | bytes 417800 | tf_op jit(solution)/shard_map/ppermute | solution.py:290
  58.6 8.4 %collective-permute-start.17 = (s16[272,256]{1,0:T(8,128)(2,1)S(1)}, s16[272,256]{1,0:T(8,128)(2,1)S(1)}, u32[]{:S(2)}, u32[]{:S(2)}) collective-permute-start(s16[272,256]{1,0:T(8,128)(2,1)S(1)} %get-tuple-element.41), channel_id=1, source_target_pairs={{0,24},{8,16},{16,8},{24,0},{1,25},{9,17},{17,9},{25,1},{2,26},{10... | collective-permute-start | bytes 417800 | tf_op jit(solution)/shard_map/ppermute | solution.py:290
  68.7 6.6 %collective-permute-start.18 = (bf16[304,256]{1,0:T(8,128)(2,1)S(1)}, bf16[304,256]{1,0:T(8,128)(2,1)S(1)}, u32[]{:S(2)}, u32[]{:S(2)}) collective-permute-start(bf16[304,256]{1,0:T(8,128)(2,1)S(1)} %get-tuple-element.45), channel_id=1, source_target_pairs={{0,8},{8,0},{16,24},{24,16},{1,9},{9,1},{17,25},{25,17},{2,10},{10... | collective-permute-start | bytes 466952 | tf_op jit(solution)/shard_map/ppermute | solution.py:290
  69.1 8.6 %collective-permute-start.19 = (bf16[304,256]{1,0:T(8,128)(2,1)S(1)}, bf16[304,256]{1,0:T(8,128)(2,1)S(1)}, u32[]{:S(2)}, u32[]{:S(2)}) collective-permute-start(bf16[304,256]{1,0:T(8,128)(2,1)S(1)} %get-tuple-element.46), channel_id=1, source_target_pairs={{0,16},{8,24},{16,0},{24,8},{1,17},{9,25},{17,1},{25,9},{2,18},{10... | collective-permute-start | bytes 466952 | tf_op jit(solution)/shard_map/ppermute | solution.py:290
  70.5 7.2 %collective-permute-start.20 = (bf16[304,256]{1,0:T(8,128)(2,1)S(1)}, bf16[304,256]{1,0:T(8,128)(2,1)S(1)}, u32[]{:S(2)}, u32[]{:S(2)}) collective-permute-start(bf16[304,256]{1,0:T(8,128)(2,1)S(1)} %get-tuple-element.47), channel_id=1, source_target_pairs={{0,24},{8,16},{16,8},{24,0},{1,25},{9,17},{17,9},{25,1},{2,26},{10... | collective-permute-start | bytes 466952 | tf_op jit(solution)/shard_map/ppermute | solution.py:290
  82.7 1.4 %collective-permute-start.21 = (f32[88,256]{1,0:T(8,128)S(1)}, f32[88,256]{1,0:T(8,128)S(1)}, u32[]{:S(2)}, u32[]{:S(2)}) collective-permute-start(f32[88,256]{1,0:T(8,128)S(1)} %pad_maximum_fusion.2), channel_id=1, source_target_pairs={{0,1},{1,0},{2,3},{3,2},{4,5},{5,4},{6,7},{7,6},{8,9},{9,8},{10,11... | collective-permute-start | bytes 270344 | tf_op jit(solution)/shard_map/ppermute | solution.py:296
  84.1 4.6 %collective-permute-start.22 = (bf16[88,256]{1,0:T(8,128)(2,1)S(1)}, bf16[88,256]{1,0:T(8,128)(2,1)S(1)}, u32[]{:S(2)}, u32[]{:S(2)}) collective-permute-start(bf16[88,256]{1,0:T(8,128)(2,1)S(1)} %fusion.18), channel_id=1, source_target_pairs={{0,2},{1,3},{2,0},{3,1},{4,6},{5,7},{6,4},{7,5},{8,10},{9,11},{10,... | collective-permute-start | bytes 135176 | tf_op jit(solution)/shard_map/ppermute | solution.py:296
  84.7 5.3 %collective-permute-start.23 = (bf16[88,256]{1,0:T(8,128)(2,1)S(1)}, bf16[88,256]{1,0:T(8,128)(2,1)S(1)}, u32[]{:S(2)}, u32[]{:S(2)}) collective-permute-start(bf16[88,256]{1,0:T(8,128)(2,1)S(1)} %fusion.18), channel_id=1, source_target_pairs={{0,4},{1,5},{2,6},{3,7},{4,0},{5,1},{6,2},{7,3},{8,12},{9,13},{10,... | collective-permute-start | bytes 135176 | tf_op jit(solution)/shard_map/ppermute | solution.py:296
  86.5 5.8 %collective-permute-start.24 = (bf16[88,256]{1,0:T(8,128)(2,1)S(1)}, bf16[88,256]{1,0:T(8,128)(2,1)S(1)}, u32[]{:S(2)}, u32[]{:S(2)}) collective-permute-start(bf16[88,256]{1,0:T(8,128)(2,1)S(1)} %fusion.18), channel_id=1, source_target_pairs={{0,6},{1,7},{2,4},{3,5},{4,2},{5,3},{6,0},{7,1},{8,14},{9,15},{10,... | collective-permute-start | bytes 135176 | tf_op jit(solution)/shard_map/ppermute | solution.py:296
  92.3 4.4 %collective-permute-start.25 = (bf16[88,256]{1,0:T(8,128)(2,1)S(1)}, bf16[88,256]{1,0:T(8,128)(2,1)S(1)}, u32[]{:S(2)}, u32[]{:S(2)}) collective-permute-start(bf16[88,256]{1,0:T(8,128)(2,1)S(1)} %add_convert_fusion), channel_id=1, source_target_pairs={{0,8},{8,0},{16,24},{24,16},{1,9},{9,1},{17,25},{25,17},{2,10},{10... | collective-permute-start | bytes 135176 | tf_op jit(solution)/shard_map/ppermute | solution.py:290
  93.6 4.0 %collective-permute-start.26 = (bf16[88,256]{1,0:T(8,128)(2,1)S(1)}, bf16[88,256]{1,0:T(8,128)(2,1)S(1)}, u32[]{:S(2)}, u32[]{:S(2)}) collective-permute-start(bf16[88,256]{1,0:T(8,128)(2,1)S(1)} %add_convert_fusion), channel_id=1, source_target_pairs={{0,16},{8,24},{16,0},{24,8},{1,17},{9,25},{17,1},{25,9},{2,18},{10... | collective-permute-start | bytes 135176 | tf_op jit(solution)/shard_map/ppermute | solution.py:290
  94.5 4.9 %collective-permute-start.27 = (bf16[88,256]{1,0:T(8,128)(2,1)S(1)}, bf16[88,256]{1,0:T(8,128)(2,1)S(1)}, u32[]{:S(2)}, u32[]{:S(2)}) collective-permute-start(bf16[88,256]{1,0:T(8,128)(2,1)S(1)} %add_convert_fusion), channel_id=1, source_target_pairs={{0,24},{8,16},{16,8},{24,0},{1,25},{9,17},{17,9},{25,1},{2,26},{10... | collective-permute-start | bytes 135176 | tf_op jit(solution)/shard_map/ppermute | solution.py:290
  99.5 1.5 %collective-permute-start.28 = (f32[160,256]{1,0:T(8,128)S(1)}, f32[160,256]{1,0:T(8,128)S(1)}, u32[]{:S(2)}, u32[]{:S(2)}) collective-permute-start(f32[160,256]{1,0:T(8,128)S(1)} %constant_dynamic-update-slice_fusion.6.total_ref), channel_id=1, source_target_pairs={{0,1},{1,0},{2,3},{3,2},{4,5},{5,4},{6,7},{7,6},{8,9},{9,8},{10,11... | collective-permute-start | bytes 491528 | tf_op jit(solution)/shard_map/ppermute | solution.py:296
  (9 other events, 44.6 us)

commit v7 on v6

--- a/solution.py
+++ b/solution.py
@@ -185,15 +185,15 @@
     )(*spot, *values)
 
 
-def dense_kernel(per_rep, tile_side, spot_ref, order_ref, moved_ref, place_ref, own_ref, *refs):
-    other_ref, dense_ref, turned_ref = refs if len(refs) == 3 else (None, refs[0], None)
+def dense_kernel(
+    per_rep, tile_side, turn, spot_ref, order_ref, moved_ref, place_ref, own_ref, *refs
+):
+    other_ref, dense_ref = refs if len(refs) == 2 else (None, refs[0])
     position = pl.program_id(0)
-    rep_index = spot_ref[0]
+    rep_index, source_rep = spot_ref[0], spot_ref[1 + position]
     edge = own_ref.shape[-1]
     slots = place_ref.shape[1]
     dense_ref[...] = jnp.zeros_like(dense_ref)
-    if turned_ref is not None:
-        turned_ref[...] = jnp.zeros_like(turned_ref)
 
     def put_all(tiles_ref):
         def put(slot, carried):
@@ -201,16 +201,17 @@
             row = place // tile_side
             column = place % tile_side
             row = ((row // per_rep) ^ rep_index) * per_rep + row % per_rep
-            column = ((column // per_rep) ^ rep_index) * per_rep + column % per_rep
+            column = ((column // per_rep) ^ source_rep) * per_rep + column % per_rep
 
             @pl.when(place >= 0)
             def _():
                 rows = pl.ds(pl.multiple_of(row * edge, edge), edge)
                 columns = pl.ds(pl.multiple_of(column * edge, edge), edge)
                 tile = tiles_ref[0, slot]
-                dense_ref[rows, columns] = tile
-                if turned_ref is not None:
-                    turned_ref[columns, rows] = tile.T
+                if turn:
+                    dense_ref[columns, rows] = tile.T
+                else:
+                    dense_ref[rows, columns] = tile
 
             return carried
 
@@ -229,9 +230,9 @@
         put_all(other_ref)
 
 
-def build_dense(tiles, others, place, spot, order, moved, own_rows, group_rows):
+def build_dense(tiles, others, place, spot, order, moved, own_rows, group_rows, turn=False):
     sections, slots, edge, _ = tiles.shape
-    body = functools.partial(dense_kernel, own_rows // edge, group_rows // edge)
+    body = functools.partial(dense_kernel, own_rows // edge, group_rows // edge, turn)
     own_block = pl.BlockSpec((1, slots, edge, edge), lambda p, spot, order, *_: (order[p], 0, 0, 0))
     other_block = pl.BlockSpec(
         (1, slots + 1, edge, edge),
@@ -239,24 +240,21 @@
     )
     both = others is not None
     block = (group_rows, group_rows)
-    flat = jax.ShapeDtypeStruct((group_rows, sections * group_rows), tiles.dtype)
-    tall = jax.ShapeDtypeStruct((sections * group_rows, group_rows), tiles.dtype)
-    flat_spec = pl.BlockSpec(block, lambda p, *_: (0, p))
-    tall_spec = pl.BlockSpec(block, lambda p, *_: (p, 0))
+    shape = (sections * group_rows, group_rows) if turn else (group_rows, sections * group_rows)
     return pl.pallas_call(
         body,
         grid_spec=pltpu.PrefetchScalarGridSpec(
             num_scalar_prefetch=4,
             grid=(sections,),
             in_specs=[own_block, other_block] if both else [own_block],
-            out_specs=[flat_spec, tall_spec] if both else flat_spec,
+            out_specs=pl.BlockSpec(block, lambda p, *_: (p, 0) if turn else (0, p)),
         ),
-        out_shape=[flat, tall] if both else flat,
+        out_shape=jax.ShapeDtypeStruct(shape, tiles.dtype),
         compiler_params=pltpu.CompilerParams(vmem_limit_bytes=40 * 1024 * 1024),
         cost_estimate=pl.CostEstimate(
             flops=0, bytes_accessed=4 * sections * group_rows * group_rows, transcendentals=0
         ),
-        name="dense_both" if both else "dense_first",
+        name="dense_turned" if turn else "dense",
     )(spot, order, moved, place, *([tiles, others] if both else [tiles]))
 
 
@@ -289,8 +287,16 @@
             return value
         return lax.ppermute(value, "rep", [(r, r ^ delta) for r in range(reps)])
 
-    def shift(value, steps):
-        return lax.ppermute(value, "blk", [(c, (c + steps) % blks) for c in range(blks)])
+    def to_section(block, j):
+        pairs = []
+        for r in range(reps):
+            for c in range(blks):
+                member = c % sections + j
+                if member < sections:
+                    pairs.append((r * blks + c, r * blks + c + j))
+                else:
+                    pairs.append((r * blks + c, (r - 1) % reps * blks + c + j - sections))
+        return lax.ppermute(block, ("rep", "blk"), pairs)
 
     def exchange(value, delta):
         return lax.ppermute(value, "blk", [(c, c ^ delta) for c in range(blks)])
@@ -370,10 +376,15 @@
     moved = (column > member).astype(jnp.int32)
     placed = jnp.where(moved[:, None] != 0, jnp.stack(other_place)[order], place[order])
     tiles = tile_values[0, 0]
-    where = rep_index.reshape(1)
-    dense = build_dense(tiles, None, place, where, position, position, own_rows, group_rows)
+    where = jnp.broadcast_to(rep_index, (sections + 1,))
+    next_rep = lax.rem(rep_index + 1, reps)
+    first_where = jnp.where(member < jnp.arange(sections + 1) - 1, next_rep, rep_index)
     block = jnp.concatenate(arrived, axis=0)
-    blocks = [block] + [shift(block, j) for j in range(1, sections)]
+    place, block = lax.optimization_barrier((place, block))
+    dense = build_dense(
+        tiles, None, place, first_where, position, position, own_rows, group_rows
+    )
+    blocks = [block] + [to_section(block, j) for j in range(1, sections)]
     pieces = [whole[d * stride : (d + 1) * stride] for whole in blocks for d in range(reps)]
     digit_sets = to_both(jnp.stack([part[own_rows:] for part in pieces[:reps]]))
     id_columns = jnp.concatenate([undo_digits(rows[d]) for rows in digit_sets for d in range(reps)])
@@ -381,21 +392,20 @@
     units = jnp.arange(hidden_width, dtype=jnp.int32)
     kept = keep_mask(id_columns[:, None], units[None, :])
     chunks = dot(dense, feature_columns).reshape(reps, own_rows, width)
-    dense, turned = build_dense(
-        tiles, jnp.stack(parcels), placed, where, order, moved, own_rows, group_rows
-    )
+    layout = (tiles, jnp.stack(parcels), placed, where, order, moved, own_rows, group_rows)
+    arrived = [swap(chunks[delta], delta) for delta in range(1, reps)]
+    dense, arrived = lax.optimization_barrier((build_dense(*layout), arrived))
     total = chunks[0]
-    for delta in range(1, reps):
-        total = total + swap(chunks[delta], delta)
+    for part in arrived:
+        total = total + part
     z_input = total.astype(bf16)
     arrived = to_pieces(z_input)
-    dense, turned, arrived = lax.optimization_barrier((dense, turned, arrived))
     z_columns = jnp.concatenate(to_both(jnp.concatenate(arrived, axis=0)), axis=0)
     kept, z_columns = lax.optimization_barrier((kept, z_columns))
     third = f32(4.0 / 3.0)
     pre_act = dot(z_columns, weight_in)
-    factor = kept.astype(f32) * third
-    dropped = (jnp.maximum(pre_act, 0.0) * factor).astype(bf16)
+    dropped = (jnp.maximum(pre_act, 0.0) * (kept.astype(f32) * third)).astype(bf16)
+    mask = jnp.where(pre_act > 0, kept, jnp.zeros_like(kept))
     second = dot(dense, dropped)
     sent = simple_call(
         encode_kernel,
@@ -403,6 +413,9 @@
         "encode", second,
     )
     arrived = [swap(sent[d - 1], d) for d in range(1, reps)]
+    turned, mask, second = lax.optimization_barrier(
+        (build_dense(*layout, turn=True), mask, second)
+    )
     classes = weight_out.shape[1]
     chunk = -(-classes // (16 * reps)) * 16
     spot = jnp.stack([side, rep_index])
@@ -423,8 +436,9 @@
     grad_block = jnp.concatenate([part[:own_rows] for part in arrived], axis=0)
     for part in arrived[1:]:
         out_total = out_total + part[own_rows:].astype(f32)
+    grad_block, out_total = lax.optimization_barrier((grad_block, out_total))
     back = dot(turned, grad_block)
-    pre_slope = (back * jnp.where(pre_act > 0, factor, 0.0)).astype(bf16)
+    pre_slope = (back * (mask.astype(f32) * third)).astype(bf16)
     pre_slope, out_total = lax.optimization_barrier((pre_slope, out_total))
     in_terms = lax.dot_general(
         z_columns, pre_slope, (((0,), (0,)), ((), ())), preferred_element_type=f32

time: 102 us -> 105 us (1.029)
  waiting for transfers between devices: 32.7 us -> 24.6 us
  starting transfers between devices: 42.2 us -> 50.2 us
  Pallas kernels: 11.4 us -> 13.7 us
    ppermute x12, waiting for transfers between devices: 18.9 us -> 13.1 us  [swap(): return lax.ppermute(value, 'rep', [(r, r ^ delta) for r in range(reps)])]
    ppermute x12, starting transfers between devices: 15.5 us -> 19.3 us  [swap(): return lax.ppermute(value, 'rep', [(r, r ^ delta) for r in range(reps)])]
    ppermute x8, starting transfers between devices: 18.7 us -> 21.2 us  [to_pieces(): pieces.append(lax.ppermute(value, ('rep', 'blk'), pairs))]
    ppermute x7, waiting for transfers between devices: 7.82 us -> 6.03 us  [exchange(): return lax.ppermute(value, 'blk', [(c, c ^ delta) for c in range(blks)])]
    ppermute x7, starting transfers between devices: 5.51 us -> 7.16 us  [exchange(): return lax.ppermute(value, 'blk', [(c, c ^ delta) for c in range(blks)])]
    pallas_call x2 -> x3, Pallas kernels: 6.1 us -> 7.64 us  [build_dense(): pl.pallas_call(body, grid_spec=pltpu.PrefetchScalarGridSpec(num_scalar_pr...]
    ppermute x1, waiting for transfers between devices: 5.95 us -> 4.45 us  [to_section(): return lax.ppermute(block, ('rep', 'blk'), pairs)]
    unnamed x35 -> x33, local copies, waits for them, and re-layouts: 2.31 us -> 3.02 us
  transfers between devices with their start and end apart: 29 -> 29, of which waited for: 17 -> 14; matrix products, arithmetic and copies ran while one was open for 6% -> 5% of each run, Pallas kernels for 6% -> 7%
where the time goes in v7:
time: 105 us
  starting transfers between devices  50.2 us (48%)
  waiting for transfers between devices  24.6 us (23%)
  Pallas kernels  13.7 us (13%)
  matrix products  8.12 us (8%)
  local copies, waits for them, and re-layouts  4.57 us (4%)
  other arithmetic  2.2 us (2%)
  between operations  1.3 us (1%)
    ppermute x8, starting transfers between devices, to_pieces(): pieces.append(lax.ppermute(value, ('rep', 'blk'), pairs))  21.2 us
    ppermute x12, starting transfers between devices, swap(): return lax.ppermute(value, 'rep', [(r, r ^ delta) for r in range(reps)])  19.3 us
    ppermute x12, waiting for transfers between devices, swap(): return lax.ppermute(value, 'rep', [(r, r ^ delta) for r in range(reps)])  13.1 us
    dot_general x4, matrix products, dot(): return jnp.dot(left, right, preferred_element_type=jnp.float32)  7.77 us
    pallas_call x3, Pallas kernels, build_dense(): pl.pallas_call(body, grid_spec=pltpu.PrefetchScalarGridSpec(num_scalar_pr...  7.64 us
    ppermute x7, starting transfers between devices, exchange(): return lax.ppermute(value, 'blk', [(c, c ^ delta) for c in range(blks)])  7.16 us
    ppermute x7, waiting for transfers between devices, exchange(): return lax.ppermute(value, 'blk', [(c, c ^ delta) for c in range(blks)])  6.03 us
    ppermute x1, waiting for transfers between devices, to_section(): return lax.ppermute(block, ('rep', 'blk'), pairs)  4.45 us
  transfers between devices with their start and end apart: 29, of which 14 were waited for; matrix products, arithmetic and copies ran while one was open for 5% of the time, Pallas kernels for 7%

profile of v7, /device:TPU:0, one launch (start us, length us, event | category | flops | bytes accessed | tf_op | source)
XLA Modules:
  0.0 104.7 jit_solution(16667272465415362056)
XLA Ops:
  0.7 2.1 %pack.1 = (bf16[272,128]{1,0:T(8,128)(2,1)}, bf16[17,128,128]{2,1,0:T(8,128)(2,1)}) custom-call(s32[2]{0:T(128)} %bitcast.61, bf16[256,128]{1,0:T(8,128)(2,1)} %bitcast.59, s32[2,128]{1,0:T(2,128)} %bitcast.65, s32[2,16]{1,0:T(2,128)} %bitcast.60, bf16[2,16,128,128]{3,2,1,0:T(8,128)(2,1)} %bitcast.51), custom_call_target="tpu_custom_call" | custom-call | tf_op jit(solution)/shard_map/pack/pallas_call | solution.py:346
  2.7 1.5 %collective-permute-start.1 = (bf16[272,128]{1,0:T(8,128)(2,1)}, bf16[272,128]{1,0:T(8,128)(2,1)S(1)}, u32[]{:S(2)}, u32[]{:S(2)}) collective-permute-start(bf16[272,128]{1,0:T(8,128)(2,1)} %get-tuple-element.32), channel_id=1, source_target_pairs={{0,0},{1,1},{2,2},{3,3},{4,4},{5,5},{6,6},{7,7},{8,10},{9,11},{10,... | collective-permute-start | bytes 208904 | tf_op jit(solution)/shard_map/ppermute | solution.py:312
  4.3 6.0 %collective-permute-start.2 = (bf16[272,128]{1,0:T(8,128)(2,1)}, bf16[272,128]{1,0:T(8,128)(2,1)S(1)}, u32[]{:S(2)}, u32[]{:S(2)}) collective-permute-start(bf16[272,128]{1,0:T(8,128)(2,1)} %get-tuple-element.32), channel_id=1, source_target_pairs={{0,10},{1,11},{2,12},{3,13},{4,14},{5,15},{6,8},{7,9},{8,0},{9,1},... | collective-permute-start | bytes 208904 | tf_op jit(solution)/shard_map/ppermute | solution.py:312
  10.2 1.3 %collective-permute-start.3 = (bf16[272,128]{1,0:T(8,128)(2,1)}, bf16[272,128]{1,0:T(8,128)(2,1)S(1)}, u32[]{:S(2)}, u32[]{:S(2)}) collective-permute-start(bf16[272,128]{1,0:T(8,128)(2,1)} %get-tuple-element.32), channel_id=1, source_target_pairs={{0,20},{1,21},{2,22},{3,23},{4,16},{5,17},{6,18},{7,19},{8,30},{9,... | collective-permute-start | bytes 208904 | tf_op jit(solution)/shard_map/ppermute | solution.py:312
  11.5 3.0 %collective-permute-start.4 = (bf16[272,128]{1,0:T(8,128)(2,1)}, bf16[272,128]{1,0:T(8,128)(2,1)S(1)}, u32[]{:S(2)}, u32[]{:S(2)}) collective-permute-start(bf16[272,128]{1,0:T(8,128)(2,1)} %get-tuple-element.32), channel_id=1, source_target_pairs={{0,30},{1,31},{2,24},{3,25},{4,26},{5,27},{6,28},{7,29},{8,20},{9,... | collective-permute-start | bytes 208904 | tf_op jit(solution)/shard_map/ppermute | solution.py:312
  14.5 2.5 %collective-permute-start = (bf16[17,128,128]{2,1,0:T(8,128)(2,1)}, bf16[17,128,128]{2,1,0:T(8,128)(2,1)S(1)}, u32[]{:S(2)}, u32[]{:S(2)}) collective-permute-start(bf16[17,128,128]{2,1,0:T(8,128)(2,1)} %get-tuple-element.31), channel_id=1, source_target_pairs={{0,8},{2,10},{4,12},{6,14},{8,16},{10,18},{12,20},{14,22},{16,24},... | collective-permute-start | bytes 1671176 | tf_op jit(solution)/shard_map/ppermute | solution.py:370
  18.7 2.5 %collective-permute-start.5 = (bf16[4,16,128]{2,1,0:T(8,128)(2,1)S(1)}, bf16[4,16,128]{2,1,0:T(8,128)(2,1)S(1)}, u32[]{:S(2)}, u32[]{:S(2)}) collective-permute-start(bf16[4,16,128]{2,1,0:T(8,128)(2,1)S(1)} %pad_maximum_fusion.4), channel_id=1, source_target_pairs={{0,1},{1,0},{2,3},{3,2},{4,5},{5,4},{6,7},{7,6},{8,9},{9,8},{10,11... | collective-permute-start | bytes 49160 | tf_op jit(solution)/shard_map/ppermute | solution.py:302
  21.3 2.3 %dense.2 = bf16[1024,2048]{1,0:T(8,128)(2,1)S(1)} custom-call(s32[3]{0:T(128)S(1)} %compare_select_fusion.6.spot_ref, s32[2]{0:T(128)S(1)} %iota.28.order_ref.moved_ref, s32[2]{0:T(128)S(1)} %iota.28.order_ref.moved_ref, s32[2,16]{1,0:T(2,128)S(1)} %compare_select_fusion.7.place_ref, bf16[2,16,128,128]{3,2,1,0:T(8,128)(2,1)S(1)} %bitcast.52), custom_call_target="tpu_custom_call" | custom-call | bytes 8388608 | tf_op jit(solution)/shard_map/dense/pallas_call | solution.py:244
  23.7 4.5 %collective-permute-done.6 = bf16[1088,128]{1,0:T(8,128)(2,1)S(1)} collective-permute-done((bf16[1088,128]{1,0:T(8,128)(2,1)S(1)}, bf16[1088,128]{1,0:T(8,128)(2,1)S(1)}, u32[]{:S(2)}, u32[]{:S(2)}) %collective-permute-start.6) | collective-permute-done | bytes 278560 | tf_op jit(solution)/shard_map/ppermute | solution.py:299
  29.5 2.7 %collective-permute-start.7 = (f32[256,128]{1,0:T(8,128)S(1)}, f32[256,128]{1,0:T(8,128)S(1)}, u32[]{:S(2)}, u32[]{:S(2)}) collective-permute-start(f32[256,128]{1,0:T(8,128)S(1)} %get-tuple-element.67), channel_id=1, source_target_pairs={{0,8},{8,0},{16,24},{24,16},{1,9},{9,1},{17,25},{25,17},{2,10},{10... | collective-permute-start | bytes 393224 | tf_op jit(solution)/shard_map/ppermute | solution.py:288
  34.4 2.2 %dense.3 = bf16[1024,2048]{1,0:T(8,128)(2,1)S(1)} custom-call(s32[3]{0:T(128)S(1)} %broadcast_in_dim.37.spot_ref, s32[2]{0:T(128)S(1)} %and_select_fusion.1.order_ref, s32[2]{0:T(128)S(1)} %compare_convert_fusion.moved_ref, s32[2,16]{1,0:T(2,128)S(1)} %broadcast_select_fusion.place_ref, bf16[2,16,128,128]{3,2,1,0:T(8,128)(2,1)S(1)} %bitcast.53, ...), custom_call_target="tpu_custom_call" | custom-call | bytes 8388608 | tf_op jit(solution)/shard_map/dense/pallas_call | solution.py:244
  36.6 2.4 %collective-permute-done.8 = f32[256,128]{1,0:T(8,128)S(1)} collective-permute-done((f32[256,128]{1,0:T(8,128)S(1)}, f32[256,128]{1,0:T(8,128)S(1)}, u32[]{:S(2)}, u32[]{:S(2)}) %collective-permute-start.8) | collective-permute-done | bytes 131104 | tf_op jit(solution)/shard_map/ppermute | solution.py:288
  39.7 3.0 %collective-permute-start.11 = (bf16[256,128]{1,0:T(8,128)(2,1)S(1)}, bf16[256,128]{1,0:T(8,128)(2,1)S(1)}, u32[]{:S(2)}, u32[]{:S(2)}) collective-permute-start(bf16[256,128]{1,0:T(8,128)(2,1)S(1)} %fusion.10), channel_id=1, source_target_pairs={{0,10},{1,11},{2,12},{3,13},{4,14},{5,15},{6,8},{7,9},{8,0},{9,1},... | collective-permute-start | bytes 196616 | tf_op jit(solution)/shard_map/ppermute | solution.py:312
  42.7 2.0 %collective-permute-start.12 = (bf16[256,128]{1,0:T(8,128)(2,1)S(1)}, bf16[256,128]{1,0:T(8,128)(2,1)S(1)}, u32[]{:S(2)}, u32[]{:S(2)}) collective-permute-start(bf16[256,128]{1,0:T(8,128)(2,1)S(1)} %fusion.10), channel_id=1, source_target_pairs={{0,20},{1,21},{2,22},{3,23},{4,16},{5,17},{6,18},{7,19},{8,30},{9,... | collective-permute-start | bytes 196616 | tf_op jit(solution)/shard_map/ppermute | solution.py:312
  44.7 3.8 %collective-permute-start.13 = (bf16[256,128]{1,0:T(8,128)(2,1)S(1)}, bf16[256,128]{1,0:T(8,128)(2,1)S(1)}, u32[]{:S(2)}, u32[]{:S(2)}) collective-permute-start(bf16[256,128]{1,0:T(8,128)(2,1)S(1)} %fusion.10), channel_id=1, source_target_pairs={{0,30},{1,31},{2,24},{3,25},{4,26},{5,27},{6,28},{7,29},{8,20},{9,... | collective-permute-start | bytes 196616 | tf_op jit(solution)/shard_map/ppermute | solution.py:312
  50.6 1.5 %collective-permute-done.14 = bf16[1024,128]{1,0:T(8,128)(2,1)S(1)} collective-permute-done((bf16[1024,128]{1,0:T(8,128)(2,1)S(1)}, bf16[1024,128]{1,0:T(8,128)(2,1)S(1)}, u32[]{:S(2)}, u32[]{:S(2)}) %collective-permute-start.14) | collective-permute-done | bytes 262176 | tf_op jit(solution)/shard_map/ppermute | solution.py:302
  52.1 1.4 %compare_select_fusion = (bf16[2048,256]{1,0:T(8,128)(2,1)}, f32[2048,256]{1,0:T(8,128)S(1)}) fusion(bf16[2048,256]{1,0:T(8,128)(2,1)S(1)} %fusion.4, bf16[2048,128]{1,0:T(8,128)(2,1)S(1)} %constant_dynamic-update-slice_fusion.1, bf16[128,256]{1,0:T(8,128)(2,1)S(1)} %copy-done), kind=kOutput, calls=%fused_computation.11 | convolution fusion | flops 135266304 | bytes 4784128 | tf_op jit(solution)/shard_map/dot_general | solution.py:32
  53.5 1.3 %fusion.5.partial_ref.own_ref = f32[1024,256]{1,0:T(8,128)S(1)} fusion(bf16[1024,2048]{1,0:T(8,128)(2,1)S(1)} %dense.3, bf16[2048,256]{1,0:T(8,128)(2,1)S(1)} %fusion.4, f32[2048,256]{1,0:T(8,128)S(1)} %get-tuple-element.77), kind=kOutput, calls=%fused_computation.12 | convolution fusion | flops 1076363264 | bytes 8388608 | tf_op jit(solution)/shard_map/dot_general | solution.py:32
  56.0 6.5 %collective-permute-start.15 = (s16[272,256]{1,0:T(8,128)(2,1)}, s16[272,256]{1,0:T(8,128)(2,1)S(1)}, u32[]{:S(2)}, u32[]{:S(2)}) collective-permute-start(s16[272,256]{1,0:T(8,128)(2,1)} %get-tuple-element.42), channel_id=1, source_target_pairs={{0,8},{8,0},{16,24},{24,16},{1,9},{9,1},{17,25},{25,17},{2,10},{10... | collective-permute-start | bytes 417800 | tf_op jit(solution)/shard_map/ppermute | solution.py:288
  62.5 1.5 %collective-permute-start.17 = (s16[272,256]{1,0:T(8,128)(2,1)}, s16[272,256]{1,0:T(8,128)(2,1)S(1)}, u32[]{:S(2)}, u32[]{:S(2)}) collective-permute-start(s16[272,256]{1,0:T(8,128)(2,1)} %get-tuple-element.44), channel_id=1, source_target_pairs={{0,24},{8,16},{16,8},{24,0},{1,25},{9,17},{17,9},{25,1},{2,26},{10... | collective-permute-start | bytes 417800 | tf_op jit(solution)/shard_map/ppermute | solution.py:288
  64.4 3.1 %dense_turned.1 = bf16[2048,1024]{1,0:T(8,128)(2,1)S(1)} custom-call(s32[3]{0:T(128)S(1)} %broadcast_in_dim.37.spot_ref, s32[2]{0:T(128)S(1)} %and_select_fusion.1.order_ref, s32[2]{0:T(128)S(1)} %compare_convert_fusion.moved_ref, s32[2,16]{1,0:T(2,128)S(1)} %broadcast_select_fusion.place_ref, bf16[2,16,128,128]{3,2,1,0:T(8,128)(2,1)S(1)} %bitcast.54, ...), custom_call_target="tpu_custom_call" | custom-call | bytes 8388608 | tf_op jit(solution)/shard_map/dense_turned/pallas_call | solution.py:244
  67.5 1.9 %copy-done.2 = bf16[2048,1024]{1,0:T(8,128)(2,1)} copy-done((bf16[2048,1024]{1,0:T(8,128)(2,1)}, bf16[2048,1024]{1,0:T(8,128)(2,1)S(1)}, u32[]{:S(2)}) %copy-start.2) | copy-done | bytes 4194328
  69.5 1.6 %collective-permute-done.16.refs_1_ = s16[272,256]{1,0:T(8,128)(2,1)S(1)} collective-permute-done((s16[272,256]{1,0:T(8,128)(2,1)}, s16[272,256]{1,0:T(8,128)(2,1)S(1)}, u32[]{:S(2)}, u32[]{:S(2)}) %collective-permute-start.16) | collective-permute-done | bytes 139296 | tf_op jit(solution)/shard_map/ppermute | solution.py:288
  71.1 1.6 %head.1 = (f32[256,172]{1,0:T(8,128)S(1)}, f32[48,256]{1,0:T(8,128)S(1)}, bf16[304,256]{1,0:T(8,128)(2,1)S(1)}, bf16[304,256]{1,0:T(8,128)(2,1)S(1)}, bf16[304,2...) custom-call(s32[2]{0:T(128)S(1)} %pad_add_fusion.1.spot_ref, bf16[256,172]{1,0:T(8,128)(2,1)S(1)} %copy.15.weight_ref, ...), custom_call_target="tpu_custom_call" | custom-call | tf_op jit(solution)/shard_map/head/pallas_call | solution.py:178
  74.5 1.7 %collective-permute-start.20 = (bf16[304,256]{1,0:T(8,128)(2,1)S(1)}, bf16[304,256]{1,0:T(8,128)(2,1)S(1)}, u32[]{:S(2)}, u32[]{:S(2)}) collective-permute-start(bf16[304,256]{1,0:T(8,128)(2,1)S(1)} %get-tuple-element.50), channel_id=1, source_target_pairs={{0,24},{8,16},{16,8},{24,0},{1,25},{9,17},{17,9},{25,1},{2,26},{10... | collective-permute-start | bytes 466952 | tf_op jit(solution)/shard_map/ppermute | solution.py:288
  76.3 3.1 %collective-permute-done.18 = bf16[304,256]{1,0:T(8,128)(2,1)S(1)} collective-permute-done((bf16[304,256]{1,0:T(8,128)(2,1)S(1)}, bf16[304,256]{1,0:T(8,128)(2,1)S(1)}, u32[]{:S(2)}, u32[]{:S(2)}) %collective-permute-start.18) | collective-permute-done | bytes 155680 | tf_op jit(solution)/shard_map/ppermute | solution.py:288
  79.4 2.8 %collective-permute-done.19 = bf16[304,256]{1,0:T(8,128)(2,1)S(1)} collective-permute-done((bf16[304,256]{1,0:T(8,128)(2,1)S(1)}, bf16[304,256]{1,0:T(8,128)(2,1)S(1)}, u32[]{:S(2)}, u32[]{:S(2)}) %collective-permute-start.19) | collective-permute-done | bytes 155680 | tf_op jit(solution)/shard_map/ppermute | solution.py:288
  82.3 3.8 %fusion = bf16[2048,256]{1,0:T(8,128)(2,1)S(1)} fusion(bf16[2048,1024]{1,0:T(8,128)(2,1)} %copy-done.2, bf16[1024,256]{1,0:T(8,128)(2,1)S(1)} %pad_maximum_fusion, bf16[2048,256]{1,0:T(8,128)(2,1)} %get-tuple-element.53), kind=kOutput, calls=%fused_computation.5 | convolution fusion | flops 1075838976 | bytes 6815744 | tf_op jit(solution)/shard_map/dot_general | solution.py:32
  88.1 4.3 %collective-permute-start.24 = (bf16[88,256]{1,0:T(8,128)(2,1)S(1)}, bf16[88,256]{1,0:T(8,128)(2,1)S(1)}, u32[]{:S(2)}, u32[]{:S(2)}) collective-permute-start(bf16[88,256]{1,0:T(8,128)(2,1)S(1)} %fusion.11), channel_id=1, source_target_pairs={{0,6},{1,7},{2,4},{3,5},{4,2},{5,3},{6,0},{7,1},{8,14},{9,15},{10,... | collective-permute-start | bytes 135176 | tf_op jit(solution)/shard_map/ppermute | solution.py:302
  92.5 2.6 %collective-permute-done.23 = bf16[88,256]{1,0:T(8,128)(2,1)S(1)} collective-permute-done((bf16[88,256]{1,0:T(8,128)(2,1)S(1)}, bf16[88,256]{1,0:T(8,128)(2,1)S(1)}, u32[]{:S(2)}, u32[]{:S(2)}) %collective-permute-start.23) | collective-permute-done | bytes 45088 | tf_op jit(solution)/shard_map/ppermute | solution.py:302
  96.9 1.8 %collective-permute-start.27 = (bf16[88,256]{1,0:T(8,128)(2,1)S(1)}, bf16[88,256]{1,0:T(8,128)(2,1)S(1)}, u32[]{:S(2)}, u32[]{:S(2)}) collective-permute-start(bf16[88,256]{1,0:T(8,128)(2,1)S(1)} %add_convert_fusion), channel_id=1, source_target_pairs={{0,24},{8,16},{16,8},{24,0},{1,25},{9,17},{17,9},{25,1},{2,26},{10... | collective-permute-start | bytes 135176 | tf_op jit(solution)/shard_map/ppermute | solution.py:288
  100.0 1.9 %collective-permute-done.27 = bf16[88,256]{1,0:T(8,128)(2,1)S(1)} collective-permute-done((bf16[88,256]{1,0:T(8,128)(2,1)S(1)}, bf16[88,256]{1,0:T(8,128)(2,1)S(1)}, u32[]{:S(2)}, u32[]{:S(2)}) %collective-permute-start.27) | collective-permute-done | bytes 45088 | tf_op jit(solution)/shard_map/ppermute | solution.py:288
  (126 shorter events, 19.4 us)
Async XLA Ops:
  0.6 51.4 %copy-start = (bf16[128,256]{1,0:T(8,128)(2,1)S(1)}, bf16[128,256]{1,0:T(8,128)(2,1)}, u32[]{:S(2)}) copy-start(bf16[128,256]{1,0:T(8,128)(2,1)} %param.17) | copy-start | bytes 196612
  0.6 20.6 %copy-start.1 = (bf16[1,1,2,16,128,128]{5,4,3,2,1,0:T(8,128)(2,1)S(1)}, bf16[1,1,2,16,128,128]{5,4,3,2,1,0:T(8,128)(2,1)}, u32[]{:S(2)}) copy-start(bf16[1,1,2,16,128,128]{5,4,3,2,1,0:T(8,128)(2,1)} %param.14) | copy-start | bytes 3145732
  2.7 15.7 %collective-permute-start.1 = (bf16[272,128]{1,0:T(8,128)(2,1)}, bf16[272,128]{1,0:T(8,128)(2,1)S(1)}, u32[]{:S(2)}, u32[]{:S(2)}) collective-permute-start(bf16[272,128]{1,0:T(8,128)(2,1)} %get-tuple-element.32), channel_id=1, source_target_pairs={{0,0},{1,1},{2,2},{3,3},{4,4},{5,5},{6,6},{7,7},{8,10},{9,11},{10,... | collective-permute-start | bytes 208904 | tf_op jit(solution)/shard_map/ppermute | solution.py:312
  4.3 14.2 %collective-permute-start.2 = (bf16[272,128]{1,0:T(8,128)(2,1)}, bf16[272,128]{1,0:T(8,128)(2,1)S(1)}, u32[]{:S(2)}, u32[]{:S(2)}) collective-permute-start(bf16[272,128]{1,0:T(8,128)(2,1)} %get-tuple-element.32), channel_id=1, source_target_pairs={{0,10},{1,11},{2,12},{3,13},{4,14},{5,15},{6,8},{7,9},{8,0},{9,1},... | collective-permute-start | bytes 208904 | tf_op jit(solution)/shard_map/ppermute | solution.py:312
  10.2 8.2 %collective-permute-start.3 = (bf16[272,128]{1,0:T(8,128)(2,1)}, bf16[272,128]{1,0:T(8,128)(2,1)S(1)}, u32[]{:S(2)}, u32[]{:S(2)}) collective-permute-start(bf16[272,128]{1,0:T(8,128)(2,1)} %get-tuple-element.32), channel_id=1, source_target_pairs={{0,20},{1,21},{2,22},{3,23},{4,16},{5,17},{6,18},{7,19},{8,30},{9,... | collective-permute-start | bytes 208904 | tf_op jit(solution)/shard_map/ppermute | solution.py:312
  11.5 6.9 %collective-permute-start.4 = (bf16[272,128]{1,0:T(8,128)(2,1)}, bf16[272,128]{1,0:T(8,128)(2,1)S(1)}, u32[]{:S(2)}, u32[]{:S(2)}) collective-permute-start(bf16[272,128]{1,0:T(8,128)(2,1)} %get-tuple-element.32), channel_id=1, source_target_pairs={{0,30},{1,31},{2,24},{3,25},{4,26},{5,27},{6,28},{7,29},{8,20},{9,... | collective-permute-start | bytes 208904 | tf_op jit(solution)/shard_map/ppermute | solution.py:312
  14.5 19.2 %collective-permute-start = (bf16[17,128,128]{2,1,0:T(8,128)(2,1)}, bf16[17,128,128]{2,1,0:T(8,128)(2,1)S(1)}, u32[]{:S(2)}, u32[]{:S(2)}) collective-permute-start(bf16[17,128,128]{2,1,0:T(8,128)(2,1)} %get-tuple-element.31), channel_id=1, source_target_pairs={{0,8},{2,10},{4,12},{6,14},{8,16},{10,18},{12,20},{14,22},{16,24},... | collective-permute-start | bytes 1671176 | tf_op jit(solution)/shard_map/ppermute | solution.py:370
  18.5 9.6 %collective-permute-start.6 = (bf16[1088,128]{1,0:T(8,128)(2,1)S(1)}, bf16[1088,128]{1,0:T(8,128)(2,1)S(1)}, u32[]{:S(2)}, u32[]{:S(2)}) collective-permute-start(bf16[1088,128]{1,0:T(8,128)(2,1)S(1)} %pad_maximum_fusion.1), channel_id=1, source_target_pairs={{0,1},{1,24},{2,3},{3,26},{4,5},{5,28},{6,7},{7,30},{8,9},{9,0},{1... | collective-permute-start | bytes 835592 | tf_op jit(solution)/shard_map/ppermute | solution.py:299
  18.7 4.9 %collective-permute-start.5 = (bf16[4,16,128]{2,1,0:T(8,128)(2,1)S(1)}, bf16[4,16,128]{2,1,0:T(8,128)(2,1)S(1)}, u32[]{:S(2)}, u32[]{:S(2)}) collective-permute-start(bf16[4,16,128]{2,1,0:T(8,128)(2,1)S(1)} %pad_maximum_fusion.4), channel_id=1, source_target_pairs={{0,1},{1,0},{2,3},{3,2},{4,5},{5,4},{6,7},{7,6},{8,9},{9,8},{10,11... | collective-permute-start | bytes 49160 | tf_op jit(solution)/shard_map/ppermute | solution.py:302
  29.5 7.1 %collective-permute-start.7 = (f32[256,128]{1,0:T(8,128)S(1)}, f32[256,128]{1,0:T(8,128)S(1)}, u32[]{:S(2)}, u32[]{:S(2)}) collective-permute-start(f32[256,128]{1,0:T(8,128)S(1)} %get-tuple-element.67), channel_id=1, source_target_pairs={{0,8},{8,0},{16,24},{24,16},{1,9},{9,1},{17,25},{25,17},{2,10},{10... | collective-permute-start | bytes 393224 | tf_op jit(solution)/shard_map/ppermute | solution.py:288
  32.2 6.8 %collective-permute-start.8 = (f32[256,128]{1,0:T(8,128)S(1)}, f32[256,128]{1,0:T(8,128)S(1)}, u32[]{:S(2)}, u32[]{:S(2)}) collective-permute-start(f32[256,128]{1,0:T(8,128)S(1)} %get-tuple-element.66), channel_id=1, source_target_pairs={{0,16},{8,24},{16,0},{24,8},{1,17},{9,25},{17,1},{25,9},{2,18},{10... | collective-permute-start | bytes 393224 | tf_op jit(solution)/shard_map/ppermute | solution.py:288
  32.6 6.4 %collective-permute-start.9 = (f32[256,128]{1,0:T(8,128)S(1)}, f32[256,128]{1,0:T(8,128)S(1)}, u32[]{:S(2)}, u32[]{:S(2)}) collective-permute-start(f32[256,128]{1,0:T(8,128)S(1)} %get-tuple-element.65), channel_id=1, source_target_pairs={{0,24},{8,16},{16,8},{24,0},{1,25},{9,17},{17,9},{25,1},{2,26},{10... | collective-permute-start | bytes 393224 | tf_op jit(solution)/shard_map/ppermute | solution.py:288
  39.1 10.3 %collective-permute-start.10 = (bf16[256,128]{1,0:T(8,128)(2,1)S(1)}, bf16[256,128]{1,0:T(8,128)(2,1)S(1)}, u32[]{:S(2)}, u32[]{:S(2)}) collective-permute-start(bf16[256,128]{1,0:T(8,128)(2,1)S(1)} %fusion.10), channel_id=1, source_target_pairs={{0,0},{1,1},{2,2},{3,3},{4,4},{5,5},{6,6},{7,7},{8,10},{9,11},{10,... | collective-permute-start | bytes 196616 | tf_op jit(solution)/shard_map/ppermute | solution.py:312
  39.7 9.7 %collective-permute-start.11 = (bf16[256,128]{1,0:T(8,128)(2,1)S(1)}, bf16[256,128]{1,0:T(8,128)(2,1)S(1)}, u32[]{:S(2)}, u32[]{:S(2)}) collective-permute-start(bf16[256,128]{1,0:T(8,128)(2,1)S(1)} %fusion.10), channel_id=1, source_target_pairs={{0,10},{1,11},{2,12},{3,13},{4,14},{5,15},{6,8},{7,9},{8,0},{9,1},... | collective-permute-start | bytes 196616 | tf_op jit(solution)/shard_map/ppermute | solution.py:312
  42.7 6.7 %collective-permute-start.12 = (bf16[256,128]{1,0:T(8,128)(2,1)S(1)}, bf16[256,128]{1,0:T(8,128)(2,1)S(1)}, u32[]{:S(2)}, u32[]{:S(2)}) collective-permute-start(bf16[256,128]{1,0:T(8,128)(2,1)S(1)} %fusion.10), channel_id=1, source_target_pairs={{0,20},{1,21},{2,22},{3,23},{4,16},{5,17},{6,18},{7,19},{8,30},{9,... | collective-permute-start | bytes 196616 | tf_op jit(solution)/shard_map/ppermute | solution.py:312
  44.7 5.7 %collective-permute-start.13 = (bf16[256,128]{1,0:T(8,128)(2,1)S(1)}, bf16[256,128]{1,0:T(8,128)(2,1)S(1)}, u32[]{:S(2)}, u32[]{:S(2)}) collective-permute-start(bf16[256,128]{1,0:T(8,128)(2,1)S(1)} %fusion.10), channel_id=1, source_target_pairs={{0,30},{1,31},{2,24},{3,25},{4,26},{5,27},{6,28},{7,29},{8,20},{9,... | collective-permute-start | bytes 196616 | tf_op jit(solution)/shard_map/ppermute | solution.py:312
  50.4 1.6 %collective-permute-start.14 = (bf16[1024,128]{1,0:T(8,128)(2,1)S(1)}, bf16[1024,128]{1,0:T(8,128)(2,1)S(1)}, u32[]{:S(2)}, u32[]{:S(2)}) collective-permute-start(bf16[1024,128]{1,0:T(8,128)(2,1)S(1)} %pad_maximum_fusion.2), channel_id=1, source_target_pairs={{0,1},{1,0},{2,3},{3,2},{4,5},{5,4},{6,7},{7,6},{8,9},{9,8},{10,11... | collective-permute-start | bytes 786440 | tf_op jit(solution)/shard_map/ppermute | solution.py:302
  53.5 10.7 %copy-start.9 = (s32[1,256]{1,0:T(1,128)S(1)}, s32[1,256]{1,0:T(1,128)}, u32[]{:S(2)}) copy-start(s32[1,256]{1,0:T(1,128)} %param.13) | copy-start | bytes 3076
  56.0 13.5 %collective-permute-start.15 = (s16[272,256]{1,0:T(8,128)(2,1)}, s16[272,256]{1,0:T(8,128)(2,1)S(1)}, u32[]{:S(2)}, u32[]{:S(2)}) collective-permute-start(s16[272,256]{1,0:T(8,128)(2,1)} %get-tuple-element.42), channel_id=1, source_target_pairs={{0,8},{8,0},{16,24},{24,16},{1,9},{9,1},{17,25},{25,17},{2,10},{10... | collective-permute-start | bytes 417800 | tf_op jit(solution)/shard_map/ppermute | solution.py:288
  62.5 8.6 %collective-permute-start.16 = (s16[272,256]{1,0:T(8,128)(2,1)}, s16[272,256]{1,0:T(8,128)(2,1)S(1)}, u32[]{:S(2)}, u32[]{:S(2)}) collective-permute-start(s16[272,256]{1,0:T(8,128)(2,1)} %get-tuple-element.43), channel_id=1, source_target_pairs={{0,16},{8,24},{16,0},{24,8},{1,17},{9,25},{17,1},{25,9},{2,18},{10... | collective-permute-start | bytes 417800 | tf_op jit(solution)/shard_map/ppermute | solution.py:288
  62.5 8.6 %collective-permute-start.17 = (s16[272,256]{1,0:T(8,128)(2,1)}, s16[272,256]{1,0:T(8,128)(2,1)S(1)}, u32[]{:S(2)}, u32[]{:S(2)}) collective-permute-start(s16[272,256]{1,0:T(8,128)(2,1)} %get-tuple-element.44), channel_id=1, source_target_pairs={{0,24},{8,16},{16,8},{24,0},{1,25},{9,17},{17,9},{25,1},{2,26},{10... | collective-permute-start | bytes 417800 | tf_op jit(solution)/shard_map/ppermute | solution.py:288
  72.7 6.7 %collective-permute-start.18 = (bf16[304,256]{1,0:T(8,128)(2,1)S(1)}, bf16[304,256]{1,0:T(8,128)(2,1)S(1)}, u32[]{:S(2)}, u32[]{:S(2)}) collective-permute-start(bf16[304,256]{1,0:T(8,128)(2,1)S(1)} %get-tuple-element.48), channel_id=1, source_target_pairs={{0,8},{8,0},{16,24},{24,16},{1,9},{9,1},{17,25},{25,17},{2,10},{10... | collective-permute-start | bytes 466952 | tf_op jit(solution)/shard_map/ppermute | solution.py:288
  73.3 9.0 %collective-permute-start.19 = (bf16[304,256]{1,0:T(8,128)(2,1)S(1)}, bf16[304,256]{1,0:T(8,128)(2,1)S(1)}, u32[]{:S(2)}, u32[]{:S(2)}) collective-permute-start(bf16[304,256]{1,0:T(8,128)(2,1)S(1)} %get-tuple-element.49), channel_id=1, source_target_pairs={{0,16},{8,24},{16,0},{24,8},{1,17},{9,25},{17,1},{25,9},{2,18},{10... | collective-permute-start | bytes 466952 | tf_op jit(solution)/shard_map/ppermute | solution.py:288
  74.5 7.7 %collective-permute-start.20 = (bf16[304,256]{1,0:T(8,128)(2,1)S(1)}, bf16[304,256]{1,0:T(8,128)(2,1)S(1)}, u32[]{:S(2)}, u32[]{:S(2)}) collective-permute-start(bf16[304,256]{1,0:T(8,128)(2,1)S(1)} %get-tuple-element.50), channel_id=1, source_target_pairs={{0,24},{8,16},{16,8},{24,0},{1,25},{9,17},{17,9},{25,1},{2,26},{10... | collective-permute-start | bytes 466952 | tf_op jit(solution)/shard_map/ppermute | solution.py:288
  86.6 1.4 %collective-permute-start.21 = (f32[88,256]{1,0:T(8,128)S(1)}, f32[88,256]{1,0:T(8,128)S(1)}, u32[]{:S(2)}, u32[]{:S(2)}) collective-permute-start(f32[88,256]{1,0:T(8,128)S(1)} %pad_maximum_fusion.3), channel_id=1, source_target_pairs={{0,1},{1,0},{2,3},{3,2},{4,5},{5,4},{6,7},{7,6},{8,9},{9,8},{10,11... | collective-permute-start | bytes 270344 | tf_op jit(solution)/shard_map/ppermute | solution.py:302
  87.9 4.6 %collective-permute-start.22 = (bf16[88,256]{1,0:T(8,128)(2,1)S(1)}, bf16[88,256]{1,0:T(8,128)(2,1)S(1)}, u32[]{:S(2)}, u32[]{:S(2)}) collective-permute-start(bf16[88,256]{1,0:T(8,128)(2,1)S(1)} %fusion.11), channel_id=1, source_target_pairs={{0,2},{1,3},{2,0},{3,1},{4,6},{5,7},{6,4},{7,5},{8,10},{9,11},{10,... | collective-permute-start | bytes 135176 | tf_op jit(solution)/shard_map/ppermute | solution.py:302
  88.0 7.1 %collective-permute-start.23 = (bf16[88,256]{1,0:T(8,128)(2,1)S(1)}, bf16[88,256]{1,0:T(8,128)(2,1)S(1)}, u32[]{:S(2)}, u32[]{:S(2)}) collective-permute-start(bf16[88,256]{1,0:T(8,128)(2,1)S(1)} %fusion.11), channel_id=1, source_target_pairs={{0,4},{1,5},{2,6},{3,7},{4,0},{5,1},{6,2},{7,3},{8,12},{9,13},{10,... | collective-permute-start | bytes 135176 | tf_op jit(solution)/shard_map/ppermute | solution.py:302
  88.1 7.0 %collective-permute-start.24 = (bf16[88,256]{1,0:T(8,128)(2,1)S(1)}, bf16[88,256]{1,0:T(8,128)(2,1)S(1)}, u32[]{:S(2)}, u32[]{:S(2)}) collective-permute-start(bf16[88,256]{1,0:T(8,128)(2,1)S(1)} %fusion.11), channel_id=1, source_target_pairs={{0,6},{1,7},{2,4},{3,5},{4,2},{5,3},{6,0},{7,1},{8,14},{9,15},{10,... | collective-permute-start | bytes 135176 | tf_op jit(solution)/shard_map/ppermute | solution.py:302
  95.2 4.1 %collective-permute-start.25 = (bf16[88,256]{1,0:T(8,128)(2,1)S(1)}, bf16[88,256]{1,0:T(8,128)(2,1)S(1)}, u32[]{:S(2)}, u32[]{:S(2)}) collective-permute-start(bf16[88,256]{1,0:T(8,128)(2,1)S(1)} %add_convert_fusion), channel_id=1, source_target_pairs={{0,8},{8,0},{16,24},{24,16},{1,9},{9,1},{17,25},{25,17},{2,10},{10... | collective-permute-start | bytes 135176 | tf_op jit(solution)/shard_map/ppermute | solution.py:288
  95.9 4.0 %collective-permute-start.26 = (bf16[88,256]{1,0:T(8,128)(2,1)S(1)}, bf16[88,256]{1,0:T(8,128)(2,1)S(1)}, u32[]{:S(2)}, u32[]{:S(2)}) collective-permute-start(bf16[88,256]{1,0:T(8,128)(2,1)S(1)} %add_convert_fusion), channel_id=1, source_target_pairs={{0,16},{8,24},{16,0},{24,8},{1,17},{9,25},{17,1},{25,9},{2,18},{10... | collective-permute-start | bytes 135176 | tf_op jit(solution)/shard_map/ppermute | solution.py:288
  96.9 4.9 %collective-permute-start.27 = (bf16[88,256]{1,0:T(8,128)(2,1)S(1)}, bf16[88,256]{1,0:T(8,128)(2,1)S(1)}, u32[]{:S(2)}, u32[]{:S(2)}) collective-permute-start(bf16[88,256]{1,0:T(8,128)(2,1)S(1)} %add_convert_fusion), channel_id=1, source_target_pairs={{0,24},{8,16},{16,8},{24,0},{1,25},{9,17},{17,9},{25,1},{2,26},{10... | collective-permute-start | bytes 135176 | tf_op jit(solution)/shard_map/ppermute | solution.py:288
  102.0 1.5 %collective-permute-start.28 = (f32[160,256]{1,0:T(8,128)S(1)}, f32[160,256]{1,0:T(8,128)S(1)}, u32[]{:S(2)}, u32[]{:S(2)}) collective-permute-start(f32[160,256]{1,0:T(8,128)S(1)} %constant_dynamic-update-slice_fusion.6.total_ref), channel_id=1, source_target_pairs={{0,1},{1,0},{2,3},{3,2},{4,5},{5,4},{6,7},{7,6},{8,9},{9,8},{10,11... | collective-permute-start | bytes 491528 | tf_op jit(solution)/shard_map/ppermute | solution.py:302
  (8 other events, 46.2 us)

commit v8 on v7

--- a/solution.py
+++ b/solution.py
@@ -105,12 +105,12 @@
     parts += [jnp.zeros((pad, lanes), jnp.int32)] if pad else []
     digit_rows = jnp.concatenate(parts, axis=0).astype(jnp.float32).astype(jnp.bfloat16)
     bundle_ref[own_rows:, :] = digit_rows
-    slot = lax.broadcasted_iota(jnp.int32, (1, slots), 1)
     first = lax.broadcasted_iota(jnp.int32, (edge, edge), 0) == 0
     for section, parcel_ref in enumerate(parcel_refs, 1):
         place = place_ref[section : section + 1, :]
-        line = jnp.where(slot < count_ref[section], place + 1, 0)
-        line = jnp.concatenate([line, jnp.zeros((1, edge - slots), jnp.int32)], axis=1)
+        line = jnp.concatenate(
+            [place, jnp.full((1, edge - slots), count_ref[section], jnp.int32)], axis=1
+        )
         parcel_ref[slots] = jnp.where(first, line, 0).astype(jnp.float32).astype(jnp.bfloat16)
     for copy in large:
         copy.wait()
@@ -180,57 +180,57 @@
         in_specs=[smem] * len(spot) + [vmem] * len(values),
         out_shape=shapes,
         scratch_shapes=scratch,
-        compiler_params=pltpu.CompilerParams(vmem_limit_bytes=32 * 1024 * 1024),
+        compiler_params=pltpu.CompilerParams(vmem_limit_bytes=8 * 1024 * 1024),
         name=name,
     )(*spot, *values)
 
 
 def dense_kernel(
-    per_rep, tile_side, turn, spot_ref, order_ref, moved_ref, place_ref, own_ref, *refs
+    per_rep, tile_side, turn, spot_ref, order_ref, moved_ref, place_ref, count_ref, own_ref, *refs
 ):
     other_ref, dense_ref = refs if len(refs) == 2 else (None, refs[0])
     position = pl.program_id(0)
     rep_index, source_rep = spot_ref[0], spot_ref[1 + position]
     edge = own_ref.shape[-1]
-    slots = place_ref.shape[1]
     dense_ref[...] = jnp.zeros_like(dense_ref)
 
-    def put_all(tiles_ref):
+    section = order_ref[position]
+
+    def put_all(tiles_ref, row_of, count):
         def put(slot, carried):
-            place = place_ref[position, slot]
+            place = place_ref[row_of, slot]
             row = place // tile_side
             column = place % tile_side
             row = ((row // per_rep) ^ rep_index) * per_rep + row % per_rep
             column = ((column // per_rep) ^ source_rep) * per_rep + column % per_rep
 
-            @pl.when(place >= 0)
-            def _():
-                rows = pl.ds(pl.multiple_of(row * edge, edge), edge)
-                columns = pl.ds(pl.multiple_of(column * edge, edge), edge)
-                tile = tiles_ref[0, slot]
-                if turn:
-                    dense_ref[columns, rows] = tile.T
-                else:
-                    dense_ref[rows, columns] = tile
-
+            rows = pl.ds(pl.multiple_of(row * edge, edge), edge)
+            columns = pl.ds(pl.multiple_of(column * edge, edge), edge)
+            tile = tiles_ref[0, slot]
+            if turn:
+                dense_ref[columns, rows] = tile.T
+            else:
+                dense_ref[rows, columns] = tile
             return carried
 
-        lax.fori_loop(0, slots, put, 0)
+        lax.fori_loop(0, count, put, 0)
 
     if other_ref is None:
-        put_all(own_ref)
+        put_all(own_ref, section, count_ref[section])
         return
 
     @pl.when(moved_ref[position] == 0)
     def _():
-        put_all(own_ref)
+        put_all(own_ref, section, count_ref[section])
 
     @pl.when(moved_ref[position] != 0)
     def _():
-        put_all(other_ref)
-
-
-def build_dense(tiles, others, place, spot, order, moved, own_rows, group_rows, turn=False):
+        put_all(other_ref, moved_ref[position], count_ref[moved_ref[position]])
+
+
+def build_dense(
+    tiles, others, place, count, spot, order, moved, own_rows, group_rows, turn=False
+):
     sections, slots, edge, _ = tiles.shape
     body = functools.partial(dense_kernel, own_rows // edge, group_rows // edge, turn)
     own_block = pl.BlockSpec((1, slots, edge, edge), lambda p, spot, order, *_: (order[p], 0, 0, 0))
@@ -244,18 +244,20 @@
     return pl.pallas_call(
         body,
         grid_spec=pltpu.PrefetchScalarGridSpec(
-            num_scalar_prefetch=4,
+            num_scalar_prefetch=5,
             grid=(sections,),
             in_specs=[own_block, other_block] if both else [own_block],
             out_specs=pl.BlockSpec(block, lambda p, *_: (p, 0) if turn else (0, p)),
         ),
         out_shape=jax.ShapeDtypeStruct(shape, tiles.dtype),
-        compiler_params=pltpu.CompilerParams(vmem_limit_bytes=40 * 1024 * 1024),
+        compiler_params=pltpu.CompilerParams(
+            vmem_limit_bytes=4 * group_rows**2 + 8 * (slots + 1) * edge**2 + (2 << 20)
+        ),
         cost_estimate=pl.CostEstimate(
             flops=0, bytes_accessed=4 * sections * group_rows * group_rows, transcendentals=0
         ),
         name="dense_turned" if turn else "dense",
-    )(spot, order, moved, place, *([tiles, others] if both else [tiles]))
+    )(spot, order, moved, place, count, *([tiles, others] if both else [tiles]))
 
 
 def on_device(
@@ -336,8 +338,7 @@
         return (parts[0] + (parts[1] << 8) + (parts[2] << 16)).reshape(own_rows)
 
     member = lax.rem(blk_index, sections)
-    live = jnp.arange(tile_values.shape[3], dtype=jnp.int32)[None, :] < tile_count[0, 0][:, None]
-    place = jnp.where(live, tile_place[0, 0], -1)
+    place, count = tile_place[0, 0], tile_count[0, 0]
     slots, edge = tile_values.shape[3], tile_values.shape[4]
     width = features.shape[2]
     digit_rows = 3 * own_rows // width
@@ -368,21 +369,21 @@
                 if c % sections < j:
                     pairs.append((r * blks + c, (r + 1) % reps * blks + c))
         parcels[j - 1] = lax.ppermute(parcels[j - 1], ("rep", "blk"), pairs)
-    other_place = [place[0]]
-    other_place += [parcel[slots, 0, :slots].astype(jnp.int32) - 1 for parcel in parcels]
+    other_place = [parcel[slots, 0, : slots + 1].astype(jnp.int32) for parcel in parcels]
     position = jnp.arange(sections, dtype=jnp.int32)
     column = position ^ member
     order = jnp.mod(member - column, sections)
-    moved = (column > member).astype(jnp.int32)
-    placed = jnp.where(moved[:, None] != 0, jnp.stack(other_place)[order], place[order])
+    moved = jnp.where(column > member, sections - 1 + order, 0)
+    both_place = jnp.concatenate([place] + [part[None, :slots] for part in other_place], axis=0)
+    both_count = jnp.concatenate([count] + [part[slots:] for part in other_place])
     tiles = tile_values[0, 0]
     where = jnp.broadcast_to(rep_index, (sections + 1,))
     next_rep = lax.rem(rep_index + 1, reps)
     first_where = jnp.where(member < jnp.arange(sections + 1) - 1, next_rep, rep_index)
     block = jnp.concatenate(arrived, axis=0)
-    place, block = lax.optimization_barrier((place, block))
+    count, block = lax.optimization_barrier((count, block))
     dense = build_dense(
-        tiles, None, place, first_where, position, position, own_rows, group_rows
+        tiles, None, place, count, first_where, position, position, own_rows, group_rows
     )
     blocks = [block] + [to_section(block, j) for j in range(1, sections)]
     pieces = [whole[d * stride : (d + 1) * stride] for whole in blocks for d in range(reps)]
@@ -392,7 +393,9 @@
     units = jnp.arange(hidden_width, dtype=jnp.int32)
     kept = keep_mask(id_columns[:, None], units[None, :])
     chunks = dot(dense, feature_columns).reshape(reps, own_rows, width)
-    layout = (tiles, jnp.stack(parcels), placed, where, order, moved, own_rows, group_rows)
+    layout = (
+        tiles, jnp.stack(parcels), both_place, both_count, where, order, moved, own_rows, group_rows
+    )
     arrived = [swap(chunks[delta], delta) for delta in range(1, reps)]
     dense, arrived = lax.optimization_barrier((build_dense(*layout), arrived))
     total = chunks[0]

time: 105 us -> 104 us (level)
    ppermute x1, waiting for transfers between devices: 4.45 us -> 5.77 us  [to_section(): return lax.ppermute(block, ('rep', 'blk'), pairs)]
    gather x2 -> x0, local copies, waits for them, and re-layouts: 1.12 us -> none  [the longest x1 0.56 us: on_device(): place[order]]
  transfers between devices with their start and end apart: 29 -> 29, of which waited for: 14 -> 14; matrix products, arithmetic and copies ran while one was open for 5% -> 6% of each run, Pallas kernels for 7% -> 7%
where the time goes in v8:
time: 104 us
  starting transfers between devices  49.7 us (48%)
  waiting for transfers between devices  25.1 us (24%)
  Pallas kernels  13 us (12%)
  matrix products  8.11 us (8%)
  local copies, waits for them, and re-layouts  4.72 us (5%)
  other arithmetic  2.02 us (2%)
  between operations  1.28 us (1%)
    ppermute x8, starting transfers between devices, to_pieces(): pieces.append(lax.ppermute(value, ('rep', 'blk'), pairs))  20.7 us
    ppermute x12, starting transfers between devices, swap(): return lax.ppermute(value, 'rep', [(r, r ^ delta) for r in range(reps)])  19.2 us
    ppermute x12, waiting for transfers between devices, swap(): return lax.ppermute(value, 'rep', [(r, r ^ delta) for r in range(reps)])  12.2 us
    dot_general x4, matrix products, dot(): return jnp.dot(left, right, preferred_element_type=jnp.float32)  7.76 us
    ppermute x7, starting transfers between devices, exchange(): return lax.ppermute(value, 'blk', [(c, c ^ delta) for c in range(blks)])  7.28 us
    pallas_call x3, Pallas kernels, build_dense(): pl.pallas_call(body, grid_spec=pltpu.PrefetchScalarGridSpec(num_scalar_pr...  6.87 us
    ppermute x7, waiting for transfers between devices, exchange(): return lax.ppermute(value, 'blk', [(c, c ^ delta) for c in range(blks)])  6.03 us
    ppermute x1, waiting for transfers between devices, to_section(): return lax.ppermute(block, ('rep', 'blk'), pairs)  5.77 us
  transfers between devices with their start and end apart: 29, of which 14 were waited for; matrix products, arithmetic and copies ran while one was open for 6% of the time, Pallas kernels for 7%

profile of v8, /device:TPU:0, one launch (start us, length us, event | category | flops | bytes accessed | tf_op | source)
XLA Modules:
  0.0 103.9 jit_solution(4706449650346806631)
XLA Ops:
  0.7 2.1 %pack.1 = (bf16[272,128]{1,0:T(8,128)(2,1)}, bf16[17,128,128]{2,1,0:T(8,128)(2,1)}) custom-call(s32[2]{0:T(128)} %bitcast.59, bf16[256,128]{1,0:T(8,128)(2,1)} %bitcast.63, s32[2,128]{1,0:T(2,128)} %bitcast.66, s32[2,16]{1,0:T(2,128)} %bitcast.56, bf16[2,16,128,128]{3,2,1,0:T(8,128)(2,1)} %bitcast.49), custom_call_target="tpu_custom_call" | custom-call | tf_op jit(solution)/shard_map/pack/pallas_call | solution.py:347
  2.8 1.5 %collective-permute-start.1 = (bf16[272,128]{1,0:T(8,128)(2,1)}, bf16[272,128]{1,0:T(8,128)(2,1)S(1)}, u32[]{:S(2)}, u32[]{:S(2)}) collective-permute-start(bf16[272,128]{1,0:T(8,128)(2,1)} %get-tuple-element.32), channel_id=1, source_target_pairs={{0,0},{1,1},{2,2},{3,3},{4,4},{5,5},{6,6},{7,7},{8,10},{9,11},{10,... | collective-permute-start | bytes 208904 | tf_op jit(solution)/shard_map/ppermute | solution.py:314
  4.3 6.0 %collective-permute-start.2 = (bf16[272,128]{1,0:T(8,128)(2,1)}, bf16[272,128]{1,0:T(8,128)(2,1)S(1)}, u32[]{:S(2)}, u32[]{:S(2)}) collective-permute-start(bf16[272,128]{1,0:T(8,128)(2,1)} %get-tuple-element.32), channel_id=1, source_target_pairs={{0,10},{1,11},{2,12},{3,13},{4,14},{5,15},{6,8},{7,9},{8,0},{9,1},... | collective-permute-start | bytes 208904 | tf_op jit(solution)/shard_map/ppermute | solution.py:314
  11.5 3.0 %collective-permute-start.4 = (bf16[272,128]{1,0:T(8,128)(2,1)}, bf16[272,128]{1,0:T(8,128)(2,1)S(1)}, u32[]{:S(2)}, u32[]{:S(2)}) collective-permute-start(bf16[272,128]{1,0:T(8,128)(2,1)} %get-tuple-element.32), channel_id=1, source_target_pairs={{0,30},{1,31},{2,24},{3,25},{4,26},{5,27},{6,28},{7,29},{8,20},{9,... | collective-permute-start | bytes 208904 | tf_op jit(solution)/shard_map/ppermute | solution.py:314
  14.6 2.5 %collective-permute-start = (bf16[17,128,128]{2,1,0:T(8,128)(2,1)}, bf16[17,128,128]{2,1,0:T(8,128)(2,1)S(1)}, u32[]{:S(2)}, u32[]{:S(2)}) collective-permute-start(bf16[17,128,128]{2,1,0:T(8,128)(2,1)} %get-tuple-element.31), channel_id=1, source_target_pairs={{0,8},{2,10},{4,12},{6,14},{8,16},{10,18},{12,20},{14,22},{16,24},... | collective-permute-start | bytes 1671176 | tf_op jit(solution)/shard_map/ppermute | solution.py:371
  17.3 2.6 %collective-permute-start.5 = (bf16[4,16,128]{2,1,0:T(8,128)(2,1)S(1)}, bf16[4,16,128]{2,1,0:T(8,128)(2,1)S(1)}, u32[]{:S(2)}, u32[]{:S(2)}) collective-permute-start(bf16[4,16,128]{2,1,0:T(8,128)(2,1)S(1)} %pad_maximum_fusion.4), channel_id=1, source_target_pairs={{0,1},{1,0},{2,3},{3,2},{4,5},{5,4},{6,7},{7,6},{8,9},{9,8},{10,11... | collective-permute-start | bytes 49160 | tf_op jit(solution)/shard_map/ppermute | solution.py:304
  20.0 2.3 %dense.2 = bf16[1024,2048]{1,0:T(8,128)(2,1)S(1)} custom-call(s32[3]{0:T(128)S(1)} %compare_select_fusion.3.spot_ref, s32[2]{0:T(128)S(1)} %iota.18.order_ref.moved_ref, s32[2]{0:T(128)S(1)} %iota.18.order_ref.moved_ref, s32[2,16]{1,0:T(2,128)S(1)} %bitcast.57, s32[2]{0:T(128)S(1)} %bitcast.60, bf16[2,16,128,128]{3,2,1,0:T(8,128)(2,1)S(1)} %bitcast.50), custom_call_target="tpu_custom_call" | custom-call | bytes 8388608 | tf_op jit(solution)/shard_map/dense/pallas_call | solution.py:244
  22.4 5.8 %collective-permute-done.6 = bf16[1088,128]{1,0:T(8,128)(2,1)S(1)} collective-permute-done((bf16[1088,128]{1,0:T(8,128)(2,1)S(1)}, bf16[1088,128]{1,0:T(8,128)(2,1)S(1)}, u32[]{:S(2)}, u32[]{:S(2)}) %collective-permute-start.6) | collective-permute-done | bytes 278560 | tf_op jit(solution)/shard_map/ppermute | solution.py:301
  29.5 2.7 %collective-permute-start.7 = (f32[256,128]{1,0:T(8,128)S(1)}, f32[256,128]{1,0:T(8,128)S(1)}, u32[]{:S(2)}, u32[]{:S(2)}) collective-permute-start(f32[256,128]{1,0:T(8,128)S(1)} %get-tuple-element.67), channel_id=1, source_target_pairs={{0,8},{8,0},{16,24},{24,16},{1,9},{9,1},{17,25},{25,17},{2,10},{10... | collective-permute-start | bytes 393224 | tf_op jit(solution)/shard_map/ppermute | solution.py:290
  32.2 1.5 %collective-permute-start.9 = (f32[256,128]{1,0:T(8,128)S(1)}, f32[256,128]{1,0:T(8,128)S(1)}, u32[]{:S(2)}, u32[]{:S(2)}) collective-permute-start(f32[256,128]{1,0:T(8,128)S(1)} %get-tuple-element.65), channel_id=1, source_target_pairs={{0,24},{8,16},{16,8},{24,0},{1,25},{9,17},{17,9},{25,1},{2,26},{10... | collective-permute-start | bytes 393224 | tf_op jit(solution)/shard_map/ppermute | solution.py:290
  35.1 2.0 %dense.3 = bf16[1024,2048]{1,0:T(8,128)(2,1)S(1)} custom-call(s32[3]{0:T(128)S(1)} %broadcast_in_dim.26.spot_ref, s32[2]{0:T(128)S(1)} %get-tuple-element.79.order_ref, s32[2]{0:T(128)S(1)} %get-tuple-element.78.moved_ref, s32[3,16]{1,0:T(4,128)S(1)} %pad_add_fusion.place_ref, s32[3]{0:T(128)S(1)} %pad_add_fusion.2.count_ref, ...), custom_call_target="tpu_custom_call" | custom-call | bytes 8388608 | tf_op jit(solution)/shard_map/dense/pallas_call | solution.py:244
  37.1 1.9 %collective-permute-done.8 = f32[256,128]{1,0:T(8,128)S(1)} collective-permute-done((f32[256,128]{1,0:T(8,128)S(1)}, f32[256,128]{1,0:T(8,128)S(1)}, u32[]{:S(2)}, u32[]{:S(2)}) %collective-permute-start.8) | collective-permute-done | bytes 131104 | tf_op jit(solution)/shard_map/ppermute | solution.py:290
  39.7 2.7 %collective-permute-start.11 = (bf16[256,128]{1,0:T(8,128)(2,1)S(1)}, bf16[256,128]{1,0:T(8,128)(2,1)S(1)}, u32[]{:S(2)}, u32[]{:S(2)}) collective-permute-start(bf16[256,128]{1,0:T(8,128)(2,1)S(1)} %fusion.10), channel_id=1, source_target_pairs={{0,10},{1,11},{2,12},{3,13},{4,14},{5,15},{6,8},{7,9},{8,0},{9,1},... | collective-permute-start | bytes 196616 | tf_op jit(solution)/shard_map/ppermute | solution.py:314
  42.4 2.3 %collective-permute-start.12 = (bf16[256,128]{1,0:T(8,128)(2,1)S(1)}, bf16[256,128]{1,0:T(8,128)(2,1)S(1)}, u32[]{:S(2)}, u32[]{:S(2)}) collective-permute-start(bf16[256,128]{1,0:T(8,128)(2,1)S(1)} %fusion.10), channel_id=1, source_target_pairs={{0,20},{1,21},{2,22},{3,23},{4,16},{5,17},{6,18},{7,19},{8,30},{9,... | collective-permute-start | bytes 196616 | tf_op jit(solution)/shard_map/ppermute | solution.py:314
  44.7 3.2 %collective-permute-start.13 = (bf16[256,128]{1,0:T(8,128)(2,1)S(1)}, bf16[256,128]{1,0:T(8,128)(2,1)S(1)}, u32[]{:S(2)}, u32[]{:S(2)}) collective-permute-start(bf16[256,128]{1,0:T(8,128)(2,1)S(1)} %fusion.10), channel_id=1, source_target_pairs={{0,30},{1,31},{2,24},{3,25},{4,26},{5,27},{6,28},{7,29},{8,20},{9,... | collective-permute-start | bytes 196616 | tf_op jit(solution)/shard_map/ppermute | solution.py:314
  50.0 1.5 %collective-permute-done.14 = bf16[1024,128]{1,0:T(8,128)(2,1)S(1)} collective-permute-done((bf16[1024,128]{1,0:T(8,128)(2,1)S(1)}, bf16[1024,128]{1,0:T(8,128)(2,1)S(1)}, u32[]{:S(2)}, u32[]{:S(2)}) %collective-permute-start.14) | collective-permute-done | bytes 262176 | tf_op jit(solution)/shard_map/ppermute | solution.py:304
  51.6 1.4 %compare_select_fusion = (bf16[2048,256]{1,0:T(8,128)(2,1)}, f32[2048,256]{1,0:T(8,128)S(1)}) fusion(bf16[2048,256]{1,0:T(8,128)(2,1)S(1)} %fusion.4, bf16[2048,128]{1,0:T(8,128)(2,1)S(1)} %constant_dynamic-update-slice_fusion.1, bf16[128,256]{1,0:T(8,128)(2,1)S(1)} %copy-done), kind=kOutput, calls=%fused_computation.9 | convolution fusion | flops 135266304 | bytes 4784128 | tf_op jit(solution)/shard_map/dot_general | solution.py:32
  55.4 6.5 %collective-permute-start.15 = (s16[272,256]{1,0:T(8,128)(2,1)}, s16[272,256]{1,0:T(8,128)(2,1)S(1)}, u32[]{:S(2)}, u32[]{:S(2)}) collective-permute-start(s16[272,256]{1,0:T(8,128)(2,1)} %get-tuple-element.42), channel_id=1, source_target_pairs={{0,8},{8,0},{16,24},{24,16},{1,9},{9,1},{17,25},{25,17},{2,10},{10... | collective-permute-start | bytes 417800 | tf_op jit(solution)/shard_map/ppermute | solution.py:290
  61.9 1.5 %collective-permute-start.17 = (s16[272,256]{1,0:T(8,128)(2,1)}, s16[272,256]{1,0:T(8,128)(2,1)S(1)}, u32[]{:S(2)}, u32[]{:S(2)}) collective-permute-start(s16[272,256]{1,0:T(8,128)(2,1)} %get-tuple-element.44), channel_id=1, source_target_pairs={{0,24},{8,16},{16,8},{24,0},{1,25},{9,17},{17,9},{25,1},{2,26},{10... | collective-permute-start | bytes 417800 | tf_op jit(solution)/shard_map/ppermute | solution.py:290
  64.5 2.6 %dense_turned.1 = bf16[2048,1024]{1,0:T(8,128)(2,1)S(1)} custom-call(s32[3]{0:T(128)S(1)} %broadcast_in_dim.26.spot_ref, s32[2]{0:T(128)S(1)} %get-tuple-element.79.order_ref, s32[2]{0:T(128)S(1)} %get-tuple-element.78.moved_ref, s32[3,16]{1,0:T(4,128)S(1)} %pad_add_fusion.place_ref, s32[3]{0:T(128)S(1)} %pad_add_fusion.2.count_ref, ...), custom_call_target="tpu_custom_call" | custom-call | bytes 8388608 | tf_op jit(solution)/shard_map/dense_turned/pallas_call | solution.py:244
  67.1 2.0 %copy-done.2 = bf16[2048,1024]{1,0:T(8,128)(2,1)} copy-done((bf16[2048,1024]{1,0:T(8,128)(2,1)}, bf16[2048,1024]{1,0:T(8,128)(2,1)S(1)}, u32[]{:S(2)}) %copy-start.2) | copy-done | bytes 4194328
  69.1 1.4 %collective-permute-done.16.refs_1_ = s16[272,256]{1,0:T(8,128)(2,1)S(1)} collective-permute-done((s16[272,256]{1,0:T(8,128)(2,1)}, s16[272,256]{1,0:T(8,128)(2,1)S(1)}, u32[]{:S(2)}, u32[]{:S(2)}) %collective-permute-start.16) | collective-permute-done | bytes 139296 | tf_op jit(solution)/shard_map/ppermute | solution.py:290
  70.5 1.6 %head.1 = (f32[256,172]{1,0:T(8,128)S(1)}, f32[48,256]{1,0:T(8,128)S(1)}, bf16[304,256]{1,0:T(8,128)(2,1)S(1)}, bf16[304,256]{1,0:T(8,128)(2,1)S(1)}, bf16[304,2...) custom-call(s32[2]{0:T(128)S(1)} %pad_add_fusion.1.spot_ref, bf16[256,172]{1,0:T(8,128)(2,1)S(1)} %copy.15.weight_ref, ...), custom_call_target="tpu_custom_call" | custom-call | tf_op jit(solution)/shard_map/head/pallas_call | solution.py:178
  72.5 1.5 %collective-permute-start.19 = (bf16[304,256]{1,0:T(8,128)(2,1)S(1)}, bf16[304,256]{1,0:T(8,128)(2,1)S(1)}, u32[]{:S(2)}, u32[]{:S(2)}) collective-permute-start(bf16[304,256]{1,0:T(8,128)(2,1)S(1)} %get-tuple-element.49), channel_id=1, source_target_pairs={{0,16},{8,24},{16,0},{24,8},{1,17},{9,25},{17,1},{25,9},{2,18},{10... | collective-permute-start | bytes 466952 | tf_op jit(solution)/shard_map/ppermute | solution.py:290
  74.0 1.7 %collective-permute-start.20 = (bf16[304,256]{1,0:T(8,128)(2,1)S(1)}, bf16[304,256]{1,0:T(8,128)(2,1)S(1)}, u32[]{:S(2)}, u32[]{:S(2)}) collective-permute-start(bf16[304,256]{1,0:T(8,128)(2,1)S(1)} %get-tuple-element.50), channel_id=1, source_target_pairs={{0,24},{8,16},{16,8},{24,0},{1,25},{9,17},{17,9},{25,1},{2,26},{10... | collective-permute-start | bytes 466952 | tf_op jit(solution)/shard_map/ppermute | solution.py:290
  75.7 3.2 %collective-permute-done.18 = bf16[304,256]{1,0:T(8,128)(2,1)S(1)} collective-permute-done((bf16[304,256]{1,0:T(8,128)(2,1)S(1)}, bf16[304,256]{1,0:T(8,128)(2,1)S(1)}, u32[]{:S(2)}, u32[]{:S(2)}) %collective-permute-start.18) | collective-permute-done | bytes 155680 | tf_op jit(solution)/shard_map/ppermute | solution.py:290
  78.9 2.1 %collective-permute-done.19 = bf16[304,256]{1,0:T(8,128)(2,1)S(1)} collective-permute-done((bf16[304,256]{1,0:T(8,128)(2,1)S(1)}, bf16[304,256]{1,0:T(8,128)(2,1)S(1)}, u32[]{:S(2)}, u32[]{:S(2)}) %collective-permute-start.19) | collective-permute-done | bytes 155680 | tf_op jit(solution)/shard_map/ppermute | solution.py:290
  81.2 3.8 %fusion = bf16[2048,256]{1,0:T(8,128)(2,1)S(1)} fusion(bf16[2048,1024]{1,0:T(8,128)(2,1)} %copy-done.2, bf16[1024,256]{1,0:T(8,128)(2,1)S(1)} %pad_maximum_fusion, bf16[2048,256]{1,0:T(8,128)(2,1)} %get-tuple-element.53), kind=kOutput, calls=%fused_computation.3 | convolution fusion | flops 1075838976 | bytes 6815744 | tf_op jit(solution)/shard_map/dot_general | solution.py:32
  87.1 4.1 %collective-permute-start.24 = (bf16[88,256]{1,0:T(8,128)(2,1)S(1)}, bf16[88,256]{1,0:T(8,128)(2,1)S(1)}, u32[]{:S(2)}, u32[]{:S(2)}) collective-permute-start(bf16[88,256]{1,0:T(8,128)(2,1)S(1)} %fusion.11), channel_id=1, source_target_pairs={{0,6},{1,7},{2,4},{3,5},{4,2},{5,3},{6,0},{7,1},{8,14},{9,15},{10,... | collective-permute-start | bytes 135176 | tf_op jit(solution)/shard_map/ppermute | solution.py:304
  91.4 2.6 %collective-permute-done.23 = bf16[88,256]{1,0:T(8,128)(2,1)S(1)} collective-permute-done((bf16[88,256]{1,0:T(8,128)(2,1)S(1)}, bf16[88,256]{1,0:T(8,128)(2,1)S(1)}, u32[]{:S(2)}, u32[]{:S(2)}) %collective-permute-start.23) | collective-permute-done | bytes 45088 | tf_op jit(solution)/shard_map/ppermute | solution.py:304
  96.1 1.5 %collective-permute-start.27 = (bf16[88,256]{1,0:T(8,128)(2,1)S(1)}, bf16[88,256]{1,0:T(8,128)(2,1)S(1)}, u32[]{:S(2)}, u32[]{:S(2)}) collective-permute-start(bf16[88,256]{1,0:T(8,128)(2,1)S(1)} %add_convert_fusion), channel_id=1, source_target_pairs={{0,24},{8,16},{16,8},{24,0},{1,25},{9,17},{17,9},{25,1},{2,26},{10... | collective-permute-start | bytes 135176 | tf_op jit(solution)/shard_map/ppermute | solution.py:290
  99.4 1.6 %collective-permute-done.27 = bf16[88,256]{1,0:T(8,128)(2,1)S(1)} collective-permute-done((bf16[88,256]{1,0:T(8,128)(2,1)S(1)}, bf16[88,256]{1,0:T(8,128)(2,1)S(1)}, u32[]{:S(2)}, u32[]{:S(2)}) %collective-permute-start.27) | collective-permute-done | bytes 45088 | tf_op jit(solution)/shard_map/ppermute | solution.py:290
  (119 shorter events, 20.1 us)
Async XLA Ops:
  0.6 50.9 %copy-start = (bf16[128,256]{1,0:T(8,128)(2,1)S(1)}, bf16[128,256]{1,0:T(8,128)(2,1)}, u32[]{:S(2)}) copy-start(bf16[128,256]{1,0:T(8,128)(2,1)} %param.17) | copy-start | bytes 196612
  0.6 19.4 %copy-start.1 = (bf16[1,1,2,16,128,128]{5,4,3,2,1,0:T(8,128)(2,1)S(1)}, bf16[1,1,2,16,128,128]{5,4,3,2,1,0:T(8,128)(2,1)}, u32[]{:S(2)}) copy-start(bf16[1,1,2,16,128,128]{5,4,3,2,1,0:T(8,128)(2,1)} %param.14) | copy-start | bytes 3145732
  0.7 19.4 %copy-start.3 = (s32[1,1,2,16]{3,2,1,0:T(2,128)S(1)}, s32[1,1,2,16]{3,2,1,0:T(2,128)}, u32[]{:S(2)}) copy-start(s32[1,1,2,16]{3,2,1,0:T(2,128)} %param.15) | copy-start | bytes 388
  2.8 14.3 %collective-permute-start.1 = (bf16[272,128]{1,0:T(8,128)(2,1)}, bf16[272,128]{1,0:T(8,128)(2,1)S(1)}, u32[]{:S(2)}, u32[]{:S(2)}) collective-permute-start(bf16[272,128]{1,0:T(8,128)(2,1)} %get-tuple-element.32), channel_id=1, source_target_pairs={{0,0},{1,1},{2,2},{3,3},{4,4},{5,5},{6,6},{7,7},{8,10},{9,11},{10,... | collective-permute-start | bytes 208904 | tf_op jit(solution)/shard_map/ppermute | solution.py:314
  4.3 12.8 %collective-permute-start.2 = (bf16[272,128]{1,0:T(8,128)(2,1)}, bf16[272,128]{1,0:T(8,128)(2,1)S(1)}, u32[]{:S(2)}, u32[]{:S(2)}) collective-permute-start(bf16[272,128]{1,0:T(8,128)(2,1)} %get-tuple-element.32), channel_id=1, source_target_pairs={{0,10},{1,11},{2,12},{3,13},{4,14},{5,15},{6,8},{7,9},{8,0},{9,1},... | collective-permute-start | bytes 208904 | tf_op jit(solution)/shard_map/ppermute | solution.py:314
  10.3 6.9 %collective-permute-start.3 = (bf16[272,128]{1,0:T(8,128)(2,1)}, bf16[272,128]{1,0:T(8,128)(2,1)S(1)}, u32[]{:S(2)}, u32[]{:S(2)}) collective-permute-start(bf16[272,128]{1,0:T(8,128)(2,1)} %get-tuple-element.32), channel_id=1, source_target_pairs={{0,20},{1,21},{2,22},{3,23},{4,16},{5,17},{6,18},{7,19},{8,30},{9,... | collective-permute-start | bytes 208904 | tf_op jit(solution)/shard_map/ppermute | solution.py:314
  11.5 5.6 %collective-permute-start.4 = (bf16[272,128]{1,0:T(8,128)(2,1)}, bf16[272,128]{1,0:T(8,128)(2,1)S(1)}, u32[]{:S(2)}, u32[]{:S(2)}) collective-permute-start(bf16[272,128]{1,0:T(8,128)(2,1)} %get-tuple-element.32), channel_id=1, source_target_pairs={{0,30},{1,31},{2,24},{3,25},{4,26},{5,27},{6,28},{7,29},{8,20},{9,... | collective-permute-start | bytes 208904 | tf_op jit(solution)/shard_map/ppermute | solution.py:314
  14.6 19.2 %collective-permute-start = (bf16[17,128,128]{2,1,0:T(8,128)(2,1)}, bf16[17,128,128]{2,1,0:T(8,128)(2,1)S(1)}, u32[]{:S(2)}, u32[]{:S(2)}) collective-permute-start(bf16[17,128,128]{2,1,0:T(8,128)(2,1)} %get-tuple-element.31), channel_id=1, source_target_pairs={{0,8},{2,10},{4,12},{6,14},{8,16},{10,18},{12,20},{14,22},{16,24},... | collective-permute-start | bytes 1671176 | tf_op jit(solution)/shard_map/ppermute | solution.py:371
  17.2 11.0 %collective-permute-start.6 = (bf16[1088,128]{1,0:T(8,128)(2,1)S(1)}, bf16[1088,128]{1,0:T(8,128)(2,1)S(1)}, u32[]{:S(2)}, u32[]{:S(2)}) collective-permute-start(bf16[1088,128]{1,0:T(8,128)(2,1)S(1)} %pad_maximum_fusion.1), channel_id=1, source_target_pairs={{0,1},{1,24},{2,3},{3,26},{4,5},{5,28},{6,7},{7,30},{8,9},{9,0},{1... | collective-permute-start | bytes 835592 | tf_op jit(solution)/shard_map/ppermute | solution.py:301
  17.3 5.0 %collective-permute-start.5 = (bf16[4,16,128]{2,1,0:T(8,128)(2,1)S(1)}, bf16[4,16,128]{2,1,0:T(8,128)(2,1)S(1)}, u32[]{:S(2)}, u32[]{:S(2)}) collective-permute-start(bf16[4,16,128]{2,1,0:T(8,128)(2,1)S(1)} %pad_maximum_fusion.4), channel_id=1, source_target_pairs={{0,1},{1,0},{2,3},{3,2},{4,5},{5,4},{6,7},{7,6},{8,9},{9,8},{10,11... | collective-permute-start | bytes 49160 | tf_op jit(solution)/shard_map/ppermute | solution.py:304
  29.5 7.5 %collective-permute-start.7 = (f32[256,128]{1,0:T(8,128)S(1)}, f32[256,128]{1,0:T(8,128)S(1)}, u32[]{:S(2)}, u32[]{:S(2)}) collective-permute-start(f32[256,128]{1,0:T(8,128)S(1)} %get-tuple-element.67), channel_id=1, source_target_pairs={{0,8},{8,0},{16,24},{24,16},{1,9},{9,1},{17,25},{25,17},{2,10},{10... | collective-permute-start | bytes 393224 | tf_op jit(solution)/shard_map/ppermute | solution.py:290
  32.2 6.8 %collective-permute-start.8 = (f32[256,128]{1,0:T(8,128)S(1)}, f32[256,128]{1,0:T(8,128)S(1)}, u32[]{:S(2)}, u32[]{:S(2)}) collective-permute-start(f32[256,128]{1,0:T(8,128)S(1)} %get-tuple-element.66), channel_id=1, source_target_pairs={{0,16},{8,24},{16,0},{24,8},{1,17},{9,25},{17,1},{25,9},{2,18},{10... | collective-permute-start | bytes 393224 | tf_op jit(solution)/shard_map/ppermute | solution.py:290
  32.2 6.8 %collective-permute-start.9 = (f32[256,128]{1,0:T(8,128)S(1)}, f32[256,128]{1,0:T(8,128)S(1)}, u32[]{:S(2)}, u32[]{:S(2)}) collective-permute-start(f32[256,128]{1,0:T(8,128)S(1)} %get-tuple-element.65), channel_id=1, source_target_pairs={{0,24},{8,16},{16,8},{24,0},{1,25},{9,17},{17,9},{25,1},{2,26},{10... | collective-permute-start | bytes 393224 | tf_op jit(solution)/shard_map/ppermute | solution.py:290
  39.0 9.7 %collective-permute-start.10 = (bf16[256,128]{1,0:T(8,128)(2,1)S(1)}, bf16[256,128]{1,0:T(8,128)(2,1)S(1)}, u32[]{:S(2)}, u32[]{:S(2)}) collective-permute-start(bf16[256,128]{1,0:T(8,128)(2,1)S(1)} %fusion.10), channel_id=1, source_target_pairs={{0,0},{1,1},{2,2},{3,3},{4,4},{5,5},{6,6},{7,7},{8,10},{9,11},{10,... | collective-permute-start | bytes 196616 | tf_op jit(solution)/shard_map/ppermute | solution.py:314
  39.7 9.1 %collective-permute-start.11 = (bf16[256,128]{1,0:T(8,128)(2,1)S(1)}, bf16[256,128]{1,0:T(8,128)(2,1)S(1)}, u32[]{:S(2)}, u32[]{:S(2)}) collective-permute-start(bf16[256,128]{1,0:T(8,128)(2,1)S(1)} %fusion.10), channel_id=1, source_target_pairs={{0,10},{1,11},{2,12},{3,13},{4,14},{5,15},{6,8},{7,9},{8,0},{9,1},... | collective-permute-start | bytes 196616 | tf_op jit(solution)/shard_map/ppermute | solution.py:314
  42.4 6.4 %collective-permute-start.12 = (bf16[256,128]{1,0:T(8,128)(2,1)S(1)}, bf16[256,128]{1,0:T(8,128)(2,1)S(1)}, u32[]{:S(2)}, u32[]{:S(2)}) collective-permute-start(bf16[256,128]{1,0:T(8,128)(2,1)S(1)} %fusion.10), channel_id=1, source_target_pairs={{0,20},{1,21},{2,22},{3,23},{4,16},{5,17},{6,18},{7,19},{8,30},{9,... | collective-permute-start | bytes 196616 | tf_op jit(solution)/shard_map/ppermute | solution.py:314
  44.7 5.2 %collective-permute-start.13 = (bf16[256,128]{1,0:T(8,128)(2,1)S(1)}, bf16[256,128]{1,0:T(8,128)(2,1)S(1)}, u32[]{:S(2)}, u32[]{:S(2)}) collective-permute-start(bf16[256,128]{1,0:T(8,128)(2,1)S(1)} %fusion.10), channel_id=1, source_target_pairs={{0,30},{1,31},{2,24},{3,25},{4,26},{5,27},{6,28},{7,29},{8,20},{9,... | collective-permute-start | bytes 196616 | tf_op jit(solution)/shard_map/ppermute | solution.py:314
  49.9 1.6 %collective-permute-start.14 = (bf16[1024,128]{1,0:T(8,128)(2,1)S(1)}, bf16[1024,128]{1,0:T(8,128)(2,1)S(1)}, u32[]{:S(2)}, u32[]{:S(2)}) collective-permute-start(bf16[1024,128]{1,0:T(8,128)(2,1)S(1)} %pad_maximum_fusion.2), channel_id=1, source_target_pairs={{0,1},{1,0},{2,3},{3,2},{4,5},{5,4},{6,7},{7,6},{8,9},{9,8},{10,11... | collective-permute-start | bytes 786440 | tf_op jit(solution)/shard_map/ppermute | solution.py:304
  55.4 13.7 %collective-permute-start.15 = (s16[272,256]{1,0:T(8,128)(2,1)}, s16[272,256]{1,0:T(8,128)(2,1)S(1)}, u32[]{:S(2)}, u32[]{:S(2)}) collective-permute-start(s16[272,256]{1,0:T(8,128)(2,1)} %get-tuple-element.42), channel_id=1, source_target_pairs={{0,8},{8,0},{16,24},{24,16},{1,9},{9,1},{17,25},{25,17},{2,10},{10... | collective-permute-start | bytes 417800 | tf_op jit(solution)/shard_map/ppermute | solution.py:290
  61.9 8.6 %collective-permute-start.16 = (s16[272,256]{1,0:T(8,128)(2,1)}, s16[272,256]{1,0:T(8,128)(2,1)S(1)}, u32[]{:S(2)}, u32[]{:S(2)}) collective-permute-start(s16[272,256]{1,0:T(8,128)(2,1)} %get-tuple-element.43), channel_id=1, source_target_pairs={{0,16},{8,24},{16,0},{24,8},{1,17},{9,25},{17,1},{25,9},{2,18},{10... | collective-permute-start | bytes 417800 | tf_op jit(solution)/shard_map/ppermute | solution.py:290
  61.9 8.6 %collective-permute-start.17 = (s16[272,256]{1,0:T(8,128)(2,1)}, s16[272,256]{1,0:T(8,128)(2,1)S(1)}, u32[]{:S(2)}, u32[]{:S(2)}) collective-permute-start(s16[272,256]{1,0:T(8,128)(2,1)} %get-tuple-element.44), channel_id=1, source_target_pairs={{0,24},{8,16},{16,8},{24,0},{1,25},{9,17},{17,9},{25,1},{2,26},{10... | collective-permute-start | bytes 417800 | tf_op jit(solution)/shard_map/ppermute | solution.py:290
  72.2 6.8 %collective-permute-start.18 = (bf16[304,256]{1,0:T(8,128)(2,1)S(1)}, bf16[304,256]{1,0:T(8,128)(2,1)S(1)}, u32[]{:S(2)}, u32[]{:S(2)}) collective-permute-start(bf16[304,256]{1,0:T(8,128)(2,1)S(1)} %get-tuple-element.48), channel_id=1, source_target_pairs={{0,8},{8,0},{16,24},{24,16},{1,9},{9,1},{17,25},{25,17},{2,10},{10... | collective-permute-start | bytes 466952 | tf_op jit(solution)/shard_map/ppermute | solution.py:290
  72.5 8.6 %collective-permute-start.19 = (bf16[304,256]{1,0:T(8,128)(2,1)S(1)}, bf16[304,256]{1,0:T(8,128)(2,1)S(1)}, u32[]{:S(2)}, u32[]{:S(2)}) collective-permute-start(bf16[304,256]{1,0:T(8,128)(2,1)S(1)} %get-tuple-element.49), channel_id=1, source_target_pairs={{0,16},{8,24},{16,0},{24,8},{1,17},{9,25},{17,1},{25,9},{2,18},{10... | collective-permute-start | bytes 466952 | tf_op jit(solution)/shard_map/ppermute | solution.py:290
  74.0 7.1 %collective-permute-start.20 = (bf16[304,256]{1,0:T(8,128)(2,1)S(1)}, bf16[304,256]{1,0:T(8,128)(2,1)S(1)}, u32[]{:S(2)}, u32[]{:S(2)}) collective-permute-start(bf16[304,256]{1,0:T(8,128)(2,1)S(1)} %get-tuple-element.50), channel_id=1, source_target_pairs={{0,24},{8,16},{16,8},{24,0},{1,25},{9,17},{17,9},{25,1},{2,26},{10... | collective-permute-start | bytes 466952 | tf_op jit(solution)/shard_map/ppermute | solution.py:290
  85.4 1.4 %collective-permute-start.21 = (f32[88,256]{1,0:T(8,128)S(1)}, f32[88,256]{1,0:T(8,128)S(1)}, u32[]{:S(2)}, u32[]{:S(2)}) collective-permute-start(f32[88,256]{1,0:T(8,128)S(1)} %pad_maximum_fusion.3), channel_id=1, source_target_pairs={{0,1},{1,0},{2,3},{3,2},{4,5},{5,4},{6,7},{7,6},{8,9},{9,8},{10,11... | collective-permute-start | bytes 270344 | tf_op jit(solution)/shard_map/ppermute | solution.py:304
  86.8 4.6 %collective-permute-start.22 = (bf16[88,256]{1,0:T(8,128)(2,1)S(1)}, bf16[88,256]{1,0:T(8,128)(2,1)S(1)}, u32[]{:S(2)}, u32[]{:S(2)}) collective-permute-start(bf16[88,256]{1,0:T(8,128)(2,1)S(1)} %fusion.11), channel_id=1, source_target_pairs={{0,2},{1,3},{2,0},{3,1},{4,6},{5,7},{6,4},{7,5},{8,10},{9,11},{10,... | collective-permute-start | bytes 135176 | tf_op jit(solution)/shard_map/ppermute | solution.py:304
  86.9 7.1 %collective-permute-start.23 = (bf16[88,256]{1,0:T(8,128)(2,1)S(1)}, bf16[88,256]{1,0:T(8,128)(2,1)S(1)}, u32[]{:S(2)}, u32[]{:S(2)}) collective-permute-start(bf16[88,256]{1,0:T(8,128)(2,1)S(1)} %fusion.11), channel_id=1, source_target_pairs={{0,4},{1,5},{2,6},{3,7},{4,0},{5,1},{6,2},{7,3},{8,12},{9,13},{10,... | collective-permute-start | bytes 135176 | tf_op jit(solution)/shard_map/ppermute | solution.py:304
  87.1 6.8 %collective-permute-start.24 = (bf16[88,256]{1,0:T(8,128)(2,1)S(1)}, bf16[88,256]{1,0:T(8,128)(2,1)S(1)}, u32[]{:S(2)}, u32[]{:S(2)}) collective-permute-start(bf16[88,256]{1,0:T(8,128)(2,1)S(1)} %fusion.11), channel_id=1, source_target_pairs={{0,6},{1,7},{2,4},{3,5},{4,2},{5,3},{6,0},{7,1},{8,14},{9,15},{10,... | collective-permute-start | bytes 135176 | tf_op jit(solution)/shard_map/ppermute | solution.py:304
  94.0 4.4 %collective-permute-start.25 = (bf16[88,256]{1,0:T(8,128)(2,1)S(1)}, bf16[88,256]{1,0:T(8,128)(2,1)S(1)}, u32[]{:S(2)}, u32[]{:S(2)}) collective-permute-start(bf16[88,256]{1,0:T(8,128)(2,1)S(1)} %add_convert_fusion), channel_id=1, source_target_pairs={{0,8},{8,0},{16,24},{24,16},{1,9},{9,1},{17,25},{25,17},{2,10},{10... | collective-permute-start | bytes 135176 | tf_op jit(solution)/shard_map/ppermute | solution.py:290
  95.4 4.0 %collective-permute-start.26 = (bf16[88,256]{1,0:T(8,128)(2,1)S(1)}, bf16[88,256]{1,0:T(8,128)(2,1)S(1)}, u32[]{:S(2)}, u32[]{:S(2)}) collective-permute-start(bf16[88,256]{1,0:T(8,128)(2,1)S(1)} %add_convert_fusion), channel_id=1, source_target_pairs={{0,16},{8,24},{16,0},{24,8},{1,17},{9,25},{17,1},{25,9},{2,18},{10... | collective-permute-start | bytes 135176 | tf_op jit(solution)/shard_map/ppermute | solution.py:290
  96.1 4.9 %collective-permute-start.27 = (bf16[88,256]{1,0:T(8,128)(2,1)S(1)}, bf16[88,256]{1,0:T(8,128)(2,1)S(1)}, u32[]{:S(2)}, u32[]{:S(2)}) collective-permute-start(bf16[88,256]{1,0:T(8,128)(2,1)S(1)} %add_convert_fusion), channel_id=1, source_target_pairs={{0,24},{8,16},{16,8},{24,0},{1,25},{9,17},{17,9},{25,1},{2,26},{10... | collective-permute-start | bytes 135176 | tf_op jit(solution)/shard_map/ppermute | solution.py:290
  101.1 1.5 %collective-permute-start.28 = (f32[160,256]{1,0:T(8,128)S(1)}, f32[160,256]{1,0:T(8,128)S(1)}, u32[]{:S(2)}, u32[]{:S(2)}) collective-permute-start(f32[160,256]{1,0:T(8,128)S(1)} %constant_dynamic-update-slice_fusion.6.total_ref), channel_id=1, source_target_pairs={{0,1},{1,0},{2,3},{3,2},{4,5},{5,4},{6,7},{7,6},{8,9},{9,8},{10,11... | collective-permute-start | bytes 491528 | tf_op jit(solution)/shard_map/ppermute | solution.py:304
  (7 other events, 53.5 us)

commit v9 on v8

--- a/solution.py
+++ b/solution.py
@@ -77,27 +77,13 @@
         coded_ref[...] = encode(partial_ref[delta * own_rows : (delta + 1) * own_rows, :])
 
 
-def pack_kernel(sections, count_hbm, feature_hbm, id_hbm, place_hbm, tiles_hbm, bundle_ref, *refs):
-    parcel_refs = refs[: sections - 1]
-    count_ref, id_ref, place_ref, sems = refs[sections - 1 :]
+def pack_kernel(feature_hbm, id_hbm, bundle_ref, id_ref, sems):
     own_rows, lanes = feature_hbm.shape
-    slots, edge = tiles_hbm.shape[1], tiles_hbm.shape[2]
-    small = [
-        pltpu.make_async_copy(id_hbm, id_ref, sems.at[0]),
-        pltpu.make_async_copy(count_hbm, count_ref, sems.at[1]),
-        pltpu.make_async_copy(place_hbm, place_ref, sems.at[2]),
-    ]
-    large = [pltpu.make_async_copy(feature_hbm, bundle_ref.at[pl.ds(0, own_rows)], sems.at[3])]
-    for section, parcel_ref in enumerate(parcel_refs, 1):
-        large.append(
-            pltpu.make_async_copy(
-                tiles_hbm.at[section], parcel_ref.at[pl.ds(0, slots)], sems.at[3 + section]
-            )
-        )
-    for copy in small + large:
-        copy.start()
-    for copy in small:
-        copy.wait()
+    small = pltpu.make_async_copy(id_hbm, id_ref, sems.at[0])
+    large = pltpu.make_async_copy(feature_hbm, bundle_ref.at[pl.ds(0, own_rows)], sems.at[1])
+    small.start()
+    large.start()
+    small.wait()
     ids = id_ref[...]
     rows = ids.shape[0]
     parts = [ids & 255, jnp.right_shift(ids, 8) & 255, jnp.right_shift(ids, 16)]
@@ -105,15 +91,7 @@
     parts += [jnp.zeros((pad, lanes), jnp.int32)] if pad else []
     digit_rows = jnp.concatenate(parts, axis=0).astype(jnp.float32).astype(jnp.bfloat16)
     bundle_ref[own_rows:, :] = digit_rows
-    first = lax.broadcasted_iota(jnp.int32, (edge, edge), 0) == 0
-    for section, parcel_ref in enumerate(parcel_refs, 1):
-        place = place_ref[section : section + 1, :]
-        line = jnp.concatenate(
-            [place, jnp.full((1, edge - slots), count_ref[section], jnp.int32)], axis=1
-        )
-        parcel_ref[slots] = jnp.where(first, line, 0).astype(jnp.float32).astype(jnp.bfloat16)
-    for copy in large:
-        copy.wait()
+    large.wait()
 
 
 def last_kernel(chunk, spot_ref, total_ref, other_ref, grad_in_ref, grad_out_ref):
@@ -186,78 +164,53 @@
 
 
 def dense_kernel(
-    per_rep, tile_side, turn, spot_ref, order_ref, moved_ref, place_ref, count_ref, own_ref, *refs
+    per_rep, tile_side, turn, spot_ref, place_ref, count_ref, tiles_ref, dense_ref
 ):
-    other_ref, dense_ref = refs if len(refs) == 2 else (None, refs[0])
-    position = pl.program_id(0)
-    rep_index, source_rep = spot_ref[0], spot_ref[1 + position]
-    edge = own_ref.shape[-1]
+    section = pl.program_id(0)
+    rep_index, source_rep = spot_ref[0], spot_ref[1 + section]
+    edge = tiles_ref.shape[-1]
     dense_ref[...] = jnp.zeros_like(dense_ref)
 
-    section = order_ref[position]
-
-    def put_all(tiles_ref, row_of, count):
-        def put(slot, carried):
-            place = place_ref[row_of, slot]
-            row = place // tile_side
-            column = place % tile_side
-            row = ((row // per_rep) ^ rep_index) * per_rep + row % per_rep
-            column = ((column // per_rep) ^ source_rep) * per_rep + column % per_rep
-
-            rows = pl.ds(pl.multiple_of(row * edge, edge), edge)
-            columns = pl.ds(pl.multiple_of(column * edge, edge), edge)
-            tile = tiles_ref[0, slot]
-            if turn:
-                dense_ref[columns, rows] = tile.T
-            else:
-                dense_ref[rows, columns] = tile
-            return carried
-
-        lax.fori_loop(0, count, put, 0)
-
-    if other_ref is None:
-        put_all(own_ref, section, count_ref[section])
-        return
-
-    @pl.when(moved_ref[position] == 0)
-    def _():
-        put_all(own_ref, section, count_ref[section])
-
-    @pl.when(moved_ref[position] != 0)
-    def _():
-        put_all(other_ref, moved_ref[position], count_ref[moved_ref[position]])
-
-
-def build_dense(
-    tiles, others, place, count, spot, order, moved, own_rows, group_rows, turn=False
-):
+    def put(slot, carried):
+        place = place_ref[section, slot]
+        row = place // tile_side
+        column = place % tile_side
+        row = ((row // per_rep) ^ rep_index) * per_rep + row % per_rep
+        column = ((column // per_rep) ^ source_rep) * per_rep + column % per_rep
+        rows = pl.ds(pl.multiple_of(row * edge, edge), edge)
+        columns = pl.ds(pl.multiple_of(column * edge, edge), edge)
+        tile = tiles_ref[0, slot]
+        if turn:
+            dense_ref[columns, rows] = tile.T
+        else:
+            dense_ref[rows, columns] = tile
+        return carried
+
+    lax.fori_loop(0, count_ref[section], put, 0)
+
+
+def build_dense(tiles, place, count, spot, own_rows, group_rows, turn):
     sections, slots, edge, _ = tiles.shape
     body = functools.partial(dense_kernel, own_rows // edge, group_rows // edge, turn)
-    own_block = pl.BlockSpec((1, slots, edge, edge), lambda p, spot, order, *_: (order[p], 0, 0, 0))
-    other_block = pl.BlockSpec(
-        (1, slots + 1, edge, edge),
-        lambda p, spot, order, *_: (jnp.maximum(order[p] - 1, 0), 0, 0, 0),
-    )
-    both = others is not None
     block = (group_rows, group_rows)
     shape = (sections * group_rows, group_rows) if turn else (group_rows, sections * group_rows)
     return pl.pallas_call(
         body,
         grid_spec=pltpu.PrefetchScalarGridSpec(
-            num_scalar_prefetch=5,
+            num_scalar_prefetch=3,
             grid=(sections,),
-            in_specs=[own_block, other_block] if both else [own_block],
+            in_specs=[pl.BlockSpec((1, slots, edge, edge), lambda p, *_: (p, 0, 0, 0))],
             out_specs=pl.BlockSpec(block, lambda p, *_: (p, 0) if turn else (0, p)),
         ),
         out_shape=jax.ShapeDtypeStruct(shape, tiles.dtype),
         compiler_params=pltpu.CompilerParams(
-            vmem_limit_bytes=4 * group_rows**2 + 8 * (slots + 1) * edge**2 + (2 << 20)
+            vmem_limit_bytes=4 * group_rows**2 + 8 * slots * edge**2 + (2 << 20)
         ),
         cost_estimate=pl.CostEstimate(
             flops=0, bytes_accessed=4 * sections * group_rows * group_rows, transcendentals=0
         ),
         name="dense_turned" if turn else "dense",
-    )(spot, order, moved, place, count, *([tiles, others] if both else [tiles]))
+    )(spot, place, count, tiles)
 
 
 def on_device(
@@ -314,8 +267,13 @@
             pieces.append(lax.ppermute(value, ("rep", "blk"), pairs))
         return pieces
 
-    def to_both(block):
-        return [block] + [exchange(block, delta) for delta in range(1, sections)]
+    def to_all(pieces):
+        cut = reps // 2
+        halves = [jnp.concatenate(pieces[:cut], axis=0), jnp.concatenate(pieces[cut:], axis=0)]
+        blocks = list(halves)
+        for j in range(1, sections):
+            blocks += [to_section(half, j) for half in halves]
+        return blocks
 
     side = lax.rem(blk_index, 2)
 
@@ -339,76 +297,45 @@
 
     member = lax.rem(blk_index, sections)
     place, count = tile_place[0, 0], tile_count[0, 0]
-    slots, edge = tile_values.shape[3], tile_values.shape[4]
     width = features.shape[2]
     digit_rows = 3 * own_rows // width
     stride = own_rows + digit_rows + -digit_rows % 16
     anywhere = pl.BlockSpec(memory_space=pl.ANY)
-    bundle, *parcels = pl.pallas_call(
-        functools.partial(pack_kernel, sections),
-        in_specs=[anywhere] * 5,
-        out_shape=[jax.ShapeDtypeStruct((stride, width), bf16)]
-        + [jax.ShapeDtypeStruct((slots + 1, edge, edge), bf16)] * (sections - 1),
+    bundle = pl.pallas_call(
+        pack_kernel,
+        in_specs=[anywhere] * 2,
+        out_shape=jax.ShapeDtypeStruct((stride, width), bf16),
         scratch_shapes=[
-            pltpu.SMEM((sections,), jnp.int32),
             pltpu.VMEM((own_rows // width, width), jnp.int32),
-            pltpu.VMEM((sections, slots), jnp.int32),
-            pltpu.SemaphoreType.DMA((sections + 3,)),
+            pltpu.SemaphoreType.DMA((2,)),
         ],
         compiler_params=pltpu.CompilerParams(vmem_limit_bytes=60 * 1024 * 1024),
         name="pack",
-    )(
-        tile_count[0, 0], features[0], node_ids.reshape(-1, width), tile_place[0, 0],
-        tile_values[0, 0],
-    )
+    )(features[0], node_ids.reshape(-1, width))
     arrived = to_pieces(bundle)
-    for j in range(1, sections):
-        pairs = []
-        for r in range(reps):
-            for c in range(blks):
-                if c % sections < j:
-                    pairs.append((r * blks + c, (r + 1) % reps * blks + c))
-        parcels[j - 1] = lax.ppermute(parcels[j - 1], ("rep", "blk"), pairs)
-    other_place = [parcel[slots, 0, : slots + 1].astype(jnp.int32) for parcel in parcels]
-    position = jnp.arange(sections, dtype=jnp.int32)
-    column = position ^ member
-    order = jnp.mod(member - column, sections)
-    moved = jnp.where(column > member, sections - 1 + order, 0)
-    both_place = jnp.concatenate([place] + [part[None, :slots] for part in other_place], axis=0)
-    both_count = jnp.concatenate([count] + [part[slots:] for part in other_place])
-    tiles = tile_values[0, 0]
-    where = jnp.broadcast_to(rep_index, (sections + 1,))
     next_rep = lax.rem(rep_index + 1, reps)
-    first_where = jnp.where(member < jnp.arange(sections + 1) - 1, next_rep, rep_index)
-    block = jnp.concatenate(arrived, axis=0)
-    count, block = lax.optimization_barrier((count, block))
-    dense = build_dense(
-        tiles, None, place, count, first_where, position, position, own_rows, group_rows
-    )
-    blocks = [block] + [to_section(block, j) for j in range(1, sections)]
-    pieces = [whole[d * stride : (d + 1) * stride] for whole in blocks for d in range(reps)]
-    digit_sets = to_both(jnp.stack([part[own_rows:] for part in pieces[:reps]]))
-    id_columns = jnp.concatenate([undo_digits(rows[d]) for rows in digit_sets for d in range(reps)])
+    where = jnp.where(member < jnp.arange(sections + 1) - 1, next_rep, rep_index)
+    layout = (where, own_rows, group_rows)
+    count, arrived[0] = lax.optimization_barrier((count, arrived[0]))
+    dense = build_dense(tile_values[0, 0], place, count, *layout, False)
+    pieces = [
+        half[d * stride : (d + 1) * stride] for half in to_all(arrived) for d in range(reps // 2)
+    ]
+    id_columns = jnp.concatenate([undo_digits(piece[own_rows:]) for piece in pieces])
     feature_columns = jnp.concatenate([piece[:own_rows] for piece in pieces], axis=0)
     units = jnp.arange(hidden_width, dtype=jnp.int32)
     kept = keep_mask(id_columns[:, None], units[None, :])
     chunks = dot(dense, feature_columns).reshape(reps, own_rows, width)
-    layout = (
-        tiles, jnp.stack(parcels), both_place, both_count, where, order, moved, own_rows, group_rows
-    )
     arrived = [swap(chunks[delta], delta) for delta in range(1, reps)]
-    dense, arrived = lax.optimization_barrier((build_dense(*layout), arrived))
     total = chunks[0]
     for part in arrived:
         total = total + part
     z_input = total.astype(bf16)
-    arrived = to_pieces(z_input)
-    z_columns = jnp.concatenate(to_both(jnp.concatenate(arrived, axis=0)), axis=0)
+    z_columns = jnp.concatenate(to_all(to_pieces(z_input)), axis=0)
     kept, z_columns = lax.optimization_barrier((kept, z_columns))
     third = f32(4.0 / 3.0)
     pre_act = dot(z_columns, weight_in)
     dropped = (jnp.maximum(pre_act, 0.0) * (kept.astype(f32) * third)).astype(bf16)
-    mask = jnp.where(pre_act > 0, kept, jnp.zeros_like(kept))
     second = dot(dense, dropped)
     sent = simple_call(
         encode_kernel,
@@ -416,9 +343,6 @@
         "encode", second,
     )
     arrived = [swap(sent[d - 1], d) for d in range(1, reps)]
-    turned, mask, second = lax.optimization_barrier(
-        (build_dense(*layout, turn=True), mask, second)
-    )
     classes = weight_out.shape[1]
     chunk = -(-classes // (16 * reps)) * 16
     spot = jnp.stack([side, rep_index])
@@ -436,10 +360,13 @@
         scratch=[pltpu.VMEM((chunk * reps, hidden_width), f32)],
     )
     arrived = [swap(sent[d], d) for d in range(reps)]
+    count, z_again, kept, out_total = lax.optimization_barrier((count, z_columns, kept, out_total))
+    turned = build_dense(tile_values[0, 0], place, count, *layout, True)
+    mask = jnp.where(dot(z_again, weight_in) > 0, kept, jnp.zeros_like(kept))
     grad_block = jnp.concatenate([part[:own_rows] for part in arrived], axis=0)
     for part in arrived[1:]:
         out_total = out_total + part[own_rows:].astype(f32)
-    grad_block, out_total = lax.optimization_barrier((grad_block, out_total))
+    grad_block, mask, out_total = lax.optimization_barrier((grad_block, mask, out_total))
     back = dot(turned, grad_block)
     pre_slope = (back * (mask.astype(f32) * third)).astype(bf16)
     pre_slope, out_total = lax.optimization_barrier((pre_slope, out_total))

time: 104 us -> 100 us (0.962)
  starting transfers between devices: 49.7 us -> 44.9 us
  Pallas kernels: 13 us -> 10.1 us
  waiting for transfers between devices: 25.1 us -> 27.1 us
  local copies, waits for them, and re-layouts: 4.72 us -> 6.41 us
    ppermute x1 -> x4, starting transfers between devices: 0.06 us -> 7.47 us  [to_section(): return lax.ppermute(block, ('rep', 'blk'), pairs)]
    ppermute x8, starting transfers between devices: 20.7 us -> 14.2 us  [to_pieces(): pieces.append(lax.ppermute(value, ('rep', 'blk'), pairs))]
    ppermute x8, waiting for transfers between devices: 1.07 us -> 5.21 us  [to_pieces(): pieces.append(lax.ppermute(value, ('rep', 'blk'), pairs))]
    unnamed x33 -> x42, local copies, waits for them, and re-layouts: 3.03 us -> 6.01 us
    ppermute x1 -> x4, waiting for transfers between devices: 5.77 us -> 3.02 us  [to_section(): return lax.ppermute(block, ('rep', 'blk'), pairs)]
    ppermute x7 -> x5, starting transfers between devices: 7.28 us -> 4.59 us  [exchange(): return lax.ppermute(value, 'blk', [(c, c ^ delta) for c in range(blks)])]
    ppermute x1 -> x0, starting transfers between devices: 2.46 us -> none  [on_device(): parcels[j - 1] = lax.ppermute(parcels[j - 1], ('rep', 'blk'), pairs)]
    ppermute x12, waiting for transfers between devices: 12.2 us -> 14.4 us  [swap(): return lax.ppermute(value, 'rep', [(r, r ^ delta) for r in range(reps)])]
  transfers between devices with their start and end apart: 29 -> 29, of which waited for: 14 -> 18; matrix products, arithmetic and copies ran while one was open for 6% -> 4% of each run, Pallas kernels for 7% -> 5%
where the time goes in v9:
time: 100 us; the launch traced here: 99.6 us
  starting transfers between devices  44.9 us (45%)
  waiting for transfers between devices  27.1 us (27%)
  Pallas kernels  10.1 us (10%)
  matrix products  8.5 us (8%)
  local copies, waits for them, and re-layouts  6.41 us (6%)
  other arithmetic  1.41 us (1%)
  between operations  1.2 us (1%)
    ppermute x12, starting transfers between devices, swap(): return lax.ppermute(value, 'rep', [(r, r ^ delta) for r in range(reps)])  18.7 us
    ppermute x12, waiting for transfers between devices, swap(): return lax.ppermute(value, 'rep', [(r, r ^ delta) for r in range(reps)])  14.4 us
    ppermute x8, starting transfers between devices, to_pieces(): pieces.append(lax.ppermute(value, ('rep', 'blk'), pairs))  14.2 us
    dot_general x4, matrix products, dot(): return jnp.dot(left, right, preferred_element_type=jnp.float32)  8.16 us
    ppermute x4, starting transfers between devices, to_section(): return lax.ppermute(block, ('rep', 'blk'), pairs)  7.47 us
    unnamed x42, local copies, waits for them, and re-layouts  6.01 us
    pallas_call x2, Pallas kernels, build_dense(): pl.pallas_call(body, grid_spec=pltpu.PrefetchScalarGridSpec(num_scalar_pr...  5.25 us
    ppermute x8, waiting for transfers between devices, to_pieces(): pieces.append(lax.ppermute(value, ('rep', 'blk'), pairs))  5.21 us
  transfers between devices with their start and end apart: 29, of which 18 were waited for; matrix products, arithmetic and copies ran while one was open for 4% of the time, Pallas kernels for 5%

profile of v9, /device:TPU:0, one launch (start us, length us, event | category | flops | bytes accessed | tf_op | source)
XLA Modules:
  0.0 99.6 jit_solution(6921455701667474687)
XLA Ops:
  0.6 1.5 %pack.1 = bf16[272,128]{1,0:T(8,128)(2,1)} custom-call(bf16[256,128]{1,0:T(8,128)(2,1)} %bitcast.47, s32[2,128]{1,0:T(2,128)} %bitcast.48), custom_call_target="tpu_custom_call" | custom-call | tf_op jit(solution)/shard_map/pack/pallas_call | solution.py:304
  2.2 7.0 %collective-permute-start.3 = (bf16[272,128]{1,0:T(8,128)(2,1)}, bf16[272,128]{1,0:T(8,128)(2,1)S(1)}, u32[]{:S(2)}, u32[]{:S(2)}) collective-permute-start(bf16[272,128]{1,0:T(8,128)(2,1)} %pack.1), channel_id=1, source_target_pairs={{0,30},{1,31},{2,24},{3,25},{4,26},{5,27},{6,28},{7,29},{8,20},{9,... | collective-permute-start | bytes 208904 | tf_op jit(solution)/shard_map/ppermute | solution.py:267
  9.7 1.5 %collective-permute-start = (bf16[272,128]{1,0:T(8,128)(2,1)}, bf16[272,128]{1,0:T(8,128)(2,1)S(1)}, u32[]{:S(2)}, u32[]{:S(2)}) collective-permute-start(bf16[272,128]{1,0:T(8,128)(2,1)} %pack.1), channel_id=1, source_target_pairs={{0,0},{1,1},{2,2},{3,3},{4,4},{5,5},{6,6},{7,7},{8,10},{9,11},{10,... | collective-permute-start | bytes 208904 | tf_op jit(solution)/shard_map/ppermute | solution.py:267
  12.1 1.6 %collective-permute-done.2 = bf16[272,128]{1,0:T(8,128)(2,1)S(1)} collective-permute-done((bf16[272,128]{1,0:T(8,128)(2,1)}, bf16[272,128]{1,0:T(8,128)(2,1)S(1)}, u32[]{:S(2)}, u32[]{:S(2)}) %collective-permute-start.2) | collective-permute-done | bytes 69664 | tf_op jit(solution)/shard_map/ppermute | solution.py:267
  14.2 5.1 %collective-permute-start.4 = (bf16[544,128]{1,0:T(8,128)(2,1)S(1)}, bf16[544,128]{1,0:T(8,128)(2,1)S(1)}, u32[]{:S(2)}, u32[]{:S(2)}) collective-permute-start(bf16[544,128]{1,0:T(8,128)(2,1)S(1)} %pad_maximum_fusion.1), channel_id=1, source_target_pairs={{0,1},{1,24},{2,3},{3,26},{4,5},{5,28},{6,7},{7,30},{8,9},{9,0},{1... | collective-permute-start | bytes 417800 | tf_op jit(solution)/shard_map/ppermute | solution.py:254
  21.8 2.1 %dense.1 = bf16[1024,2048]{1,0:T(8,128)(2,1)S(1)} custom-call(s32[3]{0:T(128)S(1)} %compare_select_fusion.spot_ref, s32[2,16]{1,0:T(2,128)S(1)} %bitcast.42, s32[2]{0:T(128)S(1)} %bitcast.44, bf16[2,16,128,128]{3,2,1,0:T(8,128)(2,1)S(1)} %bitcast.39), custom_call_target="tpu_custom_call" | custom-call | bytes 8388608 | tf_op jit(solution)/shard_map/dense/pallas_call | solution.py:197
  26.0 2.4 %collective-permute-start.6 = (f32[256,128]{1,0:T(8,128)S(1)}, f32[256,128]{1,0:T(8,128)S(1)}, u32[]{:S(2)}, u32[]{:S(2)}) collective-permute-start(f32[256,128]{1,0:T(8,128)S(1)} %get-tuple-element.57), channel_id=1, source_target_pairs={{0,8},{8,0},{16,24},{24,16},{1,9},{9,1},{17,25},{25,17},{2,10},{10... | collective-permute-start | bytes 393224 | tf_op jit(solution)/shard_map/ppermute | solution.py:243
  28.3 1.4 %collective-permute-start.8 = (f32[256,128]{1,0:T(8,128)S(1)}, f32[256,128]{1,0:T(8,128)S(1)}, u32[]{:S(2)}, u32[]{:S(2)}) collective-permute-start(f32[256,128]{1,0:T(8,128)S(1)} %get-tuple-element.58), channel_id=1, source_target_pairs={{0,24},{8,16},{16,8},{24,0},{1,25},{9,17},{17,9},{25,1},{2,26},{10... | collective-permute-start | bytes 393224 | tf_op jit(solution)/shard_map/ppermute | solution.py:243
  29.9 2.0 %collective-permute-done.6 = f32[256,128]{1,0:T(8,128)S(1)} collective-permute-done((f32[256,128]{1,0:T(8,128)S(1)}, f32[256,128]{1,0:T(8,128)S(1)}, u32[]{:S(2)}, u32[]{:S(2)}) %collective-permute-start.6) | collective-permute-done | bytes 131104 | tf_op jit(solution)/shard_map/ppermute | solution.py:243
  32.0 3.6 %collective-permute-done.8 = f32[256,128]{1,0:T(8,128)S(1)} collective-permute-done((f32[256,128]{1,0:T(8,128)S(1)}, f32[256,128]{1,0:T(8,128)S(1)}, u32[]{:S(2)}, u32[]{:S(2)}) %collective-permute-start.8) | collective-permute-done | bytes 131104 | tf_op jit(solution)/shard_map/ppermute | solution.py:243
  35.6 1.3 %collective-permute-done.7 = f32[256,128]{1,0:T(8,128)S(1)} collective-permute-done((f32[256,128]{1,0:T(8,128)S(1)}, f32[256,128]{1,0:T(8,128)S(1)}, u32[]{:S(2)}, u32[]{:S(2)}) %collective-permute-start.7) | collective-permute-done | bytes 131104 | tf_op jit(solution)/shard_map/ppermute | solution.py:243
  37.0 1.6 %collective-permute-start.12 = (bf16[256,128]{1,0:T(8,128)(2,1)S(1)}, bf16[256,128]{1,0:T(8,128)(2,1)S(1)}, u32[]{:S(2)}, u32[]{:S(2)}) collective-permute-start(bf16[256,128]{1,0:T(8,128)(2,1)S(1)} %fusion.12), channel_id=1, source_target_pairs={{0,30},{1,31},{2,24},{3,25},{4,26},{5,27},{6,28},{7,29},{8,20},{9,... | collective-permute-start | bytes 196616 | tf_op jit(solution)/shard_map/ppermute | solution.py:267
  38.6 1.7 %collective-permute-start.11 = (bf16[256,128]{1,0:T(8,128)(2,1)S(1)}, bf16[256,128]{1,0:T(8,128)(2,1)S(1)}, u32[]{:S(2)}, u32[]{:S(2)}) collective-permute-start(bf16[256,128]{1,0:T(8,128)(2,1)S(1)} %fusion.12), channel_id=1, source_target_pairs={{0,20},{1,21},{2,22},{3,23},{4,16},{5,17},{6,18},{7,19},{8,30},{9,... | collective-permute-start | bytes 196616 | tf_op jit(solution)/shard_map/ppermute | solution.py:267
  43.1 2.4 %collective-permute-done.10 = bf16[256,128]{1,0:T(8,128)(2,1)S(1)} collective-permute-done((bf16[256,128]{1,0:T(8,128)(2,1)S(1)}, bf16[256,128]{1,0:T(8,128)(2,1)S(1)}, u32[]{:S(2)}, u32[]{:S(2)}) %collective-permute-start.10) | collective-permute-done | bytes 65568 | tf_op jit(solution)/shard_map/ppermute | solution.py:267
  45.5 2.3 %collective-permute-start.13 = (bf16[512,128]{1,0:T(8,128)(2,1)S(1)}, bf16[512,128]{1,0:T(8,128)(2,1)S(1)}, u32[]{:S(2)}, u32[]{:S(2)}) collective-permute-start(bf16[512,128]{1,0:T(8,128)(2,1)S(1)} %pad_maximum_fusion.3), channel_id=1, source_target_pairs={{0,1},{1,24},{2,3},{3,26},{4,5},{5,28},{6,7},{7,30},{8,9},{9,0},{1... | collective-permute-start | bytes 393224 | tf_op jit(solution)/shard_map/ppermute | solution.py:254
  47.9 3.0 %collective-permute-done.13 = bf16[512,128]{1,0:T(8,128)(2,1)S(1)} collective-permute-done((bf16[512,128]{1,0:T(8,128)(2,1)S(1)}, bf16[512,128]{1,0:T(8,128)(2,1)S(1)}, u32[]{:S(2)}, u32[]{:S(2)}) %collective-permute-start.13) | collective-permute-done | bytes 131104 | tf_op jit(solution)/shard_map/ppermute | solution.py:254
  51.8 4.1 %fusion.7.partial_ref.own_ref = f32[1024,256]{1,0:T(8,128)S(1)} fusion(bf16[1024,2048]{1,0:T(8,128)(2,1)} %copy-done.1, bf16[2048,128]{1,0:T(8,128)(2,1)S(1)} %constant_dynamic-update-slice_fusion.1, bf16[128,256]{1,0:T(8,128)(2,1)S(1)} %copy-done, bf16[2048,256]{1,0:T(8,128)(2,1)S(1)} %fusion.6), kind=kOutput, calls=%fused_computation.12 | convolution fusion | flops 1210580992 | bytes 6881280 | tf_op jit(solution)/shard_map/dot_general | solution.py:32
  56.4 5.7 %collective-permute-start.15 = (s16[272,256]{1,0:T(8,128)(2,1)S(1)}, s16[272,256]{1,0:T(8,128)(2,1)S(1)}, u32[]{:S(2)}, u32[]{:S(2)}) collective-permute-start(s16[272,256]{1,0:T(8,128)(2,1)S(1)} %get-tuple-element.31), channel_id=1, source_target_pairs={{0,8},{8,0},{16,24},{24,16},{1,9},{9,1},{17,25},{25,17},{2,10},{10... | collective-permute-start | bytes 417800 | tf_op jit(solution)/shard_map/ppermute | solution.py:243
  62.7 1.4 %collective-permute-start.17 = (s16[272,256]{1,0:T(8,128)(2,1)S(1)}, s16[272,256]{1,0:T(8,128)(2,1)S(1)}, u32[]{:S(2)}, u32[]{:S(2)}) collective-permute-start(s16[272,256]{1,0:T(8,128)(2,1)S(1)} %get-tuple-element.33), channel_id=1, source_target_pairs={{0,24},{8,16},{16,8},{24,0},{1,25},{9,17},{17,9},{25,1},{2,26},{10... | collective-permute-start | bytes 417800 | tf_op jit(solution)/shard_map/ppermute | solution.py:243
  64.5 1.8 %collective-permute-done.15.refs_0_ = s16[272,256]{1,0:T(8,128)(2,1)S(1)} collective-permute-done((s16[272,256]{1,0:T(8,128)(2,1)S(1)}, s16[272,256]{1,0:T(8,128)(2,1)S(1)}, u32[]{:S(2)}, u32[]{:S(2)}) %collective-permute-start.15) | collective-permute-done | bytes 139296 | tf_op jit(solution)/shard_map/ppermute | solution.py:243
  66.3 1.9 %collective-permute-done.16.refs_1_ = s16[272,256]{1,0:T(8,128)(2,1)S(1)} collective-permute-done((s16[272,256]{1,0:T(8,128)(2,1)S(1)}, s16[272,256]{1,0:T(8,128)(2,1)S(1)}, u32[]{:S(2)}, u32[]{:S(2)}) %collective-permute-start.16) | collective-permute-done | bytes 139296 | tf_op jit(solution)/shard_map/ppermute | solution.py:243
  68.3 1.5 %collective-permute-done.17.refs_2_ = s16[272,256]{1,0:T(8,128)(2,1)S(1)} collective-permute-done((s16[272,256]{1,0:T(8,128)(2,1)S(1)}, s16[272,256]{1,0:T(8,128)(2,1)S(1)}, u32[]{:S(2)}, u32[]{:S(2)}) %collective-permute-start.17) | collective-permute-done | bytes 139296 | tf_op jit(solution)/shard_map/ppermute | solution.py:243
  69.8 1.6 %head.1 = (f32[256,172]{1,0:T(8,128)S(1)}, f32[48,256]{1,0:T(8,128)S(1)}, bf16[304,256]{1,0:T(8,128)(2,1)S(1)}, bf16[304,256]{1,0:T(8,128)(2,1)S(1)}, bf16[304,2...) custom-call(s32[2]{0:T(128)S(1)} %pad_add_fusion.spot_ref, bf16[256,172]{1,0:T(8,128)(2,1)S(1)} %copy.15.weight_ref, ...), custom_call_target="tpu_custom_call" | custom-call | tf_op jit(solution)/shard_map/head/pallas_call | solution.py:156
  72.8 2.1 %collective-permute-start.20 = (bf16[304,256]{1,0:T(8,128)(2,1)S(1)}, bf16[304,256]{1,0:T(8,128)(2,1)S(1)}, u32[]{:S(2)}, u32[]{:S(2)}) collective-permute-start(bf16[304,256]{1,0:T(8,128)(2,1)S(1)} %get-tuple-element.40), channel_id=1, source_target_pairs={{0,24},{8,16},{16,8},{24,0},{1,25},{9,17},{17,9},{25,1},{2,26},{10... | collective-permute-start | bytes 466952 | tf_op jit(solution)/shard_map/ppermute | solution.py:243
  74.9 1.5 %convolution_compare_fusion = pred[2048,256]{1,0:T(8,128)(4,1)S(1)} fusion(bf16[2048,128]{1,0:T(8,128)(2,1)} %copy-done.9, bf16[128,256]{1,0:T(8,128)(2,1)S(1)} %copy-done), kind=kOutput, calls=%fused_computation.7 | convolution fusion | flops 134742016 | bytes 1114112 | tf_op jit(solution)/shard_map/dot_general | solution.py:32
  77.7 3.1 %dense_turned.1 = bf16[2048,1024]{1,0:T(8,128)(2,1)S(1)} custom-call(s32[3]{0:T(128)S(1)} %compare_select_fusion.spot_ref, s32[2,16]{1,0:T(2,128)S(1)} %bitcast.43, s32[2]{0:T(128)S(1)} %bitcast.45, bf16[2,16,128,128]{3,2,1,0:T(8,128)(2,1)S(1)} %bitcast.40), custom_call_target="tpu_custom_call" | custom-call | bytes 8388608 | tf_op jit(solution)/shard_map/dense_turned/pallas_call | solution.py:197
  80.9 1.3 %fusion.2 = bf16[2048,256]{1,0:T(8,128)(2,1)S(1)} fusion(bf16[2048,1024]{1,0:T(8,128)(2,1)S(1)} %dense_turned.1, bf16[1024,256]{1,0:T(8,128)(2,1)S(1)} %pad_maximum_fusion, bf16[2048,256]{1,0:T(8,128)(2,1)S(1)} %broadcast_select_fusion), kind=kOutput, calls=%fused_computation.6 | convolution fusion | flops 1075838976 | bytes 6815744 | tf_op jit(solution)/shard_map/dot_general | solution.py:32
  84.7 3.8 %collective-permute-start.22 = (bf16[88,256]{1,0:T(8,128)(2,1)S(1)}, bf16[88,256]{1,0:T(8,128)(2,1)S(1)}, u32[]{:S(2)}, u32[]{:S(2)}) collective-permute-start(bf16[88,256]{1,0:T(8,128)(2,1)S(1)} %fusion.13), channel_id=1, source_target_pairs={{0,2},{1,3},{2,0},{3,1},{4,6},{5,7},{6,4},{7,5},{8,10},{9,11},{10,... | collective-permute-start | bytes 135176 | tf_op jit(solution)/shard_map/ppermute | solution.py:257
  88.5 2.0 %collective-permute-done.24 = bf16[88,256]{1,0:T(8,128)(2,1)S(1)} collective-permute-done((bf16[88,256]{1,0:T(8,128)(2,1)S(1)}, bf16[88,256]{1,0:T(8,128)(2,1)S(1)}, u32[]{:S(2)}, u32[]{:S(2)}) %collective-permute-start.24) | collective-permute-done | bytes 45088 | tf_op jit(solution)/shard_map/ppermute | solution.py:257
  92.8 1.9 %collective-permute-start.25 = (bf16[88,256]{1,0:T(8,128)(2,1)S(1)}, bf16[88,256]{1,0:T(8,128)(2,1)S(1)}, u32[]{:S(2)}, u32[]{:S(2)}) collective-permute-start(bf16[88,256]{1,0:T(8,128)(2,1)S(1)} %add_convert_fusion), channel_id=1, source_target_pairs={{0,8},{8,0},{16,24},{24,16},{1,9},{9,1},{17,25},{25,17},{2,10},{10... | collective-permute-start | bytes 135176 | tf_op jit(solution)/shard_map/ppermute | solution.py:243
  94.7 1.8 %collective-permute-done.27 = bf16[88,256]{1,0:T(8,128)(2,1)S(1)} collective-permute-done((bf16[88,256]{1,0:T(8,128)(2,1)S(1)}, bf16[88,256]{1,0:T(8,128)(2,1)S(1)}, u32[]{:S(2)}, u32[]{:S(2)}) %collective-permute-start.27) | collective-permute-done | bytes 45088 | tf_op jit(solution)/shard_map/ppermute | solution.py:243
  98.4 1.3 %last.1 = (f32[128,256]{1,0:T(8,128)}, f32[172,256]{1,0:T(8,128)}) custom-call(s32[2]{0:T(128)S(1)} %pad_add_fusion.spot_ref, f32[160,256]{1,0:T(8,128)S(1)} %constant_dynamic-update-slice_fusion.7.total_ref, f32[160,256]{1,0:T(8,128)S(1)} %collective-permute-done.28.other_ref), custom_call_target="tpu_custom_call" | custom-call | tf_op jit(solution)/shard_map/last/pallas_call | solution.py:156
  (120 shorter events, 20.9 us)
Async XLA Ops:
  0.6 51.1 %copy-start = (bf16[128,256]{1,0:T(8,128)(2,1)S(1)}, bf16[128,256]{1,0:T(8,128)(2,1)}, u32[]{:S(2)}) copy-start(bf16[128,256]{1,0:T(8,128)(2,1)} %param.17) | copy-start | bytes 196612
  2.2 9.9 %collective-permute-start.3 = (bf16[272,128]{1,0:T(8,128)(2,1)}, bf16[272,128]{1,0:T(8,128)(2,1)S(1)}, u32[]{:S(2)}, u32[]{:S(2)}) collective-permute-start(bf16[272,128]{1,0:T(8,128)(2,1)} %pack.1), channel_id=1, source_target_pairs={{0,30},{1,31},{2,24},{3,25},{4,26},{5,27},{6,28},{7,29},{8,20},{9,... | collective-permute-start | bytes 208904 | tf_op jit(solution)/shard_map/ppermute | solution.py:267
  9.2 4.5 %collective-permute-start.2 = (bf16[272,128]{1,0:T(8,128)(2,1)}, bf16[272,128]{1,0:T(8,128)(2,1)S(1)}, u32[]{:S(2)}, u32[]{:S(2)}) collective-permute-start(bf16[272,128]{1,0:T(8,128)(2,1)} %pack.1), channel_id=1, source_target_pairs={{0,20},{1,21},{2,22},{3,23},{4,16},{5,17},{6,18},{7,19},{8,30},{9,... | collective-permute-start | bytes 208904 | tf_op jit(solution)/shard_map/ppermute | solution.py:267
  9.7 4.5 %collective-permute-start.1 = (bf16[272,128]{1,0:T(8,128)(2,1)}, bf16[272,128]{1,0:T(8,128)(2,1)S(1)}, u32[]{:S(2)}, u32[]{:S(2)}) collective-permute-start(bf16[272,128]{1,0:T(8,128)(2,1)} %pack.1), channel_id=1, source_target_pairs={{0,10},{1,11},{2,12},{3,13},{4,14},{5,15},{6,8},{7,9},{8,0},{9,1},... | collective-permute-start | bytes 208904 | tf_op jit(solution)/shard_map/ppermute | solution.py:267
  9.7 1.5 %collective-permute-start = (bf16[272,128]{1,0:T(8,128)(2,1)}, bf16[272,128]{1,0:T(8,128)(2,1)S(1)}, u32[]{:S(2)}, u32[]{:S(2)}) collective-permute-start(bf16[272,128]{1,0:T(8,128)(2,1)} %pack.1), channel_id=1, source_target_pairs={{0,0},{1,1},{2,2},{3,3},{4,4},{5,5},{6,6},{7,7},{8,10},{9,11},{10,... | collective-permute-start | bytes 208904 | tf_op jit(solution)/shard_map/ppermute | solution.py:267
  13.7 10.4 %collective-permute-start.5 = (bf16[544,128]{1,0:T(8,128)(2,1)S(1)}, bf16[544,128]{1,0:T(8,128)(2,1)S(1)}, u32[]{:S(2)}, u32[]{:S(2)}) collective-permute-start(bf16[544,128]{1,0:T(8,128)(2,1)S(1)} %pad_maximum_fusion.2), channel_id=1, source_target_pairs={{0,1},{1,24},{2,3},{3,26},{4,5},{5,28},{6,7},{7,30},{8,9},{9,0},{1... | collective-permute-start | bytes 417800 | tf_op jit(solution)/shard_map/ppermute | solution.py:254
  14.2 9.9 %collective-permute-start.4 = (bf16[544,128]{1,0:T(8,128)(2,1)S(1)}, bf16[544,128]{1,0:T(8,128)(2,1)S(1)}, u32[]{:S(2)}, u32[]{:S(2)}) collective-permute-start(bf16[544,128]{1,0:T(8,128)(2,1)S(1)} %pad_maximum_fusion.1), channel_id=1, source_target_pairs={{0,1},{1,24},{2,3},{3,26},{4,5},{5,28},{6,7},{7,30},{8,9},{9,0},{1... | collective-permute-start | bytes 417800 | tf_op jit(solution)/shard_map/ppermute | solution.py:254
  26.0 6.0 %collective-permute-start.6 = (f32[256,128]{1,0:T(8,128)S(1)}, f32[256,128]{1,0:T(8,128)S(1)}, u32[]{:S(2)}, u32[]{:S(2)}) collective-permute-start(f32[256,128]{1,0:T(8,128)S(1)} %get-tuple-element.57), channel_id=1, source_target_pairs={{0,8},{8,0},{16,24},{24,16},{1,9},{9,1},{17,25},{25,17},{2,10},{10... | collective-permute-start | bytes 393224 | tf_op jit(solution)/shard_map/ppermute | solution.py:243
  28.3 7.3 %collective-permute-start.8 = (f32[256,128]{1,0:T(8,128)S(1)}, f32[256,128]{1,0:T(8,128)S(1)}, u32[]{:S(2)}, u32[]{:S(2)}) collective-permute-start(f32[256,128]{1,0:T(8,128)S(1)} %get-tuple-element.58), channel_id=1, source_target_pairs={{0,24},{8,16},{16,8},{24,0},{1,25},{9,17},{17,9},{25,1},{2,26},{10... | collective-permute-start | bytes 393224 | tf_op jit(solution)/shard_map/ppermute | solution.py:243
  29.7 7.3 %collective-permute-start.7 = (f32[256,128]{1,0:T(8,128)S(1)}, f32[256,128]{1,0:T(8,128)S(1)}, u32[]{:S(2)}, u32[]{:S(2)}) collective-permute-start(f32[256,128]{1,0:T(8,128)S(1)} %get-tuple-element.59), channel_id=1, source_target_pairs={{0,16},{8,24},{16,0},{24,8},{1,17},{9,25},{17,1},{25,9},{2,18},{10... | collective-permute-start | bytes 393224 | tf_op jit(solution)/shard_map/ppermute | solution.py:243
  37.0 6.0 %collective-permute-start.12 = (bf16[256,128]{1,0:T(8,128)(2,1)S(1)}, bf16[256,128]{1,0:T(8,128)(2,1)S(1)}, u32[]{:S(2)}, u32[]{:S(2)}) collective-permute-start(bf16[256,128]{1,0:T(8,128)(2,1)S(1)} %fusion.12), channel_id=1, source_target_pairs={{0,30},{1,31},{2,24},{3,25},{4,26},{5,27},{6,28},{7,29},{8,20},{9,... | collective-permute-start | bytes 196616 | tf_op jit(solution)/shard_map/ppermute | solution.py:267
  38.6 4.5 %collective-permute-start.11 = (bf16[256,128]{1,0:T(8,128)(2,1)S(1)}, bf16[256,128]{1,0:T(8,128)(2,1)S(1)}, u32[]{:S(2)}, u32[]{:S(2)}) collective-permute-start(bf16[256,128]{1,0:T(8,128)(2,1)S(1)} %fusion.12), channel_id=1, source_target_pairs={{0,20},{1,21},{2,22},{3,23},{4,16},{5,17},{6,18},{7,19},{8,30},{9,... | collective-permute-start | bytes 196616 | tf_op jit(solution)/shard_map/ppermute | solution.py:267
  41.2 4.3 %collective-permute-start.10 = (bf16[256,128]{1,0:T(8,128)(2,1)S(1)}, bf16[256,128]{1,0:T(8,128)(2,1)S(1)}, u32[]{:S(2)}, u32[]{:S(2)}) collective-permute-start(bf16[256,128]{1,0:T(8,128)(2,1)S(1)} %fusion.12), channel_id=1, source_target_pairs={{0,10},{1,11},{2,12},{3,13},{4,14},{5,15},{6,8},{7,9},{8,0},{9,1},... | collective-permute-start | bytes 196616 | tf_op jit(solution)/shard_map/ppermute | solution.py:267
  42.4 3.1 %collective-permute-start.9 = (bf16[256,128]{1,0:T(8,128)(2,1)S(1)}, bf16[256,128]{1,0:T(8,128)(2,1)S(1)}, u32[]{:S(2)}, u32[]{:S(2)}) collective-permute-start(bf16[256,128]{1,0:T(8,128)(2,1)S(1)} %fusion.12), channel_id=1, source_target_pairs={{0,0},{1,1},{2,2},{3,3},{4,4},{5,5},{6,6},{7,7},{8,10},{9,11},{10,... | collective-permute-start | bytes 196616 | tf_op jit(solution)/shard_map/ppermute | solution.py:267
  43.1 7.8 %collective-permute-start.14 = (bf16[512,128]{1,0:T(8,128)(2,1)S(1)}, bf16[512,128]{1,0:T(8,128)(2,1)S(1)}, u32[]{:S(2)}, u32[]{:S(2)}) collective-permute-start(bf16[512,128]{1,0:T(8,128)(2,1)S(1)} %pad_maximum_fusion.4), channel_id=1, source_target_pairs={{0,1},{1,24},{2,3},{3,26},{4,5},{5,28},{6,7},{7,30},{8,9},{9,0},{1... | collective-permute-start | bytes 393224 | tf_op jit(solution)/shard_map/ppermute | solution.py:254
  45.5 5.4 %collective-permute-start.13 = (bf16[512,128]{1,0:T(8,128)(2,1)S(1)}, bf16[512,128]{1,0:T(8,128)(2,1)S(1)}, u32[]{:S(2)}, u32[]{:S(2)}) collective-permute-start(bf16[512,128]{1,0:T(8,128)(2,1)S(1)} %pad_maximum_fusion.3), channel_id=1, source_target_pairs={{0,1},{1,24},{2,3},{3,26},{4,5},{5,28},{6,7},{7,30},{8,9},{9,0},{1... | collective-permute-start | bytes 393224 | tf_op jit(solution)/shard_map/ppermute | solution.py:254
  51.8 12.6 %copy-start.11 = (bf16[256,172]{0,1:T(8,128)(2,1)S(1)}, bf16[256,172]{0,1:T(8,128)(2,1)}, u32[]{:S(2)}) copy-start(bf16[256,172]{0,1:T(8,128)(2,1)} %param.18) | copy-start | bytes 264196
  51.8 18.0 %copy-start.8 = (f32[172]{0:T(256)S(1)}, f32[172]{0:T(256)}, u32[]{:S(2)}) copy-start(f32[172]{0:T(256)} %param.19) | copy-start | bytes 2068
  56.4 10.0 %collective-permute-start.15 = (s16[272,256]{1,0:T(8,128)(2,1)S(1)}, s16[272,256]{1,0:T(8,128)(2,1)S(1)}, u32[]{:S(2)}, u32[]{:S(2)}) collective-permute-start(s16[272,256]{1,0:T(8,128)(2,1)S(1)} %get-tuple-element.31), channel_id=1, source_target_pairs={{0,8},{8,0},{16,24},{24,16},{1,9},{9,1},{17,25},{25,17},{2,10},{10... | collective-permute-start | bytes 417800 | tf_op jit(solution)/shard_map/ppermute | solution.py:243
  62.1 6.2 %collective-permute-start.16 = (s16[272,256]{1,0:T(8,128)(2,1)S(1)}, s16[272,256]{1,0:T(8,128)(2,1)S(1)}, u32[]{:S(2)}, u32[]{:S(2)}) collective-permute-start(s16[272,256]{1,0:T(8,128)(2,1)S(1)} %get-tuple-element.32), channel_id=1, source_target_pairs={{0,16},{8,24},{16,0},{24,8},{1,17},{9,25},{17,1},{25,9},{2,18},{10... | collective-permute-start | bytes 417800 | tf_op jit(solution)/shard_map/ppermute | solution.py:243
  62.7 7.1 %collective-permute-start.17 = (s16[272,256]{1,0:T(8,128)(2,1)S(1)}, s16[272,256]{1,0:T(8,128)(2,1)S(1)}, u32[]{:S(2)}, u32[]{:S(2)}) collective-permute-start(s16[272,256]{1,0:T(8,128)(2,1)S(1)} %get-tuple-element.33), channel_id=1, source_target_pairs={{0,24},{8,16},{16,8},{24,0},{1,25},{9,17},{17,9},{25,1},{2,26},{10... | collective-permute-start | bytes 417800 | tf_op jit(solution)/shard_map/ppermute | solution.py:243
  71.4 9.4 %collective-permute-start.18 = (bf16[304,256]{1,0:T(8,128)(2,1)S(1)}, bf16[304,256]{1,0:T(8,128)(2,1)S(1)}, u32[]{:S(2)}, u32[]{:S(2)}) collective-permute-start(bf16[304,256]{1,0:T(8,128)(2,1)S(1)} %get-tuple-element.38), channel_id=1, source_target_pairs={{0,8},{8,0},{16,24},{24,16},{1,9},{9,1},{17,25},{25,17},{2,10},{10... | collective-permute-start | bytes 466952 | tf_op jit(solution)/shard_map/ppermute | solution.py:243
  72.2 8.6 %collective-permute-start.19 = (bf16[304,256]{1,0:T(8,128)(2,1)S(1)}, bf16[304,256]{1,0:T(8,128)(2,1)S(1)}, u32[]{:S(2)}, u32[]{:S(2)}) collective-permute-start(bf16[304,256]{1,0:T(8,128)(2,1)S(1)} %get-tuple-element.39), channel_id=1, source_target_pairs={{0,16},{8,24},{16,0},{24,8},{1,17},{9,25},{17,1},{25,9},{2,18},{10... | collective-permute-start | bytes 466952 | tf_op jit(solution)/shard_map/ppermute | solution.py:243
  72.8 8.0 %collective-permute-start.20 = (bf16[304,256]{1,0:T(8,128)(2,1)S(1)}, bf16[304,256]{1,0:T(8,128)(2,1)S(1)}, u32[]{:S(2)}, u32[]{:S(2)}) collective-permute-start(bf16[304,256]{1,0:T(8,128)(2,1)S(1)} %get-tuple-element.40), channel_id=1, source_target_pairs={{0,24},{8,16},{16,8},{24,0},{1,25},{9,17},{17,9},{25,1},{2,26},{10... | collective-permute-start | bytes 466952 | tf_op jit(solution)/shard_map/ppermute | solution.py:243
  82.7 1.4 %collective-permute-start.21 = (f32[88,256]{1,0:T(8,128)S(1)}, f32[88,256]{1,0:T(8,128)S(1)}, u32[]{:S(2)}, u32[]{:S(2)}) collective-permute-start(f32[88,256]{1,0:T(8,128)S(1)} %pad_maximum_fusion.5), channel_id=1, source_target_pairs={{0,1},{1,0},{2,3},{3,2},{4,5},{5,4},{6,7},{7,6},{8,9},{9,8},{10,11... | collective-permute-start | bytes 270344 | tf_op jit(solution)/shard_map/ppermute | solution.py:257
  84.1 6.5 %collective-permute-start.24 = (bf16[88,256]{1,0:T(8,128)(2,1)S(1)}, bf16[88,256]{1,0:T(8,128)(2,1)S(1)}, u32[]{:S(2)}, u32[]{:S(2)}) collective-permute-start(bf16[88,256]{1,0:T(8,128)(2,1)S(1)} %fusion.13), channel_id=1, source_target_pairs={{0,6},{1,7},{2,4},{3,5},{4,2},{5,3},{6,0},{7,1},{8,14},{9,15},{10,... | collective-permute-start | bytes 135176 | tf_op jit(solution)/shard_map/ppermute | solution.py:257
  84.1 6.6 %collective-permute-start.23 = (bf16[88,256]{1,0:T(8,128)(2,1)S(1)}, bf16[88,256]{1,0:T(8,128)(2,1)S(1)}, u32[]{:S(2)}, u32[]{:S(2)}) collective-permute-start(bf16[88,256]{1,0:T(8,128)(2,1)S(1)} %fusion.13), channel_id=1, source_target_pairs={{0,4},{1,5},{2,6},{3,7},{4,0},{5,1},{6,2},{7,3},{8,12},{9,13},{10,... | collective-permute-start | bytes 135176 | tf_op jit(solution)/shard_map/ppermute | solution.py:257
  84.7 6.4 %collective-permute-start.22 = (bf16[88,256]{1,0:T(8,128)(2,1)S(1)}, bf16[88,256]{1,0:T(8,128)(2,1)S(1)}, u32[]{:S(2)}, u32[]{:S(2)}) collective-permute-start(bf16[88,256]{1,0:T(8,128)(2,1)S(1)} %fusion.13), channel_id=1, source_target_pairs={{0,2},{1,3},{2,0},{3,1},{4,6},{5,7},{6,4},{7,5},{8,10},{9,11},{10,... | collective-permute-start | bytes 135176 | tf_op jit(solution)/shard_map/ppermute | solution.py:257
  91.1 5.4 %collective-permute-start.27 = (bf16[88,256]{1,0:T(8,128)(2,1)S(1)}, bf16[88,256]{1,0:T(8,128)(2,1)S(1)}, u32[]{:S(2)}, u32[]{:S(2)}) collective-permute-start(bf16[88,256]{1,0:T(8,128)(2,1)S(1)} %add_convert_fusion), channel_id=1, source_target_pairs={{0,24},{8,16},{16,8},{24,0},{1,25},{9,17},{17,9},{25,1},{2,26},{10... | collective-permute-start | bytes 135176 | tf_op jit(solution)/shard_map/ppermute | solution.py:243
  91.9 4.5 %collective-permute-start.26 = (bf16[88,256]{1,0:T(8,128)(2,1)S(1)}, bf16[88,256]{1,0:T(8,128)(2,1)S(1)}, u32[]{:S(2)}, u32[]{:S(2)}) collective-permute-start(bf16[88,256]{1,0:T(8,128)(2,1)S(1)} %add_convert_fusion), channel_id=1, source_target_pairs={{0,16},{8,24},{16,0},{24,8},{1,17},{9,25},{17,1},{25,9},{2,18},{10... | collective-permute-start | bytes 135176 | tf_op jit(solution)/shard_map/ppermute | solution.py:243
  92.8 4.0 %collective-permute-start.25 = (bf16[88,256]{1,0:T(8,128)(2,1)S(1)}, bf16[88,256]{1,0:T(8,128)(2,1)S(1)}, u32[]{:S(2)}, u32[]{:S(2)}) collective-permute-start(bf16[88,256]{1,0:T(8,128)(2,1)S(1)} %add_convert_fusion), channel_id=1, source_target_pairs={{0,8},{8,0},{16,24},{24,16},{1,9},{9,1},{17,25},{25,17},{2,10},{10... | collective-permute-start | bytes 135176 | tf_op jit(solution)/shard_map/ppermute | solution.py:243
  96.9 1.5 %collective-permute-start.28 = (f32[160,256]{1,0:T(8,128)S(1)}, f32[160,256]{1,0:T(8,128)S(1)}, u32[]{:S(2)}, u32[]{:S(2)}) collective-permute-start(f32[160,256]{1,0:T(8,128)S(1)} %constant_dynamic-update-slice_fusion.7.total_ref), channel_id=1, source_target_pairs={{0,1},{1,0},{2,3},{3,2},{4,5},{5,4},{6,7},{7,6},{8,9},{9,8},{10,11... | collective-permute-start | bytes 491528 | tf_op jit(solution)/shard_map/ppermute | solution.py:257
  (11 other events, 35.0 us)

commit v10 on v9

--- a/solution.py
+++ b/solution.py
@@ -75,23 +75,6 @@
     own_rows = partial_ref.shape[0] // (len(coded_refs) + 1)
     for delta, coded_ref in enumerate(coded_refs, 1):
         coded_ref[...] = encode(partial_ref[delta * own_rows : (delta + 1) * own_rows, :])
-
-
-def pack_kernel(feature_hbm, id_hbm, bundle_ref, id_ref, sems):
-    own_rows, lanes = feature_hbm.shape
-    small = pltpu.make_async_copy(id_hbm, id_ref, sems.at[0])
-    large = pltpu.make_async_copy(feature_hbm, bundle_ref.at[pl.ds(0, own_rows)], sems.at[1])
-    small.start()
-    large.start()
-    small.wait()
-    ids = id_ref[...]
-    rows = ids.shape[0]
-    parts = [ids & 255, jnp.right_shift(ids, 8) & 255, jnp.right_shift(ids, 16)]
-    pad = bundle_ref.shape[0] - own_rows - 3 * rows
-    parts += [jnp.zeros((pad, lanes), jnp.int32)] if pad else []
-    digit_rows = jnp.concatenate(parts, axis=0).astype(jnp.float32).astype(jnp.bfloat16)
-    bundle_ref[own_rows:, :] = digit_rows
-    large.wait()
 
 
 def last_kernel(chunk, spot_ref, total_ref, other_ref, grad_in_ref, grad_out_ref):
@@ -163,13 +146,11 @@
     )(*spot, *values)
 
 
-def dense_kernel(
-    per_rep, tile_side, turn, spot_ref, place_ref, count_ref, tiles_ref, dense_ref
-):
-    section = pl.program_id(0)
+def put_tiles(own_rows, turn, section, spot_ref, place_ref, count_ref, tiles_ref, dense_ref):
+    edge = tiles_ref.shape[-1]
+    per_rep = own_rows // edge
+    tile_side = dense_ref.shape[0] // edge
     rep_index, source_rep = spot_ref[0], spot_ref[1 + section]
-    edge = tiles_ref.shape[-1]
-    dense_ref[...] = jnp.zeros_like(dense_ref)
 
     def put(slot, carried):
         place = place_ref[section, slot]
@@ -179,38 +160,83 @@
         column = ((column // per_rep) ^ source_rep) * per_rep + column % per_rep
         rows = pl.ds(pl.multiple_of(row * edge, edge), edge)
         columns = pl.ds(pl.multiple_of(column * edge, edge), edge)
-        tile = tiles_ref[0, slot]
         if turn:
-            dense_ref[columns, rows] = tile.T
+            dense_ref[columns, rows] = tiles_ref[slot].T
         else:
-            dense_ref[rows, columns] = tile
+            dense_ref[rows, columns] = tiles_ref[slot]
         return carried
 
     lax.fori_loop(0, count_ref[section], put, 0)
 
 
-def build_dense(tiles, place, count, spot, own_rows, group_rows, turn):
+def turned_kernel(own_rows, spot_ref, place_ref, count_ref, tiles_ref, dense_ref):
+    dense_ref[...] = jnp.zeros_like(dense_ref)
+    put_tiles(
+        own_rows, True, pl.program_id(0), spot_ref, place_ref, count_ref, tiles_ref.at[0], dense_ref
+    )
+
+
+def build_turned(tiles, place, count, spot, own_rows, group_rows):
     sections, slots, edge, _ = tiles.shape
-    body = functools.partial(dense_kernel, own_rows // edge, group_rows // edge, turn)
-    block = (group_rows, group_rows)
-    shape = (sections * group_rows, group_rows) if turn else (group_rows, sections * group_rows)
     return pl.pallas_call(
-        body,
+        functools.partial(turned_kernel, own_rows),
         grid_spec=pltpu.PrefetchScalarGridSpec(
             num_scalar_prefetch=3,
             grid=(sections,),
             in_specs=[pl.BlockSpec((1, slots, edge, edge), lambda p, *_: (p, 0, 0, 0))],
-            out_specs=pl.BlockSpec(block, lambda p, *_: (p, 0) if turn else (0, p)),
+            out_specs=pl.BlockSpec((group_rows, group_rows), lambda p, *_: (p, 0)),
         ),
-        out_shape=jax.ShapeDtypeStruct(shape, tiles.dtype),
+        out_shape=jax.ShapeDtypeStruct((sections * group_rows, group_rows), tiles.dtype),
         compiler_params=pltpu.CompilerParams(
             vmem_limit_bytes=4 * group_rows**2 + 8 * slots * edge**2 + (2 << 20)
         ),
-        cost_estimate=pl.CostEstimate(
-            flops=0, bytes_accessed=4 * sections * group_rows * group_rows, transcendentals=0
-        ),
-        name="dense_turned" if turn else "dense",
+        name="dense_turned",
     )(spot, place, count, tiles)
+
+
+def pack_kernel(
+    spot_ref, feature_hbm, id_hbm, place_hbm, count_hbm, tiles_hbm, bundle_ref, dense_hbm,
+    id_ref, place_ref, count_ref, tiles_ref, dense_ref, sems,
+):
+    own_rows, lanes = feature_hbm.shape
+    sections = tiles_hbm.shape[0]
+    group_rows = dense_hbm.shape[0]
+    ids_in = pltpu.make_async_copy(id_hbm, id_ref, sems.at[0])
+    features_in = pltpu.make_async_copy(
+        feature_hbm, bundle_ref.at[pl.ds(0, own_rows)], sems.at[1]
+    )
+    place_in = pltpu.make_async_copy(place_hbm, place_ref, sems.at[2])
+    count_in = pltpu.make_async_copy(count_hbm, count_ref, sems.at[3])
+    tiles_in = [
+        pltpu.make_async_copy(tiles_hbm.at[j], tiles_ref.at[j], sems.at[4 + j])
+        for j in range(sections)
+    ]
+    for copy in [ids_in, features_in, place_in, count_in] + tiles_in:
+        copy.start()
+    dense_ref[...] = jnp.zeros_like(dense_ref)
+    ids_in.wait()
+    ids = id_ref[...]
+    rows = ids.shape[0]
+    parts = [ids & 255, jnp.right_shift(ids, 8) & 255, jnp.right_shift(ids, 16)]
+    pad = bundle_ref.shape[0] - own_rows - 3 * rows
+    parts += [jnp.zeros((pad, lanes), jnp.int32)] if pad else []
+    digit_rows = jnp.concatenate(parts, axis=0).astype(jnp.float32).astype(jnp.bfloat16)
+    bundle_ref[own_rows:, :] = digit_rows
+    place_in.wait()
+    count_in.wait()
+    out = []
+    for j in range(sections):
+        tiles_in[j].wait()
+        part = dense_ref.at[:, pl.ds(j * group_rows, group_rows)]
+        put_tiles(own_rows, False, j, spot_ref, place_ref, count_ref, tiles_ref.at[j], part)
+        copy = pltpu.make_async_copy(
+            part, dense_hbm.at[:, pl.ds(j * group_rows, group_rows)], sems.at[4 + sections + j]
+        )
+        copy.start()
+        out.append(copy)
+    features_in.wait()
+    for copy in out:
+        copy.wait()
 
 
 def on_device(
@@ -300,24 +326,30 @@
     width = features.shape[2]
     digit_rows = 3 * own_rows // width
     stride = own_rows + digit_rows + -digit_rows % 16
+    tiles = tile_values[0, 0]
+    next_rep = lax.rem(rep_index + 1, reps)
+    where = jnp.where(member < jnp.arange(sections + 1) - 1, next_rep, rep_index)
     anywhere = pl.BlockSpec(memory_space=pl.ANY)
-    bundle = pl.pallas_call(
+    bundle, dense = pl.pallas_call(
         pack_kernel,
-        in_specs=[anywhere] * 2,
-        out_shape=jax.ShapeDtypeStruct((stride, width), bf16),
+        in_specs=[pl.BlockSpec(memory_space=pltpu.SMEM)] + [anywhere] * 5,
+        out_specs=[pl.BlockSpec(memory_space=pltpu.VMEM), anywhere],
+        out_shape=[
+            jax.ShapeDtypeStruct((stride, width), bf16),
+            jax.ShapeDtypeStruct((group_rows, sections * group_rows), bf16),
+        ],
         scratch_shapes=[
             pltpu.VMEM((own_rows // width, width), jnp.int32),
-            pltpu.SemaphoreType.DMA((2,)),
+            pltpu.SMEM(place.shape, jnp.int32),
+            pltpu.SMEM(count.shape, jnp.int32),
+            pltpu.VMEM(tiles.shape, bf16),
+            pltpu.VMEM((group_rows, sections * group_rows), bf16),
+            pltpu.SemaphoreType.DMA((4 + 2 * sections,)),
         ],
         compiler_params=pltpu.CompilerParams(vmem_limit_bytes=60 * 1024 * 1024),
         name="pack",
-    )(features[0], node_ids.reshape(-1, width))
+    )(where, features[0], node_ids.reshape(-1, width), place, count, tiles)
     arrived = to_pieces(bundle)
-    next_rep = lax.rem(rep_index + 1, reps)
-    where = jnp.where(member < jnp.arange(sections + 1) - 1, next_rep, rep_index)
-    layout = (where, own_rows, group_rows)
-    count, arrived[0] = lax.optimization_barrier((count, arrived[0]))
-    dense = build_dense(tile_values[0, 0], place, count, *layout, False)
     pieces = [
         half[d * stride : (d + 1) * stride] for half in to_all(arrived) for d in range(reps // 2)
     ]
@@ -336,7 +368,10 @@
     third = f32(4.0 / 3.0)
     pre_act = dot(z_columns, weight_in)
     dropped = (jnp.maximum(pre_act, 0.0) * (kept.astype(f32) * third)).astype(bf16)
+    dropped, z_again = lax.optimization_barrier((dropped, z_columns))
     second = dot(dense, dropped)
+    mask = jnp.where(dot(z_again, weight_in) > 0, kept, jnp.zeros_like(kept))
+    mask, ready = lax.optimization_barrier((mask, second))
     sent = simple_call(
         encode_kernel,
         [jax.ShapeDtypeStruct((own_rows + HEAD_ROWS, hidden_width), jnp.int16)] * (reps - 1),
@@ -355,14 +390,13 @@
         + [jax.ShapeDtypeStruct((own_rows + chunk, hidden_width), bf16)] * reps,
         "head",
         weight_out, class_bias[None], labels[0][:, None], train_mask[0][:, None],
-        second, *arrived,
+        ready, *arrived,
         spot=(spot,),
         scratch=[pltpu.VMEM((chunk * reps, hidden_width), f32)],
     )
     arrived = [swap(sent[d], d) for d in range(reps)]
-    count, z_again, kept, out_total = lax.optimization_barrier((count, z_columns, kept, out_total))
-    turned = build_dense(tile_values[0, 0], place, count, *layout, True)
-    mask = jnp.where(dot(z_again, weight_in) > 0, kept, jnp.zeros_like(kept))
+    count, out_total = lax.optimization_barrier((count, out_total))
+    turned = build_turned(tiles, place, count, where, own_rows, group_rows)
     grad_block = jnp.concatenate([part[:own_rows] for part in arrived], axis=0)
     for part in arrived[1:]:
         out_total = out_total + part[own_rows:].astype(f32)

time: 100 us -> 103 us (1.030)
  waiting for transfers between devices: 27.1 us -> 32.4 us
  local copies, waits for them, and re-layouts: 6.41 us -> 3.73 us
  Pallas kernels: 10.1 us -> 11.3 us
    ppermute x4, starting transfers between devices: 7.47 us -> 0.72 us  [to_section(): return lax.ppermute(block, ('rep', 'blk'), pairs)]
    ppermute x4, waiting for transfers between devices: 3.02 us -> 9.69 us  [to_section(): return lax.ppermute(block, ('rep', 'blk'), pairs)]
    unnamed x42 -> x30, local copies, waits for them, and re-layouts: 6.01 us -> 1.98 us
    ppermute x12, starting transfers between devices: 18.7 us -> 21.9 us  [swap(): return lax.ppermute(value, 'rep', [(r, r ^ delta) for r in range(reps)])]
    ppermute x8, starting transfers between devices: 14.2 us -> 17.2 us  [to_pieces(): pieces.append(lax.ppermute(value, ('rep', 'blk'), pairs))]
    ppermute x8, waiting for transfers between devices: 5.21 us -> 3.7 us  [to_pieces(): pieces.append(lax.ppermute(value, ('rep', 'blk'), pairs))]
    pallas_call x3 -> x2, Pallas kernels: 6.79 us -> 8.02 us  [the longest x1 4.89 us: on_device(): pl.pallas_call(pack_kernel, in_specs=[pl.BlockSpec(memory_space=pltpu.SME...]
    dot_general x4 -> x5, matrix products: 8.16 us -> 7.85 us  [dot(): return jnp.dot(left, right, preferred_element_type=jnp.float32)]
  transfers between devices with their start and end apart: 29 -> 29, of which waited for: 18 -> 17; matrix products, arithmetic and copies ran while one was open for 4% -> 6% of each run, Pallas kernels for 5% -> 3%
where the time goes in v10:
time: 103 us
  starting transfers between devices  44.5 us (43%)
  waiting for transfers between devices  32.4 us (31%)
  Pallas kernels  11.3 us (11%)
  matrix products  8.21 us (8%)
  local copies, waits for them, and re-layouts  3.73 us (4%)
  other arithmetic  1.78 us (2%)
  between operations  1.2 us (1%)
    ppermute x12, starting transfers between devices, swap(): return lax.ppermute(value, 'rep', [(r, r ^ delta) for r in range(reps)])  21.9 us
    ppermute x8, starting transfers between devices, to_pieces(): pieces.append(lax.ppermute(value, ('rep', 'blk'), pairs))  17.2 us
    ppermute x12, waiting for transfers between devices, swap(): return lax.ppermute(value, 'rep', [(r, r ^ delta) for r in range(reps)])  14.5 us
    ppermute x4, waiting for transfers between devices, to_section(): return lax.ppermute(block, ('rep', 'blk'), pairs)  9.69 us
    dot_general x5, matrix products, dot(): return jnp.dot(left, right, preferred_element_type=jnp.float32)  7.85 us
    pallas_call x1, Pallas kernels, on_device(): pl.pallas_call(pack_kernel, in_specs=[pl.BlockSpec(memory_space=pltpu.SME...  4.89 us
    ppermute x5, waiting for transfers between devices, exchange(): return lax.ppermute(value, 'blk', [(c, c ^ delta) for c in range(blks)])  4.58 us
    ppermute x5, starting transfers between devices, exchange(): return lax.ppermute(value, 'blk', [(c, c ^ delta) for c in range(blks)])  4.58 us
  transfers between devices with their start and end apart: 29, of which 17 were waited for; matrix products, arithmetic and copies ran while one was open for 6% of the time, Pallas kernels for 3%

profile of v10, /device:TPU:0, one launch (start us, length us, event | category | flops | bytes accessed | tf_op | source)
XLA Modules:
  0.0 103.1 jit_solution(14904194481609868153)
XLA Ops:
  1.1 4.9 %pack.1 = (bf16[272,128]{1,0:T(8,128)(2,1)}, bf16[1024,2048]{1,0:T(8,128)(2,1)}) custom-call(s32[3]{0:T(128)} %compare_select_fusion.spot_ref, bf16[256,128]{1,0:T(8,128)(2,1)} %bitcast.48, s32[2,128]{1,0:T(2,128)} %bitcast.49, s32[2,16]{1,0:T(2,128)} %bitcast.43, s32[2]{0:T(128)} %bitcast.45, bf16[2,16,128,128]{3,2,1,0:T(8,128)(2,1)} %bitcast.40), custom_call_target="tpu_custom_call" | custom-call | tf_op jit(solution)/shard_map/pack/pallas_call | solution.py:333
  6.0 1.5 %collective-permute-start = (bf16[272,128]{1,0:T(8,128)(2,1)}, bf16[272,128]{1,0:T(8,128)(2,1)S(1)}, u32[]{:S(2)}, u32[]{:S(2)}) collective-permute-start(bf16[272,128]{1,0:T(8,128)(2,1)} %get-tuple-element.29), channel_id=1, source_target_pairs={{0,0},{1,1},{2,2},{3,3},{4,4},{5,5},{6,6},{7,7},{8,10},{9,11},{10,... | collective-permute-start | bytes 208904 | tf_op jit(solution)/shard_map/ppermute | solution.py:293
  7.6 5.6 %collective-permute-start.1 = (bf16[272,128]{1,0:T(8,128)(2,1)}, bf16[272,128]{1,0:T(8,128)(2,1)S(1)}, u32[]{:S(2)}, u32[]{:S(2)}) collective-permute-start(bf16[272,128]{1,0:T(8,128)(2,1)} %get-tuple-element.29), channel_id=1, source_target_pairs={{0,10},{1,11},{2,12},{3,13},{4,14},{5,15},{6,8},{7,9},{8,0},{9,1},... | collective-permute-start | bytes 208904 | tf_op jit(solution)/shard_map/ppermute | solution.py:293
  13.1 1.4 %collective-permute-start.2 = (bf16[272,128]{1,0:T(8,128)(2,1)}, bf16[272,128]{1,0:T(8,128)(2,1)S(1)}, u32[]{:S(2)}, u32[]{:S(2)}) collective-permute-start(bf16[272,128]{1,0:T(8,128)(2,1)} %get-tuple-element.29), channel_id=1, source_target_pairs={{0,20},{1,21},{2,22},{3,23},{4,16},{5,17},{6,18},{7,19},{8,30},{9,... | collective-permute-start | bytes 208904 | tf_op jit(solution)/shard_map/ppermute | solution.py:293
  14.6 3.0 %collective-permute-start.3 = (bf16[272,128]{1,0:T(8,128)(2,1)}, bf16[272,128]{1,0:T(8,128)(2,1)S(1)}, u32[]{:S(2)}, u32[]{:S(2)}) collective-permute-start(bf16[272,128]{1,0:T(8,128)(2,1)} %get-tuple-element.29), channel_id=1, source_target_pairs={{0,30},{1,31},{2,24},{3,25},{4,26},{5,27},{6,28},{7,29},{8,20},{9,... | collective-permute-start | bytes 208904 | tf_op jit(solution)/shard_map/ppermute | solution.py:293
  21.0 3.7 %collective-permute-done.4 = bf16[544,128]{1,0:T(8,128)(2,1)S(1)} collective-permute-done((bf16[544,128]{1,0:T(8,128)(2,1)S(1)}, bf16[544,128]{1,0:T(8,128)(2,1)S(1)}, u32[]{:S(2)}, u32[]{:S(2)}) %collective-permute-start.4) | collective-permute-done | bytes 139296 | tf_op jit(solution)/shard_map/ppermute | solution.py:280
  24.8 1.6 %collective-permute-done.5 = bf16[544,128]{1,0:T(8,128)(2,1)S(1)} collective-permute-done((bf16[544,128]{1,0:T(8,128)(2,1)S(1)}, bf16[544,128]{1,0:T(8,128)(2,1)S(1)}, u32[]{:S(2)}, u32[]{:S(2)}) %collective-permute-start.5) | collective-permute-done | bytes 139296 | tf_op jit(solution)/shard_map/ppermute | solution.py:280
  26.5 3.4 %fusion.13 = f32[1024,128]{1,0:T(8,128)S(1)} fusion(bf16[1024,2048]{1,0:T(8,128)(2,1)} %get-tuple-element.30, bf16[2048,128]{1,0:T(8,128)(2,1)S(1)} %slice_dynamic-update-slice_fusion), kind=kOutput, calls=%fused_computation.63 | convolution fusion | flops 536870912 | bytes 5242880 | tf_op jit(solution)/shard_map/dot_general | solution.py:32
  30.0 5.3 %collective-permute-start.6 = (f32[256,128]{1,0:T(8,128)S(1)}, f32[256,128]{1,0:T(8,128)S(1)}, u32[]{:S(2)}, u32[]{:S(2)}) collective-permute-start(f32[256,128]{1,0:T(8,128)S(1)} %get-tuple-element.61), channel_id=1, source_target_pairs={{0,8},{8,0},{16,24},{24,16},{1,9},{9,1},{17,25},{25,17},{2,10},{10... | collective-permute-start | bytes 393224 | tf_op jit(solution)/shard_map/ppermute | solution.py:269
  35.3 1.5 %collective-permute-start.8 = (f32[256,128]{1,0:T(8,128)S(1)}, f32[256,128]{1,0:T(8,128)S(1)}, u32[]{:S(2)}, u32[]{:S(2)}) collective-permute-start(f32[256,128]{1,0:T(8,128)S(1)} %get-tuple-element.62), channel_id=1, source_target_pairs={{0,24},{8,16},{16,8},{24,0},{1,25},{9,17},{17,9},{25,1},{2,26},{10... | collective-permute-start | bytes 393224 | tf_op jit(solution)/shard_map/ppermute | solution.py:269
  36.9 1.8 %collective-permute-done.6 = f32[256,128]{1,0:T(8,128)S(1)} collective-permute-done((f32[256,128]{1,0:T(8,128)S(1)}, f32[256,128]{1,0:T(8,128)S(1)}, u32[]{:S(2)}, u32[]{:S(2)}) %collective-permute-start.6) | collective-permute-done | bytes 131104 | tf_op jit(solution)/shard_map/ppermute | solution.py:269
  38.7 3.3 %collective-permute-done.7 = f32[256,128]{1,0:T(8,128)S(1)} collective-permute-done((f32[256,128]{1,0:T(8,128)S(1)}, f32[256,128]{1,0:T(8,128)S(1)}, u32[]{:S(2)}, u32[]{:S(2)}) %collective-permute-start.7) | collective-permute-done | bytes 131104 | tf_op jit(solution)/shard_map/ppermute | solution.py:269
  42.1 4.8 %collective-permute-start.12 = (bf16[256,128]{1,0:T(8,128)(2,1)S(1)}, bf16[256,128]{1,0:T(8,128)(2,1)S(1)}, u32[]{:S(2)}, u32[]{:S(2)}) collective-permute-start(bf16[256,128]{1,0:T(8,128)(2,1)S(1)} %fusion.10), channel_id=1, source_target_pairs={{0,30},{1,31},{2,24},{3,25},{4,26},{5,27},{6,28},{7,29},{8,20},{9,... | collective-permute-start | bytes 196616 | tf_op jit(solution)/shard_map/ppermute | solution.py:293
  48.9 3.5 %collective-permute-done.10 = bf16[256,128]{1,0:T(8,128)(2,1)S(1)} collective-permute-done((bf16[256,128]{1,0:T(8,128)(2,1)S(1)}, bf16[256,128]{1,0:T(8,128)(2,1)S(1)}, u32[]{:S(2)}, u32[]{:S(2)}) %collective-permute-start.10) | collective-permute-done | bytes 65568 | tf_op jit(solution)/shard_map/ppermute | solution.py:293
  52.6 4.3 %collective-permute-done.13 = bf16[512,128]{1,0:T(8,128)(2,1)S(1)} collective-permute-done((bf16[512,128]{1,0:T(8,128)(2,1)S(1)}, bf16[512,128]{1,0:T(8,128)(2,1)S(1)}, u32[]{:S(2)}, u32[]{:S(2)}) %collective-permute-start.13) | collective-permute-done | bytes 131104 | tf_op jit(solution)/shard_map/ppermute | solution.py:280
  57.5 1.3 %fusion.14.partial_ref.own_ref = f32[1024,256]{1,0:T(8,128)S(1)} fusion(bf16[1024,2048]{1,0:T(8,128)(2,1)S(1)} %copy-done.6, bf16[2048,256]{1,0:T(8,128)(2,1)S(1)} %fusion.1), kind=kOutput, calls=%fused_computation.64 | convolution fusion | flops 1073741824 | bytes 6291456 | tf_op jit(solution)/shard_map/dot_general | solution.py:32
  59.2 6.3 %collective-permute-start.15 = (s16[272,256]{1,0:T(8,128)(2,1)S(1)}, s16[272,256]{1,0:T(8,128)(2,1)S(1)}, u32[]{:S(2)}, u32[]{:S(2)}) collective-permute-start(s16[272,256]{1,0:T(8,128)(2,1)S(1)} %get-tuple-element.36), channel_id=1, source_target_pairs={{0,8},{8,0},{16,24},{24,16},{1,9},{9,1},{17,25},{25,17},{2,10},{10... | collective-permute-start | bytes 417800 | tf_op jit(solution)/shard_map/ppermute | solution.py:269
  65.5 1.6 %collective-permute-start.17 = (s16[272,256]{1,0:T(8,128)(2,1)S(1)}, s16[272,256]{1,0:T(8,128)(2,1)S(1)}, u32[]{:S(2)}, u32[]{:S(2)}) collective-permute-start(s16[272,256]{1,0:T(8,128)(2,1)S(1)} %get-tuple-element.38), channel_id=1, source_target_pairs={{0,24},{8,16},{16,8},{24,0},{1,25},{9,17},{17,9},{25,1},{2,26},{10... | collective-permute-start | bytes 417800 | tf_op jit(solution)/shard_map/ppermute | solution.py:269
  67.1 1.4 %fusion.3 = bf16[2048,256]{1,0:T(8,128)(2,1)} fusion(bf16[2048,256]{1,0:T(8,128)(2,1)S(1)} %fusion.7, bf16[2048,128]{1,0:T(8,128)(2,1)S(1)} %constant_dynamic-update-slice_fusion.1, bf16[128,256]{1,0:T(8,128)(2,1)S(1)} %copy-done), kind=kOutput, calls=%fused_computation.8 | convolution fusion | flops 135266304 | bytes 2686976 | tf_op jit(solution)/shard_map/dot_general | solution.py:32
  69.1 3.9 %collective-permute-done.16.refs_1_ = s16[272,256]{1,0:T(8,128)(2,1)S(1)} collective-permute-done((s16[272,256]{1,0:T(8,128)(2,1)S(1)}, s16[272,256]{1,0:T(8,128)(2,1)S(1)}, u32[]{:S(2)}, u32[]{:S(2)}) %collective-permute-start.16) | collective-permute-done | bytes 139296 | tf_op jit(solution)/shard_map/ppermute | solution.py:269
  73.0 1.6 %head.1 = (f32[256,172]{1,0:T(8,128)S(1)}, f32[48,256]{1,0:T(8,128)S(1)}, bf16[304,256]{1,0:T(8,128)(2,1)S(1)}, bf16[304,256]{1,0:T(8,128)(2,1)S(1)}, bf16[304,2...) custom-call(s32[2]{0:T(128)S(1)} %pad_add_fusion.spot_ref, bf16[256,172]{1,0:T(8,128)(2,1)S(1)} %copy.15.weight_ref, ...), custom_call_target="tpu_custom_call" | custom-call | tf_op jit(solution)/shard_map/head/pallas_call | solution.py:139
  75.7 2.5 %collective-permute-start.20 = (bf16[304,256]{1,0:T(8,128)(2,1)S(1)}, bf16[304,256]{1,0:T(8,128)(2,1)S(1)}, u32[]{:S(2)}, u32[]{:S(2)}) collective-permute-start(bf16[304,256]{1,0:T(8,128)(2,1)S(1)} %get-tuple-element.45), channel_id=1, source_target_pairs={{0,24},{8,16},{16,8},{24,0},{1,25},{9,17},{17,9},{25,1},{2,26},{10... | collective-permute-start | bytes 466952 | tf_op jit(solution)/shard_map/ppermute | solution.py:269
  78.3 3.1 %dense_turned.1 = bf16[2048,1024]{1,0:T(8,128)(2,1)S(1)} custom-call(s32[3]{0:T(128)S(1)} %copy-done.2, s32[2,16]{1,0:T(2,128)S(1)} %bitcast.44, s32[2]{0:T(128)S(1)} %bitcast.46, bf16[2,16,128,128]{3,2,1,0:T(8,128)(2,1)S(1)} %bitcast.41), custom_call_target="tpu_custom_call" | custom-call | tf_op jit(solution)/shard_map/dense_turned/pallas_call | solution.py:181
  82.2 1.3 %fusion.2 = bf16[2048,256]{1,0:T(8,128)(2,1)S(1)} fusion(bf16[2048,1024]{1,0:T(8,128)(2,1)S(1)} %dense_turned.1, bf16[1024,256]{1,0:T(8,128)(2,1)S(1)} %pad_maximum_fusion, bf16[2048,256]{1,0:T(8,128)(2,1)S(1)} %copy-done.7), kind=kOutput, calls=%fused_computation.6 | convolution fusion | flops 1075838976 | bytes 6815744 | tf_op jit(solution)/shard_map/dot_general | solution.py:32
  84.0 1.3 %collective-permute-done.21 = f32[88,256]{1,0:T(8,128)S(1)} collective-permute-done((f32[88,256]{1,0:T(8,128)S(1)}, f32[88,256]{1,0:T(8,128)S(1)}, u32[]{:S(2)}, u32[]{:S(2)}) %collective-permute-start.21) | collective-permute-done | bytes 90144 | tf_op jit(solution)/shard_map/ppermute | solution.py:283
  85.5 4.3 %collective-permute-start.24 = (bf16[88,256]{1,0:T(8,128)(2,1)S(1)}, bf16[88,256]{1,0:T(8,128)(2,1)S(1)}, u32[]{:S(2)}, u32[]{:S(2)}) collective-permute-start(bf16[88,256]{1,0:T(8,128)(2,1)S(1)} %fusion.11), channel_id=1, source_target_pairs={{0,6},{1,7},{2,4},{3,5},{4,2},{5,3},{6,0},{7,1},{8,14},{9,15},{10,... | collective-permute-start | bytes 135176 | tf_op jit(solution)/shard_map/ppermute | solution.py:283
  89.9 2.6 %collective-permute-done.23 = bf16[88,256]{1,0:T(8,128)(2,1)S(1)} collective-permute-done((bf16[88,256]{1,0:T(8,128)(2,1)S(1)}, bf16[88,256]{1,0:T(8,128)(2,1)S(1)}, u32[]{:S(2)}, u32[]{:S(2)}) %collective-permute-start.23) | collective-permute-done | bytes 45088 | tf_op jit(solution)/shard_map/ppermute | solution.py:283
  92.5 1.6 %collective-permute-start.25 = (bf16[88,256]{1,0:T(8,128)(2,1)S(1)}, bf16[88,256]{1,0:T(8,128)(2,1)S(1)}, u32[]{:S(2)}, u32[]{:S(2)}) collective-permute-start(bf16[88,256]{1,0:T(8,128)(2,1)S(1)} %add_convert_fusion), channel_id=1, source_target_pairs={{0,8},{8,0},{16,24},{24,16},{1,9},{9,1},{17,25},{25,17},{2,10},{10... | collective-permute-start | bytes 135176 | tf_op jit(solution)/shard_map/ppermute | solution.py:269
  94.1 1.2 %collective-permute-start.26 = (bf16[88,256]{1,0:T(8,128)(2,1)S(1)}, bf16[88,256]{1,0:T(8,128)(2,1)S(1)}, u32[]{:S(2)}, u32[]{:S(2)}) collective-permute-start(bf16[88,256]{1,0:T(8,128)(2,1)S(1)} %add_convert_fusion), channel_id=1, source_target_pairs={{0,16},{8,24},{16,0},{24,8},{1,17},{9,25},{17,1},{25,9},{2,18},{10... | collective-permute-start | bytes 135176 | tf_op jit(solution)/shard_map/ppermute | solution.py:269
  97.0 1.3 %collective-permute-done.26 = bf16[88,256]{1,0:T(8,128)(2,1)S(1)} collective-permute-done((bf16[88,256]{1,0:T(8,128)(2,1)S(1)}, bf16[88,256]{1,0:T(8,128)(2,1)S(1)}, u32[]{:S(2)}, u32[]{:S(2)}) %collective-permute-start.26) | collective-permute-done | bytes 45088 | tf_op jit(solution)/shard_map/ppermute | solution.py:269
  98.2 2.1 %collective-permute-done.27 = bf16[88,256]{1,0:T(8,128)(2,1)S(1)} collective-permute-done((bf16[88,256]{1,0:T(8,128)(2,1)S(1)}, bf16[88,256]{1,0:T(8,128)(2,1)S(1)}, u32[]{:S(2)}, u32[]{:S(2)}) %collective-permute-start.27) | collective-permute-done | bytes 45088 | tf_op jit(solution)/shard_map/ppermute | solution.py:269
  101.9 1.3 %last.1 = (f32[128,256]{1,0:T(8,128)}, f32[172,256]{1,0:T(8,128)}) custom-call(s32[2]{0:T(128)S(1)} %pad_add_fusion.spot_ref, f32[160,256]{1,0:T(8,128)S(1)} %constant_dynamic-update-slice_fusion.7.total_ref, f32[160,256]{1,0:T(8,128)S(1)} %collective-permute-done.28.other_ref), custom_call_target="tpu_custom_call" | custom-call | tf_op jit(solution)/shard_map/last/pallas_call | solution.py:139
  (107 shorter events, 13.4 us)
Async XLA Ops:
  0.6 56.4 %copy-start = (bf16[128,256]{1,0:T(8,128)(2,1)S(1)}, bf16[128,256]{1,0:T(8,128)(2,1)}, u32[]{:S(2)}) copy-start(bf16[128,256]{1,0:T(8,128)(2,1)} %param.17) | copy-start | bytes 196612
  6.0 14.2 %collective-permute-start = (bf16[272,128]{1,0:T(8,128)(2,1)}, bf16[272,128]{1,0:T(8,128)(2,1)S(1)}, u32[]{:S(2)}, u32[]{:S(2)}) collective-permute-start(bf16[272,128]{1,0:T(8,128)(2,1)} %get-tuple-element.29), channel_id=1, source_target_pairs={{0,0},{1,1},{2,2},{3,3},{4,4},{5,5},{6,6},{7,7},{8,10},{9,11},{10,... | collective-permute-start | bytes 208904 | tf_op jit(solution)/shard_map/ppermute | solution.py:293
  7.6 12.7 %collective-permute-start.1 = (bf16[272,128]{1,0:T(8,128)(2,1)}, bf16[272,128]{1,0:T(8,128)(2,1)S(1)}, u32[]{:S(2)}, u32[]{:S(2)}) collective-permute-start(bf16[272,128]{1,0:T(8,128)(2,1)} %get-tuple-element.29), channel_id=1, source_target_pairs={{0,10},{1,11},{2,12},{3,13},{4,14},{5,15},{6,8},{7,9},{8,0},{9,1},... | collective-permute-start | bytes 208904 | tf_op jit(solution)/shard_map/ppermute | solution.py:293
  13.1 7.2 %collective-permute-start.2 = (bf16[272,128]{1,0:T(8,128)(2,1)}, bf16[272,128]{1,0:T(8,128)(2,1)S(1)}, u32[]{:S(2)}, u32[]{:S(2)}) collective-permute-start(bf16[272,128]{1,0:T(8,128)(2,1)} %get-tuple-element.29), channel_id=1, source_target_pairs={{0,20},{1,21},{2,22},{3,23},{4,16},{5,17},{6,18},{7,19},{8,30},{9,... | collective-permute-start | bytes 208904 | tf_op jit(solution)/shard_map/ppermute | solution.py:293
  14.6 5.8 %collective-permute-start.3 = (bf16[272,128]{1,0:T(8,128)(2,1)}, bf16[272,128]{1,0:T(8,128)(2,1)S(1)}, u32[]{:S(2)}, u32[]{:S(2)}) collective-permute-start(bf16[272,128]{1,0:T(8,128)(2,1)} %get-tuple-element.29), channel_id=1, source_target_pairs={{0,30},{1,31},{2,24},{3,25},{4,26},{5,27},{6,28},{7,29},{8,20},{9,... | collective-permute-start | bytes 208904 | tf_op jit(solution)/shard_map/ppermute | solution.py:293
  20.3 4.5 %collective-permute-start.4 = (bf16[544,128]{1,0:T(8,128)(2,1)S(1)}, bf16[544,128]{1,0:T(8,128)(2,1)S(1)}, u32[]{:S(2)}, u32[]{:S(2)}) collective-permute-start(bf16[544,128]{1,0:T(8,128)(2,1)S(1)} %pad_maximum_fusion.1), channel_id=1, source_target_pairs={{0,1},{1,24},{2,3},{3,26},{4,5},{5,28},{6,7},{7,30},{8,9},{9,0},{1... | collective-permute-start | bytes 417800 | tf_op jit(solution)/shard_map/ppermute | solution.py:280
  20.4 6.1 %collective-permute-start.5 = (bf16[544,128]{1,0:T(8,128)(2,1)S(1)}, bf16[544,128]{1,0:T(8,128)(2,1)S(1)}, u32[]{:S(2)}, u32[]{:S(2)}) collective-permute-start(bf16[544,128]{1,0:T(8,128)(2,1)S(1)} %pad_maximum_fusion.2), channel_id=1, source_target_pairs={{0,1},{1,24},{2,3},{3,26},{4,5},{5,28},{6,7},{7,30},{8,9},{9,0},{1... | collective-permute-start | bytes 417800 | tf_op jit(solution)/shard_map/ppermute | solution.py:280
  30.0 8.7 %collective-permute-start.6 = (f32[256,128]{1,0:T(8,128)S(1)}, f32[256,128]{1,0:T(8,128)S(1)}, u32[]{:S(2)}, u32[]{:S(2)}) collective-permute-start(f32[256,128]{1,0:T(8,128)S(1)} %get-tuple-element.61), channel_id=1, source_target_pairs={{0,8},{8,0},{16,24},{24,16},{1,9},{9,1},{17,25},{25,17},{2,10},{10... | collective-permute-start | bytes 393224 | tf_op jit(solution)/shard_map/ppermute | solution.py:269
  35.3 6.7 %collective-permute-start.7 = (f32[256,128]{1,0:T(8,128)S(1)}, f32[256,128]{1,0:T(8,128)S(1)}, u32[]{:S(2)}, u32[]{:S(2)}) collective-permute-start(f32[256,128]{1,0:T(8,128)S(1)} %get-tuple-element.63), channel_id=1, source_target_pairs={{0,16},{8,24},{16,0},{24,8},{1,17},{9,25},{17,1},{25,9},{2,18},{10... | collective-permute-start | bytes 393224 | tf_op jit(solution)/shard_map/ppermute | solution.py:269
  35.3 6.7 %collective-permute-start.8 = (f32[256,128]{1,0:T(8,128)S(1)}, f32[256,128]{1,0:T(8,128)S(1)}, u32[]{:S(2)}, u32[]{:S(2)}) collective-permute-start(f32[256,128]{1,0:T(8,128)S(1)} %get-tuple-element.62), channel_id=1, source_target_pairs={{0,24},{8,16},{16,8},{24,0},{1,25},{9,17},{17,9},{25,1},{2,26},{10... | collective-permute-start | bytes 393224 | tf_op jit(solution)/shard_map/ppermute | solution.py:269
  42.1 6.7 %collective-permute-start.11 = (bf16[256,128]{1,0:T(8,128)(2,1)S(1)}, bf16[256,128]{1,0:T(8,128)(2,1)S(1)}, u32[]{:S(2)}, u32[]{:S(2)}) collective-permute-start(bf16[256,128]{1,0:T(8,128)(2,1)S(1)} %fusion.10), channel_id=1, source_target_pairs={{0,20},{1,21},{2,22},{3,23},{4,16},{5,17},{6,18},{7,19},{8,30},{9,... | collective-permute-start | bytes 196616 | tf_op jit(solution)/shard_map/ppermute | solution.py:293
  42.1 6.8 %collective-permute-start.12 = (bf16[256,128]{1,0:T(8,128)(2,1)S(1)}, bf16[256,128]{1,0:T(8,128)(2,1)S(1)}, u32[]{:S(2)}, u32[]{:S(2)}) collective-permute-start(bf16[256,128]{1,0:T(8,128)(2,1)S(1)} %fusion.10), channel_id=1, source_target_pairs={{0,30},{1,31},{2,24},{3,25},{4,26},{5,27},{6,28},{7,29},{8,20},{9,... | collective-permute-start | bytes 196616 | tf_op jit(solution)/shard_map/ppermute | solution.py:293
  47.9 4.6 %collective-permute-start.10 = (bf16[256,128]{1,0:T(8,128)(2,1)S(1)}, bf16[256,128]{1,0:T(8,128)(2,1)S(1)}, u32[]{:S(2)}, u32[]{:S(2)}) collective-permute-start(bf16[256,128]{1,0:T(8,128)(2,1)S(1)} %fusion.10), channel_id=1, source_target_pairs={{0,10},{1,11},{2,12},{3,13},{4,14},{5,15},{6,8},{7,9},{8,0},{9,1},... | collective-permute-start | bytes 196616 | tf_op jit(solution)/shard_map/ppermute | solution.py:293
  47.9 4.6 %collective-permute-start.9 = (bf16[256,128]{1,0:T(8,128)(2,1)S(1)}, bf16[256,128]{1,0:T(8,128)(2,1)S(1)}, u32[]{:S(2)}, u32[]{:S(2)}) collective-permute-start(bf16[256,128]{1,0:T(8,128)(2,1)S(1)} %fusion.10), channel_id=1, source_target_pairs={{0,0},{1,1},{2,2},{3,3},{4,4},{5,5},{6,6},{7,7},{8,10},{9,11},{10,... | collective-permute-start | bytes 196616 | tf_op jit(solution)/shard_map/ppermute | solution.py:293
  48.9 8.1 %collective-permute-start.14 = (bf16[512,128]{1,0:T(8,128)(2,1)S(1)}, bf16[512,128]{1,0:T(8,128)(2,1)S(1)}, u32[]{:S(2)}, u32[]{:S(2)}) collective-permute-start(bf16[512,128]{1,0:T(8,128)(2,1)S(1)} %pad_maximum_fusion.4), channel_id=1, source_target_pairs={{0,1},{1,24},{2,3},{3,26},{4,5},{5,28},{6,7},{7,30},{8,9},{9,0},{1... | collective-permute-start | bytes 393224 | tf_op jit(solution)/shard_map/ppermute | solution.py:280
  52.5 4.4 %collective-permute-start.13 = (bf16[512,128]{1,0:T(8,128)(2,1)S(1)}, bf16[512,128]{1,0:T(8,128)(2,1)S(1)}, u32[]{:S(2)}, u32[]{:S(2)}) collective-permute-start(bf16[512,128]{1,0:T(8,128)(2,1)S(1)} %pad_maximum_fusion.3), channel_id=1, source_target_pairs={{0,1},{1,24},{2,3},{3,26},{4,5},{5,28},{6,7},{7,30},{8,9},{9,0},{1... | collective-permute-start | bytes 393224 | tf_op jit(solution)/shard_map/ppermute | solution.py:280
  58.7 14.3 %copy-start.5 = (f32[172]{0:T(256)S(1)}, f32[172]{0:T(256)}, u32[]{:S(2)}) copy-start(f32[172]{0:T(256)} %param.19) | copy-start | bytes 2068
  59.2 10.0 %collective-permute-start.15 = (s16[272,256]{1,0:T(8,128)(2,1)S(1)}, s16[272,256]{1,0:T(8,128)(2,1)S(1)}, u32[]{:S(2)}, u32[]{:S(2)}) collective-permute-start(s16[272,256]{1,0:T(8,128)(2,1)S(1)} %get-tuple-element.36), channel_id=1, source_target_pairs={{0,8},{8,0},{16,24},{24,16},{1,9},{9,1},{17,25},{25,17},{2,10},{10... | collective-permute-start | bytes 417800 | tf_op jit(solution)/shard_map/ppermute | solution.py:269
  65.5 7.5 %collective-permute-start.16 = (s16[272,256]{1,0:T(8,128)(2,1)S(1)}, s16[272,256]{1,0:T(8,128)(2,1)S(1)}, u32[]{:S(2)}, u32[]{:S(2)}) collective-permute-start(s16[272,256]{1,0:T(8,128)(2,1)S(1)} %get-tuple-element.37), channel_id=1, source_target_pairs={{0,16},{8,24},{16,0},{24,8},{1,17},{9,25},{17,1},{25,9},{2,18},{10... | collective-permute-start | bytes 417800 | tf_op jit(solution)/shard_map/ppermute | solution.py:269
  65.5 12.7 %copy-start.4 = (s32[1,1,2]{2,1,0:T(1,128)S(1)}, s32[1,1,2]{2,1,0:T(1,128)}, u32[]{:S(2)}) copy-start(s32[1,1,2]{2,1,0:T(1,128)} %param.16) | copy-start | bytes 28
  65.5 7.5 %collective-permute-start.17 = (s16[272,256]{1,0:T(8,128)(2,1)S(1)}, s16[272,256]{1,0:T(8,128)(2,1)S(1)}, u32[]{:S(2)}, u32[]{:S(2)}) collective-permute-start(s16[272,256]{1,0:T(8,128)(2,1)S(1)} %get-tuple-element.38), channel_id=1, source_target_pairs={{0,24},{8,16},{16,8},{24,0},{1,25},{9,17},{17,9},{25,1},{2,26},{10... | collective-permute-start | bytes 417800 | tf_op jit(solution)/shard_map/ppermute | solution.py:269
  74.7 6.8 %collective-permute-start.18 = (bf16[304,256]{1,0:T(8,128)(2,1)S(1)}, bf16[304,256]{1,0:T(8,128)(2,1)S(1)}, u32[]{:S(2)}, u32[]{:S(2)}) collective-permute-start(bf16[304,256]{1,0:T(8,128)(2,1)S(1)} %get-tuple-element.43), channel_id=1, source_target_pairs={{0,8},{8,0},{16,24},{24,16},{1,9},{9,1},{17,25},{25,17},{2,10},{10... | collective-permute-start | bytes 466952 | tf_op jit(solution)/shard_map/ppermute | solution.py:269
  75.2 6.9 %collective-permute-start.19 = (bf16[304,256]{1,0:T(8,128)(2,1)S(1)}, bf16[304,256]{1,0:T(8,128)(2,1)S(1)}, u32[]{:S(2)}, u32[]{:S(2)}) collective-permute-start(bf16[304,256]{1,0:T(8,128)(2,1)S(1)} %get-tuple-element.44), channel_id=1, source_target_pairs={{0,16},{8,24},{16,0},{24,8},{1,17},{9,25},{17,1},{25,9},{2,18},{10... | collective-permute-start | bytes 466952 | tf_op jit(solution)/shard_map/ppermute | solution.py:269
  75.7 6.3 %collective-permute-start.20 = (bf16[304,256]{1,0:T(8,128)(2,1)S(1)}, bf16[304,256]{1,0:T(8,128)(2,1)S(1)}, u32[]{:S(2)}, u32[]{:S(2)}) collective-permute-start(bf16[304,256]{1,0:T(8,128)(2,1)S(1)} %get-tuple-element.45), channel_id=1, source_target_pairs={{0,24},{8,16},{16,8},{24,0},{1,25},{9,17},{17,9},{25,1},{2,26},{10... | collective-permute-start | bytes 466952 | tf_op jit(solution)/shard_map/ppermute | solution.py:269
  83.9 1.4 %collective-permute-start.21 = (f32[88,256]{1,0:T(8,128)S(1)}, f32[88,256]{1,0:T(8,128)S(1)}, u32[]{:S(2)}, u32[]{:S(2)}) collective-permute-start(f32[88,256]{1,0:T(8,128)S(1)} %pad_maximum_fusion.5), channel_id=1, source_target_pairs={{0,1},{1,0},{2,3},{3,2},{4,5},{5,4},{6,7},{7,6},{8,9},{9,8},{10,11... | collective-permute-start | bytes 270344 | tf_op jit(solution)/shard_map/ppermute | solution.py:283
  85.3 4.6 %collective-permute-start.22 = (bf16[88,256]{1,0:T(8,128)(2,1)S(1)}, bf16[88,256]{1,0:T(8,128)(2,1)S(1)}, u32[]{:S(2)}, u32[]{:S(2)}) collective-permute-start(bf16[88,256]{1,0:T(8,128)(2,1)S(1)} %fusion.11), channel_id=1, source_target_pairs={{0,2},{1,3},{2,0},{3,1},{4,6},{5,7},{6,4},{7,5},{8,10},{9,11},{10,... | collective-permute-start | bytes 135176 | tf_op jit(solution)/shard_map/ppermute | solution.py:283
  85.4 7.1 %collective-permute-start.23 = (bf16[88,256]{1,0:T(8,128)(2,1)S(1)}, bf16[88,256]{1,0:T(8,128)(2,1)S(1)}, u32[]{:S(2)}, u32[]{:S(2)}) collective-permute-start(bf16[88,256]{1,0:T(8,128)(2,1)S(1)} %fusion.11), channel_id=1, source_target_pairs={{0,4},{1,5},{2,6},{3,7},{4,0},{5,1},{6,2},{7,3},{8,12},{9,13},{10,... | collective-permute-start | bytes 135176 | tf_op jit(solution)/shard_map/ppermute | solution.py:283
  85.5 7.0 %collective-permute-start.24 = (bf16[88,256]{1,0:T(8,128)(2,1)S(1)}, bf16[88,256]{1,0:T(8,128)(2,1)S(1)}, u32[]{:S(2)}, u32[]{:S(2)}) collective-permute-start(bf16[88,256]{1,0:T(8,128)(2,1)S(1)} %fusion.11), channel_id=1, source_target_pairs={{0,6},{1,7},{2,4},{3,5},{4,2},{5,3},{6,0},{7,1},{8,14},{9,15},{10,... | collective-permute-start | bytes 135176 | tf_op jit(solution)/shard_map/ppermute | solution.py:283
  92.5 4.5 %collective-permute-start.25 = (bf16[88,256]{1,0:T(8,128)(2,1)S(1)}, bf16[88,256]{1,0:T(8,128)(2,1)S(1)}, u32[]{:S(2)}, u32[]{:S(2)}) collective-permute-start(bf16[88,256]{1,0:T(8,128)(2,1)S(1)} %add_convert_fusion), channel_id=1, source_target_pairs={{0,8},{8,0},{16,24},{24,16},{1,9},{9,1},{17,25},{25,17},{2,10},{10... | collective-permute-start | bytes 135176 | tf_op jit(solution)/shard_map/ppermute | solution.py:269
  94.1 4.1 %collective-permute-start.26 = (bf16[88,256]{1,0:T(8,128)(2,1)S(1)}, bf16[88,256]{1,0:T(8,128)(2,1)S(1)}, u32[]{:S(2)}, u32[]{:S(2)}) collective-permute-start(bf16[88,256]{1,0:T(8,128)(2,1)S(1)} %add_convert_fusion), channel_id=1, source_target_pairs={{0,16},{8,24},{16,0},{24,8},{1,17},{9,25},{17,1},{25,9},{2,18},{10... | collective-permute-start | bytes 135176 | tf_op jit(solution)/shard_map/ppermute | solution.py:269
  95.4 4.9 %collective-permute-start.27 = (bf16[88,256]{1,0:T(8,128)(2,1)S(1)}, bf16[88,256]{1,0:T(8,128)(2,1)S(1)}, u32[]{:S(2)}, u32[]{:S(2)}) collective-permute-start(bf16[88,256]{1,0:T(8,128)(2,1)S(1)} %add_convert_fusion), channel_id=1, source_target_pairs={{0,24},{8,16},{16,8},{24,0},{1,25},{9,17},{17,9},{25,1},{2,26},{10... | collective-permute-start | bytes 135176 | tf_op jit(solution)/shard_map/ppermute | solution.py:269
  100.4 1.5 %collective-permute-start.28 = (f32[160,256]{1,0:T(8,128)S(1)}, f32[160,256]{1,0:T(8,128)S(1)}, u32[]{:S(2)}, u32[]{:S(2)}) collective-permute-start(f32[160,256]{1,0:T(8,128)S(1)} %constant_dynamic-update-slice_fusion.7.total_ref), channel_id=1, source_target_pairs={{0,1},{1,0},{2,3},{3,2},{4,5},{5,4},{6,7},{7,6},{8,9},{9,8},{10,11... | collective-permute-start | bytes 491528 | tf_op jit(solution)/shard_map/ppermute | solution.py:283
  (5 other events, 51.7 us)

commit v11 on v9

--- a/solution.py
+++ b/solution.py
@@ -77,23 +77,6 @@
         coded_ref[...] = encode(partial_ref[delta * own_rows : (delta + 1) * own_rows, :])
 
 
-def pack_kernel(feature_hbm, id_hbm, bundle_ref, id_ref, sems):
-    own_rows, lanes = feature_hbm.shape
-    small = pltpu.make_async_copy(id_hbm, id_ref, sems.at[0])
-    large = pltpu.make_async_copy(feature_hbm, bundle_ref.at[pl.ds(0, own_rows)], sems.at[1])
-    small.start()
-    large.start()
-    small.wait()
-    ids = id_ref[...]
-    rows = ids.shape[0]
-    parts = [ids & 255, jnp.right_shift(ids, 8) & 255, jnp.right_shift(ids, 16)]
-    pad = bundle_ref.shape[0] - own_rows - 3 * rows
-    parts += [jnp.zeros((pad, lanes), jnp.int32)] if pad else []
-    digit_rows = jnp.concatenate(parts, axis=0).astype(jnp.float32).astype(jnp.bfloat16)
-    bundle_ref[own_rows:, :] = digit_rows
-    large.wait()
-
-
 def last_kernel(chunk, spot_ref, total_ref, other_ref, grad_in_ref, grad_out_ref):
     side, rep_index = spot_ref[0], spot_ref[1]
     half = grad_in_ref.shape[0] // 2
@@ -125,14 +108,19 @@
     for coded_ref in coded_refs:
         total += decode(coded_ref[...])
     z_output = total.astype(jnp.bfloat16)
-    logits = dot(z_output, weight_ref[...]) + bias_ref[...]
+    square = eye_of(own_rows)
+    label, mask = (
+        jnp.sum(jnp.where(square, ref[...].astype(jnp.float32), 0.0), axis=1, keepdims=True)
+        for ref in (label_ref, mask_ref)
+    )
+    logits = dot_wide(z_output, weight_ref[...]) + bias_ref[...]
     logits_ref[...] = logits
     shifted = jnp.exp(logits - jnp.max(logits, axis=1, keepdims=True))
     likelihood = shifted / jnp.sum(shifted, axis=1, keepdims=True)
-    onehot = label_ref[...] == lax.broadcasted_iota(jnp.int32, logits.shape, 1)
-    slope = (likelihood - onehot.astype(jnp.float32)) * mask_ref[...].astype(jnp.float32) * scale
+    onehot = label.astype(jnp.int32) == lax.broadcasted_iota(jnp.int32, logits.shape, 1)
+    slope = (likelihood - onehot.astype(jnp.float32)) * mask * scale
     slope = slope.astype(jnp.bfloat16)
-    grad_rows = dot_wide(slope, weight_ref[...]).astype(jnp.bfloat16)
+    grad_rows = dot(slope, weight_ref[...]).astype(jnp.bfloat16)
     terms = lax.dot_general(
         slope, z_output, (((0,), (0,)), ((), ())), preferred_element_type=jnp.float32
     )
@@ -163,16 +151,15 @@
     )(*spot, *values)
 
 
-def dense_kernel(
-    per_rep, tile_side, turn, spot_ref, place_ref, count_ref, tiles_ref, dense_ref
-):
+def dense_kernel(per_rep, tile_side, turn, meta_ref, tiles_ref, dense_ref):
     section = pl.program_id(0)
-    rep_index, source_rep = spot_ref[0], spot_ref[1 + section]
-    edge = tiles_ref.shape[-1]
+    sections = pl.num_programs(0)
+    rep_index, source_rep = meta_ref[0], meta_ref[1 + section]
+    slots, edge = tiles_ref.shape[1], tiles_ref.shape[-1]
     dense_ref[...] = jnp.zeros_like(dense_ref)
 
     def put(slot, carried):
-        place = place_ref[section, slot]
+        place = meta_ref[1 + 2 * sections + section * slots + slot]
         row = place // tile_side
         column = place % tile_side
         row = ((row // per_rep) ^ rep_index) * per_rep + row % per_rep
@@ -186,10 +173,10 @@
             dense_ref[rows, columns] = tile
         return carried
 
-    lax.fori_loop(0, count_ref[section], put, 0)
-
-
-def build_dense(tiles, place, count, spot, own_rows, group_rows, turn):
+    lax.fori_loop(0, meta_ref[1 + sections + section], put, 0)
+
+
+def build_dense(tiles, meta, own_rows, group_rows, turn):
     sections, slots, edge, _ = tiles.shape
     body = functools.partial(dense_kernel, own_rows // edge, group_rows // edge, turn)
     block = (group_rows, group_rows)
@@ -197,7 +184,7 @@
     return pl.pallas_call(
         body,
         grid_spec=pltpu.PrefetchScalarGridSpec(
-            num_scalar_prefetch=3,
+            num_scalar_prefetch=1,
             grid=(sections,),
             in_specs=[pl.BlockSpec((1, slots, edge, edge), lambda p, *_: (p, 0, 0, 0))],
             out_specs=pl.BlockSpec(block, lambda p, *_: (p, 0) if turn else (0, p)),
@@ -210,7 +197,7 @@
             flops=0, bytes_accessed=4 * sections * group_rows * group_rows, transcendentals=0
         ),
         name="dense_turned" if turn else "dense",
-    )(spot, place, count, tiles)
+    )(meta, tiles)
 
 
 def on_device(
@@ -290,6 +277,12 @@
             parts = [parts[i] + parts[i + 1] for i in range(0, len(parts), 2)]
         return parts[0]
 
+    def digits(ids):
+        lanes = features.shape[2]
+        parts = [ids & 255, (ids >> 8) & 255, ids >> 16]
+        rows = jnp.concatenate([part.reshape(-1, lanes) for part in parts], axis=0)
+        return jnp.pad(rows, ((0, -rows.shape[0] % 16), (0, 0))).astype(bf16)
+
     def undo_digits(rows):
         count = own_rows // rows.shape[1]
         parts = [rows[i * count : (i + 1) * count].astype(jnp.int32) for i in range(3)]
@@ -298,26 +291,15 @@
     member = lax.rem(blk_index, sections)
     place, count = tile_place[0, 0], tile_count[0, 0]
     width = features.shape[2]
-    digit_rows = 3 * own_rows // width
-    stride = own_rows + digit_rows + -digit_rows % 16
-    anywhere = pl.BlockSpec(memory_space=pl.ANY)
-    bundle = pl.pallas_call(
-        pack_kernel,
-        in_specs=[anywhere] * 2,
-        out_shape=jax.ShapeDtypeStruct((stride, width), bf16),
-        scratch_shapes=[
-            pltpu.VMEM((own_rows // width, width), jnp.int32),
-            pltpu.SemaphoreType.DMA((2,)),
-        ],
-        compiler_params=pltpu.CompilerParams(vmem_limit_bytes=60 * 1024 * 1024),
-        name="pack",
-    )(features[0], node_ids.reshape(-1, width))
+    bundle = jnp.concatenate([features[0], digits(node_ids[0])], axis=0)
+    stride = bundle.shape[0]
     arrived = to_pieces(bundle)
+    tiles = tile_values[0, 0]
     next_rep = lax.rem(rep_index + 1, reps)
     where = jnp.where(member < jnp.arange(sections + 1) - 1, next_rep, rep_index)
-    layout = (where, own_rows, group_rows)
-    count, arrived[0] = lax.optimization_barrier((count, arrived[0]))
-    dense = build_dense(tile_values[0, 0], place, count, *layout, False)
+    meta = jnp.concatenate([where, count, place.reshape(-1)])
+    meta, arrived[0] = lax.optimization_barrier((meta, arrived[0]))
+    dense = build_dense(tiles, meta, own_rows, group_rows, False)
     pieces = [
         half[d * stride : (d + 1) * stride] for half in to_all(arrived) for d in range(reps // 2)
     ]
@@ -336,7 +318,10 @@
     third = f32(4.0 / 3.0)
     pre_act = dot(z_columns, weight_in)
     dropped = (jnp.maximum(pre_act, 0.0) * (kept.astype(f32) * third)).astype(bf16)
+    dropped, z_again = lax.optimization_barrier((dropped, z_columns))
     second = dot(dense, dropped)
+    mask = jnp.where(dot(z_again, weight_in) > 0, kept, jnp.zeros_like(kept))
+    mask, ready = lax.optimization_barrier((mask, second))
     sent = simple_call(
         encode_kernel,
         [jax.ShapeDtypeStruct((own_rows + HEAD_ROWS, hidden_width), jnp.int16)] * (reps - 1),
@@ -354,15 +339,14 @@
         ]
         + [jax.ShapeDtypeStruct((own_rows + chunk, hidden_width), bf16)] * reps,
         "head",
-        weight_out, class_bias[None], labels[0][:, None], train_mask[0][:, None],
-        second, *arrived,
+        weight_out.T, class_bias[None], labels, train_mask,
+        ready, *arrived,
         spot=(spot,),
         scratch=[pltpu.VMEM((chunk * reps, hidden_width), f32)],
     )
     arrived = [swap(sent[d], d) for d in range(reps)]
-    count, z_again, kept, out_total = lax.optimization_barrier((count, z_columns, kept, out_total))
-    turned = build_dense(tile_values[0, 0], place, count, *layout, True)
-    mask = jnp.where(dot(z_again, weight_in) > 0, kept, jnp.zeros_like(kept))
+    meta, out_total = lax.optimization_barrier((meta, out_total))
+    turned = build_dense(tiles, meta, own_rows, group_rows, True)
     grad_block = jnp.concatenate([part[:own_rows] for part in arrived], axis=0)
     for part in arrived[1:]:
         out_total = out_total + part[own_rows:].astype(f32)

time: 100 us -> 97.5 us (0.975)
  local copies, waits for them, and re-layouts: 6.41 us -> 3.11 us
  waiting for transfers between devices: 27.1 us -> 30.1 us
  matrix products: 8.5 us -> 6.03 us
  other arithmetic: 1.41 us -> 3.6 us
  Pallas kernels: 10.1 us -> 8.25 us
    ppermute x4, starting transfers between devices: 7.47 us -> 1.08 us  [to_section(): return lax.ppermute(block, ('rep', 'blk'), pairs)]
    unnamed x42 -> x29, local copies, waits for them, and re-layouts: 6.01 us -> 2.22 us
    ppermute x4, waiting for transfers between devices: 3.02 us -> 6.45 us  [to_section(): return lax.ppermute(block, ('rep', 'blk'), pairs)]
    ppermute x8, starting transfers between devices: 14.2 us -> 17.4 us  [to_pieces(): pieces.append(lax.ppermute(value, ('rep', 'blk'), pairs))]
    ppermute x12, starting transfers between devices: 18.7 us -> 21.9 us  [swap(): return lax.ppermute(value, 'rep', [(r, r ^ delta) for r in range(reps)])]
    dot_general x4 -> x5, matrix products: 8.16 us -> 5.67 us  [dot(): return jnp.dot(left, right, preferred_element_type=jnp.float32)]
    concatenate x0 -> x3, other arithmetic: none -> 1.59 us  [the longest x1 0.85 us: on_device(): bundle = jnp.concatenate([features[0], digits(node_ids[0])], axis=0)]
    pallas_call x1 -> x0, Pallas kernels: 1.53 us -> none  [on_device(): pl.pallas_call(pack_kernel, in_specs=[anywhere] * 2, out_shape=jax.ShapeD...]
  transfers between devices with their start and end apart: 29 -> 29, of which waited for: 18 -> 17; matrix products, arithmetic and copies ran while one was open for 4% -> 5% of each run, Pallas kernels for 5% -> 5%
where the time goes in v11:
time: 97.5 us; the launch traced here: 97.2 us
  starting transfers between devices  45 us (46%)
  waiting for transfers between devices  30.1 us (31%)
  Pallas kernels  8.25 us (8%)
  matrix products  6.03 us (6%)
  other arithmetic  3.6 us (4%)
  local copies, waits for them, and re-layouts  3.11 us (3%)
  between operations  1.18 us (1%)
    ppermute x12, starting transfers between devices, swap(): return lax.ppermute(value, 'rep', [(r, r ^ delta) for r in range(reps)])  21.9 us
    ppermute x8, starting transfers between devices, to_pieces(): pieces.append(lax.ppermute(value, ('rep', 'blk'), pairs))  17.4 us
    ppermute x12, waiting for transfers between devices, swap(): return lax.ppermute(value, 'rep', [(r, r ^ delta) for r in range(reps)])  14.7 us
    ppermute x4, waiting for transfers between devices, to_section(): return lax.ppermute(block, ('rep', 'blk'), pairs)  6.45 us
    dot_general x5, matrix products, dot(): return jnp.dot(left, right, preferred_element_type=jnp.float32)  5.67 us
    pallas_call x2, Pallas kernels, build_dense(): pl.pallas_call(body, grid_spec=pltpu.PrefetchScalarGridSpec(num_scalar_pr...  5.2 us
    ppermute x5, starting transfers between devices, exchange(): return lax.ppermute(value, 'blk', [(c, c ^ delta) for c in range(blks)])  4.59 us
    ppermute x5, waiting for transfers between devices, exchange(): return lax.ppermute(value, 'blk', [(c, c ^ delta) for c in range(blks)])  4.58 us
  transfers between devices with their start and end apart: 29, of which 17 were waited for; matrix products, arithmetic and copies ran while one was open for 5% of the time, Pallas kernels for 5%

profile of v11, /device:TPU:0, one launch (start us, length us, event | category | flops | bytes accessed | tf_op | source)
XLA Modules:
  0.0 97.2 jit_solution(14695147840846413644)
XLA Ops:
  2.9 6.8 %collective-permute-start.1 = (bf16[272,128]{1,0:T(8,128)(2,1)S(1)}, bf16[272,128]{1,0:T(8,128)(2,1)S(1)}, u32[]{:S(2)}, u32[]{:S(2)}) collective-permute-start(bf16[272,128]{1,0:T(8,128)(2,1)S(1)} %pad_maximum_fusion.6), channel_id=1, source_target_pairs={{0,10},{1,11},{2,12},{3,13},{4,14},{5,15},{6,8},{7,9},{8,0},{9,1},... | collective-permute-start | bytes 208904 | tf_op jit(solution)/shard_map/ppermute | solution.py:254
  9.7 1.3 %collective-permute-start.2 = (bf16[272,128]{1,0:T(8,128)(2,1)S(1)}, bf16[272,128]{1,0:T(8,128)(2,1)S(1)}, u32[]{:S(2)}, u32[]{:S(2)}) collective-permute-start(bf16[272,128]{1,0:T(8,128)(2,1)S(1)} %pad_maximum_fusion.6), channel_id=1, source_target_pairs={{0,20},{1,21},{2,22},{3,23},{4,16},{5,17},{6,18},{7,19},{8,30},{9,... | collective-permute-start | bytes 208904 | tf_op jit(solution)/shard_map/ppermute | solution.py:254
  11.0 3.0 %collective-permute-start.3 = (bf16[272,128]{1,0:T(8,128)(2,1)S(1)}, bf16[272,128]{1,0:T(8,128)(2,1)S(1)}, u32[]{:S(2)}, u32[]{:S(2)}) collective-permute-start(bf16[272,128]{1,0:T(8,128)(2,1)S(1)} %pad_maximum_fusion.6), channel_id=1, source_target_pairs={{0,30},{1,31},{2,24},{3,25},{4,26},{5,27},{6,28},{7,29},{8,20},{9,... | collective-permute-start | bytes 208904 | tf_op jit(solution)/shard_map/ppermute | solution.py:254
  17.2 1.2 %copy-done.1 = bf16[1,1,2,16,128,128]{5,4,3,2,1,0:T(8,128)(2,1)S(1)} copy-done((bf16[1,1,2,16,128,128]{5,4,3,2,1,0:T(8,128)(2,1)S(1)}, bf16[1,1,2,16,128,128]{5,4,3,2,1,0:T(8,128)(2,1)}, u32[]{:S(2)}) %copy-start.1) | copy-done | bytes 1048600
  18.4 2.1 %dense.1 = bf16[1024,2048]{1,0:T(8,128)(2,1)S(1)} custom-call(s32[37]{0:T(128)S(1)} %pad_add_fusion.1.meta_ref, bf16[2,16,128,128]{3,2,1,0:T(8,128)(2,1)S(1)} %bitcast.40), custom_call_target="tpu_custom_call" | custom-call | bytes 8388608 | tf_op jit(solution)/shard_map/dense/pallas_call | solution.py:184
  20.7 2.1 %collective-permute-done.5 = bf16[544,128]{1,0:T(8,128)(2,1)S(1)} collective-permute-done((bf16[544,128]{1,0:T(8,128)(2,1)S(1)}, bf16[544,128]{1,0:T(8,128)(2,1)S(1)}, u32[]{:S(2)}, u32[]{:S(2)}) %collective-permute-start.5) | collective-permute-done | bytes 139296 | tf_op jit(solution)/shard_map/ppermute | solution.py:241
  22.8 1.3 %fusion.18 = f32[1024,128]{1,0:T(8,128)S(1)} fusion(bf16[1024,2048]{1,0:T(8,128)(2,1)S(1)} %dense.1, bf16[2048,128]{1,0:T(8,128)(2,1)S(1)} %slice_dynamic-update-slice_fusion), kind=kOutput, calls=%fused_computation.74 | convolution fusion | flops 536870912 | bytes 5242880 | tf_op jit(solution)/shard_map/dot_general | solution.py:32
  24.1 5.3 %collective-permute-start.6 = (f32[256,128]{1,0:T(8,128)S(1)}, f32[256,128]{1,0:T(8,128)S(1)}, u32[]{:S(2)}, u32[]{:S(2)}) collective-permute-start(f32[256,128]{1,0:T(8,128)S(1)} %get-tuple-element.61), channel_id=1, source_target_pairs={{0,8},{8,0},{16,24},{24,16},{1,9},{9,1},{17,25},{25,17},{2,10},{10... | collective-permute-start | bytes 393224 | tf_op jit(solution)/shard_map/ppermute | solution.py:230
  29.4 1.5 %collective-permute-start.8 = (f32[256,128]{1,0:T(8,128)S(1)}, f32[256,128]{1,0:T(8,128)S(1)}, u32[]{:S(2)}, u32[]{:S(2)}) collective-permute-start(f32[256,128]{1,0:T(8,128)S(1)} %get-tuple-element.62), channel_id=1, source_target_pairs={{0,24},{8,16},{16,8},{24,0},{1,25},{9,17},{17,9},{25,1},{2,26},{10... | collective-permute-start | bytes 393224 | tf_op jit(solution)/shard_map/ppermute | solution.py:230
  31.1 2.6 %collective-permute-done.6 = f32[256,128]{1,0:T(8,128)S(1)} collective-permute-done((f32[256,128]{1,0:T(8,128)S(1)}, f32[256,128]{1,0:T(8,128)S(1)}, u32[]{:S(2)}, u32[]{:S(2)}) %collective-permute-start.6) | collective-permute-done | bytes 131104 | tf_op jit(solution)/shard_map/ppermute | solution.py:230
  33.6 2.9 %collective-permute-done.7 = f32[256,128]{1,0:T(8,128)S(1)} collective-permute-done((f32[256,128]{1,0:T(8,128)S(1)}, f32[256,128]{1,0:T(8,128)S(1)}, u32[]{:S(2)}, u32[]{:S(2)}) %collective-permute-start.7) | collective-permute-done | bytes 131104 | tf_op jit(solution)/shard_map/ppermute | solution.py:230
  36.7 4.9 %collective-permute-start.12 = (bf16[256,128]{1,0:T(8,128)(2,1)S(1)}, bf16[256,128]{1,0:T(8,128)(2,1)S(1)}, u32[]{:S(2)}, u32[]{:S(2)}) collective-permute-start(bf16[256,128]{1,0:T(8,128)(2,1)S(1)} %fusion.10), channel_id=1, source_target_pairs={{0,30},{1,31},{2,24},{3,25},{4,26},{5,27},{6,28},{7,29},{8,20},{9,... | collective-permute-start | bytes 196616 | tf_op jit(solution)/shard_map/ppermute | solution.py:254
  43.5 3.5 %collective-permute-done.10 = bf16[256,128]{1,0:T(8,128)(2,1)S(1)} collective-permute-done((bf16[256,128]{1,0:T(8,128)(2,1)S(1)}, bf16[256,128]{1,0:T(8,128)(2,1)S(1)}, u32[]{:S(2)}, u32[]{:S(2)}) %collective-permute-start.10) | collective-permute-done | bytes 65568 | tf_op jit(solution)/shard_map/ppermute | solution.py:254
  47.2 4.3 %collective-permute-done.13 = bf16[512,128]{1,0:T(8,128)(2,1)S(1)} collective-permute-done((bf16[512,128]{1,0:T(8,128)(2,1)S(1)}, bf16[512,128]{1,0:T(8,128)(2,1)S(1)}, u32[]{:S(2)}, u32[]{:S(2)}) %collective-permute-start.13) | collective-permute-done | bytes 131104 | tf_op jit(solution)/shard_map/ppermute | solution.py:241
  52.0 1.3 %fusion.19.partial_ref.own_ref = f32[1024,256]{1,0:T(8,128)S(1)} fusion(bf16[1024,2048]{1,0:T(8,128)(2,1)S(1)} %dense.1, bf16[2048,256]{1,0:T(8,128)(2,1)S(1)} %fusion.1), kind=kOutput, calls=%fused_computation.75 | convolution fusion | flops 1073741824 | bytes 6291456 | tf_op jit(solution)/shard_map/dot_general | solution.py:32
  53.8 6.4 %collective-permute-start.15 = (s16[272,256]{1,0:T(8,128)(2,1)S(1)}, s16[272,256]{1,0:T(8,128)(2,1)S(1)}, u32[]{:S(2)}, u32[]{:S(2)}) collective-permute-start(s16[272,256]{1,0:T(8,128)(2,1)S(1)} %get-tuple-element.36), channel_id=1, source_target_pairs={{0,8},{8,0},{16,24},{24,16},{1,9},{9,1},{17,25},{25,17},{2,10},{10... | collective-permute-start | bytes 417800 | tf_op jit(solution)/shard_map/ppermute | solution.py:230
  60.1 1.5 %collective-permute-start.17 = (s16[272,256]{1,0:T(8,128)(2,1)S(1)}, s16[272,256]{1,0:T(8,128)(2,1)S(1)}, u32[]{:S(2)}, u32[]{:S(2)}) collective-permute-start(s16[272,256]{1,0:T(8,128)(2,1)S(1)} %get-tuple-element.38), channel_id=1, source_target_pairs={{0,24},{8,16},{16,8},{24,0},{1,25},{9,17},{17,9},{25,1},{2,26},{10... | collective-permute-start | bytes 417800 | tf_op jit(solution)/shard_map/ppermute | solution.py:230
  61.7 1.4 %fusion.3 = bf16[2048,256]{1,0:T(8,128)(2,1)} fusion(bf16[2048,256]{1,0:T(8,128)(2,1)S(1)} %fusion.7, bf16[2048,128]{1,0:T(8,128)(2,1)S(1)} %constant_dynamic-update-slice_fusion.1, bf16[128,256]{1,0:T(8,128)(2,1)S(1)} %copy-done), kind=kOutput, calls=%fused_computation.8 | convolution fusion | flops 135266304 | bytes 2686976 | tf_op jit(solution)/shard_map/dot_general | solution.py:32
  63.7 3.6 %collective-permute-done.16.refs_1_ = s16[272,256]{1,0:T(8,128)(2,1)S(1)} collective-permute-done((s16[272,256]{1,0:T(8,128)(2,1)S(1)}, s16[272,256]{1,0:T(8,128)(2,1)S(1)}, u32[]{:S(2)}, u32[]{:S(2)}) %collective-permute-start.16) | collective-permute-done | bytes 139296 | tf_op jit(solution)/shard_map/ppermute | solution.py:230
  67.4 1.3 %head.1 = (f32[256,172]{1,0:T(8,128)S(1)}, f32[48,256]{1,0:T(8,128)S(1)}, bf16[304,256]{1,0:T(8,128)(2,1)S(1)}, bf16[304,256]{1,0:T(8,128)(2,1)S(1)}, bf16[304,2...) custom-call(s32[2]{0:T(128)S(1)} %pad_add_fusion.spot_ref, bf16[172,256]{1,0:T(8,128)(2,1)S(1)} %bitcast.43, ...), custom_call_target="tpu_custom_call" | custom-call | tf_op jit(solution)/shard_map/head/pallas_call | solution.py:144
  70.1 2.2 %collective-permute-start.20 = (bf16[304,256]{1,0:T(8,128)(2,1)S(1)}, bf16[304,256]{1,0:T(8,128)(2,1)S(1)}, u32[]{:S(2)}, u32[]{:S(2)}) collective-permute-start(bf16[304,256]{1,0:T(8,128)(2,1)S(1)} %get-tuple-element.45), channel_id=1, source_target_pairs={{0,24},{8,16},{16,8},{24,0},{1,25},{9,17},{17,9},{25,1},{2,26},{10... | collective-permute-start | bytes 466952 | tf_op jit(solution)/shard_map/ppermute | solution.py:230
  72.3 3.1 %dense_turned.1 = bf16[2048,1024]{1,0:T(8,128)(2,1)S(1)} custom-call(s32[37]{0:T(128)S(1)} %pad_add_fusion.1.meta_ref, bf16[2,16,128,128]{3,2,1,0:T(8,128)(2,1)S(1)} %bitcast.41), custom_call_target="tpu_custom_call" | custom-call | bytes 8388608 | tf_op jit(solution)/shard_map/dense_turned/pallas_call | solution.py:184
  75.4 1.0 %collective-permute-done.19 = bf16[304,256]{1,0:T(8,128)(2,1)S(1)} collective-permute-done((bf16[304,256]{1,0:T(8,128)(2,1)S(1)}, bf16[304,256]{1,0:T(8,128)(2,1)S(1)}, u32[]{:S(2)}, u32[]{:S(2)}) %collective-permute-start.19) | collective-permute-done | bytes 155680 | tf_op jit(solution)/shard_map/ppermute | solution.py:230
  76.6 1.3 %fusion.2 = bf16[2048,256]{1,0:T(8,128)(2,1)S(1)} fusion(bf16[2048,1024]{1,0:T(8,128)(2,1)S(1)} %dense_turned.1, bf16[1024,256]{1,0:T(8,128)(2,1)S(1)} %pad_maximum_fusion, bf16[2048,256]{1,0:T(8,128)(2,1)S(1)} %copy-done.7), kind=kOutput, calls=%fused_computation.6 | convolution fusion | flops 1075838976 | bytes 6815744 | tf_op jit(solution)/shard_map/dot_general | solution.py:32
  78.4 1.3 %collective-permute-done.21 = f32[88,256]{1,0:T(8,128)S(1)} collective-permute-done((f32[88,256]{1,0:T(8,128)S(1)}, f32[88,256]{1,0:T(8,128)S(1)}, u32[]{:S(2)}, u32[]{:S(2)}) %collective-permute-start.21) | collective-permute-done | bytes 90144 | tf_op jit(solution)/shard_map/ppermute | solution.py:244
  80.4 3.8 %collective-permute-start.24 = (bf16[88,256]{1,0:T(8,128)(2,1)S(1)}, bf16[88,256]{1,0:T(8,128)(2,1)S(1)}, u32[]{:S(2)}, u32[]{:S(2)}) collective-permute-start(bf16[88,256]{1,0:T(8,128)(2,1)S(1)} %fusion.11), channel_id=1, source_target_pairs={{0,6},{1,7},{2,4},{3,5},{4,2},{5,3},{6,0},{7,1},{8,14},{9,15},{10,... | collective-permute-start | bytes 135176 | tf_op jit(solution)/shard_map/ppermute | solution.py:244
  84.3 2.6 %collective-permute-done.23 = bf16[88,256]{1,0:T(8,128)(2,1)S(1)} collective-permute-done((bf16[88,256]{1,0:T(8,128)(2,1)S(1)}, bf16[88,256]{1,0:T(8,128)(2,1)S(1)}, u32[]{:S(2)}, u32[]{:S(2)}) %collective-permute-start.23) | collective-permute-done | bytes 45088 | tf_op jit(solution)/shard_map/ppermute | solution.py:244
  86.9 1.3 %collective-permute-start.25 = (bf16[88,256]{1,0:T(8,128)(2,1)S(1)}, bf16[88,256]{1,0:T(8,128)(2,1)S(1)}, u32[]{:S(2)}, u32[]{:S(2)}) collective-permute-start(bf16[88,256]{1,0:T(8,128)(2,1)S(1)} %add_convert_fusion), channel_id=1, source_target_pairs={{0,8},{8,0},{16,24},{24,16},{1,9},{9,1},{17,25},{25,17},{2,10},{10... | collective-permute-start | bytes 135176 | tf_op jit(solution)/shard_map/ppermute | solution.py:230
  88.2 1.3 %collective-permute-start.26 = (bf16[88,256]{1,0:T(8,128)(2,1)S(1)}, bf16[88,256]{1,0:T(8,128)(2,1)S(1)}, u32[]{:S(2)}, u32[]{:S(2)}) collective-permute-start(bf16[88,256]{1,0:T(8,128)(2,1)S(1)} %add_convert_fusion), channel_id=1, source_target_pairs={{0,16},{8,24},{16,0},{24,8},{1,17},{9,25},{17,1},{25,9},{2,18},{10... | collective-permute-start | bytes 135176 | tf_op jit(solution)/shard_map/ppermute | solution.py:230
  89.5 1.0 %collective-permute-start.27 = (bf16[88,256]{1,0:T(8,128)(2,1)S(1)}, bf16[88,256]{1,0:T(8,128)(2,1)S(1)}, u32[]{:S(2)}, u32[]{:S(2)}) collective-permute-start(bf16[88,256]{1,0:T(8,128)(2,1)S(1)} %add_convert_fusion), channel_id=1, source_target_pairs={{0,24},{8,16},{16,8},{24,0},{1,25},{9,17},{17,9},{25,1},{2,26},{10... | collective-permute-start | bytes 135176 | tf_op jit(solution)/shard_map/ppermute | solution.py:230
  92.3 2.2 %collective-permute-done.27 = bf16[88,256]{1,0:T(8,128)(2,1)S(1)} collective-permute-done((bf16[88,256]{1,0:T(8,128)(2,1)S(1)}, bf16[88,256]{1,0:T(8,128)(2,1)S(1)}, u32[]{:S(2)}, u32[]{:S(2)}) %collective-permute-start.27) | collective-permute-done | bytes 45088 | tf_op jit(solution)/shard_map/ppermute | solution.py:230
  95.9 1.3 %last.1 = (f32[128,256]{1,0:T(8,128)}, f32[172,256]{1,0:T(8,128)}) custom-call(s32[2]{0:T(128)S(1)} %pad_add_fusion.spot_ref, f32[160,256]{1,0:T(8,128)S(1)} %constant_dynamic-update-slice_fusion.7.total_ref, f32[160,256]{1,0:T(8,128)S(1)} %collective-permute-done.28.other_ref), custom_call_target="tpu_custom_call" | custom-call | tf_op jit(solution)/shard_map/last/pallas_call | solution.py:144
  (109 shorter events, 15.3 us)
Async XLA Ops:
  0.6 50.9 %copy-start = (bf16[128,256]{1,0:T(8,128)(2,1)S(1)}, bf16[128,256]{1,0:T(8,128)(2,1)}, u32[]{:S(2)}) copy-start(bf16[128,256]{1,0:T(8,128)(2,1)} %param.17) | copy-start | bytes 196612
  2.2 13.4 %collective-permute-start = (bf16[272,128]{1,0:T(8,128)(2,1)S(1)}, bf16[272,128]{1,0:T(8,128)(2,1)S(1)}, u32[]{:S(2)}, u32[]{:S(2)}) collective-permute-start(bf16[272,128]{1,0:T(8,128)(2,1)S(1)} %pad_maximum_fusion.6), channel_id=1, source_target_pairs={{0,0},{1,1},{2,2},{3,3},{4,4},{5,5},{6,6},{7,7},{8,10},{9,11},{10,... | collective-permute-start | bytes 208904 | tf_op jit(solution)/shard_map/ppermute | solution.py:254
  2.9 12.7 %collective-permute-start.1 = (bf16[272,128]{1,0:T(8,128)(2,1)S(1)}, bf16[272,128]{1,0:T(8,128)(2,1)S(1)}, u32[]{:S(2)}, u32[]{:S(2)}) collective-permute-start(bf16[272,128]{1,0:T(8,128)(2,1)S(1)} %pad_maximum_fusion.6), channel_id=1, source_target_pairs={{0,10},{1,11},{2,12},{3,13},{4,14},{5,15},{6,8},{7,9},{8,0},{9,1},... | collective-permute-start | bytes 208904 | tf_op jit(solution)/shard_map/ppermute | solution.py:254
  9.7 6.0 %collective-permute-start.2 = (bf16[272,128]{1,0:T(8,128)(2,1)S(1)}, bf16[272,128]{1,0:T(8,128)(2,1)S(1)}, u32[]{:S(2)}, u32[]{:S(2)}) collective-permute-start(bf16[272,128]{1,0:T(8,128)(2,1)S(1)} %pad_maximum_fusion.6), channel_id=1, source_target_pairs={{0,20},{1,21},{2,22},{3,23},{4,16},{5,17},{6,18},{7,19},{8,30},{9,... | collective-permute-start | bytes 208904 | tf_op jit(solution)/shard_map/ppermute | solution.py:254
  11.0 5.2 %collective-permute-start.3 = (bf16[272,128]{1,0:T(8,128)(2,1)S(1)}, bf16[272,128]{1,0:T(8,128)(2,1)S(1)}, u32[]{:S(2)}, u32[]{:S(2)}) collective-permute-start(bf16[272,128]{1,0:T(8,128)(2,1)S(1)} %pad_maximum_fusion.6), channel_id=1, source_target_pairs={{0,30},{1,31},{2,24},{3,25},{4,26},{5,27},{6,28},{7,29},{8,20},{9,... | collective-permute-start | bytes 208904 | tf_op jit(solution)/shard_map/ppermute | solution.py:254
  15.6 5.0 %collective-permute-start.4 = (bf16[544,128]{1,0:T(8,128)(2,1)S(1)}, bf16[544,128]{1,0:T(8,128)(2,1)S(1)}, u32[]{:S(2)}, u32[]{:S(2)}) collective-permute-start(bf16[544,128]{1,0:T(8,128)(2,1)S(1)} %pad_maximum_fusion.1), channel_id=1, source_target_pairs={{0,1},{1,24},{2,3},{3,26},{4,5},{5,28},{6,7},{7,30},{8,9},{9,0},{1... | collective-permute-start | bytes 417800 | tf_op jit(solution)/shard_map/ppermute | solution.py:241
  16.3 6.5 %collective-permute-start.5 = (bf16[544,128]{1,0:T(8,128)(2,1)S(1)}, bf16[544,128]{1,0:T(8,128)(2,1)S(1)}, u32[]{:S(2)}, u32[]{:S(2)}) collective-permute-start(bf16[544,128]{1,0:T(8,128)(2,1)S(1)} %pad_maximum_fusion.2), channel_id=1, source_target_pairs={{0,1},{1,24},{2,3},{3,26},{4,5},{5,28},{6,7},{7,30},{8,9},{9,0},{1... | collective-permute-start | bytes 417800 | tf_op jit(solution)/shard_map/ppermute | solution.py:241
  24.1 9.5 %collective-permute-start.6 = (f32[256,128]{1,0:T(8,128)S(1)}, f32[256,128]{1,0:T(8,128)S(1)}, u32[]{:S(2)}, u32[]{:S(2)}) collective-permute-start(f32[256,128]{1,0:T(8,128)S(1)} %get-tuple-element.61), channel_id=1, source_target_pairs={{0,8},{8,0},{16,24},{24,16},{1,9},{9,1},{17,25},{25,17},{2,10},{10... | collective-permute-start | bytes 393224 | tf_op jit(solution)/shard_map/ppermute | solution.py:230
  29.4 7.1 %collective-permute-start.7 = (f32[256,128]{1,0:T(8,128)S(1)}, f32[256,128]{1,0:T(8,128)S(1)}, u32[]{:S(2)}, u32[]{:S(2)}) collective-permute-start(f32[256,128]{1,0:T(8,128)S(1)} %get-tuple-element.63), channel_id=1, source_target_pairs={{0,16},{8,24},{16,0},{24,8},{1,17},{9,25},{17,1},{25,9},{2,18},{10... | collective-permute-start | bytes 393224 | tf_op jit(solution)/shard_map/ppermute | solution.py:230
  29.4 7.1 %collective-permute-start.8 = (f32[256,128]{1,0:T(8,128)S(1)}, f32[256,128]{1,0:T(8,128)S(1)}, u32[]{:S(2)}, u32[]{:S(2)}) collective-permute-start(f32[256,128]{1,0:T(8,128)S(1)} %get-tuple-element.62), channel_id=1, source_target_pairs={{0,24},{8,16},{16,8},{24,0},{1,25},{9,17},{17,9},{25,1},{2,26},{10... | collective-permute-start | bytes 393224 | tf_op jit(solution)/shard_map/ppermute | solution.py:230
  36.6 6.6 %collective-permute-start.11 = (bf16[256,128]{1,0:T(8,128)(2,1)S(1)}, bf16[256,128]{1,0:T(8,128)(2,1)S(1)}, u32[]{:S(2)}, u32[]{:S(2)}) collective-permute-start(bf16[256,128]{1,0:T(8,128)(2,1)S(1)} %fusion.10), channel_id=1, source_target_pairs={{0,20},{1,21},{2,22},{3,23},{4,16},{5,17},{6,18},{7,19},{8,30},{9,... | collective-permute-start | bytes 196616 | tf_op jit(solution)/shard_map/ppermute | solution.py:254
  36.7 6.8 %collective-permute-start.12 = (bf16[256,128]{1,0:T(8,128)(2,1)S(1)}, bf16[256,128]{1,0:T(8,128)(2,1)S(1)}, u32[]{:S(2)}, u32[]{:S(2)}) collective-permute-start(bf16[256,128]{1,0:T(8,128)(2,1)S(1)} %fusion.10), channel_id=1, source_target_pairs={{0,30},{1,31},{2,24},{3,25},{4,26},{5,27},{6,28},{7,29},{8,20},{9,... | collective-permute-start | bytes 196616 | tf_op jit(solution)/shard_map/ppermute | solution.py:254
  42.4 4.6 %collective-permute-start.10 = (bf16[256,128]{1,0:T(8,128)(2,1)S(1)}, bf16[256,128]{1,0:T(8,128)(2,1)S(1)}, u32[]{:S(2)}, u32[]{:S(2)}) collective-permute-start(bf16[256,128]{1,0:T(8,128)(2,1)S(1)} %fusion.10), channel_id=1, source_target_pairs={{0,10},{1,11},{2,12},{3,13},{4,14},{5,15},{6,8},{7,9},{8,0},{9,1},... | collective-permute-start | bytes 196616 | tf_op jit(solution)/shard_map/ppermute | solution.py:254
  42.5 4.6 %collective-permute-start.9 = (bf16[256,128]{1,0:T(8,128)(2,1)S(1)}, bf16[256,128]{1,0:T(8,128)(2,1)S(1)}, u32[]{:S(2)}, u32[]{:S(2)}) collective-permute-start(bf16[256,128]{1,0:T(8,128)(2,1)S(1)} %fusion.10), channel_id=1, source_target_pairs={{0,0},{1,1},{2,2},{3,3},{4,4},{5,5},{6,6},{7,7},{8,10},{9,11},{10,... | collective-permute-start | bytes 196616 | tf_op jit(solution)/shard_map/ppermute | solution.py:254
  43.5 8.1 %collective-permute-start.14 = (bf16[512,128]{1,0:T(8,128)(2,1)S(1)}, bf16[512,128]{1,0:T(8,128)(2,1)S(1)}, u32[]{:S(2)}, u32[]{:S(2)}) collective-permute-start(bf16[512,128]{1,0:T(8,128)(2,1)S(1)} %pad_maximum_fusion.4), channel_id=1, source_target_pairs={{0,1},{1,24},{2,3},{3,26},{4,5},{5,28},{6,7},{7,30},{8,9},{9,0},{1... | collective-permute-start | bytes 393224 | tf_op jit(solution)/shard_map/ppermute | solution.py:241
  47.1 4.4 %collective-permute-start.13 = (bf16[512,128]{1,0:T(8,128)(2,1)S(1)}, bf16[512,128]{1,0:T(8,128)(2,1)S(1)}, u32[]{:S(2)}, u32[]{:S(2)}) collective-permute-start(bf16[512,128]{1,0:T(8,128)(2,1)S(1)} %pad_maximum_fusion.3), channel_id=1, source_target_pairs={{0,1},{1,24},{2,3},{3,26},{4,5},{5,28},{6,7},{7,30},{8,9},{9,0},{1... | collective-permute-start | bytes 393224 | tf_op jit(solution)/shard_map/ppermute | solution.py:241
  53.3 14.0 %copy-start.3 = (bf16[256,172]{0,1:T(8,128)(2,1)S(1)}, bf16[256,172]{0,1:T(8,128)(2,1)}, u32[]{:S(2)}) copy-start(bf16[256,172]{0,1:T(8,128)(2,1)} %param.18) | copy-start | bytes 264196
  53.3 14.0 %copy-start.4 = (f32[172]{0:T(256)S(1)}, f32[172]{0:T(256)}, u32[]{:S(2)}) copy-start(f32[172]{0:T(256)} %param.19) | copy-start | bytes 2068
  53.8 9.9 %collective-permute-start.15 = (s16[272,256]{1,0:T(8,128)(2,1)S(1)}, s16[272,256]{1,0:T(8,128)(2,1)S(1)}, u32[]{:S(2)}, u32[]{:S(2)}) collective-permute-start(s16[272,256]{1,0:T(8,128)(2,1)S(1)} %get-tuple-element.36), channel_id=1, source_target_pairs={{0,8},{8,0},{16,24},{24,16},{1,9},{9,1},{17,25},{25,17},{2,10},{10... | collective-permute-start | bytes 417800 | tf_op jit(solution)/shard_map/ppermute | solution.py:230
  60.1 7.2 %collective-permute-start.16 = (s16[272,256]{1,0:T(8,128)(2,1)S(1)}, s16[272,256]{1,0:T(8,128)(2,1)S(1)}, u32[]{:S(2)}, u32[]{:S(2)}) collective-permute-start(s16[272,256]{1,0:T(8,128)(2,1)S(1)} %get-tuple-element.37), channel_id=1, source_target_pairs={{0,16},{8,24},{16,0},{24,8},{1,17},{9,25},{17,1},{25,9},{2,18},{10... | collective-permute-start | bytes 417800 | tf_op jit(solution)/shard_map/ppermute | solution.py:230
  60.1 7.2 %collective-permute-start.17 = (s16[272,256]{1,0:T(8,128)(2,1)S(1)}, s16[272,256]{1,0:T(8,128)(2,1)S(1)}, u32[]{:S(2)}, u32[]{:S(2)}) collective-permute-start(s16[272,256]{1,0:T(8,128)(2,1)S(1)} %get-tuple-element.38), channel_id=1, source_target_pairs={{0,24},{8,16},{16,8},{24,0},{1,25},{9,17},{17,9},{25,1},{2,26},{10... | collective-permute-start | bytes 417800 | tf_op jit(solution)/shard_map/ppermute | solution.py:230
  68.7 6.7 %collective-permute-start.18 = (bf16[304,256]{1,0:T(8,128)(2,1)S(1)}, bf16[304,256]{1,0:T(8,128)(2,1)S(1)}, u32[]{:S(2)}, u32[]{:S(2)}) collective-permute-start(bf16[304,256]{1,0:T(8,128)(2,1)S(1)} %get-tuple-element.43), channel_id=1, source_target_pairs={{0,8},{8,0},{16,24},{24,16},{1,9},{9,1},{17,25},{25,17},{2,10},{10... | collective-permute-start | bytes 466952 | tf_op jit(solution)/shard_map/ppermute | solution.py:230
  69.6 6.9 %collective-permute-start.19 = (bf16[304,256]{1,0:T(8,128)(2,1)S(1)}, bf16[304,256]{1,0:T(8,128)(2,1)S(1)}, u32[]{:S(2)}, u32[]{:S(2)}) collective-permute-start(bf16[304,256]{1,0:T(8,128)(2,1)S(1)} %get-tuple-element.44), channel_id=1, source_target_pairs={{0,16},{8,24},{16,0},{24,8},{1,17},{9,25},{17,1},{25,9},{2,18},{10... | collective-permute-start | bytes 466952 | tf_op jit(solution)/shard_map/ppermute | solution.py:230
  70.1 6.4 %collective-permute-start.20 = (bf16[304,256]{1,0:T(8,128)(2,1)S(1)}, bf16[304,256]{1,0:T(8,128)(2,1)S(1)}, u32[]{:S(2)}, u32[]{:S(2)}) collective-permute-start(bf16[304,256]{1,0:T(8,128)(2,1)S(1)} %get-tuple-element.45), channel_id=1, source_target_pairs={{0,24},{8,16},{16,8},{24,0},{1,25},{9,17},{17,9},{25,1},{2,26},{10... | collective-permute-start | bytes 466952 | tf_op jit(solution)/shard_map/ppermute | solution.py:230
  78.4 1.4 %collective-permute-start.21 = (f32[88,256]{1,0:T(8,128)S(1)}, f32[88,256]{1,0:T(8,128)S(1)}, u32[]{:S(2)}, u32[]{:S(2)}) collective-permute-start(f32[88,256]{1,0:T(8,128)S(1)} %pad_maximum_fusion.5), channel_id=1, source_target_pairs={{0,1},{1,0},{2,3},{3,2},{4,5},{5,4},{6,7},{7,6},{8,9},{9,8},{10,11... | collective-permute-start | bytes 270344 | tf_op jit(solution)/shard_map/ppermute | solution.py:244
  79.7 4.6 %collective-permute-start.22 = (bf16[88,256]{1,0:T(8,128)(2,1)S(1)}, bf16[88,256]{1,0:T(8,128)(2,1)S(1)}, u32[]{:S(2)}, u32[]{:S(2)}) collective-permute-start(bf16[88,256]{1,0:T(8,128)(2,1)S(1)} %fusion.11), channel_id=1, source_target_pairs={{0,2},{1,3},{2,0},{3,1},{4,6},{5,7},{6,4},{7,5},{8,10},{9,11},{10,... | collective-permute-start | bytes 135176 | tf_op jit(solution)/shard_map/ppermute | solution.py:244
  79.8 7.1 %collective-permute-start.23 = (bf16[88,256]{1,0:T(8,128)(2,1)S(1)}, bf16[88,256]{1,0:T(8,128)(2,1)S(1)}, u32[]{:S(2)}, u32[]{:S(2)}) collective-permute-start(bf16[88,256]{1,0:T(8,128)(2,1)S(1)} %fusion.11), channel_id=1, source_target_pairs={{0,4},{1,5},{2,6},{3,7},{4,0},{5,1},{6,2},{7,3},{8,12},{9,13},{10,... | collective-permute-start | bytes 135176 | tf_op jit(solution)/shard_map/ppermute | solution.py:244
  80.4 6.5 %collective-permute-start.24 = (bf16[88,256]{1,0:T(8,128)(2,1)S(1)}, bf16[88,256]{1,0:T(8,128)(2,1)S(1)}, u32[]{:S(2)}, u32[]{:S(2)}) collective-permute-start(bf16[88,256]{1,0:T(8,128)(2,1)S(1)} %fusion.11), channel_id=1, source_target_pairs={{0,6},{1,7},{2,4},{3,5},{4,2},{5,3},{6,0},{7,1},{8,14},{9,15},{10,... | collective-permute-start | bytes 135176 | tf_op jit(solution)/shard_map/ppermute | solution.py:244
  86.9 4.3 %collective-permute-start.25 = (bf16[88,256]{1,0:T(8,128)(2,1)S(1)}, bf16[88,256]{1,0:T(8,128)(2,1)S(1)}, u32[]{:S(2)}, u32[]{:S(2)}) collective-permute-start(bf16[88,256]{1,0:T(8,128)(2,1)S(1)} %add_convert_fusion), channel_id=1, source_target_pairs={{0,8},{8,0},{16,24},{24,16},{1,9},{9,1},{17,25},{25,17},{2,10},{10... | collective-permute-start | bytes 135176 | tf_op jit(solution)/shard_map/ppermute | solution.py:230
  88.2 4.0 %collective-permute-start.26 = (bf16[88,256]{1,0:T(8,128)(2,1)S(1)}, bf16[88,256]{1,0:T(8,128)(2,1)S(1)}, u32[]{:S(2)}, u32[]{:S(2)}) collective-permute-start(bf16[88,256]{1,0:T(8,128)(2,1)S(1)} %add_convert_fusion), channel_id=1, source_target_pairs={{0,16},{8,24},{16,0},{24,8},{1,17},{9,25},{17,1},{25,9},{2,18},{10... | collective-permute-start | bytes 135176 | tf_op jit(solution)/shard_map/ppermute | solution.py:230
  89.5 4.9 %collective-permute-start.27 = (bf16[88,256]{1,0:T(8,128)(2,1)S(1)}, bf16[88,256]{1,0:T(8,128)(2,1)S(1)}, u32[]{:S(2)}, u32[]{:S(2)}) collective-permute-start(bf16[88,256]{1,0:T(8,128)(2,1)S(1)} %add_convert_fusion), channel_id=1, source_target_pairs={{0,24},{8,16},{16,8},{24,0},{1,25},{9,17},{17,9},{25,1},{2,26},{10... | collective-permute-start | bytes 135176 | tf_op jit(solution)/shard_map/ppermute | solution.py:230
  94.5 1.5 %collective-permute-start.28 = (f32[160,256]{1,0:T(8,128)S(1)}, f32[160,256]{1,0:T(8,128)S(1)}, u32[]{:S(2)}, u32[]{:S(2)}) collective-permute-start(f32[160,256]{1,0:T(8,128)S(1)} %constant_dynamic-update-slice_fusion.7.total_ref), channel_id=1, source_target_pairs={{0,1},{1,0},{2,3},{3,2},{4,5},{5,4},{6,7},{7,6},{8,9},{9,8},{10,11... | collective-permute-start | bytes 491528 | tf_op jit(solution)/shard_map/ppermute | solution.py:244
  (5 other events, 45.7 us)

commit v12 on v11

--- a/solution.py
+++ b/solution.py
@@ -153,13 +153,12 @@
 
 def dense_kernel(per_rep, tile_side, turn, meta_ref, tiles_ref, dense_ref):
     section = pl.program_id(0)
-    sections = pl.num_programs(0)
-    rep_index, source_rep = meta_ref[0], meta_ref[1 + section]
-    slots, edge = tiles_ref.shape[1], tiles_ref.shape[-1]
+    rep_index, source_rep = meta_ref[section, 0], meta_ref[section, 1]
+    edge = tiles_ref.shape[-1]
     dense_ref[...] = jnp.zeros_like(dense_ref)
 
     def put(slot, carried):
-        place = meta_ref[1 + 2 * sections + section * slots + slot]
+        place = meta_ref[section, 3 + slot]
         row = place // tile_side
         column = place % tile_side
         row = ((row // per_rep) ^ rep_index) * per_rep + row % per_rep
@@ -173,7 +172,7 @@
             dense_ref[rows, columns] = tile
         return carried
 
-    lax.fori_loop(0, meta_ref[1 + sections + section], put, 0)
+    lax.fori_loop(0, meta_ref[section, 2], put, 0)
 
 
 def build_dense(tiles, meta, own_rows, group_rows, turn):
@@ -297,8 +296,9 @@
     tiles = tile_values[0, 0]
     next_rep = lax.rem(rep_index + 1, reps)
     where = jnp.where(member < jnp.arange(sections + 1) - 1, next_rep, rep_index)
-    meta = jnp.concatenate([where, count, place.reshape(-1)])
-    meta, arrived[0] = lax.optimization_barrier((meta, arrived[0]))
+    where, arrived[0] = lax.optimization_barrier((where, arrived[0]))
+    columns = [jnp.broadcast_to(where[0], (sections, 1)), where[1:, None], count[:, None], place]
+    meta = jnp.concatenate(columns, axis=1)
     dense = build_dense(tiles, meta, own_rows, group_rows, False)
     pieces = [
         half[d * stride : (d + 1) * stride] for half in to_all(arrived) for d in range(reps // 2)
@@ -309,6 +309,7 @@
     kept = keep_mask(id_columns[:, None], units[None, :])
     chunks = dot(dense, feature_columns).reshape(reps, own_rows, width)
     arrived = [swap(chunks[delta], delta) for delta in range(1, reps)]
+    kept, arrived = lax.optimization_barrier((kept, arrived))
     total = chunks[0]
     for part in arrived:
         total = total + part

time: 97.5 us -> 97.1 us (level)
  starting transfers between devices: 45 us -> 43.8 us
  transfers between devices with their start and end apart: 29 -> 29, of which waited for: 17 -> 18; matrix products, arithmetic and copies ran while one was open for 5% -> 5% of each run, Pallas kernels for 5% -> 5%
where the time goes in v12:
time: 97.1 us; the launch traced here: 96.9 us
  starting transfers between devices  43.8 us (45%)
  waiting for transfers between devices  30.6 us (32%)
  Pallas kernels  8.3 us (9%)
  matrix products  6.04 us (6%)
  other arithmetic  3.66 us (4%)
  local copies, waits for them, and re-layouts  3.3 us (3%)
  between operations  1.18 us (1%)
    ppermute x12, starting transfers between devices, swap(): return lax.ppermute(value, 'rep', [(r, r ^ delta) for r in range(reps)])  20.9 us
    ppermute x8, starting transfers between devices, to_pieces(): pieces.append(lax.ppermute(value, ('rep', 'blk'), pairs))  17.2 us
    ppermute x12, waiting for transfers between devices, swap(): return lax.ppermute(value, 'rep', [(r, r ^ delta) for r in range(reps)])  14.5 us
    ppermute x4, waiting for transfers between devices, to_section(): return lax.ppermute(block, ('rep', 'blk'), pairs)  6.7 us
    dot_general x5, matrix products, dot(): return jnp.dot(left, right, preferred_element_type=jnp.float32)  5.68 us
    pallas_call x2, Pallas kernels, build_dense(): pl.pallas_call(body, grid_spec=pltpu.PrefetchScalarGridSpec(num_scalar_pr...  5.26 us
    ppermute x8, waiting for transfers between devices, to_pieces(): pieces.append(lax.ppermute(value, ('rep', 'blk'), pairs))  4.87 us
    ppermute x5, starting transfers between devices, exchange(): return lax.ppermute(value, 'blk', [(c, c ^ delta) for c in range(blks)])  4.59 us
  transfers between devices with their start and end apart: 29, of which 18 were waited for; matrix products, arithmetic and copies ran while one was open for 5% of the time, Pallas kernels for 5%

profile of v12, /device:TPU:0, one launch (start us, length us, event | category | flops | bytes accessed | tf_op | source)
XLA Modules:
  0.0 96.9 jit_solution(6539382224795828391)
XLA Ops:
  2.9 6.8 %collective-permute-start.1 = (bf16[272,128]{1,0:T(8,128)(2,1)S(1)}, bf16[272,128]{1,0:T(8,128)(2,1)S(1)}, u32[]{:S(2)}, u32[]{:S(2)}) collective-permute-start(bf16[272,128]{1,0:T(8,128)(2,1)S(1)} %pad_maximum_fusion.6), channel_id=1, source_target_pairs={{0,10},{1,11},{2,12},{3,13},{4,14},{5,15},{6,8},{7,9},{8,0},{9,1},... | collective-permute-start | bytes 208904 | tf_op jit(solution)/shard_map/ppermute | solution.py:253
  9.7 1.3 %collective-permute-start.2 = (bf16[272,128]{1,0:T(8,128)(2,1)S(1)}, bf16[272,128]{1,0:T(8,128)(2,1)S(1)}, u32[]{:S(2)}, u32[]{:S(2)}) collective-permute-start(bf16[272,128]{1,0:T(8,128)(2,1)S(1)} %pad_maximum_fusion.6), channel_id=1, source_target_pairs={{0,20},{1,21},{2,22},{3,23},{4,16},{5,17},{6,18},{7,19},{8,30},{9,... | collective-permute-start | bytes 208904 | tf_op jit(solution)/shard_map/ppermute | solution.py:253
  11.0 3.0 %collective-permute-start.3 = (bf16[272,128]{1,0:T(8,128)(2,1)S(1)}, bf16[272,128]{1,0:T(8,128)(2,1)S(1)}, u32[]{:S(2)}, u32[]{:S(2)}) collective-permute-start(bf16[272,128]{1,0:T(8,128)(2,1)S(1)} %pad_maximum_fusion.6), channel_id=1, source_target_pairs={{0,30},{1,31},{2,24},{3,25},{4,26},{5,27},{6,28},{7,29},{8,20},{9,... | collective-permute-start | bytes 208904 | tf_op jit(solution)/shard_map/ppermute | solution.py:253
  15.2 1.1 %collective-permute-done.3 = bf16[272,128]{1,0:T(8,128)(2,1)S(1)} collective-permute-done((bf16[272,128]{1,0:T(8,128)(2,1)S(1)}, bf16[272,128]{1,0:T(8,128)(2,1)S(1)}, u32[]{:S(2)}, u32[]{:S(2)}) %collective-permute-start.3) | collective-permute-done | bytes 69664 | tf_op jit(solution)/shard_map/ppermute | solution.py:253
  18.1 1.2 %copy-done.1 = bf16[1,1,2,16,128,128]{5,4,3,2,1,0:T(8,128)(2,1)S(1)} copy-done((bf16[1,1,2,16,128,128]{5,4,3,2,1,0:T(8,128)(2,1)S(1)}, bf16[1,1,2,16,128,128]{5,4,3,2,1,0:T(8,128)(2,1)}, u32[]{:S(2)}) %copy-start.1) | copy-done | bytes 1048600
  19.4 2.1 %dense.1 = bf16[1024,2048]{1,0:T(8,128)(2,1)S(1)} custom-call(s32[2,19]{1,0:T(2,128)S(1)} %pad_add_fusion.meta_ref, bf16[2,16,128,128]{3,2,1,0:T(8,128)(2,1)S(1)} %bitcast.45), custom_call_target="tpu_custom_call" | custom-call | bytes 8388608 | tf_op jit(solution)/shard_map/dense/pallas_call | solution.py:183
  21.7 1.2 %collective-permute-done.5 = bf16[544,128]{1,0:T(8,128)(2,1)S(1)} collective-permute-done((bf16[544,128]{1,0:T(8,128)(2,1)S(1)}, bf16[544,128]{1,0:T(8,128)(2,1)S(1)}, u32[]{:S(2)}, u32[]{:S(2)}) %collective-permute-start.5) | collective-permute-done | bytes 139296 | tf_op jit(solution)/shard_map/ppermute | solution.py:240
  22.9 1.3 %fusion.18 = f32[1024,128]{1,0:T(8,128)S(1)} fusion(bf16[1024,2048]{1,0:T(8,128)(2,1)S(1)} %dense.1, bf16[2048,128]{1,0:T(8,128)(2,1)S(1)} %slice_dynamic-update-slice_fusion), kind=kOutput, calls=%fused_computation.75 | convolution fusion | flops 536870912 | bytes 5242880 | tf_op jit(solution)/shard_map/dot_general | solution.py:32
  24.2 5.3 %collective-permute-start.6 = (f32[256,128]{1,0:T(8,128)S(1)}, f32[256,128]{1,0:T(8,128)S(1)}, u32[]{:S(2)}, u32[]{:S(2)}) collective-permute-start(f32[256,128]{1,0:T(8,128)S(1)} %get-tuple-element.71), channel_id=1, source_target_pairs={{0,8},{8,0},{16,24},{24,16},{1,9},{9,1},{17,25},{25,17},{2,10},{10... | collective-permute-start | bytes 393224 | tf_op jit(solution)/shard_map/ppermute | solution.py:229
  29.4 1.5 %collective-permute-start.8 = (f32[256,128]{1,0:T(8,128)S(1)}, f32[256,128]{1,0:T(8,128)S(1)}, u32[]{:S(2)}, u32[]{:S(2)}) collective-permute-start(f32[256,128]{1,0:T(8,128)S(1)} %get-tuple-element.69), channel_id=1, source_target_pairs={{0,24},{8,16},{16,8},{24,0},{1,25},{9,17},{17,9},{25,1},{2,26},{10... | collective-permute-start | bytes 393224 | tf_op jit(solution)/shard_map/ppermute | solution.py:229
  33.0 4.2 %collective-permute-done.7 = f32[256,128]{1,0:T(8,128)S(1)} collective-permute-done((f32[256,128]{1,0:T(8,128)S(1)}, f32[256,128]{1,0:T(8,128)S(1)}, u32[]{:S(2)}, u32[]{:S(2)}) %collective-permute-start.7) | collective-permute-done | bytes 131104 | tf_op jit(solution)/shard_map/ppermute | solution.py:229
  37.3 4.7 %collective-permute-start.12 = (bf16[256,128]{1,0:T(8,128)(2,1)S(1)}, bf16[256,128]{1,0:T(8,128)(2,1)S(1)}, u32[]{:S(2)}, u32[]{:S(2)}) collective-permute-start(bf16[256,128]{1,0:T(8,128)(2,1)S(1)} %fusion.10), channel_id=1, source_target_pairs={{0,30},{1,31},{2,24},{3,25},{4,26},{5,27},{6,28},{7,29},{8,20},{9,... | collective-permute-start | bytes 196616 | tf_op jit(solution)/shard_map/ppermute | solution.py:253
  42.8 1.2 %collective-permute-done.12 = bf16[256,128]{1,0:T(8,128)(2,1)S(1)} collective-permute-done((bf16[256,128]{1,0:T(8,128)(2,1)S(1)}, bf16[256,128]{1,0:T(8,128)(2,1)S(1)}, u32[]{:S(2)}, u32[]{:S(2)}) %collective-permute-start.12) | collective-permute-done | bytes 65568 | tf_op jit(solution)/shard_map/ppermute | solution.py:253
  44.0 2.4 %collective-permute-done.10 = bf16[256,128]{1,0:T(8,128)(2,1)S(1)} collective-permute-done((bf16[256,128]{1,0:T(8,128)(2,1)S(1)}, bf16[256,128]{1,0:T(8,128)(2,1)S(1)}, u32[]{:S(2)}, u32[]{:S(2)}) %collective-permute-start.10) | collective-permute-done | bytes 65568 | tf_op jit(solution)/shard_map/ppermute | solution.py:253
  46.5 5.5 %collective-permute-done.13 = bf16[512,128]{1,0:T(8,128)(2,1)S(1)} collective-permute-done((bf16[512,128]{1,0:T(8,128)(2,1)S(1)}, bf16[512,128]{1,0:T(8,128)(2,1)S(1)}, u32[]{:S(2)}, u32[]{:S(2)}) %collective-permute-start.13) | collective-permute-done | bytes 131104 | tf_op jit(solution)/shard_map/ppermute | solution.py:240
  52.5 1.3 %fusion.19.partial_ref.own_ref = f32[1024,256]{1,0:T(8,128)S(1)} fusion(bf16[1024,2048]{1,0:T(8,128)(2,1)S(1)} %dense.1, bf16[2048,256]{1,0:T(8,128)(2,1)S(1)} %fusion.1), kind=kOutput, calls=%fused_computation.76 | convolution fusion | flops 1073741824 | bytes 6291456 | tf_op jit(solution)/shard_map/dot_general | solution.py:32
  54.3 5.5 %collective-permute-start.15 = (s16[272,256]{1,0:T(8,128)(2,1)S(1)}, s16[272,256]{1,0:T(8,128)(2,1)S(1)}, u32[]{:S(2)}, u32[]{:S(2)}) collective-permute-start(s16[272,256]{1,0:T(8,128)(2,1)S(1)} %get-tuple-element.44), channel_id=1, source_target_pairs={{0,8},{8,0},{16,24},{24,16},{1,9},{9,1},{17,25},{25,17},{2,10},{10... | collective-permute-start | bytes 417800 | tf_op jit(solution)/shard_map/ppermute | solution.py:229
  59.8 1.5 %collective-permute-start.17 = (s16[272,256]{1,0:T(8,128)(2,1)S(1)}, s16[272,256]{1,0:T(8,128)(2,1)S(1)}, u32[]{:S(2)}, u32[]{:S(2)}) collective-permute-start(s16[272,256]{1,0:T(8,128)(2,1)S(1)} %get-tuple-element.46), channel_id=1, source_target_pairs={{0,24},{8,16},{16,8},{24,0},{1,25},{9,17},{17,9},{25,1},{2,26},{10... | collective-permute-start | bytes 417800 | tf_op jit(solution)/shard_map/ppermute | solution.py:229
  61.3 1.4 %fusion.3 = bf16[2048,256]{1,0:T(8,128)(2,1)} fusion(bf16[2048,256]{1,0:T(8,128)(2,1)S(1)} %fusion.7, bf16[2048,128]{1,0:T(8,128)(2,1)S(1)} %constant_dynamic-update-slice_fusion.1, bf16[128,256]{1,0:T(8,128)(2,1)S(1)} %copy-done), kind=kOutput, calls=%fused_computation.8 | convolution fusion | flops 135266304 | bytes 2686976 | tf_op jit(solution)/shard_map/dot_general | solution.py:32
  63.3 3.6 %collective-permute-done.16.refs_1_ = s16[272,256]{1,0:T(8,128)(2,1)S(1)} collective-permute-done((s16[272,256]{1,0:T(8,128)(2,1)S(1)}, s16[272,256]{1,0:T(8,128)(2,1)S(1)}, u32[]{:S(2)}, u32[]{:S(2)}) %collective-permute-start.16) | collective-permute-done | bytes 139296 | tf_op jit(solution)/shard_map/ppermute | solution.py:229
  67.0 1.3 %head.1 = (f32[256,172]{1,0:T(8,128)S(1)}, f32[48,256]{1,0:T(8,128)S(1)}, bf16[304,256]{1,0:T(8,128)(2,1)S(1)}, bf16[304,256]{1,0:T(8,128)(2,1)S(1)}, bf16[304,2...) custom-call(s32[2]{0:T(128)S(1)} %pad_add_fusion.1.spot_ref, bf16[172,256]{1,0:T(8,128)(2,1)S(1)} %bitcast.48, ...), custom_call_target="tpu_custom_call" | custom-call | tf_op jit(solution)/shard_map/head/pallas_call | solution.py:144
  69.7 2.2 %collective-permute-start.20 = (bf16[304,256]{1,0:T(8,128)(2,1)S(1)}, bf16[304,256]{1,0:T(8,128)(2,1)S(1)}, u32[]{:S(2)}, u32[]{:S(2)}) collective-permute-start(bf16[304,256]{1,0:T(8,128)(2,1)S(1)} %get-tuple-element.53), channel_id=1, source_target_pairs={{0,24},{8,16},{16,8},{24,0},{1,25},{9,17},{17,9},{25,1},{2,26},{10... | collective-permute-start | bytes 466952 | tf_op jit(solution)/shard_map/ppermute | solution.py:229
  71.9 3.1 %dense_turned.1 = bf16[2048,1024]{1,0:T(8,128)(2,1)S(1)} custom-call(s32[2,19]{1,0:T(2,128)S(1)} %pad_add_fusion.meta_ref, bf16[2,16,128,128]{3,2,1,0:T(8,128)(2,1)S(1)} %bitcast.46), custom_call_target="tpu_custom_call" | custom-call | bytes 8388608 | tf_op jit(solution)/shard_map/dense_turned/pallas_call | solution.py:183
  76.0 1.3 %fusion.2 = bf16[2048,256]{1,0:T(8,128)(2,1)S(1)} fusion(bf16[2048,1024]{1,0:T(8,128)(2,1)S(1)} %dense_turned.1, bf16[1024,256]{1,0:T(8,128)(2,1)S(1)} %pad_maximum_fusion, bf16[2048,256]{1,0:T(8,128)(2,1)S(1)} %copy-done.7), kind=kOutput, calls=%fused_computation.6 | convolution fusion | flops 1075838976 | bytes 6815744 | tf_op jit(solution)/shard_map/dot_general | solution.py:32
  77.8 1.3 %collective-permute-done.21 = f32[88,256]{1,0:T(8,128)S(1)} collective-permute-done((f32[88,256]{1,0:T(8,128)S(1)}, f32[88,256]{1,0:T(8,128)S(1)}, u32[]{:S(2)}, u32[]{:S(2)}) %collective-permute-start.21) | collective-permute-done | bytes 90144 | tf_op jit(solution)/shard_map/ppermute | solution.py:243
  79.4 4.2 %collective-permute-start.24 = (bf16[88,256]{1,0:T(8,128)(2,1)S(1)}, bf16[88,256]{1,0:T(8,128)(2,1)S(1)}, u32[]{:S(2)}, u32[]{:S(2)}) collective-permute-start(bf16[88,256]{1,0:T(8,128)(2,1)S(1)} %fusion.11), channel_id=1, source_target_pairs={{0,6},{1,7},{2,4},{3,5},{4,2},{5,3},{6,0},{7,1},{8,14},{9,15},{10,... | collective-permute-start | bytes 135176 | tf_op jit(solution)/shard_map/ppermute | solution.py:243
  83.7 2.6 %collective-permute-done.23 = bf16[88,256]{1,0:T(8,128)(2,1)S(1)} collective-permute-done((bf16[88,256]{1,0:T(8,128)(2,1)S(1)}, bf16[88,256]{1,0:T(8,128)(2,1)S(1)}, u32[]{:S(2)}, u32[]{:S(2)}) %collective-permute-start.23) | collective-permute-done | bytes 45088 | tf_op jit(solution)/shard_map/ppermute | solution.py:243
  86.3 1.5 %collective-permute-start.25 = (bf16[88,256]{1,0:T(8,128)(2,1)S(1)}, bf16[88,256]{1,0:T(8,128)(2,1)S(1)}, u32[]{:S(2)}, u32[]{:S(2)}) collective-permute-start(bf16[88,256]{1,0:T(8,128)(2,1)S(1)} %add_convert_fusion), channel_id=1, source_target_pairs={{0,8},{8,0},{16,24},{24,16},{1,9},{9,1},{17,25},{25,17},{2,10},{10... | collective-permute-start | bytes 135176 | tf_op jit(solution)/shard_map/ppermute | solution.py:229
  87.8 1.3 %collective-permute-start.26 = (bf16[88,256]{1,0:T(8,128)(2,1)S(1)}, bf16[88,256]{1,0:T(8,128)(2,1)S(1)}, u32[]{:S(2)}, u32[]{:S(2)}) collective-permute-start(bf16[88,256]{1,0:T(8,128)(2,1)S(1)} %add_convert_fusion), channel_id=1, source_target_pairs={{0,16},{8,24},{16,0},{24,8},{1,17},{9,25},{17,1},{25,9},{2,18},{10... | collective-permute-start | bytes 135176 | tf_op jit(solution)/shard_map/ppermute | solution.py:229
  90.9 1.1 %collective-permute-done.26 = bf16[88,256]{1,0:T(8,128)(2,1)S(1)} collective-permute-done((bf16[88,256]{1,0:T(8,128)(2,1)S(1)}, bf16[88,256]{1,0:T(8,128)(2,1)S(1)}, u32[]{:S(2)}, u32[]{:S(2)}) %collective-permute-start.26) | collective-permute-done | bytes 45088 | tf_op jit(solution)/shard_map/ppermute | solution.py:229
  92.0 2.1 %collective-permute-done.27 = bf16[88,256]{1,0:T(8,128)(2,1)S(1)} collective-permute-done((bf16[88,256]{1,0:T(8,128)(2,1)S(1)}, bf16[88,256]{1,0:T(8,128)(2,1)S(1)}, u32[]{:S(2)}, u32[]{:S(2)}) %collective-permute-start.27) | collective-permute-done | bytes 45088 | tf_op jit(solution)/shard_map/ppermute | solution.py:229
  95.6 1.3 %last.1 = (f32[128,256]{1,0:T(8,128)}, f32[172,256]{1,0:T(8,128)}) custom-call(s32[2]{0:T(128)S(1)} %pad_add_fusion.1.spot_ref, f32[160,256]{1,0:T(8,128)S(1)} %constant_dynamic-update-slice_fusion.7.total_ref, f32[160,256]{1,0:T(8,128)S(1)} %collective-permute-done.28.other_ref), custom_call_target="tpu_custom_call" | custom-call | tf_op jit(solution)/shard_map/last/pallas_call | solution.py:144
  (112 shorter events, 16.5 us)
Async XLA Ops:
  0.6 51.5 %copy-start = (bf16[128,256]{1,0:T(8,128)(2,1)S(1)}, bf16[128,256]{1,0:T(8,128)(2,1)}, u32[]{:S(2)}) copy-start(bf16[128,256]{1,0:T(8,128)(2,1)} %param.17) | copy-start | bytes 196612
  2.2 12.5 %collective-permute-start = (bf16[272,128]{1,0:T(8,128)(2,1)S(1)}, bf16[272,128]{1,0:T(8,128)(2,1)S(1)}, u32[]{:S(2)}, u32[]{:S(2)}) collective-permute-start(bf16[272,128]{1,0:T(8,128)(2,1)S(1)} %pad_maximum_fusion.6), channel_id=1, source_target_pairs={{0,0},{1,1},{2,2},{3,3},{4,4},{5,5},{6,6},{7,7},{8,10},{9,11},{10,... | collective-permute-start | bytes 208904 | tf_op jit(solution)/shard_map/ppermute | solution.py:253
  2.9 11.9 %collective-permute-start.1 = (bf16[272,128]{1,0:T(8,128)(2,1)S(1)}, bf16[272,128]{1,0:T(8,128)(2,1)S(1)}, u32[]{:S(2)}, u32[]{:S(2)}) collective-permute-start(bf16[272,128]{1,0:T(8,128)(2,1)S(1)} %pad_maximum_fusion.6), channel_id=1, source_target_pairs={{0,10},{1,11},{2,12},{3,13},{4,14},{5,15},{6,8},{7,9},{8,0},{9,1},... | collective-permute-start | bytes 208904 | tf_op jit(solution)/shard_map/ppermute | solution.py:253
  9.7 5.4 %collective-permute-start.2 = (bf16[272,128]{1,0:T(8,128)(2,1)S(1)}, bf16[272,128]{1,0:T(8,128)(2,1)S(1)}, u32[]{:S(2)}, u32[]{:S(2)}) collective-permute-start(bf16[272,128]{1,0:T(8,128)(2,1)S(1)} %pad_maximum_fusion.6), channel_id=1, source_target_pairs={{0,20},{1,21},{2,22},{3,23},{4,16},{5,17},{6,18},{7,19},{8,30},{9,... | collective-permute-start | bytes 208904 | tf_op jit(solution)/shard_map/ppermute | solution.py:253
  11.0 5.2 %collective-permute-start.3 = (bf16[272,128]{1,0:T(8,128)(2,1)S(1)}, bf16[272,128]{1,0:T(8,128)(2,1)S(1)}, u32[]{:S(2)}, u32[]{:S(2)}) collective-permute-start(bf16[272,128]{1,0:T(8,128)(2,1)S(1)} %pad_maximum_fusion.6), channel_id=1, source_target_pairs={{0,30},{1,31},{2,24},{3,25},{4,26},{5,27},{6,28},{7,29},{8,20},{9,... | collective-permute-start | bytes 208904 | tf_op jit(solution)/shard_map/ppermute | solution.py:253
  14.8 6.8 %collective-permute-start.4 = (bf16[544,128]{1,0:T(8,128)(2,1)S(1)}, bf16[544,128]{1,0:T(8,128)(2,1)S(1)}, u32[]{:S(2)}, u32[]{:S(2)}) collective-permute-start(bf16[544,128]{1,0:T(8,128)(2,1)S(1)} %pad_maximum_fusion.1), channel_id=1, source_target_pairs={{0,1},{1,24},{2,3},{3,26},{4,5},{5,28},{6,7},{7,30},{8,9},{9,0},{1... | collective-permute-start | bytes 417800 | tf_op jit(solution)/shard_map/ppermute | solution.py:240
  16.3 6.6 %collective-permute-start.5 = (bf16[544,128]{1,0:T(8,128)(2,1)S(1)}, bf16[544,128]{1,0:T(8,128)(2,1)S(1)}, u32[]{:S(2)}, u32[]{:S(2)}) collective-permute-start(bf16[544,128]{1,0:T(8,128)(2,1)S(1)} %pad_maximum_fusion.2), channel_id=1, source_target_pairs={{0,1},{1,24},{2,3},{3,26},{4,5},{5,28},{6,7},{7,30},{8,9},{9,0},{1... | collective-permute-start | bytes 417800 | tf_op jit(solution)/shard_map/ppermute | solution.py:240
  24.2 8.8 %collective-permute-start.6 = (f32[256,128]{1,0:T(8,128)S(1)}, f32[256,128]{1,0:T(8,128)S(1)}, u32[]{:S(2)}, u32[]{:S(2)}) collective-permute-start(f32[256,128]{1,0:T(8,128)S(1)} %get-tuple-element.71), channel_id=1, source_target_pairs={{0,8},{8,0},{16,24},{24,16},{1,9},{9,1},{17,25},{25,17},{2,10},{10... | collective-permute-start | bytes 393224 | tf_op jit(solution)/shard_map/ppermute | solution.py:229
  29.4 7.8 %collective-permute-start.7 = (f32[256,128]{1,0:T(8,128)S(1)}, f32[256,128]{1,0:T(8,128)S(1)}, u32[]{:S(2)}, u32[]{:S(2)}) collective-permute-start(f32[256,128]{1,0:T(8,128)S(1)} %get-tuple-element.70), channel_id=1, source_target_pairs={{0,16},{8,24},{16,0},{24,8},{1,17},{9,25},{17,1},{25,9},{2,18},{10... | collective-permute-start | bytes 393224 | tf_op jit(solution)/shard_map/ppermute | solution.py:229
  29.4 7.8 %collective-permute-start.8 = (f32[256,128]{1,0:T(8,128)S(1)}, f32[256,128]{1,0:T(8,128)S(1)}, u32[]{:S(2)}, u32[]{:S(2)}) collective-permute-start(f32[256,128]{1,0:T(8,128)S(1)} %get-tuple-element.69), channel_id=1, source_target_pairs={{0,24},{8,16},{16,8},{24,0},{1,25},{9,17},{17,9},{25,1},{2,26},{10... | collective-permute-start | bytes 393224 | tf_op jit(solution)/shard_map/ppermute | solution.py:229
  37.2 5.5 %collective-permute-start.11 = (bf16[256,128]{1,0:T(8,128)(2,1)S(1)}, bf16[256,128]{1,0:T(8,128)(2,1)S(1)}, u32[]{:S(2)}, u32[]{:S(2)}) collective-permute-start(bf16[256,128]{1,0:T(8,128)(2,1)S(1)} %fusion.10), channel_id=1, source_target_pairs={{0,20},{1,21},{2,22},{3,23},{4,16},{5,17},{6,18},{7,19},{8,30},{9,... | collective-permute-start | bytes 196616 | tf_op jit(solution)/shard_map/ppermute | solution.py:253
  37.3 6.6 %collective-permute-start.12 = (bf16[256,128]{1,0:T(8,128)(2,1)S(1)}, bf16[256,128]{1,0:T(8,128)(2,1)S(1)}, u32[]{:S(2)}, u32[]{:S(2)}) collective-permute-start(bf16[256,128]{1,0:T(8,128)(2,1)S(1)} %fusion.10), channel_id=1, source_target_pairs={{0,30},{1,31},{2,24},{3,25},{4,26},{5,27},{6,28},{7,29},{8,20},{9,... | collective-permute-start | bytes 196616 | tf_op jit(solution)/shard_map/ppermute | solution.py:253
  42.1 4.3 %collective-permute-start.10 = (bf16[256,128]{1,0:T(8,128)(2,1)S(1)}, bf16[256,128]{1,0:T(8,128)(2,1)S(1)}, u32[]{:S(2)}, u32[]{:S(2)}) collective-permute-start(bf16[256,128]{1,0:T(8,128)(2,1)S(1)} %fusion.10), channel_id=1, source_target_pairs={{0,10},{1,11},{2,12},{3,13},{4,14},{5,15},{6,8},{7,9},{8,0},{9,1},... | collective-permute-start | bytes 196616 | tf_op jit(solution)/shard_map/ppermute | solution.py:253
  42.1 4.3 %collective-permute-start.9 = (bf16[256,128]{1,0:T(8,128)(2,1)S(1)}, bf16[256,128]{1,0:T(8,128)(2,1)S(1)}, u32[]{:S(2)}, u32[]{:S(2)}) collective-permute-start(bf16[256,128]{1,0:T(8,128)(2,1)S(1)} %fusion.10), channel_id=1, source_target_pairs={{0,0},{1,1},{2,2},{3,3},{4,4},{5,5},{6,6},{7,7},{8,10},{9,11},{10,... | collective-permute-start | bytes 196616 | tf_op jit(solution)/shard_map/ppermute | solution.py:253
  43.9 8.1 %collective-permute-start.14 = (bf16[512,128]{1,0:T(8,128)(2,1)S(1)}, bf16[512,128]{1,0:T(8,128)(2,1)S(1)}, u32[]{:S(2)}, u32[]{:S(2)}) collective-permute-start(bf16[512,128]{1,0:T(8,128)(2,1)S(1)} %pad_maximum_fusion.4), channel_id=1, source_target_pairs={{0,1},{1,24},{2,3},{3,26},{4,5},{5,28},{6,7},{7,30},{8,9},{9,0},{1... | collective-permute-start | bytes 393224 | tf_op jit(solution)/shard_map/ppermute | solution.py:240
  46.4 5.6 %collective-permute-start.13 = (bf16[512,128]{1,0:T(8,128)(2,1)S(1)}, bf16[512,128]{1,0:T(8,128)(2,1)S(1)}, u32[]{:S(2)}, u32[]{:S(2)}) collective-permute-start(bf16[512,128]{1,0:T(8,128)(2,1)S(1)} %pad_maximum_fusion.3), channel_id=1, source_target_pairs={{0,1},{1,24},{2,3},{3,26},{4,5},{5,28},{6,7},{7,30},{8,9},{9,0},{1... | collective-permute-start | bytes 393224 | tf_op jit(solution)/shard_map/ppermute | solution.py:240
  53.8 13.2 %copy-start.3 = (bf16[256,172]{0,1:T(8,128)(2,1)S(1)}, bf16[256,172]{0,1:T(8,128)(2,1)}, u32[]{:S(2)}) copy-start(bf16[256,172]{0,1:T(8,128)(2,1)} %param.18) | copy-start | bytes 264196
  53.8 13.1 %copy-start.4 = (f32[172]{0:T(256)S(1)}, f32[172]{0:T(256)}, u32[]{:S(2)}) copy-start(f32[172]{0:T(256)} %param.19) | copy-start | bytes 2068
  54.3 9.0 %collective-permute-start.15 = (s16[272,256]{1,0:T(8,128)(2,1)S(1)}, s16[272,256]{1,0:T(8,128)(2,1)S(1)}, u32[]{:S(2)}, u32[]{:S(2)}) collective-permute-start(s16[272,256]{1,0:T(8,128)(2,1)S(1)} %get-tuple-element.44), channel_id=1, source_target_pairs={{0,8},{8,0},{16,24},{24,16},{1,9},{9,1},{17,25},{25,17},{2,10},{10... | collective-permute-start | bytes 417800 | tf_op jit(solution)/shard_map/ppermute | solution.py:229
  59.7 7.2 %collective-permute-start.16 = (s16[272,256]{1,0:T(8,128)(2,1)S(1)}, s16[272,256]{1,0:T(8,128)(2,1)S(1)}, u32[]{:S(2)}, u32[]{:S(2)}) collective-permute-start(s16[272,256]{1,0:T(8,128)(2,1)S(1)} %get-tuple-element.45), channel_id=1, source_target_pairs={{0,16},{8,24},{16,0},{24,8},{1,17},{9,25},{17,1},{25,9},{2,18},{10... | collective-permute-start | bytes 417800 | tf_op jit(solution)/shard_map/ppermute | solution.py:229
  59.8 7.2 %collective-permute-start.17 = (s16[272,256]{1,0:T(8,128)(2,1)S(1)}, s16[272,256]{1,0:T(8,128)(2,1)S(1)}, u32[]{:S(2)}, u32[]{:S(2)}) collective-permute-start(s16[272,256]{1,0:T(8,128)(2,1)S(1)} %get-tuple-element.46), channel_id=1, source_target_pairs={{0,24},{8,16},{16,8},{24,0},{1,25},{9,17},{17,9},{25,1},{2,26},{10... | collective-permute-start | bytes 417800 | tf_op jit(solution)/shard_map/ppermute | solution.py:229
  68.3 6.7 %collective-permute-start.18 = (bf16[304,256]{1,0:T(8,128)(2,1)S(1)}, bf16[304,256]{1,0:T(8,128)(2,1)S(1)}, u32[]{:S(2)}, u32[]{:S(2)}) collective-permute-start(bf16[304,256]{1,0:T(8,128)(2,1)S(1)} %get-tuple-element.51), channel_id=1, source_target_pairs={{0,8},{8,0},{16,24},{24,16},{1,9},{9,1},{17,25},{25,17},{2,10},{10... | collective-permute-start | bytes 466952 | tf_op jit(solution)/shard_map/ppermute | solution.py:229
  68.9 6.2 %collective-permute-start.19 = (bf16[304,256]{1,0:T(8,128)(2,1)S(1)}, bf16[304,256]{1,0:T(8,128)(2,1)S(1)}, u32[]{:S(2)}, u32[]{:S(2)}) collective-permute-start(bf16[304,256]{1,0:T(8,128)(2,1)S(1)} %get-tuple-element.52), channel_id=1, source_target_pairs={{0,16},{8,24},{16,0},{24,8},{1,17},{9,25},{17,1},{25,9},{2,18},{10... | collective-permute-start | bytes 466952 | tf_op jit(solution)/shard_map/ppermute | solution.py:229
  69.7 6.1 %collective-permute-start.20 = (bf16[304,256]{1,0:T(8,128)(2,1)S(1)}, bf16[304,256]{1,0:T(8,128)(2,1)S(1)}, u32[]{:S(2)}, u32[]{:S(2)}) collective-permute-start(bf16[304,256]{1,0:T(8,128)(2,1)S(1)} %get-tuple-element.53), channel_id=1, source_target_pairs={{0,24},{8,16},{16,8},{24,0},{1,25},{9,17},{17,9},{25,1},{2,26},{10... | collective-permute-start | bytes 466952 | tf_op jit(solution)/shard_map/ppermute | solution.py:229
  77.7 1.4 %collective-permute-start.21 = (f32[88,256]{1,0:T(8,128)S(1)}, f32[88,256]{1,0:T(8,128)S(1)}, u32[]{:S(2)}, u32[]{:S(2)}) collective-permute-start(f32[88,256]{1,0:T(8,128)S(1)} %pad_maximum_fusion.5), channel_id=1, source_target_pairs={{0,1},{1,0},{2,3},{3,2},{4,5},{5,4},{6,7},{7,6},{8,9},{9,8},{10,11... | collective-permute-start | bytes 270344 | tf_op jit(solution)/shard_map/ppermute | solution.py:243
  79.1 4.6 %collective-permute-start.22 = (bf16[88,256]{1,0:T(8,128)(2,1)S(1)}, bf16[88,256]{1,0:T(8,128)(2,1)S(1)}, u32[]{:S(2)}, u32[]{:S(2)}) collective-permute-start(bf16[88,256]{1,0:T(8,128)(2,1)S(1)} %fusion.11), channel_id=1, source_target_pairs={{0,2},{1,3},{2,0},{3,1},{4,6},{5,7},{6,4},{7,5},{8,10},{9,11},{10,... | collective-permute-start | bytes 135176 | tf_op jit(solution)/shard_map/ppermute | solution.py:243
  79.2 7.1 %collective-permute-start.23 = (bf16[88,256]{1,0:T(8,128)(2,1)S(1)}, bf16[88,256]{1,0:T(8,128)(2,1)S(1)}, u32[]{:S(2)}, u32[]{:S(2)}) collective-permute-start(bf16[88,256]{1,0:T(8,128)(2,1)S(1)} %fusion.11), channel_id=1, source_target_pairs={{0,4},{1,5},{2,6},{3,7},{4,0},{5,1},{6,2},{7,3},{8,12},{9,13},{10,... | collective-permute-start | bytes 135176 | tf_op jit(solution)/shard_map/ppermute | solution.py:243
  79.4 6.9 %collective-permute-start.24 = (bf16[88,256]{1,0:T(8,128)(2,1)S(1)}, bf16[88,256]{1,0:T(8,128)(2,1)S(1)}, u32[]{:S(2)}, u32[]{:S(2)}) collective-permute-start(bf16[88,256]{1,0:T(8,128)(2,1)S(1)} %fusion.11), channel_id=1, source_target_pairs={{0,6},{1,7},{2,4},{3,5},{4,2},{5,3},{6,0},{7,1},{8,14},{9,15},{10,... | collective-permute-start | bytes 135176 | tf_op jit(solution)/shard_map/ppermute | solution.py:243
  86.3 4.6 %collective-permute-start.25 = (bf16[88,256]{1,0:T(8,128)(2,1)S(1)}, bf16[88,256]{1,0:T(8,128)(2,1)S(1)}, u32[]{:S(2)}, u32[]{:S(2)}) collective-permute-start(bf16[88,256]{1,0:T(8,128)(2,1)S(1)} %add_convert_fusion), channel_id=1, source_target_pairs={{0,8},{8,0},{16,24},{24,16},{1,9},{9,1},{17,25},{25,17},{2,10},{10... | collective-permute-start | bytes 135176 | tf_op jit(solution)/shard_map/ppermute | solution.py:229
  87.8 4.1 %collective-permute-start.26 = (bf16[88,256]{1,0:T(8,128)(2,1)S(1)}, bf16[88,256]{1,0:T(8,128)(2,1)S(1)}, u32[]{:S(2)}, u32[]{:S(2)}) collective-permute-start(bf16[88,256]{1,0:T(8,128)(2,1)S(1)} %add_convert_fusion), channel_id=1, source_target_pairs={{0,16},{8,24},{16,0},{24,8},{1,17},{9,25},{17,1},{25,9},{2,18},{10... | collective-permute-start | bytes 135176 | tf_op jit(solution)/shard_map/ppermute | solution.py:229
  89.1 4.9 %collective-permute-start.27 = (bf16[88,256]{1,0:T(8,128)(2,1)S(1)}, bf16[88,256]{1,0:T(8,128)(2,1)S(1)}, u32[]{:S(2)}, u32[]{:S(2)}) collective-permute-start(bf16[88,256]{1,0:T(8,128)(2,1)S(1)} %add_convert_fusion), channel_id=1, source_target_pairs={{0,24},{8,16},{16,8},{24,0},{1,25},{9,17},{17,9},{25,1},{2,26},{10... | collective-permute-start | bytes 135176 | tf_op jit(solution)/shard_map/ppermute | solution.py:229
  94.1 1.5 %collective-permute-start.28 = (f32[160,256]{1,0:T(8,128)S(1)}, f32[160,256]{1,0:T(8,128)S(1)}, u32[]{:S(2)}, u32[]{:S(2)}) collective-permute-start(f32[160,256]{1,0:T(8,128)S(1)} %constant_dynamic-update-slice_fusion.7.total_ref), channel_id=1, source_target_pairs={{0,1},{1,0},{2,3},{3,2},{4,5},{5,4},{6,7},{7,6},{8,9},{9,8},{10,11... | collective-permute-start | bytes 491528 | tf_op jit(solution)/shard_map/ppermute | solution.py:243
  (5 other events, 43.7 us)

commit v13 on v12

--- a/solution.py
+++ b/solution.py
@@ -253,12 +253,14 @@
             pieces.append(lax.ppermute(value, ("rep", "blk"), pairs))
         return pieces
 
-    def to_all(pieces):
-        cut = reps // 2
-        halves = [jnp.concatenate(pieces[:cut], axis=0), jnp.concatenate(pieces[cut:], axis=0)]
-        blocks = list(halves)
+    def to_all(pieces, size):
+        parts = [
+            jnp.concatenate(pieces[start : start + size], axis=0)
+            for start in range(0, reps, size)
+        ]
+        blocks = list(parts)
         for j in range(1, sections):
-            blocks += [to_section(half, j) for half in halves]
+            blocks += [to_section(part, j) for part in parts]
         return blocks
 
     side = lax.rem(blk_index, 2)
@@ -301,7 +303,9 @@
     meta = jnp.concatenate(columns, axis=1)
     dense = build_dense(tiles, meta, own_rows, group_rows, False)
     pieces = [
-        half[d * stride : (d + 1) * stride] for half in to_all(arrived) for d in range(reps // 2)
+        half[d * stride : (d + 1) * stride]
+        for half in to_all(arrived, reps // 2)
+        for d in range(reps // 2)
     ]
     id_columns = jnp.concatenate([undo_digits(piece[own_rows:]) for piece in pieces])
     feature_columns = jnp.concatenate([piece[:own_rows] for piece in pieces], axis=0)
@@ -314,7 +318,7 @@
     for part in arrived:
         total = total + part
     z_input = total.astype(bf16)
-    z_columns = jnp.concatenate(to_all(to_pieces(z_input)), axis=0)
+    z_columns = jnp.concatenate(to_all(to_pieces(z_input), 1), axis=0)
     kept, z_columns = lax.optimization_barrier((kept, z_columns))
     third = f32(4.0 / 3.0)
     pre_act = dot(z_columns, weight_in)

time: 97.1 us -> 96.6 us (level)
  waiting for transfers between devices: 30.6 us -> 26 us
  starting transfers between devices: 43.8 us -> 47.8 us
    ppermute x4 -> x6, starting transfers between devices: 1.08 us -> 4.16 us  [to_section(): return lax.ppermute(block, ('rep', 'blk'), pairs)]
    ppermute x4 -> x6, waiting for transfers between devices: 6.7 us -> 3.73 us  [to_section(): return lax.ppermute(block, ('rep', 'blk'), pairs)]
    ppermute x8, waiting for transfers between devices: 4.87 us -> 3.23 us  [to_pieces(): pieces.append(lax.ppermute(value, ('rep', 'blk'), pairs))]
    ppermute x8, starting transfers between devices: 17.2 us -> 18.6 us  [to_pieces(): pieces.append(lax.ppermute(value, ('rep', 'blk'), pairs))]
    unnamed x29 -> x31, local copies, waits for them, and re-layouts: 2.22 us -> 2.24 us
  transfers between devices with their start and end apart: 29 -> 31, of which waited for: 18 -> 19; matrix products, arithmetic and copies ran while one was open for 5% -> 5% of each run, Pallas kernels for 5% -> 5%
where the time goes in v13:
time: 96.6 us; the launch traced here: 96.3 us
  starting transfers between devices  47.8 us (49%)
  waiting for transfers between devices  26 us (27%)
  Pallas kernels  8.3 us (9%)
  matrix products  6.03 us (6%)
  other arithmetic  3.65 us (4%)
  local copies, waits for them, and re-layouts  3.31 us (3%)
  between operations  1.14 us (1%)
    ppermute x12, starting transfers between devices, swap(): return lax.ppermute(value, 'rep', [(r, r ^ delta) for r in range(reps)])  20.4 us
    ppermute x8, starting transfers between devices, to_pieces(): pieces.append(lax.ppermute(value, ('rep', 'blk'), pairs))  18.6 us
    ppermute x12, waiting for transfers between devices, swap(): return lax.ppermute(value, 'rep', [(r, r ^ delta) for r in range(reps)])  14.3 us
    dot_general x5, matrix products, dot(): return jnp.dot(left, right, preferred_element_type=jnp.float32)  5.67 us
    pallas_call x2, Pallas kernels, build_dense(): pl.pallas_call(body, grid_spec=pltpu.PrefetchScalarGridSpec(num_scalar_pr...  5.26 us
    ppermute x5, waiting for transfers between devices, exchange(): return lax.ppermute(value, 'blk', [(c, c ^ delta) for c in range(blks)])  4.71 us
    ppermute x5, starting transfers between devices, exchange(): return lax.ppermute(value, 'blk', [(c, c ^ delta) for c in range(blks)])  4.59 us
    ppermute x6, starting transfers between devices, to_section(): return lax.ppermute(block, ('rep', 'blk'), pairs)  4.16 us
  transfers between devices with their start and end apart: 31, of which 19 were waited for; matrix products, arithmetic and copies ran while one was open for 5% of the time, Pallas kernels for 5%

profile of v13, /device:TPU:0, one launch (start us, length us, event | category | flops | bytes accessed | tf_op | source)
XLA Modules:
  0.0 96.3 jit_solution(8803310872388439416)
XLA Ops:
  2.9 6.8 %collective-permute-start.1 = (bf16[272,128]{1,0:T(8,128)(2,1)S(1)}, bf16[272,128]{1,0:T(8,128)(2,1)S(1)}, u32[]{:S(2)}, u32[]{:S(2)}) collective-permute-start(bf16[272,128]{1,0:T(8,128)(2,1)S(1)} %pad_maximum_fusion.4), channel_id=1, source_target_pairs={{0,10},{1,11},{2,12},{3,13},{4,14},{5,15},{6,8},{7,9},{8,0},{9,1},... | collective-permute-start | bytes 208904 | tf_op jit(solution)/shard_map/ppermute | solution.py:253
  9.7 1.3 %collective-permute-start.2 = (bf16[272,128]{1,0:T(8,128)(2,1)S(1)}, bf16[272,128]{1,0:T(8,128)(2,1)S(1)}, u32[]{:S(2)}, u32[]{:S(2)}) collective-permute-start(bf16[272,128]{1,0:T(8,128)(2,1)S(1)} %pad_maximum_fusion.4), channel_id=1, source_target_pairs={{0,20},{1,21},{2,22},{3,23},{4,16},{5,17},{6,18},{7,19},{8,30},{9,... | collective-permute-start | bytes 208904 | tf_op jit(solution)/shard_map/ppermute | solution.py:253
  11.0 3.0 %collective-permute-start.3 = (bf16[272,128]{1,0:T(8,128)(2,1)S(1)}, bf16[272,128]{1,0:T(8,128)(2,1)S(1)}, u32[]{:S(2)}, u32[]{:S(2)}) collective-permute-start(bf16[272,128]{1,0:T(8,128)(2,1)S(1)} %pad_maximum_fusion.4), channel_id=1, source_target_pairs={{0,30},{1,31},{2,24},{3,25},{4,26},{5,27},{6,28},{7,29},{8,20},{9,... | collective-permute-start | bytes 208904 | tf_op jit(solution)/shard_map/ppermute | solution.py:253
  18.1 1.2 %copy-done.1 = bf16[1,1,2,16,128,128]{5,4,3,2,1,0:T(8,128)(2,1)S(1)} copy-done((bf16[1,1,2,16,128,128]{5,4,3,2,1,0:T(8,128)(2,1)S(1)}, bf16[1,1,2,16,128,128]{5,4,3,2,1,0:T(8,128)(2,1)}, u32[]{:S(2)}) %copy-start.1) | copy-done | bytes 1048600
  19.4 2.1 %dense.1 = bf16[1024,2048]{1,0:T(8,128)(2,1)S(1)} custom-call(s32[2,19]{1,0:T(2,128)S(1)} %pad_add_fusion.meta_ref, bf16[2,16,128,128]{3,2,1,0:T(8,128)(2,1)S(1)} %bitcast.45), custom_call_target="tpu_custom_call" | custom-call | bytes 8388608 | tf_op jit(solution)/shard_map/dense/pallas_call | solution.py:183
  21.7 1.2 %collective-permute-done.5 = bf16[544,128]{1,0:T(8,128)(2,1)S(1)} collective-permute-done((bf16[544,128]{1,0:T(8,128)(2,1)S(1)}, bf16[544,128]{1,0:T(8,128)(2,1)S(1)}, u32[]{:S(2)}, u32[]{:S(2)}) %collective-permute-start.5) | collective-permute-done | bytes 139296 | tf_op jit(solution)/shard_map/ppermute | solution.py:240
  22.9 1.3 %fusion.18 = f32[1024,128]{1,0:T(8,128)S(1)} fusion(bf16[1024,2048]{1,0:T(8,128)(2,1)S(1)} %dense.1, bf16[2048,128]{1,0:T(8,128)(2,1)S(1)} %slice_dynamic-update-slice_fusion), kind=kOutput, calls=%fused_computation.75 | convolution fusion | flops 536870912 | bytes 5242880 | tf_op jit(solution)/shard_map/dot_general | solution.py:32
  24.2 5.3 %collective-permute-start.6 = (f32[256,128]{1,0:T(8,128)S(1)}, f32[256,128]{1,0:T(8,128)S(1)}, u32[]{:S(2)}, u32[]{:S(2)}) collective-permute-start(f32[256,128]{1,0:T(8,128)S(1)} %get-tuple-element.71), channel_id=1, source_target_pairs={{0,8},{8,0},{16,24},{24,16},{1,9},{9,1},{17,25},{25,17},{2,10},{10... | collective-permute-start | bytes 393224 | tf_op jit(solution)/shard_map/ppermute | solution.py:229
  29.4 1.5 %collective-permute-start.8 = (f32[256,128]{1,0:T(8,128)S(1)}, f32[256,128]{1,0:T(8,128)S(1)}, u32[]{:S(2)}, u32[]{:S(2)}) collective-permute-start(f32[256,128]{1,0:T(8,128)S(1)} %get-tuple-element.69), channel_id=1, source_target_pairs={{0,24},{8,16},{16,8},{24,0},{1,25},{9,17},{17,9},{25,1},{2,26},{10... | collective-permute-start | bytes 393224 | tf_op jit(solution)/shard_map/ppermute | solution.py:229
  33.0 4.2 %collective-permute-done.7 = f32[256,128]{1,0:T(8,128)S(1)} collective-permute-done((f32[256,128]{1,0:T(8,128)S(1)}, f32[256,128]{1,0:T(8,128)S(1)}, u32[]{:S(2)}, u32[]{:S(2)}) %collective-permute-start.7) | collective-permute-done | bytes 131104 | tf_op jit(solution)/shard_map/ppermute | solution.py:229
  38.9 4.2 %collective-permute-start.11 = (bf16[256,128]{1,0:T(8,128)(2,1)S(1)}, bf16[256,128]{1,0:T(8,128)(2,1)S(1)}, u32[]{:S(2)}, u32[]{:S(2)}) collective-permute-start(bf16[256,128]{1,0:T(8,128)(2,1)S(1)} %fusion.10), channel_id=1, source_target_pairs={{0,20},{1,21},{2,22},{3,23},{4,16},{5,17},{6,18},{7,19},{8,30},{9,... | collective-permute-start | bytes 196616 | tf_op jit(solution)/shard_map/ppermute | solution.py:253
  43.1 1.1 %collective-permute-start.12 = (bf16[256,128]{1,0:T(8,128)(2,1)S(1)}, bf16[256,128]{1,0:T(8,128)(2,1)S(1)}, u32[]{:S(2)}, u32[]{:S(2)}) collective-permute-start(bf16[256,128]{1,0:T(8,128)(2,1)S(1)} %fusion.10), channel_id=1, source_target_pairs={{0,30},{1,31},{2,24},{3,25},{4,26},{5,27},{6,28},{7,29},{8,20},{9,... | collective-permute-start | bytes 196616 | tf_op jit(solution)/shard_map/ppermute | solution.py:253
  44.2 2.0 %collective-permute-start.14 = (bf16[256,128]{1,0:T(8,128)(2,1)S(1)}, bf16[256,128]{1,0:T(8,128)(2,1)S(1)}, u32[]{:S(2)}, u32[]{:S(2)}) collective-permute-start(bf16[256,128]{1,0:T(8,128)(2,1)S(1)} %collective-permute-done.10), channel_id=1, source_target_pairs={{0,1},{1,24},{2,3},{3,26},{4,5},{5,28},{6,7},{7,30},{8,9},{9,0},{1... | collective-permute-start | bytes 196616 | tf_op jit(solution)/shard_map/ppermute | solution.py:240
  46.4 1.9 %collective-permute-done.12 = bf16[256,128]{1,0:T(8,128)(2,1)S(1)} collective-permute-done((bf16[256,128]{1,0:T(8,128)(2,1)S(1)}, bf16[256,128]{1,0:T(8,128)(2,1)S(1)}, u32[]{:S(2)}, u32[]{:S(2)}) %collective-permute-start.12) | collective-permute-done | bytes 65568 | tf_op jit(solution)/shard_map/ppermute | solution.py:253
  50.0 2.0 %collective-permute-done.16 = bf16[256,128]{1,0:T(8,128)(2,1)S(1)} collective-permute-done((bf16[256,128]{1,0:T(8,128)(2,1)S(1)}, bf16[256,128]{1,0:T(8,128)(2,1)S(1)}, u32[]{:S(2)}, u32[]{:S(2)}) %collective-permute-start.16) | collective-permute-done | bytes 65568 | tf_op jit(solution)/shard_map/ppermute | solution.py:240
  52.4 1.3 %fusion.19.partial_ref.own_ref = f32[1024,256]{1,0:T(8,128)S(1)} fusion(bf16[1024,2048]{1,0:T(8,128)(2,1)S(1)} %dense.1, bf16[2048,256]{1,0:T(8,128)(2,1)S(1)} %fusion.1), kind=kOutput, calls=%fused_computation.76 | convolution fusion | flops 1073741824 | bytes 6291456 | tf_op jit(solution)/shard_map/dot_general | solution.py:32
  54.2 5.0 %collective-permute-start.17 = (s16[272,256]{1,0:T(8,128)(2,1)S(1)}, s16[272,256]{1,0:T(8,128)(2,1)S(1)}, u32[]{:S(2)}, u32[]{:S(2)}) collective-permute-start(s16[272,256]{1,0:T(8,128)(2,1)S(1)} %get-tuple-element.44), channel_id=1, source_target_pairs={{0,8},{8,0},{16,24},{24,16},{1,9},{9,1},{17,25},{25,17},{2,10},{10... | collective-permute-start | bytes 417800 | tf_op jit(solution)/shard_map/ppermute | solution.py:229
  59.2 1.5 %collective-permute-start.19 = (s16[272,256]{1,0:T(8,128)(2,1)S(1)}, s16[272,256]{1,0:T(8,128)(2,1)S(1)}, u32[]{:S(2)}, u32[]{:S(2)}) collective-permute-start(s16[272,256]{1,0:T(8,128)(2,1)S(1)} %get-tuple-element.46), channel_id=1, source_target_pairs={{0,24},{8,16},{16,8},{24,0},{1,25},{9,17},{17,9},{25,1},{2,26},{10... | collective-permute-start | bytes 417800 | tf_op jit(solution)/shard_map/ppermute | solution.py:229
  60.7 1.4 %fusion.3 = bf16[2048,256]{1,0:T(8,128)(2,1)} fusion(bf16[2048,256]{1,0:T(8,128)(2,1)S(1)} %fusion.7, bf16[2048,128]{1,0:T(8,128)(2,1)S(1)} %constant_dynamic-update-slice_fusion.1, bf16[128,256]{1,0:T(8,128)(2,1)S(1)} %copy-done), kind=kOutput, calls=%fused_computation.8 | convolution fusion | flops 135266304 | bytes 2686976 | tf_op jit(solution)/shard_map/dot_general | solution.py:32
  62.8 3.6 %collective-permute-done.18.refs_1_ = s16[272,256]{1,0:T(8,128)(2,1)S(1)} collective-permute-done((s16[272,256]{1,0:T(8,128)(2,1)S(1)}, s16[272,256]{1,0:T(8,128)(2,1)S(1)}, u32[]{:S(2)}, u32[]{:S(2)}) %collective-permute-start.18) | collective-permute-done | bytes 139296 | tf_op jit(solution)/shard_map/ppermute | solution.py:229
  66.4 1.3 %head.1 = (f32[256,172]{1,0:T(8,128)S(1)}, f32[48,256]{1,0:T(8,128)S(1)}, bf16[304,256]{1,0:T(8,128)(2,1)S(1)}, bf16[304,256]{1,0:T(8,128)(2,1)S(1)}, bf16[304,2...) custom-call(s32[2]{0:T(128)S(1)} %pad_add_fusion.1.spot_ref, bf16[172,256]{1,0:T(8,128)(2,1)S(1)} %bitcast.48, ...), custom_call_target="tpu_custom_call" | custom-call | tf_op jit(solution)/shard_map/head/pallas_call | solution.py:144
  69.3 2.0 %collective-permute-start.22 = (bf16[304,256]{1,0:T(8,128)(2,1)S(1)}, bf16[304,256]{1,0:T(8,128)(2,1)S(1)}, u32[]{:S(2)}, u32[]{:S(2)}) collective-permute-start(bf16[304,256]{1,0:T(8,128)(2,1)S(1)} %get-tuple-element.53), channel_id=1, source_target_pairs={{0,24},{8,16},{16,8},{24,0},{1,25},{9,17},{17,9},{25,1},{2,26},{10... | collective-permute-start | bytes 466952 | tf_op jit(solution)/shard_map/ppermute | solution.py:229
  71.3 3.1 %dense_turned.1 = bf16[2048,1024]{1,0:T(8,128)(2,1)S(1)} custom-call(s32[2,19]{1,0:T(2,128)S(1)} %pad_add_fusion.meta_ref, bf16[2,16,128,128]{3,2,1,0:T(8,128)(2,1)S(1)} %bitcast.46), custom_call_target="tpu_custom_call" | custom-call | bytes 8388608 | tf_op jit(solution)/shard_map/dense_turned/pallas_call | solution.py:183
  75.6 1.3 %fusion.2 = bf16[2048,256]{1,0:T(8,128)(2,1)S(1)} fusion(bf16[2048,1024]{1,0:T(8,128)(2,1)S(1)} %dense_turned.1, bf16[1024,256]{1,0:T(8,128)(2,1)S(1)} %pad_maximum_fusion, bf16[2048,256]{1,0:T(8,128)(2,1)S(1)} %copy-done.7), kind=kOutput, calls=%fused_computation.6 | convolution fusion | flops 1075838976 | bytes 6815744 | tf_op jit(solution)/shard_map/dot_general | solution.py:32
  77.5 1.3 %collective-permute-done.23 = f32[88,256]{1,0:T(8,128)S(1)} collective-permute-done((f32[88,256]{1,0:T(8,128)S(1)}, f32[88,256]{1,0:T(8,128)S(1)}, u32[]{:S(2)}, u32[]{:S(2)}) %collective-permute-start.23) | collective-permute-done | bytes 90144 | tf_op jit(solution)/shard_map/ppermute | solution.py:243
  78.8 1.3 %collective-permute-start.25 = (bf16[88,256]{1,0:T(8,128)(2,1)S(1)}, bf16[88,256]{1,0:T(8,128)(2,1)S(1)}, u32[]{:S(2)}, u32[]{:S(2)}) collective-permute-start(bf16[88,256]{1,0:T(8,128)(2,1)S(1)} %fusion.11), channel_id=1, source_target_pairs={{0,4},{1,5},{2,6},{3,7},{4,0},{5,1},{6,2},{7,3},{8,12},{9,13},{10,... | collective-permute-start | bytes 135176 | tf_op jit(solution)/shard_map/ppermute | solution.py:243
  80.2 3.0 %collective-permute-start.26 = (bf16[88,256]{1,0:T(8,128)(2,1)S(1)}, bf16[88,256]{1,0:T(8,128)(2,1)S(1)}, u32[]{:S(2)}, u32[]{:S(2)}) collective-permute-start(bf16[88,256]{1,0:T(8,128)(2,1)S(1)} %fusion.11), channel_id=1, source_target_pairs={{0,6},{1,7},{2,4},{3,5},{4,2},{5,3},{6,0},{7,1},{8,14},{9,15},{10,... | collective-permute-start | bytes 135176 | tf_op jit(solution)/shard_map/ppermute | solution.py:243
  83.3 2.1 %collective-permute-done.25 = bf16[88,256]{1,0:T(8,128)(2,1)S(1)} collective-permute-done((bf16[88,256]{1,0:T(8,128)(2,1)S(1)}, bf16[88,256]{1,0:T(8,128)(2,1)S(1)}, u32[]{:S(2)}, u32[]{:S(2)}) %collective-permute-start.25) | collective-permute-done | bytes 45088 | tf_op jit(solution)/shard_map/ppermute | solution.py:243
  86.1 1.5 %collective-permute-start.27 = (bf16[88,256]{1,0:T(8,128)(2,1)S(1)}, bf16[88,256]{1,0:T(8,128)(2,1)S(1)}, u32[]{:S(2)}, u32[]{:S(2)}) collective-permute-start(bf16[88,256]{1,0:T(8,128)(2,1)S(1)} %add_convert_fusion), channel_id=1, source_target_pairs={{0,8},{8,0},{16,24},{24,16},{1,9},{9,1},{17,25},{25,17},{2,10},{10... | collective-permute-start | bytes 135176 | tf_op jit(solution)/shard_map/ppermute | solution.py:229
  88.5 1.1 %collective-permute-start.29 = (bf16[88,256]{1,0:T(8,128)(2,1)S(1)}, bf16[88,256]{1,0:T(8,128)(2,1)S(1)}, u32[]{:S(2)}, u32[]{:S(2)}) collective-permute-start(bf16[88,256]{1,0:T(8,128)(2,1)S(1)} %add_convert_fusion), channel_id=1, source_target_pairs={{0,24},{8,16},{16,8},{24,0},{1,25},{9,17},{17,9},{25,1},{2,26},{10... | collective-permute-start | bytes 135176 | tf_op jit(solution)/shard_map/ppermute | solution.py:229
  91.7 1.8 %collective-permute-done.29 = bf16[88,256]{1,0:T(8,128)(2,1)S(1)} collective-permute-done((bf16[88,256]{1,0:T(8,128)(2,1)S(1)}, bf16[88,256]{1,0:T(8,128)(2,1)S(1)}, u32[]{:S(2)}, u32[]{:S(2)}) %collective-permute-start.29) | collective-permute-done | bytes 45088 | tf_op jit(solution)/shard_map/ppermute | solution.py:229
  95.0 1.3 %last.1 = (f32[128,256]{1,0:T(8,128)}, f32[172,256]{1,0:T(8,128)}) custom-call(s32[2]{0:T(128)S(1)} %pad_add_fusion.1.spot_ref, f32[160,256]{1,0:T(8,128)S(1)} %constant_dynamic-update-slice_fusion.9.total_ref, f32[160,256]{1,0:T(8,128)S(1)} %collective-permute-done.30.other_ref), custom_call_target="tpu_custom_call" | custom-call | tf_op jit(solution)/shard_map/last/pallas_call | solution.py:144
  (116 shorter events, 22.0 us)
Async XLA Ops:
  0.6 51.3 %copy-start = (bf16[128,256]{1,0:T(8,128)(2,1)S(1)}, bf16[128,256]{1,0:T(8,128)(2,1)}, u32[]{:S(2)}) copy-start(bf16[128,256]{1,0:T(8,128)(2,1)} %param.17) | copy-start | bytes 196612
  2.2 12.5 %collective-permute-start = (bf16[272,128]{1,0:T(8,128)(2,1)S(1)}, bf16[272,128]{1,0:T(8,128)(2,1)S(1)}, u32[]{:S(2)}, u32[]{:S(2)}) collective-permute-start(bf16[272,128]{1,0:T(8,128)(2,1)S(1)} %pad_maximum_fusion.4), channel_id=1, source_target_pairs={{0,0},{1,1},{2,2},{3,3},{4,4},{5,5},{6,6},{7,7},{8,10},{9,11},{10,... | collective-permute-start | bytes 208904 | tf_op jit(solution)/shard_map/ppermute | solution.py:253
  2.9 11.9 %collective-permute-start.1 = (bf16[272,128]{1,0:T(8,128)(2,1)S(1)}, bf16[272,128]{1,0:T(8,128)(2,1)S(1)}, u32[]{:S(2)}, u32[]{:S(2)}) collective-permute-start(bf16[272,128]{1,0:T(8,128)(2,1)S(1)} %pad_maximum_fusion.4), channel_id=1, source_target_pairs={{0,10},{1,11},{2,12},{3,13},{4,14},{5,15},{6,8},{7,9},{8,0},{9,1},... | collective-permute-start | bytes 208904 | tf_op jit(solution)/shard_map/ppermute | solution.py:253
  9.7 5.4 %collective-permute-start.2 = (bf16[272,128]{1,0:T(8,128)(2,1)S(1)}, bf16[272,128]{1,0:T(8,128)(2,1)S(1)}, u32[]{:S(2)}, u32[]{:S(2)}) collective-permute-start(bf16[272,128]{1,0:T(8,128)(2,1)S(1)} %pad_maximum_fusion.4), channel_id=1, source_target_pairs={{0,20},{1,21},{2,22},{3,23},{4,16},{5,17},{6,18},{7,19},{8,30},{9,... | collective-permute-start | bytes 208904 | tf_op jit(solution)/shard_map/ppermute | solution.py:253
  11.0 5.2 %collective-permute-start.3 = (bf16[272,128]{1,0:T(8,128)(2,1)S(1)}, bf16[272,128]{1,0:T(8,128)(2,1)S(1)}, u32[]{:S(2)}, u32[]{:S(2)}) collective-permute-start(bf16[272,128]{1,0:T(8,128)(2,1)S(1)} %pad_maximum_fusion.4), channel_id=1, source_target_pairs={{0,30},{1,31},{2,24},{3,25},{4,26},{5,27},{6,28},{7,29},{8,20},{9,... | collective-permute-start | bytes 208904 | tf_op jit(solution)/shard_map/ppermute | solution.py:253
  14.8 6.8 %collective-permute-start.4 = (bf16[544,128]{1,0:T(8,128)(2,1)S(1)}, bf16[544,128]{1,0:T(8,128)(2,1)S(1)}, u32[]{:S(2)}, u32[]{:S(2)}) collective-permute-start(bf16[544,128]{1,0:T(8,128)(2,1)S(1)} %pad_maximum_fusion.1), channel_id=1, source_target_pairs={{0,1},{1,24},{2,3},{3,26},{4,5},{5,28},{6,7},{7,30},{8,9},{9,0},{1... | collective-permute-start | bytes 417800 | tf_op jit(solution)/shard_map/ppermute | solution.py:240
  16.3 6.6 %collective-permute-start.5 = (bf16[544,128]{1,0:T(8,128)(2,1)S(1)}, bf16[544,128]{1,0:T(8,128)(2,1)S(1)}, u32[]{:S(2)}, u32[]{:S(2)}) collective-permute-start(bf16[544,128]{1,0:T(8,128)(2,1)S(1)} %pad_maximum_fusion.2), channel_id=1, source_target_pairs={{0,1},{1,24},{2,3},{3,26},{4,5},{5,28},{6,7},{7,30},{8,9},{9,0},{1... | collective-permute-start | bytes 417800 | tf_op jit(solution)/shard_map/ppermute | solution.py:240
  24.2 8.8 %collective-permute-start.6 = (f32[256,128]{1,0:T(8,128)S(1)}, f32[256,128]{1,0:T(8,128)S(1)}, u32[]{:S(2)}, u32[]{:S(2)}) collective-permute-start(f32[256,128]{1,0:T(8,128)S(1)} %get-tuple-element.71), channel_id=1, source_target_pairs={{0,8},{8,0},{16,24},{24,16},{1,9},{9,1},{17,25},{25,17},{2,10},{10... | collective-permute-start | bytes 393224 | tf_op jit(solution)/shard_map/ppermute | solution.py:229
  29.4 7.8 %collective-permute-start.7 = (f32[256,128]{1,0:T(8,128)S(1)}, f32[256,128]{1,0:T(8,128)S(1)}, u32[]{:S(2)}, u32[]{:S(2)}) collective-permute-start(f32[256,128]{1,0:T(8,128)S(1)} %get-tuple-element.70), channel_id=1, source_target_pairs={{0,16},{8,24},{16,0},{24,8},{1,17},{9,25},{17,1},{25,9},{2,18},{10... | collective-permute-start | bytes 393224 | tf_op jit(solution)/shard_map/ppermute | solution.py:229
  29.4 7.8 %collective-permute-start.8 = (f32[256,128]{1,0:T(8,128)S(1)}, f32[256,128]{1,0:T(8,128)S(1)}, u32[]{:S(2)}, u32[]{:S(2)}) collective-permute-start(f32[256,128]{1,0:T(8,128)S(1)} %get-tuple-element.69), channel_id=1, source_target_pairs={{0,24},{8,16},{16,8},{24,0},{1,25},{9,17},{17,9},{25,1},{2,26},{10... | collective-permute-start | bytes 393224 | tf_op jit(solution)/shard_map/ppermute | solution.py:229
  37.3 6.9 %collective-permute-start.9 = (bf16[256,128]{1,0:T(8,128)(2,1)S(1)}, bf16[256,128]{1,0:T(8,128)(2,1)S(1)}, u32[]{:S(2)}, u32[]{:S(2)}) collective-permute-start(bf16[256,128]{1,0:T(8,128)(2,1)S(1)} %fusion.10), channel_id=1, source_target_pairs={{0,0},{1,1},{2,2},{3,3},{4,4},{5,5},{6,6},{7,7},{8,10},{9,11},{10,... | collective-permute-start | bytes 196616 | tf_op jit(solution)/shard_map/ppermute | solution.py:253
  38.0 6.2 %collective-permute-start.10 = (bf16[256,128]{1,0:T(8,128)(2,1)S(1)}, bf16[256,128]{1,0:T(8,128)(2,1)S(1)}, u32[]{:S(2)}, u32[]{:S(2)}) collective-permute-start(bf16[256,128]{1,0:T(8,128)(2,1)S(1)} %fusion.10), channel_id=1, source_target_pairs={{0,10},{1,11},{2,12},{3,13},{4,14},{5,15},{6,8},{7,9},{8,0},{9,1},... | collective-permute-start | bytes 196616 | tf_op jit(solution)/shard_map/ppermute | solution.py:253
  38.9 7.3 %collective-permute-start.11 = (bf16[256,128]{1,0:T(8,128)(2,1)S(1)}, bf16[256,128]{1,0:T(8,128)(2,1)S(1)}, u32[]{:S(2)}, u32[]{:S(2)}) collective-permute-start(bf16[256,128]{1,0:T(8,128)(2,1)S(1)} %fusion.10), channel_id=1, source_target_pairs={{0,20},{1,21},{2,22},{3,23},{4,16},{5,17},{6,18},{7,19},{8,30},{9,... | collective-permute-start | bytes 196616 | tf_op jit(solution)/shard_map/ppermute | solution.py:253
  43.1 5.2 %collective-permute-start.12 = (bf16[256,128]{1,0:T(8,128)(2,1)S(1)}, bf16[256,128]{1,0:T(8,128)(2,1)S(1)}, u32[]{:S(2)}, u32[]{:S(2)}) collective-permute-start(bf16[256,128]{1,0:T(8,128)(2,1)S(1)} %fusion.10), channel_id=1, source_target_pairs={{0,30},{1,31},{2,24},{3,25},{4,26},{5,27},{6,28},{7,29},{8,20},{9,... | collective-permute-start | bytes 196616 | tf_op jit(solution)/shard_map/ppermute | solution.py:253
  44.2 5.1 %collective-permute-start.13 = (bf16[256,128]{1,0:T(8,128)(2,1)S(1)}, bf16[256,128]{1,0:T(8,128)(2,1)S(1)}, u32[]{:S(2)}, u32[]{:S(2)}) collective-permute-start(bf16[256,128]{1,0:T(8,128)(2,1)S(1)} %collective-permute-done.9), channel_id=1, source_target_pairs={{0,1},{1,24},{2,3},{3,26},{4,5},{5,28},{6,7},{7,30},{8,9},{9,0},{1... | collective-permute-start | bytes 196616 | tf_op jit(solution)/shard_map/ppermute | solution.py:240
  44.2 5.2 %collective-permute-start.14 = (bf16[256,128]{1,0:T(8,128)(2,1)S(1)}, bf16[256,128]{1,0:T(8,128)(2,1)S(1)}, u32[]{:S(2)}, u32[]{:S(2)}) collective-permute-start(bf16[256,128]{1,0:T(8,128)(2,1)S(1)} %collective-permute-done.10), channel_id=1, source_target_pairs={{0,1},{1,24},{2,3},{3,26},{4,5},{5,28},{6,7},{7,30},{8,9},{9,0},{1... | collective-permute-start | bytes 196616 | tf_op jit(solution)/shard_map/ppermute | solution.py:240
  46.2 3.7 %collective-permute-start.15 = (bf16[256,128]{1,0:T(8,128)(2,1)S(1)}, bf16[256,128]{1,0:T(8,128)(2,1)S(1)}, u32[]{:S(2)}, u32[]{:S(2)}) collective-permute-start(bf16[256,128]{1,0:T(8,128)(2,1)S(1)} %collective-permute-done.11), channel_id=1, source_target_pairs={{0,1},{1,24},{2,3},{3,26},{4,5},{5,28},{6,7},{7,30},{8,9},{9,0},{1... | collective-permute-start | bytes 196616 | tf_op jit(solution)/shard_map/ppermute | solution.py:240
  48.3 3.7 %collective-permute-start.16 = (bf16[256,128]{1,0:T(8,128)(2,1)S(1)}, bf16[256,128]{1,0:T(8,128)(2,1)S(1)}, u32[]{:S(2)}, u32[]{:S(2)}) collective-permute-start(bf16[256,128]{1,0:T(8,128)(2,1)S(1)} %collective-permute-done.12), channel_id=1, source_target_pairs={{0,1},{1,24},{2,3},{3,26},{4,5},{5,28},{6,7},{7,30},{8,9},{9,0},{1... | collective-permute-start | bytes 196616 | tf_op jit(solution)/shard_map/ppermute | solution.py:240
  54.2 8.6 %collective-permute-start.17 = (s16[272,256]{1,0:T(8,128)(2,1)S(1)}, s16[272,256]{1,0:T(8,128)(2,1)S(1)}, u32[]{:S(2)}, u32[]{:S(2)}) collective-permute-start(s16[272,256]{1,0:T(8,128)(2,1)S(1)} %get-tuple-element.44), channel_id=1, source_target_pairs={{0,8},{8,0},{16,24},{24,16},{1,9},{9,1},{17,25},{25,17},{2,10},{10... | collective-permute-start | bytes 417800 | tf_op jit(solution)/shard_map/ppermute | solution.py:229
  59.2 7.2 %collective-permute-start.18 = (s16[272,256]{1,0:T(8,128)(2,1)S(1)}, s16[272,256]{1,0:T(8,128)(2,1)S(1)}, u32[]{:S(2)}, u32[]{:S(2)}) collective-permute-start(s16[272,256]{1,0:T(8,128)(2,1)S(1)} %get-tuple-element.45), channel_id=1, source_target_pairs={{0,16},{8,24},{16,0},{24,8},{1,17},{9,25},{17,1},{25,9},{2,18},{10... | collective-permute-start | bytes 417800 | tf_op jit(solution)/shard_map/ppermute | solution.py:229
  59.2 7.2 %collective-permute-start.19 = (s16[272,256]{1,0:T(8,128)(2,1)S(1)}, s16[272,256]{1,0:T(8,128)(2,1)S(1)}, u32[]{:S(2)}, u32[]{:S(2)}) collective-permute-start(s16[272,256]{1,0:T(8,128)(2,1)S(1)} %get-tuple-element.46), channel_id=1, source_target_pairs={{0,24},{8,16},{16,8},{24,0},{1,25},{9,17},{17,9},{25,1},{2,26},{10... | collective-permute-start | bytes 417800 | tf_op jit(solution)/shard_map/ppermute | solution.py:229
  67.7 6.7 %collective-permute-start.20 = (bf16[304,256]{1,0:T(8,128)(2,1)S(1)}, bf16[304,256]{1,0:T(8,128)(2,1)S(1)}, u32[]{:S(2)}, u32[]{:S(2)}) collective-permute-start(bf16[304,256]{1,0:T(8,128)(2,1)S(1)} %get-tuple-element.51), channel_id=1, source_target_pairs={{0,8},{8,0},{16,24},{24,16},{1,9},{9,1},{17,25},{25,17},{2,10},{10... | collective-permute-start | bytes 466952 | tf_op jit(solution)/shard_map/ppermute | solution.py:229
  68.6 6.9 %collective-permute-start.21 = (bf16[304,256]{1,0:T(8,128)(2,1)S(1)}, bf16[304,256]{1,0:T(8,128)(2,1)S(1)}, u32[]{:S(2)}, u32[]{:S(2)}) collective-permute-start(bf16[304,256]{1,0:T(8,128)(2,1)S(1)} %get-tuple-element.52), channel_id=1, source_target_pairs={{0,16},{8,24},{16,0},{24,8},{1,17},{9,25},{17,1},{25,9},{2,18},{10... | collective-permute-start | bytes 466952 | tf_op jit(solution)/shard_map/ppermute | solution.py:229
  69.3 6.2 %collective-permute-start.22 = (bf16[304,256]{1,0:T(8,128)(2,1)S(1)}, bf16[304,256]{1,0:T(8,128)(2,1)S(1)}, u32[]{:S(2)}, u32[]{:S(2)}) collective-permute-start(bf16[304,256]{1,0:T(8,128)(2,1)S(1)} %get-tuple-element.53), channel_id=1, source_target_pairs={{0,24},{8,16},{16,8},{24,0},{1,25},{9,17},{17,9},{25,1},{2,26},{10... | collective-permute-start | bytes 466952 | tf_op jit(solution)/shard_map/ppermute | solution.py:229
  77.4 1.4 %collective-permute-start.23 = (f32[88,256]{1,0:T(8,128)S(1)}, f32[88,256]{1,0:T(8,128)S(1)}, u32[]{:S(2)}, u32[]{:S(2)}) collective-permute-start(f32[88,256]{1,0:T(8,128)S(1)} %pad_maximum_fusion.3), channel_id=1, source_target_pairs={{0,1},{1,0},{2,3},{3,2},{4,5},{5,4},{6,7},{7,6},{8,9},{9,8},{10,11... | collective-permute-start | bytes 270344 | tf_op jit(solution)/shard_map/ppermute | solution.py:243
  78.8 4.6 %collective-permute-start.24 = (bf16[88,256]{1,0:T(8,128)(2,1)S(1)}, bf16[88,256]{1,0:T(8,128)(2,1)S(1)}, u32[]{:S(2)}, u32[]{:S(2)}) collective-permute-start(bf16[88,256]{1,0:T(8,128)(2,1)S(1)} %fusion.11), channel_id=1, source_target_pairs={{0,2},{1,3},{2,0},{3,1},{4,6},{5,7},{6,4},{7,5},{8,10},{9,11},{10,... | collective-permute-start | bytes 135176 | tf_op jit(solution)/shard_map/ppermute | solution.py:243
  78.8 6.6 %collective-permute-start.25 = (bf16[88,256]{1,0:T(8,128)(2,1)S(1)}, bf16[88,256]{1,0:T(8,128)(2,1)S(1)}, u32[]{:S(2)}, u32[]{:S(2)}) collective-permute-start(bf16[88,256]{1,0:T(8,128)(2,1)S(1)} %fusion.11), channel_id=1, source_target_pairs={{0,4},{1,5},{2,6},{3,7},{4,0},{5,1},{6,2},{7,3},{8,12},{9,13},{10,... | collective-permute-start | bytes 135176 | tf_op jit(solution)/shard_map/ppermute | solution.py:243
  80.2 5.9 %collective-permute-start.26 = (bf16[88,256]{1,0:T(8,128)(2,1)S(1)}, bf16[88,256]{1,0:T(8,128)(2,1)S(1)}, u32[]{:S(2)}, u32[]{:S(2)}) collective-permute-start(bf16[88,256]{1,0:T(8,128)(2,1)S(1)} %fusion.11), channel_id=1, source_target_pairs={{0,6},{1,7},{2,4},{3,5},{4,2},{5,3},{6,0},{7,1},{8,14},{9,15},{10,... | collective-permute-start | bytes 135176 | tf_op jit(solution)/shard_map/ppermute | solution.py:243
  86.1 4.6 %collective-permute-start.27 = (bf16[88,256]{1,0:T(8,128)(2,1)S(1)}, bf16[88,256]{1,0:T(8,128)(2,1)S(1)}, u32[]{:S(2)}, u32[]{:S(2)}) collective-permute-start(bf16[88,256]{1,0:T(8,128)(2,1)S(1)} %add_convert_fusion), channel_id=1, source_target_pairs={{0,8},{8,0},{16,24},{24,16},{1,9},{9,1},{17,25},{25,17},{2,10},{10... | collective-permute-start | bytes 135176 | tf_op jit(solution)/shard_map/ppermute | solution.py:229
  87.6 4.0 %collective-permute-start.28 = (bf16[88,256]{1,0:T(8,128)(2,1)S(1)}, bf16[88,256]{1,0:T(8,128)(2,1)S(1)}, u32[]{:S(2)}, u32[]{:S(2)}) collective-permute-start(bf16[88,256]{1,0:T(8,128)(2,1)S(1)} %add_convert_fusion), channel_id=1, source_target_pairs={{0,16},{8,24},{16,0},{24,8},{1,17},{9,25},{17,1},{25,9},{2,18},{10... | collective-permute-start | bytes 135176 | tf_op jit(solution)/shard_map/ppermute | solution.py:229
  88.5 4.9 %collective-permute-start.29 = (bf16[88,256]{1,0:T(8,128)(2,1)S(1)}, bf16[88,256]{1,0:T(8,128)(2,1)S(1)}, u32[]{:S(2)}, u32[]{:S(2)}) collective-permute-start(bf16[88,256]{1,0:T(8,128)(2,1)S(1)} %add_convert_fusion), channel_id=1, source_target_pairs={{0,24},{8,16},{16,8},{24,0},{1,25},{9,17},{17,9},{25,1},{2,26},{10... | collective-permute-start | bytes 135176 | tf_op jit(solution)/shard_map/ppermute | solution.py:229
  93.5 1.5 %collective-permute-start.30 = (f32[160,256]{1,0:T(8,128)S(1)}, f32[160,256]{1,0:T(8,128)S(1)}, u32[]{:S(2)}, u32[]{:S(2)}) collective-permute-start(f32[160,256]{1,0:T(8,128)S(1)} %constant_dynamic-update-slice_fusion.9.total_ref), channel_id=1, source_target_pairs={{0,1},{1,0},{2,3},{3,2},{4,5},{5,4},{6,7},{7,6},{8,9},{9,8},{10,11... | collective-permute-start | bytes 491528 | tf_op jit(solution)/shard_map/ppermute | solution.py:243
  (7 other events, 68.3 us)

commit v14 on v13

--- a/solution.py
+++ b/solution.py
@@ -292,9 +292,7 @@
     member = lax.rem(blk_index, sections)
     place, count = tile_place[0, 0], tile_count[0, 0]
     width = features.shape[2]
-    bundle = jnp.concatenate([features[0], digits(node_ids[0])], axis=0)
-    stride = bundle.shape[0]
-    arrived = to_pieces(bundle)
+    arrived = to_pieces(features[0])
     tiles = tile_values[0, 0]
     next_rep = lax.rem(rep_index + 1, reps)
     where = jnp.where(member < jnp.arange(sections + 1) - 1, next_rep, rep_index)
@@ -302,24 +300,19 @@
     columns = [jnp.broadcast_to(where[0], (sections, 1)), where[1:, None], count[:, None], place]
     meta = jnp.concatenate(columns, axis=1)
     dense = build_dense(tiles, meta, own_rows, group_rows, False)
-    pieces = [
-        half[d * stride : (d + 1) * stride]
-        for half in to_all(arrived, reps // 2)
-        for d in range(reps // 2)
-    ]
-    id_columns = jnp.concatenate([undo_digits(piece[own_rows:]) for piece in pieces])
-    feature_columns = jnp.concatenate([piece[:own_rows] for piece in pieces], axis=0)
-    units = jnp.arange(hidden_width, dtype=jnp.int32)
-    kept = keep_mask(id_columns[:, None], units[None, :])
+    feature_columns = jnp.concatenate(to_all(arrived, reps // 2), axis=0)
     chunks = dot(dense, feature_columns).reshape(reps, own_rows, width)
     arrived = [swap(chunks[delta], delta) for delta in range(1, reps)]
-    kept, arrived = lax.optimization_barrier((kept, arrived))
     total = chunks[0]
     for part in arrived:
         total = total + part
     z_input = total.astype(bf16)
-    z_columns = jnp.concatenate(to_all(to_pieces(z_input), 1), axis=0)
-    kept, z_columns = lax.optimization_barrier((kept, z_columns))
+    z_bundle = jnp.concatenate([z_input, digits(node_ids[0])], axis=0)
+    pieces = to_all(to_pieces(z_bundle), 1)
+    units = jnp.arange(hidden_width, dtype=jnp.int32)
+    id_columns = jnp.concatenate([undo_digits(part[own_rows:]) for part in pieces])
+    kept = keep_mask(id_columns[:, None], units[None, :])
+    z_columns = jnp.concatenate([part[:own_rows] for part in pieces], axis=0)
     third = f32(4.0 / 3.0)
     pre_act = dot(z_columns, weight_in)
     dropped = (jnp.maximum(pre_act, 0.0) * (kept.astype(f32) * third)).astype(bf16)

time: 96.6 us -> 96.3 us (level)
  starting transfers between devices: 47.8 us -> 43.8 us
  waiting for transfers between devices: 26 us -> 28.6 us
  other arithmetic: 3.65 us -> 1.85 us
  local copies, waits for them, and re-layouts: 3.31 us -> 4.87 us
  matrix products: 6.03 us -> 7.36 us
    ppermute x12, starting transfers between devices: 20.4 us -> 15.2 us  [swap(): return lax.ppermute(value, 'rep', [(r, r ^ delta) for r in range(reps)])]
    ppermute x6, starting transfers between devices: 4.16 us -> 6.92 us  [to_section(): return lax.ppermute(block, ('rep', 'blk'), pairs)]
    ppermute x8, starting transfers between devices: 18.6 us -> 17.1 us  [to_pieces(): pieces.append(lax.ppermute(value, ('rep', 'blk'), pairs))]
    unnamed x31 -> x33, local copies, waits for them, and re-layouts: 2.24 us -> 3.79 us
    dot_general x5, matrix products: 5.67 us -> 7 us  [dot(): return jnp.dot(left, right, preferred_element_type=jnp.float32)]
    ppermute x5, waiting for transfers between devices: 4.71 us -> 5.94 us  [exchange(): return lax.ppermute(value, 'blk', [(c, c ^ delta) for c in range(blks)])]
    ppermute x8, waiting for transfers between devices: 3.23 us -> 4.33 us  [to_pieces(): pieces.append(lax.ppermute(value, ('rep', 'blk'), pairs))]
  transfers between devices with their start and end apart: 31 -> 31, of which waited for: 19 -> 18; matrix products, arithmetic and copies ran while one was open for 5% -> 6% of each run, Pallas kernels for 5% -> 5%
where the time goes in v14:
time: 96.3 us; the launch traced here: 95.9 us
  starting transfers between devices  43.8 us (45%)
  waiting for transfers between devices  28.6 us (30%)
  Pallas kernels  8.3 us (9%)
  matrix products  7.36 us (8%)
  local copies, waits for them, and re-layouts  4.87 us (5%)
  other arithmetic  1.85 us (2%)
  between operations  1.17 us (1%)
    ppermute x8, starting transfers between devices, to_pieces(): pieces.append(lax.ppermute(value, ('rep', 'blk'), pairs))  17.1 us
    ppermute x12, starting transfers between devices, swap(): return lax.ppermute(value, 'rep', [(r, r ^ delta) for r in range(reps)])  15.2 us
    ppermute x12, waiting for transfers between devices, swap(): return lax.ppermute(value, 'rep', [(r, r ^ delta) for r in range(reps)])  14.7 us
    dot_general x5, matrix products, dot(): return jnp.dot(left, right, preferred_element_type=jnp.float32)  7 us
    ppermute x6, starting transfers between devices, to_section(): return lax.ppermute(block, ('rep', 'blk'), pairs)  6.92 us
    ppermute x5, waiting for transfers between devices, exchange(): return lax.ppermute(value, 'blk', [(c, c ^ delta) for c in range(blks)])  5.94 us
    pallas_call x2, Pallas kernels, build_dense(): pl.pallas_call(body, grid_spec=pltpu.PrefetchScalarGridSpec(num_scalar_pr...  5.26 us
    ppermute x5, starting transfers between devices, exchange(): return lax.ppermute(value, 'blk', [(c, c ^ delta) for c in range(blks)])  4.59 us
  transfers between devices with their start and end apart: 31, of which 18 were waited for; matrix products, arithmetic and copies ran while one was open for 6% of the time, Pallas kernels for 5%

profile of v14, /device:TPU:0, one launch (start us, length us, event | category | flops | bytes accessed | tf_op | source)
XLA Modules:
  0.0 95.9 jit_solution(18331879519963037409)
XLA Ops:
  0.6 7.0 %collective-permute-start.3 = (bf16[256,128]{1,0:T(8,128)(2,1)}, bf16[256,128]{1,0:T(8,128)(2,1)S(1)}, u32[]{:S(2)}, u32[]{:S(2)}) collective-permute-start(bf16[256,128]{1,0:T(8,128)(2,1)} %bitcast.56), channel_id=1, source_target_pairs={{0,30},{1,31},{2,24},{3,25},{4,26},{5,27},{6,28},{7,29},{8,20},{9,... | collective-permute-start | bytes 196616 | tf_op jit(solution)/shard_map/ppermute | solution.py:253
  8.2 1.5 %collective-permute-start = (bf16[256,128]{1,0:T(8,128)(2,1)}, bf16[256,128]{1,0:T(8,128)(2,1)S(1)}, u32[]{:S(2)}, u32[]{:S(2)}) collective-permute-start(bf16[256,128]{1,0:T(8,128)(2,1)} %bitcast.59), channel_id=1, source_target_pairs={{0,0},{1,1},{2,2},{3,3},{4,4},{5,5},{6,6},{7,7},{8,10},{9,11},{10,... | collective-permute-start | bytes 196616 | tf_op jit(solution)/shard_map/ppermute | solution.py:253
  12.6 5.0 %collective-permute-start.4 = (bf16[512,128]{1,0:T(8,128)(2,1)S(1)}, bf16[512,128]{1,0:T(8,128)(2,1)S(1)}, u32[]{:S(2)}, u32[]{:S(2)}) collective-permute-start(bf16[512,128]{1,0:T(8,128)(2,1)S(1)} %pad_maximum_fusion.1), channel_id=1, source_target_pairs={{0,1},{1,24},{2,3},{3,26},{4,5},{5,28},{6,7},{7,30},{8,9},{9,0},{1... | collective-permute-start | bytes 393224 | tf_op jit(solution)/shard_map/ppermute | solution.py:240
  19.6 2.1 %dense.1 = bf16[1024,2048]{1,0:T(8,128)(2,1)S(1)} custom-call(s32[2,19]{1,0:T(2,128)S(1)} %pad_add_fusion.meta_ref, bf16[2,16,128,128]{3,2,1,0:T(8,128)(2,1)S(1)} %bitcast.45), custom_call_target="tpu_custom_call" | custom-call | bytes 8388608 | tf_op jit(solution)/shard_map/dense/pallas_call | solution.py:183
  21.9 1.3 %fusion.18 = f32[1024,128]{1,0:T(8,128)S(1)} fusion(bf16[1024,2048]{1,0:T(8,128)(2,1)S(1)} %dense.1, bf16[2048,128]{1,0:T(8,128)(2,1)S(1)} %constant_dynamic-update-slice_fusion), kind=kOutput, calls=%fused_computation.73 | convolution fusion | flops 536870912 | bytes 5242880 | tf_op jit(solution)/shard_map/dot_general | solution.py:32
  23.8 2.9 %collective-permute-start.6 = (f32[256,128]{1,0:T(8,128)S(1)}, f32[256,128]{1,0:T(8,128)S(1)}, u32[]{:S(2)}, u32[]{:S(2)}) collective-permute-start(f32[256,128]{1,0:T(8,128)S(1)} %get-tuple-element.57), channel_id=1, source_target_pairs={{0,8},{8,0},{16,24},{24,16},{1,9},{9,1},{17,25},{25,17},{2,10},{10... | collective-permute-start | bytes 393224 | tf_op jit(solution)/shard_map/ppermute | solution.py:229
  26.7 1.4 %collective-permute-start.8 = (f32[256,128]{1,0:T(8,128)S(1)}, f32[256,128]{1,0:T(8,128)S(1)}, u32[]{:S(2)}, u32[]{:S(2)}) collective-permute-start(f32[256,128]{1,0:T(8,128)S(1)} %get-tuple-element.58), channel_id=1, source_target_pairs={{0,24},{8,16},{16,8},{24,0},{1,25},{9,17},{17,9},{25,1},{2,26},{10... | collective-permute-start | bytes 393224 | tf_op jit(solution)/shard_map/ppermute | solution.py:229
  28.3 2.3 %collective-permute-done.6 = f32[256,128]{1,0:T(8,128)S(1)} collective-permute-done((f32[256,128]{1,0:T(8,128)S(1)}, f32[256,128]{1,0:T(8,128)S(1)}, u32[]{:S(2)}, u32[]{:S(2)}) %collective-permute-start.6) | collective-permute-done | bytes 131104 | tf_op jit(solution)/shard_map/ppermute | solution.py:229
  30.6 2.9 %collective-permute-done.8 = f32[256,128]{1,0:T(8,128)S(1)} collective-permute-done((f32[256,128]{1,0:T(8,128)S(1)}, f32[256,128]{1,0:T(8,128)S(1)}, u32[]{:S(2)}, u32[]{:S(2)}) %collective-permute-start.8) | collective-permute-done | bytes 131104 | tf_op jit(solution)/shard_map/ppermute | solution.py:229
  33.5 1.3 %collective-permute-done.7 = f32[256,128]{1,0:T(8,128)S(1)} collective-permute-done((f32[256,128]{1,0:T(8,128)S(1)}, f32[256,128]{1,0:T(8,128)S(1)}, u32[]{:S(2)}, u32[]{:S(2)}) %collective-permute-start.7) | collective-permute-done | bytes 131104 | tf_op jit(solution)/shard_map/ppermute | solution.py:229
  35.6 4.1 %collective-permute-start.12 = (bf16[272,128]{1,0:T(8,128)(2,1)S(1)}, bf16[272,128]{1,0:T(8,128)(2,1)S(1)}, u32[]{:S(2)}, u32[]{:S(2)}) collective-permute-start(bf16[272,128]{1,0:T(8,128)(2,1)S(1)} %pad_maximum_fusion.4), channel_id=1, source_target_pairs={{0,30},{1,31},{2,24},{3,25},{4,26},{5,27},{6,28},{7,29},{8,20},{9,... | collective-permute-start | bytes 208904 | tf_op jit(solution)/shard_map/ppermute | solution.py:253
  39.6 3.3 %collective-permute-start.11 = (bf16[272,128]{1,0:T(8,128)(2,1)S(1)}, bf16[272,128]{1,0:T(8,128)(2,1)S(1)}, u32[]{:S(2)}, u32[]{:S(2)}) collective-permute-start(bf16[272,128]{1,0:T(8,128)(2,1)S(1)} %pad_maximum_fusion.4), channel_id=1, source_target_pairs={{0,20},{1,21},{2,22},{3,23},{4,16},{5,17},{6,18},{7,19},{8,30},{9,... | collective-permute-start | bytes 208904 | tf_op jit(solution)/shard_map/ppermute | solution.py:253
  43.0 1.6 %collective-permute-start.16 = (bf16[272,128]{1,0:T(8,128)(2,1)S(1)}, bf16[272,128]{1,0:T(8,128)(2,1)S(1)}, u32[]{:S(2)}, u32[]{:S(2)}) collective-permute-start(bf16[272,128]{1,0:T(8,128)(2,1)S(1)} %collective-permute-done.12), channel_id=1, source_target_pairs={{0,1},{1,24},{2,3},{3,26},{4,5},{5,28},{6,7},{7,30},{8,9},{9,0},{1... | collective-permute-start | bytes 208904 | tf_op jit(solution)/shard_map/ppermute | solution.py:240
  45.2 2.8 %collective-permute-done.10 = bf16[272,128]{1,0:T(8,128)(2,1)S(1)} collective-permute-done((bf16[272,128]{1,0:T(8,128)(2,1)S(1)}, bf16[272,128]{1,0:T(8,128)(2,1)S(1)}, u32[]{:S(2)}, u32[]{:S(2)}) %collective-permute-start.10) | collective-permute-done | bytes 69664 | tf_op jit(solution)/shard_map/ppermute | solution.py:253
  48.1 3.6 %collective-permute-done.14 = bf16[272,128]{1,0:T(8,128)(2,1)S(1)} collective-permute-done((bf16[272,128]{1,0:T(8,128)(2,1)S(1)}, bf16[272,128]{1,0:T(8,128)(2,1)S(1)}, u32[]{:S(2)}, u32[]{:S(2)}) %collective-permute-start.14) | collective-permute-done | bytes 69664 | tf_op jit(solution)/shard_map/ppermute | solution.py:240
  51.9 1.2 %fusion.1 = bf16[2048,256]{1,0:T(8,128)(2,1)S(1)} fusion(bf16[2048,128]{1,0:T(8,128)(2,1)S(1)} %slice_dynamic-update-slice_fusion, bf16[128,256]{1,0:T(8,128)(2,1)S(1)} %copy-done, s32[256]{0:T(256)S(1)} %iota_multiply_fusion, s32[2048]{0:T(1024)S(1)} %broadcast_multiply_fusion), kind=kOutput, calls=%fused_computation.5 | convolution fusion | flops 142082048 | bytes 1647616 | tf_op jit(solution)/shard_map/dot_general | solution.py:32
  54.1 1.3 %fusion.19.partial_ref.own_ref = f32[1024,256]{1,0:T(8,128)S(1)} fusion(bf16[1024,2048]{1,0:T(8,128)(2,1)S(1)} %copy-done.2, bf16[2048,256]{1,0:T(8,128)(2,1)S(1)} %fusion.1), kind=kOutput, calls=%fused_computation.74 | convolution fusion | flops 1073741824 | bytes 6291456 | tf_op jit(solution)/shard_map/dot_general | solution.py:32
  55.8 1.9 %collective-permute-start.17 = (s16[272,256]{1,0:T(8,128)(2,1)S(1)}, s16[272,256]{1,0:T(8,128)(2,1)S(1)}, u32[]{:S(2)}, u32[]{:S(2)}) collective-permute-start(s16[272,256]{1,0:T(8,128)(2,1)S(1)} %get-tuple-element.32), channel_id=1, source_target_pairs={{0,8},{8,0},{16,24},{24,16},{1,9},{9,1},{17,25},{25,17},{2,10},{10... | collective-permute-start | bytes 417800 | tf_op jit(solution)/shard_map/ppermute | solution.py:229
  59.4 1.9 %fusion.3 = bf16[2048,256]{1,0:T(8,128)(2,1)} fusion(bf16[2048,128]{1,0:T(8,128)(2,1)S(1)} %slice_dynamic-update-slice_fusion, bf16[128,256]{1,0:T(8,128)(2,1)S(1)} %copy-done, s32[256]{0:T(256)S(1)} %iota_multiply_fusion, s32[2048]{0:T(1024)S(1)} %broadcast_multiply_fusion), kind=kOutput, calls=%fused_computation.8 | convolution fusion | flops 140509184 | bytes 1647616 | tf_op jit(solution)/shard_map/dot_general | solution.py:32
  62.2 2.8 %collective-permute-done.18.refs_1_ = s16[272,256]{1,0:T(8,128)(2,1)S(1)} collective-permute-done((s16[272,256]{1,0:T(8,128)(2,1)S(1)}, s16[272,256]{1,0:T(8,128)(2,1)S(1)}, u32[]{:S(2)}, u32[]{:S(2)}) %collective-permute-start.18) | collective-permute-done | bytes 139296 | tf_op jit(solution)/shard_map/ppermute | solution.py:229
  65.0 1.3 %head.1 = (f32[256,172]{1,0:T(8,128)S(1)}, f32[48,256]{1,0:T(8,128)S(1)}, bf16[304,256]{1,0:T(8,128)(2,1)S(1)}, bf16[304,256]{1,0:T(8,128)(2,1)S(1)}, bf16[304,2...) custom-call(s32[2]{0:T(128)S(1)} %pad_add_fusion.1.spot_ref, bf16[172,256]{1,0:T(8,128)(2,1)S(1)} %bitcast.48, ...), custom_call_target="tpu_custom_call" | custom-call | tf_op jit(solution)/shard_map/head/pallas_call | solution.py:144
  68.1 1.9 %collective-permute-start.22 = (bf16[304,256]{1,0:T(8,128)(2,1)S(1)}, bf16[304,256]{1,0:T(8,128)(2,1)S(1)}, u32[]{:S(2)}, u32[]{:S(2)}) collective-permute-start(bf16[304,256]{1,0:T(8,128)(2,1)S(1)} %get-tuple-element.41), channel_id=1, source_target_pairs={{0,24},{8,16},{16,8},{24,0},{1,25},{9,17},{17,9},{25,1},{2,26},{10... | collective-permute-start | bytes 466952 | tf_op jit(solution)/shard_map/ppermute | solution.py:229
  70.0 3.1 %dense_turned.1 = bf16[2048,1024]{1,0:T(8,128)(2,1)S(1)} custom-call(s32[2,19]{1,0:T(2,128)S(1)} %pad_add_fusion.meta_ref, bf16[2,16,128,128]{3,2,1,0:T(8,128)(2,1)S(1)} %bitcast.46), custom_call_target="tpu_custom_call" | custom-call | bytes 8388608 | tf_op jit(solution)/shard_map/dense_turned/pallas_call | solution.py:183
  74.3 1.3 %fusion.2 = bf16[2048,256]{1,0:T(8,128)(2,1)S(1)} fusion(bf16[2048,1024]{1,0:T(8,128)(2,1)S(1)} %dense_turned.1, bf16[1024,256]{1,0:T(8,128)(2,1)S(1)} %pad_maximum_fusion, bf16[2048,256]{1,0:T(8,128)(2,1)S(1)} %copy-done.9), kind=kOutput, calls=%fused_computation.6 | convolution fusion | flops 1075838976 | bytes 6815744 | tf_op jit(solution)/shard_map/dot_general | solution.py:32
  76.1 1.3 %collective-permute-done.23 = f32[88,256]{1,0:T(8,128)S(1)} collective-permute-done((f32[88,256]{1,0:T(8,128)S(1)}, f32[88,256]{1,0:T(8,128)S(1)}, u32[]{:S(2)}, u32[]{:S(2)}) %collective-permute-start.23) | collective-permute-done | bytes 90144 | tf_op jit(solution)/shard_map/ppermute | solution.py:243
  77.4 3.6 %collective-permute-start.26 = (bf16[88,256]{1,0:T(8,128)(2,1)S(1)}, bf16[88,256]{1,0:T(8,128)(2,1)S(1)}, u32[]{:S(2)}, u32[]{:S(2)}) collective-permute-start(bf16[88,256]{1,0:T(8,128)(2,1)S(1)} %fusion.11), channel_id=1, source_target_pairs={{0,6},{1,7},{2,4},{3,5},{4,2},{5,3},{6,0},{7,1},{8,14},{9,15},{10,... | collective-permute-start | bytes 135176 | tf_op jit(solution)/shard_map/ppermute | solution.py:243
  81.9 1.6 %collective-permute-done.26 = bf16[88,256]{1,0:T(8,128)(2,1)S(1)} collective-permute-done((bf16[88,256]{1,0:T(8,128)(2,1)S(1)}, bf16[88,256]{1,0:T(8,128)(2,1)S(1)}, u32[]{:S(2)}, u32[]{:S(2)}) %collective-permute-start.26) | collective-permute-done | bytes 45088 | tf_op jit(solution)/shard_map/ppermute | solution.py:243
  83.5 2.5 %collective-permute-done.25 = bf16[88,256]{1,0:T(8,128)(2,1)S(1)} collective-permute-done((bf16[88,256]{1,0:T(8,128)(2,1)S(1)}, bf16[88,256]{1,0:T(8,128)(2,1)S(1)}, u32[]{:S(2)}, u32[]{:S(2)}) %collective-permute-start.25) | collective-permute-done | bytes 45088 | tf_op jit(solution)/shard_map/ppermute | solution.py:243
  86.0 1.8 %collective-permute-start.29 = (bf16[88,256]{1,0:T(8,128)(2,1)S(1)}, bf16[88,256]{1,0:T(8,128)(2,1)S(1)}, u32[]{:S(2)}, u32[]{:S(2)}) collective-permute-start(bf16[88,256]{1,0:T(8,128)(2,1)S(1)} %add_convert_fusion), channel_id=1, source_target_pairs={{0,24},{8,16},{16,8},{24,0},{1,25},{9,17},{17,9},{25,1},{2,26},{10... | collective-permute-start | bytes 135176 | tf_op jit(solution)/shard_map/ppermute | solution.py:229
  87.8 1.2 %collective-permute-start.28 = (bf16[88,256]{1,0:T(8,128)(2,1)S(1)}, bf16[88,256]{1,0:T(8,128)(2,1)S(1)}, u32[]{:S(2)}, u32[]{:S(2)}) collective-permute-start(bf16[88,256]{1,0:T(8,128)(2,1)S(1)} %add_convert_fusion), channel_id=1, source_target_pairs={{0,16},{8,24},{16,0},{24,8},{1,17},{9,25},{17,1},{25,9},{2,18},{10... | collective-permute-start | bytes 135176 | tf_op jit(solution)/shard_map/ppermute | solution.py:229
  89.5 1.5 %collective-permute-done.29 = bf16[88,256]{1,0:T(8,128)(2,1)S(1)} collective-permute-done((bf16[88,256]{1,0:T(8,128)(2,1)S(1)}, bf16[88,256]{1,0:T(8,128)(2,1)S(1)}, u32[]{:S(2)}, u32[]{:S(2)}) %collective-permute-start.29) | collective-permute-done | bytes 45088 | tf_op jit(solution)/shard_map/ppermute | solution.py:229
  94.6 1.3 %last.1 = (f32[128,256]{1,0:T(8,128)}, f32[172,256]{1,0:T(8,128)}) custom-call(s32[2]{0:T(128)S(1)} %pad_add_fusion.1.spot_ref, f32[160,256]{1,0:T(8,128)S(1)} %constant_dynamic-update-slice_fusion.7.total_ref, f32[160,256]{1,0:T(8,128)S(1)} %collective-permute-done.30.other_ref), custom_call_target="tpu_custom_call" | custom-call | tf_op jit(solution)/shard_map/last/pallas_call | solution.py:144
  (117 shorter events, 20.1 us)
Async XLA Ops:
  0.6 51.3 %copy-start = (bf16[128,256]{1,0:T(8,128)(2,1)S(1)}, bf16[128,256]{1,0:T(8,128)(2,1)}, u32[]{:S(2)}) copy-start(bf16[128,256]{1,0:T(8,128)(2,1)} %param.17) | copy-start | bytes 196612
  0.6 10.7 %collective-permute-start.3 = (bf16[256,128]{1,0:T(8,128)(2,1)}, bf16[256,128]{1,0:T(8,128)(2,1)S(1)}, u32[]{:S(2)}, u32[]{:S(2)}) collective-permute-start(bf16[256,128]{1,0:T(8,128)(2,1)} %bitcast.56), channel_id=1, source_target_pairs={{0,30},{1,31},{2,24},{3,25},{4,26},{5,27},{6,28},{7,29},{8,20},{9,... | collective-permute-start | bytes 196616 | tf_op jit(solution)/shard_map/ppermute | solution.py:253
  7.6 4.5 %collective-permute-start.2 = (bf16[256,128]{1,0:T(8,128)(2,1)}, bf16[256,128]{1,0:T(8,128)(2,1)S(1)}, u32[]{:S(2)}, u32[]{:S(2)}) collective-permute-start(bf16[256,128]{1,0:T(8,128)(2,1)} %bitcast.57), channel_id=1, source_target_pairs={{0,20},{1,21},{2,22},{3,23},{4,16},{5,17},{6,18},{7,19},{8,30},{9,... | collective-permute-start | bytes 196616 | tf_op jit(solution)/shard_map/ppermute | solution.py:253
  8.1 4.5 %collective-permute-start.1 = (bf16[256,128]{1,0:T(8,128)(2,1)}, bf16[256,128]{1,0:T(8,128)(2,1)S(1)}, u32[]{:S(2)}, u32[]{:S(2)}) collective-permute-start(bf16[256,128]{1,0:T(8,128)(2,1)} %bitcast.58), channel_id=1, source_target_pairs={{0,10},{1,11},{2,12},{3,13},{4,14},{5,15},{6,8},{7,9},{8,0},{9,1},... | collective-permute-start | bytes 196616 | tf_op jit(solution)/shard_map/ppermute | solution.py:253
  8.2 2.9 %collective-permute-start = (bf16[256,128]{1,0:T(8,128)(2,1)}, bf16[256,128]{1,0:T(8,128)(2,1)S(1)}, u32[]{:S(2)}, u32[]{:S(2)}) collective-permute-start(bf16[256,128]{1,0:T(8,128)(2,1)} %bitcast.59), channel_id=1, source_target_pairs={{0,0},{1,1},{2,2},{3,3},{4,4},{5,5},{6,6},{7,7},{8,10},{9,11},{10,... | collective-permute-start | bytes 196616 | tf_op jit(solution)/shard_map/ppermute | solution.py:253
  12.1 9.7 %collective-permute-start.5 = (bf16[512,128]{1,0:T(8,128)(2,1)S(1)}, bf16[512,128]{1,0:T(8,128)(2,1)S(1)}, u32[]{:S(2)}, u32[]{:S(2)}) collective-permute-start(bf16[512,128]{1,0:T(8,128)(2,1)S(1)} %pad_maximum_fusion.2), channel_id=1, source_target_pairs={{0,1},{1,24},{2,3},{3,26},{4,5},{5,28},{6,7},{7,30},{8,9},{9,0},{1... | collective-permute-start | bytes 393224 | tf_op jit(solution)/shard_map/ppermute | solution.py:240
  12.6 9.2 %collective-permute-start.4 = (bf16[512,128]{1,0:T(8,128)(2,1)S(1)}, bf16[512,128]{1,0:T(8,128)(2,1)S(1)}, u32[]{:S(2)}, u32[]{:S(2)}) collective-permute-start(bf16[512,128]{1,0:T(8,128)(2,1)S(1)} %pad_maximum_fusion.1), channel_id=1, source_target_pairs={{0,1},{1,24},{2,3},{3,26},{4,5},{5,28},{6,7},{7,30},{8,9},{9,0},{1... | collective-permute-start | bytes 393224 | tf_op jit(solution)/shard_map/ppermute | solution.py:240
  23.8 6.8 %collective-permute-start.6 = (f32[256,128]{1,0:T(8,128)S(1)}, f32[256,128]{1,0:T(8,128)S(1)}, u32[]{:S(2)}, u32[]{:S(2)}) collective-permute-start(f32[256,128]{1,0:T(8,128)S(1)} %get-tuple-element.57), channel_id=1, source_target_pairs={{0,8},{8,0},{16,24},{24,16},{1,9},{9,1},{17,25},{25,17},{2,10},{10... | collective-permute-start | bytes 393224 | tf_op jit(solution)/shard_map/ppermute | solution.py:229
  26.7 6.7 %collective-permute-start.8 = (f32[256,128]{1,0:T(8,128)S(1)}, f32[256,128]{1,0:T(8,128)S(1)}, u32[]{:S(2)}, u32[]{:S(2)}) collective-permute-start(f32[256,128]{1,0:T(8,128)S(1)} %get-tuple-element.58), channel_id=1, source_target_pairs={{0,24},{8,16},{16,8},{24,0},{1,25},{9,17},{17,9},{25,1},{2,26},{10... | collective-permute-start | bytes 393224 | tf_op jit(solution)/shard_map/ppermute | solution.py:229
  28.1 6.7 %collective-permute-start.7 = (f32[256,128]{1,0:T(8,128)S(1)}, f32[256,128]{1,0:T(8,128)S(1)}, u32[]{:S(2)}, u32[]{:S(2)}) collective-permute-start(f32[256,128]{1,0:T(8,128)S(1)} %get-tuple-element.59), channel_id=1, source_target_pairs={{0,16},{8,24},{16,0},{24,8},{1,17},{9,25},{17,1},{25,9},{2,18},{10... | collective-permute-start | bytes 393224 | tf_op jit(solution)/shard_map/ppermute | solution.py:229
  34.8 8.1 %collective-permute-start.9 = (bf16[272,128]{1,0:T(8,128)(2,1)S(1)}, bf16[272,128]{1,0:T(8,128)(2,1)S(1)}, u32[]{:S(2)}, u32[]{:S(2)}) collective-permute-start(bf16[272,128]{1,0:T(8,128)(2,1)S(1)} %pad_maximum_fusion.4), channel_id=1, source_target_pairs={{0,0},{1,1},{2,2},{3,3},{4,4},{5,5},{6,6},{7,7},{8,10},{9,11},{10,... | collective-permute-start | bytes 208904 | tf_op jit(solution)/shard_map/ppermute | solution.py:253
  35.6 7.4 %collective-permute-start.12 = (bf16[272,128]{1,0:T(8,128)(2,1)S(1)}, bf16[272,128]{1,0:T(8,128)(2,1)S(1)}, u32[]{:S(2)}, u32[]{:S(2)}) collective-permute-start(bf16[272,128]{1,0:T(8,128)(2,1)S(1)} %pad_maximum_fusion.4), channel_id=1, source_target_pairs={{0,30},{1,31},{2,24},{3,25},{4,26},{5,27},{6,28},{7,29},{8,20},{9,... | collective-permute-start | bytes 208904 | tf_op jit(solution)/shard_map/ppermute | solution.py:253
  39.6 5.2 %collective-permute-start.11 = (bf16[272,128]{1,0:T(8,128)(2,1)S(1)}, bf16[272,128]{1,0:T(8,128)(2,1)S(1)}, u32[]{:S(2)}, u32[]{:S(2)}) collective-permute-start(bf16[272,128]{1,0:T(8,128)(2,1)S(1)} %pad_maximum_fusion.4), channel_id=1, source_target_pairs={{0,20},{1,21},{2,22},{3,23},{4,16},{5,17},{6,18},{7,19},{8,30},{9,... | collective-permute-start | bytes 208904 | tf_op jit(solution)/shard_map/ppermute | solution.py:253
  42.9 5.1 %collective-permute-start.10 = (bf16[272,128]{1,0:T(8,128)(2,1)S(1)}, bf16[272,128]{1,0:T(8,128)(2,1)S(1)}, u32[]{:S(2)}, u32[]{:S(2)}) collective-permute-start(bf16[272,128]{1,0:T(8,128)(2,1)S(1)} %pad_maximum_fusion.4), channel_id=1, source_target_pairs={{0,10},{1,11},{2,12},{3,13},{4,14},{5,15},{6,8},{7,9},{8,0},{9,1},... | collective-permute-start | bytes 208904 | tf_op jit(solution)/shard_map/ppermute | solution.py:253
  42.9 5.2 %collective-permute-start.13 = (bf16[272,128]{1,0:T(8,128)(2,1)S(1)}, bf16[272,128]{1,0:T(8,128)(2,1)S(1)}, u32[]{:S(2)}, u32[]{:S(2)}) collective-permute-start(bf16[272,128]{1,0:T(8,128)(2,1)S(1)} %collective-permute-done.9), channel_id=1, source_target_pairs={{0,1},{1,24},{2,3},{3,26},{4,5},{5,28},{6,7},{7,30},{8,9},{9,0},{1... | collective-permute-start | bytes 208904 | tf_op jit(solution)/shard_map/ppermute | solution.py:240
  43.0 8.8 %collective-permute-start.16 = (bf16[272,128]{1,0:T(8,128)(2,1)S(1)}, bf16[272,128]{1,0:T(8,128)(2,1)S(1)}, u32[]{:S(2)}, u32[]{:S(2)}) collective-permute-start(bf16[272,128]{1,0:T(8,128)(2,1)S(1)} %collective-permute-done.12), channel_id=1, source_target_pairs={{0,1},{1,24},{2,3},{3,26},{4,5},{5,28},{6,7},{7,30},{8,9},{9,0},{1... | collective-permute-start | bytes 208904 | tf_op jit(solution)/shard_map/ppermute | solution.py:240
  44.9 6.9 %collective-permute-start.15 = (bf16[272,128]{1,0:T(8,128)(2,1)S(1)}, bf16[272,128]{1,0:T(8,128)(2,1)S(1)}, u32[]{:S(2)}, u32[]{:S(2)}) collective-permute-start(bf16[272,128]{1,0:T(8,128)(2,1)S(1)} %collective-permute-done.11), channel_id=1, source_target_pairs={{0,1},{1,24},{2,3},{3,26},{4,5},{5,28},{6,7},{7,30},{8,9},{9,0},{1... | collective-permute-start | bytes 208904 | tf_op jit(solution)/shard_map/ppermute | solution.py:240
  48.0 3.7 %collective-permute-start.14 = (bf16[272,128]{1,0:T(8,128)(2,1)S(1)}, bf16[272,128]{1,0:T(8,128)(2,1)S(1)}, u32[]{:S(2)}, u32[]{:S(2)}) collective-permute-start(bf16[272,128]{1,0:T(8,128)(2,1)S(1)} %collective-permute-done.10), channel_id=1, source_target_pairs={{0,1},{1,24},{2,3},{3,26},{4,5},{5,28},{6,7},{7,30},{8,9},{9,0},{1... | collective-permute-start | bytes 208904 | tf_op jit(solution)/shard_map/ppermute | solution.py:240
  55.8 6.4 %collective-permute-start.17 = (s16[272,256]{1,0:T(8,128)(2,1)S(1)}, s16[272,256]{1,0:T(8,128)(2,1)S(1)}, u32[]{:S(2)}, u32[]{:S(2)}) collective-permute-start(s16[272,256]{1,0:T(8,128)(2,1)S(1)} %get-tuple-element.32), channel_id=1, source_target_pairs={{0,8},{8,0},{16,24},{24,16},{1,9},{9,1},{17,25},{25,17},{2,10},{10... | collective-permute-start | bytes 417800 | tf_op jit(solution)/shard_map/ppermute | solution.py:229
  57.7 7.3 %collective-permute-start.18 = (s16[272,256]{1,0:T(8,128)(2,1)S(1)}, s16[272,256]{1,0:T(8,128)(2,1)S(1)}, u32[]{:S(2)}, u32[]{:S(2)}) collective-permute-start(s16[272,256]{1,0:T(8,128)(2,1)S(1)} %get-tuple-element.33), channel_id=1, source_target_pairs={{0,16},{8,24},{16,0},{24,8},{1,17},{9,25},{17,1},{25,9},{2,18},{10... | collective-permute-start | bytes 417800 | tf_op jit(solution)/shard_map/ppermute | solution.py:229
  58.7 6.3 %collective-permute-start.19 = (s16[272,256]{1,0:T(8,128)(2,1)S(1)}, s16[272,256]{1,0:T(8,128)(2,1)S(1)}, u32[]{:S(2)}, u32[]{:S(2)}) collective-permute-start(s16[272,256]{1,0:T(8,128)(2,1)S(1)} %get-tuple-element.34), channel_id=1, source_target_pairs={{0,24},{8,16},{16,8},{24,0},{1,25},{9,17},{17,9},{25,1},{2,26},{10... | collective-permute-start | bytes 417800 | tf_op jit(solution)/shard_map/ppermute | solution.py:229
  66.4 6.7 %collective-permute-start.20 = (bf16[304,256]{1,0:T(8,128)(2,1)S(1)}, bf16[304,256]{1,0:T(8,128)(2,1)S(1)}, u32[]{:S(2)}, u32[]{:S(2)}) collective-permute-start(bf16[304,256]{1,0:T(8,128)(2,1)S(1)} %get-tuple-element.39), channel_id=1, source_target_pairs={{0,8},{8,0},{16,24},{24,16},{1,9},{9,1},{17,25},{25,17},{2,10},{10... | collective-permute-start | bytes 466952 | tf_op jit(solution)/shard_map/ppermute | solution.py:229
  66.9 6.3 %collective-permute-start.21 = (bf16[304,256]{1,0:T(8,128)(2,1)S(1)}, bf16[304,256]{1,0:T(8,128)(2,1)S(1)}, u32[]{:S(2)}, u32[]{:S(2)}) collective-permute-start(bf16[304,256]{1,0:T(8,128)(2,1)S(1)} %get-tuple-element.40), channel_id=1, source_target_pairs={{0,16},{8,24},{16,0},{24,8},{1,17},{9,25},{17,1},{25,9},{2,18},{10... | collective-permute-start | bytes 466952 | tf_op jit(solution)/shard_map/ppermute | solution.py:229
  68.1 6.1 %collective-permute-start.22 = (bf16[304,256]{1,0:T(8,128)(2,1)S(1)}, bf16[304,256]{1,0:T(8,128)(2,1)S(1)}, u32[]{:S(2)}, u32[]{:S(2)}) collective-permute-start(bf16[304,256]{1,0:T(8,128)(2,1)S(1)} %get-tuple-element.41), channel_id=1, source_target_pairs={{0,24},{8,16},{16,8},{24,0},{1,25},{9,17},{17,9},{25,1},{2,26},{10... | collective-permute-start | bytes 466952 | tf_op jit(solution)/shard_map/ppermute | solution.py:229
  76.1 1.4 %collective-permute-start.23 = (f32[88,256]{1,0:T(8,128)S(1)}, f32[88,256]{1,0:T(8,128)S(1)}, u32[]{:S(2)}, u32[]{:S(2)}) collective-permute-start(f32[88,256]{1,0:T(8,128)S(1)} %pad_maximum_fusion.3), channel_id=1, source_target_pairs={{0,1},{1,0},{2,3},{3,2},{4,5},{5,4},{6,7},{7,6},{8,9},{9,8},{10,11... | collective-permute-start | bytes 270344 | tf_op jit(solution)/shard_map/ppermute | solution.py:243
  77.4 6.1 %collective-permute-start.26 = (bf16[88,256]{1,0:T(8,128)(2,1)S(1)}, bf16[88,256]{1,0:T(8,128)(2,1)S(1)}, u32[]{:S(2)}, u32[]{:S(2)}) collective-permute-start(bf16[88,256]{1,0:T(8,128)(2,1)S(1)} %fusion.11), channel_id=1, source_target_pairs={{0,6},{1,7},{2,4},{3,5},{4,2},{5,3},{6,0},{7,1},{8,14},{9,15},{10,... | collective-permute-start | bytes 135176 | tf_op jit(solution)/shard_map/ppermute | solution.py:243
  81.0 4.9 %collective-permute-start.25 = (bf16[88,256]{1,0:T(8,128)(2,1)S(1)}, bf16[88,256]{1,0:T(8,128)(2,1)S(1)}, u32[]{:S(2)}, u32[]{:S(2)}) collective-permute-start(bf16[88,256]{1,0:T(8,128)(2,1)S(1)} %fusion.11), channel_id=1, source_target_pairs={{0,4},{1,5},{2,6},{3,7},{4,0},{5,1},{6,2},{7,3},{8,12},{9,13},{10,... | collective-permute-start | bytes 135176 | tf_op jit(solution)/shard_map/ppermute | solution.py:243
  81.0 4.9 %collective-permute-start.24 = (bf16[88,256]{1,0:T(8,128)(2,1)S(1)}, bf16[88,256]{1,0:T(8,128)(2,1)S(1)}, u32[]{:S(2)}, u32[]{:S(2)}) collective-permute-start(bf16[88,256]{1,0:T(8,128)(2,1)S(1)} %fusion.11), channel_id=1, source_target_pairs={{0,2},{1,3},{2,0},{3,1},{4,6},{5,7},{6,4},{7,5},{8,10},{9,11},{10,... | collective-permute-start | bytes 135176 | tf_op jit(solution)/shard_map/ppermute | solution.py:243
  86.0 5.1 %collective-permute-start.29 = (bf16[88,256]{1,0:T(8,128)(2,1)S(1)}, bf16[88,256]{1,0:T(8,128)(2,1)S(1)}, u32[]{:S(2)}, u32[]{:S(2)}) collective-permute-start(bf16[88,256]{1,0:T(8,128)(2,1)S(1)} %add_convert_fusion), channel_id=1, source_target_pairs={{0,24},{8,16},{16,8},{24,0},{1,25},{9,17},{17,9},{25,1},{2,26},{10... | collective-permute-start | bytes 135176 | tf_op jit(solution)/shard_map/ppermute | solution.py:229
  87.8 4.0 %collective-permute-start.28 = (bf16[88,256]{1,0:T(8,128)(2,1)S(1)}, bf16[88,256]{1,0:T(8,128)(2,1)S(1)}, u32[]{:S(2)}, u32[]{:S(2)}) collective-permute-start(bf16[88,256]{1,0:T(8,128)(2,1)S(1)} %add_convert_fusion), channel_id=1, source_target_pairs={{0,16},{8,24},{16,0},{24,8},{1,17},{9,25},{17,1},{25,9},{2,18},{10... | collective-permute-start | bytes 135176 | tf_op jit(solution)/shard_map/ppermute | solution.py:229
  89.1 4.0 %collective-permute-start.27 = (bf16[88,256]{1,0:T(8,128)(2,1)S(1)}, bf16[88,256]{1,0:T(8,128)(2,1)S(1)}, u32[]{:S(2)}, u32[]{:S(2)}) collective-permute-start(bf16[88,256]{1,0:T(8,128)(2,1)S(1)} %add_convert_fusion), channel_id=1, source_target_pairs={{0,8},{8,0},{16,24},{24,16},{1,9},{9,1},{17,25},{25,17},{2,10},{10... | collective-permute-start | bytes 135176 | tf_op jit(solution)/shard_map/ppermute | solution.py:229
  93.2 1.5 %collective-permute-start.30 = (f32[160,256]{1,0:T(8,128)S(1)}, f32[160,256]{1,0:T(8,128)S(1)}, u32[]{:S(2)}, u32[]{:S(2)}) collective-permute-start(f32[160,256]{1,0:T(8,128)S(1)} %constant_dynamic-update-slice_fusion.7.total_ref), channel_id=1, source_target_pairs={{0,1},{1,0},{2,3},{3,2},{4,5},{5,4},{6,7},{7,6},{8,9},{9,8},{10,11... | collective-permute-start | bytes 491528 | tf_op jit(solution)/shard_map/ppermute | solution.py:243
  (9 other events, 43.5 us)

commit v15 on v14

--- a/solution.py
+++ b/solution.py
@@ -310,9 +310,17 @@
     z_bundle = jnp.concatenate([z_input, digits(node_ids[0])], axis=0)
     pieces = to_all(to_pieces(z_bundle), 1)
     units = jnp.arange(hidden_width, dtype=jnp.int32)
-    id_columns = jnp.concatenate([undo_digits(part[own_rows:]) for part in pieces])
-    kept = keep_mask(id_columns[:, None], units[None, :])
+
+    def kept_of(parts):
+        ids = jnp.concatenate([undo_digits(part) for part in parts])
+        return keep_mask(ids[:, None], units[None, :])
+
+    rows = [part[own_rows:] for part in pieces]
+    rows[:reps], pieces[reps] = lax.optimization_barrier((rows[:reps], pieces[reps]))
+    kept_own, rows[-1] = lax.optimization_barrier((kept_of(rows[:reps]), rows[-1]))
+    kept = jnp.concatenate([kept_own, kept_of(rows[reps:])], axis=0)
     z_columns = jnp.concatenate([part[:own_rows] for part in pieces], axis=0)
+    kept, z_columns = lax.optimization_barrier((kept, z_columns))
     third = f32(4.0 / 3.0)
     pre_act = dot(z_columns, weight_in)
     dropped = (jnp.maximum(pre_act, 0.0) * (kept.astype(f32) * third)).astype(bf16)

time: 96.3 us -> 96.2 us (level)
  starting transfers between devices: 43.8 us -> 47.3 us
  waiting for transfers between devices: 28.6 us -> 26.8 us
  local copies, waits for them, and re-layouts: 4.87 us -> 3.3 us
  matrix products: 7.36 us -> 6.03 us
    ppermute x12, starting transfers between devices: 15.2 us -> 20 us  [swap(): return lax.ppermute(value, 'rep', [(r, r ^ delta) for r in range(reps)])]
    ppermute x6, starting transfers between devices: 6.92 us -> 3.94 us  [to_section(): return lax.ppermute(block, ('rep', 'blk'), pairs)]
    ppermute x8, starting transfers between devices: 17.1 us -> 18.8 us  [to_pieces(): pieces.append(lax.ppermute(value, ('rep', 'blk'), pairs))]
    unnamed x33 -> x29, local copies, waits for them, and re-layouts: 3.79 us -> 2.21 us
    ppermute x8, waiting for transfers between devices: 4.33 us -> 2.75 us  [to_pieces(): pieces.append(lax.ppermute(value, ('rep', 'blk'), pairs))]
    dot_general x5, matrix products: 7 us -> 5.67 us  [dot(): return jnp.dot(left, right, preferred_element_type=jnp.float32)]
    ppermute x5, waiting for transfers between devices: 5.94 us -> 4.92 us  [exchange(): return lax.ppermute(value, 'blk', [(c, c ^ delta) for c in range(blks)])]
  transfers between devices with their start and end apart: 31 -> 31, of which waited for: 18 -> 17; matrix products, arithmetic and copies ran while one was open for 6% -> 6% of each run, Pallas kernels for 5% -> 5%
where the time goes in v15:
time: 96.2 us; the launch traced here: 95.7 us
  starting transfers between devices  47.3 us (49%)
  waiting for transfers between devices  26.8 us (28%)
  Pallas kernels  8.3 us (9%)
  matrix products  6.03 us (6%)
  local copies, waits for them, and re-layouts  3.3 us (3%)
  other arithmetic  2.76 us (3%)
  between operations  1.25 us (1%)
    ppermute x12, starting transfers between devices, swap(): return lax.ppermute(value, 'rep', [(r, r ^ delta) for r in range(reps)])  20 us
    ppermute x8, starting transfers between devices, to_pieces(): pieces.append(lax.ppermute(value, ('rep', 'blk'), pairs))  18.8 us
    ppermute x12, waiting for transfers between devices, swap(): return lax.ppermute(value, 'rep', [(r, r ^ delta) for r in range(reps)])  15.7 us
    dot_general x5, matrix products, dot(): return jnp.dot(left, right, preferred_element_type=jnp.float32)  5.67 us
    pallas_call x2, Pallas kernels, build_dense(): pl.pallas_call(body, grid_spec=pltpu.PrefetchScalarGridSpec(num_scalar_pr...  5.26 us
    ppermute x5, waiting for transfers between devices, exchange(): return lax.ppermute(value, 'blk', [(c, c ^ delta) for c in range(blks)])  4.92 us
    ppermute x5, starting transfers between devices, exchange(): return lax.ppermute(value, 'blk', [(c, c ^ delta) for c in range(blks)])  4.59 us
    ppermute x6, starting transfers between devices, to_section(): return lax.ppermute(block, ('rep', 'blk'), pairs)  3.94 us
  transfers between devices with their start and end apart: 31, of which 17 were waited for; matrix products, arithmetic and copies ran while one was open for 6% of the time, Pallas kernels for 5%

profile of v15, /device:TPU:0, one launch (start us, length us, event | category | flops | bytes accessed | tf_op | source)
XLA Modules:
  0.0 95.7 jit_solution(8466418038279678611)
XLA Ops:
  0.6 1.6 %collective-permute-start = (bf16[256,128]{1,0:T(8,128)(2,1)}, bf16[256,128]{1,0:T(8,128)(2,1)S(1)}, u32[]{:S(2)}, u32[]{:S(2)}) collective-permute-start(bf16[256,128]{1,0:T(8,128)(2,1)} %bitcast.56), channel_id=1, source_target_pairs={{0,0},{1,1},{2,2},{3,3},{4,4},{5,5},{6,6},{7,7},{8,10},{9,11},{10,... | collective-permute-start | bytes 196616 | tf_op jit(solution)/shard_map/ppermute | solution.py:253
  2.3 6.0 %collective-permute-start.1 = (bf16[256,128]{1,0:T(8,128)(2,1)}, bf16[256,128]{1,0:T(8,128)(2,1)S(1)}, u32[]{:S(2)}, u32[]{:S(2)}) collective-permute-start(bf16[256,128]{1,0:T(8,128)(2,1)} %bitcast.57), channel_id=1, source_target_pairs={{0,10},{1,11},{2,12},{3,13},{4,14},{5,15},{6,8},{7,9},{8,0},{9,1},... | collective-permute-start | bytes 196616 | tf_op jit(solution)/shard_map/ppermute | solution.py:253
  8.3 1.3 %collective-permute-start.2 = (bf16[256,128]{1,0:T(8,128)(2,1)}, bf16[256,128]{1,0:T(8,128)(2,1)S(1)}, u32[]{:S(2)}, u32[]{:S(2)}) collective-permute-start(bf16[256,128]{1,0:T(8,128)(2,1)} %bitcast.58), channel_id=1, source_target_pairs={{0,20},{1,21},{2,22},{3,23},{4,16},{5,17},{6,18},{7,19},{8,30},{9,... | collective-permute-start | bytes 196616 | tf_op jit(solution)/shard_map/ppermute | solution.py:253
  9.6 3.0 %collective-permute-start.3 = (bf16[256,128]{1,0:T(8,128)(2,1)}, bf16[256,128]{1,0:T(8,128)(2,1)S(1)}, u32[]{:S(2)}, u32[]{:S(2)}) collective-permute-start(bf16[256,128]{1,0:T(8,128)(2,1)} %bitcast.59), channel_id=1, source_target_pairs={{0,30},{1,31},{2,24},{3,25},{4,26},{5,27},{6,28},{7,29},{8,20},{9,... | collective-permute-start | bytes 196616 | tf_op jit(solution)/shard_map/ppermute | solution.py:253
  18.1 2.1 %dense.1 = bf16[1024,2048]{1,0:T(8,128)(2,1)S(1)} custom-call(s32[2,19]{1,0:T(2,128)S(1)} %pad_add_fusion.meta_ref, bf16[2,16,128,128]{3,2,1,0:T(8,128)(2,1)S(1)} %bitcast.45), custom_call_target="tpu_custom_call" | custom-call | bytes 8388608 | tf_op jit(solution)/shard_map/dense/pallas_call | solution.py:183
  21.5 1.2 %fusion.22 = f32[1024,128]{1,0:T(8,128)S(1)} fusion(bf16[1024,2048]{1,0:T(8,128)(2,1)S(1)} %dense.1, bf16[2048,128]{1,0:T(8,128)(2,1)S(1)} %constant_dynamic-update-slice_fusion), kind=kOutput, calls=%fused_computation.81 | convolution fusion | flops 536870912 | bytes 5242880 | tf_op jit(solution)/shard_map/dot_general | solution.py:32
  22.8 5.3 %collective-permute-start.6 = (f32[256,128]{1,0:T(8,128)S(1)}, f32[256,128]{1,0:T(8,128)S(1)}, u32[]{:S(2)}, u32[]{:S(2)}) collective-permute-start(f32[256,128]{1,0:T(8,128)S(1)} %get-tuple-element.75), channel_id=1, source_target_pairs={{0,8},{8,0},{16,24},{24,16},{1,9},{9,1},{17,25},{25,17},{2,10},{10... | collective-permute-start | bytes 393224 | tf_op jit(solution)/shard_map/ppermute | solution.py:229
  28.1 1.5 %collective-permute-start.8 = (f32[256,128]{1,0:T(8,128)S(1)}, f32[256,128]{1,0:T(8,128)S(1)}, u32[]{:S(2)}, u32[]{:S(2)}) collective-permute-start(f32[256,128]{1,0:T(8,128)S(1)} %get-tuple-element.76), channel_id=1, source_target_pairs={{0,24},{8,16},{16,8},{24,0},{1,25},{9,17},{17,9},{25,1},{2,26},{10... | collective-permute-start | bytes 393224 | tf_op jit(solution)/shard_map/ppermute | solution.py:229
  29.6 2.0 %collective-permute-done.6 = f32[256,128]{1,0:T(8,128)S(1)} collective-permute-done((f32[256,128]{1,0:T(8,128)S(1)}, f32[256,128]{1,0:T(8,128)S(1)}, u32[]{:S(2)}, u32[]{:S(2)}) %collective-permute-start.6) | collective-permute-done | bytes 131104 | tf_op jit(solution)/shard_map/ppermute | solution.py:229
  31.6 4.2 %collective-permute-done.7 = f32[256,128]{1,0:T(8,128)S(1)} collective-permute-done((f32[256,128]{1,0:T(8,128)S(1)}, f32[256,128]{1,0:T(8,128)S(1)}, u32[]{:S(2)}, u32[]{:S(2)}) %collective-permute-start.7) | collective-permute-done | bytes 131104 | tf_op jit(solution)/shard_map/ppermute | solution.py:229
  36.6 1.3 %collective-permute-start.10 = (bf16[272,128]{1,0:T(8,128)(2,1)S(1)}, bf16[272,128]{1,0:T(8,128)(2,1)S(1)}, u32[]{:S(2)}, u32[]{:S(2)}) collective-permute-start(bf16[272,128]{1,0:T(8,128)(2,1)S(1)} %pad_maximum_fusion.5), channel_id=1, source_target_pairs={{0,10},{1,11},{2,12},{3,13},{4,14},{5,15},{6,8},{7,9},{8,0},{9,1},... | collective-permute-start | bytes 208904 | tf_op jit(solution)/shard_map/ppermute | solution.py:253
  38.0 3.8 %collective-permute-start.11 = (bf16[272,128]{1,0:T(8,128)(2,1)S(1)}, bf16[272,128]{1,0:T(8,128)(2,1)S(1)}, u32[]{:S(2)}, u32[]{:S(2)}) collective-permute-start(bf16[272,128]{1,0:T(8,128)(2,1)S(1)} %pad_maximum_fusion.5), channel_id=1, source_target_pairs={{0,20},{1,21},{2,22},{3,23},{4,16},{5,17},{6,18},{7,19},{8,30},{9,... | collective-permute-start | bytes 208904 | tf_op jit(solution)/shard_map/ppermute | solution.py:253
  42.9 1.9 %collective-permute-start.15 = (bf16[272,128]{1,0:T(8,128)(2,1)S(1)}, bf16[272,128]{1,0:T(8,128)(2,1)S(1)}, u32[]{:S(2)}, u32[]{:S(2)}) collective-permute-start(bf16[272,128]{1,0:T(8,128)(2,1)S(1)} %collective-permute-done.10), channel_id=1, source_target_pairs={{0,1},{1,24},{2,3},{3,26},{4,5},{5,28},{6,7},{7,30},{8,9},{9,0},{1... | collective-permute-start | bytes 208904 | tf_op jit(solution)/shard_map/ppermute | solution.py:240
  45.0 1.9 %collective-permute-done.12 = bf16[272,128]{1,0:T(8,128)(2,1)S(1)} collective-permute-done((bf16[272,128]{1,0:T(8,128)(2,1)S(1)}, bf16[272,128]{1,0:T(8,128)(2,1)S(1)}, u32[]{:S(2)}, u32[]{:S(2)}) %collective-permute-start.12) | collective-permute-done | bytes 69664 | tf_op jit(solution)/shard_map/ppermute | solution.py:253
  48.3 2.3 %collective-permute-done.14 = bf16[272,128]{1,0:T(8,128)(2,1)S(1)} collective-permute-done((bf16[272,128]{1,0:T(8,128)(2,1)S(1)}, bf16[272,128]{1,0:T(8,128)(2,1)S(1)}, u32[]{:S(2)}, u32[]{:S(2)}) %collective-permute-start.14) | collective-permute-done | bytes 69664 | tf_op jit(solution)/shard_map/ppermute | solution.py:240
  51.8 1.3 %fusion.23.partial_ref.own_ref = f32[1024,256]{1,0:T(8,128)S(1)} fusion(bf16[1024,2048]{1,0:T(8,128)(2,1)S(1)} %dense.1, bf16[2048,256]{1,0:T(8,128)(2,1)S(1)} %fusion.1), kind=kOutput, calls=%fused_computation.82 | convolution fusion | flops 1073741824 | bytes 6291456 | tf_op jit(solution)/shard_map/dot_general | solution.py:32
  53.5 4.5 %collective-permute-start.17 = (s16[272,256]{1,0:T(8,128)(2,1)S(1)}, s16[272,256]{1,0:T(8,128)(2,1)S(1)}, u32[]{:S(2)}, u32[]{:S(2)}) collective-permute-start(s16[272,256]{1,0:T(8,128)(2,1)S(1)} %get-tuple-element.50), channel_id=1, source_target_pairs={{0,8},{8,0},{16,24},{24,16},{1,9},{9,1},{17,25},{25,17},{2,10},{10... | collective-permute-start | bytes 417800 | tf_op jit(solution)/shard_map/ppermute | solution.py:229
  58.1 1.5 %collective-permute-start.19 = (s16[272,256]{1,0:T(8,128)(2,1)S(1)}, s16[272,256]{1,0:T(8,128)(2,1)S(1)}, u32[]{:S(2)}, u32[]{:S(2)}) collective-permute-start(s16[272,256]{1,0:T(8,128)(2,1)S(1)} %get-tuple-element.52), channel_id=1, source_target_pairs={{0,24},{8,16},{16,8},{24,0},{1,25},{9,17},{17,9},{25,1},{2,26},{10... | collective-permute-start | bytes 417800 | tf_op jit(solution)/shard_map/ppermute | solution.py:229
  59.6 1.4 %fusion.3 = bf16[2048,256]{1,0:T(8,128)(2,1)} fusion(bf16[2048,256]{1,0:T(8,128)(2,1)S(1)} %pad_maximum_fusion, bf16[2048,128]{1,0:T(8,128)(2,1)S(1)} %slice_dynamic-update-slice_fusion, bf16[128,256]{1,0:T(8,128)(2,1)S(1)} %copy-done), kind=kOutput, calls=%fused_computation.6 | convolution fusion | flops 135266304 | bytes 2686976 | tf_op jit(solution)/shard_map/dot_general | solution.py:32
  61.7 4.2 %collective-permute-done.18.refs_1_ = s16[272,256]{1,0:T(8,128)(2,1)S(1)} collective-permute-done((s16[272,256]{1,0:T(8,128)(2,1)S(1)}, s16[272,256]{1,0:T(8,128)(2,1)S(1)}, u32[]{:S(2)}, u32[]{:S(2)}) %collective-permute-start.18) | collective-permute-done | bytes 139296 | tf_op jit(solution)/shard_map/ppermute | solution.py:229
  65.9 1.3 %head.1 = (f32[256,172]{1,0:T(8,128)S(1)}, f32[48,256]{1,0:T(8,128)S(1)}, bf16[304,256]{1,0:T(8,128)(2,1)S(1)}, bf16[304,256]{1,0:T(8,128)(2,1)S(1)}, bf16[304,2...) custom-call(s32[2]{0:T(128)S(1)} %pad_add_fusion.1.spot_ref, bf16[172,256]{1,0:T(8,128)(2,1)S(1)} %bitcast.48, ...), custom_call_target="tpu_custom_call" | custom-call | tf_op jit(solution)/shard_map/head/pallas_call | solution.py:144
  68.1 2.6 %collective-permute-start.22 = (bf16[304,256]{1,0:T(8,128)(2,1)S(1)}, bf16[304,256]{1,0:T(8,128)(2,1)S(1)}, u32[]{:S(2)}, u32[]{:S(2)}) collective-permute-start(bf16[304,256]{1,0:T(8,128)(2,1)S(1)} %get-tuple-element.59), channel_id=1, source_target_pairs={{0,24},{8,16},{16,8},{24,0},{1,25},{9,17},{17,9},{25,1},{2,26},{10... | collective-permute-start | bytes 466952 | tf_op jit(solution)/shard_map/ppermute | solution.py:229
  70.8 3.1 %dense_turned.1 = bf16[2048,1024]{1,0:T(8,128)(2,1)S(1)} custom-call(s32[2,19]{1,0:T(2,128)S(1)} %pad_add_fusion.meta_ref, bf16[2,16,128,128]{3,2,1,0:T(8,128)(2,1)S(1)} %bitcast.46), custom_call_target="tpu_custom_call" | custom-call | bytes 8388608 | tf_op jit(solution)/shard_map/dense_turned/pallas_call | solution.py:183
  74.7 1.3 %fusion.2 = bf16[2048,256]{1,0:T(8,128)(2,1)S(1)} fusion(bf16[2048,1024]{1,0:T(8,128)(2,1)S(1)} %dense_turned.1, bf16[1024,256]{1,0:T(8,128)(2,1)S(1)} %pad_maximum_fusion.1, bf16[2048,256]{1,0:T(8,128)(2,1)S(1)} %copy-done.7), kind=kOutput, calls=%fused_computation.4 | convolution fusion | flops 1075838976 | bytes 6815744 | tf_op jit(solution)/shard_map/dot_general | solution.py:32
  76.6 1.3 %collective-permute-done.23 = f32[88,256]{1,0:T(8,128)S(1)} collective-permute-done((f32[88,256]{1,0:T(8,128)S(1)}, f32[88,256]{1,0:T(8,128)S(1)}, u32[]{:S(2)}, u32[]{:S(2)}) %collective-permute-start.23) | collective-permute-done | bytes 90144 | tf_op jit(solution)/shard_map/ppermute | solution.py:243
  78.0 1.5 %collective-permute-start.25 = (bf16[88,256]{1,0:T(8,128)(2,1)S(1)}, bf16[88,256]{1,0:T(8,128)(2,1)S(1)}, u32[]{:S(2)}, u32[]{:S(2)}) collective-permute-start(bf16[88,256]{1,0:T(8,128)(2,1)S(1)} %fusion.15), channel_id=1, source_target_pairs={{0,4},{1,5},{2,6},{3,7},{4,0},{5,1},{6,2},{7,3},{8,12},{9,13},{10,... | collective-permute-start | bytes 135176 | tf_op jit(solution)/shard_map/ppermute | solution.py:243
  79.5 2.8 %collective-permute-start.26 = (bf16[88,256]{1,0:T(8,128)(2,1)S(1)}, bf16[88,256]{1,0:T(8,128)(2,1)S(1)}, u32[]{:S(2)}, u32[]{:S(2)}) collective-permute-start(bf16[88,256]{1,0:T(8,128)(2,1)S(1)} %fusion.15), channel_id=1, source_target_pairs={{0,6},{1,7},{2,4},{3,5},{4,2},{5,3},{6,0},{7,1},{8,14},{9,15},{10,... | collective-permute-start | bytes 135176 | tf_op jit(solution)/shard_map/ppermute | solution.py:243
  82.5 2.1 %collective-permute-done.25 = bf16[88,256]{1,0:T(8,128)(2,1)S(1)} collective-permute-done((bf16[88,256]{1,0:T(8,128)(2,1)S(1)}, bf16[88,256]{1,0:T(8,128)(2,1)S(1)}, u32[]{:S(2)}, u32[]{:S(2)}) %collective-permute-start.25) | collective-permute-done | bytes 45088 | tf_op jit(solution)/shard_map/ppermute | solution.py:243
  85.4 1.7 %collective-permute-start.27 = (bf16[88,256]{1,0:T(8,128)(2,1)S(1)}, bf16[88,256]{1,0:T(8,128)(2,1)S(1)}, u32[]{:S(2)}, u32[]{:S(2)}) collective-permute-start(bf16[88,256]{1,0:T(8,128)(2,1)S(1)} %add_convert_fusion), channel_id=1, source_target_pairs={{0,8},{8,0},{16,24},{24,16},{1,9},{9,1},{17,25},{25,17},{2,10},{10... | collective-permute-start | bytes 135176 | tf_op jit(solution)/shard_map/ppermute | solution.py:229
  89.9 1.3 %collective-permute-done.28 = bf16[88,256]{1,0:T(8,128)(2,1)S(1)} collective-permute-done((bf16[88,256]{1,0:T(8,128)(2,1)S(1)}, bf16[88,256]{1,0:T(8,128)(2,1)S(1)}, u32[]{:S(2)}, u32[]{:S(2)}) %collective-permute-start.28) | collective-permute-done | bytes 45088 | tf_op jit(solution)/shard_map/ppermute | solution.py:229
  91.2 1.7 %collective-permute-done.29 = bf16[88,256]{1,0:T(8,128)(2,1)S(1)} collective-permute-done((bf16[88,256]{1,0:T(8,128)(2,1)S(1)}, bf16[88,256]{1,0:T(8,128)(2,1)S(1)}, u32[]{:S(2)}, u32[]{:S(2)}) %collective-permute-start.29) | collective-permute-done | bytes 45088 | tf_op jit(solution)/shard_map/ppermute | solution.py:229
  94.5 1.3 %last.1 = (f32[128,256]{1,0:T(8,128)}, f32[172,256]{1,0:T(8,128)}) custom-call(s32[2]{0:T(128)S(1)} %pad_add_fusion.1.spot_ref, f32[160,256]{1,0:T(8,128)S(1)} %constant_dynamic-update-slice_fusion.6.total_ref, f32[160,256]{1,0:T(8,128)S(1)} %collective-permute-done.30.other_ref), custom_call_target="tpu_custom_call" | custom-call | tf_op jit(solution)/shard_map/last/pallas_call | solution.py:144
  (119 shorter events, 19.7 us)
Async XLA Ops:
  0.6 50.7 %copy-start = (bf16[128,256]{1,0:T(8,128)(2,1)S(1)}, bf16[128,256]{1,0:T(8,128)(2,1)}, u32[]{:S(2)}) copy-start(bf16[128,256]{1,0:T(8,128)(2,1)} %param.17) | copy-start | bytes 196612
  0.6 13.4 %collective-permute-start = (bf16[256,128]{1,0:T(8,128)(2,1)}, bf16[256,128]{1,0:T(8,128)(2,1)S(1)}, u32[]{:S(2)}, u32[]{:S(2)}) collective-permute-start(bf16[256,128]{1,0:T(8,128)(2,1)} %bitcast.56), channel_id=1, source_target_pairs={{0,0},{1,1},{2,2},{3,3},{4,4},{5,5},{6,6},{7,7},{8,10},{9,11},{10,... | collective-permute-start | bytes 196616 | tf_op jit(solution)/shard_map/ppermute | solution.py:253
  2.3 11.8 %collective-permute-start.1 = (bf16[256,128]{1,0:T(8,128)(2,1)}, bf16[256,128]{1,0:T(8,128)(2,1)S(1)}, u32[]{:S(2)}, u32[]{:S(2)}) collective-permute-start(bf16[256,128]{1,0:T(8,128)(2,1)} %bitcast.57), channel_id=1, source_target_pairs={{0,10},{1,11},{2,12},{3,13},{4,14},{5,15},{6,8},{7,9},{8,0},{9,1},... | collective-permute-start | bytes 196616 | tf_op jit(solution)/shard_map/ppermute | solution.py:253
  8.3 5.9 %collective-permute-start.2 = (bf16[256,128]{1,0:T(8,128)(2,1)}, bf16[256,128]{1,0:T(8,128)(2,1)S(1)}, u32[]{:S(2)}, u32[]{:S(2)}) collective-permute-start(bf16[256,128]{1,0:T(8,128)(2,1)} %bitcast.58), channel_id=1, source_target_pairs={{0,20},{1,21},{2,22},{3,23},{4,16},{5,17},{6,18},{7,19},{8,30},{9,... | collective-permute-start | bytes 196616 | tf_op jit(solution)/shard_map/ppermute | solution.py:253
  9.6 5.4 %collective-permute-start.3 = (bf16[256,128]{1,0:T(8,128)(2,1)}, bf16[256,128]{1,0:T(8,128)(2,1)S(1)}, u32[]{:S(2)}, u32[]{:S(2)}) collective-permute-start(bf16[256,128]{1,0:T(8,128)(2,1)} %bitcast.59), channel_id=1, source_target_pairs={{0,30},{1,31},{2,24},{3,25},{4,26},{5,27},{6,28},{7,29},{8,20},{9,... | collective-permute-start | bytes 196616 | tf_op jit(solution)/shard_map/ppermute | solution.py:253
  14.1 6.2 %collective-permute-start.4 = (bf16[512,128]{1,0:T(8,128)(2,1)S(1)}, bf16[512,128]{1,0:T(8,128)(2,1)S(1)}, u32[]{:S(2)}, u32[]{:S(2)}) collective-permute-start(bf16[512,128]{1,0:T(8,128)(2,1)S(1)} %pad_maximum_fusion.2), channel_id=1, source_target_pairs={{0,1},{1,24},{2,3},{3,26},{4,5},{5,28},{6,7},{7,30},{8,9},{9,0},{1... | collective-permute-start | bytes 393224 | tf_op jit(solution)/shard_map/ppermute | solution.py:240
  15.0 6.5 %collective-permute-start.5 = (bf16[512,128]{1,0:T(8,128)(2,1)S(1)}, bf16[512,128]{1,0:T(8,128)(2,1)S(1)}, u32[]{:S(2)}, u32[]{:S(2)}) collective-permute-start(bf16[512,128]{1,0:T(8,128)(2,1)S(1)} %pad_maximum_fusion.3), channel_id=1, source_target_pairs={{0,1},{1,24},{2,3},{3,26},{4,5},{5,28},{6,7},{7,30},{8,9},{9,0},{1... | collective-permute-start | bytes 393224 | tf_op jit(solution)/shard_map/ppermute | solution.py:240
  22.8 8.8 %collective-permute-start.6 = (f32[256,128]{1,0:T(8,128)S(1)}, f32[256,128]{1,0:T(8,128)S(1)}, u32[]{:S(2)}, u32[]{:S(2)}) collective-permute-start(f32[256,128]{1,0:T(8,128)S(1)} %get-tuple-element.75), channel_id=1, source_target_pairs={{0,8},{8,0},{16,24},{24,16},{1,9},{9,1},{17,25},{25,17},{2,10},{10... | collective-permute-start | bytes 393224 | tf_op jit(solution)/shard_map/ppermute | solution.py:229
  28.1 7.8 %collective-permute-start.7 = (f32[256,128]{1,0:T(8,128)S(1)}, f32[256,128]{1,0:T(8,128)S(1)}, u32[]{:S(2)}, u32[]{:S(2)}) collective-permute-start(f32[256,128]{1,0:T(8,128)S(1)} %get-tuple-element.77), channel_id=1, source_target_pairs={{0,16},{8,24},{16,0},{24,8},{1,17},{9,25},{17,1},{25,9},{2,18},{10... | collective-permute-start | bytes 393224 | tf_op jit(solution)/shard_map/ppermute | solution.py:229
  28.1 7.8 %collective-permute-start.8 = (f32[256,128]{1,0:T(8,128)S(1)}, f32[256,128]{1,0:T(8,128)S(1)}, u32[]{:S(2)}, u32[]{:S(2)}) collective-permute-start(f32[256,128]{1,0:T(8,128)S(1)} %get-tuple-element.76), channel_id=1, source_target_pairs={{0,24},{8,16},{16,8},{24,0},{1,25},{9,17},{17,9},{25,1},{2,26},{10... | collective-permute-start | bytes 393224 | tf_op jit(solution)/shard_map/ppermute | solution.py:229
  35.9 6.9 %collective-permute-start.9 = (bf16[272,128]{1,0:T(8,128)(2,1)S(1)}, bf16[272,128]{1,0:T(8,128)(2,1)S(1)}, u32[]{:S(2)}, u32[]{:S(2)}) collective-permute-start(bf16[272,128]{1,0:T(8,128)(2,1)S(1)} %pad_maximum_fusion.5), channel_id=1, source_target_pairs={{0,0},{1,1},{2,2},{3,3},{4,4},{5,5},{6,6},{7,7},{8,10},{9,11},{10,... | collective-permute-start | bytes 208904 | tf_op jit(solution)/shard_map/ppermute | solution.py:253
  36.6 6.3 %collective-permute-start.10 = (bf16[272,128]{1,0:T(8,128)(2,1)S(1)}, bf16[272,128]{1,0:T(8,128)(2,1)S(1)}, u32[]{:S(2)}, u32[]{:S(2)}) collective-permute-start(bf16[272,128]{1,0:T(8,128)(2,1)S(1)} %pad_maximum_fusion.5), channel_id=1, source_target_pairs={{0,10},{1,11},{2,12},{3,13},{4,14},{5,15},{6,8},{7,9},{8,0},{9,1},... | collective-permute-start | bytes 208904 | tf_op jit(solution)/shard_map/ppermute | solution.py:253
  38.0 6.9 %collective-permute-start.11 = (bf16[272,128]{1,0:T(8,128)(2,1)S(1)}, bf16[272,128]{1,0:T(8,128)(2,1)S(1)}, u32[]{:S(2)}, u32[]{:S(2)}) collective-permute-start(bf16[272,128]{1,0:T(8,128)(2,1)S(1)} %pad_maximum_fusion.5), channel_id=1, source_target_pairs={{0,20},{1,21},{2,22},{3,23},{4,16},{5,17},{6,18},{7,19},{8,30},{9,... | collective-permute-start | bytes 208904 | tf_op jit(solution)/shard_map/ppermute | solution.py:253
  41.7 5.2 %collective-permute-start.12 = (bf16[272,128]{1,0:T(8,128)(2,1)S(1)}, bf16[272,128]{1,0:T(8,128)(2,1)S(1)}, u32[]{:S(2)}, u32[]{:S(2)}) collective-permute-start(bf16[272,128]{1,0:T(8,128)(2,1)S(1)} %pad_maximum_fusion.5), channel_id=1, source_target_pairs={{0,30},{1,31},{2,24},{3,25},{4,26},{5,27},{6,28},{7,29},{8,20},{9,... | collective-permute-start | bytes 208904 | tf_op jit(solution)/shard_map/ppermute | solution.py:253
  42.8 5.0 %collective-permute-start.13 = (bf16[272,128]{1,0:T(8,128)(2,1)S(1)}, bf16[272,128]{1,0:T(8,128)(2,1)S(1)}, u32[]{:S(2)}, u32[]{:S(2)}) collective-permute-start(bf16[272,128]{1,0:T(8,128)(2,1)S(1)} %collective-permute-done.9), channel_id=1, source_target_pairs={{0,1},{1,24},{2,3},{3,26},{4,5},{5,28},{6,7},{7,30},{8,9},{9,0},{1... | collective-permute-start | bytes 208904 | tf_op jit(solution)/shard_map/ppermute | solution.py:240
  42.9 7.8 %collective-permute-start.15 = (bf16[272,128]{1,0:T(8,128)(2,1)S(1)}, bf16[272,128]{1,0:T(8,128)(2,1)S(1)}, u32[]{:S(2)}, u32[]{:S(2)}) collective-permute-start(bf16[272,128]{1,0:T(8,128)(2,1)S(1)} %collective-permute-done.10), channel_id=1, source_target_pairs={{0,1},{1,24},{2,3},{3,26},{4,5},{5,28},{6,7},{7,30},{8,9},{9,0},{1... | collective-permute-start | bytes 208904 | tf_op jit(solution)/shard_map/ppermute | solution.py:240
  44.9 5.8 %collective-permute-start.16 = (bf16[272,128]{1,0:T(8,128)(2,1)S(1)}, bf16[272,128]{1,0:T(8,128)(2,1)S(1)}, u32[]{:S(2)}, u32[]{:S(2)}) collective-permute-start(bf16[272,128]{1,0:T(8,128)(2,1)S(1)} %collective-permute-done.11), channel_id=1, source_target_pairs={{0,1},{1,24},{2,3},{3,26},{4,5},{5,28},{6,7},{7,30},{8,9},{9,0},{1... | collective-permute-start | bytes 208904 | tf_op jit(solution)/shard_map/ppermute | solution.py:240
  46.9 3.7 %collective-permute-start.14 = (bf16[272,128]{1,0:T(8,128)(2,1)S(1)}, bf16[272,128]{1,0:T(8,128)(2,1)S(1)}, u32[]{:S(2)}, u32[]{:S(2)}) collective-permute-start(bf16[272,128]{1,0:T(8,128)(2,1)S(1)} %collective-permute-done.12), channel_id=1, source_target_pairs={{0,1},{1,24},{2,3},{3,26},{4,5},{5,28},{6,7},{7,30},{8,9},{9,0},{1... | collective-permute-start | bytes 208904 | tf_op jit(solution)/shard_map/ppermute | solution.py:240
  53.5 8.1 %collective-permute-start.17 = (s16[272,256]{1,0:T(8,128)(2,1)S(1)}, s16[272,256]{1,0:T(8,128)(2,1)S(1)}, u32[]{:S(2)}, u32[]{:S(2)}) collective-permute-start(s16[272,256]{1,0:T(8,128)(2,1)S(1)} %get-tuple-element.50), channel_id=1, source_target_pairs={{0,8},{8,0},{16,24},{24,16},{1,9},{9,1},{17,25},{25,17},{2,10},{10... | collective-permute-start | bytes 417800 | tf_op jit(solution)/shard_map/ppermute | solution.py:229
  58.1 7.8 %collective-permute-start.18 = (s16[272,256]{1,0:T(8,128)(2,1)S(1)}, s16[272,256]{1,0:T(8,128)(2,1)S(1)}, u32[]{:S(2)}, u32[]{:S(2)}) collective-permute-start(s16[272,256]{1,0:T(8,128)(2,1)S(1)} %get-tuple-element.51), channel_id=1, source_target_pairs={{0,16},{8,24},{16,0},{24,8},{1,17},{9,25},{17,1},{25,9},{2,18},{10... | collective-permute-start | bytes 417800 | tf_op jit(solution)/shard_map/ppermute | solution.py:229
  58.1 7.8 %collective-permute-start.19 = (s16[272,256]{1,0:T(8,128)(2,1)S(1)}, s16[272,256]{1,0:T(8,128)(2,1)S(1)}, u32[]{:S(2)}, u32[]{:S(2)}) collective-permute-start(s16[272,256]{1,0:T(8,128)(2,1)S(1)} %get-tuple-element.52), channel_id=1, source_target_pairs={{0,24},{8,16},{16,8},{24,0},{1,25},{9,17},{17,9},{25,1},{2,26},{10... | collective-permute-start | bytes 417800 | tf_op jit(solution)/shard_map/ppermute | solution.py:229
  67.2 6.7 %collective-permute-start.20 = (bf16[304,256]{1,0:T(8,128)(2,1)S(1)}, bf16[304,256]{1,0:T(8,128)(2,1)S(1)}, u32[]{:S(2)}, u32[]{:S(2)}) collective-permute-start(bf16[304,256]{1,0:T(8,128)(2,1)S(1)} %get-tuple-element.57), channel_id=1, source_target_pairs={{0,8},{8,0},{16,24},{24,16},{1,9},{9,1},{17,25},{25,17},{2,10},{10... | collective-permute-start | bytes 466952 | tf_op jit(solution)/shard_map/ppermute | solution.py:229
  67.4 7.2 %collective-permute-start.21 = (bf16[304,256]{1,0:T(8,128)(2,1)S(1)}, bf16[304,256]{1,0:T(8,128)(2,1)S(1)}, u32[]{:S(2)}, u32[]{:S(2)}) collective-permute-start(bf16[304,256]{1,0:T(8,128)(2,1)S(1)} %get-tuple-element.58), channel_id=1, source_target_pairs={{0,16},{8,24},{16,0},{24,8},{1,17},{9,25},{17,1},{25,9},{2,18},{10... | collective-permute-start | bytes 466952 | tf_op jit(solution)/shard_map/ppermute | solution.py:229
  68.1 6.5 %collective-permute-start.22 = (bf16[304,256]{1,0:T(8,128)(2,1)S(1)}, bf16[304,256]{1,0:T(8,128)(2,1)S(1)}, u32[]{:S(2)}, u32[]{:S(2)}) collective-permute-start(bf16[304,256]{1,0:T(8,128)(2,1)S(1)} %get-tuple-element.59), channel_id=1, source_target_pairs={{0,24},{8,16},{16,8},{24,0},{1,25},{9,17},{17,9},{25,1},{2,26},{10... | collective-permute-start | bytes 466952 | tf_op jit(solution)/shard_map/ppermute | solution.py:229
  76.5 1.4 %collective-permute-start.23 = (f32[88,256]{1,0:T(8,128)S(1)}, f32[88,256]{1,0:T(8,128)S(1)}, u32[]{:S(2)}, u32[]{:S(2)}) collective-permute-start(f32[88,256]{1,0:T(8,128)S(1)} %pad_maximum_fusion.4), channel_id=1, source_target_pairs={{0,1},{1,0},{2,3},{3,2},{4,5},{5,4},{6,7},{7,6},{8,9},{9,8},{10,11... | collective-permute-start | bytes 270344 | tf_op jit(solution)/shard_map/ppermute | solution.py:243
  77.9 4.6 %collective-permute-start.24 = (bf16[88,256]{1,0:T(8,128)(2,1)S(1)}, bf16[88,256]{1,0:T(8,128)(2,1)S(1)}, u32[]{:S(2)}, u32[]{:S(2)}) collective-permute-start(bf16[88,256]{1,0:T(8,128)(2,1)S(1)} %fusion.15), channel_id=1, source_target_pairs={{0,2},{1,3},{2,0},{3,1},{4,6},{5,7},{6,4},{7,5},{8,10},{9,11},{10,... | collective-permute-start | bytes 135176 | tf_op jit(solution)/shard_map/ppermute | solution.py:243
  78.0 6.6 %collective-permute-start.25 = (bf16[88,256]{1,0:T(8,128)(2,1)S(1)}, bf16[88,256]{1,0:T(8,128)(2,1)S(1)}, u32[]{:S(2)}, u32[]{:S(2)}) collective-permute-start(bf16[88,256]{1,0:T(8,128)(2,1)S(1)} %fusion.15), channel_id=1, source_target_pairs={{0,4},{1,5},{2,6},{3,7},{4,0},{5,1},{6,2},{7,3},{8,12},{9,13},{10,... | collective-permute-start | bytes 135176 | tf_op jit(solution)/shard_map/ppermute | solution.py:243
  79.5 5.9 %collective-permute-start.26 = (bf16[88,256]{1,0:T(8,128)(2,1)S(1)}, bf16[88,256]{1,0:T(8,128)(2,1)S(1)}, u32[]{:S(2)}, u32[]{:S(2)}) collective-permute-start(bf16[88,256]{1,0:T(8,128)(2,1)S(1)} %fusion.15), channel_id=1, source_target_pairs={{0,6},{1,7},{2,4},{3,5},{4,2},{5,3},{6,0},{7,1},{8,14},{9,15},{10,... | collective-permute-start | bytes 135176 | tf_op jit(solution)/shard_map/ppermute | solution.py:243
  85.4 4.4 %collective-permute-start.27 = (bf16[88,256]{1,0:T(8,128)(2,1)S(1)}, bf16[88,256]{1,0:T(8,128)(2,1)S(1)}, u32[]{:S(2)}, u32[]{:S(2)}) collective-permute-start(bf16[88,256]{1,0:T(8,128)(2,1)S(1)} %add_convert_fusion), channel_id=1, source_target_pairs={{0,8},{8,0},{16,24},{24,16},{1,9},{9,1},{17,25},{25,17},{2,10},{10... | collective-permute-start | bytes 135176 | tf_op jit(solution)/shard_map/ppermute | solution.py:229
  87.2 4.0 %collective-permute-start.28 = (bf16[88,256]{1,0:T(8,128)(2,1)S(1)}, bf16[88,256]{1,0:T(8,128)(2,1)S(1)}, u32[]{:S(2)}, u32[]{:S(2)}) collective-permute-start(bf16[88,256]{1,0:T(8,128)(2,1)S(1)} %add_convert_fusion), channel_id=1, source_target_pairs={{0,16},{8,24},{16,0},{24,8},{1,17},{9,25},{17,1},{25,9},{2,18},{10... | collective-permute-start | bytes 135176 | tf_op jit(solution)/shard_map/ppermute | solution.py:229
  88.0 4.9 %collective-permute-start.29 = (bf16[88,256]{1,0:T(8,128)(2,1)S(1)}, bf16[88,256]{1,0:T(8,128)(2,1)S(1)}, u32[]{:S(2)}, u32[]{:S(2)}) collective-permute-start(bf16[88,256]{1,0:T(8,128)(2,1)S(1)} %add_convert_fusion), channel_id=1, source_target_pairs={{0,24},{8,16},{16,8},{24,0},{1,25},{9,17},{17,9},{25,1},{2,26},{10... | collective-permute-start | bytes 135176 | tf_op jit(solution)/shard_map/ppermute | solution.py:229
  93.0 1.5 %collective-permute-start.30 = (f32[160,256]{1,0:T(8,128)S(1)}, f32[160,256]{1,0:T(8,128)S(1)}, u32[]{:S(2)}, u32[]{:S(2)}) collective-permute-start(f32[160,256]{1,0:T(8,128)S(1)} %constant_dynamic-update-slice_fusion.6.total_ref), channel_id=1, source_target_pairs={{0,1},{1,0},{2,3},{3,2},{4,5},{5,4},{6,7},{7,6},{8,9},{9,8},{10,11... | collective-permute-start | bytes 491528 | tf_op jit(solution)/shard_map/ppermute | solution.py:243
  (7 other events, 69.0 us)

commit v16 on v15

--- a/solution.py
+++ b/solution.py
@@ -296,9 +296,9 @@
     tiles = tile_values[0, 0]
     next_rep = lax.rem(rep_index + 1, reps)
     where = jnp.where(member < jnp.arange(sections + 1) - 1, next_rep, rep_index)
-    where, arrived[0] = lax.optimization_barrier((where, arrived[0]))
+    where, count, arrived[0] = lax.optimization_barrier((where, count, arrived[0]))
     columns = [jnp.broadcast_to(where[0], (sections, 1)), where[1:, None], count[:, None], place]
-    meta = jnp.concatenate(columns, axis=1)
+    meta, late_ids = lax.optimization_barrier((jnp.concatenate(columns, axis=1), node_ids[0]))
     dense = build_dense(tiles, meta, own_rows, group_rows, False)
     feature_columns = jnp.concatenate(to_all(arrived, reps // 2), axis=0)
     chunks = dot(dense, feature_columns).reshape(reps, own_rows, width)
@@ -307,7 +307,7 @@
     for part in arrived:
         total = total + part
     z_input = total.astype(bf16)
-    z_bundle = jnp.concatenate([z_input, digits(node_ids[0])], axis=0)
+    z_bundle = jnp.concatenate([z_input, digits(late_ids)], axis=0)
     pieces = to_all(to_pieces(z_bundle), 1)
     units = jnp.arange(hidden_width, dtype=jnp.int32)
 

time: 96.2 us -> 95.8 us (level)
    unnamed x29 -> x31, local copies, waits for them, and re-layouts: 2.21 us -> 2.22 us
  transfers between devices with their start and end apart: 31 -> 31, of which waited for: 17 -> 18; matrix products, arithmetic and copies ran while one was open for 6% -> 5% of each run, Pallas kernels for 5% -> 5%
where the time goes in v16:
time: 95.8 us; the launch traced here: 95.6 us
  starting transfers between devices  47.1 us (49%)
  waiting for transfers between devices  27.5 us (29%)
  Pallas kernels  8.3 us (9%)
  matrix products  6.07 us (6%)
  local copies, waits for them, and re-layouts  3.31 us (3%)
  other arithmetic  2.06 us (2%)
  between operations  1.23 us (1%)
    ppermute x12, starting transfers between devices, swap(): return lax.ppermute(value, 'rep', [(r, r ^ delta) for r in range(reps)])  19.8 us
    ppermute x8, starting transfers between devices, to_pieces(): pieces.append(lax.ppermute(value, ('rep', 'blk'), pairs))  18.8 us
    ppermute x12, waiting for transfers between devices, swap(): return lax.ppermute(value, 'rep', [(r, r ^ delta) for r in range(reps)])  15.4 us
    dot_general x5, matrix products, dot(): return jnp.dot(left, right, preferred_element_type=jnp.float32)  5.71 us
    pallas_call x2, Pallas kernels, build_dense(): pl.pallas_call(body, grid_spec=pltpu.PrefetchScalarGridSpec(num_scalar_pr...  5.26 us
    ppermute x5, waiting for transfers between devices, exchange(): return lax.ppermute(value, 'blk', [(c, c ^ delta) for c in range(blks)])  4.85 us
    ppermute x5, starting transfers between devices, exchange(): return lax.ppermute(value, 'blk', [(c, c ^ delta) for c in range(blks)])  4.59 us
    ppermute x6, waiting for transfers between devices, to_section(): return lax.ppermute(block, ('rep', 'blk'), pairs)  4.02 us
  transfers between devices with their start and end apart: 31, of which 18 were waited for; matrix products, arithmetic and copies ran while one was open for 5% of the time, Pallas kernels for 5%

profile of v16, /device:TPU:0, one launch (start us, length us, event | category | flops | bytes accessed | tf_op | source)
XLA Modules:
  0.0 95.6 jit_solution(18171491314381088221)
XLA Ops:
  0.6 1.6 %collective-permute-start = (bf16[256,128]{1,0:T(8,128)(2,1)}, bf16[256,128]{1,0:T(8,128)(2,1)S(1)}, u32[]{:S(2)}, u32[]{:S(2)}) collective-permute-start(bf16[256,128]{1,0:T(8,128)(2,1)} %bitcast.59), channel_id=1, source_target_pairs={{0,0},{1,1},{2,2},{3,3},{4,4},{5,5},{6,6},{7,7},{8,10},{9,11},{10,... | collective-permute-start | bytes 196616 | tf_op jit(solution)/shard_map/ppermute | solution.py:253
  2.3 6.0 %collective-permute-start.1 = (bf16[256,128]{1,0:T(8,128)(2,1)}, bf16[256,128]{1,0:T(8,128)(2,1)S(1)}, u32[]{:S(2)}, u32[]{:S(2)}) collective-permute-start(bf16[256,128]{1,0:T(8,128)(2,1)} %bitcast.60), channel_id=1, source_target_pairs={{0,10},{1,11},{2,12},{3,13},{4,14},{5,15},{6,8},{7,9},{8,0},{9,1},... | collective-permute-start | bytes 196616 | tf_op jit(solution)/shard_map/ppermute | solution.py:253
  8.3 1.3 %collective-permute-start.2 = (bf16[256,128]{1,0:T(8,128)(2,1)}, bf16[256,128]{1,0:T(8,128)(2,1)S(1)}, u32[]{:S(2)}, u32[]{:S(2)}) collective-permute-start(bf16[256,128]{1,0:T(8,128)(2,1)} %bitcast.61), channel_id=1, source_target_pairs={{0,20},{1,21},{2,22},{3,23},{4,16},{5,17},{6,18},{7,19},{8,30},{9,... | collective-permute-start | bytes 196616 | tf_op jit(solution)/shard_map/ppermute | solution.py:253
  9.6 3.0 %collective-permute-start.3 = (bf16[256,128]{1,0:T(8,128)(2,1)}, bf16[256,128]{1,0:T(8,128)(2,1)S(1)}, u32[]{:S(2)}, u32[]{:S(2)}) collective-permute-start(bf16[256,128]{1,0:T(8,128)(2,1)} %bitcast.62), channel_id=1, source_target_pairs={{0,30},{1,31},{2,24},{3,25},{4,26},{5,27},{6,28},{7,29},{8,20},{9,... | collective-permute-start | bytes 196616 | tf_op jit(solution)/shard_map/ppermute | solution.py:253
  17.9 2.1 %dense.1 = bf16[1024,2048]{1,0:T(8,128)(2,1)S(1)} custom-call(s32[2,19]{1,0:T(2,128)S(1)} %pad_add_fusion.meta_ref, bf16[2,16,128,128]{3,2,1,0:T(8,128)(2,1)S(1)} %bitcast.50), custom_call_target="tpu_custom_call" | custom-call | bytes 8388608 | tf_op jit(solution)/shard_map/dense/pallas_call | solution.py:183
  20.1 1.4 %collective-permute-done.5 = bf16[512,128]{1,0:T(8,128)(2,1)S(1)} collective-permute-done((bf16[512,128]{1,0:T(8,128)(2,1)S(1)}, bf16[512,128]{1,0:T(8,128)(2,1)S(1)}, u32[]{:S(2)}, u32[]{:S(2)}) %collective-permute-start.5) | collective-permute-done | bytes 131104 | tf_op jit(solution)/shard_map/ppermute | solution.py:240
  21.5 1.3 %fusion.25 = f32[1024,128]{1,0:T(8,128)S(1)} fusion(bf16[1024,2048]{1,0:T(8,128)(2,1)S(1)} %dense.1, bf16[2048,128]{1,0:T(8,128)(2,1)S(1)} %constant_dynamic-update-slice_fusion), kind=kOutput, calls=%fused_computation.84 | convolution fusion | flops 536870912 | bytes 5242880 | tf_op jit(solution)/shard_map/dot_general | solution.py:32
  22.8 5.2 %collective-permute-start.6 = (f32[256,128]{1,0:T(8,128)S(1)}, f32[256,128]{1,0:T(8,128)S(1)}, u32[]{:S(2)}, u32[]{:S(2)}) collective-permute-start(f32[256,128]{1,0:T(8,128)S(1)} %get-tuple-element.78), channel_id=1, source_target_pairs={{0,8},{8,0},{16,24},{24,16},{1,9},{9,1},{17,25},{25,17},{2,10},{10... | collective-permute-start | bytes 393224 | tf_op jit(solution)/shard_map/ppermute | solution.py:229
  28.0 1.5 %collective-permute-start.8 = (f32[256,128]{1,0:T(8,128)S(1)}, f32[256,128]{1,0:T(8,128)S(1)}, u32[]{:S(2)}, u32[]{:S(2)}) collective-permute-start(f32[256,128]{1,0:T(8,128)S(1)} %get-tuple-element.79), channel_id=1, source_target_pairs={{0,24},{8,16},{16,8},{24,0},{1,25},{9,17},{17,9},{25,1},{2,26},{10... | collective-permute-start | bytes 393224 | tf_op jit(solution)/shard_map/ppermute | solution.py:229
  29.6 2.3 %collective-permute-done.6 = f32[256,128]{1,0:T(8,128)S(1)} collective-permute-done((f32[256,128]{1,0:T(8,128)S(1)}, f32[256,128]{1,0:T(8,128)S(1)}, u32[]{:S(2)}, u32[]{:S(2)}) %collective-permute-start.6) | collective-permute-done | bytes 131104 | tf_op jit(solution)/shard_map/ppermute | solution.py:229
  31.9 3.5 %collective-permute-done.7 = f32[256,128]{1,0:T(8,128)S(1)} collective-permute-done((f32[256,128]{1,0:T(8,128)S(1)}, f32[256,128]{1,0:T(8,128)S(1)}, u32[]{:S(2)}, u32[]{:S(2)}) %collective-permute-start.7) | collective-permute-done | bytes 131104 | tf_op jit(solution)/shard_map/ppermute | solution.py:229
  37.4 4.3 %collective-permute-start.11 = (bf16[272,128]{1,0:T(8,128)(2,1)S(1)}, bf16[272,128]{1,0:T(8,128)(2,1)S(1)}, u32[]{:S(2)}, u32[]{:S(2)}) collective-permute-start(bf16[272,128]{1,0:T(8,128)(2,1)S(1)} %pad_maximum_fusion.5), channel_id=1, source_target_pairs={{0,20},{1,21},{2,22},{3,23},{4,16},{5,17},{6,18},{7,19},{8,30},{9,... | collective-permute-start | bytes 208904 | tf_op jit(solution)/shard_map/ppermute | solution.py:253
  42.5 2.3 %collective-permute-start.15 = (bf16[272,128]{1,0:T(8,128)(2,1)S(1)}, bf16[272,128]{1,0:T(8,128)(2,1)S(1)}, u32[]{:S(2)}, u32[]{:S(2)}) collective-permute-start(bf16[272,128]{1,0:T(8,128)(2,1)S(1)} %collective-permute-done.10), channel_id=1, source_target_pairs={{0,1},{1,24},{2,3},{3,26},{4,5},{5,28},{6,7},{7,30},{8,9},{9,0},{1... | collective-permute-start | bytes 208904 | tf_op jit(solution)/shard_map/ppermute | solution.py:240
  45.0 1.9 %collective-permute-done.12 = bf16[272,128]{1,0:T(8,128)(2,1)S(1)} collective-permute-done((bf16[272,128]{1,0:T(8,128)(2,1)S(1)}, bf16[272,128]{1,0:T(8,128)(2,1)S(1)}, u32[]{:S(2)}, u32[]{:S(2)}) %collective-permute-start.12) | collective-permute-done | bytes 69664 | tf_op jit(solution)/shard_map/ppermute | solution.py:253
  48.0 2.6 %collective-permute-done.14 = bf16[272,128]{1,0:T(8,128)(2,1)S(1)} collective-permute-done((bf16[272,128]{1,0:T(8,128)(2,1)S(1)}, bf16[272,128]{1,0:T(8,128)(2,1)S(1)}, u32[]{:S(2)}, u32[]{:S(2)}) %collective-permute-start.14) | collective-permute-done | bytes 69664 | tf_op jit(solution)/shard_map/ppermute | solution.py:240
  51.8 1.3 %fusion.26.partial_ref.own_ref = f32[1024,256]{1,0:T(8,128)S(1)} fusion(bf16[1024,2048]{1,0:T(8,128)(2,1)S(1)} %dense.1, bf16[2048,256]{1,0:T(8,128)(2,1)S(1)} %fusion.1), kind=kOutput, calls=%fused_computation.85 | convolution fusion | flops 1073741824 | bytes 6291456 | tf_op jit(solution)/shard_map/dot_general | solution.py:32
  53.5 4.3 %collective-permute-start.17 = (s16[272,256]{1,0:T(8,128)(2,1)S(1)}, s16[272,256]{1,0:T(8,128)(2,1)S(1)}, u32[]{:S(2)}, u32[]{:S(2)}) collective-permute-start(s16[272,256]{1,0:T(8,128)(2,1)S(1)} %get-tuple-element.56), channel_id=1, source_target_pairs={{0,8},{8,0},{16,24},{24,16},{1,9},{9,1},{17,25},{25,17},{2,10},{10... | collective-permute-start | bytes 417800 | tf_op jit(solution)/shard_map/ppermute | solution.py:229
  57.9 1.5 %collective-permute-start.19 = (s16[272,256]{1,0:T(8,128)(2,1)S(1)}, s16[272,256]{1,0:T(8,128)(2,1)S(1)}, u32[]{:S(2)}, u32[]{:S(2)}) collective-permute-start(s16[272,256]{1,0:T(8,128)(2,1)S(1)} %get-tuple-element.58), channel_id=1, source_target_pairs={{0,24},{8,16},{16,8},{24,0},{1,25},{9,17},{17,9},{25,1},{2,26},{10... | collective-permute-start | bytes 417800 | tf_op jit(solution)/shard_map/ppermute | solution.py:229
  59.4 1.4 %fusion.3 = bf16[2048,256]{1,0:T(8,128)(2,1)} fusion(bf16[2048,256]{1,0:T(8,128)(2,1)S(1)} %pad_maximum_fusion, bf16[2048,128]{1,0:T(8,128)(2,1)S(1)} %slice_dynamic-update-slice_fusion, bf16[128,256]{1,0:T(8,128)(2,1)S(1)} %copy-done), kind=kOutput, calls=%fused_computation.6 | convolution fusion | flops 135266304 | bytes 2686976 | tf_op jit(solution)/shard_map/dot_general | solution.py:32
  61.5 4.2 %collective-permute-done.18.refs_1_ = s16[272,256]{1,0:T(8,128)(2,1)S(1)} collective-permute-done((s16[272,256]{1,0:T(8,128)(2,1)S(1)}, s16[272,256]{1,0:T(8,128)(2,1)S(1)}, u32[]{:S(2)}, u32[]{:S(2)}) %collective-permute-start.18) | collective-permute-done | bytes 139296 | tf_op jit(solution)/shard_map/ppermute | solution.py:229
  65.7 1.3 %head.1 = (f32[256,172]{1,0:T(8,128)S(1)}, f32[48,256]{1,0:T(8,128)S(1)}, bf16[304,256]{1,0:T(8,128)(2,1)S(1)}, bf16[304,256]{1,0:T(8,128)(2,1)S(1)}, bf16[304,2...) custom-call(s32[2]{0:T(128)S(1)} %pad_add_fusion.1.spot_ref, bf16[172,256]{1,0:T(8,128)(2,1)S(1)} %bitcast.53, ...), custom_call_target="tpu_custom_call" | custom-call | tf_op jit(solution)/shard_map/head/pallas_call | solution.py:144
  67.9 2.7 %collective-permute-start.22 = (bf16[304,256]{1,0:T(8,128)(2,1)S(1)}, bf16[304,256]{1,0:T(8,128)(2,1)S(1)}, u32[]{:S(2)}, u32[]{:S(2)}) collective-permute-start(bf16[304,256]{1,0:T(8,128)(2,1)S(1)} %get-tuple-element.65), channel_id=1, source_target_pairs={{0,24},{8,16},{16,8},{24,0},{1,25},{9,17},{17,9},{25,1},{2,26},{10... | collective-permute-start | bytes 466952 | tf_op jit(solution)/shard_map/ppermute | solution.py:229
  70.6 3.1 %dense_turned.1 = bf16[2048,1024]{1,0:T(8,128)(2,1)S(1)} custom-call(s32[2,19]{1,0:T(2,128)S(1)} %pad_add_fusion.meta_ref, bf16[2,16,128,128]{3,2,1,0:T(8,128)(2,1)S(1)} %bitcast.51), custom_call_target="tpu_custom_call" | custom-call | bytes 8388608 | tf_op jit(solution)/shard_map/dense_turned/pallas_call | solution.py:183
  74.3 1.3 %fusion.2 = bf16[2048,256]{1,0:T(8,128)(2,1)S(1)} fusion(bf16[2048,1024]{1,0:T(8,128)(2,1)S(1)} %dense_turned.1, bf16[1024,256]{1,0:T(8,128)(2,1)S(1)} %pad_maximum_fusion.1, bf16[2048,256]{1,0:T(8,128)(2,1)S(1)} %copy-done.7), kind=kOutput, calls=%fused_computation.4 | convolution fusion | flops 1075838976 | bytes 6815744 | tf_op jit(solution)/shard_map/dot_general | solution.py:32
  76.1 1.3 %collective-permute-done.23 = f32[88,256]{1,0:T(8,128)S(1)} collective-permute-done((f32[88,256]{1,0:T(8,128)S(1)}, f32[88,256]{1,0:T(8,128)S(1)}, u32[]{:S(2)}, u32[]{:S(2)}) %collective-permute-start.23) | collective-permute-done | bytes 90144 | tf_op jit(solution)/shard_map/ppermute | solution.py:243
  77.5 1.5 %collective-permute-start.25 = (bf16[88,256]{1,0:T(8,128)(2,1)S(1)}, bf16[88,256]{1,0:T(8,128)(2,1)S(1)}, u32[]{:S(2)}, u32[]{:S(2)}) collective-permute-start(bf16[88,256]{1,0:T(8,128)(2,1)S(1)} %fusion.15), channel_id=1, source_target_pairs={{0,4},{1,5},{2,6},{3,7},{4,0},{5,1},{6,2},{7,3},{8,12},{9,13},{10,... | collective-permute-start | bytes 135176 | tf_op jit(solution)/shard_map/ppermute | solution.py:243
  79.0 2.9 %collective-permute-start.26 = (bf16[88,256]{1,0:T(8,128)(2,1)S(1)}, bf16[88,256]{1,0:T(8,128)(2,1)S(1)}, u32[]{:S(2)}, u32[]{:S(2)}) collective-permute-start(bf16[88,256]{1,0:T(8,128)(2,1)S(1)} %fusion.15), channel_id=1, source_target_pairs={{0,6},{1,7},{2,4},{3,5},{4,2},{5,3},{6,0},{7,1},{8,14},{9,15},{10,... | collective-permute-start | bytes 135176 | tf_op jit(solution)/shard_map/ppermute | solution.py:243
  82.0 2.1 %collective-permute-done.25 = bf16[88,256]{1,0:T(8,128)(2,1)S(1)} collective-permute-done((bf16[88,256]{1,0:T(8,128)(2,1)S(1)}, bf16[88,256]{1,0:T(8,128)(2,1)S(1)}, u32[]{:S(2)}, u32[]{:S(2)}) %collective-permute-start.25) | collective-permute-done | bytes 45088 | tf_op jit(solution)/shard_map/ppermute | solution.py:243
  84.9 1.7 %collective-permute-start.27 = (bf16[88,256]{1,0:T(8,128)(2,1)S(1)}, bf16[88,256]{1,0:T(8,128)(2,1)S(1)}, u32[]{:S(2)}, u32[]{:S(2)}) collective-permute-start(bf16[88,256]{1,0:T(8,128)(2,1)S(1)} %add_convert_fusion), channel_id=1, source_target_pairs={{0,8},{8,0},{16,24},{24,16},{1,9},{9,1},{17,25},{25,17},{2,10},{10... | collective-permute-start | bytes 135176 | tf_op jit(solution)/shard_map/ppermute | solution.py:229
  89.4 1.3 %collective-permute-done.28 = bf16[88,256]{1,0:T(8,128)(2,1)S(1)} collective-permute-done((bf16[88,256]{1,0:T(8,128)(2,1)S(1)}, bf16[88,256]{1,0:T(8,128)(2,1)S(1)}, u32[]{:S(2)}, u32[]{:S(2)}) %collective-permute-start.28) | collective-permute-done | bytes 45088 | tf_op jit(solution)/shard_map/ppermute | solution.py:229
  90.6 2.1 %collective-permute-done.29 = bf16[88,256]{1,0:T(8,128)(2,1)S(1)} collective-permute-done((bf16[88,256]{1,0:T(8,128)(2,1)S(1)}, bf16[88,256]{1,0:T(8,128)(2,1)S(1)}, u32[]{:S(2)}, u32[]{:S(2)}) %collective-permute-start.29) | collective-permute-done | bytes 45088 | tf_op jit(solution)/shard_map/ppermute | solution.py:229
  94.3 1.3 %last.1 = (f32[128,256]{1,0:T(8,128)}, f32[172,256]{1,0:T(8,128)}) custom-call(s32[2]{0:T(128)S(1)} %pad_add_fusion.1.spot_ref, f32[160,256]{1,0:T(8,128)S(1)} %constant_dynamic-update-slice_fusion.6.total_ref, f32[160,256]{1,0:T(8,128)S(1)} %collective-permute-done.30.other_ref), custom_call_target="tpu_custom_call" | custom-call | tf_op jit(solution)/shard_map/last/pallas_call | solution.py:144
  (121 shorter events, 18.5 us)
Async XLA Ops:
  0.6 50.7 %copy-start = (bf16[128,256]{1,0:T(8,128)(2,1)S(1)}, bf16[128,256]{1,0:T(8,128)(2,1)}, u32[]{:S(2)}) copy-start(bf16[128,256]{1,0:T(8,128)(2,1)} %param.17) | copy-start | bytes 196612
  0.6 11.9 %collective-permute-start = (bf16[256,128]{1,0:T(8,128)(2,1)}, bf16[256,128]{1,0:T(8,128)(2,1)S(1)}, u32[]{:S(2)}, u32[]{:S(2)}) collective-permute-start(bf16[256,128]{1,0:T(8,128)(2,1)} %bitcast.59), channel_id=1, source_target_pairs={{0,0},{1,1},{2,2},{3,3},{4,4},{5,5},{6,6},{7,7},{8,10},{9,11},{10,... | collective-permute-start | bytes 196616 | tf_op jit(solution)/shard_map/ppermute | solution.py:253
  2.3 11.3 %collective-permute-start.1 = (bf16[256,128]{1,0:T(8,128)(2,1)}, bf16[256,128]{1,0:T(8,128)(2,1)S(1)}, u32[]{:S(2)}, u32[]{:S(2)}) collective-permute-start(bf16[256,128]{1,0:T(8,128)(2,1)} %bitcast.60), channel_id=1, source_target_pairs={{0,10},{1,11},{2,12},{3,13},{4,14},{5,15},{6,8},{7,9},{8,0},{9,1},... | collective-permute-start | bytes 196616 | tf_op jit(solution)/shard_map/ppermute | solution.py:253
  8.3 5.6 %collective-permute-start.2 = (bf16[256,128]{1,0:T(8,128)(2,1)}, bf16[256,128]{1,0:T(8,128)(2,1)S(1)}, u32[]{:S(2)}, u32[]{:S(2)}) collective-permute-start(bf16[256,128]{1,0:T(8,128)(2,1)} %bitcast.61), channel_id=1, source_target_pairs={{0,20},{1,21},{2,22},{3,23},{4,16},{5,17},{6,18},{7,19},{8,30},{9,... | collective-permute-start | bytes 196616 | tf_op jit(solution)/shard_map/ppermute | solution.py:253
  9.6 5.4 %collective-permute-start.3 = (bf16[256,128]{1,0:T(8,128)(2,1)}, bf16[256,128]{1,0:T(8,128)(2,1)S(1)}, u32[]{:S(2)}, u32[]{:S(2)}) collective-permute-start(bf16[256,128]{1,0:T(8,128)(2,1)} %bitcast.62), channel_id=1, source_target_pairs={{0,30},{1,31},{2,24},{3,25},{4,26},{5,27},{6,28},{7,29},{8,20},{9,... | collective-permute-start | bytes 196616 | tf_op jit(solution)/shard_map/ppermute | solution.py:253
  13.6 6.5 %collective-permute-start.4 = (bf16[512,128]{1,0:T(8,128)(2,1)S(1)}, bf16[512,128]{1,0:T(8,128)(2,1)S(1)}, u32[]{:S(2)}, u32[]{:S(2)}) collective-permute-start(bf16[512,128]{1,0:T(8,128)(2,1)S(1)} %pad_maximum_fusion.2), channel_id=1, source_target_pairs={{0,1},{1,24},{2,3},{3,26},{4,5},{5,28},{6,7},{7,30},{8,9},{9,0},{1... | collective-permute-start | bytes 393224 | tf_op jit(solution)/shard_map/ppermute | solution.py:240
  15.0 6.5 %collective-permute-start.5 = (bf16[512,128]{1,0:T(8,128)(2,1)S(1)}, bf16[512,128]{1,0:T(8,128)(2,1)S(1)}, u32[]{:S(2)}, u32[]{:S(2)}) collective-permute-start(bf16[512,128]{1,0:T(8,128)(2,1)S(1)} %pad_maximum_fusion.3), channel_id=1, source_target_pairs={{0,1},{1,24},{2,3},{3,26},{4,5},{5,28},{6,7},{7,30},{8,9},{9,0},{1... | collective-permute-start | bytes 393224 | tf_op jit(solution)/shard_map/ppermute | solution.py:240
  22.8 9.1 %collective-permute-start.6 = (f32[256,128]{1,0:T(8,128)S(1)}, f32[256,128]{1,0:T(8,128)S(1)}, u32[]{:S(2)}, u32[]{:S(2)}) collective-permute-start(f32[256,128]{1,0:T(8,128)S(1)} %get-tuple-element.78), channel_id=1, source_target_pairs={{0,8},{8,0},{16,24},{24,16},{1,9},{9,1},{17,25},{25,17},{2,10},{10... | collective-permute-start | bytes 393224 | tf_op jit(solution)/shard_map/ppermute | solution.py:229
  28.0 7.4 %collective-permute-start.7 = (f32[256,128]{1,0:T(8,128)S(1)}, f32[256,128]{1,0:T(8,128)S(1)}, u32[]{:S(2)}, u32[]{:S(2)}) collective-permute-start(f32[256,128]{1,0:T(8,128)S(1)} %get-tuple-element.80), channel_id=1, source_target_pairs={{0,16},{8,24},{16,0},{24,8},{1,17},{9,25},{17,1},{25,9},{2,18},{10... | collective-permute-start | bytes 393224 | tf_op jit(solution)/shard_map/ppermute | solution.py:229
  28.0 7.4 %collective-permute-start.8 = (f32[256,128]{1,0:T(8,128)S(1)}, f32[256,128]{1,0:T(8,128)S(1)}, u32[]{:S(2)}, u32[]{:S(2)}) collective-permute-start(f32[256,128]{1,0:T(8,128)S(1)} %get-tuple-element.79), channel_id=1, source_target_pairs={{0,24},{8,16},{16,8},{24,0},{1,25},{9,17},{17,9},{25,1},{2,26},{10... | collective-permute-start | bytes 393224 | tf_op jit(solution)/shard_map/ppermute | solution.py:229
  35.5 6.9 %collective-permute-start.9 = (bf16[272,128]{1,0:T(8,128)(2,1)S(1)}, bf16[272,128]{1,0:T(8,128)(2,1)S(1)}, u32[]{:S(2)}, u32[]{:S(2)}) collective-permute-start(bf16[272,128]{1,0:T(8,128)(2,1)S(1)} %pad_maximum_fusion.5), channel_id=1, source_target_pairs={{0,0},{1,1},{2,2},{3,3},{4,4},{5,5},{6,6},{7,7},{8,10},{9,11},{10,... | collective-permute-start | bytes 208904 | tf_op jit(solution)/shard_map/ppermute | solution.py:253
  36.3 6.3 %collective-permute-start.10 = (bf16[272,128]{1,0:T(8,128)(2,1)S(1)}, bf16[272,128]{1,0:T(8,128)(2,1)S(1)}, u32[]{:S(2)}, u32[]{:S(2)}) collective-permute-start(bf16[272,128]{1,0:T(8,128)(2,1)S(1)} %pad_maximum_fusion.5), channel_id=1, source_target_pairs={{0,10},{1,11},{2,12},{3,13},{4,14},{5,15},{6,8},{7,9},{8,0},{9,1},... | collective-permute-start | bytes 208904 | tf_op jit(solution)/shard_map/ppermute | solution.py:253
  37.4 7.4 %collective-permute-start.11 = (bf16[272,128]{1,0:T(8,128)(2,1)S(1)}, bf16[272,128]{1,0:T(8,128)(2,1)S(1)}, u32[]{:S(2)}, u32[]{:S(2)}) collective-permute-start(bf16[272,128]{1,0:T(8,128)(2,1)S(1)} %pad_maximum_fusion.5), channel_id=1, source_target_pairs={{0,20},{1,21},{2,22},{3,23},{4,16},{5,17},{6,18},{7,19},{8,30},{9,... | collective-permute-start | bytes 208904 | tf_op jit(solution)/shard_map/ppermute | solution.py:253
  41.7 5.2 %collective-permute-start.12 = (bf16[272,128]{1,0:T(8,128)(2,1)S(1)}, bf16[272,128]{1,0:T(8,128)(2,1)S(1)}, u32[]{:S(2)}, u32[]{:S(2)}) collective-permute-start(bf16[272,128]{1,0:T(8,128)(2,1)S(1)} %pad_maximum_fusion.5), channel_id=1, source_target_pairs={{0,30},{1,31},{2,24},{3,25},{4,26},{5,27},{6,28},{7,29},{8,20},{9,... | collective-permute-start | bytes 208904 | tf_op jit(solution)/shard_map/ppermute | solution.py:253
  42.5 5.1 %collective-permute-start.13 = (bf16[272,128]{1,0:T(8,128)(2,1)S(1)}, bf16[272,128]{1,0:T(8,128)(2,1)S(1)}, u32[]{:S(2)}, u32[]{:S(2)}) collective-permute-start(bf16[272,128]{1,0:T(8,128)(2,1)S(1)} %collective-permute-done.9), channel_id=1, source_target_pairs={{0,1},{1,24},{2,3},{3,26},{4,5},{5,28},{6,7},{7,30},{8,9},{9,0},{1... | collective-permute-start | bytes 208904 | tf_op jit(solution)/shard_map/ppermute | solution.py:240
  42.5 8.2 %collective-permute-start.15 = (bf16[272,128]{1,0:T(8,128)(2,1)S(1)}, bf16[272,128]{1,0:T(8,128)(2,1)S(1)}, u32[]{:S(2)}, u32[]{:S(2)}) collective-permute-start(bf16[272,128]{1,0:T(8,128)(2,1)S(1)} %collective-permute-done.10), channel_id=1, source_target_pairs={{0,1},{1,24},{2,3},{3,26},{4,5},{5,28},{6,7},{7,30},{8,9},{9,0},{1... | collective-permute-start | bytes 208904 | tf_op jit(solution)/shard_map/ppermute | solution.py:240
  44.8 5.8 %collective-permute-start.16 = (bf16[272,128]{1,0:T(8,128)(2,1)S(1)}, bf16[272,128]{1,0:T(8,128)(2,1)S(1)}, u32[]{:S(2)}, u32[]{:S(2)}) collective-permute-start(bf16[272,128]{1,0:T(8,128)(2,1)S(1)} %collective-permute-done.11), channel_id=1, source_target_pairs={{0,1},{1,24},{2,3},{3,26},{4,5},{5,28},{6,7},{7,30},{8,9},{9,0},{1... | collective-permute-start | bytes 208904 | tf_op jit(solution)/shard_map/ppermute | solution.py:240
  46.9 3.7 %collective-permute-start.14 = (bf16[272,128]{1,0:T(8,128)(2,1)S(1)}, bf16[272,128]{1,0:T(8,128)(2,1)S(1)}, u32[]{:S(2)}, u32[]{:S(2)}) collective-permute-start(bf16[272,128]{1,0:T(8,128)(2,1)S(1)} %collective-permute-done.12), channel_id=1, source_target_pairs={{0,1},{1,24},{2,3},{3,26},{4,5},{5,28},{6,7},{7,30},{8,9},{9,0},{1... | collective-permute-start | bytes 208904 | tf_op jit(solution)/shard_map/ppermute | solution.py:240
  53.5 7.9 %collective-permute-start.17 = (s16[272,256]{1,0:T(8,128)(2,1)S(1)}, s16[272,256]{1,0:T(8,128)(2,1)S(1)}, u32[]{:S(2)}, u32[]{:S(2)}) collective-permute-start(s16[272,256]{1,0:T(8,128)(2,1)S(1)} %get-tuple-element.56), channel_id=1, source_target_pairs={{0,8},{8,0},{16,24},{24,16},{1,9},{9,1},{17,25},{25,17},{2,10},{10... | collective-permute-start | bytes 417800 | tf_op jit(solution)/shard_map/ppermute | solution.py:229
  57.9 7.8 %collective-permute-start.18 = (s16[272,256]{1,0:T(8,128)(2,1)S(1)}, s16[272,256]{1,0:T(8,128)(2,1)S(1)}, u32[]{:S(2)}, u32[]{:S(2)}) collective-permute-start(s16[272,256]{1,0:T(8,128)(2,1)S(1)} %get-tuple-element.57), channel_id=1, source_target_pairs={{0,16},{8,24},{16,0},{24,8},{1,17},{9,25},{17,1},{25,9},{2,18},{10... | collective-permute-start | bytes 417800 | tf_op jit(solution)/shard_map/ppermute | solution.py:229
  57.9 7.8 %collective-permute-start.19 = (s16[272,256]{1,0:T(8,128)(2,1)S(1)}, s16[272,256]{1,0:T(8,128)(2,1)S(1)}, u32[]{:S(2)}, u32[]{:S(2)}) collective-permute-start(s16[272,256]{1,0:T(8,128)(2,1)S(1)} %get-tuple-element.58), channel_id=1, source_target_pairs={{0,24},{8,16},{16,8},{24,0},{1,25},{9,17},{17,9},{25,1},{2,26},{10... | collective-permute-start | bytes 417800 | tf_op jit(solution)/shard_map/ppermute | solution.py:229
  67.1 6.7 %collective-permute-start.20 = (bf16[304,256]{1,0:T(8,128)(2,1)S(1)}, bf16[304,256]{1,0:T(8,128)(2,1)S(1)}, u32[]{:S(2)}, u32[]{:S(2)}) collective-permute-start(bf16[304,256]{1,0:T(8,128)(2,1)S(1)} %get-tuple-element.63), channel_id=1, source_target_pairs={{0,8},{8,0},{16,24},{24,16},{1,9},{9,1},{17,25},{25,17},{2,10},{10... | collective-permute-start | bytes 466952 | tf_op jit(solution)/shard_map/ppermute | solution.py:229
  67.3 6.9 %collective-permute-start.21 = (bf16[304,256]{1,0:T(8,128)(2,1)S(1)}, bf16[304,256]{1,0:T(8,128)(2,1)S(1)}, u32[]{:S(2)}, u32[]{:S(2)}) collective-permute-start(bf16[304,256]{1,0:T(8,128)(2,1)S(1)} %get-tuple-element.64), channel_id=1, source_target_pairs={{0,16},{8,24},{16,0},{24,8},{1,17},{9,25},{17,1},{25,9},{2,18},{10... | collective-permute-start | bytes 466952 | tf_op jit(solution)/shard_map/ppermute | solution.py:229
  67.9 6.2 %collective-permute-start.22 = (bf16[304,256]{1,0:T(8,128)(2,1)S(1)}, bf16[304,256]{1,0:T(8,128)(2,1)S(1)}, u32[]{:S(2)}, u32[]{:S(2)}) collective-permute-start(bf16[304,256]{1,0:T(8,128)(2,1)S(1)} %get-tuple-element.65), channel_id=1, source_target_pairs={{0,24},{8,16},{16,8},{24,0},{1,25},{9,17},{17,9},{25,1},{2,26},{10... | collective-permute-start | bytes 466952 | tf_op jit(solution)/shard_map/ppermute | solution.py:229
  76.1 1.4 %collective-permute-start.23 = (f32[88,256]{1,0:T(8,128)S(1)}, f32[88,256]{1,0:T(8,128)S(1)}, u32[]{:S(2)}, u32[]{:S(2)}) collective-permute-start(f32[88,256]{1,0:T(8,128)S(1)} %pad_maximum_fusion.4), channel_id=1, source_target_pairs={{0,1},{1,0},{2,3},{3,2},{4,5},{5,4},{6,7},{7,6},{8,9},{9,8},{10,11... | collective-permute-start | bytes 270344 | tf_op jit(solution)/shard_map/ppermute | solution.py:243
  77.4 4.6 %collective-permute-start.24 = (bf16[88,256]{1,0:T(8,128)(2,1)S(1)}, bf16[88,256]{1,0:T(8,128)(2,1)S(1)}, u32[]{:S(2)}, u32[]{:S(2)}) collective-permute-start(bf16[88,256]{1,0:T(8,128)(2,1)S(1)} %fusion.15), channel_id=1, source_target_pairs={{0,2},{1,3},{2,0},{3,1},{4,6},{5,7},{6,4},{7,5},{8,10},{9,11},{10,... | collective-permute-start | bytes 135176 | tf_op jit(solution)/shard_map/ppermute | solution.py:243
  77.5 6.6 %collective-permute-start.25 = (bf16[88,256]{1,0:T(8,128)(2,1)S(1)}, bf16[88,256]{1,0:T(8,128)(2,1)S(1)}, u32[]{:S(2)}, u32[]{:S(2)}) collective-permute-start(bf16[88,256]{1,0:T(8,128)(2,1)S(1)} %fusion.15), channel_id=1, source_target_pairs={{0,4},{1,5},{2,6},{3,7},{4,0},{5,1},{6,2},{7,3},{8,12},{9,13},{10,... | collective-permute-start | bytes 135176 | tf_op jit(solution)/shard_map/ppermute | solution.py:243
  79.0 5.9 %collective-permute-start.26 = (bf16[88,256]{1,0:T(8,128)(2,1)S(1)}, bf16[88,256]{1,0:T(8,128)(2,1)S(1)}, u32[]{:S(2)}, u32[]{:S(2)}) collective-permute-start(bf16[88,256]{1,0:T(8,128)(2,1)S(1)} %fusion.15), channel_id=1, source_target_pairs={{0,6},{1,7},{2,4},{3,5},{4,2},{5,3},{6,0},{7,1},{8,14},{9,15},{10,... | collective-permute-start | bytes 135176 | tf_op jit(solution)/shard_map/ppermute | solution.py:243
  84.9 4.4 %collective-permute-start.27 = (bf16[88,256]{1,0:T(8,128)(2,1)S(1)}, bf16[88,256]{1,0:T(8,128)(2,1)S(1)}, u32[]{:S(2)}, u32[]{:S(2)}) collective-permute-start(bf16[88,256]{1,0:T(8,128)(2,1)S(1)} %add_convert_fusion), channel_id=1, source_target_pairs={{0,8},{8,0},{16,24},{24,16},{1,9},{9,1},{17,25},{25,17},{2,10},{10... | collective-permute-start | bytes 135176 | tf_op jit(solution)/shard_map/ppermute | solution.py:229
  86.6 4.0 %collective-permute-start.28 = (bf16[88,256]{1,0:T(8,128)(2,1)S(1)}, bf16[88,256]{1,0:T(8,128)(2,1)S(1)}, u32[]{:S(2)}, u32[]{:S(2)}) collective-permute-start(bf16[88,256]{1,0:T(8,128)(2,1)S(1)} %add_convert_fusion), channel_id=1, source_target_pairs={{0,16},{8,24},{16,0},{24,8},{1,17},{9,25},{17,1},{25,9},{2,18},{10... | collective-permute-start | bytes 135176 | tf_op jit(solution)/shard_map/ppermute | solution.py:229
  87.8 4.9 %collective-permute-start.29 = (bf16[88,256]{1,0:T(8,128)(2,1)S(1)}, bf16[88,256]{1,0:T(8,128)(2,1)S(1)}, u32[]{:S(2)}, u32[]{:S(2)}) collective-permute-start(bf16[88,256]{1,0:T(8,128)(2,1)S(1)} %add_convert_fusion), channel_id=1, source_target_pairs={{0,24},{8,16},{16,8},{24,0},{1,25},{9,17},{17,9},{25,1},{2,26},{10... | collective-permute-start | bytes 135176 | tf_op jit(solution)/shard_map/ppermute | solution.py:229
  92.8 1.5 %collective-permute-start.30 = (f32[160,256]{1,0:T(8,128)S(1)}, f32[160,256]{1,0:T(8,128)S(1)}, u32[]{:S(2)}, u32[]{:S(2)}) collective-permute-start(f32[160,256]{1,0:T(8,128)S(1)} %constant_dynamic-update-slice_fusion.6.total_ref), channel_id=1, source_target_pairs={{0,1},{1,0},{2,3},{3,2},{4,5},{5,4},{6,7},{7,6},{8,9},{9,8},{10,11... | collective-permute-start | bytes 491528 | tf_op jit(solution)/shard_map/ppermute | solution.py:243
  (8 other events, 76.1 us)

commit v17 on v16

--- a/solution.py
+++ b/solution.py
@@ -302,7 +302,8 @@
     dense = build_dense(tiles, meta, own_rows, group_rows, False)
     feature_columns = jnp.concatenate(to_all(arrived, reps // 2), axis=0)
     chunks = dot(dense, feature_columns).reshape(reps, own_rows, width)
-    arrived = [swap(chunks[delta], delta) for delta in range(1, reps)]
+    far_first = range(reps - 1, 0, -1)
+    arrived = [swap(chunks[delta], delta) for delta in far_first]
     total = chunks[0]
     for part in arrived:
         total = total + part
@@ -333,7 +334,7 @@
         [jax.ShapeDtypeStruct((own_rows + HEAD_ROWS, hidden_width), jnp.int16)] * (reps - 1),
         "encode", second,
     )
-    arrived = [swap(sent[d - 1], d) for d in range(1, reps)]
+    arrived = [swap(sent[d - 1], d) for d in far_first]
     classes = weight_out.shape[1]
     chunk = -(-classes // (16 * reps)) * 16
     spot = jnp.stack([side, rep_index])
@@ -350,7 +351,7 @@
         spot=(spot,),
         scratch=[pltpu.VMEM((chunk * reps, hidden_width), f32)],
     )
-    arrived = [swap(sent[d], d) for d in range(reps)]
+    arrived = [swap(sent[d], d) for d in range(reps - 1, -1, -1)][::-1]
     meta, out_total = lax.optimization_barrier((meta, out_total))
     turned = build_dense(tiles, meta, own_rows, group_rows, True)
     grad_block = jnp.concatenate([part[:own_rows] for part in arrived], axis=0)
@@ -374,7 +375,7 @@
 
     total = halves(side) + exchange(halves(1 - side), 1)
     total = sum_over(total, exchange, 2, blks).astype(bf16)
-    arrived = [swap(total, d) for d in range(reps)]
+    arrived = [swap(total, d) for d in range(reps - 1, -1, -1)][::-1]
     parts = [part[:half].astype(f32) for part in arrived]
     while len(parts) > 1:
         parts = [parts[i] + parts[i + 1] for i in range(0, len(parts), 2)]

time: 95.8 us -> 95.6 us (level)
    ppermute x5, waiting for transfers between devices: 4.85 us -> 6.67 us  [exchange(): return lax.ppermute(value, 'blk', [(c, c ^ delta) for c in range(blks)])]
    ppermute x12, waiting for transfers between devices: 15.4 us -> 13.8 us  [swap(): return lax.ppermute(value, 'rep', [(r, r ^ delta) for r in range(reps)])]
    ppermute x6, starting transfers between devices: 3.99 us -> 4.98 us  [to_section(): return lax.ppermute(block, ('rep', 'blk'), pairs)]
  transfers between devices with their start and end apart: 31 -> 31, of which waited for: 18 -> 18; matrix products, arithmetic and copies ran while one was open for 5% -> 5% of each run, Pallas kernels for 5% -> 6%
where the time goes in v17:
time: 95.6 us; the launch traced here: 95.4 us
  starting transfers between devices  47.5 us (50%)
  waiting for transfers between devices  26.9 us (28%)
  Pallas kernels  8.3 us (9%)
  matrix products  6.06 us (6%)
  local copies, waits for them, and re-layouts  3.31 us (3%)
  other arithmetic  2.06 us (2%)
  between operations  1.22 us (1%)
    ppermute x12, starting transfers between devices, swap(): return lax.ppermute(value, 'rep', [(r, r ^ delta) for r in range(reps)])  19.2 us
    ppermute x8, starting transfers between devices, to_pieces(): pieces.append(lax.ppermute(value, ('rep', 'blk'), pairs))  18.8 us
    ppermute x12, waiting for transfers between devices, swap(): return lax.ppermute(value, 'rep', [(r, r ^ delta) for r in range(reps)])  13.8 us
    ppermute x5, waiting for transfers between devices, exchange(): return lax.ppermute(value, 'blk', [(c, c ^ delta) for c in range(blks)])  6.67 us
    dot_general x5, matrix products, dot(): return jnp.dot(left, right, preferred_element_type=jnp.float32)  5.7 us
    pallas_call x2, Pallas kernels, build_dense(): pl.pallas_call(body, grid_spec=pltpu.PrefetchScalarGridSpec(num_scalar_pr...  5.26 us
    ppermute x6, starting transfers between devices, to_section(): return lax.ppermute(block, ('rep', 'blk'), pairs)  4.98 us
    ppermute x5, starting transfers between devices, exchange(): return lax.ppermute(value, 'blk', [(c, c ^ delta) for c in range(blks)])  4.59 us
  transfers between devices with their start and end apart: 31, of which 18 were waited for; matrix products, arithmetic and copies ran while one was open for 5% of the time, Pallas kernels for 6%

profile of v17, /device:TPU:0, one launch (start us, length us, event | category | flops | bytes accessed | tf_op | source)
XLA Modules:
  0.0 95.4 jit_solution(2009583738766916425)
XLA Ops:
  0.6 1.6 %collective-permute-start = (bf16[256,128]{1,0:T(8,128)(2,1)}, bf16[256,128]{1,0:T(8,128)(2,1)S(1)}, u32[]{:S(2)}, u32[]{:S(2)}) collective-permute-start(bf16[256,128]{1,0:T(8,128)(2,1)} %bitcast.59), channel_id=1, source_target_pairs={{0,0},{1,1},{2,2},{3,3},{4,4},{5,5},{6,6},{7,7},{8,10},{9,11},{10,... | collective-permute-start | bytes 196616 | tf_op jit(solution)/shard_map/ppermute | solution.py:253
  2.3 6.0 %collective-permute-start.1 = (bf16[256,128]{1,0:T(8,128)(2,1)}, bf16[256,128]{1,0:T(8,128)(2,1)S(1)}, u32[]{:S(2)}, u32[]{:S(2)}) collective-permute-start(bf16[256,128]{1,0:T(8,128)(2,1)} %bitcast.60), channel_id=1, source_target_pairs={{0,10},{1,11},{2,12},{3,13},{4,14},{5,15},{6,8},{7,9},{8,0},{9,1},... | collective-permute-start | bytes 196616 | tf_op jit(solution)/shard_map/ppermute | solution.py:253
  8.3 1.3 %collective-permute-start.2 = (bf16[256,128]{1,0:T(8,128)(2,1)}, bf16[256,128]{1,0:T(8,128)(2,1)S(1)}, u32[]{:S(2)}, u32[]{:S(2)}) collective-permute-start(bf16[256,128]{1,0:T(8,128)(2,1)} %bitcast.61), channel_id=1, source_target_pairs={{0,20},{1,21},{2,22},{3,23},{4,16},{5,17},{6,18},{7,19},{8,30},{9,... | collective-permute-start | bytes 196616 | tf_op jit(solution)/shard_map/ppermute | solution.py:253
  9.6 3.0 %collective-permute-start.3 = (bf16[256,128]{1,0:T(8,128)(2,1)}, bf16[256,128]{1,0:T(8,128)(2,1)S(1)}, u32[]{:S(2)}, u32[]{:S(2)}) collective-permute-start(bf16[256,128]{1,0:T(8,128)(2,1)} %bitcast.62), channel_id=1, source_target_pairs={{0,30},{1,31},{2,24},{3,25},{4,26},{5,27},{6,28},{7,29},{8,20},{9,... | collective-permute-start | bytes 196616 | tf_op jit(solution)/shard_map/ppermute | solution.py:253
  17.9 2.1 %dense.1 = bf16[1024,2048]{1,0:T(8,128)(2,1)S(1)} custom-call(s32[2,19]{1,0:T(2,128)S(1)} %pad_add_fusion.meta_ref, bf16[2,16,128,128]{3,2,1,0:T(8,128)(2,1)S(1)} %bitcast.50), custom_call_target="tpu_custom_call" | custom-call | bytes 8388608 | tf_op jit(solution)/shard_map/dense/pallas_call | solution.py:183
  20.1 1.4 %collective-permute-done.5 = bf16[512,128]{1,0:T(8,128)(2,1)S(1)} collective-permute-done((bf16[512,128]{1,0:T(8,128)(2,1)S(1)}, bf16[512,128]{1,0:T(8,128)(2,1)S(1)}, u32[]{:S(2)}, u32[]{:S(2)}) %collective-permute-start.5) | collective-permute-done | bytes 131104 | tf_op jit(solution)/shard_map/ppermute | solution.py:240
  22.8 1.3 %collective-permute-start.6 = (f32[256,128]{1,0:T(8,128)S(1)}, f32[256,128]{1,0:T(8,128)S(1)}, u32[]{:S(2)}, u32[]{:S(2)}) collective-permute-start(f32[256,128]{1,0:T(8,128)S(1)} %get-tuple-element.78), channel_id=1, source_target_pairs={{0,24},{8,16},{16,8},{24,0},{1,25},{9,17},{17,9},{25,1},{2,26},{10... | collective-permute-start | bytes 393224 | tf_op jit(solution)/shard_map/ppermute | solution.py:229
  24.1 5.4 %collective-permute-start.7 = (f32[256,128]{1,0:T(8,128)S(1)}, f32[256,128]{1,0:T(8,128)S(1)}, u32[]{:S(2)}, u32[]{:S(2)}) collective-permute-start(f32[256,128]{1,0:T(8,128)S(1)} %get-tuple-element.80), channel_id=1, source_target_pairs={{0,16},{8,24},{16,0},{24,8},{1,17},{9,25},{17,1},{25,9},{2,18},{10... | collective-permute-start | bytes 393224 | tf_op jit(solution)/shard_map/ppermute | solution.py:229
  29.5 4.2 %collective-permute-done.7 = f32[256,128]{1,0:T(8,128)S(1)} collective-permute-done((f32[256,128]{1,0:T(8,128)S(1)}, f32[256,128]{1,0:T(8,128)S(1)}, u32[]{:S(2)}, u32[]{:S(2)}) %collective-permute-start.7) | collective-permute-done | bytes 131104 | tf_op jit(solution)/shard_map/ppermute | solution.py:229
  33.8 1.5 %collective-permute-done.8 = f32[256,128]{1,0:T(8,128)S(1)} collective-permute-done((f32[256,128]{1,0:T(8,128)S(1)}, f32[256,128]{1,0:T(8,128)S(1)}, u32[]{:S(2)}, u32[]{:S(2)}) %collective-permute-start.8) | collective-permute-done | bytes 131104 | tf_op jit(solution)/shard_map/ppermute | solution.py:229
  37.1 4.6 %collective-permute-start.11 = (bf16[272,128]{1,0:T(8,128)(2,1)S(1)}, bf16[272,128]{1,0:T(8,128)(2,1)S(1)}, u32[]{:S(2)}, u32[]{:S(2)}) collective-permute-start(bf16[272,128]{1,0:T(8,128)(2,1)S(1)} %pad_maximum_fusion.5), channel_id=1, source_target_pairs={{0,20},{1,21},{2,22},{3,23},{4,16},{5,17},{6,18},{7,19},{8,30},{9,... | collective-permute-start | bytes 208904 | tf_op jit(solution)/shard_map/ppermute | solution.py:253
  42.3 2.5 %collective-permute-start.15 = (bf16[272,128]{1,0:T(8,128)(2,1)S(1)}, bf16[272,128]{1,0:T(8,128)(2,1)S(1)}, u32[]{:S(2)}, u32[]{:S(2)}) collective-permute-start(bf16[272,128]{1,0:T(8,128)(2,1)S(1)} %collective-permute-done.10), channel_id=1, source_target_pairs={{0,1},{1,24},{2,3},{3,26},{4,5},{5,28},{6,7},{7,30},{8,9},{9,0},{1... | collective-permute-start | bytes 208904 | tf_op jit(solution)/shard_map/ppermute | solution.py:240
  45.4 1.5 %collective-permute-done.12 = bf16[272,128]{1,0:T(8,128)(2,1)S(1)} collective-permute-done((bf16[272,128]{1,0:T(8,128)(2,1)S(1)}, bf16[272,128]{1,0:T(8,128)(2,1)S(1)}, u32[]{:S(2)}, u32[]{:S(2)}) %collective-permute-start.12) | collective-permute-done | bytes 69664 | tf_op jit(solution)/shard_map/ppermute | solution.py:253
  48.3 2.3 %collective-permute-done.14 = bf16[272,128]{1,0:T(8,128)(2,1)S(1)} collective-permute-done((bf16[272,128]{1,0:T(8,128)(2,1)S(1)}, bf16[272,128]{1,0:T(8,128)(2,1)S(1)}, u32[]{:S(2)}, u32[]{:S(2)}) %collective-permute-start.14) | collective-permute-done | bytes 69664 | tf_op jit(solution)/shard_map/ppermute | solution.py:240
  51.8 1.3 %fusion.26.partial_ref.own_ref = f32[1024,256]{1,0:T(8,128)S(1)} fusion(bf16[1024,2048]{1,0:T(8,128)(2,1)S(1)} %dense.1, bf16[2048,256]{1,0:T(8,128)(2,1)S(1)} %fusion.1), kind=kOutput, calls=%fused_computation.85 | convolution fusion | flops 1073741824 | bytes 6291456 | tf_op jit(solution)/shard_map/dot_general | solution.py:32
  53.5 3.3 %collective-permute-start.17 = (s16[272,256]{1,0:T(8,128)(2,1)S(1)}, s16[272,256]{1,0:T(8,128)(2,1)S(1)}, u32[]{:S(2)}, u32[]{:S(2)}) collective-permute-start(s16[272,256]{1,0:T(8,128)(2,1)S(1)} %get-tuple-element.56), channel_id=1, source_target_pairs={{0,24},{8,16},{16,8},{24,0},{1,25},{9,17},{17,9},{25,1},{2,26},{10... | collective-permute-start | bytes 417800 | tf_op jit(solution)/shard_map/ppermute | solution.py:229
  56.8 2.1 %collective-permute-start.18 = (s16[272,256]{1,0:T(8,128)(2,1)S(1)}, s16[272,256]{1,0:T(8,128)(2,1)S(1)}, u32[]{:S(2)}, u32[]{:S(2)}) collective-permute-start(s16[272,256]{1,0:T(8,128)(2,1)S(1)} %get-tuple-element.57), channel_id=1, source_target_pairs={{0,16},{8,24},{16,0},{24,8},{1,17},{9,25},{17,1},{25,9},{2,18},{10... | collective-permute-start | bytes 417800 | tf_op jit(solution)/shard_map/ppermute | solution.py:229
  58.9 1.4 %fusion.3 = bf16[2048,256]{1,0:T(8,128)(2,1)} fusion(bf16[2048,256]{1,0:T(8,128)(2,1)S(1)} %pad_maximum_fusion, bf16[2048,128]{1,0:T(8,128)(2,1)S(1)} %slice_dynamic-update-slice_fusion, bf16[128,256]{1,0:T(8,128)(2,1)S(1)} %copy-done), kind=kOutput, calls=%fused_computation.6 | convolution fusion | flops 135266304 | bytes 2686976 | tf_op jit(solution)/shard_map/dot_general | solution.py:32
  61.3 1.5 %collective-permute-done.18.refs_1_ = s16[272,256]{1,0:T(8,128)(2,1)S(1)} collective-permute-done((s16[272,256]{1,0:T(8,128)(2,1)S(1)}, s16[272,256]{1,0:T(8,128)(2,1)S(1)}, u32[]{:S(2)}, u32[]{:S(2)}) %collective-permute-start.18) | collective-permute-done | bytes 139296 | tf_op jit(solution)/shard_map/ppermute | solution.py:229
  64.0 1.3 %head.1 = (f32[256,172]{1,0:T(8,128)S(1)}, f32[48,256]{1,0:T(8,128)S(1)}, bf16[304,256]{1,0:T(8,128)(2,1)S(1)}, bf16[304,256]{1,0:T(8,128)(2,1)S(1)}, bf16[304,2...) custom-call(s32[2]{0:T(128)S(1)} %pad_add_fusion.1.spot_ref, bf16[172,256]{1,0:T(8,128)(2,1)S(1)} %bitcast.53, ...), custom_call_target="tpu_custom_call" | custom-call | tf_op jit(solution)/shard_map/head/pallas_call | solution.py:144
  65.5 1.8 %collective-permute-start.21 = (bf16[304,256]{1,0:T(8,128)(2,1)S(1)}, bf16[304,256]{1,0:T(8,128)(2,1)S(1)}, u32[]{:S(2)}, u32[]{:S(2)}) collective-permute-start(bf16[304,256]{1,0:T(8,128)(2,1)S(1)} %get-tuple-element.64), channel_id=1, source_target_pairs={{0,16},{8,24},{16,0},{24,8},{1,17},{9,25},{17,1},{25,9},{2,18},{10... | collective-permute-start | bytes 466952 | tf_op jit(solution)/shard_map/ppermute | solution.py:229
  67.2 1.6 %collective-permute-start.22 = (bf16[304,256]{1,0:T(8,128)(2,1)S(1)}, bf16[304,256]{1,0:T(8,128)(2,1)S(1)}, u32[]{:S(2)}, u32[]{:S(2)}) collective-permute-start(bf16[304,256]{1,0:T(8,128)(2,1)S(1)} %get-tuple-element.65), channel_id=1, source_target_pairs={{0,24},{8,16},{16,8},{24,0},{1,25},{9,17},{17,9},{25,1},{2,26},{10... | collective-permute-start | bytes 466952 | tf_op jit(solution)/shard_map/ppermute | solution.py:229
  68.9 3.1 %dense_turned.1 = bf16[2048,1024]{1,0:T(8,128)(2,1)S(1)} custom-call(s32[2,19]{1,0:T(2,128)S(1)} %pad_add_fusion.meta_ref, bf16[2,16,128,128]{3,2,1,0:T(8,128)(2,1)S(1)} %bitcast.51), custom_call_target="tpu_custom_call" | custom-call | bytes 8388608 | tf_op jit(solution)/shard_map/dense_turned/pallas_call | solution.py:183
  72.1 1.3 %collective-permute-done.22 = bf16[304,256]{1,0:T(8,128)(2,1)S(1)} collective-permute-done((bf16[304,256]{1,0:T(8,128)(2,1)S(1)}, bf16[304,256]{1,0:T(8,128)(2,1)S(1)}, u32[]{:S(2)}, u32[]{:S(2)}) %collective-permute-start.22) | collective-permute-done | bytes 155680 | tf_op jit(solution)/shard_map/ppermute | solution.py:229
  73.5 1.3 %fusion.2 = bf16[2048,256]{1,0:T(8,128)(2,1)S(1)} fusion(bf16[2048,1024]{1,0:T(8,128)(2,1)S(1)} %dense_turned.1, bf16[1024,256]{1,0:T(8,128)(2,1)S(1)} %pad_maximum_fusion.1, bf16[2048,256]{1,0:T(8,128)(2,1)S(1)} %copy-done.7), kind=kOutput, calls=%fused_computation.4 | convolution fusion | flops 1075838976 | bytes 6815744 | tf_op jit(solution)/shard_map/dot_general | solution.py:32
  75.3 1.3 %collective-permute-done.23 = f32[88,256]{1,0:T(8,128)S(1)} collective-permute-done((f32[88,256]{1,0:T(8,128)S(1)}, f32[88,256]{1,0:T(8,128)S(1)}, u32[]{:S(2)}, u32[]{:S(2)}) %collective-permute-start.23) | collective-permute-done | bytes 90144 | tf_op jit(solution)/shard_map/ppermute | solution.py:243
  77.6 2.4 %collective-permute-start.25 = (bf16[88,256]{1,0:T(8,128)(2,1)S(1)}, bf16[88,256]{1,0:T(8,128)(2,1)S(1)}, u32[]{:S(2)}, u32[]{:S(2)}) collective-permute-start(bf16[88,256]{1,0:T(8,128)(2,1)S(1)} %fusion.15), channel_id=1, source_target_pairs={{0,4},{1,5},{2,6},{3,7},{4,0},{5,1},{6,2},{7,3},{8,12},{9,13},{10,... | collective-permute-start | bytes 135176 | tf_op jit(solution)/shard_map/ppermute | solution.py:243
  81.1 2.5 %collective-permute-done.25 = bf16[88,256]{1,0:T(8,128)(2,1)S(1)} collective-permute-done((bf16[88,256]{1,0:T(8,128)(2,1)S(1)}, bf16[88,256]{1,0:T(8,128)(2,1)S(1)}, u32[]{:S(2)}, u32[]{:S(2)}) %collective-permute-start.25) | collective-permute-done | bytes 45088 | tf_op jit(solution)/shard_map/ppermute | solution.py:243
  83.6 2.3 %collective-permute-done.26 = bf16[88,256]{1,0:T(8,128)(2,1)S(1)} collective-permute-done((bf16[88,256]{1,0:T(8,128)(2,1)S(1)}, bf16[88,256]{1,0:T(8,128)(2,1)S(1)}, u32[]{:S(2)}, u32[]{:S(2)}) %collective-permute-start.26) | collective-permute-done | bytes 45088 | tf_op jit(solution)/shard_map/ppermute | solution.py:243
  87.7 1.8 %collective-permute-start.29 = (bf16[88,256]{1,0:T(8,128)(2,1)S(1)}, bf16[88,256]{1,0:T(8,128)(2,1)S(1)}, u32[]{:S(2)}, u32[]{:S(2)}) collective-permute-start(bf16[88,256]{1,0:T(8,128)(2,1)S(1)} %add_convert_fusion), channel_id=1, source_target_pairs={{0,24},{8,16},{16,8},{24,0},{1,25},{9,17},{17,9},{25,1},{2,26},{10... | collective-permute-start | bytes 135176 | tf_op jit(solution)/shard_map/ppermute | solution.py:229
  90.9 1.7 %collective-permute-done.29 = bf16[88,256]{1,0:T(8,128)(2,1)S(1)} collective-permute-done((bf16[88,256]{1,0:T(8,128)(2,1)S(1)}, bf16[88,256]{1,0:T(8,128)(2,1)S(1)}, u32[]{:S(2)}, u32[]{:S(2)}) %collective-permute-start.29) | collective-permute-done | bytes 45088 | tf_op jit(solution)/shard_map/ppermute | solution.py:229
  94.1 1.3 %last.1 = (f32[128,256]{1,0:T(8,128)}, f32[172,256]{1,0:T(8,128)}) custom-call(s32[2]{0:T(128)S(1)} %pad_add_fusion.1.spot_ref, f32[160,256]{1,0:T(8,128)S(1)} %constant_dynamic-update-slice_fusion.6.total_ref, f32[160,256]{1,0:T(8,128)S(1)} %collective-permute-done.30.other_ref), custom_call_target="tpu_custom_call" | custom-call | tf_op jit(solution)/shard_map/last/pallas_call | solution.py:144
  (121 shorter events, 22.2 us)
Async XLA Ops:
  0.6 50.7 %copy-start = (bf16[128,256]{1,0:T(8,128)(2,1)S(1)}, bf16[128,256]{1,0:T(8,128)(2,1)}, u32[]{:S(2)}) copy-start(bf16[128,256]{1,0:T(8,128)(2,1)} %param.17) | copy-start | bytes 196612
  0.6 11.9 %collective-permute-start = (bf16[256,128]{1,0:T(8,128)(2,1)}, bf16[256,128]{1,0:T(8,128)(2,1)S(1)}, u32[]{:S(2)}, u32[]{:S(2)}) collective-permute-start(bf16[256,128]{1,0:T(8,128)(2,1)} %bitcast.59), channel_id=1, source_target_pairs={{0,0},{1,1},{2,2},{3,3},{4,4},{5,5},{6,6},{7,7},{8,10},{9,11},{10,... | collective-permute-start | bytes 196616 | tf_op jit(solution)/shard_map/ppermute | solution.py:253
  2.3 11.3 %collective-permute-start.1 = (bf16[256,128]{1,0:T(8,128)(2,1)}, bf16[256,128]{1,0:T(8,128)(2,1)S(1)}, u32[]{:S(2)}, u32[]{:S(2)}) collective-permute-start(bf16[256,128]{1,0:T(8,128)(2,1)} %bitcast.60), channel_id=1, source_target_pairs={{0,10},{1,11},{2,12},{3,13},{4,14},{5,15},{6,8},{7,9},{8,0},{9,1},... | collective-permute-start | bytes 196616 | tf_op jit(solution)/shard_map/ppermute | solution.py:253
  8.3 5.6 %collective-permute-start.2 = (bf16[256,128]{1,0:T(8,128)(2,1)}, bf16[256,128]{1,0:T(8,128)(2,1)S(1)}, u32[]{:S(2)}, u32[]{:S(2)}) collective-permute-start(bf16[256,128]{1,0:T(8,128)(2,1)} %bitcast.61), channel_id=1, source_target_pairs={{0,20},{1,21},{2,22},{3,23},{4,16},{5,17},{6,18},{7,19},{8,30},{9,... | collective-permute-start | bytes 196616 | tf_op jit(solution)/shard_map/ppermute | solution.py:253
  9.6 5.4 %collective-permute-start.3 = (bf16[256,128]{1,0:T(8,128)(2,1)}, bf16[256,128]{1,0:T(8,128)(2,1)S(1)}, u32[]{:S(2)}, u32[]{:S(2)}) collective-permute-start(bf16[256,128]{1,0:T(8,128)(2,1)} %bitcast.62), channel_id=1, source_target_pairs={{0,30},{1,31},{2,24},{3,25},{4,26},{5,27},{6,28},{7,29},{8,20},{9,... | collective-permute-start | bytes 196616 | tf_op jit(solution)/shard_map/ppermute | solution.py:253
  13.6 6.5 %collective-permute-start.4 = (bf16[512,128]{1,0:T(8,128)(2,1)S(1)}, bf16[512,128]{1,0:T(8,128)(2,1)S(1)}, u32[]{:S(2)}, u32[]{:S(2)}) collective-permute-start(bf16[512,128]{1,0:T(8,128)(2,1)S(1)} %pad_maximum_fusion.2), channel_id=1, source_target_pairs={{0,1},{1,24},{2,3},{3,26},{4,5},{5,28},{6,7},{7,30},{8,9},{9,0},{1... | collective-permute-start | bytes 393224 | tf_op jit(solution)/shard_map/ppermute | solution.py:240
  15.0 6.5 %collective-permute-start.5 = (bf16[512,128]{1,0:T(8,128)(2,1)S(1)}, bf16[512,128]{1,0:T(8,128)(2,1)S(1)}, u32[]{:S(2)}, u32[]{:S(2)}) collective-permute-start(bf16[512,128]{1,0:T(8,128)(2,1)S(1)} %pad_maximum_fusion.3), channel_id=1, source_target_pairs={{0,1},{1,24},{2,3},{3,26},{4,5},{5,28},{6,7},{7,30},{8,9},{9,0},{1... | collective-permute-start | bytes 393224 | tf_op jit(solution)/shard_map/ppermute | solution.py:240
  22.8 6.7 %collective-permute-start.6 = (f32[256,128]{1,0:T(8,128)S(1)}, f32[256,128]{1,0:T(8,128)S(1)}, u32[]{:S(2)}, u32[]{:S(2)}) collective-permute-start(f32[256,128]{1,0:T(8,128)S(1)} %get-tuple-element.78), channel_id=1, source_target_pairs={{0,24},{8,16},{16,8},{24,0},{1,25},{9,17},{17,9},{25,1},{2,26},{10... | collective-permute-start | bytes 393224 | tf_op jit(solution)/shard_map/ppermute | solution.py:229
  24.1 9.7 %collective-permute-start.7 = (f32[256,128]{1,0:T(8,128)S(1)}, f32[256,128]{1,0:T(8,128)S(1)}, u32[]{:S(2)}, u32[]{:S(2)}) collective-permute-start(f32[256,128]{1,0:T(8,128)S(1)} %get-tuple-element.80), channel_id=1, source_target_pairs={{0,16},{8,24},{16,0},{24,8},{1,17},{9,25},{17,1},{25,9},{2,18},{10... | collective-permute-start | bytes 393224 | tf_op jit(solution)/shard_map/ppermute | solution.py:229
  29.5 5.7 %collective-permute-start.8 = (f32[256,128]{1,0:T(8,128)S(1)}, f32[256,128]{1,0:T(8,128)S(1)}, u32[]{:S(2)}, u32[]{:S(2)}) collective-permute-start(f32[256,128]{1,0:T(8,128)S(1)} %get-tuple-element.79), channel_id=1, source_target_pairs={{0,8},{8,0},{16,24},{24,16},{1,9},{9,1},{17,25},{25,17},{2,10},{10... | collective-permute-start | bytes 393224 | tf_op jit(solution)/shard_map/ppermute | solution.py:229
  35.3 6.9 %collective-permute-start.9 = (bf16[272,128]{1,0:T(8,128)(2,1)S(1)}, bf16[272,128]{1,0:T(8,128)(2,1)S(1)}, u32[]{:S(2)}, u32[]{:S(2)}) collective-permute-start(bf16[272,128]{1,0:T(8,128)(2,1)S(1)} %pad_maximum_fusion.5), channel_id=1, source_target_pairs={{0,0},{1,1},{2,2},{3,3},{4,4},{5,5},{6,6},{7,7},{8,10},{9,11},{10,... | collective-permute-start | bytes 208904 | tf_op jit(solution)/shard_map/ppermute | solution.py:253
  36.1 6.3 %collective-permute-start.10 = (bf16[272,128]{1,0:T(8,128)(2,1)S(1)}, bf16[272,128]{1,0:T(8,128)(2,1)S(1)}, u32[]{:S(2)}, u32[]{:S(2)}) collective-permute-start(bf16[272,128]{1,0:T(8,128)(2,1)S(1)} %pad_maximum_fusion.5), channel_id=1, source_target_pairs={{0,10},{1,11},{2,12},{3,13},{4,14},{5,15},{6,8},{7,9},{8,0},{9,1},... | collective-permute-start | bytes 208904 | tf_op jit(solution)/shard_map/ppermute | solution.py:253
  37.1 7.7 %collective-permute-start.11 = (bf16[272,128]{1,0:T(8,128)(2,1)S(1)}, bf16[272,128]{1,0:T(8,128)(2,1)S(1)}, u32[]{:S(2)}, u32[]{:S(2)}) collective-permute-start(bf16[272,128]{1,0:T(8,128)(2,1)S(1)} %pad_maximum_fusion.5), channel_id=1, source_target_pairs={{0,20},{1,21},{2,22},{3,23},{4,16},{5,17},{6,18},{7,19},{8,30},{9,... | collective-permute-start | bytes 208904 | tf_op jit(solution)/shard_map/ppermute | solution.py:253
  41.7 5.2 %collective-permute-start.12 = (bf16[272,128]{1,0:T(8,128)(2,1)S(1)}, bf16[272,128]{1,0:T(8,128)(2,1)S(1)}, u32[]{:S(2)}, u32[]{:S(2)}) collective-permute-start(bf16[272,128]{1,0:T(8,128)(2,1)S(1)} %pad_maximum_fusion.5), channel_id=1, source_target_pairs={{0,30},{1,31},{2,24},{3,25},{4,26},{5,27},{6,28},{7,29},{8,20},{9,... | collective-permute-start | bytes 208904 | tf_op jit(solution)/shard_map/ppermute | solution.py:253
  42.2 5.6 %collective-permute-start.13 = (bf16[272,128]{1,0:T(8,128)(2,1)S(1)}, bf16[272,128]{1,0:T(8,128)(2,1)S(1)}, u32[]{:S(2)}, u32[]{:S(2)}) collective-permute-start(bf16[272,128]{1,0:T(8,128)(2,1)S(1)} %collective-permute-done.9), channel_id=1, source_target_pairs={{0,1},{1,24},{2,3},{3,26},{4,5},{5,28},{6,7},{7,30},{8,9},{9,0},{1... | collective-permute-start | bytes 208904 | tf_op jit(solution)/shard_map/ppermute | solution.py:240
  42.3 8.4 %collective-permute-start.15 = (bf16[272,128]{1,0:T(8,128)(2,1)S(1)}, bf16[272,128]{1,0:T(8,128)(2,1)S(1)}, u32[]{:S(2)}, u32[]{:S(2)}) collective-permute-start(bf16[272,128]{1,0:T(8,128)(2,1)S(1)} %collective-permute-done.10), channel_id=1, source_target_pairs={{0,1},{1,24},{2,3},{3,26},{4,5},{5,28},{6,7},{7,30},{8,9},{9,0},{1... | collective-permute-start | bytes 208904 | tf_op jit(solution)/shard_map/ppermute | solution.py:240
  44.8 5.8 %collective-permute-start.16 = (bf16[272,128]{1,0:T(8,128)(2,1)S(1)}, bf16[272,128]{1,0:T(8,128)(2,1)S(1)}, u32[]{:S(2)}, u32[]{:S(2)}) collective-permute-start(bf16[272,128]{1,0:T(8,128)(2,1)S(1)} %collective-permute-done.11), channel_id=1, source_target_pairs={{0,1},{1,24},{2,3},{3,26},{4,5},{5,28},{6,7},{7,30},{8,9},{9,0},{1... | collective-permute-start | bytes 208904 | tf_op jit(solution)/shard_map/ppermute | solution.py:240
  46.9 3.7 %collective-permute-start.14 = (bf16[272,128]{1,0:T(8,128)(2,1)S(1)}, bf16[272,128]{1,0:T(8,128)(2,1)S(1)}, u32[]{:S(2)}, u32[]{:S(2)}) collective-permute-start(bf16[272,128]{1,0:T(8,128)(2,1)S(1)} %collective-permute-done.12), channel_id=1, source_target_pairs={{0,1},{1,24},{2,3},{3,26},{4,5},{5,28},{6,7},{7,30},{8,9},{9,0},{1... | collective-permute-start | bytes 208904 | tf_op jit(solution)/shard_map/ppermute | solution.py:240
  53.5 7.8 %collective-permute-start.17 = (s16[272,256]{1,0:T(8,128)(2,1)S(1)}, s16[272,256]{1,0:T(8,128)(2,1)S(1)}, u32[]{:S(2)}, u32[]{:S(2)}) collective-permute-start(s16[272,256]{1,0:T(8,128)(2,1)S(1)} %get-tuple-element.56), channel_id=1, source_target_pairs={{0,24},{8,16},{16,8},{24,0},{1,25},{9,17},{17,9},{25,1},{2,26},{10... | collective-permute-start | bytes 417800 | tf_op jit(solution)/shard_map/ppermute | solution.py:229
  56.8 6.1 %collective-permute-start.18 = (s16[272,256]{1,0:T(8,128)(2,1)S(1)}, s16[272,256]{1,0:T(8,128)(2,1)S(1)}, u32[]{:S(2)}, u32[]{:S(2)}) collective-permute-start(s16[272,256]{1,0:T(8,128)(2,1)S(1)} %get-tuple-element.57), channel_id=1, source_target_pairs={{0,16},{8,24},{16,0},{24,8},{1,17},{9,25},{17,1},{25,9},{2,18},{10... | collective-permute-start | bytes 417800 | tf_op jit(solution)/shard_map/ppermute | solution.py:229
  58.9 5.1 %collective-permute-start.19 = (s16[272,256]{1,0:T(8,128)(2,1)S(1)}, s16[272,256]{1,0:T(8,128)(2,1)S(1)}, u32[]{:S(2)}, u32[]{:S(2)}) collective-permute-start(s16[272,256]{1,0:T(8,128)(2,1)S(1)} %get-tuple-element.58), channel_id=1, source_target_pairs={{0,8},{8,0},{16,24},{24,16},{1,9},{9,1},{17,25},{25,17},{2,10},{10... | collective-permute-start | bytes 417800 | tf_op jit(solution)/shard_map/ppermute | solution.py:229
  65.3 6.7 %collective-permute-start.20 = (bf16[304,256]{1,0:T(8,128)(2,1)S(1)}, bf16[304,256]{1,0:T(8,128)(2,1)S(1)}, u32[]{:S(2)}, u32[]{:S(2)}) collective-permute-start(bf16[304,256]{1,0:T(8,128)(2,1)S(1)} %get-tuple-element.63), channel_id=1, source_target_pairs={{0,8},{8,0},{16,24},{24,16},{1,9},{9,1},{17,25},{25,17},{2,10},{10... | collective-permute-start | bytes 466952 | tf_op jit(solution)/shard_map/ppermute | solution.py:229
  65.5 6.6 %collective-permute-start.21 = (bf16[304,256]{1,0:T(8,128)(2,1)S(1)}, bf16[304,256]{1,0:T(8,128)(2,1)S(1)}, u32[]{:S(2)}, u32[]{:S(2)}) collective-permute-start(bf16[304,256]{1,0:T(8,128)(2,1)S(1)} %get-tuple-element.64), channel_id=1, source_target_pairs={{0,16},{8,24},{16,0},{24,8},{1,17},{9,25},{17,1},{25,9},{2,18},{10... | collective-permute-start | bytes 466952 | tf_op jit(solution)/shard_map/ppermute | solution.py:229
  67.2 6.1 %collective-permute-start.22 = (bf16[304,256]{1,0:T(8,128)(2,1)S(1)}, bf16[304,256]{1,0:T(8,128)(2,1)S(1)}, u32[]{:S(2)}, u32[]{:S(2)}) collective-permute-start(bf16[304,256]{1,0:T(8,128)(2,1)S(1)} %get-tuple-element.65), channel_id=1, source_target_pairs={{0,24},{8,16},{16,8},{24,0},{1,25},{9,17},{17,9},{25,1},{2,26},{10... | collective-permute-start | bytes 466952 | tf_op jit(solution)/shard_map/ppermute | solution.py:229
  75.2 1.4 %collective-permute-start.23 = (f32[88,256]{1,0:T(8,128)S(1)}, f32[88,256]{1,0:T(8,128)S(1)}, u32[]{:S(2)}, u32[]{:S(2)}) collective-permute-start(f32[88,256]{1,0:T(8,128)S(1)} %pad_maximum_fusion.4), channel_id=1, source_target_pairs={{0,1},{1,0},{2,3},{3,2},{4,5},{5,4},{6,7},{7,6},{8,9},{9,8},{10,11... | collective-permute-start | bytes 270344 | tf_op jit(solution)/shard_map/ppermute | solution.py:243
  76.6 4.5 %collective-permute-start.24 = (bf16[88,256]{1,0:T(8,128)(2,1)S(1)}, bf16[88,256]{1,0:T(8,128)(2,1)S(1)}, u32[]{:S(2)}, u32[]{:S(2)}) collective-permute-start(bf16[88,256]{1,0:T(8,128)(2,1)S(1)} %fusion.15), channel_id=1, source_target_pairs={{0,2},{1,3},{2,0},{3,1},{4,6},{5,7},{6,4},{7,5},{8,10},{9,11},{10,... | collective-permute-start | bytes 135176 | tf_op jit(solution)/shard_map/ppermute | solution.py:243
  77.6 5.9 %collective-permute-start.25 = (bf16[88,256]{1,0:T(8,128)(2,1)S(1)}, bf16[88,256]{1,0:T(8,128)(2,1)S(1)}, u32[]{:S(2)}, u32[]{:S(2)}) collective-permute-start(bf16[88,256]{1,0:T(8,128)(2,1)S(1)} %fusion.15), channel_id=1, source_target_pairs={{0,4},{1,5},{2,6},{3,7},{4,0},{5,1},{6,2},{7,3},{8,12},{9,13},{10,... | collective-permute-start | bytes 135176 | tf_op jit(solution)/shard_map/ppermute | solution.py:243
  80.0 5.8 %collective-permute-start.26 = (bf16[88,256]{1,0:T(8,128)(2,1)S(1)}, bf16[88,256]{1,0:T(8,128)(2,1)S(1)}, u32[]{:S(2)}, u32[]{:S(2)}) collective-permute-start(bf16[88,256]{1,0:T(8,128)(2,1)S(1)} %fusion.15), channel_id=1, source_target_pairs={{0,6},{1,7},{2,4},{3,5},{4,2},{5,3},{6,0},{7,1},{8,14},{9,15},{10,... | collective-permute-start | bytes 135176 | tf_op jit(solution)/shard_map/ppermute | solution.py:243
  85.9 4.1 %collective-permute-start.27 = (bf16[88,256]{1,0:T(8,128)(2,1)S(1)}, bf16[88,256]{1,0:T(8,128)(2,1)S(1)}, u32[]{:S(2)}, u32[]{:S(2)}) collective-permute-start(bf16[88,256]{1,0:T(8,128)(2,1)S(1)} %add_convert_fusion), channel_id=1, source_target_pairs={{0,8},{8,0},{16,24},{24,16},{1,9},{9,1},{17,25},{25,17},{2,10},{10... | collective-permute-start | bytes 135176 | tf_op jit(solution)/shard_map/ppermute | solution.py:229
  86.8 4.0 %collective-permute-start.28 = (bf16[88,256]{1,0:T(8,128)(2,1)S(1)}, bf16[88,256]{1,0:T(8,128)(2,1)S(1)}, u32[]{:S(2)}, u32[]{:S(2)}) collective-permute-start(bf16[88,256]{1,0:T(8,128)(2,1)S(1)} %add_convert_fusion), channel_id=1, source_target_pairs={{0,16},{8,24},{16,0},{24,8},{1,17},{9,25},{17,1},{25,9},{2,18},{10... | collective-permute-start | bytes 135176 | tf_op jit(solution)/shard_map/ppermute | solution.py:229
  87.7 4.9 %collective-permute-start.29 = (bf16[88,256]{1,0:T(8,128)(2,1)S(1)}, bf16[88,256]{1,0:T(8,128)(2,1)S(1)}, u32[]{:S(2)}, u32[]{:S(2)}) collective-permute-start(bf16[88,256]{1,0:T(8,128)(2,1)S(1)} %add_convert_fusion), channel_id=1, source_target_pairs={{0,24},{8,16},{16,8},{24,0},{1,25},{9,17},{17,9},{25,1},{2,26},{10... | collective-permute-start | bytes 135176 | tf_op jit(solution)/shard_map/ppermute | solution.py:229
  92.7 1.5 %collective-permute-start.30 = (f32[160,256]{1,0:T(8,128)S(1)}, f32[160,256]{1,0:T(8,128)S(1)}, u32[]{:S(2)}, u32[]{:S(2)}) collective-permute-start(f32[160,256]{1,0:T(8,128)S(1)} %constant_dynamic-update-slice_fusion.6.total_ref), channel_id=1, source_target_pairs={{0,1},{1,0},{2,3},{3,2},{4,5},{5,4},{6,7},{7,6},{8,9},{9,8},{10,11... | collective-permute-start | bytes 491528 | tf_op jit(solution)/shard_map/ppermute | solution.py:243
  (8 other events, 67.4 us)

commit v18 on v17

--- a/solution.py
+++ b/solution.py
@@ -351,7 +351,8 @@
         spot=(spot,),
         scratch=[pltpu.VMEM((chunk * reps, hidden_width), f32)],
     )
-    arrived = [swap(sent[d], d) for d in range(reps - 1, -1, -1)][::-1]
+    arrived = lax.optimization_barrier([swap(sent[d], d) for d in far_first]) + [sent[0]]
+    arrived = arrived[::-1]
     meta, out_total = lax.optimization_barrier((meta, out_total))
     turned = build_dense(tiles, meta, own_rows, group_rows, True)
     grad_block = jnp.concatenate([part[:own_rows] for part in arrived], axis=0)
@@ -375,7 +376,8 @@
 
     total = halves(side) + exchange(halves(1 - side), 1)
     total = sum_over(total, exchange, 2, blks).astype(bf16)
-    arrived = [swap(total, d) for d in range(reps - 1, -1, -1)][::-1]
+    arrived = lax.optimization_barrier([swap(total, d) for d in far_first]) + [total]
+    arrived = arrived[::-1]
     parts = [part[:half].astype(f32) for part in arrived]
     while len(parts) > 1:
         parts = [parts[i] + parts[i + 1] for i in range(0, len(parts), 2)]

time: 95.6 us -> 95.2 us (level)
  transfers between devices with their start and end apart: 31 -> 31, of which waited for: 18 -> 20; matrix products, arithmetic and copies ran while one was open for 5% -> 5% of each run, Pallas kernels for 6% -> 6%
where the time goes in v18:
time: 95.2 us; the launch traced here: 95.1 us
  starting transfers between devices  48 us (50%)
  waiting for transfers between devices  26.2 us (28%)
  Pallas kernels  8.3 us (9%)
  matrix products  6.06 us (6%)
  local copies, waits for them, and re-layouts  3.31 us (3%)
  other arithmetic  2.06 us (2%)
  between operations  1.2 us (1%)
    ppermute x8, starting transfers between devices, to_pieces(): pieces.append(lax.ppermute(value, ('rep', 'blk'), pairs))  19.3 us
    ppermute x12, starting transfers between devices, swap(): return lax.ppermute(value, 'rep', [(r, r ^ delta) for r in range(reps)])  19 us
    ppermute x12, waiting for transfers between devices, swap(): return lax.ppermute(value, 'rep', [(r, r ^ delta) for r in range(reps)])  13.2 us
    ppermute x5, waiting for transfers between devices, exchange(): return lax.ppermute(value, 'blk', [(c, c ^ delta) for c in range(blks)])  6.96 us
    dot_general x5, matrix products, dot(): return jnp.dot(left, right, preferred_element_type=jnp.float32)  5.7 us
    pallas_call x2, Pallas kernels, build_dense(): pl.pallas_call(body, grid_spec=pltpu.PrefetchScalarGridSpec(num_scalar_pr...  5.26 us
    ppermute x6, starting transfers between devices, to_section(): return lax.ppermute(block, ('rep', 'blk'), pairs)  5.13 us
    ppermute x5, starting transfers between devices, exchange(): return lax.ppermute(value, 'blk', [(c, c ^ delta) for c in range(blks)])  4.59 us
  transfers between devices with their start and end apart: 31, of which 20 were waited for; matrix products, arithmetic and copies ran while one was open for 5% of the time, Pallas kernels for 6%

profile of v18, /device:TPU:0, one launch (start us, length us, event | category | flops | bytes accessed | tf_op | source)
XLA Modules:
  0.0 95.1 jit_solution(13911069091881896790)
XLA Ops:
  0.6 1.6 %collective-permute-start = (bf16[256,128]{1,0:T(8,128)(2,1)}, bf16[256,128]{1,0:T(8,128)(2,1)S(1)}, u32[]{:S(2)}, u32[]{:S(2)}) collective-permute-start(bf16[256,128]{1,0:T(8,128)(2,1)} %bitcast.59), channel_id=1, source_target_pairs={{0,0},{1,1},{2,2},{3,3},{4,4},{5,5},{6,6},{7,7},{8,10},{9,11},{10,... | collective-permute-start | bytes 196616 | tf_op jit(solution)/shard_map/ppermute | solution.py:253
  2.3 6.0 %collective-permute-start.1 = (bf16[256,128]{1,0:T(8,128)(2,1)}, bf16[256,128]{1,0:T(8,128)(2,1)S(1)}, u32[]{:S(2)}, u32[]{:S(2)}) collective-permute-start(bf16[256,128]{1,0:T(8,128)(2,1)} %bitcast.60), channel_id=1, source_target_pairs={{0,10},{1,11},{2,12},{3,13},{4,14},{5,15},{6,8},{7,9},{8,0},{9,1},... | collective-permute-start | bytes 196616 | tf_op jit(solution)/shard_map/ppermute | solution.py:253
  8.3 1.3 %collective-permute-start.2 = (bf16[256,128]{1,0:T(8,128)(2,1)}, bf16[256,128]{1,0:T(8,128)(2,1)S(1)}, u32[]{:S(2)}, u32[]{:S(2)}) collective-permute-start(bf16[256,128]{1,0:T(8,128)(2,1)} %bitcast.61), channel_id=1, source_target_pairs={{0,20},{1,21},{2,22},{3,23},{4,16},{5,17},{6,18},{7,19},{8,30},{9,... | collective-permute-start | bytes 196616 | tf_op jit(solution)/shard_map/ppermute | solution.py:253
  9.6 3.0 %collective-permute-start.3 = (bf16[256,128]{1,0:T(8,128)(2,1)}, bf16[256,128]{1,0:T(8,128)(2,1)S(1)}, u32[]{:S(2)}, u32[]{:S(2)}) collective-permute-start(bf16[256,128]{1,0:T(8,128)(2,1)} %bitcast.62), channel_id=1, source_target_pairs={{0,30},{1,31},{2,24},{3,25},{4,26},{5,27},{6,28},{7,29},{8,20},{9,... | collective-permute-start | bytes 196616 | tf_op jit(solution)/shard_map/ppermute | solution.py:253
  17.9 2.1 %dense.1 = bf16[1024,2048]{1,0:T(8,128)(2,1)S(1)} custom-call(s32[2,19]{1,0:T(2,128)S(1)} %pad_add_fusion.meta_ref, bf16[2,16,128,128]{3,2,1,0:T(8,128)(2,1)S(1)} %bitcast.50), custom_call_target="tpu_custom_call" | custom-call | bytes 8388608 | tf_op jit(solution)/shard_map/dense/pallas_call | solution.py:183
  20.1 1.4 %collective-permute-done.5 = bf16[512,128]{1,0:T(8,128)(2,1)S(1)} collective-permute-done((bf16[512,128]{1,0:T(8,128)(2,1)S(1)}, bf16[512,128]{1,0:T(8,128)(2,1)S(1)}, u32[]{:S(2)}, u32[]{:S(2)}) %collective-permute-start.5) | collective-permute-done | bytes 131104 | tf_op jit(solution)/shard_map/ppermute | solution.py:240
  22.8 1.5 %collective-permute-start.6 = (f32[256,128]{1,0:T(8,128)S(1)}, f32[256,128]{1,0:T(8,128)S(1)}, u32[]{:S(2)}, u32[]{:S(2)}) collective-permute-start(f32[256,128]{1,0:T(8,128)S(1)} %get-tuple-element.90), channel_id=1, source_target_pairs={{0,24},{8,16},{16,8},{24,0},{1,25},{9,17},{17,9},{25,1},{2,26},{10... | collective-permute-start | bytes 393224 | tf_op jit(solution)/shard_map/ppermute | solution.py:229
  24.3 5.2 %collective-permute-start.7 = (f32[256,128]{1,0:T(8,128)S(1)}, f32[256,128]{1,0:T(8,128)S(1)}, u32[]{:S(2)}, u32[]{:S(2)}) collective-permute-start(f32[256,128]{1,0:T(8,128)S(1)} %get-tuple-element.92), channel_id=1, source_target_pairs={{0,16},{8,24},{16,0},{24,8},{1,17},{9,25},{17,1},{25,9},{2,18},{10... | collective-permute-start | bytes 393224 | tf_op jit(solution)/shard_map/ppermute | solution.py:229
  30.0 4.2 %collective-permute-done.7 = f32[256,128]{1,0:T(8,128)S(1)} collective-permute-done((f32[256,128]{1,0:T(8,128)S(1)}, f32[256,128]{1,0:T(8,128)S(1)}, u32[]{:S(2)}, u32[]{:S(2)}) %collective-permute-start.7) | collective-permute-done | bytes 131104 | tf_op jit(solution)/shard_map/ppermute | solution.py:229
  37.0 4.7 %collective-permute-start.11 = (bf16[272,128]{1,0:T(8,128)(2,1)S(1)}, bf16[272,128]{1,0:T(8,128)(2,1)S(1)}, u32[]{:S(2)}, u32[]{:S(2)}) collective-permute-start(bf16[272,128]{1,0:T(8,128)(2,1)S(1)} %pad_maximum_fusion.5), channel_id=1, source_target_pairs={{0,20},{1,21},{2,22},{3,23},{4,16},{5,17},{6,18},{7,19},{8,30},{9,... | collective-permute-start | bytes 208904 | tf_op jit(solution)/shard_map/ppermute | solution.py:253
  42.8 2.0 %collective-permute-start.15 = (bf16[272,128]{1,0:T(8,128)(2,1)S(1)}, bf16[272,128]{1,0:T(8,128)(2,1)S(1)}, u32[]{:S(2)}, u32[]{:S(2)}) collective-permute-start(bf16[272,128]{1,0:T(8,128)(2,1)S(1)} %collective-permute-done.10), channel_id=1, source_target_pairs={{0,1},{1,24},{2,3},{3,26},{4,5},{5,28},{6,7},{7,30},{8,9},{9,0},{1... | collective-permute-start | bytes 208904 | tf_op jit(solution)/shard_map/ppermute | solution.py:240
  45.5 1.5 %collective-permute-done.12 = bf16[272,128]{1,0:T(8,128)(2,1)S(1)} collective-permute-done((bf16[272,128]{1,0:T(8,128)(2,1)S(1)}, bf16[272,128]{1,0:T(8,128)(2,1)S(1)}, u32[]{:S(2)}, u32[]{:S(2)}) %collective-permute-start.12) | collective-permute-done | bytes 69664 | tf_op jit(solution)/shard_map/ppermute | solution.py:253
  47.0 1.4 %collective-permute-start.14 = (bf16[272,128]{1,0:T(8,128)(2,1)S(1)}, bf16[272,128]{1,0:T(8,128)(2,1)S(1)}, u32[]{:S(2)}, u32[]{:S(2)}) collective-permute-start(bf16[272,128]{1,0:T(8,128)(2,1)S(1)} %collective-permute-done.12), channel_id=1, source_target_pairs={{0,1},{1,24},{2,3},{3,26},{4,5},{5,28},{6,7},{7,30},{8,9},{9,0},{1... | collective-permute-start | bytes 208904 | tf_op jit(solution)/shard_map/ppermute | solution.py:240
  49.0 1.8 %collective-permute-done.14 = bf16[272,128]{1,0:T(8,128)(2,1)S(1)} collective-permute-done((bf16[272,128]{1,0:T(8,128)(2,1)S(1)}, bf16[272,128]{1,0:T(8,128)(2,1)S(1)}, u32[]{:S(2)}, u32[]{:S(2)}) %collective-permute-start.14) | collective-permute-done | bytes 69664 | tf_op jit(solution)/shard_map/ppermute | solution.py:240
  53.7 3.8 %collective-permute-start.17 = (s16[272,256]{1,0:T(8,128)(2,1)S(1)}, s16[272,256]{1,0:T(8,128)(2,1)S(1)}, u32[]{:S(2)}, u32[]{:S(2)}) collective-permute-start(s16[272,256]{1,0:T(8,128)(2,1)S(1)} %get-tuple-element.62), channel_id=1, source_target_pairs={{0,24},{8,16},{16,8},{24,0},{1,25},{9,17},{17,9},{25,1},{2,26},{10... | collective-permute-start | bytes 417800 | tf_op jit(solution)/shard_map/ppermute | solution.py:229
  57.5 1.4 %collective-permute-start.18 = (s16[272,256]{1,0:T(8,128)(2,1)S(1)}, s16[272,256]{1,0:T(8,128)(2,1)S(1)}, u32[]{:S(2)}, u32[]{:S(2)}) collective-permute-start(s16[272,256]{1,0:T(8,128)(2,1)S(1)} %get-tuple-element.63), channel_id=1, source_target_pairs={{0,16},{8,24},{16,0},{24,8},{1,17},{9,25},{17,1},{25,9},{2,18},{10... | collective-permute-start | bytes 417800 | tf_op jit(solution)/shard_map/ppermute | solution.py:229
  58.9 1.4 %fusion.3 = bf16[2048,256]{1,0:T(8,128)(2,1)} fusion(bf16[2048,256]{1,0:T(8,128)(2,1)S(1)} %pad_maximum_fusion, bf16[2048,128]{1,0:T(8,128)(2,1)S(1)} %slice_dynamic-update-slice_fusion, bf16[128,256]{1,0:T(8,128)(2,1)S(1)} %copy-done), kind=kOutput, calls=%fused_computation.6 | convolution fusion | flops 135266304 | bytes 2686976 | tf_op jit(solution)/shard_map/dot_general | solution.py:32
  60.3 1.7 %collective-permute-done.17.refs_0_ = s16[272,256]{1,0:T(8,128)(2,1)S(1)} collective-permute-done((s16[272,256]{1,0:T(8,128)(2,1)S(1)}, s16[272,256]{1,0:T(8,128)(2,1)S(1)}, u32[]{:S(2)}, u32[]{:S(2)}) %collective-permute-start.17) | collective-permute-done | bytes 139296 | tf_op jit(solution)/shard_map/ppermute | solution.py:229
  62.0 1.4 %collective-permute-done.18.refs_1_ = s16[272,256]{1,0:T(8,128)(2,1)S(1)} collective-permute-done((s16[272,256]{1,0:T(8,128)(2,1)S(1)}, s16[272,256]{1,0:T(8,128)(2,1)S(1)}, u32[]{:S(2)}, u32[]{:S(2)}) %collective-permute-start.18) | collective-permute-done | bytes 139296 | tf_op jit(solution)/shard_map/ppermute | solution.py:229
  63.9 1.3 %head.1 = (f32[256,172]{1,0:T(8,128)S(1)}, f32[48,256]{1,0:T(8,128)S(1)}, bf16[304,256]{1,0:T(8,128)(2,1)S(1)}, bf16[304,256]{1,0:T(8,128)(2,1)S(1)}, bf16[304,2...) custom-call(s32[2]{0:T(128)S(1)} %pad_add_fusion.1.spot_ref, bf16[172,256]{1,0:T(8,128)(2,1)S(1)} %bitcast.53, ...), custom_call_target="tpu_custom_call" | custom-call | tf_op jit(solution)/shard_map/head/pallas_call | solution.py:144
  65.3 1.3 %collective-permute-start.20 = (bf16[304,256]{1,0:T(8,128)(2,1)S(1)}, bf16[304,256]{1,0:T(8,128)(2,1)S(1)}, u32[]{:S(2)}, u32[]{:S(2)}) collective-permute-start(bf16[304,256]{1,0:T(8,128)(2,1)S(1)} %get-tuple-element.69), channel_id=1, source_target_pairs={{0,24},{8,16},{16,8},{24,0},{1,25},{9,17},{17,9},{25,1},{2,26},{10... | collective-permute-start | bytes 466952 | tf_op jit(solution)/shard_map/ppermute | solution.py:229
  67.3 1.6 %collective-permute-start.22 = (bf16[304,256]{1,0:T(8,128)(2,1)S(1)}, bf16[304,256]{1,0:T(8,128)(2,1)S(1)}, u32[]{:S(2)}, u32[]{:S(2)}) collective-permute-start(bf16[304,256]{1,0:T(8,128)(2,1)S(1)} %get-tuple-element.71), channel_id=1, source_target_pairs={{0,8},{8,0},{16,24},{24,16},{1,9},{9,1},{17,25},{25,17},{2,10},{10... | collective-permute-start | bytes 466952 | tf_op jit(solution)/shard_map/ppermute | solution.py:229
  68.9 3.1 %dense_turned.1 = bf16[2048,1024]{1,0:T(8,128)(2,1)S(1)} custom-call(s32[2,19]{1,0:T(2,128)S(1)} %pad_add_fusion.meta_ref, bf16[2,16,128,128]{3,2,1,0:T(8,128)(2,1)S(1)} %bitcast.51), custom_call_target="tpu_custom_call" | custom-call | bytes 8388608 | tf_op jit(solution)/shard_map/dense_turned/pallas_call | solution.py:183
  73.5 1.3 %fusion.2 = bf16[2048,256]{1,0:T(8,128)(2,1)S(1)} fusion(bf16[2048,1024]{1,0:T(8,128)(2,1)S(1)} %dense_turned.1, bf16[1024,256]{1,0:T(8,128)(2,1)S(1)} %pad_maximum_fusion.1, bf16[2048,256]{1,0:T(8,128)(2,1)S(1)} %copy-done.7), kind=kOutput, calls=%fused_computation.4 | convolution fusion | flops 1075838976 | bytes 6815744 | tf_op jit(solution)/shard_map/dot_general | solution.py:32
  76.6 1.4 %collective-permute-start.24 = (bf16[88,256]{1,0:T(8,128)(2,1)S(1)}, bf16[88,256]{1,0:T(8,128)(2,1)S(1)}, u32[]{:S(2)}, u32[]{:S(2)}) collective-permute-start(bf16[88,256]{1,0:T(8,128)(2,1)S(1)} %fusion.15), channel_id=1, source_target_pairs={{0,2},{1,3},{2,0},{3,1},{4,6},{5,7},{6,4},{7,5},{8,10},{9,11},{10,... | collective-permute-start | bytes 135176 | tf_op jit(solution)/shard_map/ppermute | solution.py:243
  78.1 2.3 %collective-permute-start.25 = (bf16[88,256]{1,0:T(8,128)(2,1)S(1)}, bf16[88,256]{1,0:T(8,128)(2,1)S(1)}, u32[]{:S(2)}, u32[]{:S(2)}) collective-permute-start(bf16[88,256]{1,0:T(8,128)(2,1)S(1)} %fusion.15), channel_id=1, source_target_pairs={{0,4},{1,5},{2,6},{3,7},{4,0},{5,1},{6,2},{7,3},{8,12},{9,13},{10,... | collective-permute-start | bytes 135176 | tf_op jit(solution)/shard_map/ppermute | solution.py:243
  81.1 2.8 %collective-permute-done.25 = bf16[88,256]{1,0:T(8,128)(2,1)S(1)} collective-permute-done((bf16[88,256]{1,0:T(8,128)(2,1)S(1)}, bf16[88,256]{1,0:T(8,128)(2,1)S(1)}, u32[]{:S(2)}, u32[]{:S(2)}) %collective-permute-start.25) | collective-permute-done | bytes 45088 | tf_op jit(solution)/shard_map/ppermute | solution.py:243
  83.9 2.3 %collective-permute-done.26 = bf16[88,256]{1,0:T(8,128)(2,1)S(1)} collective-permute-done((bf16[88,256]{1,0:T(8,128)(2,1)S(1)}, bf16[88,256]{1,0:T(8,128)(2,1)S(1)}, u32[]{:S(2)}, u32[]{:S(2)}) %collective-permute-start.26) | collective-permute-done | bytes 45088 | tf_op jit(solution)/shard_map/ppermute | solution.py:243
  86.2 1.5 %collective-permute-start.27 = (bf16[88,256]{1,0:T(8,128)(2,1)S(1)}, bf16[88,256]{1,0:T(8,128)(2,1)S(1)}, u32[]{:S(2)}, u32[]{:S(2)}) collective-permute-start(bf16[88,256]{1,0:T(8,128)(2,1)S(1)} %add_convert_fusion), channel_id=1, source_target_pairs={{0,24},{8,16},{16,8},{24,0},{1,25},{9,17},{17,9},{25,1},{2,26},{10... | collective-permute-start | bytes 135176 | tf_op jit(solution)/shard_map/ppermute | solution.py:229
  88.2 1.5 %collective-permute-start.29 = (bf16[88,256]{1,0:T(8,128)(2,1)S(1)}, bf16[88,256]{1,0:T(8,128)(2,1)S(1)}, u32[]{:S(2)}, u32[]{:S(2)}) collective-permute-start(bf16[88,256]{1,0:T(8,128)(2,1)S(1)} %add_convert_fusion), channel_id=1, source_target_pairs={{0,8},{8,0},{16,24},{24,16},{1,9},{9,1},{17,25},{25,17},{2,10},{10... | collective-permute-start | bytes 135176 | tf_op jit(solution)/shard_map/ppermute | solution.py:229
  89.8 1.5 %collective-permute-done.27 = bf16[88,256]{1,0:T(8,128)(2,1)S(1)} collective-permute-done((bf16[88,256]{1,0:T(8,128)(2,1)S(1)}, bf16[88,256]{1,0:T(8,128)(2,1)S(1)}, u32[]{:S(2)}, u32[]{:S(2)}) %collective-permute-start.27) | collective-permute-done | bytes 45088 | tf_op jit(solution)/shard_map/ppermute | solution.py:229
  93.8 1.3 %last.1 = (f32[128,256]{1,0:T(8,128)}, f32[172,256]{1,0:T(8,128)}) custom-call(s32[2]{0:T(128)S(1)} %pad_add_fusion.1.spot_ref, f32[160,256]{1,0:T(8,128)S(1)} %constant_dynamic-update-slice_fusion.6.total_ref, f32[160,256]{1,0:T(8,128)S(1)} %collective-permute-done.30.other_ref), custom_call_target="tpu_custom_call" | custom-call | tf_op jit(solution)/shard_map/last/pallas_call | solution.py:144
  (121 shorter events, 23.2 us)
Async XLA Ops:
  0.6 50.8 %copy-start = (bf16[128,256]{1,0:T(8,128)(2,1)S(1)}, bf16[128,256]{1,0:T(8,128)(2,1)}, u32[]{:S(2)}) copy-start(bf16[128,256]{1,0:T(8,128)(2,1)} %param.17) | copy-start | bytes 196612
  0.6 11.9 %collective-permute-start = (bf16[256,128]{1,0:T(8,128)(2,1)}, bf16[256,128]{1,0:T(8,128)(2,1)S(1)}, u32[]{:S(2)}, u32[]{:S(2)}) collective-permute-start(bf16[256,128]{1,0:T(8,128)(2,1)} %bitcast.59), channel_id=1, source_target_pairs={{0,0},{1,1},{2,2},{3,3},{4,4},{5,5},{6,6},{7,7},{8,10},{9,11},{10,... | collective-permute-start | bytes 196616 | tf_op jit(solution)/shard_map/ppermute | solution.py:253
  2.3 11.3 %collective-permute-start.1 = (bf16[256,128]{1,0:T(8,128)(2,1)}, bf16[256,128]{1,0:T(8,128)(2,1)S(1)}, u32[]{:S(2)}, u32[]{:S(2)}) collective-permute-start(bf16[256,128]{1,0:T(8,128)(2,1)} %bitcast.60), channel_id=1, source_target_pairs={{0,10},{1,11},{2,12},{3,13},{4,14},{5,15},{6,8},{7,9},{8,0},{9,1},... | collective-permute-start | bytes 196616 | tf_op jit(solution)/shard_map/ppermute | solution.py:253
  8.3 5.6 %collective-permute-start.2 = (bf16[256,128]{1,0:T(8,128)(2,1)}, bf16[256,128]{1,0:T(8,128)(2,1)S(1)}, u32[]{:S(2)}, u32[]{:S(2)}) collective-permute-start(bf16[256,128]{1,0:T(8,128)(2,1)} %bitcast.61), channel_id=1, source_target_pairs={{0,20},{1,21},{2,22},{3,23},{4,16},{5,17},{6,18},{7,19},{8,30},{9,... | collective-permute-start | bytes 196616 | tf_op jit(solution)/shard_map/ppermute | solution.py:253
  9.6 5.4 %collective-permute-start.3 = (bf16[256,128]{1,0:T(8,128)(2,1)}, bf16[256,128]{1,0:T(8,128)(2,1)S(1)}, u32[]{:S(2)}, u32[]{:S(2)}) collective-permute-start(bf16[256,128]{1,0:T(8,128)(2,1)} %bitcast.62), channel_id=1, source_target_pairs={{0,30},{1,31},{2,24},{3,25},{4,26},{5,27},{6,28},{7,29},{8,20},{9,... | collective-permute-start | bytes 196616 | tf_op jit(solution)/shard_map/ppermute | solution.py:253
  13.6 6.5 %collective-permute-start.4 = (bf16[512,128]{1,0:T(8,128)(2,1)S(1)}, bf16[512,128]{1,0:T(8,128)(2,1)S(1)}, u32[]{:S(2)}, u32[]{:S(2)}) collective-permute-start(bf16[512,128]{1,0:T(8,128)(2,1)S(1)} %pad_maximum_fusion.2), channel_id=1, source_target_pairs={{0,1},{1,24},{2,3},{3,26},{4,5},{5,28},{6,7},{7,30},{8,9},{9,0},{1... | collective-permute-start | bytes 393224 | tf_op jit(solution)/shard_map/ppermute | solution.py:240
  15.0 6.5 %collective-permute-start.5 = (bf16[512,128]{1,0:T(8,128)(2,1)S(1)}, bf16[512,128]{1,0:T(8,128)(2,1)S(1)}, u32[]{:S(2)}, u32[]{:S(2)}) collective-permute-start(bf16[512,128]{1,0:T(8,128)(2,1)S(1)} %pad_maximum_fusion.3), channel_id=1, source_target_pairs={{0,1},{1,24},{2,3},{3,26},{4,5},{5,28},{6,7},{7,30},{8,9},{9,0},{1... | collective-permute-start | bytes 393224 | tf_op jit(solution)/shard_map/ppermute | solution.py:240
  22.8 7.2 %collective-permute-start.6 = (f32[256,128]{1,0:T(8,128)S(1)}, f32[256,128]{1,0:T(8,128)S(1)}, u32[]{:S(2)}, u32[]{:S(2)}) collective-permute-start(f32[256,128]{1,0:T(8,128)S(1)} %get-tuple-element.90), channel_id=1, source_target_pairs={{0,24},{8,16},{16,8},{24,0},{1,25},{9,17},{17,9},{25,1},{2,26},{10... | collective-permute-start | bytes 393224 | tf_op jit(solution)/shard_map/ppermute | solution.py:229
  24.3 9.8 %collective-permute-start.7 = (f32[256,128]{1,0:T(8,128)S(1)}, f32[256,128]{1,0:T(8,128)S(1)}, u32[]{:S(2)}, u32[]{:S(2)}) collective-permute-start(f32[256,128]{1,0:T(8,128)S(1)} %get-tuple-element.92), channel_id=1, source_target_pairs={{0,16},{8,24},{16,0},{24,8},{1,17},{9,25},{17,1},{25,9},{2,18},{10... | collective-permute-start | bytes 393224 | tf_op jit(solution)/shard_map/ppermute | solution.py:229
  29.5 5.7 %collective-permute-start.8 = (f32[256,128]{1,0:T(8,128)S(1)}, f32[256,128]{1,0:T(8,128)S(1)}, u32[]{:S(2)}, u32[]{:S(2)}) collective-permute-start(f32[256,128]{1,0:T(8,128)S(1)} %get-tuple-element.91), channel_id=1, source_target_pairs={{0,8},{8,0},{16,24},{24,16},{1,9},{9,1},{17,25},{25,17},{2,10},{10... | collective-permute-start | bytes 393224 | tf_op jit(solution)/shard_map/ppermute | solution.py:229
  35.3 7.4 %collective-permute-start.9 = (bf16[272,128]{1,0:T(8,128)(2,1)S(1)}, bf16[272,128]{1,0:T(8,128)(2,1)S(1)}, u32[]{:S(2)}, u32[]{:S(2)}) collective-permute-start(bf16[272,128]{1,0:T(8,128)(2,1)S(1)} %pad_maximum_fusion.5), channel_id=1, source_target_pairs={{0,0},{1,1},{2,2},{3,3},{4,4},{5,5},{6,6},{7,7},{8,10},{9,11},{10,... | collective-permute-start | bytes 208904 | tf_op jit(solution)/shard_map/ppermute | solution.py:253
  36.0 6.7 %collective-permute-start.10 = (bf16[272,128]{1,0:T(8,128)(2,1)S(1)}, bf16[272,128]{1,0:T(8,128)(2,1)S(1)}, u32[]{:S(2)}, u32[]{:S(2)}) collective-permute-start(bf16[272,128]{1,0:T(8,128)(2,1)S(1)} %pad_maximum_fusion.5), channel_id=1, source_target_pairs={{0,10},{1,11},{2,12},{3,13},{4,14},{5,15},{6,8},{7,9},{8,0},{9,1},... | collective-permute-start | bytes 208904 | tf_op jit(solution)/shard_map/ppermute | solution.py:253
  37.0 7.8 %collective-permute-start.11 = (bf16[272,128]{1,0:T(8,128)(2,1)S(1)}, bf16[272,128]{1,0:T(8,128)(2,1)S(1)}, u32[]{:S(2)}, u32[]{:S(2)}) collective-permute-start(bf16[272,128]{1,0:T(8,128)(2,1)S(1)} %pad_maximum_fusion.5), channel_id=1, source_target_pairs={{0,20},{1,21},{2,22},{3,23},{4,16},{5,17},{6,18},{7,19},{8,30},{9,... | collective-permute-start | bytes 208904 | tf_op jit(solution)/shard_map/ppermute | solution.py:253
  41.7 5.4 %collective-permute-start.12 = (bf16[272,128]{1,0:T(8,128)(2,1)S(1)}, bf16[272,128]{1,0:T(8,128)(2,1)S(1)}, u32[]{:S(2)}, u32[]{:S(2)}) collective-permute-start(bf16[272,128]{1,0:T(8,128)(2,1)S(1)} %pad_maximum_fusion.5), channel_id=1, source_target_pairs={{0,30},{1,31},{2,24},{3,25},{4,26},{5,27},{6,28},{7,29},{8,20},{9,... | collective-permute-start | bytes 208904 | tf_op jit(solution)/shard_map/ppermute | solution.py:253
  42.7 5.8 %collective-permute-start.13 = (bf16[272,128]{1,0:T(8,128)(2,1)S(1)}, bf16[272,128]{1,0:T(8,128)(2,1)S(1)}, u32[]{:S(2)}, u32[]{:S(2)}) collective-permute-start(bf16[272,128]{1,0:T(8,128)(2,1)S(1)} %collective-permute-done.9), channel_id=1, source_target_pairs={{0,1},{1,24},{2,3},{3,26},{4,5},{5,28},{6,7},{7,30},{8,9},{9,0},{1... | collective-permute-start | bytes 208904 | tf_op jit(solution)/shard_map/ppermute | solution.py:240
  42.8 8.0 %collective-permute-start.15 = (bf16[272,128]{1,0:T(8,128)(2,1)S(1)}, bf16[272,128]{1,0:T(8,128)(2,1)S(1)}, u32[]{:S(2)}, u32[]{:S(2)}) collective-permute-start(bf16[272,128]{1,0:T(8,128)(2,1)S(1)} %collective-permute-done.10), channel_id=1, source_target_pairs={{0,1},{1,24},{2,3},{3,26},{4,5},{5,28},{6,7},{7,30},{8,9},{9,0},{1... | collective-permute-start | bytes 208904 | tf_op jit(solution)/shard_map/ppermute | solution.py:240
  44.8 6.0 %collective-permute-start.16 = (bf16[272,128]{1,0:T(8,128)(2,1)S(1)}, bf16[272,128]{1,0:T(8,128)(2,1)S(1)}, u32[]{:S(2)}, u32[]{:S(2)}) collective-permute-start(bf16[272,128]{1,0:T(8,128)(2,1)S(1)} %collective-permute-done.11), channel_id=1, source_target_pairs={{0,1},{1,24},{2,3},{3,26},{4,5},{5,28},{6,7},{7,30},{8,9},{9,0},{1... | collective-permute-start | bytes 208904 | tf_op jit(solution)/shard_map/ppermute | solution.py:240
  47.0 3.7 %collective-permute-start.14 = (bf16[272,128]{1,0:T(8,128)(2,1)S(1)}, bf16[272,128]{1,0:T(8,128)(2,1)S(1)}, u32[]{:S(2)}, u32[]{:S(2)}) collective-permute-start(bf16[272,128]{1,0:T(8,128)(2,1)S(1)} %collective-permute-done.12), channel_id=1, source_target_pairs={{0,1},{1,24},{2,3},{3,26},{4,5},{5,28},{6,7},{7,30},{8,9},{9,0},{1... | collective-permute-start | bytes 208904 | tf_op jit(solution)/shard_map/ppermute | solution.py:240
  53.7 8.4 %collective-permute-start.17 = (s16[272,256]{1,0:T(8,128)(2,1)S(1)}, s16[272,256]{1,0:T(8,128)(2,1)S(1)}, u32[]{:S(2)}, u32[]{:S(2)}) collective-permute-start(s16[272,256]{1,0:T(8,128)(2,1)S(1)} %get-tuple-element.62), channel_id=1, source_target_pairs={{0,24},{8,16},{16,8},{24,0},{1,25},{9,17},{17,9},{25,1},{2,26},{10... | collective-permute-start | bytes 417800 | tf_op jit(solution)/shard_map/ppermute | solution.py:229
  57.5 6.0 %collective-permute-start.18 = (s16[272,256]{1,0:T(8,128)(2,1)S(1)}, s16[272,256]{1,0:T(8,128)(2,1)S(1)}, u32[]{:S(2)}, u32[]{:S(2)}) collective-permute-start(s16[272,256]{1,0:T(8,128)(2,1)S(1)} %get-tuple-element.63), channel_id=1, source_target_pairs={{0,16},{8,24},{16,0},{24,8},{1,17},{9,25},{17,1},{25,9},{2,18},{10... | collective-permute-start | bytes 417800 | tf_op jit(solution)/shard_map/ppermute | solution.py:229
  58.9 5.1 %collective-permute-start.19 = (s16[272,256]{1,0:T(8,128)(2,1)S(1)}, s16[272,256]{1,0:T(8,128)(2,1)S(1)}, u32[]{:S(2)}, u32[]{:S(2)}) collective-permute-start(s16[272,256]{1,0:T(8,128)(2,1)S(1)} %get-tuple-element.64), channel_id=1, source_target_pairs={{0,8},{8,0},{16,24},{24,16},{1,9},{9,1},{17,25},{25,17},{2,10},{10... | collective-permute-start | bytes 417800 | tf_op jit(solution)/shard_map/ppermute | solution.py:229
  65.3 7.3 %collective-permute-start.20 = (bf16[304,256]{1,0:T(8,128)(2,1)S(1)}, bf16[304,256]{1,0:T(8,128)(2,1)S(1)}, u32[]{:S(2)}, u32[]{:S(2)}) collective-permute-start(bf16[304,256]{1,0:T(8,128)(2,1)S(1)} %get-tuple-element.69), channel_id=1, source_target_pairs={{0,24},{8,16},{16,8},{24,0},{1,25},{9,17},{17,9},{25,1},{2,26},{10... | collective-permute-start | bytes 466952 | tf_op jit(solution)/shard_map/ppermute | solution.py:229
  66.6 6.7 %collective-permute-start.21 = (bf16[304,256]{1,0:T(8,128)(2,1)S(1)}, bf16[304,256]{1,0:T(8,128)(2,1)S(1)}, u32[]{:S(2)}, u32[]{:S(2)}) collective-permute-start(bf16[304,256]{1,0:T(8,128)(2,1)S(1)} %get-tuple-element.70), channel_id=1, source_target_pairs={{0,16},{8,24},{16,0},{24,8},{1,17},{9,25},{17,1},{25,9},{2,18},{10... | collective-permute-start | bytes 466952 | tf_op jit(solution)/shard_map/ppermute | solution.py:229
  67.3 6.1 %collective-permute-start.22 = (bf16[304,256]{1,0:T(8,128)(2,1)S(1)}, bf16[304,256]{1,0:T(8,128)(2,1)S(1)}, u32[]{:S(2)}, u32[]{:S(2)}) collective-permute-start(bf16[304,256]{1,0:T(8,128)(2,1)S(1)} %get-tuple-element.71), channel_id=1, source_target_pairs={{0,8},{8,0},{16,24},{24,16},{1,9},{9,1},{17,25},{25,17},{2,10},{10... | collective-permute-start | bytes 466952 | tf_op jit(solution)/shard_map/ppermute | solution.py:229
  75.3 1.4 %collective-permute-start.23 = (f32[88,256]{1,0:T(8,128)S(1)}, f32[88,256]{1,0:T(8,128)S(1)}, u32[]{:S(2)}, u32[]{:S(2)}) collective-permute-start(f32[88,256]{1,0:T(8,128)S(1)} %pad_maximum_fusion.4), channel_id=1, source_target_pairs={{0,1},{1,0},{2,3},{3,2},{4,5},{5,4},{6,7},{7,6},{8,9},{9,8},{10,11... | collective-permute-start | bytes 270344 | tf_op jit(solution)/shard_map/ppermute | solution.py:243
  76.6 4.5 %collective-permute-start.24 = (bf16[88,256]{1,0:T(8,128)(2,1)S(1)}, bf16[88,256]{1,0:T(8,128)(2,1)S(1)}, u32[]{:S(2)}, u32[]{:S(2)}) collective-permute-start(bf16[88,256]{1,0:T(8,128)(2,1)S(1)} %fusion.15), channel_id=1, source_target_pairs={{0,2},{1,3},{2,0},{3,1},{4,6},{5,7},{6,4},{7,5},{8,10},{9,11},{10,... | collective-permute-start | bytes 135176 | tf_op jit(solution)/shard_map/ppermute | solution.py:243
  78.1 5.8 %collective-permute-start.25 = (bf16[88,256]{1,0:T(8,128)(2,1)S(1)}, bf16[88,256]{1,0:T(8,128)(2,1)S(1)}, u32[]{:S(2)}, u32[]{:S(2)}) collective-permute-start(bf16[88,256]{1,0:T(8,128)(2,1)S(1)} %fusion.15), channel_id=1, source_target_pairs={{0,4},{1,5},{2,6},{3,7},{4,0},{5,1},{6,2},{7,3},{8,12},{9,13},{10,... | collective-permute-start | bytes 135176 | tf_op jit(solution)/shard_map/ppermute | solution.py:243
  80.3 5.8 %collective-permute-start.26 = (bf16[88,256]{1,0:T(8,128)(2,1)S(1)}, bf16[88,256]{1,0:T(8,128)(2,1)S(1)}, u32[]{:S(2)}, u32[]{:S(2)}) collective-permute-start(bf16[88,256]{1,0:T(8,128)(2,1)S(1)} %fusion.15), channel_id=1, source_target_pairs={{0,6},{1,7},{2,4},{3,5},{4,2},{5,3},{6,0},{7,1},{8,14},{9,15},{10,... | collective-permute-start | bytes 135176 | tf_op jit(solution)/shard_map/ppermute | solution.py:243
  86.2 5.0 %collective-permute-start.27 = (bf16[88,256]{1,0:T(8,128)(2,1)S(1)}, bf16[88,256]{1,0:T(8,128)(2,1)S(1)}, u32[]{:S(2)}, u32[]{:S(2)}) collective-permute-start(bf16[88,256]{1,0:T(8,128)(2,1)S(1)} %add_convert_fusion), channel_id=1, source_target_pairs={{0,24},{8,16},{16,8},{24,0},{1,25},{9,17},{17,9},{25,1},{2,26},{10... | collective-permute-start | bytes 135176 | tf_op jit(solution)/shard_map/ppermute | solution.py:229
  87.7 4.0 %collective-permute-start.28 = (bf16[88,256]{1,0:T(8,128)(2,1)S(1)}, bf16[88,256]{1,0:T(8,128)(2,1)S(1)}, u32[]{:S(2)}, u32[]{:S(2)}) collective-permute-start(bf16[88,256]{1,0:T(8,128)(2,1)S(1)} %add_convert_fusion), channel_id=1, source_target_pairs={{0,16},{8,24},{16,0},{24,8},{1,17},{9,25},{17,1},{25,9},{2,18},{10... | collective-permute-start | bytes 135176 | tf_op jit(solution)/shard_map/ppermute | solution.py:229
  88.2 4.0 %collective-permute-start.29 = (bf16[88,256]{1,0:T(8,128)(2,1)S(1)}, bf16[88,256]{1,0:T(8,128)(2,1)S(1)}, u32[]{:S(2)}, u32[]{:S(2)}) collective-permute-start(bf16[88,256]{1,0:T(8,128)(2,1)S(1)} %add_convert_fusion), channel_id=1, source_target_pairs={{0,8},{8,0},{16,24},{24,16},{1,9},{9,1},{17,25},{25,17},{2,10},{10... | collective-permute-start | bytes 135176 | tf_op jit(solution)/shard_map/ppermute | solution.py:229
  92.4 1.5 %collective-permute-start.30 = (f32[160,256]{1,0:T(8,128)S(1)}, f32[160,256]{1,0:T(8,128)S(1)}, u32[]{:S(2)}, u32[]{:S(2)}) collective-permute-start(f32[160,256]{1,0:T(8,128)S(1)} %constant_dynamic-update-slice_fusion.6.total_ref), channel_id=1, source_target_pairs={{0,1},{1,0},{2,3},{3,2},{4,5},{5,4},{6,7},{7,6},{8,9},{9,8},{10,11... | collective-permute-start | bytes 491528 | tf_op jit(solution)/shard_map/ppermute | solution.py:243
  (8 other events, 66.8 us)

commit v19 on v17

--- a/solution.py
+++ b/solution.py
@@ -272,7 +272,8 @@
 
     def sum_over(value, move, first, size):
         rounded = value.astype(bf16)
-        parts = [rounded if d == 0 else move(rounded, d) for d in range(0, size, first)]
+        moved = [move(rounded, d) for d in range(first, size, first)][::-1]
+        parts = [rounded] + lax.optimization_barrier(moved)[::-1]
         parts = [part.astype(f32) for part in parts]
         while len(parts) > 1:
             parts = [parts[i] + parts[i + 1] for i in range(0, len(parts), 2)]

time: 95.6 us -> 95.2 us (level)
    ppermute x5, waiting for transfers between devices: 6.67 us -> 5.25 us  [exchange(): return lax.ppermute(value, 'blk', [(c, c ^ delta) for c in range(blks)])]
where the time goes in v19:
time: 95.2 us; the launch traced here: 94.9 us
  starting transfers between devices  47.8 us (50%)
  waiting for transfers between devices  26.1 us (27%)
  Pallas kernels  8.3 us (9%)
  matrix products  6.06 us (6%)
  local copies, waits for them, and re-layouts  3.31 us (3%)
  other arithmetic  2.06 us (2%)
  between operations  1.23 us (1%)
    ppermute x12, starting transfers between devices, swap(): return lax.ppermute(value, 'rep', [(r, r ^ delta) for r in range(reps)])  19.3 us
    ppermute x8, starting transfers between devices, to_pieces(): pieces.append(lax.ppermute(value, ('rep', 'blk'), pairs))  18.8 us
    ppermute x12, waiting for transfers between devices, swap(): return lax.ppermute(value, 'rep', [(r, r ^ delta) for r in range(reps)])  14.6 us
    dot_general x5, matrix products, dot(): return jnp.dot(left, right, preferred_element_type=jnp.float32)  5.7 us
    pallas_call x2, Pallas kernels, build_dense(): pl.pallas_call(body, grid_spec=pltpu.PrefetchScalarGridSpec(num_scalar_pr...  5.26 us
    ppermute x5, waiting for transfers between devices, exchange(): return lax.ppermute(value, 'blk', [(c, c ^ delta) for c in range(blks)])  5.25 us
    ppermute x6, starting transfers between devices, to_section(): return lax.ppermute(block, ('rep', 'blk'), pairs)  5.11 us
    ppermute x5, starting transfers between devices, exchange(): return lax.ppermute(value, 'blk', [(c, c ^ delta) for c in range(blks)])  4.59 us
  transfers between devices with their start and end apart: 31, of which 18 were waited for; matrix products, arithmetic and copies ran while one was open for 5% of the time, Pallas kernels for 6%

profile of v19, /device:TPU:0, one launch (start us, length us, event | category | flops | bytes accessed | tf_op | source)
XLA Modules:
  0.0 94.9 jit_solution(11540814094518792272)
XLA Ops:
  0.6 1.6 %collective-permute-start = (bf16[256,128]{1,0:T(8,128)(2,1)}, bf16[256,128]{1,0:T(8,128)(2,1)S(1)}, u32[]{:S(2)}, u32[]{:S(2)}) collective-permute-start(bf16[256,128]{1,0:T(8,128)(2,1)} %bitcast.59), channel_id=1, source_target_pairs={{0,0},{1,1},{2,2},{3,3},{4,4},{5,5},{6,6},{7,7},{8,10},{9,11},{10,... | collective-permute-start | bytes 196616 | tf_op jit(solution)/shard_map/ppermute | solution.py:253
  2.3 6.0 %collective-permute-start.1 = (bf16[256,128]{1,0:T(8,128)(2,1)}, bf16[256,128]{1,0:T(8,128)(2,1)S(1)}, u32[]{:S(2)}, u32[]{:S(2)}) collective-permute-start(bf16[256,128]{1,0:T(8,128)(2,1)} %bitcast.60), channel_id=1, source_target_pairs={{0,10},{1,11},{2,12},{3,13},{4,14},{5,15},{6,8},{7,9},{8,0},{9,1},... | collective-permute-start | bytes 196616 | tf_op jit(solution)/shard_map/ppermute | solution.py:253
  8.3 1.3 %collective-permute-start.2 = (bf16[256,128]{1,0:T(8,128)(2,1)}, bf16[256,128]{1,0:T(8,128)(2,1)S(1)}, u32[]{:S(2)}, u32[]{:S(2)}) collective-permute-start(bf16[256,128]{1,0:T(8,128)(2,1)} %bitcast.61), channel_id=1, source_target_pairs={{0,20},{1,21},{2,22},{3,23},{4,16},{5,17},{6,18},{7,19},{8,30},{9,... | collective-permute-start | bytes 196616 | tf_op jit(solution)/shard_map/ppermute | solution.py:253
  9.6 3.0 %collective-permute-start.3 = (bf16[256,128]{1,0:T(8,128)(2,1)}, bf16[256,128]{1,0:T(8,128)(2,1)S(1)}, u32[]{:S(2)}, u32[]{:S(2)}) collective-permute-start(bf16[256,128]{1,0:T(8,128)(2,1)} %bitcast.62), channel_id=1, source_target_pairs={{0,30},{1,31},{2,24},{3,25},{4,26},{5,27},{6,28},{7,29},{8,20},{9,... | collective-permute-start | bytes 196616 | tf_op jit(solution)/shard_map/ppermute | solution.py:253
  17.9 2.1 %dense.1 = bf16[1024,2048]{1,0:T(8,128)(2,1)S(1)} custom-call(s32[2,19]{1,0:T(2,128)S(1)} %pad_add_fusion.meta_ref, bf16[2,16,128,128]{3,2,1,0:T(8,128)(2,1)S(1)} %bitcast.50), custom_call_target="tpu_custom_call" | custom-call | bytes 8388608 | tf_op jit(solution)/shard_map/dense/pallas_call | solution.py:183
  20.1 1.4 %collective-permute-done.5 = bf16[512,128]{1,0:T(8,128)(2,1)S(1)} collective-permute-done((bf16[512,128]{1,0:T(8,128)(2,1)S(1)}, bf16[512,128]{1,0:T(8,128)(2,1)S(1)}, u32[]{:S(2)}, u32[]{:S(2)}) %collective-permute-start.5) | collective-permute-done | bytes 131104 | tf_op jit(solution)/shard_map/ppermute | solution.py:240
  22.8 1.3 %collective-permute-start.6 = (f32[256,128]{1,0:T(8,128)S(1)}, f32[256,128]{1,0:T(8,128)S(1)}, u32[]{:S(2)}, u32[]{:S(2)}) collective-permute-start(f32[256,128]{1,0:T(8,128)S(1)} %get-tuple-element.84), channel_id=1, source_target_pairs={{0,24},{8,16},{16,8},{24,0},{1,25},{9,17},{17,9},{25,1},{2,26},{10... | collective-permute-start | bytes 393224 | tf_op jit(solution)/shard_map/ppermute | solution.py:229
  24.1 5.4 %collective-permute-start.7 = (f32[256,128]{1,0:T(8,128)S(1)}, f32[256,128]{1,0:T(8,128)S(1)}, u32[]{:S(2)}, u32[]{:S(2)}) collective-permute-start(f32[256,128]{1,0:T(8,128)S(1)} %get-tuple-element.86), channel_id=1, source_target_pairs={{0,16},{8,24},{16,0},{24,8},{1,17},{9,25},{17,1},{25,9},{2,18},{10... | collective-permute-start | bytes 393224 | tf_op jit(solution)/shard_map/ppermute | solution.py:229
  29.5 4.3 %collective-permute-done.7 = f32[256,128]{1,0:T(8,128)S(1)} collective-permute-done((f32[256,128]{1,0:T(8,128)S(1)}, f32[256,128]{1,0:T(8,128)S(1)}, u32[]{:S(2)}, u32[]{:S(2)}) %collective-permute-start.7) | collective-permute-done | bytes 131104 | tf_op jit(solution)/shard_map/ppermute | solution.py:229
  33.8 1.4 %collective-permute-done.8 = f32[256,128]{1,0:T(8,128)S(1)} collective-permute-done((f32[256,128]{1,0:T(8,128)S(1)}, f32[256,128]{1,0:T(8,128)S(1)}, u32[]{:S(2)}, u32[]{:S(2)}) %collective-permute-start.8) | collective-permute-done | bytes 131104 | tf_op jit(solution)/shard_map/ppermute | solution.py:229
  37.1 4.6 %collective-permute-start.11 = (bf16[272,128]{1,0:T(8,128)(2,1)S(1)}, bf16[272,128]{1,0:T(8,128)(2,1)S(1)}, u32[]{:S(2)}, u32[]{:S(2)}) collective-permute-start(bf16[272,128]{1,0:T(8,128)(2,1)S(1)} %pad_maximum_fusion.5), channel_id=1, source_target_pairs={{0,20},{1,21},{2,22},{3,23},{4,16},{5,17},{6,18},{7,19},{8,30},{9,... | collective-permute-start | bytes 208904 | tf_op jit(solution)/shard_map/ppermute | solution.py:253
  42.3 2.5 %collective-permute-start.15 = (bf16[272,128]{1,0:T(8,128)(2,1)S(1)}, bf16[272,128]{1,0:T(8,128)(2,1)S(1)}, u32[]{:S(2)}, u32[]{:S(2)}) collective-permute-start(bf16[272,128]{1,0:T(8,128)(2,1)S(1)} %collective-permute-done.10), channel_id=1, source_target_pairs={{0,1},{1,24},{2,3},{3,26},{4,5},{5,28},{6,7},{7,30},{8,9},{9,0},{1... | collective-permute-start | bytes 208904 | tf_op jit(solution)/shard_map/ppermute | solution.py:240
  45.5 1.4 %collective-permute-done.12 = bf16[272,128]{1,0:T(8,128)(2,1)S(1)} collective-permute-done((bf16[272,128]{1,0:T(8,128)(2,1)S(1)}, bf16[272,128]{1,0:T(8,128)(2,1)S(1)}, u32[]{:S(2)}, u32[]{:S(2)}) %collective-permute-start.12) | collective-permute-done | bytes 69664 | tf_op jit(solution)/shard_map/ppermute | solution.py:253
  48.4 2.2 %collective-permute-done.14 = bf16[272,128]{1,0:T(8,128)(2,1)S(1)} collective-permute-done((bf16[272,128]{1,0:T(8,128)(2,1)S(1)}, bf16[272,128]{1,0:T(8,128)(2,1)S(1)}, u32[]{:S(2)}, u32[]{:S(2)}) %collective-permute-start.14) | collective-permute-done | bytes 69664 | tf_op jit(solution)/shard_map/ppermute | solution.py:240
  53.5 3.3 %collective-permute-start.17 = (s16[272,256]{1,0:T(8,128)(2,1)S(1)}, s16[272,256]{1,0:T(8,128)(2,1)S(1)}, u32[]{:S(2)}, u32[]{:S(2)}) collective-permute-start(s16[272,256]{1,0:T(8,128)(2,1)S(1)} %get-tuple-element.59), channel_id=1, source_target_pairs={{0,24},{8,16},{16,8},{24,0},{1,25},{9,17},{17,9},{25,1},{2,26},{10... | collective-permute-start | bytes 417800 | tf_op jit(solution)/shard_map/ppermute | solution.py:229
  56.8 2.2 %collective-permute-start.18 = (s16[272,256]{1,0:T(8,128)(2,1)S(1)}, s16[272,256]{1,0:T(8,128)(2,1)S(1)}, u32[]{:S(2)}, u32[]{:S(2)}) collective-permute-start(s16[272,256]{1,0:T(8,128)(2,1)S(1)} %get-tuple-element.60), channel_id=1, source_target_pairs={{0,16},{8,24},{16,0},{24,8},{1,17},{9,25},{17,1},{25,9},{2,18},{10... | collective-permute-start | bytes 417800 | tf_op jit(solution)/shard_map/ppermute | solution.py:229
  59.0 1.4 %fusion.3 = bf16[2048,256]{1,0:T(8,128)(2,1)} fusion(bf16[2048,256]{1,0:T(8,128)(2,1)S(1)} %pad_maximum_fusion, bf16[2048,128]{1,0:T(8,128)(2,1)S(1)} %slice_dynamic-update-slice_fusion, bf16[128,256]{1,0:T(8,128)(2,1)S(1)} %copy-done), kind=kOutput, calls=%fused_computation.6 | convolution fusion | flops 135266304 | bytes 2686976 | tf_op jit(solution)/shard_map/dot_general | solution.py:32
  61.4 1.5 %collective-permute-done.18.refs_1_ = s16[272,256]{1,0:T(8,128)(2,1)S(1)} collective-permute-done((s16[272,256]{1,0:T(8,128)(2,1)S(1)}, s16[272,256]{1,0:T(8,128)(2,1)S(1)}, u32[]{:S(2)}, u32[]{:S(2)}) %collective-permute-start.18) | collective-permute-done | bytes 139296 | tf_op jit(solution)/shard_map/ppermute | solution.py:229
  64.1 1.3 %head.1 = (f32[256,172]{1,0:T(8,128)S(1)}, f32[48,256]{1,0:T(8,128)S(1)}, bf16[304,256]{1,0:T(8,128)(2,1)S(1)}, bf16[304,256]{1,0:T(8,128)(2,1)S(1)}, bf16[304,2...) custom-call(s32[2]{0:T(128)S(1)} %pad_add_fusion.1.spot_ref, bf16[172,256]{1,0:T(8,128)(2,1)S(1)} %bitcast.53, ...), custom_call_target="tpu_custom_call" | custom-call | tf_op jit(solution)/shard_map/head/pallas_call | solution.py:144
  65.6 1.7 %collective-permute-start.21 = (bf16[304,256]{1,0:T(8,128)(2,1)S(1)}, bf16[304,256]{1,0:T(8,128)(2,1)S(1)}, u32[]{:S(2)}, u32[]{:S(2)}) collective-permute-start(bf16[304,256]{1,0:T(8,128)(2,1)S(1)} %get-tuple-element.67), channel_id=1, source_target_pairs={{0,16},{8,24},{16,0},{24,8},{1,17},{9,25},{17,1},{25,9},{2,18},{10... | collective-permute-start | bytes 466952 | tf_op jit(solution)/shard_map/ppermute | solution.py:229
  67.4 1.6 %collective-permute-start.22 = (bf16[304,256]{1,0:T(8,128)(2,1)S(1)}, bf16[304,256]{1,0:T(8,128)(2,1)S(1)}, u32[]{:S(2)}, u32[]{:S(2)}) collective-permute-start(bf16[304,256]{1,0:T(8,128)(2,1)S(1)} %get-tuple-element.68), channel_id=1, source_target_pairs={{0,24},{8,16},{16,8},{24,0},{1,25},{9,17},{17,9},{25,1},{2,26},{10... | collective-permute-start | bytes 466952 | tf_op jit(solution)/shard_map/ppermute | solution.py:229
  69.0 3.1 %dense_turned.1 = bf16[2048,1024]{1,0:T(8,128)(2,1)S(1)} custom-call(s32[2,19]{1,0:T(2,128)S(1)} %pad_add_fusion.meta_ref, bf16[2,16,128,128]{3,2,1,0:T(8,128)(2,1)S(1)} %bitcast.51), custom_call_target="tpu_custom_call" | custom-call | bytes 8388608 | tf_op jit(solution)/shard_map/dense_turned/pallas_call | solution.py:183
  72.2 1.3 %collective-permute-done.22 = bf16[304,256]{1,0:T(8,128)(2,1)S(1)} collective-permute-done((bf16[304,256]{1,0:T(8,128)(2,1)S(1)}, bf16[304,256]{1,0:T(8,128)(2,1)S(1)}, u32[]{:S(2)}, u32[]{:S(2)}) %collective-permute-start.22) | collective-permute-done | bytes 155680 | tf_op jit(solution)/shard_map/ppermute | solution.py:229
  73.6 1.3 %fusion.2 = bf16[2048,256]{1,0:T(8,128)(2,1)S(1)} fusion(bf16[2048,1024]{1,0:T(8,128)(2,1)S(1)} %dense_turned.1, bf16[1024,256]{1,0:T(8,128)(2,1)S(1)} %pad_maximum_fusion.1, bf16[2048,256]{1,0:T(8,128)(2,1)S(1)} %copy-done.7), kind=kOutput, calls=%fused_computation.4 | convolution fusion | flops 1075838976 | bytes 6815744 | tf_op jit(solution)/shard_map/dot_general | solution.py:32
  75.4 1.3 %collective-permute-done.23 = f32[88,256]{1,0:T(8,128)S(1)} collective-permute-done((f32[88,256]{1,0:T(8,128)S(1)}, f32[88,256]{1,0:T(8,128)S(1)}, u32[]{:S(2)}, u32[]{:S(2)}) %collective-permute-start.23) | collective-permute-done | bytes 90144 | tf_op jit(solution)/shard_map/ppermute | solution.py:243
  76.7 2.8 %collective-permute-start.24 = (bf16[88,256]{1,0:T(8,128)(2,1)S(1)}, bf16[88,256]{1,0:T(8,128)(2,1)S(1)}, u32[]{:S(2)}, u32[]{:S(2)}) collective-permute-start(bf16[88,256]{1,0:T(8,128)(2,1)S(1)} %fusion.15), channel_id=1, source_target_pairs={{0,6},{1,7},{2,4},{3,5},{4,2},{5,3},{6,0},{7,1},{8,14},{9,15},{10,... | collective-permute-start | bytes 135176 | tf_op jit(solution)/shard_map/ppermute | solution.py:243
  79.6 1.6 %collective-permute-start.26 = (bf16[88,256]{1,0:T(8,128)(2,1)S(1)}, bf16[88,256]{1,0:T(8,128)(2,1)S(1)}, u32[]{:S(2)}, u32[]{:S(2)}) collective-permute-start(bf16[88,256]{1,0:T(8,128)(2,1)S(1)} %fusion.15), channel_id=1, source_target_pairs={{0,2},{1,3},{2,0},{3,1},{4,6},{5,7},{6,4},{7,5},{8,10},{9,11},{10,... | collective-permute-start | bytes 135176 | tf_op jit(solution)/shard_map/ppermute | solution.py:243
  81.2 1.6 %collective-permute-done.24 = bf16[88,256]{1,0:T(8,128)(2,1)S(1)} collective-permute-done((bf16[88,256]{1,0:T(8,128)(2,1)S(1)}, bf16[88,256]{1,0:T(8,128)(2,1)S(1)}, u32[]{:S(2)}, u32[]{:S(2)}) %collective-permute-start.24) | collective-permute-done | bytes 45088 | tf_op jit(solution)/shard_map/ppermute | solution.py:243
  82.8 1.7 %collective-permute-done.25 = bf16[88,256]{1,0:T(8,128)(2,1)S(1)} collective-permute-done((bf16[88,256]{1,0:T(8,128)(2,1)S(1)}, bf16[88,256]{1,0:T(8,128)(2,1)S(1)}, u32[]{:S(2)}, u32[]{:S(2)}) %collective-permute-start.25) | collective-permute-done | bytes 45088 | tf_op jit(solution)/shard_map/ppermute | solution.py:243
  85.8 1.3 %collective-permute-start.28 = (bf16[88,256]{1,0:T(8,128)(2,1)S(1)}, bf16[88,256]{1,0:T(8,128)(2,1)S(1)}, u32[]{:S(2)}, u32[]{:S(2)}) collective-permute-start(bf16[88,256]{1,0:T(8,128)(2,1)S(1)} %add_convert_fusion), channel_id=1, source_target_pairs={{0,16},{8,24},{16,0},{24,8},{1,17},{9,25},{17,1},{25,9},{2,18},{10... | collective-permute-start | bytes 135176 | tf_op jit(solution)/shard_map/ppermute | solution.py:229
  89.9 2.2 %collective-permute-done.29 = bf16[88,256]{1,0:T(8,128)(2,1)S(1)} collective-permute-done((bf16[88,256]{1,0:T(8,128)(2,1)S(1)}, bf16[88,256]{1,0:T(8,128)(2,1)S(1)}, u32[]{:S(2)}, u32[]{:S(2)}) %collective-permute-start.29) | collective-permute-done | bytes 45088 | tf_op jit(solution)/shard_map/ppermute | solution.py:229
  93.6 1.3 %last.1 = (f32[128,256]{1,0:T(8,128)}, f32[172,256]{1,0:T(8,128)}) custom-call(s32[2]{0:T(128)S(1)} %pad_add_fusion.1.spot_ref, f32[160,256]{1,0:T(8,128)S(1)} %constant_dynamic-update-slice_fusion.6.total_ref, f32[160,256]{1,0:T(8,128)S(1)} %collective-permute-done.30.other_ref), custom_call_target="tpu_custom_call" | custom-call | tf_op jit(solution)/shard_map/last/pallas_call | solution.py:144
  (121 shorter events, 22.3 us)
Async XLA Ops:
  0.6 50.7 %copy-start = (bf16[128,256]{1,0:T(8,128)(2,1)S(1)}, bf16[128,256]{1,0:T(8,128)(2,1)}, u32[]{:S(2)}) copy-start(bf16[128,256]{1,0:T(8,128)(2,1)} %param.17) | copy-start | bytes 196612
  0.6 11.9 %collective-permute-start = (bf16[256,128]{1,0:T(8,128)(2,1)}, bf16[256,128]{1,0:T(8,128)(2,1)S(1)}, u32[]{:S(2)}, u32[]{:S(2)}) collective-permute-start(bf16[256,128]{1,0:T(8,128)(2,1)} %bitcast.59), channel_id=1, source_target_pairs={{0,0},{1,1},{2,2},{3,3},{4,4},{5,5},{6,6},{7,7},{8,10},{9,11},{10,... | collective-permute-start | bytes 196616 | tf_op jit(solution)/shard_map/ppermute | solution.py:253
  2.3 11.3 %collective-permute-start.1 = (bf16[256,128]{1,0:T(8,128)(2,1)}, bf16[256,128]{1,0:T(8,128)(2,1)S(1)}, u32[]{:S(2)}, u32[]{:S(2)}) collective-permute-start(bf16[256,128]{1,0:T(8,128)(2,1)} %bitcast.60), channel_id=1, source_target_pairs={{0,10},{1,11},{2,12},{3,13},{4,14},{5,15},{6,8},{7,9},{8,0},{9,1},... | collective-permute-start | bytes 196616 | tf_op jit(solution)/shard_map/ppermute | solution.py:253
  8.3 5.6 %collective-permute-start.2 = (bf16[256,128]{1,0:T(8,128)(2,1)}, bf16[256,128]{1,0:T(8,128)(2,1)S(1)}, u32[]{:S(2)}, u32[]{:S(2)}) collective-permute-start(bf16[256,128]{1,0:T(8,128)(2,1)} %bitcast.61), channel_id=1, source_target_pairs={{0,20},{1,21},{2,22},{3,23},{4,16},{5,17},{6,18},{7,19},{8,30},{9,... | collective-permute-start | bytes 196616 | tf_op jit(solution)/shard_map/ppermute | solution.py:253
  9.6 5.4 %collective-permute-start.3 = (bf16[256,128]{1,0:T(8,128)(2,1)}, bf16[256,128]{1,0:T(8,128)(2,1)S(1)}, u32[]{:S(2)}, u32[]{:S(2)}) collective-permute-start(bf16[256,128]{1,0:T(8,128)(2,1)} %bitcast.62), channel_id=1, source_target_pairs={{0,30},{1,31},{2,24},{3,25},{4,26},{5,27},{6,28},{7,29},{8,20},{9,... | collective-permute-start | bytes 196616 | tf_op jit(solution)/shard_map/ppermute | solution.py:253
  13.6 6.5 %collective-permute-start.4 = (bf16[512,128]{1,0:T(8,128)(2,1)S(1)}, bf16[512,128]{1,0:T(8,128)(2,1)S(1)}, u32[]{:S(2)}, u32[]{:S(2)}) collective-permute-start(bf16[512,128]{1,0:T(8,128)(2,1)S(1)} %pad_maximum_fusion.2), channel_id=1, source_target_pairs={{0,1},{1,24},{2,3},{3,26},{4,5},{5,28},{6,7},{7,30},{8,9},{9,0},{1... | collective-permute-start | bytes 393224 | tf_op jit(solution)/shard_map/ppermute | solution.py:240
  15.0 6.5 %collective-permute-start.5 = (bf16[512,128]{1,0:T(8,128)(2,1)S(1)}, bf16[512,128]{1,0:T(8,128)(2,1)S(1)}, u32[]{:S(2)}, u32[]{:S(2)}) collective-permute-start(bf16[512,128]{1,0:T(8,128)(2,1)S(1)} %pad_maximum_fusion.3), channel_id=1, source_target_pairs={{0,1},{1,24},{2,3},{3,26},{4,5},{5,28},{6,7},{7,30},{8,9},{9,0},{1... | collective-permute-start | bytes 393224 | tf_op jit(solution)/shard_map/ppermute | solution.py:240
  22.8 6.7 %collective-permute-start.6 = (f32[256,128]{1,0:T(8,128)S(1)}, f32[256,128]{1,0:T(8,128)S(1)}, u32[]{:S(2)}, u32[]{:S(2)}) collective-permute-start(f32[256,128]{1,0:T(8,128)S(1)} %get-tuple-element.84), channel_id=1, source_target_pairs={{0,24},{8,16},{16,8},{24,0},{1,25},{9,17},{17,9},{25,1},{2,26},{10... | collective-permute-start | bytes 393224 | tf_op jit(solution)/shard_map/ppermute | solution.py:229
  24.1 9.8 %collective-permute-start.7 = (f32[256,128]{1,0:T(8,128)S(1)}, f32[256,128]{1,0:T(8,128)S(1)}, u32[]{:S(2)}, u32[]{:S(2)}) collective-permute-start(f32[256,128]{1,0:T(8,128)S(1)} %get-tuple-element.86), channel_id=1, source_target_pairs={{0,16},{8,24},{16,0},{24,8},{1,17},{9,25},{17,1},{25,9},{2,18},{10... | collective-permute-start | bytes 393224 | tf_op jit(solution)/shard_map/ppermute | solution.py:229
  29.5 5.7 %collective-permute-start.8 = (f32[256,128]{1,0:T(8,128)S(1)}, f32[256,128]{1,0:T(8,128)S(1)}, u32[]{:S(2)}, u32[]{:S(2)}) collective-permute-start(f32[256,128]{1,0:T(8,128)S(1)} %get-tuple-element.85), channel_id=1, source_target_pairs={{0,8},{8,0},{16,24},{24,16},{1,9},{9,1},{17,25},{25,17},{2,10},{10... | collective-permute-start | bytes 393224 | tf_op jit(solution)/shard_map/ppermute | solution.py:229
  35.3 6.9 %collective-permute-start.9 = (bf16[272,128]{1,0:T(8,128)(2,1)S(1)}, bf16[272,128]{1,0:T(8,128)(2,1)S(1)}, u32[]{:S(2)}, u32[]{:S(2)}) collective-permute-start(bf16[272,128]{1,0:T(8,128)(2,1)S(1)} %pad_maximum_fusion.5), channel_id=1, source_target_pairs={{0,0},{1,1},{2,2},{3,3},{4,4},{5,5},{6,6},{7,7},{8,10},{9,11},{10,... | collective-permute-start | bytes 208904 | tf_op jit(solution)/shard_map/ppermute | solution.py:253
  36.1 6.3 %collective-permute-start.10 = (bf16[272,128]{1,0:T(8,128)(2,1)S(1)}, bf16[272,128]{1,0:T(8,128)(2,1)S(1)}, u32[]{:S(2)}, u32[]{:S(2)}) collective-permute-start(bf16[272,128]{1,0:T(8,128)(2,1)S(1)} %pad_maximum_fusion.5), channel_id=1, source_target_pairs={{0,10},{1,11},{2,12},{3,13},{4,14},{5,15},{6,8},{7,9},{8,0},{9,1},... | collective-permute-start | bytes 208904 | tf_op jit(solution)/shard_map/ppermute | solution.py:253
  37.1 7.7 %collective-permute-start.11 = (bf16[272,128]{1,0:T(8,128)(2,1)S(1)}, bf16[272,128]{1,0:T(8,128)(2,1)S(1)}, u32[]{:S(2)}, u32[]{:S(2)}) collective-permute-start(bf16[272,128]{1,0:T(8,128)(2,1)S(1)} %pad_maximum_fusion.5), channel_id=1, source_target_pairs={{0,20},{1,21},{2,22},{3,23},{4,16},{5,17},{6,18},{7,19},{8,30},{9,... | collective-permute-start | bytes 208904 | tf_op jit(solution)/shard_map/ppermute | solution.py:253
  41.7 5.2 %collective-permute-start.12 = (bf16[272,128]{1,0:T(8,128)(2,1)S(1)}, bf16[272,128]{1,0:T(8,128)(2,1)S(1)}, u32[]{:S(2)}, u32[]{:S(2)}) collective-permute-start(bf16[272,128]{1,0:T(8,128)(2,1)S(1)} %pad_maximum_fusion.5), channel_id=1, source_target_pairs={{0,30},{1,31},{2,24},{3,25},{4,26},{5,27},{6,28},{7,29},{8,20},{9,... | collective-permute-start | bytes 208904 | tf_op jit(solution)/shard_map/ppermute | solution.py:253
  42.2 5.7 %collective-permute-start.13 = (bf16[272,128]{1,0:T(8,128)(2,1)S(1)}, bf16[272,128]{1,0:T(8,128)(2,1)S(1)}, u32[]{:S(2)}, u32[]{:S(2)}) collective-permute-start(bf16[272,128]{1,0:T(8,128)(2,1)S(1)} %collective-permute-done.9), channel_id=1, source_target_pairs={{0,1},{1,24},{2,3},{3,26},{4,5},{5,28},{6,7},{7,30},{8,9},{9,0},{1... | collective-permute-start | bytes 208904 | tf_op jit(solution)/shard_map/ppermute | solution.py:240
  42.3 8.4 %collective-permute-start.15 = (bf16[272,128]{1,0:T(8,128)(2,1)S(1)}, bf16[272,128]{1,0:T(8,128)(2,1)S(1)}, u32[]{:S(2)}, u32[]{:S(2)}) collective-permute-start(bf16[272,128]{1,0:T(8,128)(2,1)S(1)} %collective-permute-done.10), channel_id=1, source_target_pairs={{0,1},{1,24},{2,3},{3,26},{4,5},{5,28},{6,7},{7,30},{8,9},{9,0},{1... | collective-permute-start | bytes 208904 | tf_op jit(solution)/shard_map/ppermute | solution.py:240
  44.8 5.8 %collective-permute-start.16 = (bf16[272,128]{1,0:T(8,128)(2,1)S(1)}, bf16[272,128]{1,0:T(8,128)(2,1)S(1)}, u32[]{:S(2)}, u32[]{:S(2)}) collective-permute-start(bf16[272,128]{1,0:T(8,128)(2,1)S(1)} %collective-permute-done.11), channel_id=1, source_target_pairs={{0,1},{1,24},{2,3},{3,26},{4,5},{5,28},{6,7},{7,30},{8,9},{9,0},{1... | collective-permute-start | bytes 208904 | tf_op jit(solution)/shard_map/ppermute | solution.py:240
  46.9 3.7 %collective-permute-start.14 = (bf16[272,128]{1,0:T(8,128)(2,1)S(1)}, bf16[272,128]{1,0:T(8,128)(2,1)S(1)}, u32[]{:S(2)}, u32[]{:S(2)}) collective-permute-start(bf16[272,128]{1,0:T(8,128)(2,1)S(1)} %collective-permute-done.12), channel_id=1, source_target_pairs={{0,1},{1,24},{2,3},{3,26},{4,5},{5,28},{6,7},{7,30},{8,9},{9,0},{1... | collective-permute-start | bytes 208904 | tf_op jit(solution)/shard_map/ppermute | solution.py:240
  53.5 7.9 %collective-permute-start.17 = (s16[272,256]{1,0:T(8,128)(2,1)S(1)}, s16[272,256]{1,0:T(8,128)(2,1)S(1)}, u32[]{:S(2)}, u32[]{:S(2)}) collective-permute-start(s16[272,256]{1,0:T(8,128)(2,1)S(1)} %get-tuple-element.59), channel_id=1, source_target_pairs={{0,24},{8,16},{16,8},{24,0},{1,25},{9,17},{17,9},{25,1},{2,26},{10... | collective-permute-start | bytes 417800 | tf_op jit(solution)/shard_map/ppermute | solution.py:229
  56.8 6.0 %collective-permute-start.18 = (s16[272,256]{1,0:T(8,128)(2,1)S(1)}, s16[272,256]{1,0:T(8,128)(2,1)S(1)}, u32[]{:S(2)}, u32[]{:S(2)}) collective-permute-start(s16[272,256]{1,0:T(8,128)(2,1)S(1)} %get-tuple-element.60), channel_id=1, source_target_pairs={{0,16},{8,24},{16,0},{24,8},{1,17},{9,25},{17,1},{25,9},{2,18},{10... | collective-permute-start | bytes 417800 | tf_op jit(solution)/shard_map/ppermute | solution.py:229
  59.0 5.1 %collective-permute-start.19 = (s16[272,256]{1,0:T(8,128)(2,1)S(1)}, s16[272,256]{1,0:T(8,128)(2,1)S(1)}, u32[]{:S(2)}, u32[]{:S(2)}) collective-permute-start(s16[272,256]{1,0:T(8,128)(2,1)S(1)} %get-tuple-element.61), channel_id=1, source_target_pairs={{0,8},{8,0},{16,24},{24,16},{1,9},{9,1},{17,25},{25,17},{2,10},{10... | collective-permute-start | bytes 417800 | tf_op jit(solution)/shard_map/ppermute | solution.py:229
  65.5 6.7 %collective-permute-start.20 = (bf16[304,256]{1,0:T(8,128)(2,1)S(1)}, bf16[304,256]{1,0:T(8,128)(2,1)S(1)}, u32[]{:S(2)}, u32[]{:S(2)}) collective-permute-start(bf16[304,256]{1,0:T(8,128)(2,1)S(1)} %get-tuple-element.66), channel_id=1, source_target_pairs={{0,8},{8,0},{16,24},{24,16},{1,9},{9,1},{17,25},{25,17},{2,10},{10... | collective-permute-start | bytes 466952 | tf_op jit(solution)/shard_map/ppermute | solution.py:229
  65.6 6.6 %collective-permute-start.21 = (bf16[304,256]{1,0:T(8,128)(2,1)S(1)}, bf16[304,256]{1,0:T(8,128)(2,1)S(1)}, u32[]{:S(2)}, u32[]{:S(2)}) collective-permute-start(bf16[304,256]{1,0:T(8,128)(2,1)S(1)} %get-tuple-element.67), channel_id=1, source_target_pairs={{0,16},{8,24},{16,0},{24,8},{1,17},{9,25},{17,1},{25,9},{2,18},{10... | collective-permute-start | bytes 466952 | tf_op jit(solution)/shard_map/ppermute | solution.py:229
  67.4 6.1 %collective-permute-start.22 = (bf16[304,256]{1,0:T(8,128)(2,1)S(1)}, bf16[304,256]{1,0:T(8,128)(2,1)S(1)}, u32[]{:S(2)}, u32[]{:S(2)}) collective-permute-start(bf16[304,256]{1,0:T(8,128)(2,1)S(1)} %get-tuple-element.68), channel_id=1, source_target_pairs={{0,24},{8,16},{16,8},{24,0},{1,25},{9,17},{17,9},{25,1},{2,26},{10... | collective-permute-start | bytes 466952 | tf_op jit(solution)/shard_map/ppermute | solution.py:229
  75.3 1.4 %collective-permute-start.23 = (f32[88,256]{1,0:T(8,128)S(1)}, f32[88,256]{1,0:T(8,128)S(1)}, u32[]{:S(2)}, u32[]{:S(2)}) collective-permute-start(f32[88,256]{1,0:T(8,128)S(1)} %pad_maximum_fusion.4), channel_id=1, source_target_pairs={{0,1},{1,0},{2,3},{3,2},{4,5},{5,4},{6,7},{7,6},{8,9},{9,8},{10,11... | collective-permute-start | bytes 270344 | tf_op jit(solution)/shard_map/ppermute | solution.py:243
  76.7 6.1 %collective-permute-start.24 = (bf16[88,256]{1,0:T(8,128)(2,1)S(1)}, bf16[88,256]{1,0:T(8,128)(2,1)S(1)}, u32[]{:S(2)}, u32[]{:S(2)}) collective-permute-start(bf16[88,256]{1,0:T(8,128)(2,1)S(1)} %fusion.15), channel_id=1, source_target_pairs={{0,6},{1,7},{2,4},{3,5},{4,2},{5,3},{6,0},{7,1},{8,14},{9,15},{10,... | collective-permute-start | bytes 135176 | tf_op jit(solution)/shard_map/ppermute | solution.py:243
  79.6 5.0 %collective-permute-start.25 = (bf16[88,256]{1,0:T(8,128)(2,1)S(1)}, bf16[88,256]{1,0:T(8,128)(2,1)S(1)}, u32[]{:S(2)}, u32[]{:S(2)}) collective-permute-start(bf16[88,256]{1,0:T(8,128)(2,1)S(1)} %fusion.15), channel_id=1, source_target_pairs={{0,4},{1,5},{2,6},{3,7},{4,0},{5,1},{6,2},{7,3},{8,12},{9,13},{10,... | collective-permute-start | bytes 135176 | tf_op jit(solution)/shard_map/ppermute | solution.py:243
  79.6 5.0 %collective-permute-start.26 = (bf16[88,256]{1,0:T(8,128)(2,1)S(1)}, bf16[88,256]{1,0:T(8,128)(2,1)S(1)}, u32[]{:S(2)}, u32[]{:S(2)}) collective-permute-start(bf16[88,256]{1,0:T(8,128)(2,1)S(1)} %fusion.15), channel_id=1, source_target_pairs={{0,2},{1,3},{2,0},{3,1},{4,6},{5,7},{6,4},{7,5},{8,10},{9,11},{10,... | collective-permute-start | bytes 135176 | tf_op jit(solution)/shard_map/ppermute | solution.py:243
  84.6 4.1 %collective-permute-start.27 = (bf16[88,256]{1,0:T(8,128)(2,1)S(1)}, bf16[88,256]{1,0:T(8,128)(2,1)S(1)}, u32[]{:S(2)}, u32[]{:S(2)}) collective-permute-start(bf16[88,256]{1,0:T(8,128)(2,1)S(1)} %add_convert_fusion), channel_id=1, source_target_pairs={{0,8},{8,0},{16,24},{24,16},{1,9},{9,1},{17,25},{25,17},{2,10},{10... | collective-permute-start | bytes 135176 | tf_op jit(solution)/shard_map/ppermute | solution.py:229
  85.8 4.0 %collective-permute-start.28 = (bf16[88,256]{1,0:T(8,128)(2,1)S(1)}, bf16[88,256]{1,0:T(8,128)(2,1)S(1)}, u32[]{:S(2)}, u32[]{:S(2)}) collective-permute-start(bf16[88,256]{1,0:T(8,128)(2,1)S(1)} %add_convert_fusion), channel_id=1, source_target_pairs={{0,16},{8,24},{16,0},{24,8},{1,17},{9,25},{17,1},{25,9},{2,18},{10... | collective-permute-start | bytes 135176 | tf_op jit(solution)/shard_map/ppermute | solution.py:229
  87.2 4.9 %collective-permute-start.29 = (bf16[88,256]{1,0:T(8,128)(2,1)S(1)}, bf16[88,256]{1,0:T(8,128)(2,1)S(1)}, u32[]{:S(2)}, u32[]{:S(2)}) collective-permute-start(bf16[88,256]{1,0:T(8,128)(2,1)S(1)} %add_convert_fusion), channel_id=1, source_target_pairs={{0,24},{8,16},{16,8},{24,0},{1,25},{9,17},{17,9},{25,1},{2,26},{10... | collective-permute-start | bytes 135176 | tf_op jit(solution)/shard_map/ppermute | solution.py:229
  92.2 1.5 %collective-permute-start.30 = (f32[160,256]{1,0:T(8,128)S(1)}, f32[160,256]{1,0:T(8,128)S(1)}, u32[]{:S(2)}, u32[]{:S(2)}) collective-permute-start(f32[160,256]{1,0:T(8,128)S(1)} %constant_dynamic-update-slice_fusion.6.total_ref), channel_id=1, source_target_pairs={{0,1},{1,0},{2,3},{3,2},{4,5},{5,4},{6,7},{7,6},{8,9},{9,8},{10,11... | collective-permute-start | bytes 491528 | tf_op jit(solution)/shard_map/ppermute | solution.py:243
  (8 other events, 67.9 us)
